TPU v7x, 32 devices: a whole 2x2x4 slice. The times are simulated.
32 devices in a mesh: row: 8 (over y, x, core), col: 4 (over z).
Axes of the slice: x: 2, y: 2, z: 4, core: 2. Of those that a mesh axis runs over, the one named last changes fastest.
Arguments:
- green: bfloat16 [16384, 8192], P('row', 'col'), may hold values from -0.09375 to 0.09375
- mask: int32 [64, 32], P('row', 'col'), may hold values from 0 to 1, as said below
- probes: bfloat16 [8192, 256], P('col', 'row'), may hold values from -6 to 6
Outputs:
- sketch: float32 [16384, 256], P('row', 'col')
- adjoint: float32 [8192, 256], P('col', 'row')
Inputs may be any that keep to these rules, and one draw needn't show every extreme that they name: `mask`: block row i belongs to gauge i % 6 and time block i // 6; block column j to window j // 8. A block is 1 when its time block is no earlier than the window's onset plus a travel delay of its gauge and subfault block.
All inputs are finite; a program needn't handle non-finite values.
Results may differ from a plain program's by a relative error of at most 0.0022.
Values may be sent and summed in bfloat16 or wider, within the bound.
No kernel may reach another device: no remote copies, remote signals or barrier semaphores. Data moves between devices by JAX's collectives and lax.ppermute only.
A program may use at most 128 MiB of HBM per device.

v0:
```python
import jax
import jax.numpy as jnp
from jax import lax
from jax.sharding import PartitionSpec as P


def local(green, mask, probes):
    row_blocks, col_blocks = mask.shape
    block_size = green.shape[0] // row_blocks
    shaped = green.reshape(row_blocks, block_size, col_blocks, block_size)
    tiles = (shaped * mask.astype(jnp.bfloat16)[:, None, :, None]).reshape(green.shape)
    partial_sketch = jnp.dot(
        tiles, lax.all_gather(probes, "row", axis=1, tiled=True), preferred_element_type=jnp.float32
    )
    summed = lax.psum(partial_sketch, "col")
    width_own = summed.shape[1] // lax.axis_size("col")
    own_sketch = lax.dynamic_slice_in_dim(summed, lax.axis_index("col") * width_own, width_own, 1)
    term = lax.dot_general(
        tiles,
        summed.astype(jnp.bfloat16),
        (((0,), (0,)), ((), ())),
        preferred_element_type=jnp.float32,
    )
    adjoint = lax.psum_scatter(term, "row", scatter_dimension=1, tiled=True)
    return (own_sketch, adjoint)


def solution(mesh):
    in_specs = (P("row", "col"), P("row", "col"), P("col", "row"))
    out_specs = (P("row", "col"), P("col", "row"))
    return jax.shard_map(local, mesh=mesh, in_specs=in_specs, out_specs=out_specs, check_vma=False)
```

profile of v0, /device:TPU:0, one launch (start us, length us, event | category | flops | bytes accessed | tf_op | source)
XLA Modules:
  0.0 184.8 jit_solution(15817741629691325850)
XLA Ops:
  7.2 0.0 all-gather.2.cloned.1.call-start
  7.2 0.7 all-gather.2.cloned.1.call-update
  7.9 0.0 all-reduce.2.cloned.1.call-start
  7.9 0.7 convert_element_type.6
  8.6 3.8 %mul.14 = bf16[8,256,8,256]{3,2,1,0:T(8,128)(2,1)} broadcast(bf16[8,8]{1,0:T(8,128)(2,1)S(1)} %convert_element_type.6), dimensions={0,2} | broadcast | bytes 8388736 | tf_op jit(solution)/shard_map/mul | solution.py:11
  12.5 10.3 %copy.6 = bf16[256,8,8,256]{3,1,2,0:T(8,128)(2,1)} copy(bf16[256,8,8,256]{3,2,1,0:T(8,128)(2,1)} %bitcast.7) | data formatting | bytes 16777216
  22.7 10.6 %mul.16 = bf16[2048,2048]{1,0:T(8,128)(2,1)} multiply(bf16[2048,2048]{1,0:T(8,128)(2,1)} %param.3, bf16[2048,2048]{1,0:T(8,128)(2,1)} %bitcast.6) | non-fusion elementwise | flops 4194304 | bytes 25165824 | tf_op jit(solution)/shard_map/mul | solution.py:11
  33.4 2.7 %all-gather.2.cloned.1.call-done = bf16[2048,256]{0,1:T(8,128)(2,1)} async-done(((bf16[2048,32]{0,1:T(8,128)(2,1)}), bf16[2048,256]{0,1:T(8,128)(2,1)}) %all-gather.2.cloned.1.call-update) | async-done | bytes 1048592 | tf_op jit(solution)/shard_map/all_gather | solution.py:13
  36.1 7.3 %fusion.2 = f32[2048,256]{1,0:T(8,128)} fusion(bf16[2048,2048]{1,0:T(8,128)(2,1)} %mul.16, bf16[2048,256]{0,1:T(8,128)(2,1)} %all-gather.2.cloned.1.call-done), kind=kOutput, calls=%fused_computation.3 | convolution fusion | flops 2147483648 | bytes 11534336 | tf_op jit(solution)/shard_map/dot_general | solution.py:12
  43.4 0.0 all-reduce.2.cloned.1.call-update
  43.4 0.0 reduce-scatter.2.cloned.1.call-start
  43.5 86.6 %all-reduce.2.cloned.1.call-done = f32[2048,256]{1,0:T(8,128)} async-done(((f32[2048,256]{1,0:T(8,128)}), f32[2048,256]{1,0:T(8,128)}) %all-reduce.2.cloned.1.call-update) | async-done | bytes 2097168 | tf_op jit(solution)/shard_map/psum | solution.py:15
  130.1 0.0 copy-start
  130.1 7.8 %fusion = f32[2048,256]{0,1:T(8,128)} fusion(bf16[2048,2048]{1,0:T(8,128)(2,1)} %mul.16, f32[2048,256]{1,0:T(8,128)} %all-reduce.2.cloned.1.call-done), kind=kOutput, calls=%fused_computation | convolution fusion | flops 2148007936 | bytes 12582912 | tf_op jit(solution)/shard_map/dot_general | solution.py:18
  137.9 0.0 reduce-scatter.2.cloned.1.call-update
  137.9 0.0 copy-done
  138.0 0.3 constant_dynamic-slice_fusion
  138.3 1.1 copy.5
  139.4 38.9 %reduce-scatter.2.cloned.1.call-done = f32[2048,32]{0,1:T(8,128)} async-done(((f32[2048,256]{0,1:T(8,128)}), f32[2048,32]{0,1:T(8,128)}) %reduce-scatter.2.cloned.1.call-update) | async-done | bytes 262160 | tf_op jit(solution)/shard_map/reduce_scatter | solution.py:24
Async XLA Ops:
  7.2 28.9 %all-gather.2.cloned.1.call-start = ((), (), s32[]{:S(2)}) async-start(), calls=%async_computation.1 | async-start | bytes 1179648 | tf_op jit(solution)/shard_map/all_gather | solution.py:13
  7.9 122.2 %all-reduce.2.cloned.1.call-start = ((), (), s32[]{:S(2)}) async-start(), calls=%async_computation.2 | async-start | bytes 4194304 | tf_op jit(solution)/shard_map/psum | solution.py:15
  43.4 134.8 %reduce-scatter.2.cloned.1.call-start = ((), (), s32[]{:S(2)}) async-start(), calls=%async_computation.3 | async-start | bytes 2359296 | tf_op jit(solution)/shard_map/reduce_scatter | solution.py:24
  130.1 7.8 %copy-start = (f32[2048,256]{1,0:T(8,128)S(1)}, f32[2048,256]{1,0:T(8,128)}, u32[]{:S(2)}) copy-start(f32[2048,256]{1,0:T(8,128)} %all-reduce.2.cloned.1.call-done) | copy-start | bytes 6291460
Sparse Core Ops, SparseCore 0:
  9.9 26.1 all-gather.1
  43.6 86.4 all-reduce.1
  138.1 40.1 reduce-scatter.1
where the time goes:
time: 185 us
  waiting for transfers between devices  129 us (70%)
  local copies, waits for them, and re-layouts  15.6 us (8%)
  matrix products  15.1 us (8%)
  between operations  13.8 us (7%)
  other arithmetic  11.3 us (6%)
    psum x1, waiting for transfers between devices, local(): summed = lax.psum(partial_sketch, 'col')  86.6 us
    reduce_scatter x1, waiting for transfers between devices, local(): adjoint = lax.psum_scatter(term, 'row', scatter_dimension=1, tiled=True)  38.9 us
    unnamed x4, local copies, waits for them, and re-layouts  11.4 us
    mul x1, other arithmetic, local(): shaped * mask.astype(jnp.bfloat16)[:, None, :, None]  10.6 us
    dot_general x1, matrix products, local(): lax.dot_general(tiles, summed.astype(jnp.bfloat16), (((0,), (0,)), ((), (...  7.8 us
    dot_general x1, matrix products, local(): jnp.dot(tiles, lax.all_gather(probes, 'row', axis=1, tiled=True), preferr...  7.31 us
    mul x1, local copies, waits for them, and re-layouts, local(): shaped * mask.astype(jnp.bfloat16)[:, None, :, None]  3.83 us
  transfers between devices with their start and end apart: 3, of which 3 were waited for; matrix products, arithmetic and copies ran while one was open for 15% of the time, Pallas kernels for 0%

commit v1 on v0

v1 whole, which is shorter than its diff:
```python
import functools

import jax
import jax.numpy as jnp
from jax import lax
from jax.experimental import pallas as pl
from jax.experimental.pallas import tpu as pltpu
from jax.sharding import PartitionSpec as P

F32, BF16 = jnp.float32, jnp.bfloat16
CHUNKS = 1


def exchange(value, axis, offset):
    size = lax.axis_size(axis)
    return lax.ppermute(value, axis, [(i, i ^ offset) for i in range(size)])


def level(mask_ref, i, j, block):
    return jnp.full((block, block), mask_ref[i, j].astype(F32)).astype(BF16)


def sketch_kernel(where, mask_ref, green_ref, *refs, offsets_row, offsets_col, base, block):
    blocks, outs = refs[: len(offsets_row)], refs[len(offsets_row) : -2]
    probes, total = refs[-2:]
    width = blocks[0].shape[0]
    share = outs[0].shape[0]

    @pl.when(pl.program_id(0) == 0)
    def _():
        for offset, ref in zip(offsets_row, blocks):
            start = pl.multiple_of((where[0] ^ offset) * width, width)
            probes[pl.ds(start, width), :] = ref[...]

    i = pl.program_id(0) + base
    tiles = jnp.concatenate(
        [
            green_ref[:, j * block : (j + 1) * block] * level(mask_ref, i, j, block)
            for j in range(green_ref.shape[1] // block)
        ],
        axis=1,
    )
    total[...] = lax.dot_general(probes[...], tiles, (((1,), (1,)), ((), ())), preferred_element_type=F32)
    for offset, out in zip(offsets_col, outs):
        start = pl.multiple_of((where[1] ^ offset) * share, share)
        out[...] = total[pl.ds(start, share), :].astype(out.dtype)


def partial_sketch(where, mask, green, blocks, offsets_row, offsets_col, chunk, chunks, width):
    rows, cols = green.shape
    block = rows // mask.shape[0]
    steps = rows // block // chunks
    share = width // len(offsets_col)
    base = chunk * steps
    kernel = functools.partial(
        sketch_kernel, offsets_row=offsets_row, offsets_col=offsets_col, base=base, block=block
    )
    smem = pl.BlockSpec(memory_space=pltpu.SMEM)
    return pl.pallas_call(
        kernel,
        grid=(steps,),
        in_specs=[smem, smem, pl.BlockSpec((block, cols), lambda i: (i + base, 0))]
        + [pl.BlockSpec(b.shape, lambda i: (0, 0)) for b in blocks],
        out_specs=[pl.BlockSpec((share, block), lambda i: (0, i))] * len(offsets_col),
        out_shape=[
            jax.ShapeDtypeStruct((share, rows // chunks), F32 if offset == 0 else BF16) for offset in offsets_col
        ],
        scratch_shapes=[pltpu.VMEM((width, cols), BF16), pltpu.VMEM((width, block), F32)],
        compiler_params=pltpu.CompilerParams(vmem_limit_bytes=32 * 2**20),
        cost_estimate=pl.CostEstimate(
            flops=2 * width * cols * rows // chunks, bytes_accessed=2 * rows * cols // chunks, transcendentals=0
        ),
        name="partial_sketch",
    )(where, mask, green, *blocks)


def adjoint_kernel(where, mask_ref, green_ref, *refs, offsets_col, offsets_core, chunks, block):
    count = len(offsets_col) * chunks
    shares, outs = refs[:count], refs[count:-2]
    lowered, total = refs[-2:]
    share, length = shares[0].shape
    width = outs[0].shape[0]

    @pl.when(pl.program_id(0) == 0)
    def _():
        for k, ref in enumerate(shares):
            start = pl.multiple_of((where[1] ^ offsets_col[k // chunks]) * share, share)
            at = (k % chunks) * length
            lowered[pl.ds(start, share), at : at + length] = ref[...]

    j = pl.program_id(0)
    tiles = jnp.concatenate(
        [
            green_ref[i * block : (i + 1) * block, :] * level(mask_ref, i, j, block)
            for i in range(green_ref.shape[0] // block)
        ],
        axis=0,
    )
    total[...] = jnp.dot(lowered[...], tiles, preferred_element_type=F32)
    sibling = outs[-1]
    for k, offset in enumerate(offsets_core):
        start = pl.multiple_of((where[0] ^ offset) * width, width)
        outs[k][...] = total[pl.ds(start, width), :]
        start = pl.multiple_of((where[0] ^ 1 ^ offset) * width, width)
        sibling[k * width : (k + 1) * width, :] = total[pl.ds(start, width), :].astype(sibling.dtype)


def partial_adjoint(where, mask, green, shares, offsets_col, offsets_core, chunks, width):
    rows, cols = green.shape
    block = cols // mask.shape[1]
    own = width // (2 * len(offsets_core))
    kernel = functools.partial(
        adjoint_kernel, offsets_col=offsets_col, offsets_core=offsets_core, chunks=chunks, block=block
    )
    smem = pl.BlockSpec(memory_space=pltpu.SMEM)
    heights = [own] * len(offsets_core) + [own * len(offsets_core)]
    return pl.pallas_call(
        kernel,
        grid=(cols // block,),
        in_specs=[smem, smem, pl.BlockSpec((rows, block), lambda j: (0, j))]
        + [pl.BlockSpec(s.shape, lambda j: (0, 0)) for s in shares],
        out_specs=[pl.BlockSpec((h, block), lambda j: (0, j)) for h in heights],
        out_shape=[jax.ShapeDtypeStruct((h, cols), F32) for h in heights],
        scratch_shapes=[pltpu.VMEM((width, rows), BF16), pltpu.VMEM((width, block), F32)],
        compiler_params=pltpu.CompilerParams(vmem_limit_bytes=32 * 2**20),
        cost_estimate=pl.CostEstimate(
            flops=2 * width * cols * rows, bytes_accessed=2 * rows * cols, transcendentals=0
        ),
        name="partial_adjoint",
    )(where, mask, green, *shares)


def local(green, mask, probes):
    n_row, n_col = lax.axis_size("row"), lax.axis_size("col")
    where = jnp.stack([lax.axis_index("row"), lax.axis_index("col")]).astype(jnp.int32)
    width = probes.shape[1] * n_row
    offsets_col = list(range(n_col))
    offsets_core = list(range(0, n_row, 2))

    own = probes.T
    held = [own] + [exchange(own, "row", offset) for offset in offsets_core[1:]]
    twins = [exchange(block, "row", 1) for block in held]
    blocks = held + twins
    offsets_row = offsets_core + [offset ^ 1 for offset in offsets_core]

    sums, shares = [], [[] for _ in offsets_col]
    for chunk in range(CHUNKS):
        parts = partial_sketch(where, mask, green, blocks, offsets_row, offsets_col, chunk, CHUNKS, width)
        total = parts[0]
        for offset in offsets_col[1:]:
            total = total + exchange(parts[offset], "col", offset).astype(F32)
        sums.append(total)
        lowered = total.astype(BF16)
        for offset in offsets_col:
            shares[offset].append(lowered if offset == 0 else exchange(lowered, "col", offset))
    sketch = jnp.concatenate(sums, axis=1) if CHUNKS > 1 else sums[0]

    flat = [share for per_offset in shares for share in per_offset]
    *mine, others = partial_adjoint(where, mask, green, flat, offsets_col, offsets_core, CHUNKS, width)
    others = exchange(others, "row", 1)
    own_width = mine[0].shape[0]
    pairs = [m + others[k * own_width : (k + 1) * own_width] for k, m in enumerate(mine)]
    adjoint = pairs[0]
    for offset, pair in zip(offsets_core[1:], pairs[1:]):
        adjoint = adjoint + exchange(pair.astype(BF16), "row", offset).astype(F32)
    return sketch.T, adjoint.T


def solution(mesh):
    in_specs = (P("row", "col"), P("row", "col"), P("col", "row"))
    out_specs = (P("row", "col"), P("col", "row"))
    return jax.shard_map(local, mesh=mesh, in_specs=in_specs, out_specs=out_specs, check_vma=False)
```

time: 185 us -> 96.2 us (0.52)
  waiting for transfers between devices: 129 us -> 52 us
  starting transfers between devices: 0.12 us -> 25.4 us
  matrix products: 15.1 us -> 0 us
  between operations: 13.8 us -> 0.68 us
  Pallas kernels: 0 us -> 11 us
  local copies, waits for them, and re-layouts: 15.6 us -> 4.97 us
  other arithmetic: 11.3 us -> 1.87 us
    psum x1 -> x0, waiting for transfers between devices: 86.6 us -> none  [local(): summed = lax.psum(partial_sketch, 'col')]
    ppermute x0 -> x17, waiting for transfers between devices: none -> 52 us  [exchange(): return lax.ppermute(value, axis, [(i, i ^ offset) for i in range(size)])]
    reduce_scatter x1 -> x0, waiting for transfers between devices: 38.9 us -> none  [local(): adjoint = lax.psum_scatter(term, 'row', scatter_dimension=1, tiled=True)]
    ppermute x0 -> x17, starting transfers between devices: none -> 25.4 us  [exchange(): return lax.ppermute(value, axis, [(i, i ^ offset) for i in range(size)])]
    dot_general x2 -> x0, matrix products: 15.1 us -> none  [the longest x1 7.8 us: local(): lax.dot_general(tiles, summed.astype(jnp.bfloat16), (((0,), (0,)), ((), (...]
    pallas_call x0 -> x2, Pallas kernels: none -> 11 us  [the longest x1 5.93 us: partial_adjoint(): pl.pallas_call(kernel, grid=(cols // block,), in_specs=[smem, smem, pl.Bl...]
    mul x1 -> x0, other arithmetic: 10.6 us -> none  [local(): shaped * mask.astype(jnp.bfloat16)[:, None, :, None]]
    unnamed x4 -> x6, local copies, waits for them, and re-layouts: 11.4 us -> 4.97 us
  transfers between devices with their start and end apart: 3 -> 17, of which waited for: 3 -> 12; matrix products, arithmetic and copies ran while one was open for 15% -> 0% of each run, Pallas kernels for 0% -> 0%
where the time goes in v1:
time: 96.2 us; the launch traced here: 96 us
  waiting for transfers between devices  52 us (54%)
  starting transfers between devices  25.4 us (26%)
  Pallas kernels  11 us (11%)
  local copies, waits for them, and re-layouts  4.97 us (5%)
  other arithmetic  1.87 us (2%)
    ppermute x17, waiting for transfers between devices, exchange(): return lax.ppermute(value, axis, [(i, i ^ offset) for i in range(size)])  52 us
    ppermute x17, starting transfers between devices, exchange(): return lax.ppermute(value, axis, [(i, i ^ offset) for i in range(size)])  25.4 us
    pallas_call x1, Pallas kernels, partial_adjoint(): pl.pallas_call(kernel, grid=(cols // block,), in_specs=[smem, smem, pl.Bl...  5.93 us
    pallas_call x1, Pallas kernels, partial_sketch(): pl.pallas_call(kernel, grid=(steps,), in_specs=[smem, smem, pl.BlockSpec(...  5.07 us
    unnamed x6, local copies, waits for them, and re-layouts  4.97 us
  transfers between devices with their start and end apart: 17, of which 12 were waited for; matrix products, arithmetic and copies ran while one was open for 0% of the time, Pallas kernels for 0%

profile of v1, /device:TPU:0, one launch (start us, length us, event | category | flops | bytes accessed | tf_op | source)
XLA Modules:
  0.0 96.0 jit_solution(4525390844741018931)
XLA Ops:
  0.6 4.0 %collective-permute-start.2 = (bf16[32,2048]{1,0:T(8,128)(2,1)}, bf16[32,2048]{1,0:T(8,128)(2,1)S(1)}, u32[]{:S(2)}, u32[]{:S(2)}) collective-permute-start(bf16[32,2048]{1,0:T(8,128)(2,1)} %bitcast.7), channel_id=1, source_target_pairs={{0,24},{4,28},{8,16},{12,20},{16,8},{20,12},{24,0},{28,4},{1,25},{... | collective-permute-start | bytes 393224 | tf_op jit(solution)/shard_map/ppermute | solution.py:16
  4.6 0.5 collective-permute-start.1
  5.1 0.1 collective-permute-start
  5.2 3.6 %collective-permute-done.2.refs_3_ = bf16[32,2048]{1,0:T(8,128)(2,1)S(1)} collective-permute-done((bf16[32,2048]{1,0:T(8,128)(2,1)}, bf16[32,2048]{1,0:T(8,128)(2,1)S(1)}, u32[]{:S(2)}, u32[]{:S(2)}) %collective-permute-start.2) | collective-permute-done | bytes 131104 | tf_op jit(solution)/shard_map/ppermute | solution.py:16
  8.8 2.3 %collective-permute-done.1.refs_2_ = bf16[32,2048]{1,0:T(8,128)(2,1)S(1)} collective-permute-done((bf16[32,2048]{1,0:T(8,128)(2,1)}, bf16[32,2048]{1,0:T(8,128)(2,1)S(1)}, u32[]{:S(2)}, u32[]{:S(2)}) %collective-permute-start.1) | collective-permute-done | bytes 131104 | tf_op jit(solution)/shard_map/ppermute | solution.py:16
  11.1 0.2 collective-permute-done.refs_1_
  11.4 0.3 collective-permute-start.4
  11.7 0.8 collective-permute-done.5.refs_6_
  12.5 0.2 collective-permute-done.4.refs_5_
  12.7 3.4 %copy-done = bf16[2048,2048]{1,0:T(8,128)(2,1)S(1)} copy-done((bf16[2048,2048]{1,0:T(8,128)(2,1)S(1)}, bf16[2048,2048]{1,0:T(8,128)(2,1)}, u32[]{:S(2)}) %copy-start) | copy-done | bytes 8388632
  16.1 0.9 copy-done.1
  17.0 0.7 copy-done.2
  17.7 5.1 %partial_sketch.1 = (f32[64,2048]{1,0:T(8,128)S(1)}, bf16[64,2048]{1,0:T(8,128)(2,1)S(1)}, bf16[64,2048]{1,0:T(8,128)(2,1)S(1)}, bf16[64,2048]{1,0:T(8,128)(2,1)S(1)}) custom-call(s32[2]{0:T(128)S(1)} %pad_add_fusion.where, s32[8,8]{1,0:T(8,128)S(1)} %copy-done.2, bf16[2048,2048]{1,0:T(8,128)(2,1)S(1)} %copy-done, bf16[32,2048]{1,0:T(8,128)(2,1)S(1)} %bitcast.11, ...), custom_call_target="tpu_custom_call" | custom-call | flops 2147483648 | bytes 8388608 | tf_op jit(solution)/shard_map/partial_sketch/pallas_call | solution.py:59
  22.8 1.8 %collective-permute-start.7 = (bf16[64,2048]{1,0:T(8,128)(2,1)S(1)}, bf16[64,2048]{1,0:T(8,128)(2,1)S(1)}, u32[]{:S(2)}, u32[]{:S(2)}) collective-permute-start(bf16[64,2048]{1,0:T(8,128)(2,1)S(1)} %get-tuple-element.12), channel_id=1, source_target_pairs={{0,1},{1,0},{2,3},{3,2},{4,5},{5,4},{6,7},{7,6},{8,9},{9,8},{10,11... | collective-permute-start | bytes 786440 | tf_op jit(solution)/shard_map/ppermute | solution.py:16
  24.5 2.6 %collective-permute-start.8 = (bf16[64,2048]{1,0:T(8,128)(2,1)S(1)}, bf16[64,2048]{1,0:T(8,128)(2,1)S(1)}, u32[]{:S(2)}, u32[]{:S(2)}) collective-permute-start(bf16[64,2048]{1,0:T(8,128)(2,1)S(1)} %get-tuple-element.13), channel_id=1, source_target_pairs={{0,2},{1,3},{2,0},{3,1},{4,6},{5,7},{6,4},{7,5},{8,10},{9,11},{10,... | collective-permute-start | bytes 786440 | tf_op jit(solution)/shard_map/ppermute | solution.py:16
  27.2 9.2 %collective-permute-done.7 = bf16[64,2048]{1,0:T(8,128)(2,1)S(1)} collective-permute-done((bf16[64,2048]{1,0:T(8,128)(2,1)S(1)}, bf16[64,2048]{1,0:T(8,128)(2,1)S(1)}, u32[]{:S(2)}, u32[]{:S(2)}) %collective-permute-start.7) | collective-permute-done | bytes 262176 | tf_op jit(solution)/shard_map/ppermute | solution.py:16
  36.4 9.4 %collective-permute-done.8 = bf16[64,2048]{1,0:T(8,128)(2,1)S(1)} collective-permute-done((bf16[64,2048]{1,0:T(8,128)(2,1)S(1)}, bf16[64,2048]{1,0:T(8,128)(2,1)S(1)}, u32[]{:S(2)}, u32[]{:S(2)}) %collective-permute-start.8) | collective-permute-done | bytes 262176 | tf_op jit(solution)/shard_map/ppermute | solution.py:16
  45.9 0.9 fusion.7
  46.8 2.5 %collective-permute-start.12 = (bf16[64,2048]{1,0:T(8,128)(2,1)S(1)}, bf16[64,2048]{1,0:T(8,128)(2,1)S(1)}, u32[]{:S(2)}, u32[]{:S(2)}) collective-permute-start(bf16[64,2048]{1,0:T(8,128)(2,1)S(1)} %get-tuple-element.20.refs_0_), channel_id=1, source_target_pairs={{0,3},{1,2},{2,1},{3,0},{4,7},{5,6},{6,5},{7,4},{8,11},{9,10},{10,... | collective-permute-start | bytes 786440 | tf_op jit(solution)/shard_map/ppermute | solution.py:16
  49.3 9.9 %collective-permute-start.11 = (bf16[64,2048]{1,0:T(8,128)(2,1)S(1)}, bf16[64,2048]{1,0:T(8,128)(2,1)S(1)}, u32[]{:S(2)}, u32[]{:S(2)}) collective-permute-start(bf16[64,2048]{1,0:T(8,128)(2,1)S(1)} %get-tuple-element.20.refs_0_), channel_id=1, source_target_pairs={{0,2},{1,3},{2,0},{3,1},{4,6},{5,7},{6,4},{7,5},{8,10},{9,11},{10,... | collective-permute-start | bytes 786440 | tf_op jit(solution)/shard_map/ppermute | solution.py:16
  59.1 0.1 collective-permute-start.10
  59.3 16.3 %collective-permute-done.11.refs_2_ = bf16[64,2048]{1,0:T(8,128)(2,1)S(1)} collective-permute-done((bf16[64,2048]{1,0:T(8,128)(2,1)S(1)}, bf16[64,2048]{1,0:T(8,128)(2,1)S(1)}, u32[]{:S(2)}, u32[]{:S(2)}) %collective-permute-start.11) | collective-permute-done | bytes 262176 | tf_op jit(solution)/shard_map/ppermute | solution.py:16
  75.6 5.9 %partial_adjoint.1 = (f32[32,2048]{1,0:T(8,128)S(1)}, f32[32,2048]{1,0:T(8,128)S(1)}, f32[32,2048]{1,0:T(8,128)S(1)}, f32[32,2048]{1,0:T(8,128)S(1)}, f32[128,2048]{1,0:T(8,128)S(1)}) custom-call(s32[2]{0:T(128)S(1)} %pad_add_fusion.where, s32[8,8]{1,0:T(8,128)S(1)} %copy-done.2, bf16[2048,2048]{1,0:T(8,128)(2,1)S(1)} %copy-done, ...), custom_call_target="tpu_custom_call" | custom-call | flops 2147483648 | bytes 8388608 | tf_op jit(solution)/shard_map/partial_adjoint/pallas_call | solution.py:117
  81.6 2.6 %collective-permute-done.13 = f32[128,2048]{1,0:T(8,128)S(1)} collective-permute-done((f32[128,2048]{1,0:T(8,128)S(1)}, f32[128,2048]{1,0:T(8,128)S(1)}, u32[]{:S(2)}, u32[]{:S(2)}) %collective-permute-start.13) | collective-permute-done | bytes 1048608 | tf_op jit(solution)/shard_map/ppermute | solution.py:16
  84.3 0.1 fusion.2
  84.4 1.6 %collective-permute-start.14 = (bf16[32,2048]{1,0:T(8,128)(2,1)S(1)}, bf16[32,2048]{1,0:T(8,128)(2,1)S(1)}, u32[]{:S(2)}, u32[]{:S(2)}) collective-permute-start(bf16[32,2048]{1,0:T(8,128)(2,1)S(1)} %get-tuple-element.22), channel_id=1, source_target_pairs={{0,8},{4,12},{8,0},{12,4},{16,24},{20,28},{24,16},{28,20},{1,9},{5... | collective-permute-start | bytes 393224 | tf_op jit(solution)/shard_map/ppermute | solution.py:16
  85.9 1.5 %collective-permute-start.16 = (bf16[32,2048]{1,0:T(8,128)(2,1)S(1)}, bf16[32,2048]{1,0:T(8,128)(2,1)S(1)}, u32[]{:S(2)}, u32[]{:S(2)}) collective-permute-start(bf16[32,2048]{1,0:T(8,128)(2,1)S(1)} %get-tuple-element.23), channel_id=1, source_target_pairs={{0,24},{4,28},{8,16},{12,20},{16,8},{20,12},{24,0},{28,4},{1,25},{... | collective-permute-start | bytes 393224 | tf_op jit(solution)/shard_map/ppermute | solution.py:16
  87.4 0.5 collective-permute-start.15
  87.9 2.9 %collective-permute-done.14 = bf16[32,2048]{1,0:T(8,128)(2,1)S(1)} collective-permute-done((bf16[32,2048]{1,0:T(8,128)(2,1)S(1)}, bf16[32,2048]{1,0:T(8,128)(2,1)S(1)}, u32[]{:S(2)}, u32[]{:S(2)}) %collective-permute-start.14) | collective-permute-done | bytes 131104 | tf_op jit(solution)/shard_map/ppermute | solution.py:16
  90.8 3.1 %collective-permute-done.16 = bf16[32,2048]{1,0:T(8,128)(2,1)S(1)} collective-permute-done((bf16[32,2048]{1,0:T(8,128)(2,1)S(1)}, bf16[32,2048]{1,0:T(8,128)(2,1)S(1)}, u32[]{:S(2)}, u32[]{:S(2)}) %collective-permute-start.16) | collective-permute-done | bytes 131104 | tf_op jit(solution)/shard_map/ppermute | solution.py:16
  93.8 1.4 %collective-permute-done.15 = bf16[32,2048]{1,0:T(8,128)(2,1)S(1)} collective-permute-done((bf16[32,2048]{1,0:T(8,128)(2,1)S(1)}, bf16[32,2048]{1,0:T(8,128)(2,1)S(1)}, u32[]{:S(2)}, u32[]{:S(2)}) %collective-permute-start.15) | collective-permute-done | bytes 131104 | tf_op jit(solution)/shard_map/ppermute | solution.py:16
  95.2 0.8 fusion.6
  (14 shorter events, 0.3 us)
Async XLA Ops:
  0.6 8.2 %collective-permute-start.2 = (bf16[32,2048]{1,0:T(8,128)(2,1)}, bf16[32,2048]{1,0:T(8,128)(2,1)S(1)}, u32[]{:S(2)}, u32[]{:S(2)}) collective-permute-start(bf16[32,2048]{1,0:T(8,128)(2,1)} %bitcast.7), channel_id=1, source_target_pairs={{0,24},{4,28},{8,16},{12,20},{16,8},{20,12},{24,0},{28,4},{1,25},{... | collective-permute-start | bytes 393224 | tf_op jit(solution)/shard_map/ppermute | solution.py:16
  4.6 6.5 %collective-permute-start.1 = (bf16[32,2048]{1,0:T(8,128)(2,1)}, bf16[32,2048]{1,0:T(8,128)(2,1)S(1)}, u32[]{:S(2)}, u32[]{:S(2)}) collective-permute-start(bf16[32,2048]{1,0:T(8,128)(2,1)} %bitcast.8), channel_id=1, source_target_pairs={{0,16},{4,20},{8,24},{12,28},{16,0},{20,4},{24,8},{28,12},{1,17},{... | collective-permute-start | bytes 393224 | tf_op jit(solution)/shard_map/ppermute | solution.py:16
  5.1 6.3 %collective-permute-start = (bf16[32,2048]{1,0:T(8,128)(2,1)}, bf16[32,2048]{1,0:T(8,128)(2,1)S(1)}, u32[]{:S(2)}, u32[]{:S(2)}) collective-permute-start(bf16[32,2048]{1,0:T(8,128)(2,1)} %bitcast.9), channel_id=1, source_target_pairs={{0,8},{4,12},{8,0},{12,4},{16,24},{20,28},{24,16},{28,20},{1,9},{5... | collective-permute-start | bytes 393224 | tf_op jit(solution)/shard_map/ppermute | solution.py:16
  5.2 6.5 %collective-permute-start.3 = (bf16[32,2048]{1,0:T(8,128)(2,1)}, bf16[32,2048]{1,0:T(8,128)(2,1)S(1)}, u32[]{:S(2)}, u32[]{:S(2)}) collective-permute-start(bf16[32,2048]{1,0:T(8,128)(2,1)} %bitcast.10), channel_id=1, source_target_pairs={{0,4},{4,0},{8,12},{12,8},{16,20},{20,16},{24,28},{28,24},{1,5},{5... | collective-permute-start | bytes 393224 | tf_op jit(solution)/shard_map/ppermute | solution.py:16
  8.8 2.9 %collective-permute-start.6 = (bf16[32,2048]{1,0:T(8,128)(2,1)S(1)}, bf16[32,2048]{1,0:T(8,128)(2,1)S(1)}, u32[]{:S(2)}, u32[]{:S(2)}) collective-permute-start(bf16[32,2048]{1,0:T(8,128)(2,1)S(1)} %collective-permute-done.2.refs_3_), channel_id=1, source_target_pairs={{0,4},{4,0},{8,12},{12,8},{16,20},{20,16},{24,28},{28,24},{1,5},{5... | collective-permute-start | bytes 393224 | tf_op jit(solution)/shard_map/ppermute | solution.py:16
  11.1 1.3 %collective-permute-start.5 = (bf16[32,2048]{1,0:T(8,128)(2,1)S(1)}, bf16[32,2048]{1,0:T(8,128)(2,1)S(1)}, u32[]{:S(2)}, u32[]{:S(2)}) collective-permute-start(bf16[32,2048]{1,0:T(8,128)(2,1)S(1)} %collective-permute-done.1.refs_2_), channel_id=1, source_target_pairs={{0,4},{4,0},{8,12},{12,8},{16,20},{20,16},{24,28},{28,24},{1,5},{5... | collective-permute-start | bytes 393224 | tf_op jit(solution)/shard_map/ppermute | solution.py:16
  11.4 1.3 %collective-permute-start.4 = (bf16[32,2048]{1,0:T(8,128)(2,1)S(1)}, bf16[32,2048]{1,0:T(8,128)(2,1)S(1)}, u32[]{:S(2)}, u32[]{:S(2)}) collective-permute-start(bf16[32,2048]{1,0:T(8,128)(2,1)S(1)} %collective-permute-done.refs_1_), channel_id=1, source_target_pairs={{0,4},{4,0},{8,12},{12,8},{16,20},{20,16},{24,28},{28,24},{1,5},{5... | collective-permute-start | bytes 393224 | tf_op jit(solution)/shard_map/ppermute | solution.py:16
  12.7 3.4 %copy-start = (bf16[2048,2048]{1,0:T(8,128)(2,1)S(1)}, bf16[2048,2048]{1,0:T(8,128)(2,1)}, u32[]{:S(2)}) copy-start(bf16[2048,2048]{1,0:T(8,128)(2,1)} %green_ref.3) | copy-start | bytes 25165828
  16.1 0.9 copy-start.1
  17.0 0.7 copy-start.2
  22.8 13.7 %collective-permute-start.7 = (bf16[64,2048]{1,0:T(8,128)(2,1)S(1)}, bf16[64,2048]{1,0:T(8,128)(2,1)S(1)}, u32[]{:S(2)}, u32[]{:S(2)}) collective-permute-start(bf16[64,2048]{1,0:T(8,128)(2,1)S(1)} %get-tuple-element.12), channel_id=1, source_target_pairs={{0,1},{1,0},{2,3},{3,2},{4,5},{5,4},{6,7},{7,6},{8,9},{9,8},{10,11... | collective-permute-start | bytes 786440 | tf_op jit(solution)/shard_map/ppermute | solution.py:16
  24.5 21.4 %collective-permute-start.8 = (bf16[64,2048]{1,0:T(8,128)(2,1)S(1)}, bf16[64,2048]{1,0:T(8,128)(2,1)S(1)}, u32[]{:S(2)}, u32[]{:S(2)}) collective-permute-start(bf16[64,2048]{1,0:T(8,128)(2,1)S(1)} %get-tuple-element.13), channel_id=1, source_target_pairs={{0,2},{1,3},{2,0},{3,1},{4,6},{5,7},{6,4},{7,5},{8,10},{9,11},{10,... | collective-permute-start | bytes 786440 | tf_op jit(solution)/shard_map/ppermute | solution.py:16
  27.1 18.8 %collective-permute-start.9 = (bf16[64,2048]{1,0:T(8,128)(2,1)S(1)}, bf16[64,2048]{1,0:T(8,128)(2,1)S(1)}, u32[]{:S(2)}, u32[]{:S(2)}) collective-permute-start(bf16[64,2048]{1,0:T(8,128)(2,1)S(1)} %get-tuple-element.14), channel_id=1, source_target_pairs={{0,3},{1,2},{2,1},{3,0},{4,7},{5,6},{6,5},{7,4},{8,11},{9,10},{10,... | collective-permute-start | bytes 786440 | tf_op jit(solution)/shard_map/ppermute | solution.py:16
  46.8 12.5 %collective-permute-start.12 = (bf16[64,2048]{1,0:T(8,128)(2,1)S(1)}, bf16[64,2048]{1,0:T(8,128)(2,1)S(1)}, u32[]{:S(2)}, u32[]{:S(2)}) collective-permute-start(bf16[64,2048]{1,0:T(8,128)(2,1)S(1)} %get-tuple-element.20.refs_0_), channel_id=1, source_target_pairs={{0,3},{1,2},{2,1},{3,0},{4,7},{5,6},{6,5},{7,4},{8,11},{9,10},{10,... | collective-permute-start | bytes 786440 | tf_op jit(solution)/shard_map/ppermute | solution.py:16
  49.3 26.3 %collective-permute-start.11 = (bf16[64,2048]{1,0:T(8,128)(2,1)S(1)}, bf16[64,2048]{1,0:T(8,128)(2,1)S(1)}, u32[]{:S(2)}, u32[]{:S(2)}) collective-permute-start(bf16[64,2048]{1,0:T(8,128)(2,1)S(1)} %get-tuple-element.20.refs_0_), channel_id=1, source_target_pairs={{0,2},{1,3},{2,0},{3,1},{4,6},{5,7},{6,4},{7,5},{8,10},{9,11},{10,... | collective-permute-start | bytes 786440 | tf_op jit(solution)/shard_map/ppermute | solution.py:16
  59.1 16.4 %collective-permute-start.10 = (bf16[64,2048]{1,0:T(8,128)(2,1)S(1)}, bf16[64,2048]{1,0:T(8,128)(2,1)S(1)}, u32[]{:S(2)}, u32[]{:S(2)}) collective-permute-start(bf16[64,2048]{1,0:T(8,128)(2,1)S(1)} %get-tuple-element.20.refs_0_), channel_id=1, source_target_pairs={{0,1},{1,0},{2,3},{3,2},{4,5},{5,4},{6,7},{7,6},{8,9},{9,8},{10,11... | collective-permute-start | bytes 786440 | tf_op jit(solution)/shard_map/ppermute | solution.py:16
  81.5 2.7 %collective-permute-start.13 = (f32[128,2048]{1,0:T(8,128)S(1)}, f32[128,2048]{1,0:T(8,128)S(1)}, u32[]{:S(2)}, u32[]{:S(2)}) collective-permute-start(f32[128,2048]{1,0:T(8,128)S(1)} %get-tuple-element.16), channel_id=1, source_target_pairs={{0,4},{4,0},{8,12},{12,8},{16,20},{20,16},{24,28},{28,24},{1,5},{5... | collective-permute-start | bytes 3145736 | tf_op jit(solution)/shard_map/ppermute | solution.py:16
  84.4 6.4 %collective-permute-start.14 = (bf16[32,2048]{1,0:T(8,128)(2,1)S(1)}, bf16[32,2048]{1,0:T(8,128)(2,1)S(1)}, u32[]{:S(2)}, u32[]{:S(2)}) collective-permute-start(bf16[32,2048]{1,0:T(8,128)(2,1)S(1)} %get-tuple-element.22), channel_id=1, source_target_pairs={{0,8},{4,12},{8,0},{12,4},{16,24},{20,28},{24,16},{28,20},{1,9},{5... | collective-permute-start | bytes 393224 | tf_op jit(solution)/shard_map/ppermute | solution.py:16
  85.9 7.9 %collective-permute-start.16 = (bf16[32,2048]{1,0:T(8,128)(2,1)S(1)}, bf16[32,2048]{1,0:T(8,128)(2,1)S(1)}, u32[]{:S(2)}, u32[]{:S(2)}) collective-permute-start(bf16[32,2048]{1,0:T(8,128)(2,1)S(1)} %get-tuple-element.23), channel_id=1, source_target_pairs={{0,24},{4,28},{8,16},{12,20},{16,8},{20,12},{24,0},{28,4},{1,25},{... | collective-permute-start | bytes 393224 | tf_op jit(solution)/shard_map/ppermute | solution.py:16
  87.4 7.8 %collective-permute-start.15 = (bf16[32,2048]{1,0:T(8,128)(2,1)S(1)}, bf16[32,2048]{1,0:T(8,128)(2,1)S(1)}, u32[]{:S(2)}, u32[]{:S(2)}) collective-permute-start(bf16[32,2048]{1,0:T(8,128)(2,1)S(1)} %get-tuple-element.24), channel_id=1, source_target_pairs={{0,16},{4,20},{8,24},{12,28},{16,0},{20,4},{24,8},{28,12},{1,17},{... | collective-permute-start | bytes 393224 | tf_op jit(solution)/shard_map/ppermute | solution.py:16

commit v2 on v0

v2 whole, which is shorter than its diff:
```python
import functools

import jax
import jax.numpy as jnp
from jax import lax
from jax.experimental import pallas as pl
from jax.experimental.pallas import tpu as pltpu
from jax.sharding import PartitionSpec as P

F32, BF16 = jnp.float32, jnp.bfloat16
VMEM_LIMIT = 28 * 2**20
STEP = 512


def exchange(value, axis, offset):
    size = lax.axis_size(axis)
    return lax.ppermute(value, axis, [(i, i ^ offset) for i in range(size)])


def relay(value, axis, hop):
    size = lax.axis_size(axis)
    return lax.ppermute(value, axis, [(i, i + hop) for i in range(size) if 0 <= i + hop < size])


def mask_kernel(mask_ref, green_ref, tiles, sems, *, block):
    rows, cols = tiles.shape
    copies = []
    for step in range(rows // STEP):
        at = pl.ds(step * STEP, STEP)
        copies.append(pltpu.make_async_copy(green_ref.at[at], tiles.at[at], sems.at[step]))
        copies[-1].start()
    for step, copy in enumerate(copies):
        copy.wait()
        for i in range(step * STEP // block, (step + 1) * STEP // block):
            for j in range(cols // block):

                @pl.when(mask_ref[i, j] == 0)
                def _():
                    tiles[i * block : (i + 1) * block, j * block : (j + 1) * block] = jnp.zeros((block, block), BF16)


def masked(green, mask):
    rows, cols = green.shape
    return pl.pallas_call(
        functools.partial(mask_kernel, block=rows // mask.shape[0]),
        in_specs=[pl.BlockSpec(memory_space=pltpu.SMEM), pl.BlockSpec(memory_space=pltpu.HBM)],
        out_specs=pl.BlockSpec(memory_space=pltpu.VMEM),
        out_shape=pltpu.VMEM((rows, cols), BF16),
        scratch_shapes=[pltpu.SemaphoreType.DMA((rows // STEP,))],
        compiler_params=pltpu.CompilerParams(vmem_limit_bytes=VMEM_LIMIT),
        cost_estimate=pl.CostEstimate(flops=0, bytes_accessed=2 * rows * cols, transcendentals=0),
        name="masked_tiles",
    )(mask, pltpu.with_memory_space_constraint(green, pltpu.HBM))


def sketch_kernel(where, tiles, *refs, offsets_row, offsets_col):
    blocks, outs = refs[: len(offsets_row)], refs[len(offsets_row) : -2]
    probes, total = refs[-2:]
    width = blocks[0].shape[0]
    share = outs[0].shape[0]
    for offset, ref in zip(offsets_row, blocks):
        start = pl.multiple_of((where[0] ^ offset) * width, width)
        probes[pl.ds(start, width), :] = ref[...]
    for step in range(tiles.shape[0] // STEP):
        at = slice(step * STEP, (step + 1) * STEP)
        total[:, at] = lax.dot_general(
            probes[...], tiles[at, :], (((1,), (1,)), ((), ())), preferred_element_type=F32
        )
    for offset, out in zip(offsets_col, outs):
        start = pl.multiple_of((where[1] ^ offset) * share, share)
        out[...] = total[pl.ds(start, share), :].astype(out.dtype)


def partial_sketch(where, tiles, blocks, offsets_row, offsets_col):
    rows, cols = tiles.shape
    width = blocks[0].shape[0] * len(blocks)
    share = width // len(offsets_col)
    vmem = pl.BlockSpec(memory_space=pltpu.VMEM)
    return pl.pallas_call(
        functools.partial(sketch_kernel, offsets_row=offsets_row, offsets_col=offsets_col),
        in_specs=[pl.BlockSpec(memory_space=pltpu.SMEM)] + [vmem] * (1 + len(blocks)),
        out_specs=[vmem] * len(offsets_col),
        out_shape=[jax.ShapeDtypeStruct((share, rows), F32 if offset == 0 else BF16) for offset in offsets_col],
        scratch_shapes=[pltpu.VMEM((width, cols), BF16), pltpu.VMEM((width, rows), F32)],
        compiler_params=pltpu.CompilerParams(vmem_limit_bytes=VMEM_LIMIT),
        cost_estimate=pl.CostEstimate(
            flops=2 * width * cols * rows, bytes_accessed=2 * rows * cols, transcendentals=0
        ),
        name="partial_sketch",
    )(where, tiles, *blocks)


def adjoint_kernel(where, tiles, *refs, hops, offsets_core):
    shares, outs = refs[: len(hops)], refs[len(hops) : -2]
    lowered, total = refs[-2:]
    share = shares[0].shape[0]
    width = outs[0].shape[0]
    for hop, ref in zip(hops, shares):
        origin = where[1] + hop

        @pl.when((origin >= 0) & (origin < lowered.shape[0] // share))
        def _():
            lowered[pl.ds(pl.multiple_of(origin * share, share), share), :] = ref[...]

    for step in range(tiles.shape[1] // STEP):
        at = slice(step * STEP, (step + 1) * STEP)
        total[:, at] = jnp.dot(lowered[...], tiles[:, at], preferred_element_type=F32)
    sibling = outs[-1]
    for k, offset in enumerate(offsets_core):
        start = pl.multiple_of((where[0] ^ offset) * width, width)
        outs[k][...] = total[pl.ds(start, width), :]
        start = pl.multiple_of((where[0] ^ 1 ^ offset) * width, width)
        sibling[k * width : (k + 1) * width, :] = total[pl.ds(start, width), :].astype(sibling.dtype)


def partial_adjoint(where, tiles, shares, hops, offsets_core, width):
    rows, cols = tiles.shape
    own = width // (2 * len(offsets_core))
    heights = [own] * len(offsets_core) + [own * len(offsets_core)]
    vmem = pl.BlockSpec(memory_space=pltpu.VMEM)
    return pl.pallas_call(
        functools.partial(adjoint_kernel, hops=hops, offsets_core=offsets_core),
        in_specs=[pl.BlockSpec(memory_space=pltpu.SMEM)] + [vmem] * (1 + len(shares)),
        out_specs=[vmem] * len(heights),
        out_shape=[jax.ShapeDtypeStruct((h, cols), F32) for h in heights],
        scratch_shapes=[pltpu.VMEM((width, rows), BF16), pltpu.VMEM((width, cols), F32)],
        compiler_params=pltpu.CompilerParams(vmem_limit_bytes=VMEM_LIMIT),
        cost_estimate=pl.CostEstimate(
            flops=2 * width * cols * rows, bytes_accessed=2 * rows * cols, transcendentals=0
        ),
        name="partial_adjoint",
    )(where, tiles, *shares)


def join(parts, group):
    length = parts[0].shape[1]
    return jnp.concatenate([p.reshape(-1, group, length) for p in parts], axis=1).reshape(-1, length)


def local(green, mask, probes):
    n_row, n_col = lax.axis_size("row"), lax.axis_size("col")
    where = jnp.stack([lax.axis_index("row"), lax.axis_index("col")]).astype(jnp.int32)
    own_width = probes.shape[1]
    chunks = 2 if own_width % 32 == 0 and n_row % n_col == 0 else 1
    piece = own_width // chunks
    width = piece * n_row
    offsets_col = list(range(n_col))
    offsets_core = list(range(0, n_row, 2))
    offsets_row = offsets_core + [offset ^ 1 for offset in offsets_core]

    tiles = masked(green, mask)

    blocks = []
    for chunk in range(chunks):
        own = probes.T[chunk * piece : (chunk + 1) * piece]
        held = [own] + [exchange(own, "row", offset) for offset in offsets_core[1:]]
        blocks.append(held + [exchange(block, "row", 1) for block in held])

    sketches, adjoints = [], []
    for chunk in range(chunks):
        parts = partial_sketch(where, tiles, blocks[chunk], offsets_row, offsets_col)
        total = parts[0]
        for offset in offsets_col[1:]:
            total = total + exchange(parts[offset], "col", offset).astype(F32)
        sketches.append(total)

        shares, hops = [total.astype(BF16)], [0]
        up = down = shares[0]
        for hop in range(1, n_col):
            up, down = relay(up, "col", 1), relay(down, "col", -1)
            shares += [up, down]
            hops += [-hop, hop]

        *mine, others = partial_adjoint(where, tiles, shares, hops, offsets_core, width)
        others = exchange(others, "row", 1)
        pairs = [m + others[k * piece : (k + 1) * piece] for k, m in enumerate(mine)]
        adjoint = pairs[0]
        for offset, pair in zip(offsets_core[1:], pairs[1:]):
            adjoint = adjoint + exchange(pair.astype(BF16), "row", offset).astype(F32)
        adjoints.append(adjoint)
    return join(sketches, piece).T, join(adjoints, piece).T


def solution(mesh):
    in_specs = (P("row", "col"), P("row", "col"), P("col", "row"))
    out_specs = (P("row", "col"), P("col", "row"))
    return jax.shard_map(local, mesh=mesh, in_specs=in_specs, out_specs=out_specs, check_vma=False)
```

time: 185 us -> 103 us (0.56)
  waiting for transfers between devices: 129 us -> 26.5 us
  starting transfers between devices: 0.12 us -> 55.9 us
  Pallas kernels: 0 us -> 15.2 us
  matrix products: 15.1 us -> 0 us
  local copies, waits for them, and re-layouts: 15.6 us -> 1.57 us
  between operations: 13.8 us -> 0.94 us
  other arithmetic: 11.3 us -> 1.92 us
    psum x1 -> x0, waiting for transfers between devices: 86.6 us -> none  [local(): summed = lax.psum(partial_sketch, 'col')]
    ppermute x0 -> x40, starting transfers between devices: none -> 55.9 us  [the longest x12 29.2 us: relay(): lax.ppermute(value, axis, [(i, i + hop) for i in range(size) if 0 <= i +...]
    reduce_scatter x1 -> x0, waiting for transfers between devices: 38.9 us -> none  [local(): adjoint = lax.psum_scatter(term, 'row', scatter_dimension=1, tiled=True)]
    ppermute x0 -> x40, waiting for transfers between devices: none -> 26.5 us  [the longest x28 20 us: exchange(): return lax.ppermute(value, axis, [(i, i ^ offset) for i in range(size)])]
    pallas_call x0 -> x5, Pallas kernels: none -> 15.2 us  [the longest x2 7 us: partial_sketch(): pl.pallas_call(functools.partial(sketch_kernel, offsets_row=offsets_row,...]
    dot_general x2 -> x0, matrix products: 15.1 us -> none  [the longest x1 7.8 us: local(): lax.dot_general(tiles, summed.astype(jnp.bfloat16), (((0,), (0,)), ((), (...]
    unnamed x4 -> x2, local copies, waits for them, and re-layouts: 11.4 us -> 0.69 us
    mul x1 -> x0, other arithmetic: 10.6 us -> none  [local(): shaped * mask.astype(jnp.bfloat16)[:, None, :, None]]
  transfers between devices with their start and end apart: 3 -> 40, of which waited for: 3 -> 10; matrix products, arithmetic and copies ran while one was open for 15% -> 1% of each run, Pallas kernels for 0% -> 15%
where the time goes in v2:
time: 103 us; the launch traced here: 102 us
  starting transfers between devices  55.9 us (54%)
  waiting for transfers between devices  26.5 us (26%)
  Pallas kernels  15.2 us (15%)
  other arithmetic  1.92 us (2%)
  local copies, waits for them, and re-layouts  1.57 us (2%)
    ppermute x12, starting transfers between devices, relay(): lax.ppermute(value, axis, [(i, i + hop) for i in range(size) if 0 <= i +...  29.2 us
    ppermute x28, starting transfers between devices, exchange(): return lax.ppermute(value, axis, [(i, i ^ offset) for i in range(size)])  26.7 us
    ppermute x28, waiting for transfers between devices, exchange(): return lax.ppermute(value, axis, [(i, i ^ offset) for i in range(size)])  20 us
    pallas_call x2, Pallas kernels, partial_sketch(): pl.pallas_call(functools.partial(sketch_kernel, offsets_row=offsets_row,...  7 us
    ppermute x12, waiting for transfers between devices, relay(): lax.ppermute(value, axis, [(i, i + hop) for i in range(size) if 0 <= i +...  6.48 us
    pallas_call x1, Pallas kernels, masked(): pl.pallas_call(functools.partial(mask_kernel, block=rows // mask.shape[0]...  4.18 us
    pallas_call x2, Pallas kernels, partial_adjoint(): pl.pallas_call(functools.partial(adjoint_kernel, hops=hops, offsets_core=...  4.04 us
  transfers between devices with their start and end apart: 40, of which 10 were waited for; matrix products, arithmetic and copies ran while one was open for 1% of the time, Pallas kernels for 15%

profile of v2, /device:TPU:0, one launch (start us, length us, event | category | flops | bytes accessed | tf_op | source)
XLA Modules:
  0.0 102.0 jit_solution(15112347829628739213)
XLA Ops:
  1.5 3.0 %collective-permute-start.10 = (bf16[16,2048]{1,0:T(8,128)(2,1)S(1)}, bf16[16,2048]{1,0:T(8,128)(2,1)S(1)}, u32[]{:S(2)}, u32[]{:S(2)}) collective-permute-start(bf16[16,2048]{1,0:T(8,128)(2,1)S(1)} %get-tuple-element.49.refs_0_), channel_id=1, source_target_pairs={{0,8},{4,12},{8,0},{12,4},{16,24},{20,28},{24,16},{28,20},{1,9},{5... | collective-permute-start | bytes 196616 | tf_op jit(solution)/shard_map/ppermute | solution.py:17
  4.5 1.5 %collective-permute-start.11 = (bf16[16,2048]{1,0:T(8,128)(2,1)S(1)}, bf16[16,2048]{1,0:T(8,128)(2,1)S(1)}, u32[]{:S(2)}, u32[]{:S(2)}) collective-permute-start(bf16[16,2048]{1,0:T(8,128)(2,1)S(1)} %get-tuple-element.49.refs_0_), channel_id=1, source_target_pairs={{0,16},{4,20},{8,24},{12,28},{16,0},{20,4},{24,8},{28,12},{1,17},{... | collective-permute-start | bytes 196616 | tf_op jit(solution)/shard_map/ppermute | solution.py:17
  6.1 1.9 %collective-permute-start = (bf16[16,2048]{1,0:T(8,128)(2,1)S(1)}, bf16[16,2048]{1,0:T(8,128)(2,1)S(1)}, u32[]{:S(2)}, u32[]{:S(2)}) collective-permute-start(bf16[16,2048]{1,0:T(8,128)(2,1)S(1)} %get-tuple-element.48.refs_0_), channel_id=1, source_target_pairs={{0,8},{4,12},{8,0},{12,4},{16,24},{20,28},{24,16},{28,20},{1,9},{5... | collective-permute-start | bytes 196616 | tf_op jit(solution)/shard_map/ppermute | solution.py:17
  8.7 4.2 %masked_tiles.1.tiles = bf16[2048,2048]{1,0:T(8,128)(2,1)S(1)} custom-call(s32[8,8]{1,0:T(8,128)S(1)} %copy-done, bf16[2048,2048]{1,0:T(8,128)(2,1)} %green_ref.1), custom_call_target="tpu_custom_call" | custom-call | bytes 8388608 | tf_op jit(solution)/shard_map/masked_tiles/pallas_call | solution.py:44
  12.9 1.5 %collective-permute-start.1 = (bf16[16,2048]{1,0:T(8,128)(2,1)S(1)}, bf16[16,2048]{1,0:T(8,128)(2,1)S(1)}, u32[]{:S(2)}, u32[]{:S(2)}) collective-permute-start(bf16[16,2048]{1,0:T(8,128)(2,1)S(1)} %get-tuple-element.48.refs_0_), channel_id=1, source_target_pairs={{0,16},{4,20},{8,24},{12,28},{16,0},{20,4},{24,8},{28,12},{1,17},{... | collective-permute-start | bytes 196616 | tf_op jit(solution)/shard_map/ppermute | solution.py:17
  15.2 2.1 %collective-permute-done.1.refs_2_ = bf16[16,2048]{1,0:T(8,128)(2,1)S(1)} collective-permute-done((bf16[16,2048]{1,0:T(8,128)(2,1)S(1)}, bf16[16,2048]{1,0:T(8,128)(2,1)S(1)}, u32[]{:S(2)}, u32[]{:S(2)}) %collective-permute-start.1) | collective-permute-done | bytes 65568 | tf_op jit(solution)/shard_map/ppermute | solution.py:17
  17.2 2.3 %collective-permute-done.2.refs_3_ = bf16[16,2048]{1,0:T(8,128)(2,1)S(1)} collective-permute-done((bf16[16,2048]{1,0:T(8,128)(2,1)S(1)}, bf16[16,2048]{1,0:T(8,128)(2,1)S(1)}, u32[]{:S(2)}, u32[]{:S(2)}) %collective-permute-start.2) | collective-permute-done | bytes 65568 | tf_op jit(solution)/shard_map/ppermute | solution.py:17
  20.2 3.5 %partial_sketch.3 = (f32[32,2048]{1,0:T(8,128)S(1)}, bf16[32,2048]{1,0:T(8,128)(2,1)S(1)}, bf16[32,2048]{1,0:T(8,128)(2,1)S(1)}, bf16[32,2048]{1,0:T(8,128)(2,1)S(1)}) custom-call(s32[2]{0:T(128)S(1)} %pad_add_fusion.where, bf16[2048,2048]{1,0:T(8,128)(2,1)S(1)} %masked_tiles.1.tiles, bf16[16,2048]{1,0:T(8,128)(2,1)S(1)} %get-tuple-element.49.refs_0_, ...), custom_call_target="tpu_custom_call" | custom-call | flops 1073741824 | bytes 8388608 | tf_op jit(solution)/shard_map/partial_sketch/pallas_call | solution.py:79
  23.7 3.7 %collective-permute-start.19 = (bf16[32,2048]{1,0:T(8,128)(2,1)S(1)}, bf16[32,2048]{1,0:T(8,128)(2,1)S(1)}, u32[]{:S(2)}, u32[]{:S(2)}) collective-permute-start(bf16[32,2048]{1,0:T(8,128)(2,1)S(1)} %get-tuple-element.27), channel_id=1, source_target_pairs={{0,3},{1,2},{2,1},{3,0},{4,7},{5,6},{6,5},{7,4},{8,11},{9,10},{10,... | collective-permute-start | bytes 393224 | tf_op jit(solution)/shard_map/ppermute | solution.py:17
  28.1 3.5 %partial_sketch.2 = (f32[32,2048]{1,0:T(8,128)S(1)}, bf16[32,2048]{1,0:T(8,128)(2,1)S(1)}, bf16[32,2048]{1,0:T(8,128)(2,1)S(1)}, bf16[32,2048]{1,0:T(8,128)(2,1)S(1)}) custom-call(s32[2]{0:T(128)S(1)} %pad_add_fusion.where, bf16[2048,2048]{1,0:T(8,128)(2,1)S(1)} %masked_tiles.1.tiles, bf16[16,2048]{1,0:T(8,128)(2,1)S(1)} %get-tuple-element.48.refs_0_, ...), custom_call_target="tpu_custom_call" | custom-call | flops 1073741824 | bytes 8388608 | tf_op jit(solution)/shard_map/partial_sketch/pallas_call | solution.py:79
  31.9 7.1 %collective-permute-done.18 = bf16[32,2048]{1,0:T(8,128)(2,1)S(1)} collective-permute-done((bf16[32,2048]{1,0:T(8,128)(2,1)S(1)}, bf16[32,2048]{1,0:T(8,128)(2,1)S(1)}, u32[]{:S(2)}, u32[]{:S(2)}) %collective-permute-start.18) | collective-permute-done | bytes 131104 | tf_op jit(solution)/shard_map/ppermute | solution.py:17
  39.1 1.8 %collective-permute-start.30 = (bf16[32,2048]{1,0:T(8,128)(2,1)S(1)}, bf16[32,2048]{1,0:T(8,128)(2,1)S(1)}, u32[]{:S(2)}, u32[]{:S(2)}) collective-permute-start(bf16[32,2048]{1,0:T(8,128)(2,1)S(1)} %get-tuple-element.40.refs_0_), channel_id=1, source_target_pairs={{0,1},{1,2},{2,3},{4,5},{5,6},{6,7},{8,9},{9,10},{10,11},{12,13},{... | collective-permute-start | bytes 393224 | tf_op jit(solution)/shard_map/ppermute | solution.py:22
  40.9 2.1 %collective-permute-start.9 = (bf16[32,2048]{1,0:T(8,128)(2,1)S(1)}, bf16[32,2048]{1,0:T(8,128)(2,1)S(1)}, u32[]{:S(2)}, u32[]{:S(2)}) collective-permute-start(bf16[32,2048]{1,0:T(8,128)(2,1)S(1)} %get-tuple-element.23), channel_id=1, source_target_pairs={{0,3},{1,2},{2,1},{3,0},{4,7},{5,6},{6,5},{7,4},{8,11},{9,10},{10,... | collective-permute-start | bytes 393224 | tf_op jit(solution)/shard_map/ppermute | solution.py:17
  44.2 3.9 %collective-permute-start.8 = (bf16[32,2048]{1,0:T(8,128)(2,1)S(1)}, bf16[32,2048]{1,0:T(8,128)(2,1)S(1)}, u32[]{:S(2)}, u32[]{:S(2)}) collective-permute-start(bf16[32,2048]{1,0:T(8,128)(2,1)S(1)} %get-tuple-element.22), channel_id=1, source_target_pairs={{0,2},{1,3},{2,0},{3,1},{4,6},{5,7},{6,4},{7,5},{8,10},{9,11},{10,... | collective-permute-start | bytes 393224 | tf_op jit(solution)/shard_map/ppermute | solution.py:17
  48.1 3.9 %collective-permute-start.32 = (bf16[32,2048]{1,0:T(8,128)(2,1)S(1)}, bf16[32,2048]{1,0:T(8,128)(2,1)S(1)}, u32[]{:S(2)}, u32[]{:S(2)}) collective-permute-start(bf16[32,2048]{1,0:T(8,128)(2,1)S(1)} %collective-permute-done.30.refs_1_), channel_id=1, source_target_pairs={{0,1},{1,2},{2,3},{4,5},{5,6},{6,7},{8,9},{9,10},{10,11},{12,13},{... | collective-permute-start | bytes 393224 | tf_op jit(solution)/shard_map/ppermute | solution.py:22
  52.1 1.3 %collective-permute-start.33 = (bf16[32,2048]{1,0:T(8,128)(2,1)S(1)}, bf16[32,2048]{1,0:T(8,128)(2,1)S(1)}, u32[]{:S(2)}, u32[]{:S(2)}) collective-permute-start(bf16[32,2048]{1,0:T(8,128)(2,1)S(1)} %collective-permute-done.31.refs_2_), channel_id=1, source_target_pairs={{1,0},{2,1},{3,2},{5,4},{6,5},{7,6},{9,8},{10,9},{11,10},{13,12},{... | collective-permute-start | bytes 393224 | tf_op jit(solution)/shard_map/ppermute | solution.py:22
  53.4 5.0 %collective-permute-done.8 = bf16[32,2048]{1,0:T(8,128)(2,1)S(1)} collective-permute-done((bf16[32,2048]{1,0:T(8,128)(2,1)S(1)}, bf16[32,2048]{1,0:T(8,128)(2,1)S(1)}, u32[]{:S(2)}, u32[]{:S(2)}) %collective-permute-start.8) | collective-permute-done | bytes 131104 | tf_op jit(solution)/shard_map/ppermute | solution.py:17
  58.4 2.1 %collective-permute-start.20 = (bf16[32,2048]{1,0:T(8,128)(2,1)S(1)}, bf16[32,2048]{1,0:T(8,128)(2,1)S(1)}, u32[]{:S(2)}, u32[]{:S(2)}) collective-permute-start(bf16[32,2048]{1,0:T(8,128)(2,1)S(1)} %get-tuple-element.38.refs_0_), channel_id=1, source_target_pairs={{0,1},{1,2},{2,3},{4,5},{5,6},{6,7},{8,9},{9,10},{10,11},{12,13},{... | collective-permute-start | bytes 393224 | tf_op jit(solution)/shard_map/ppermute | solution.py:22
  60.6 1.3 %collective-permute-start.21 = (bf16[32,2048]{1,0:T(8,128)(2,1)S(1)}, bf16[32,2048]{1,0:T(8,128)(2,1)S(1)}, u32[]{:S(2)}, u32[]{:S(2)}) collective-permute-start(bf16[32,2048]{1,0:T(8,128)(2,1)S(1)} %get-tuple-element.38.refs_0_), channel_id=1, source_target_pairs={{1,0},{2,1},{3,2},{5,4},{6,5},{7,6},{9,8},{10,9},{11,10},{13,12},{... | collective-permute-start | bytes 393224 | tf_op jit(solution)/shard_map/ppermute | solution.py:22
  61.9 4.6 %collective-permute-start.34 = (bf16[32,2048]{1,0:T(8,128)(2,1)S(1)}, bf16[32,2048]{1,0:T(8,128)(2,1)S(1)}, u32[]{:S(2)}, u32[]{:S(2)}) collective-permute-start(bf16[32,2048]{1,0:T(8,128)(2,1)S(1)} %collective-permute-done.32.refs_3_), channel_id=1, source_target_pairs={{0,1},{1,2},{2,3},{4,5},{5,6},{6,7},{8,9},{9,10},{10,11},{12,13},{... | collective-permute-start | bytes 393224 | tf_op jit(solution)/shard_map/ppermute | solution.py:22
  66.5 1.3 %collective-permute-start.35 = (bf16[32,2048]{1,0:T(8,128)(2,1)S(1)}, bf16[32,2048]{1,0:T(8,128)(2,1)S(1)}, u32[]{:S(2)}, u32[]{:S(2)}) collective-permute-start(bf16[32,2048]{1,0:T(8,128)(2,1)S(1)} %collective-permute-done.33.refs_4_), channel_id=1, source_target_pairs={{1,0},{2,1},{3,2},{5,4},{6,5},{7,6},{9,8},{10,9},{11,10},{13,12},{... | collective-permute-start | bytes 393224 | tf_op jit(solution)/shard_map/ppermute | solution.py:22
  67.8 4.6 %collective-permute-start.22 = (bf16[32,2048]{1,0:T(8,128)(2,1)S(1)}, bf16[32,2048]{1,0:T(8,128)(2,1)S(1)}, u32[]{:S(2)}, u32[]{:S(2)}) collective-permute-start(bf16[32,2048]{1,0:T(8,128)(2,1)S(1)} %collective-permute-done.20.refs_1_), channel_id=1, source_target_pairs={{0,1},{1,2},{2,3},{4,5},{5,6},{6,7},{8,9},{9,10},{10,11},{12,13},{... | collective-permute-start | bytes 393224 | tf_op jit(solution)/shard_map/ppermute | solution.py:22
  72.3 1.3 %collective-permute-start.23 = (bf16[32,2048]{1,0:T(8,128)(2,1)S(1)}, bf16[32,2048]{1,0:T(8,128)(2,1)S(1)}, u32[]{:S(2)}, u32[]{:S(2)}) collective-permute-start(bf16[32,2048]{1,0:T(8,128)(2,1)S(1)} %collective-permute-done.21.refs_2_), channel_id=1, source_target_pairs={{1,0},{2,1},{3,2},{5,4},{6,5},{7,6},{9,8},{10,9},{11,10},{13,12},{... | collective-permute-start | bytes 393224 | tf_op jit(solution)/shard_map/ppermute | solution.py:22
  73.7 2.0 %partial_adjoint.3 = (f32[16,2048]{1,0:T(8,128)S(1)}, f32[16,2048]{1,0:T(8,128)S(1)}, f32[16,2048]{1,0:T(8,128)S(1)}, f32[16,2048]{1,0:T(8,128)S(1)}, f32[64,2048]{1,0:T(8,128)S(1)}) custom-call(s32[2]{0:T(128)S(1)} %pad_add_fusion.where, bf16[2048,2048]{1,0:T(8,128)(2,1)S(1)} %masked_tiles.1.tiles, bf16[32,2048]{1,0:T(8,128)(2,1)S(1)} %get-tuple-element.40.refs_0_, ...), custom_call_target="tpu_custom_call" | custom-call | flops 1073741824 | bytes 8388608 | tf_op jit(solution)/shard_map/partial_adjoint/pallas_call | solution.py:121
  75.8 4.6 %collective-permute-start.24 = (bf16[32,2048]{1,0:T(8,128)(2,1)S(1)}, bf16[32,2048]{1,0:T(8,128)(2,1)S(1)}, u32[]{:S(2)}, u32[]{:S(2)}) collective-permute-start(bf16[32,2048]{1,0:T(8,128)(2,1)S(1)} %collective-permute-done.22.refs_3_), channel_id=1, source_target_pairs={{0,1},{1,2},{2,3},{4,5},{5,6},{6,7},{8,9},{9,10},{10,11},{12,13},{... | collective-permute-start | bytes 393224 | tf_op jit(solution)/shard_map/ppermute | solution.py:22
  81.7 2.1 %collective-permute-done.24.refs_5_ = bf16[32,2048]{1,0:T(8,128)(2,1)S(1)} collective-permute-done((bf16[32,2048]{1,0:T(8,128)(2,1)S(1)}, bf16[32,2048]{1,0:T(8,128)(2,1)S(1)}, u32[]{:S(2)}, u32[]{:S(2)}) %collective-permute-start.24) | collective-permute-done | bytes 131104 | tf_op jit(solution)/shard_map/ppermute | solution.py:22
  83.7 4.4 %collective-permute-done.25.refs_6_ = bf16[32,2048]{1,0:T(8,128)(2,1)S(1)} collective-permute-done((bf16[32,2048]{1,0:T(8,128)(2,1)S(1)}, bf16[32,2048]{1,0:T(8,128)(2,1)S(1)}, u32[]{:S(2)}, u32[]{:S(2)}) %collective-permute-start.25) | collective-permute-done | bytes 131104 | tf_op jit(solution)/shard_map/ppermute | solution.py:22
  88.1 2.0 %partial_adjoint.2 = (f32[16,2048]{1,0:T(8,128)S(1)}, f32[16,2048]{1,0:T(8,128)S(1)}, f32[16,2048]{1,0:T(8,128)S(1)}, f32[16,2048]{1,0:T(8,128)S(1)}, f32[64,2048]{1,0:T(8,128)S(1)}) custom-call(s32[2]{0:T(128)S(1)} %pad_add_fusion.where, bf16[2048,2048]{1,0:T(8,128)(2,1)S(1)} %masked_tiles.1.tiles, bf16[32,2048]{1,0:T(8,128)(2,1)S(1)} %get-tuple-element.38.refs_0_, ...), custom_call_target="tpu_custom_call" | custom-call | flops 1073741824 | bytes 8388608 | tf_op jit(solution)/shard_map/partial_adjoint/pallas_call | solution.py:121
  91.8 1.3 %collective-permute-start.38 = (bf16[16,2048]{1,0:T(8,128)(2,1)S(1)}, bf16[16,2048]{1,0:T(8,128)(2,1)S(1)}, u32[]{:S(2)}, u32[]{:S(2)}) collective-permute-start(bf16[16,2048]{1,0:T(8,128)(2,1)S(1)} %get-tuple-element.47), channel_id=1, source_target_pairs={{0,16},{4,20},{8,24},{12,28},{16,0},{20,4},{24,8},{28,12},{1,17},{... | collective-permute-start | bytes 196616 | tf_op jit(solution)/shard_map/ppermute | solution.py:17
  93.2 1.5 %collective-permute-start.37 = (bf16[16,2048]{1,0:T(8,128)(2,1)S(1)}, bf16[16,2048]{1,0:T(8,128)(2,1)S(1)}, u32[]{:S(2)}, u32[]{:S(2)}) collective-permute-start(bf16[16,2048]{1,0:T(8,128)(2,1)S(1)} %get-tuple-element.45), channel_id=1, source_target_pairs={{0,8},{4,12},{8,0},{12,4},{16,24},{20,28},{24,16},{28,20},{1,9},{5... | collective-permute-start | bytes 196616 | tf_op jit(solution)/shard_map/ppermute | solution.py:17
  95.4 1.3 %collective-permute-start.28 = (bf16[16,2048]{1,0:T(8,128)(2,1)S(1)}, bf16[16,2048]{1,0:T(8,128)(2,1)S(1)}, u32[]{:S(2)}, u32[]{:S(2)}) collective-permute-start(bf16[16,2048]{1,0:T(8,128)(2,1)S(1)} %get-tuple-element.44), channel_id=1, source_target_pairs={{0,16},{4,20},{8,24},{12,28},{16,0},{20,4},{24,8},{28,12},{1,17},{... | collective-permute-start | bytes 196616 | tf_op jit(solution)/shard_map/ppermute | solution.py:17
  98.3 2.2 %collective-permute-done.29 = bf16[16,2048]{1,0:T(8,128)(2,1)S(1)} collective-permute-done((bf16[16,2048]{1,0:T(8,128)(2,1)S(1)}, bf16[16,2048]{1,0:T(8,128)(2,1)S(1)}, u32[]{:S(2)}, u32[]{:S(2)}) %collective-permute-start.29) | collective-permute-done | bytes 65568 | tf_op jit(solution)/shard_map/ppermute | solution.py:17
  (65 shorter events, 12.3 us)
Async XLA Ops:
  1.5 11.4 %collective-permute-start.10 = (bf16[16,2048]{1,0:T(8,128)(2,1)S(1)}, bf16[16,2048]{1,0:T(8,128)(2,1)S(1)}, u32[]{:S(2)}, u32[]{:S(2)}) collective-permute-start(bf16[16,2048]{1,0:T(8,128)(2,1)S(1)} %get-tuple-element.49.refs_0_), channel_id=1, source_target_pairs={{0,8},{4,12},{8,0},{12,4},{16,24},{20,28},{24,16},{28,20},{1,9},{5... | collective-permute-start | bytes 196616 | tf_op jit(solution)/shard_map/ppermute | solution.py:17
  4.5 9.9 %collective-permute-start.11 = (bf16[16,2048]{1,0:T(8,128)(2,1)S(1)}, bf16[16,2048]{1,0:T(8,128)(2,1)S(1)}, u32[]{:S(2)}, u32[]{:S(2)}) collective-permute-start(bf16[16,2048]{1,0:T(8,128)(2,1)S(1)} %get-tuple-element.49.refs_0_), channel_id=1, source_target_pairs={{0,16},{4,20},{8,24},{12,28},{16,0},{20,4},{24,8},{28,12},{1,17},{... | collective-permute-start | bytes 196616 | tf_op jit(solution)/shard_map/ppermute | solution.py:17
  6.0 8.4 %collective-permute-start.12 = (bf16[16,2048]{1,0:T(8,128)(2,1)S(1)}, bf16[16,2048]{1,0:T(8,128)(2,1)S(1)}, u32[]{:S(2)}, u32[]{:S(2)}) collective-permute-start(bf16[16,2048]{1,0:T(8,128)(2,1)S(1)} %get-tuple-element.49.refs_0_), channel_id=1, source_target_pairs={{0,24},{4,28},{8,16},{12,20},{16,8},{20,12},{24,0},{28,4},{1,25},{... | collective-permute-start | bytes 196616 | tf_op jit(solution)/shard_map/ppermute | solution.py:17
  6.1 8.4 %collective-permute-start.13 = (bf16[16,2048]{1,0:T(8,128)(2,1)S(1)}, bf16[16,2048]{1,0:T(8,128)(2,1)S(1)}, u32[]{:S(2)}, u32[]{:S(2)}) collective-permute-start(bf16[16,2048]{1,0:T(8,128)(2,1)S(1)} %get-tuple-element.49.refs_0_), channel_id=1, source_target_pairs={{0,4},{4,0},{8,12},{12,8},{16,20},{20,16},{24,28},{28,24},{1,5},{5... | collective-permute-start | bytes 196616 | tf_op jit(solution)/shard_map/ppermute | solution.py:17
  6.1 8.9 %collective-permute-start = (bf16[16,2048]{1,0:T(8,128)(2,1)S(1)}, bf16[16,2048]{1,0:T(8,128)(2,1)S(1)}, u32[]{:S(2)}, u32[]{:S(2)}) collective-permute-start(bf16[16,2048]{1,0:T(8,128)(2,1)S(1)} %get-tuple-element.48.refs_0_), channel_id=1, source_target_pairs={{0,8},{4,12},{8,0},{12,4},{16,24},{20,28},{24,16},{28,20},{1,9},{5... | collective-permute-start | bytes 196616 | tf_op jit(solution)/shard_map/ppermute | solution.py:17
  14.5 5.6 %collective-permute-start.15 = (bf16[16,2048]{1,0:T(8,128)(2,1)S(1)}, bf16[16,2048]{1,0:T(8,128)(2,1)S(1)}, u32[]{:S(2)}, u32[]{:S(2)}) collective-permute-start(bf16[16,2048]{1,0:T(8,128)(2,1)S(1)} %collective-permute-done.11.refs_2_), channel_id=1, source_target_pairs={{0,4},{4,0},{8,12},{12,8},{16,20},{20,16},{24,28},{28,24},{1,5},{5... | collective-permute-start | bytes 196616 | tf_op jit(solution)/shard_map/ppermute | solution.py:17
  17.2 10.1 %collective-permute-start.3 = (bf16[16,2048]{1,0:T(8,128)(2,1)S(1)}, bf16[16,2048]{1,0:T(8,128)(2,1)S(1)}, u32[]{:S(2)}, u32[]{:S(2)}) collective-permute-start(bf16[16,2048]{1,0:T(8,128)(2,1)S(1)} %get-tuple-element.48.refs_0_), channel_id=1, source_target_pairs={{0,4},{4,0},{8,12},{12,8},{16,20},{20,16},{24,28},{28,24},{1,5},{5... | collective-permute-start | bytes 196616 | tf_op jit(solution)/shard_map/ppermute | solution.py:17
  19.6 7.8 %collective-permute-start.4 = (bf16[16,2048]{1,0:T(8,128)(2,1)S(1)}, bf16[16,2048]{1,0:T(8,128)(2,1)S(1)}, u32[]{:S(2)}, u32[]{:S(2)}) collective-permute-start(bf16[16,2048]{1,0:T(8,128)(2,1)S(1)} %collective-permute-done.refs_1_), channel_id=1, source_target_pairs={{0,4},{4,0},{8,12},{12,8},{16,20},{20,16},{24,28},{28,24},{1,5},{5... | collective-permute-start | bytes 196616 | tf_op jit(solution)/shard_map/ppermute | solution.py:17
  19.6 8.6 %collective-permute-start.5 = (bf16[16,2048]{1,0:T(8,128)(2,1)S(1)}, bf16[16,2048]{1,0:T(8,128)(2,1)S(1)}, u32[]{:S(2)}, u32[]{:S(2)}) collective-permute-start(bf16[16,2048]{1,0:T(8,128)(2,1)S(1)} %collective-permute-done.1.refs_2_), channel_id=1, source_target_pairs={{0,4},{4,0},{8,12},{12,8},{16,20},{20,16},{24,28},{28,24},{1,5},{5... | collective-permute-start | bytes 196616 | tf_op jit(solution)/shard_map/ppermute | solution.py:17
  20.1 8.1 %collective-permute-start.6 = (bf16[16,2048]{1,0:T(8,128)(2,1)S(1)}, bf16[16,2048]{1,0:T(8,128)(2,1)S(1)}, u32[]{:S(2)}, u32[]{:S(2)}) collective-permute-start(bf16[16,2048]{1,0:T(8,128)(2,1)S(1)} %collective-permute-done.2.refs_3_), channel_id=1, source_target_pairs={{0,4},{4,0},{8,12},{12,8},{16,20},{20,16},{24,28},{28,24},{1,5},{5... | collective-permute-start | bytes 196616 | tf_op jit(solution)/shard_map/ppermute | solution.py:17
  23.7 8.3 %collective-permute-start.19 = (bf16[32,2048]{1,0:T(8,128)(2,1)S(1)}, bf16[32,2048]{1,0:T(8,128)(2,1)S(1)}, u32[]{:S(2)}, u32[]{:S(2)}) collective-permute-start(bf16[32,2048]{1,0:T(8,128)(2,1)S(1)} %get-tuple-element.27), channel_id=1, source_target_pairs={{0,3},{1,2},{2,1},{3,0},{4,7},{5,6},{6,5},{7,4},{8,11},{9,10},{10,... | collective-permute-start | bytes 393224 | tf_op jit(solution)/shard_map/ppermute | solution.py:17
  27.3 11.7 %collective-permute-start.18 = (bf16[32,2048]{1,0:T(8,128)(2,1)S(1)}, bf16[32,2048]{1,0:T(8,128)(2,1)S(1)}, u32[]{:S(2)}, u32[]{:S(2)}) collective-permute-start(bf16[32,2048]{1,0:T(8,128)(2,1)S(1)} %get-tuple-element.26), channel_id=1, source_target_pairs={{0,2},{1,3},{2,0},{3,1},{4,6},{5,7},{6,4},{7,5},{8,10},{9,11},{10,... | collective-permute-start | bytes 393224 | tf_op jit(solution)/shard_map/ppermute | solution.py:17
  27.4 11.7 %collective-permute-start.17 = (bf16[32,2048]{1,0:T(8,128)(2,1)S(1)}, bf16[32,2048]{1,0:T(8,128)(2,1)S(1)}, u32[]{:S(2)}, u32[]{:S(2)}) collective-permute-start(bf16[32,2048]{1,0:T(8,128)(2,1)S(1)} %get-tuple-element.25), channel_id=1, source_target_pairs={{0,1},{1,0},{2,3},{3,2},{4,5},{5,4},{6,7},{7,6},{8,9},{9,8},{10,11... | collective-permute-start | bytes 393224 | tf_op jit(solution)/shard_map/ppermute | solution.py:17
  39.1 9.0 %collective-permute-start.30 = (bf16[32,2048]{1,0:T(8,128)(2,1)S(1)}, bf16[32,2048]{1,0:T(8,128)(2,1)S(1)}, u32[]{:S(2)}, u32[]{:S(2)}) collective-permute-start(bf16[32,2048]{1,0:T(8,128)(2,1)S(1)} %get-tuple-element.40.refs_0_), channel_id=1, source_target_pairs={{0,1},{1,2},{2,3},{4,5},{5,6},{6,7},{8,9},{9,10},{10,11},{12,13},{... | collective-permute-start | bytes 393224 | tf_op jit(solution)/shard_map/ppermute | solution.py:22
  40.9 12.5 %collective-permute-start.9 = (bf16[32,2048]{1,0:T(8,128)(2,1)S(1)}, bf16[32,2048]{1,0:T(8,128)(2,1)S(1)}, u32[]{:S(2)}, u32[]{:S(2)}) collective-permute-start(bf16[32,2048]{1,0:T(8,128)(2,1)S(1)} %get-tuple-element.23), channel_id=1, source_target_pairs={{0,3},{1,2},{2,1},{3,0},{4,7},{5,6},{6,5},{7,4},{8,11},{9,10},{10,... | collective-permute-start | bytes 393224 | tf_op jit(solution)/shard_map/ppermute | solution.py:17
  42.9 9.1 %collective-permute-start.31 = (bf16[32,2048]{1,0:T(8,128)(2,1)S(1)}, bf16[32,2048]{1,0:T(8,128)(2,1)S(1)}, u32[]{:S(2)}, u32[]{:S(2)}) collective-permute-start(bf16[32,2048]{1,0:T(8,128)(2,1)S(1)} %get-tuple-element.40.refs_0_), channel_id=1, source_target_pairs={{1,0},{2,1},{3,2},{5,4},{6,5},{7,6},{9,8},{10,9},{11,10},{13,12},{... | collective-permute-start | bytes 393224 | tf_op jit(solution)/shard_map/ppermute | solution.py:22
  44.2 14.2 %collective-permute-start.8 = (bf16[32,2048]{1,0:T(8,128)(2,1)S(1)}, bf16[32,2048]{1,0:T(8,128)(2,1)S(1)}, u32[]{:S(2)}, u32[]{:S(2)}) collective-permute-start(bf16[32,2048]{1,0:T(8,128)(2,1)S(1)} %get-tuple-element.22), channel_id=1, source_target_pairs={{0,2},{1,3},{2,0},{3,1},{4,6},{5,7},{6,4},{7,5},{8,10},{9,11},{10,... | collective-permute-start | bytes 393224 | tf_op jit(solution)/shard_map/ppermute | solution.py:17
  48.1 10.3 %collective-permute-start.7 = (bf16[32,2048]{1,0:T(8,128)(2,1)S(1)}, bf16[32,2048]{1,0:T(8,128)(2,1)S(1)}, u32[]{:S(2)}, u32[]{:S(2)}) collective-permute-start(bf16[32,2048]{1,0:T(8,128)(2,1)S(1)} %get-tuple-element.21), channel_id=1, source_target_pairs={{0,1},{1,0},{2,3},{3,2},{4,5},{5,4},{6,7},{7,6},{8,9},{9,8},{10,11... | collective-permute-start | bytes 393224 | tf_op jit(solution)/shard_map/ppermute | solution.py:17
  48.1 13.7 %collective-permute-start.32 = (bf16[32,2048]{1,0:T(8,128)(2,1)S(1)}, bf16[32,2048]{1,0:T(8,128)(2,1)S(1)}, u32[]{:S(2)}, u32[]{:S(2)}) collective-permute-start(bf16[32,2048]{1,0:T(8,128)(2,1)S(1)} %collective-permute-done.30.refs_1_), channel_id=1, source_target_pairs={{0,1},{1,2},{2,3},{4,5},{5,6},{6,7},{8,9},{9,10},{10,11},{12,13},{... | collective-permute-start | bytes 393224 | tf_op jit(solution)/shard_map/ppermute | solution.py:22
  52.1 14.4 %collective-permute-start.33 = (bf16[32,2048]{1,0:T(8,128)(2,1)S(1)}, bf16[32,2048]{1,0:T(8,128)(2,1)S(1)}, u32[]{:S(2)}, u32[]{:S(2)}) collective-permute-start(bf16[32,2048]{1,0:T(8,128)(2,1)S(1)} %collective-permute-done.31.refs_2_), channel_id=1, source_target_pairs={{1,0},{2,1},{3,2},{5,4},{6,5},{7,6},{9,8},{10,9},{11,10},{13,12},{... | collective-permute-start | bytes 393224 | tf_op jit(solution)/shard_map/ppermute | solution.py:22
  58.4 9.3 %collective-permute-start.20 = (bf16[32,2048]{1,0:T(8,128)(2,1)S(1)}, bf16[32,2048]{1,0:T(8,128)(2,1)S(1)}, u32[]{:S(2)}, u32[]{:S(2)}) collective-permute-start(bf16[32,2048]{1,0:T(8,128)(2,1)S(1)} %get-tuple-element.38.refs_0_), channel_id=1, source_target_pairs={{0,1},{1,2},{2,3},{4,5},{5,6},{6,7},{8,9},{9,10},{10,11},{12,13},{... | collective-permute-start | bytes 393224 | tf_op jit(solution)/shard_map/ppermute | solution.py:22
  60.6 11.8 %collective-permute-start.21 = (bf16[32,2048]{1,0:T(8,128)(2,1)S(1)}, bf16[32,2048]{1,0:T(8,128)(2,1)S(1)}, u32[]{:S(2)}, u32[]{:S(2)}) collective-permute-start(bf16[32,2048]{1,0:T(8,128)(2,1)S(1)} %get-tuple-element.38.refs_0_), channel_id=1, source_target_pairs={{1,0},{2,1},{3,2},{5,4},{6,5},{7,6},{9,8},{10,9},{11,10},{13,12},{... | collective-permute-start | bytes 393224 | tf_op jit(solution)/shard_map/ppermute | solution.py:22
  61.9 11.8 %collective-permute-start.34 = (bf16[32,2048]{1,0:T(8,128)(2,1)S(1)}, bf16[32,2048]{1,0:T(8,128)(2,1)S(1)}, u32[]{:S(2)}, u32[]{:S(2)}) collective-permute-start(bf16[32,2048]{1,0:T(8,128)(2,1)S(1)} %collective-permute-done.32.refs_3_), channel_id=1, source_target_pairs={{0,1},{1,2},{2,3},{4,5},{5,6},{6,7},{8,9},{9,10},{10,11},{12,13},{... | collective-permute-start | bytes 393224 | tf_op jit(solution)/shard_map/ppermute | solution.py:22
  66.5 7.2 %collective-permute-start.35 = (bf16[32,2048]{1,0:T(8,128)(2,1)S(1)}, bf16[32,2048]{1,0:T(8,128)(2,1)S(1)}, u32[]{:S(2)}, u32[]{:S(2)}) collective-permute-start(bf16[32,2048]{1,0:T(8,128)(2,1)S(1)} %collective-permute-done.33.refs_4_), channel_id=1, source_target_pairs={{1,0},{2,1},{3,2},{5,4},{6,5},{7,6},{9,8},{10,9},{11,10},{13,12},{... | collective-permute-start | bytes 393224 | tf_op jit(solution)/shard_map/ppermute | solution.py:22
  67.8 8.0 %collective-permute-start.22 = (bf16[32,2048]{1,0:T(8,128)(2,1)S(1)}, bf16[32,2048]{1,0:T(8,128)(2,1)S(1)}, u32[]{:S(2)}, u32[]{:S(2)}) collective-permute-start(bf16[32,2048]{1,0:T(8,128)(2,1)S(1)} %collective-permute-done.20.refs_1_), channel_id=1, source_target_pairs={{0,1},{1,2},{2,3},{4,5},{5,6},{6,7},{8,9},{9,10},{10,11},{12,13},{... | collective-permute-start | bytes 393224 | tf_op jit(solution)/shard_map/ppermute | solution.py:22
  72.3 8.0 %collective-permute-start.23 = (bf16[32,2048]{1,0:T(8,128)(2,1)S(1)}, bf16[32,2048]{1,0:T(8,128)(2,1)S(1)}, u32[]{:S(2)}, u32[]{:S(2)}) collective-permute-start(bf16[32,2048]{1,0:T(8,128)(2,1)S(1)} %collective-permute-done.21.refs_2_), channel_id=1, source_target_pairs={{1,0},{2,1},{3,2},{5,4},{6,5},{7,6},{9,8},{10,9},{11,10},{13,12},{... | collective-permute-start | bytes 393224 | tf_op jit(solution)/shard_map/ppermute | solution.py:22
  75.7 15.4 %collective-permute-start.36 = (f32[64,2048]{1,0:T(8,128)S(1)}, f32[64,2048]{1,0:T(8,128)S(1)}, u32[]{:S(2)}, u32[]{:S(2)}) collective-permute-start(f32[64,2048]{1,0:T(8,128)S(1)} %get-tuple-element.34), channel_id=1, source_target_pairs={{0,4},{4,0},{8,12},{12,8},{16,20},{20,16},{24,28},{28,24},{1,5},{5... | collective-permute-start | bytes 1572872 | tf_op jit(solution)/shard_map/ppermute | solution.py:17
  75.8 7.9 %collective-permute-start.24 = (bf16[32,2048]{1,0:T(8,128)(2,1)S(1)}, bf16[32,2048]{1,0:T(8,128)(2,1)S(1)}, u32[]{:S(2)}, u32[]{:S(2)}) collective-permute-start(bf16[32,2048]{1,0:T(8,128)(2,1)S(1)} %collective-permute-done.22.refs_3_), channel_id=1, source_target_pairs={{0,1},{1,2},{2,3},{4,5},{5,6},{6,7},{8,9},{9,10},{10,11},{12,13},{... | collective-permute-start | bytes 393224 | tf_op jit(solution)/shard_map/ppermute | solution.py:22
  80.4 7.8 %collective-permute-start.25 = (bf16[32,2048]{1,0:T(8,128)(2,1)S(1)}, bf16[32,2048]{1,0:T(8,128)(2,1)S(1)}, u32[]{:S(2)}, u32[]{:S(2)}) collective-permute-start(bf16[32,2048]{1,0:T(8,128)(2,1)S(1)} %collective-permute-done.23.refs_4_), channel_id=1, source_target_pairs={{1,0},{2,1},{3,2},{5,4},{6,5},{7,6},{9,8},{10,9},{11,10},{13,12},{... | collective-permute-start | bytes 393224 | tf_op jit(solution)/shard_map/ppermute | solution.py:22
  91.1 5.9 %collective-permute-start.39 = (bf16[16,2048]{1,0:T(8,128)(2,1)S(1)}, bf16[16,2048]{1,0:T(8,128)(2,1)S(1)}, u32[]{:S(2)}, u32[]{:S(2)}) collective-permute-start(bf16[16,2048]{1,0:T(8,128)(2,1)S(1)} %get-tuple-element.46), channel_id=1, source_target_pairs={{0,24},{4,28},{8,16},{12,20},{16,8},{20,12},{24,0},{28,4},{1,25},{... | collective-permute-start | bytes 196616 | tf_op jit(solution)/shard_map/ppermute | solution.py:17
  91.8 6.4 %collective-permute-start.38 = (bf16[16,2048]{1,0:T(8,128)(2,1)S(1)}, bf16[16,2048]{1,0:T(8,128)(2,1)S(1)}, u32[]{:S(2)}, u32[]{:S(2)}) collective-permute-start(bf16[16,2048]{1,0:T(8,128)(2,1)S(1)} %get-tuple-element.47), channel_id=1, source_target_pairs={{0,16},{4,20},{8,24},{12,28},{16,0},{20,4},{24,8},{28,12},{1,17},{... | collective-permute-start | bytes 196616 | tf_op jit(solution)/shard_map/ppermute | solution.py:17
  94.7 5.8 %collective-permute-start.29 = (bf16[16,2048]{1,0:T(8,128)(2,1)S(1)}, bf16[16,2048]{1,0:T(8,128)(2,1)S(1)}, u32[]{:S(2)}, u32[]{:S(2)}) collective-permute-start(bf16[16,2048]{1,0:T(8,128)(2,1)S(1)} %get-tuple-element.43), channel_id=1, source_target_pairs={{0,24},{4,28},{8,16},{12,20},{16,8},{20,12},{24,0},{28,4},{1,25},{... | collective-permute-start | bytes 196616 | tf_op jit(solution)/shard_map/ppermute | solution.py:17
  (9 other events, 39.4 us)

commit v3 on v0

v3 whole, which is shorter than its diff:
```python
import functools

import jax
import jax.numpy as jnp
from jax import lax
from jax.experimental import pallas as pl
from jax.experimental.pallas import tpu as pltpu
from jax.sharding import PartitionSpec as P

F32, BF16 = jnp.float32, jnp.bfloat16
VMEM_LIMIT = 28 * 2**20
STEP = 512


def spread(value, axis):
    copies = jnp.broadcast_to(value, (lax.axis_size(axis), *value.shape)).reshape(-1, value.shape[1])
    return lax.all_to_all(copies, axis, 0, 0, tiled=True)


def gathered_sum(own, parts, axis):
    size = lax.axis_size(axis)
    terms = lax.all_to_all(parts, axis, 0, 0, tiled=True).reshape(size, *own.shape)
    me = lax.axis_index(axis)
    total = own
    for k in range(size):
        total = total + jnp.where(me == k, 0.0, terms[k].astype(F32))
    return total


def mask_kernel(mask_ref, green_ref, tiles, sems, *, block):
    rows, cols = tiles.shape
    copies = []
    for step in range(rows // STEP):
        at = pl.ds(step * STEP, STEP)
        copies.append(pltpu.make_async_copy(green_ref.at[at], tiles.at[at], sems.at[step]))
        copies[-1].start()
    for step, copy in enumerate(copies):
        copy.wait()
        for i in range(step * STEP // block, (step + 1) * STEP // block):
            for j in range(cols // block):

                @pl.when(mask_ref[i, j] == 0)
                def _():
                    tiles[i * block : (i + 1) * block, j * block : (j + 1) * block] = jnp.zeros((block, block), BF16)


def masked(green, mask):
    rows, cols = green.shape
    return pl.pallas_call(
        functools.partial(mask_kernel, block=rows // mask.shape[0]),
        in_specs=[pl.BlockSpec(memory_space=pltpu.SMEM), pl.BlockSpec(memory_space=pltpu.HBM)],
        out_specs=pl.BlockSpec(memory_space=pltpu.VMEM),
        out_shape=pltpu.VMEM((rows, cols), BF16),
        scratch_shapes=[pltpu.SemaphoreType.DMA((rows // STEP,))],
        compiler_params=pltpu.CompilerParams(vmem_limit_bytes=VMEM_LIMIT),
        cost_estimate=pl.CostEstimate(flops=0, bytes_accessed=2 * rows * cols, transcendentals=0),
        name="masked_tiles",
    )(mask, pltpu.with_memory_space_constraint(green, pltpu.HBM))


def product_kernel(me, tiles, left, parts, own, total, *, transposed):
    for step in range(tiles.shape[0] // STEP):
        at = slice(step * STEP, (step + 1) * STEP)
        if transposed:
            term = lax.dot_general(left[...], tiles[at, :], (((1,), (1,)), ((), ())), preferred_element_type=F32)
        else:
            term = jnp.dot(left[...], tiles[:, at], preferred_element_type=F32)
        total[:, at] = term
        parts[:, at] = term.astype(BF16)
    share = own.shape[0]
    own[...] = total[pl.ds(pl.multiple_of(me[0] * share, share), share), :]


def product(tiles, left, axis, transposed):
    length = tiles.shape[0 if transposed else 1]
    width = left.shape[0]
    share = width // lax.axis_size(axis)
    me = lax.axis_index(axis).astype(jnp.int32).reshape(1)
    vmem = pl.BlockSpec(memory_space=pltpu.VMEM)
    return pl.pallas_call(
        functools.partial(product_kernel, transposed=transposed),
        in_specs=[pl.BlockSpec(memory_space=pltpu.SMEM), vmem, vmem],
        out_specs=[vmem, vmem],
        out_shape=[jax.ShapeDtypeStruct((width, length), BF16), jax.ShapeDtypeStruct((share, length), F32)],
        scratch_shapes=[pltpu.VMEM((width, length), F32)],
        compiler_params=pltpu.CompilerParams(vmem_limit_bytes=VMEM_LIMIT),
        cost_estimate=pl.CostEstimate(
            flops=2 * width * tiles.shape[0] * tiles.shape[1],
            bytes_accessed=2 * tiles.shape[0] * tiles.shape[1],
            transcendentals=0,
        ),
        name="partial_sketch" if transposed else "partial_adjoint",
    )(me, tiles, left)


def local(green, mask, probes):
    tiles = masked(green, mask)
    parts, own = product(tiles, spread(probes.T, "row"), "col", True)
    sketch = gathered_sum(own, parts, "col")
    parts, own = product(tiles, spread(sketch.astype(BF16), "col"), "row", False)
    return sketch.T, gathered_sum(own, parts, "row").T


def solution(mesh):
    in_specs = (P("row", "col"), P("row", "col"), P("col", "row"))
    out_specs = (P("row", "col"), P("col", "row"))
    return jax.shard_map(local, mesh=mesh, in_specs=in_specs, out_specs=out_specs, check_vma=False)
```

time: 185 us -> 117 us (0.63)
  waiting for transfers between devices: 129 us -> 70.5 us
  starting transfers between devices: 0.12 us -> 18.8 us
  matrix products: 15.1 us -> 0 us
  between operations: 13.8 us -> 0.67 us
  Pallas kernels: 0 us -> 10.9 us
  other arithmetic: 11.3 us -> 1.93 us
    psum x1 -> x0, waiting for transfers between devices: 86.6 us -> none  [local(): summed = lax.psum(partial_sketch, 'col')]
    all_to_all x0 -> x4, waiting for transfers between devices: none -> 70.5 us  [the longest x2 38.4 us: gathered_sum(): lax.all_to_all(parts, axis, 0, 0, tiled=True).reshape(size, *own.shape)]
    reduce_scatter x1 -> x0, waiting for transfers between devices: 38.9 us -> none  [local(): adjoint = lax.psum_scatter(term, 'row', scatter_dimension=1, tiled=True)]
    all_to_all x0 -> x4, starting transfers between devices: none -> 18.8 us  [the longest x2 10.1 us: gathered_sum(): lax.all_to_all(parts, axis, 0, 0, tiled=True).reshape(size, *own.shape)]
    dot_general x2 -> x0, matrix products: 15.1 us -> none  [the longest x1 7.8 us: local(): lax.dot_general(tiles, summed.astype(jnp.bfloat16), (((0,), (0,)), ((), (...]
    pallas_call x0 -> x3, Pallas kernels: none -> 10.9 us  [the longest x2 6.74 us: product(): pl.pallas_call(functools.partial(product_kernel, transposed=transposed),...]
    mul x1 -> x0, other arithmetic: 10.6 us -> none  [local(): shaped * mask.astype(jnp.bfloat16)[:, None, :, None]]
    mul x1 -> x0, local copies, waits for them, and re-layouts: 3.83 us -> none  [local(): shaped * mask.astype(jnp.bfloat16)[:, None, :, None]]
  transfers between devices with their start and end apart: 3 -> 4, of which waited for: 3 -> 4; matrix products, arithmetic and copies ran while one was open for 15% -> 0% of each run, Pallas kernels for 0% -> 4%
where the time goes in v3:
time: 117 us
  waiting for transfers between devices  70.5 us (60%)
  starting transfers between devices  18.8 us (16%)
  local copies, waits for them, and re-layouts  13.9 us (12%)
  Pallas kernels  10.9 us (9%)
  other arithmetic  1.93 us (2%)
    all_to_all x2, waiting for transfers between devices, gathered_sum(): lax.all_to_all(parts, axis, 0, 0, tiled=True).reshape(size, *own.shape)  38.4 us
    all_to_all x2, waiting for transfers between devices, spread(): return lax.all_to_all(copies, axis, 0, 0, tiled=True)  32.1 us
    unnamed x8, local copies, waits for them, and re-layouts  10.7 us
    all_to_all x2, starting transfers between devices, gathered_sum(): lax.all_to_all(parts, axis, 0, 0, tiled=True).reshape(size, *own.shape)  10.1 us
    all_to_all x2, starting transfers between devices, spread(): return lax.all_to_all(copies, axis, 0, 0, tiled=True)  8.69 us
    pallas_call x2, Pallas kernels, product(): pl.pallas_call(functools.partial(product_kernel, transposed=transposed),...  6.74 us
    pallas_call x1, Pallas kernels, masked(): pl.pallas_call(functools.partial(mask_kernel, block=rows // mask.shape[0]...  4.13 us
    broadcast_in_dim x2, local copies, waits for them, and re-layouts, spread(): jnp.broadcast_to(value, (lax.axis_size(axis), *value.shape))  3.28 us
  transfers between devices with their start and end apart: 4, of which 4 were waited for; matrix products, arithmetic and copies ran while one was open for 0% of the time, Pallas kernels for 4%

profile of v3, /device:TPU:0, one launch (start us, length us, event | category | flops | bytes accessed | tf_op | source)
XLA Modules:
  0.0 116.7 jit_solution(16254882589304161723)
XLA Ops:
  0.6 2.1 %broadcast_in_dim.24 = bf16[8,32,2048]{2,1,0:T(8,128)(2,1)} broadcast(bf16[32,2048]{1,0:T(8,128)(2,1)} %bitcast.63), dimensions={1,2} | broadcast | bytes 1179648 | tf_op jit(solution)/shard_map/broadcast_in_dim | solution.py:16
  2.7 5.2 %all-to-all-start = ((bf16[8,32,2048]{2,1,0:T(8,128)(2,1)}), bf16[8,32,2048]{2,1,0:T(8,128)(2,1)S(1)}, u32[]{:S(2)}, u32[]{:S(2)}) async-start(bf16[8,32,2048]{2,1,0:T(8,128)(2,1)} %broadcast_in_dim.24), calls=%async_computation | async-start | bytes 2097152 | tf_op jit(solution)/shard_map/all_to_all | solution.py:17
  7.9 0.0 copy-start.3
  7.9 0.7 copy-done.3
  8.6 4.1 %masked_tiles.1.tiles = bf16[2048,2048]{1,0:T(8,128)(2,1)S(1)} custom-call(s32[8,8]{1,0:T(8,128)S(1)} %copy-done.3, bf16[2048,2048]{1,0:T(8,128)(2,1)} %green_ref.1), custom_call_target="tpu_custom_call" | custom-call | bytes 8388608 | tf_op jit(solution)/shard_map/masked_tiles/pallas_call | solution.py:49
  12.7 0.0 copy-start
  12.7 3.2 %copy-done = bf16[2048,2048]{1,0:T(8,128)(2,1)} copy-done((bf16[2048,2048]{1,0:T(8,128)(2,1)}, bf16[2048,2048]{1,0:T(8,128)(2,1)S(1)}, u32[]{:S(2)}) %copy-start) | copy-done | bytes 8388632
  15.9 7.4 %all-to-all-done = bf16[8,32,2048]{2,1,0:T(8,128)(2,1)S(1)} async-done(((bf16[8,32,2048]{2,1,0:T(8,128)(2,1)}), bf16[8,32,2048]{2,1,0:T(8,128)(2,1)S(1)}, u32[]{:S(2)}, u32[]{:S(2)}) %all-to-all-start) | async-done | bytes 1048608 | tf_op jit(solution)/shard_map/all_to_all | solution.py:17
  23.3 0.0 copy-start.1
  23.3 3.4 %copy-done.1 = bf16[2048,2048]{1,0:T(8,128)(2,1)S(1)} copy-done((bf16[2048,2048]{1,0:T(8,128)(2,1)S(1)}, bf16[2048,2048]{1,0:T(8,128)(2,1)}, u32[]{:S(2)}) %copy-start.1) | copy-done | bytes 8388632
  26.7 3.4 %partial_sketch.1 = (bf16[256,2048]{1,0:T(8,128)(2,1)}, f32[64,2048]{1,0:T(8,128)S(1)}) custom-call(s32[1]{0:T(128)} %bitcast.me, bf16[2048,2048]{1,0:T(8,128)(2,1)S(1)} %copy-done.1, bf16[256,2048]{1,0:T(8,128)(2,1)S(1)} %bitcast.61), custom_call_target="tpu_custom_call" | custom-call | flops 2147483648 | bytes 8388608 | tf_op jit(solution)/shard_map/partial_sketch/pallas_call | solution.py:80
  30.1 4.9 %all-to-all-start.1 = ((bf16[4,64,2048]{2,1,0:T(8,128)(2,1)}), bf16[4,64,2048]{2,1,0:T(8,128)(2,1)S(1)}, u32[]{:S(2)}, u32[]{:S(2)}) async-start(bf16[4,64,2048]{2,1,0:T(8,128)(2,1)} %bitcast.3), calls=%async_computation.1 | async-start | bytes 2097152 | tf_op jit(solution)/shard_map/all_to_all | solution.py:22
  35.0 22.9 %all-to-all-done.1 = bf16[4,64,2048]{2,1,0:T(8,128)(2,1)S(1)} async-done(((bf16[4,64,2048]{2,1,0:T(8,128)(2,1)}), bf16[4,64,2048]{2,1,0:T(8,128)(2,1)S(1)}, u32[]{:S(2)}, u32[]{:S(2)}) %all-to-all-start.1) | async-done | bytes 1048608 | tf_op jit(solution)/shard_map/all_to_all | solution.py:22
  57.9 1.0 fusion.1
  58.9 1.2 %broadcast_in_dim.26 = bf16[4,64,2048]{2,1,0:T(8,128)(2,1)} broadcast(bf16[64,2048]{1,0:T(8,128)(2,1)S(1)} %get-tuple-element.10), dimensions={1,2} | broadcast | bytes 1310720 | tf_op jit(solution)/shard_map/broadcast_in_dim | solution.py:16
  60.1 3.5 %all-to-all-start.2 = ((bf16[4,64,2048]{2,1,0:T(8,128)(2,1)}), bf16[4,64,2048]{2,1,0:T(8,128)(2,1)S(1)}, u32[]{:S(2)}, u32[]{:S(2)}) async-start(bf16[4,64,2048]{2,1,0:T(8,128)(2,1)} %broadcast_in_dim.26), calls=%async_computation.2 | async-start | bytes 2097152 | tf_op jit(solution)/shard_map/all_to_all | solution.py:17
  63.7 24.8 %all-to-all-done.2 = bf16[4,64,2048]{2,1,0:T(8,128)(2,1)S(1)} async-done(((bf16[4,64,2048]{2,1,0:T(8,128)(2,1)}), bf16[4,64,2048]{2,1,0:T(8,128)(2,1)S(1)}, u32[]{:S(2)}, u32[]{:S(2)}) %all-to-all-start.2) | async-done | bytes 1048608 | tf_op jit(solution)/shard_map/all_to_all | solution.py:17
  88.4 0.0 copy-start.2
  88.5 3.4 %copy-done.2 = bf16[2048,2048]{1,0:T(8,128)(2,1)S(1)} copy-done((bf16[2048,2048]{1,0:T(8,128)(2,1)S(1)}, bf16[2048,2048]{1,0:T(8,128)(2,1)}, u32[]{:S(2)}) %copy-start.2) | copy-done | bytes 8388632
  91.8 3.3 %partial_adjoint.1 = (bf16[256,2048]{1,0:T(8,128)(2,1)}, f32[32,2048]{1,0:T(8,128)S(1)}) custom-call(s32[1]{0:T(128)} %bitcast.9.me, bf16[2048,2048]{1,0:T(8,128)(2,1)S(1)} %copy-done.2, bf16[256,2048]{1,0:T(8,128)(2,1)S(1)} %bitcast.60), custom_call_target="tpu_custom_call" | custom-call | flops 2147483648 | bytes 8388608 | tf_op jit(solution)/shard_map/partial_adjoint/pallas_call | solution.py:80
  95.1 5.2 %all-to-all-start.3 = ((bf16[8,32,2048]{2,1,0:T(8,128)(2,1)}), bf16[8,32,2048]{2,1,0:T(8,128)(2,1)S(1)}, u32[]{:S(2)}, u32[]{:S(2)}) async-start(bf16[8,32,2048]{2,1,0:T(8,128)(2,1)} %bitcast.11), calls=%async_computation.3 | async-start | bytes 2097152 | tf_op jit(solution)/shard_map/all_to_all | solution.py:22
  100.4 15.4 %all-to-all-done.3 = bf16[8,32,2048]{2,1,0:T(8,128)(2,1)S(1)} async-done(((bf16[8,32,2048]{2,1,0:T(8,128)(2,1)}), bf16[8,32,2048]{2,1,0:T(8,128)(2,1)S(1)}, u32[]{:S(2)}, u32[]{:S(2)}) %all-to-all-start.3) | async-done | bytes 1048608 | tf_op jit(solution)/shard_map/all_to_all | solution.py:22
  115.8 0.9 fusion
Async XLA Ops:
  2.7 20.6 %all-to-all-start = ((bf16[8,32,2048]{2,1,0:T(8,128)(2,1)}), bf16[8,32,2048]{2,1,0:T(8,128)(2,1)S(1)}, u32[]{:S(2)}, u32[]{:S(2)}) async-start(bf16[8,32,2048]{2,1,0:T(8,128)(2,1)} %broadcast_in_dim.24), calls=%async_computation | async-start | bytes 2097152 | tf_op jit(solution)/shard_map/all_to_all | solution.py:17
  7.9 0.7 copy-start.3
  12.7 3.2 %copy-start = (bf16[2048,2048]{1,0:T(8,128)(2,1)}, bf16[2048,2048]{1,0:T(8,128)(2,1)S(1)}, u32[]{:S(2)}) copy-start(bf16[2048,2048]{1,0:T(8,128)(2,1)S(1)} %masked_tiles.1.tiles) | copy-start | bytes 25165828
  23.3 3.4 %copy-start.1 = (bf16[2048,2048]{1,0:T(8,128)(2,1)S(1)}, bf16[2048,2048]{1,0:T(8,128)(2,1)}, u32[]{:S(2)}) copy-start(bf16[2048,2048]{1,0:T(8,128)(2,1)} %copy-done) | copy-start | bytes 25165828
  30.1 27.8 %all-to-all-start.1 = ((bf16[4,64,2048]{2,1,0:T(8,128)(2,1)}), bf16[4,64,2048]{2,1,0:T(8,128)(2,1)S(1)}, u32[]{:S(2)}, u32[]{:S(2)}) async-start(bf16[4,64,2048]{2,1,0:T(8,128)(2,1)} %bitcast.3), calls=%async_computation.1 | async-start | bytes 2097152 | tf_op jit(solution)/shard_map/all_to_all | solution.py:22
  60.1 28.3 %all-to-all-start.2 = ((bf16[4,64,2048]{2,1,0:T(8,128)(2,1)}), bf16[4,64,2048]{2,1,0:T(8,128)(2,1)S(1)}, u32[]{:S(2)}, u32[]{:S(2)}) async-start(bf16[4,64,2048]{2,1,0:T(8,128)(2,1)} %broadcast_in_dim.26), calls=%async_computation.2 | async-start | bytes 2097152 | tf_op jit(solution)/shard_map/all_to_all | solution.py:17
  88.4 3.4 %copy-start.2 = (bf16[2048,2048]{1,0:T(8,128)(2,1)S(1)}, bf16[2048,2048]{1,0:T(8,128)(2,1)}, u32[]{:S(2)}) copy-start(bf16[2048,2048]{1,0:T(8,128)(2,1)} %copy-done) | copy-start | bytes 25165828
  95.1 20.6 %all-to-all-start.3 = ((bf16[8,32,2048]{2,1,0:T(8,128)(2,1)}), bf16[8,32,2048]{2,1,0:T(8,128)(2,1)S(1)}, u32[]{:S(2)}, u32[]{:S(2)}) async-start(bf16[8,32,2048]{2,1,0:T(8,128)(2,1)} %bitcast.11), calls=%async_computation.3 | async-start | bytes 2097152 | tf_op jit(solution)/shard_map/all_to_all | solution.py:22

commit v4 on v2

--- a/solution.py
+++ b/solution.py
@@ -10,16 +10,12 @@
 F32, BF16 = jnp.float32, jnp.bfloat16
 VMEM_LIMIT = 28 * 2**20
 STEP = 512
+CHUNKS = 1
 
 
 def exchange(value, axis, offset):
     size = lax.axis_size(axis)
     return lax.ppermute(value, axis, [(i, i ^ offset) for i in range(size)])
-
-
-def relay(value, axis, hop):
-    size = lax.axis_size(axis)
-    return lax.ppermute(value, axis, [(i, i + hop) for i in range(size) if 0 <= i + hop < size])
 
 
 def mask_kernel(mask_ref, green_ref, tiles, sems, *, block):
@@ -90,18 +86,14 @@
     )(where, tiles, *blocks)
 
 
-def adjoint_kernel(where, tiles, *refs, hops, offsets_core):
-    shares, outs = refs[: len(hops)], refs[len(hops) : -2]
+def adjoint_kernel(where, tiles, *refs, offsets_col, offsets_core):
+    shares, outs = refs[: len(offsets_col)], refs[len(offsets_col) : -2]
     lowered, total = refs[-2:]
     share = shares[0].shape[0]
     width = outs[0].shape[0]
-    for hop, ref in zip(hops, shares):
-        origin = where[1] + hop
-
-        @pl.when((origin >= 0) & (origin < lowered.shape[0] // share))
-        def _():
-            lowered[pl.ds(pl.multiple_of(origin * share, share), share), :] = ref[...]
-
+    for offset, ref in zip(offsets_col, shares):
+        start = pl.multiple_of((where[1] ^ offset) * share, share)
+        lowered[pl.ds(start, share), :] = ref[...]
     for step in range(tiles.shape[1] // STEP):
         at = slice(step * STEP, (step + 1) * STEP)
         total[:, at] = jnp.dot(lowered[...], tiles[:, at], preferred_element_type=F32)
@@ -113,13 +105,13 @@
         sibling[k * width : (k + 1) * width, :] = total[pl.ds(start, width), :].astype(sibling.dtype)
 
 
-def partial_adjoint(where, tiles, shares, hops, offsets_core, width):
+def partial_adjoint(where, tiles, shares, offsets_col, offsets_core, width):
     rows, cols = tiles.shape
     own = width // (2 * len(offsets_core))
     heights = [own] * len(offsets_core) + [own * len(offsets_core)]
     vmem = pl.BlockSpec(memory_space=pltpu.VMEM)
     return pl.pallas_call(
-        functools.partial(adjoint_kernel, hops=hops, offsets_core=offsets_core),
+        functools.partial(adjoint_kernel, offsets_col=offsets_col, offsets_core=offsets_core),
         in_specs=[pl.BlockSpec(memory_space=pltpu.SMEM)] + [vmem] * (1 + len(shares)),
         out_specs=[vmem] * len(heights),
         out_shape=[jax.ShapeDtypeStruct((h, cols), F32) for h in heights],
@@ -141,19 +133,21 @@
     n_row, n_col = lax.axis_size("row"), lax.axis_size("col")
     where = jnp.stack([lax.axis_index("row"), lax.axis_index("col")]).astype(jnp.int32)
     own_width = probes.shape[1]
-    chunks = 2 if own_width % 32 == 0 and n_row % n_col == 0 else 1
+    chunks = CHUNKS if own_width % (16 * CHUNKS) == 0 and n_row % n_col == 0 else 1
     piece = own_width // chunks
     width = piece * n_row
     offsets_col = list(range(n_col))
     offsets_core = list(range(0, n_row, 2))
-    offsets_row = offsets_core + [offset ^ 1 for offset in offsets_core]
+    gather_core = [0] + offsets_core[:0:-1]
+    offsets_row = gather_core + [offset ^ 1 for offset in gather_core]
+    far_first = [0] + offsets_col[:0:-1]
 
     tiles = masked(green, mask)
 
     blocks = []
     for chunk in range(chunks):
         own = probes.T[chunk * piece : (chunk + 1) * piece]
-        held = [own] + [exchange(own, "row", offset) for offset in offsets_core[1:]]
+        held = [own] + [exchange(own, "row", offset) for offset in gather_core[1:]]
         blocks.append(held + [exchange(block, "row", 1) for block in held])
 
     sketches, adjoints = [], []
@@ -164,14 +158,10 @@
             total = total + exchange(parts[offset], "col", offset).astype(F32)
         sketches.append(total)
 
-        shares, hops = [total.astype(BF16)], [0]
-        up = down = shares[0]
-        for hop in range(1, n_col):
-            up, down = relay(up, "col", 1), relay(down, "col", -1)
-            shares += [up, down]
-            hops += [-hop, hop]
+        lowered = total.astype(BF16)
+        shares = [lowered] + [exchange(lowered, "col", offset) for offset in far_first[1:]]
 
-        *mine, others = partial_adjoint(where, tiles, shares, hops, offsets_core, width)
+        *mine, others = partial_adjoint(where, tiles, shares, far_first, offsets_core, width)
         others = exchange(others, "row", 1)
         pairs = [m + others[k * piece : (k + 1) * piece] for k, m in enumerate(mine)]
         adjoint = pairs[0]

time: 103 us -> 88.8 us (0.86)
  starting transfers between devices: 55.9 us -> 20.6 us
  waiting for transfers between devices: 26.5 us -> 53.7 us
  Pallas kernels: 15.2 us -> 10.4 us
    ppermute x28 -> x17, waiting for transfers between devices: 20 us -> 53.7 us  [exchange(): return lax.ppermute(value, axis, [(i, i ^ offset) for i in range(size)])]
    ppermute x12 -> x0, starting transfers between devices: 29.2 us -> none  [relay(): lax.ppermute(value, axis, [(i, i + hop) for i in range(size) if 0 <= i +...]
    ppermute x12 -> x0, waiting for transfers between devices: 6.48 us -> none  [relay(): lax.ppermute(value, axis, [(i, i + hop) for i in range(size) if 0 <= i +...]
    ppermute x28 -> x17, starting transfers between devices: 26.7 us -> 20.6 us  [exchange(): return lax.ppermute(value, axis, [(i, i ^ offset) for i in range(size)])]
    pallas_call x2 -> x1, Pallas kernels: 7 us -> 3.04 us  [partial_sketch(): pl.pallas_call(functools.partial(sketch_kernel, offsets_row=offsets_row,...]
    pallas_call x2 -> x1, Pallas kernels: 4.04 us -> 3.12 us  [partial_adjoint(): pl.pallas_call(functools.partial(adjoint_kernel, offsets_col=offsets_col,...]
  transfers between devices with their start and end apart: 40 -> 17, of which waited for: 10 -> 10; matrix products, arithmetic and copies ran while one was open for 1% -> 0% of each run, Pallas kernels for 15% -> 5%
where the time goes in v4:
time: 88.8 us; the launch traced here: 87.9 us
  waiting for transfers between devices  53.7 us (60%)
  starting transfers between devices  20.6 us (23%)
  Pallas kernels  10.4 us (12%)
  other arithmetic  1.87 us (2%)
    ppermute x17, waiting for transfers between devices, exchange(): return lax.ppermute(value, axis, [(i, i ^ offset) for i in range(size)])  53.7 us
    ppermute x17, starting transfers between devices, exchange(): return lax.ppermute(value, axis, [(i, i ^ offset) for i in range(size)])  20.6 us
    pallas_call x1, Pallas kernels, masked(): pl.pallas_call(functools.partial(mask_kernel, block=rows // mask.shape[0]...  4.21 us
    pallas_call x1, Pallas kernels, partial_adjoint(): pl.pallas_call(functools.partial(adjoint_kernel, offsets_col=offsets_col,...  3.12 us
    pallas_call x1, Pallas kernels, partial_sketch(): pl.pallas_call(functools.partial(sketch_kernel, offsets_row=offsets_row,...  3.04 us
  transfers between devices with their start and end apart: 17, of which 10 were waited for; matrix products, arithmetic and copies ran while one was open for 0% of the time, Pallas kernels for 5%

profile of v4, /device:TPU:0, one launch (start us, length us, event | category | flops | bytes accessed | tf_op | source)
XLA Modules:
  0.0 87.9 jit_solution(8371217927431009947)
XLA Ops:
  0.6 3.0 %collective-permute-start.2 = (bf16[32,2048]{1,0:T(8,128)(2,1)}, bf16[32,2048]{1,0:T(8,128)(2,1)S(1)}, u32[]{:S(2)}, u32[]{:S(2)}) collective-permute-start(bf16[32,2048]{1,0:T(8,128)(2,1)} %bitcast.7), channel_id=1, source_target_pairs={{0,8},{4,12},{8,0},{12,4},{16,24},{20,28},{24,16},{28,20},{1,9},{5... | collective-permute-start | bytes 393224 | tf_op jit(solution)/shard_map/ppermute | solution.py:18
  3.6 1.5 %collective-permute-start.1 = (bf16[32,2048]{1,0:T(8,128)(2,1)}, bf16[32,2048]{1,0:T(8,128)(2,1)S(1)}, u32[]{:S(2)}, u32[]{:S(2)}) collective-permute-start(bf16[32,2048]{1,0:T(8,128)(2,1)} %bitcast.8), channel_id=1, source_target_pairs={{0,16},{4,20},{8,24},{12,28},{16,0},{20,4},{24,8},{28,12},{1,17},{... | collective-permute-start | bytes 393224 | tf_op jit(solution)/shard_map/ppermute | solution.py:18
  5.2 0.0 collective-permute-start
  5.2 2.7 %collective-permute-done.2.refs_3_ = bf16[32,2048]{1,0:T(8,128)(2,1)S(1)} collective-permute-done((bf16[32,2048]{1,0:T(8,128)(2,1)}, bf16[32,2048]{1,0:T(8,128)(2,1)S(1)}, u32[]{:S(2)}, u32[]{:S(2)}) %collective-permute-start.2) | collective-permute-done | bytes 131104 | tf_op jit(solution)/shard_map/ppermute | solution.py:18
  7.9 3.8 %collective-permute-done.1.refs_2_ = bf16[32,2048]{1,0:T(8,128)(2,1)S(1)} collective-permute-done((bf16[32,2048]{1,0:T(8,128)(2,1)}, bf16[32,2048]{1,0:T(8,128)(2,1)S(1)}, u32[]{:S(2)}, u32[]{:S(2)}) %collective-permute-start.1) | collective-permute-done | bytes 131104 | tf_op jit(solution)/shard_map/ppermute | solution.py:18
  11.6 0.5 collective-permute-start.4
  12.1 0.7 copy-done.1
  12.8 4.2 %masked_tiles.1.tiles = bf16[2048,2048]{1,0:T(8,128)(2,1)S(1)} custom-call(s32[8,8]{1,0:T(8,128)S(1)} %copy-done.1, bf16[2048,2048]{1,0:T(8,128)(2,1)} %green_ref.1), custom_call_target="tpu_custom_call" | custom-call | bytes 8388608 | tf_op jit(solution)/shard_map/masked_tiles/pallas_call | solution.py:40
  17.0 0.1 pad_add_fusion.where
  17.2 3.0 %partial_sketch.1 = (f32[64,2048]{1,0:T(8,128)S(1)}, bf16[64,2048]{1,0:T(8,128)(2,1)S(1)}, bf16[64,2048]{1,0:T(8,128)(2,1)S(1)}, bf16[64,2048]{1,0:T(8,128)(2,1)S(1)}) custom-call(s32[2]{0:T(128)S(1)} %pad_add_fusion.where, bf16[2048,2048]{1,0:T(8,128)(2,1)S(1)} %masked_tiles.1.tiles, bf16[32,2048]{1,0:T(8,128)(2,1)S(1)} %bitcast.11, ...), custom_call_target="tpu_custom_call" | custom-call | flops 2147483648 | bytes 8388608 | tf_op jit(solution)/shard_map/partial_sketch/pallas_call | solution.py:75
  20.2 1.7 %collective-permute-start.7 = (bf16[64,2048]{1,0:T(8,128)(2,1)S(1)}, bf16[64,2048]{1,0:T(8,128)(2,1)S(1)}, u32[]{:S(2)}, u32[]{:S(2)}) collective-permute-start(bf16[64,2048]{1,0:T(8,128)(2,1)S(1)} %get-tuple-element.12), channel_id=1, source_target_pairs={{0,1},{1,0},{2,3},{3,2},{4,5},{5,4},{6,7},{7,6},{8,9},{9,8},{10,11... | collective-permute-start | bytes 786440 | tf_op jit(solution)/shard_map/ppermute | solution.py:18
  21.9 2.7 %collective-permute-start.8 = (bf16[64,2048]{1,0:T(8,128)(2,1)S(1)}, bf16[64,2048]{1,0:T(8,128)(2,1)S(1)}, u32[]{:S(2)}, u32[]{:S(2)}) collective-permute-start(bf16[64,2048]{1,0:T(8,128)(2,1)S(1)} %get-tuple-element.13), channel_id=1, source_target_pairs={{0,2},{1,3},{2,0},{3,1},{4,6},{5,7},{6,4},{7,5},{8,10},{9,11},{10,... | collective-permute-start | bytes 786440 | tf_op jit(solution)/shard_map/ppermute | solution.py:18
  24.6 0.1 collective-permute-start.9
  24.7 8.7 %collective-permute-done.7 = bf16[64,2048]{1,0:T(8,128)(2,1)S(1)} collective-permute-done((bf16[64,2048]{1,0:T(8,128)(2,1)S(1)}, bf16[64,2048]{1,0:T(8,128)(2,1)S(1)}, u32[]{:S(2)}, u32[]{:S(2)}) %collective-permute-start.7) | collective-permute-done | bytes 262176 | tf_op jit(solution)/shard_map/ppermute | solution.py:18
  33.3 9.9 %collective-permute-done.8 = bf16[64,2048]{1,0:T(8,128)(2,1)S(1)} collective-permute-done((bf16[64,2048]{1,0:T(8,128)(2,1)S(1)}, bf16[64,2048]{1,0:T(8,128)(2,1)S(1)}, u32[]{:S(2)}, u32[]{:S(2)}) %collective-permute-start.8) | collective-permute-done | bytes 262176 | tf_op jit(solution)/shard_map/ppermute | solution.py:18
  43.3 0.9 %fusion.7 = (bf16[64,2048]{1,0:T(8,128)(2,1)S(1)}, f32[2048,64]{0,1:T(8,128)}) fusion(bf16[64,2048]{1,0:T(8,128)(2,1)S(1)} %collective-permute-done.9, bf16[64,2048]{1,0:T(8,128)(2,1)S(1)} %collective-permute-done.8, f32[64,2048]{1,0:T(8,128)S(1)} %get-tuple-element.11, bf16[64,2048]{1,0:T(8,128)(2,1)S(1)} %collective-permute-done.7), kind=kLoop, calls=%fused_computation.12 | loop fusion | flops 917504 | bytes 2097152 | tf_op jit(solution)/shard_map/convert_element_type | solution.py:161
  44.2 5.0 %collective-permute-start.12 = (bf16[64,2048]{1,0:T(8,128)(2,1)S(1)}, bf16[64,2048]{1,0:T(8,128)(2,1)S(1)}, u32[]{:S(2)}, u32[]{:S(2)}) collective-permute-start(bf16[64,2048]{1,0:T(8,128)(2,1)S(1)} %get-tuple-element.20.refs_0_), channel_id=1, source_target_pairs={{0,1},{1,0},{2,3},{3,2},{4,5},{5,4},{6,7},{7,6},{8,9},{9,8},{10,11... | collective-permute-start | bytes 786440 | tf_op jit(solution)/shard_map/ppermute | solution.py:18
  49.1 1.0 %collective-permute-start.11 = (bf16[64,2048]{1,0:T(8,128)(2,1)S(1)}, bf16[64,2048]{1,0:T(8,128)(2,1)S(1)}, u32[]{:S(2)}, u32[]{:S(2)}) collective-permute-start(bf16[64,2048]{1,0:T(8,128)(2,1)S(1)} %get-tuple-element.20.refs_0_), channel_id=1, source_target_pairs={{0,2},{1,3},{2,0},{3,1},{4,6},{5,7},{6,4},{7,5},{8,10},{9,11},{10,... | collective-permute-start | bytes 786440 | tf_op jit(solution)/shard_map/ppermute | solution.py:18
  50.1 1.5 %collective-permute-start.10 = (bf16[64,2048]{1,0:T(8,128)(2,1)S(1)}, bf16[64,2048]{1,0:T(8,128)(2,1)S(1)}, u32[]{:S(2)}, u32[]{:S(2)}) collective-permute-start(bf16[64,2048]{1,0:T(8,128)(2,1)S(1)} %get-tuple-element.20.refs_0_), channel_id=1, source_target_pairs={{0,3},{1,2},{2,1},{3,0},{4,7},{5,6},{6,5},{7,4},{8,11},{9,10},{10,... | collective-permute-start | bytes 786440 | tf_op jit(solution)/shard_map/ppermute | solution.py:18
  51.6 7.2 %collective-permute-done.12.refs_3_ = bf16[64,2048]{1,0:T(8,128)(2,1)S(1)} collective-permute-done((bf16[64,2048]{1,0:T(8,128)(2,1)S(1)}, bf16[64,2048]{1,0:T(8,128)(2,1)S(1)}, u32[]{:S(2)}, u32[]{:S(2)}) %collective-permute-start.12) | collective-permute-done | bytes 262176 | tf_op jit(solution)/shard_map/ppermute | solution.py:18
  58.8 11.7 %collective-permute-done.11.refs_2_ = bf16[64,2048]{1,0:T(8,128)(2,1)S(1)} collective-permute-done((bf16[64,2048]{1,0:T(8,128)(2,1)S(1)}, bf16[64,2048]{1,0:T(8,128)(2,1)S(1)}, u32[]{:S(2)}, u32[]{:S(2)}) %collective-permute-start.11) | collective-permute-done | bytes 262176 | tf_op jit(solution)/shard_map/ppermute | solution.py:18
  70.5 3.1 %partial_adjoint.1 = (f32[32,2048]{1,0:T(8,128)S(1)}, f32[32,2048]{1,0:T(8,128)S(1)}, f32[32,2048]{1,0:T(8,128)S(1)}, f32[32,2048]{1,0:T(8,128)S(1)}, f32[128,2048]{1,0:T(8,128)S(1)}) custom-call(s32[2]{0:T(128)S(1)} %pad_add_fusion.where, bf16[2048,2048]{1,0:T(8,128)(2,1)S(1)} %masked_tiles.1.tiles, bf16[64,2048]{1,0:T(8,128)(2,1)S(1)} %get-tuple-element.20.refs_0_, ...), custom_call_target="tpu_custom_call" | custom-call | flops 2147483648 | bytes 8388608 | tf_op jit(solution)/shard_map/partial_adjoint/pallas_call | solution.py:113
  73.7 0.1 collective-permute-start.13
  73.7 2.6 %collective-permute-done.13 = f32[128,2048]{1,0:T(8,128)S(1)} collective-permute-done((f32[128,2048]{1,0:T(8,128)S(1)}, f32[128,2048]{1,0:T(8,128)S(1)}, u32[]{:S(2)}, u32[]{:S(2)}) %collective-permute-start.13) | collective-permute-done | bytes 1048608 | tf_op jit(solution)/shard_map/ppermute | solution.py:18
  76.4 0.1 fusion.2
  76.5 1.1 %collective-permute-start.14 = (bf16[32,2048]{1,0:T(8,128)(2,1)S(1)}, bf16[32,2048]{1,0:T(8,128)(2,1)S(1)}, u32[]{:S(2)}, u32[]{:S(2)}) collective-permute-start(bf16[32,2048]{1,0:T(8,128)(2,1)S(1)} %get-tuple-element.22), channel_id=1, source_target_pairs={{0,8},{4,12},{8,0},{12,4},{16,24},{20,28},{24,16},{28,20},{1,9},{5... | collective-permute-start | bytes 393224 | tf_op jit(solution)/shard_map/ppermute | solution.py:18
  77.6 1.8 %collective-permute-start.16 = (bf16[32,2048]{1,0:T(8,128)(2,1)S(1)}, bf16[32,2048]{1,0:T(8,128)(2,1)S(1)}, u32[]{:S(2)}, u32[]{:S(2)}) collective-permute-start(bf16[32,2048]{1,0:T(8,128)(2,1)S(1)} %get-tuple-element.23), channel_id=1, source_target_pairs={{0,24},{4,28},{8,16},{12,20},{16,8},{20,12},{24,0},{28,4},{1,25},{... | collective-permute-start | bytes 393224 | tf_op jit(solution)/shard_map/ppermute | solution.py:18
  79.3 0.7 collective-permute-start.15
  80.0 2.9 %collective-permute-done.14 = bf16[32,2048]{1,0:T(8,128)(2,1)S(1)} collective-permute-done((bf16[32,2048]{1,0:T(8,128)(2,1)S(1)}, bf16[32,2048]{1,0:T(8,128)(2,1)S(1)}, u32[]{:S(2)}, u32[]{:S(2)}) %collective-permute-start.14) | collective-permute-done | bytes 131104 | tf_op jit(solution)/shard_map/ppermute | solution.py:18
  82.9 2.9 %collective-permute-done.16 = bf16[32,2048]{1,0:T(8,128)(2,1)S(1)} collective-permute-done((bf16[32,2048]{1,0:T(8,128)(2,1)S(1)}, bf16[32,2048]{1,0:T(8,128)(2,1)S(1)}, u32[]{:S(2)}, u32[]{:S(2)}) %collective-permute-start.16) | collective-permute-done | bytes 131104 | tf_op jit(solution)/shard_map/ppermute | solution.py:18
  85.8 1.4 %collective-permute-done.15 = bf16[32,2048]{1,0:T(8,128)(2,1)S(1)} collective-permute-done((bf16[32,2048]{1,0:T(8,128)(2,1)S(1)}, bf16[32,2048]{1,0:T(8,128)(2,1)S(1)}, u32[]{:S(2)}, u32[]{:S(2)}) %collective-permute-start.15) | collective-permute-done | bytes 131104 | tf_op jit(solution)/shard_map/ppermute | solution.py:18
  87.1 0.8 fusion.6
  (13 shorter events, 0.0 us)
Async XLA Ops:
  0.6 7.2 %collective-permute-start.2 = (bf16[32,2048]{1,0:T(8,128)(2,1)}, bf16[32,2048]{1,0:T(8,128)(2,1)S(1)}, u32[]{:S(2)}, u32[]{:S(2)}) collective-permute-start(bf16[32,2048]{1,0:T(8,128)(2,1)} %bitcast.7), channel_id=1, source_target_pairs={{0,8},{4,12},{8,0},{12,4},{16,24},{20,28},{24,16},{28,20},{1,9},{5... | collective-permute-start | bytes 393224 | tf_op jit(solution)/shard_map/ppermute | solution.py:18
  3.6 8.0 %collective-permute-start.1 = (bf16[32,2048]{1,0:T(8,128)(2,1)}, bf16[32,2048]{1,0:T(8,128)(2,1)S(1)}, u32[]{:S(2)}, u32[]{:S(2)}) collective-permute-start(bf16[32,2048]{1,0:T(8,128)(2,1)} %bitcast.8), channel_id=1, source_target_pairs={{0,16},{4,20},{8,24},{12,28},{16,0},{20,4},{24,8},{28,12},{1,17},{... | collective-permute-start | bytes 393224 | tf_op jit(solution)/shard_map/ppermute | solution.py:18
  5.2 6.5 %collective-permute-start = (bf16[32,2048]{1,0:T(8,128)(2,1)}, bf16[32,2048]{1,0:T(8,128)(2,1)S(1)}, u32[]{:S(2)}, u32[]{:S(2)}) collective-permute-start(bf16[32,2048]{1,0:T(8,128)(2,1)} %bitcast.9), channel_id=1, source_target_pairs={{0,24},{4,28},{8,16},{12,20},{16,8},{20,12},{24,0},{28,4},{1,25},{... | collective-permute-start | bytes 393224 | tf_op jit(solution)/shard_map/ppermute | solution.py:18
  5.2 12.0 %collective-permute-start.3 = (bf16[32,2048]{1,0:T(8,128)(2,1)}, bf16[32,2048]{1,0:T(8,128)(2,1)S(1)}, u32[]{:S(2)}, u32[]{:S(2)}) collective-permute-start(bf16[32,2048]{1,0:T(8,128)(2,1)} %bitcast.10), channel_id=1, source_target_pairs={{0,4},{4,0},{8,12},{12,8},{16,20},{20,16},{24,28},{28,24},{1,5},{5... | collective-permute-start | bytes 393224 | tf_op jit(solution)/shard_map/ppermute | solution.py:18
  7.9 9.3 %collective-permute-start.6 = (bf16[32,2048]{1,0:T(8,128)(2,1)S(1)}, bf16[32,2048]{1,0:T(8,128)(2,1)S(1)}, u32[]{:S(2)}, u32[]{:S(2)}) collective-permute-start(bf16[32,2048]{1,0:T(8,128)(2,1)S(1)} %collective-permute-done.2.refs_3_), channel_id=1, source_target_pairs={{0,4},{4,0},{8,12},{12,8},{16,20},{20,16},{24,28},{28,24},{1,5},{5... | collective-permute-start | bytes 393224 | tf_op jit(solution)/shard_map/ppermute | solution.py:18
  11.6 5.5 %collective-permute-start.5 = (bf16[32,2048]{1,0:T(8,128)(2,1)S(1)}, bf16[32,2048]{1,0:T(8,128)(2,1)S(1)}, u32[]{:S(2)}, u32[]{:S(2)}) collective-permute-start(bf16[32,2048]{1,0:T(8,128)(2,1)S(1)} %collective-permute-done.1.refs_2_), channel_id=1, source_target_pairs={{0,4},{4,0},{8,12},{12,8},{16,20},{20,16},{24,28},{28,24},{1,5},{5... | collective-permute-start | bytes 393224 | tf_op jit(solution)/shard_map/ppermute | solution.py:18
  11.6 5.5 %collective-permute-start.4 = (bf16[32,2048]{1,0:T(8,128)(2,1)S(1)}, bf16[32,2048]{1,0:T(8,128)(2,1)S(1)}, u32[]{:S(2)}, u32[]{:S(2)}) collective-permute-start(bf16[32,2048]{1,0:T(8,128)(2,1)S(1)} %collective-permute-done.refs_1_), channel_id=1, source_target_pairs={{0,4},{4,0},{8,12},{12,8},{16,20},{20,16},{24,28},{28,24},{1,5},{5... | collective-permute-start | bytes 393224 | tf_op jit(solution)/shard_map/ppermute | solution.py:18
  12.1 0.7 copy-start.1
  12.8 4.3 %copy-start = (bf16[2048,32]{0,1:T(8,128)(2,1)S(1)}, bf16[2048,32]{0,1:T(8,128)(2,1)}, u32[]{:S(2)}) copy-start(bf16[2048,32]{0,1:T(8,128)(2,1)} %param.5) | copy-start | bytes 393220
  20.2 13.1 %collective-permute-start.7 = (bf16[64,2048]{1,0:T(8,128)(2,1)S(1)}, bf16[64,2048]{1,0:T(8,128)(2,1)S(1)}, u32[]{:S(2)}, u32[]{:S(2)}) collective-permute-start(bf16[64,2048]{1,0:T(8,128)(2,1)S(1)} %get-tuple-element.12), channel_id=1, source_target_pairs={{0,1},{1,0},{2,3},{3,2},{4,5},{5,4},{6,7},{7,6},{8,9},{9,8},{10,11... | collective-permute-start | bytes 786440 | tf_op jit(solution)/shard_map/ppermute | solution.py:18
  21.9 21.3 %collective-permute-start.8 = (bf16[64,2048]{1,0:T(8,128)(2,1)S(1)}, bf16[64,2048]{1,0:T(8,128)(2,1)S(1)}, u32[]{:S(2)}, u32[]{:S(2)}) collective-permute-start(bf16[64,2048]{1,0:T(8,128)(2,1)S(1)} %get-tuple-element.13), channel_id=1, source_target_pairs={{0,2},{1,3},{2,0},{3,1},{4,6},{5,7},{6,4},{7,5},{8,10},{9,11},{10,... | collective-permute-start | bytes 786440 | tf_op jit(solution)/shard_map/ppermute | solution.py:18
  24.6 18.7 %collective-permute-start.9 = (bf16[64,2048]{1,0:T(8,128)(2,1)S(1)}, bf16[64,2048]{1,0:T(8,128)(2,1)S(1)}, u32[]{:S(2)}, u32[]{:S(2)}) collective-permute-start(bf16[64,2048]{1,0:T(8,128)(2,1)S(1)} %get-tuple-element.14), channel_id=1, source_target_pairs={{0,3},{1,2},{2,1},{3,0},{4,7},{5,6},{6,5},{7,4},{8,11},{9,10},{10,... | collective-permute-start | bytes 786440 | tf_op jit(solution)/shard_map/ppermute | solution.py:18
  44.2 14.6 %collective-permute-start.12 = (bf16[64,2048]{1,0:T(8,128)(2,1)S(1)}, bf16[64,2048]{1,0:T(8,128)(2,1)S(1)}, u32[]{:S(2)}, u32[]{:S(2)}) collective-permute-start(bf16[64,2048]{1,0:T(8,128)(2,1)S(1)} %get-tuple-element.20.refs_0_), channel_id=1, source_target_pairs={{0,1},{1,0},{2,3},{3,2},{4,5},{5,4},{6,7},{7,6},{8,9},{9,8},{10,11... | collective-permute-start | bytes 786440 | tf_op jit(solution)/shard_map/ppermute | solution.py:18
  49.1 21.4 %collective-permute-start.11 = (bf16[64,2048]{1,0:T(8,128)(2,1)S(1)}, bf16[64,2048]{1,0:T(8,128)(2,1)S(1)}, u32[]{:S(2)}, u32[]{:S(2)}) collective-permute-start(bf16[64,2048]{1,0:T(8,128)(2,1)S(1)} %get-tuple-element.20.refs_0_), channel_id=1, source_target_pairs={{0,2},{1,3},{2,0},{3,1},{4,6},{5,7},{6,4},{7,5},{8,10},{9,11},{10,... | collective-permute-start | bytes 786440 | tf_op jit(solution)/shard_map/ppermute | solution.py:18
  50.1 20.4 %collective-permute-start.10 = (bf16[64,2048]{1,0:T(8,128)(2,1)S(1)}, bf16[64,2048]{1,0:T(8,128)(2,1)S(1)}, u32[]{:S(2)}, u32[]{:S(2)}) collective-permute-start(bf16[64,2048]{1,0:T(8,128)(2,1)S(1)} %get-tuple-element.20.refs_0_), channel_id=1, source_target_pairs={{0,3},{1,2},{2,1},{3,0},{4,7},{5,6},{6,5},{7,4},{8,11},{9,10},{10,... | collective-permute-start | bytes 786440 | tf_op jit(solution)/shard_map/ppermute | solution.py:18
  73.7 2.7 %collective-permute-start.13 = (f32[128,2048]{1,0:T(8,128)S(1)}, f32[128,2048]{1,0:T(8,128)S(1)}, u32[]{:S(2)}, u32[]{:S(2)}) collective-permute-start(f32[128,2048]{1,0:T(8,128)S(1)} %get-tuple-element.16), channel_id=1, source_target_pairs={{0,4},{4,0},{8,12},{12,8},{16,20},{20,16},{24,28},{28,24},{1,5},{5... | collective-permute-start | bytes 3145736 | tf_op jit(solution)/shard_map/ppermute | solution.py:18
  76.5 6.4 %collective-permute-start.14 = (bf16[32,2048]{1,0:T(8,128)(2,1)S(1)}, bf16[32,2048]{1,0:T(8,128)(2,1)S(1)}, u32[]{:S(2)}, u32[]{:S(2)}) collective-permute-start(bf16[32,2048]{1,0:T(8,128)(2,1)S(1)} %get-tuple-element.22), channel_id=1, source_target_pairs={{0,8},{4,12},{8,0},{12,4},{16,24},{20,28},{24,16},{28,20},{1,9},{5... | collective-permute-start | bytes 393224 | tf_op jit(solution)/shard_map/ppermute | solution.py:18
  77.6 8.2 %collective-permute-start.16 = (bf16[32,2048]{1,0:T(8,128)(2,1)S(1)}, bf16[32,2048]{1,0:T(8,128)(2,1)S(1)}, u32[]{:S(2)}, u32[]{:S(2)}) collective-permute-start(bf16[32,2048]{1,0:T(8,128)(2,1)S(1)} %get-tuple-element.23), channel_id=1, source_target_pairs={{0,24},{4,28},{8,16},{12,20},{16,8},{20,12},{24,0},{28,4},{1,25},{... | collective-permute-start | bytes 393224 | tf_op jit(solution)/shard_map/ppermute | solution.py:18
  79.3 7.8 %collective-permute-start.15 = (bf16[32,2048]{1,0:T(8,128)(2,1)S(1)}, bf16[32,2048]{1,0:T(8,128)(2,1)S(1)}, u32[]{:S(2)}, u32[]{:S(2)}) collective-permute-start(bf16[32,2048]{1,0:T(8,128)(2,1)S(1)} %get-tuple-element.24), channel_id=1, source_target_pairs={{0,16},{4,20},{8,24},{12,28},{16,0},{20,4},{24,8},{28,12},{1,17},{... | collective-permute-start | bytes 393224 | tf_op jit(solution)/shard_map/ppermute | solution.py:18

commit v5 on v4

--- a/solution.py
+++ b/solution.py
@@ -16,6 +16,10 @@
 def exchange(value, axis, offset):
     size = lax.axis_size(axis)
     return lax.ppermute(value, axis, [(i, i ^ offset) for i in range(size)])
+
+
+def after(value, *earlier):
+    return lax.optimization_barrier((value, earlier))[0]
 
 
 def mask_kernel(mask_ref, green_ref, tiles, sems, *, block):
@@ -80,7 +84,7 @@
         scratch_shapes=[pltpu.VMEM((width, cols), BF16), pltpu.VMEM((width, rows), F32)],
         compiler_params=pltpu.CompilerParams(vmem_limit_bytes=VMEM_LIMIT),
         cost_estimate=pl.CostEstimate(
-            flops=2 * width * cols * rows, bytes_accessed=2 * rows * cols, transcendentals=0
+            flops=2 * width * cols * rows, bytes_accessed=4 * width * (rows + cols), transcendentals=0
         ),
         name="partial_sketch",
     )(where, tiles, *blocks)
@@ -118,7 +122,7 @@
         scratch_shapes=[pltpu.VMEM((width, rows), BF16), pltpu.VMEM((width, cols), F32)],
         compiler_params=pltpu.CompilerParams(vmem_limit_bytes=VMEM_LIMIT),
         cost_estimate=pl.CostEstimate(
-            flops=2 * width * cols * rows, bytes_accessed=2 * rows * cols, transcendentals=0
+            flops=2 * width * cols * rows, bytes_accessed=4 * width * (rows + cols), transcendentals=0
         ),
         name="partial_adjoint",
     )(where, tiles, *shares)
@@ -148,6 +152,7 @@
     for chunk in range(chunks):
         own = probes.T[chunk * piece : (chunk + 1) * piece]
         held = [own] + [exchange(own, "row", offset) for offset in gather_core[1:]]
+        held = after(held, tiles)
         blocks.append(held + [exchange(block, "row", 1) for block in held])
 
     sketches, adjoints = [], []

time: 88.8 us -> 91.6 us (1.032)
  local copies, waits for them, and re-layouts: 0.69 us -> 7.31 us
  waiting for transfers between devices: 53.7 us -> 48.2 us
  starting transfers between devices: 20.6 us -> 21.8 us
    unnamed x4 -> x8, local copies, waits for them, and re-layouts: 0.69 us -> 7.31 us
    ppermute x17, waiting for transfers between devices: 53.7 us -> 48.2 us  [exchange(): return lax.ppermute(value, axis, [(i, i ^ offset) for i in range(size)])]
    ppermute x17, starting transfers between devices: 20.6 us -> 21.8 us  [exchange(): return lax.ppermute(value, axis, [(i, i ^ offset) for i in range(size)])]
  transfers between devices with their start and end apart: 17 -> 17, of which waited for: 10 -> 12; matrix products, arithmetic and copies ran while one was open for 0% -> 0% of each run, Pallas kernels for 5% -> 5%
where the time goes in v5:
time: 91.6 us; the launch traced here: 90.3 us
  waiting for transfers between devices  48.2 us (53%)
  starting transfers between devices  21.8 us (24%)
  Pallas kernels  10.3 us (11%)
  local copies, waits for them, and re-layouts  7.31 us (8%)
  other arithmetic  1.88 us (2%)
    ppermute x17, waiting for transfers between devices, exchange(): return lax.ppermute(value, axis, [(i, i ^ offset) for i in range(size)])  48.2 us
    ppermute x17, starting transfers between devices, exchange(): return lax.ppermute(value, axis, [(i, i ^ offset) for i in range(size)])  21.8 us
    unnamed x8, local copies, waits for them, and re-layouts  7.31 us
    pallas_call x1, Pallas kernels, masked(): pl.pallas_call(functools.partial(mask_kernel, block=rows // mask.shape[0]...  4.24 us
    pallas_call x1, Pallas kernels, partial_adjoint(): pl.pallas_call(functools.partial(adjoint_kernel, offsets_col=offsets_col,...  3.06 us
    pallas_call x1, Pallas kernels, partial_sketch(): pl.pallas_call(functools.partial(sketch_kernel, offsets_row=offsets_row,...  3.02 us
  transfers between devices with their start and end apart: 17, of which 12 were waited for; matrix products, arithmetic and copies ran while one was open for 0% of the time, Pallas kernels for 5%

profile of v5, /device:TPU:0, one launch (start us, length us, event | category | flops | bytes accessed | tf_op | source)
XLA Modules:
  0.0 90.3 jit_solution(11323049701453435012)
XLA Ops:
  0.6 3.0 %collective-permute-start.2 = (bf16[32,2048]{1,0:T(8,128)(2,1)}, bf16[32,2048]{1,0:T(8,128)(2,1)S(1)}, u32[]{:S(2)}, u32[]{:S(2)}) collective-permute-start(bf16[32,2048]{1,0:T(8,128)(2,1)} %bitcast.7), channel_id=1, source_target_pairs={{0,8},{4,12},{8,0},{12,4},{16,24},{20,28},{24,16},{28,20},{1,9},{5... | collective-permute-start | bytes 393224 | tf_op jit(solution)/shard_map/ppermute | solution.py:18
  3.6 1.5 %collective-permute-start.1 = (bf16[32,2048]{1,0:T(8,128)(2,1)}, bf16[32,2048]{1,0:T(8,128)(2,1)S(1)}, u32[]{:S(2)}, u32[]{:S(2)}) collective-permute-start(bf16[32,2048]{1,0:T(8,128)(2,1)} %bitcast.8), channel_id=1, source_target_pairs={{0,16},{4,20},{8,24},{12,28},{16,0},{20,4},{24,8},{28,12},{1,17},{... | collective-permute-start | bytes 393224 | tf_op jit(solution)/shard_map/ppermute | solution.py:18
  5.2 0.7 copy-done.3
  5.9 4.2 %masked_tiles.1.tiles = bf16[2048,2048]{1,0:T(8,128)(2,1)S(1)} custom-call(s32[8,8]{1,0:T(8,128)S(1)} %copy-done.3, bf16[2048,2048]{1,0:T(8,128)(2,1)} %green_ref.1), custom_call_target="tpu_custom_call" | custom-call | bytes 8388608 | tf_op jit(solution)/shard_map/masked_tiles/pallas_call | solution.py:44
  10.1 3.2 %copy-done = bf16[2048,2048]{1,0:T(8,128)(2,1)} copy-done((bf16[2048,2048]{1,0:T(8,128)(2,1)}, bf16[2048,2048]{1,0:T(8,128)(2,1)S(1)}, u32[]{:S(2)}) %copy-start) | copy-done | bytes 8388632
  13.5 0.5 collective-permute-start.4
  14.0 0.4 collective-permute-start.6
  14.6 0.3 collective-permute-done.3.refs_4_
  14.8 0.2 collective-permute-done.4.refs_5_
  15.0 0.3 collective-permute-done.5.refs_6_
  15.3 0.2 collective-permute-done.6.refs_7_
  15.5 3.4 %copy-done.1 = bf16[2048,2048]{1,0:T(8,128)(2,1)S(1)} copy-done((bf16[2048,2048]{1,0:T(8,128)(2,1)S(1)}, bf16[2048,2048]{1,0:T(8,128)(2,1)}, u32[]{:S(2)}) %copy-start.1) | copy-done | bytes 8388632
  18.9 3.0 %partial_sketch.1 = (f32[64,2048]{1,0:T(8,128)S(1)}, bf16[64,2048]{1,0:T(8,128)(2,1)S(1)}, bf16[64,2048]{1,0:T(8,128)(2,1)S(1)}, bf16[64,2048]{1,0:T(8,128)(2,1)S(1)}) custom-call(s32[2]{0:T(128)S(1)} %pad_add_fusion.where, bf16[2048,2048]{1,0:T(8,128)(2,1)S(1)} %copy-done.1, bf16[32,2048]{1,0:T(8,128)(2,1)S(1)} %bitcast.11, ...), custom_call_target="tpu_custom_call" | custom-call | flops 2147483648 | bytes 4194304 | tf_op jit(solution)/shard_map/partial_sketch/pallas_call | solution.py:79
  21.9 2.2 %collective-permute-start.7 = (bf16[64,2048]{1,0:T(8,128)(2,1)S(1)}, bf16[64,2048]{1,0:T(8,128)(2,1)S(1)}, u32[]{:S(2)}, u32[]{:S(2)}) collective-permute-start(bf16[64,2048]{1,0:T(8,128)(2,1)S(1)} %get-tuple-element.20), channel_id=1, source_target_pairs={{0,1},{1,0},{2,3},{3,2},{4,5},{5,4},{6,7},{7,6},{8,9},{9,8},{10,11... | collective-permute-start | bytes 786440 | tf_op jit(solution)/shard_map/ppermute | solution.py:18
  24.1 2.6 %collective-permute-start.8 = (bf16[64,2048]{1,0:T(8,128)(2,1)S(1)}, bf16[64,2048]{1,0:T(8,128)(2,1)S(1)}, u32[]{:S(2)}, u32[]{:S(2)}) collective-permute-start(bf16[64,2048]{1,0:T(8,128)(2,1)S(1)} %get-tuple-element.21), channel_id=1, source_target_pairs={{0,2},{1,3},{2,0},{3,1},{4,6},{5,7},{6,4},{7,5},{8,10},{9,11},{10,... | collective-permute-start | bytes 786440 | tf_op jit(solution)/shard_map/ppermute | solution.py:18
  26.7 9.3 %collective-permute-done.7 = bf16[64,2048]{1,0:T(8,128)(2,1)S(1)} collective-permute-done((bf16[64,2048]{1,0:T(8,128)(2,1)S(1)}, bf16[64,2048]{1,0:T(8,128)(2,1)S(1)}, u32[]{:S(2)}, u32[]{:S(2)}) %collective-permute-start.7) | collective-permute-done | bytes 262176 | tf_op jit(solution)/shard_map/ppermute | solution.py:18
  36.0 9.4 %collective-permute-done.8 = bf16[64,2048]{1,0:T(8,128)(2,1)S(1)} collective-permute-done((bf16[64,2048]{1,0:T(8,128)(2,1)S(1)}, bf16[64,2048]{1,0:T(8,128)(2,1)S(1)}, u32[]{:S(2)}, u32[]{:S(2)}) %collective-permute-start.8) | collective-permute-done | bytes 262176 | tf_op jit(solution)/shard_map/ppermute | solution.py:18
  45.4 0.9 %fusion.7 = (bf16[64,2048]{1,0:T(8,128)(2,1)S(1)}, f32[2048,64]{0,1:T(8,128)}) fusion(bf16[64,2048]{1,0:T(8,128)(2,1)S(1)} %collective-permute-done.9, bf16[64,2048]{1,0:T(8,128)(2,1)S(1)} %collective-permute-done.8, f32[64,2048]{1,0:T(8,128)S(1)} %get-tuple-element.19, bf16[64,2048]{1,0:T(8,128)(2,1)S(1)} %collective-permute-done.7), kind=kLoop, calls=%fused_computation.12 | loop fusion | flops 917504 | bytes 2097152 | tf_op jit(solution)/shard_map/convert_element_type | solution.py:166
  46.4 5.3 %collective-permute-start.12 = (bf16[64,2048]{1,0:T(8,128)(2,1)S(1)}, bf16[64,2048]{1,0:T(8,128)(2,1)S(1)}, u32[]{:S(2)}, u32[]{:S(2)}) collective-permute-start(bf16[64,2048]{1,0:T(8,128)(2,1)S(1)} %get-tuple-element.28.refs_0_), channel_id=1, source_target_pairs={{0,1},{1,0},{2,3},{3,2},{4,5},{5,4},{6,7},{7,6},{8,9},{9,8},{10,11... | collective-permute-start | bytes 786440 | tf_op jit(solution)/shard_map/ppermute | solution.py:18
  51.6 1.1 %collective-permute-start.11 = (bf16[64,2048]{1,0:T(8,128)(2,1)S(1)}, bf16[64,2048]{1,0:T(8,128)(2,1)S(1)}, u32[]{:S(2)}, u32[]{:S(2)}) collective-permute-start(bf16[64,2048]{1,0:T(8,128)(2,1)S(1)} %get-tuple-element.28.refs_0_), channel_id=1, source_target_pairs={{0,2},{1,3},{2,0},{3,1},{4,6},{5,7},{6,4},{7,5},{8,10},{9,11},{10,... | collective-permute-start | bytes 786440 | tf_op jit(solution)/shard_map/ppermute | solution.py:18
  52.7 1.5 %collective-permute-start.10 = (bf16[64,2048]{1,0:T(8,128)(2,1)S(1)}, bf16[64,2048]{1,0:T(8,128)(2,1)S(1)}, u32[]{:S(2)}, u32[]{:S(2)}) collective-permute-start(bf16[64,2048]{1,0:T(8,128)(2,1)S(1)} %get-tuple-element.28.refs_0_), channel_id=1, source_target_pairs={{0,3},{1,2},{2,1},{3,0},{4,7},{5,6},{6,5},{7,4},{8,11},{9,10},{10,... | collective-permute-start | bytes 786440 | tf_op jit(solution)/shard_map/ppermute | solution.py:18
  54.1 7.7 %collective-permute-done.12.refs_3_ = bf16[64,2048]{1,0:T(8,128)(2,1)S(1)} collective-permute-done((bf16[64,2048]{1,0:T(8,128)(2,1)S(1)}, bf16[64,2048]{1,0:T(8,128)(2,1)S(1)}, u32[]{:S(2)}, u32[]{:S(2)}) %collective-permute-start.12) | collective-permute-done | bytes 262176 | tf_op jit(solution)/shard_map/ppermute | solution.py:18
  61.8 11.2 %collective-permute-done.11.refs_2_ = bf16[64,2048]{1,0:T(8,128)(2,1)S(1)} collective-permute-done((bf16[64,2048]{1,0:T(8,128)(2,1)S(1)}, bf16[64,2048]{1,0:T(8,128)(2,1)S(1)}, u32[]{:S(2)}, u32[]{:S(2)}) %collective-permute-start.11) | collective-permute-done | bytes 262176 | tf_op jit(solution)/shard_map/ppermute | solution.py:18
  73.0 3.1 %partial_adjoint.1 = (f32[32,2048]{1,0:T(8,128)S(1)}, f32[32,2048]{1,0:T(8,128)S(1)}, f32[32,2048]{1,0:T(8,128)S(1)}, f32[32,2048]{1,0:T(8,128)S(1)}, f32[128,2048]{1,0:T(8,128)S(1)}) custom-call(s32[2]{0:T(128)S(1)} %pad_add_fusion.where, bf16[2048,2048]{1,0:T(8,128)(2,1)S(1)} %copy-done.1, bf16[64,2048]{1,0:T(8,128)(2,1)S(1)} %get-tuple-element.28.refs_0_, ...), custom_call_target="tpu_custom_call" | custom-call | flops 2147483648 | bytes 4194304 | tf_op jit(solution)/shard_map/partial_adjoint/pallas_call | solution.py:117
  76.1 2.6 %collective-permute-done.13 = f32[128,2048]{1,0:T(8,128)S(1)} collective-permute-done((f32[128,2048]{1,0:T(8,128)S(1)}, f32[128,2048]{1,0:T(8,128)S(1)}, u32[]{:S(2)}, u32[]{:S(2)}) %collective-permute-start.13) | collective-permute-done | bytes 1048608 | tf_op jit(solution)/shard_map/ppermute | solution.py:18
  78.9 1.5 %collective-permute-start.14 = (bf16[32,2048]{1,0:T(8,128)(2,1)S(1)}, bf16[32,2048]{1,0:T(8,128)(2,1)S(1)}, u32[]{:S(2)}, u32[]{:S(2)}) collective-permute-start(bf16[32,2048]{1,0:T(8,128)(2,1)S(1)} %get-tuple-element.30), channel_id=1, source_target_pairs={{0,8},{4,12},{8,0},{12,4},{16,24},{20,28},{24,16},{28,20},{1,9},{5... | collective-permute-start | bytes 393224 | tf_op jit(solution)/shard_map/ppermute | solution.py:18
  80.4 1.4 %collective-permute-start.16 = (bf16[32,2048]{1,0:T(8,128)(2,1)S(1)}, bf16[32,2048]{1,0:T(8,128)(2,1)S(1)}, u32[]{:S(2)}, u32[]{:S(2)}) collective-permute-start(bf16[32,2048]{1,0:T(8,128)(2,1)S(1)} %get-tuple-element.31), channel_id=1, source_target_pairs={{0,24},{4,28},{8,16},{12,20},{16,8},{20,12},{24,0},{28,4},{1,25},{... | collective-permute-start | bytes 393224 | tf_op jit(solution)/shard_map/ppermute | solution.py:18
  81.7 0.7 collective-permute-start.15
  82.5 2.9 %collective-permute-done.14 = bf16[32,2048]{1,0:T(8,128)(2,1)S(1)} collective-permute-done((bf16[32,2048]{1,0:T(8,128)(2,1)S(1)}, bf16[32,2048]{1,0:T(8,128)(2,1)S(1)}, u32[]{:S(2)}, u32[]{:S(2)}) %collective-permute-start.14) | collective-permute-done | bytes 131104 | tf_op jit(solution)/shard_map/ppermute | solution.py:18
  85.3 2.9 %collective-permute-done.16 = bf16[32,2048]{1,0:T(8,128)(2,1)S(1)} collective-permute-done((bf16[32,2048]{1,0:T(8,128)(2,1)S(1)}, bf16[32,2048]{1,0:T(8,128)(2,1)S(1)}, u32[]{:S(2)}, u32[]{:S(2)}) %collective-permute-start.16) | collective-permute-done | bytes 131104 | tf_op jit(solution)/shard_map/ppermute | solution.py:18
  88.2 1.4 %collective-permute-done.15 = bf16[32,2048]{1,0:T(8,128)(2,1)S(1)} collective-permute-done((bf16[32,2048]{1,0:T(8,128)(2,1)S(1)}, bf16[32,2048]{1,0:T(8,128)(2,1)S(1)}, u32[]{:S(2)}, u32[]{:S(2)}) %collective-permute-start.15) | collective-permute-done | bytes 131104 | tf_op jit(solution)/shard_map/ppermute | solution.py:18
  89.5 0.8 fusion.6
  (17 shorter events, 0.4 us)
Async XLA Ops:
  0.6 12.8 %copy-start.2 = (bf16[2048,32]{0,1:T(8,128)(2,1)S(1)}, bf16[2048,32]{0,1:T(8,128)(2,1)}, u32[]{:S(2)}) copy-start(bf16[2048,32]{0,1:T(8,128)(2,1)} %param.5) | copy-start | bytes 393220
  0.6 12.7 %collective-permute-start.2 = (bf16[32,2048]{1,0:T(8,128)(2,1)}, bf16[32,2048]{1,0:T(8,128)(2,1)S(1)}, u32[]{:S(2)}, u32[]{:S(2)}) collective-permute-start(bf16[32,2048]{1,0:T(8,128)(2,1)} %bitcast.7), channel_id=1, source_target_pairs={{0,8},{4,12},{8,0},{12,4},{16,24},{20,28},{24,16},{28,20},{1,9},{5... | collective-permute-start | bytes 393224 | tf_op jit(solution)/shard_map/ppermute | solution.py:18
  3.6 9.7 %collective-permute-start.1 = (bf16[32,2048]{1,0:T(8,128)(2,1)}, bf16[32,2048]{1,0:T(8,128)(2,1)S(1)}, u32[]{:S(2)}, u32[]{:S(2)}) collective-permute-start(bf16[32,2048]{1,0:T(8,128)(2,1)} %bitcast.8), channel_id=1, source_target_pairs={{0,16},{4,20},{8,24},{12,28},{16,0},{20,4},{24,8},{28,12},{1,17},{... | collective-permute-start | bytes 393224 | tf_op jit(solution)/shard_map/ppermute | solution.py:18
  5.2 8.2 %collective-permute-start = (bf16[32,2048]{1,0:T(8,128)(2,1)}, bf16[32,2048]{1,0:T(8,128)(2,1)S(1)}, u32[]{:S(2)}, u32[]{:S(2)}) collective-permute-start(bf16[32,2048]{1,0:T(8,128)(2,1)} %bitcast.9), channel_id=1, source_target_pairs={{0,24},{4,28},{8,16},{12,20},{16,8},{20,12},{24,0},{28,4},{1,25},{... | collective-permute-start | bytes 393224 | tf_op jit(solution)/shard_map/ppermute | solution.py:18
  5.2 0.7 copy-start.3
  10.1 3.2 %copy-start = (bf16[2048,2048]{1,0:T(8,128)(2,1)}, bf16[2048,2048]{1,0:T(8,128)(2,1)S(1)}, u32[]{:S(2)}) copy-start(bf16[2048,2048]{1,0:T(8,128)(2,1)S(1)} %masked_tiles.1.tiles) | copy-start | bytes 25165828
  13.4 1.4 %collective-permute-start.3 = (bf16[32,2048]{1,0:T(8,128)(2,1)S(1)}, bf16[32,2048]{1,0:T(8,128)(2,1)S(1)}, u32[]{:S(2)}, u32[]{:S(2)}) collective-permute-start(bf16[32,2048]{1,0:T(8,128)(2,1)S(1)} %bitcast.10), channel_id=1, source_target_pairs={{0,4},{4,0},{8,12},{12,8},{16,20},{20,16},{24,28},{28,24},{1,5},{5... | collective-permute-start | bytes 393224 | tf_op jit(solution)/shard_map/ppermute | solution.py:18
  13.5 1.5 %collective-permute-start.4 = (bf16[32,2048]{1,0:T(8,128)(2,1)S(1)}, bf16[32,2048]{1,0:T(8,128)(2,1)S(1)}, u32[]{:S(2)}, u32[]{:S(2)}) collective-permute-start(bf16[32,2048]{1,0:T(8,128)(2,1)S(1)} %collective-permute-done.refs_1_), channel_id=1, source_target_pairs={{0,4},{4,0},{8,12},{12,8},{16,20},{20,16},{24,28},{28,24},{1,5},{5... | collective-permute-start | bytes 393224 | tf_op jit(solution)/shard_map/ppermute | solution.py:18
  14.0 1.3 %collective-permute-start.5 = (bf16[32,2048]{1,0:T(8,128)(2,1)S(1)}, bf16[32,2048]{1,0:T(8,128)(2,1)S(1)}, u32[]{:S(2)}, u32[]{:S(2)}) collective-permute-start(bf16[32,2048]{1,0:T(8,128)(2,1)S(1)} %collective-permute-done.1.refs_2_), channel_id=1, source_target_pairs={{0,4},{4,0},{8,12},{12,8},{16,20},{20,16},{24,28},{28,24},{1,5},{5... | collective-permute-start | bytes 393224 | tf_op jit(solution)/shard_map/ppermute | solution.py:18
  14.0 1.5 %collective-permute-start.6 = (bf16[32,2048]{1,0:T(8,128)(2,1)S(1)}, bf16[32,2048]{1,0:T(8,128)(2,1)S(1)}, u32[]{:S(2)}, u32[]{:S(2)}) collective-permute-start(bf16[32,2048]{1,0:T(8,128)(2,1)S(1)} %collective-permute-done.2.refs_3_), channel_id=1, source_target_pairs={{0,4},{4,0},{8,12},{12,8},{16,20},{20,16},{24,28},{28,24},{1,5},{5... | collective-permute-start | bytes 393224 | tf_op jit(solution)/shard_map/ppermute | solution.py:18
  15.5 3.4 %copy-start.1 = (bf16[2048,2048]{1,0:T(8,128)(2,1)S(1)}, bf16[2048,2048]{1,0:T(8,128)(2,1)}, u32[]{:S(2)}) copy-start(bf16[2048,2048]{1,0:T(8,128)(2,1)} %copy-done) | copy-start | bytes 25165828
  21.9 14.1 %collective-permute-start.7 = (bf16[64,2048]{1,0:T(8,128)(2,1)S(1)}, bf16[64,2048]{1,0:T(8,128)(2,1)S(1)}, u32[]{:S(2)}, u32[]{:S(2)}) collective-permute-start(bf16[64,2048]{1,0:T(8,128)(2,1)S(1)} %get-tuple-element.20), channel_id=1, source_target_pairs={{0,1},{1,0},{2,3},{3,2},{4,5},{5,4},{6,7},{7,6},{8,9},{9,8},{10,11... | collective-permute-start | bytes 786440 | tf_op jit(solution)/shard_map/ppermute | solution.py:18
  24.1 21.3 %collective-permute-start.8 = (bf16[64,2048]{1,0:T(8,128)(2,1)S(1)}, bf16[64,2048]{1,0:T(8,128)(2,1)S(1)}, u32[]{:S(2)}, u32[]{:S(2)}) collective-permute-start(bf16[64,2048]{1,0:T(8,128)(2,1)S(1)} %get-tuple-element.21), channel_id=1, source_target_pairs={{0,2},{1,3},{2,0},{3,1},{4,6},{5,7},{6,4},{7,5},{8,10},{9,11},{10,... | collective-permute-start | bytes 786440 | tf_op jit(solution)/shard_map/ppermute | solution.py:18
  26.7 18.7 %collective-permute-start.9 = (bf16[64,2048]{1,0:T(8,128)(2,1)S(1)}, bf16[64,2048]{1,0:T(8,128)(2,1)S(1)}, u32[]{:S(2)}, u32[]{:S(2)}) collective-permute-start(bf16[64,2048]{1,0:T(8,128)(2,1)S(1)} %get-tuple-element.22), channel_id=1, source_target_pairs={{0,3},{1,2},{2,1},{3,0},{4,7},{5,6},{6,5},{7,4},{8,11},{9,10},{10,... | collective-permute-start | bytes 786440 | tf_op jit(solution)/shard_map/ppermute | solution.py:18
  46.4 15.5 %collective-permute-start.12 = (bf16[64,2048]{1,0:T(8,128)(2,1)S(1)}, bf16[64,2048]{1,0:T(8,128)(2,1)S(1)}, u32[]{:S(2)}, u32[]{:S(2)}) collective-permute-start(bf16[64,2048]{1,0:T(8,128)(2,1)S(1)} %get-tuple-element.28.refs_0_), channel_id=1, source_target_pairs={{0,1},{1,0},{2,3},{3,2},{4,5},{5,4},{6,7},{7,6},{8,9},{9,8},{10,11... | collective-permute-start | bytes 786440 | tf_op jit(solution)/shard_map/ppermute | solution.py:18
  51.6 21.4 %collective-permute-start.11 = (bf16[64,2048]{1,0:T(8,128)(2,1)S(1)}, bf16[64,2048]{1,0:T(8,128)(2,1)S(1)}, u32[]{:S(2)}, u32[]{:S(2)}) collective-permute-start(bf16[64,2048]{1,0:T(8,128)(2,1)S(1)} %get-tuple-element.28.refs_0_), channel_id=1, source_target_pairs={{0,2},{1,3},{2,0},{3,1},{4,6},{5,7},{6,4},{7,5},{8,10},{9,11},{10,... | collective-permute-start | bytes 786440 | tf_op jit(solution)/shard_map/ppermute | solution.py:18
  52.7 20.3 %collective-permute-start.10 = (bf16[64,2048]{1,0:T(8,128)(2,1)S(1)}, bf16[64,2048]{1,0:T(8,128)(2,1)S(1)}, u32[]{:S(2)}, u32[]{:S(2)}) collective-permute-start(bf16[64,2048]{1,0:T(8,128)(2,1)S(1)} %get-tuple-element.28.refs_0_), channel_id=1, source_target_pairs={{0,3},{1,2},{2,1},{3,0},{4,7},{5,6},{6,5},{7,4},{8,11},{9,10},{10,... | collective-permute-start | bytes 786440 | tf_op jit(solution)/shard_map/ppermute | solution.py:18
  76.1 2.7 %collective-permute-start.13 = (f32[128,2048]{1,0:T(8,128)S(1)}, f32[128,2048]{1,0:T(8,128)S(1)}, u32[]{:S(2)}, u32[]{:S(2)}) collective-permute-start(f32[128,2048]{1,0:T(8,128)S(1)} %get-tuple-element.24), channel_id=1, source_target_pairs={{0,4},{4,0},{8,12},{12,8},{16,20},{20,16},{24,28},{28,24},{1,5},{5... | collective-permute-start | bytes 3145736 | tf_op jit(solution)/shard_map/ppermute | solution.py:18
  78.9 6.4 %collective-permute-start.14 = (bf16[32,2048]{1,0:T(8,128)(2,1)S(1)}, bf16[32,2048]{1,0:T(8,128)(2,1)S(1)}, u32[]{:S(2)}, u32[]{:S(2)}) collective-permute-start(bf16[32,2048]{1,0:T(8,128)(2,1)S(1)} %get-tuple-element.30), channel_id=1, source_target_pairs={{0,8},{4,12},{8,0},{12,4},{16,24},{20,28},{24,16},{28,20},{1,9},{5... | collective-permute-start | bytes 393224 | tf_op jit(solution)/shard_map/ppermute | solution.py:18
  80.4 7.8 %collective-permute-start.16 = (bf16[32,2048]{1,0:T(8,128)(2,1)S(1)}, bf16[32,2048]{1,0:T(8,128)(2,1)S(1)}, u32[]{:S(2)}, u32[]{:S(2)}) collective-permute-start(bf16[32,2048]{1,0:T(8,128)(2,1)S(1)} %get-tuple-element.31), channel_id=1, source_target_pairs={{0,24},{4,28},{8,16},{12,20},{16,8},{20,12},{24,0},{28,4},{1,25},{... | collective-permute-start | bytes 393224 | tf_op jit(solution)/shard_map/ppermute | solution.py:18
  81.7 7.8 %collective-permute-start.15 = (bf16[32,2048]{1,0:T(8,128)(2,1)S(1)}, bf16[32,2048]{1,0:T(8,128)(2,1)S(1)}, u32[]{:S(2)}, u32[]{:S(2)}) collective-permute-start(bf16[32,2048]{1,0:T(8,128)(2,1)S(1)} %get-tuple-element.32), channel_id=1, source_target_pairs={{0,16},{4,20},{8,24},{12,28},{16,0},{20,4},{24,8},{28,12},{1,17},{... | collective-permute-start | bytes 393224 | tf_op jit(solution)/shard_map/ppermute | solution.py:18

commit v6 on v5

v6 whole, which is shorter than its diff:
```python
import functools

import jax
import jax.numpy as jnp
from jax import lax
from jax.experimental import pallas as pl
from jax.experimental.pallas import tpu as pltpu
from jax.sharding import PartitionSpec as P

F32, BF16 = jnp.float32, jnp.bfloat16
VMEM_LIMIT = 28 * 2**20
STEP = 512
CHUNKS = 2


def exchange(value, axis, offset):
    size = lax.axis_size(axis)
    return lax.ppermute(value, axis, [(i, i ^ offset) for i in range(size)])


def mask_kernel(mask_ref, green_ref, tiles, token, sems, *, block):
    rows, cols = tiles.shape
    token[...] = jnp.zeros(token.shape, token.dtype)
    copies = []
    for step in range(rows // STEP):
        at = pl.ds(step * STEP, STEP)
        copies.append(pltpu.make_async_copy(green_ref.at[at], tiles.at[at], sems.at[step]))
        copies[-1].start()
    for step, copy in enumerate(copies):
        copy.wait()
        for i in range(step * STEP // block, (step + 1) * STEP // block):
            for j in range(cols // block):

                @pl.when(mask_ref[i, j] == 0)
                def _():
                    tiles[i * block : (i + 1) * block, j * block : (j + 1) * block] = jnp.zeros((block, block), BF16)


def masked(green, mask):
    rows, cols = green.shape
    return pl.pallas_call(
        functools.partial(mask_kernel, block=rows // mask.shape[0]),
        in_specs=[pl.BlockSpec(memory_space=pltpu.SMEM), pl.BlockSpec(memory_space=pltpu.HBM)],
        out_specs=[pl.BlockSpec(memory_space=pltpu.VMEM)] * 2,
        out_shape=[pltpu.VMEM((rows, cols), BF16), jax.ShapeDtypeStruct((8, 128), F32)],
        scratch_shapes=[pltpu.SemaphoreType.DMA((rows // STEP,))],
        compiler_params=pltpu.CompilerParams(vmem_limit_bytes=VMEM_LIMIT),
        cost_estimate=pl.CostEstimate(flops=0, bytes_accessed=2 * rows * cols, transcendentals=0),
        name="masked_tiles",
    )(mask, pltpu.with_memory_space_constraint(green, pltpu.HBM))


def sketch_kernel(where, tiles, token, *refs, offsets_row, offsets_col, piece):
    blocks, outs = refs[: len(offsets_row)], refs[len(offsets_row) : -2]
    probes, total = refs[-2:]
    width = blocks[0].shape[0]
    for offset, ref in zip(offsets_row, blocks):
        start = pl.multiple_of((where[0] ^ offset) * width, width)
        probes[pl.ds(start, width), :] = ref[...]
    for step in range(tiles.shape[0] // STEP):
        at = slice(step * STEP, (step + 1) * STEP)
        total[:, at] = lax.dot_general(
            probes[...], tiles[at, :], (((1,), (1,)), ((), ())), preferred_element_type=F32
        )
    share = total.shape[0] // len(offsets_col)
    for k, out in enumerate(outs):
        chunk, offset = k // len(offsets_col), offsets_col[k % len(offsets_col)]
        for n in range(out.shape[0] // piece):
            start = pl.multiple_of((where[1] ^ offset) * share + n * width + chunk * piece, piece)
            out[n * piece : (n + 1) * piece, :] = total[pl.ds(start, piece), :].astype(out.dtype)


def partial_sketch(where, tiles, blocks, token, offsets_row, offsets_col, chunks):
    rows, cols = tiles.shape
    width = blocks[0].shape[0] * len(blocks)
    share = width // len(offsets_col) // chunks
    vmem = pl.BlockSpec(memory_space=pltpu.VMEM)
    outs = [jax.ShapeDtypeStruct((share, rows), F32 if offset == 0 else BF16) for offset in offsets_col] * chunks
    return pl.pallas_call(
        functools.partial(
            sketch_kernel, offsets_row=offsets_row, offsets_col=offsets_col, piece=blocks[0].shape[0] // chunks
        ),
        in_specs=[pl.BlockSpec(memory_space=pltpu.SMEM)] + [vmem] * (2 + len(blocks)),
        out_specs=[vmem] * len(outs),
        out_shape=outs,
        scratch_shapes=[pltpu.VMEM((width, cols), BF16), pltpu.VMEM((width, rows), F32)],
        compiler_params=pltpu.CompilerParams(vmem_limit_bytes=VMEM_LIMIT),
        cost_estimate=pl.CostEstimate(
            flops=2 * width * cols * rows, bytes_accessed=4 * width * (rows + cols), transcendentals=0
        ),
        name="partial_sketch",
    )(where, tiles, token, *blocks)


def adjoint_kernel(where, tiles, *refs, offsets_col, offsets_core, chunks):
    count = len(offsets_col) * chunks
    shares, outs = refs[:count], refs[count:-2]
    lowered, total = refs[-2:]
    share = shares[0].shape[0] * chunks
    width = outs[0].shape[0]
    piece = width // chunks
    for k, ref in enumerate(shares):
        chunk, offset = k // len(offsets_col), offsets_col[k % len(offsets_col)]
        for n in range(ref.shape[0] // piece):
            start = pl.multiple_of((where[1] ^ offset) * share + n * width + chunk * piece, piece)
            lowered[pl.ds(start, piece), :] = ref[n * piece : (n + 1) * piece, :]
    for step in range(tiles.shape[1] // STEP):
        at = slice(step * STEP, (step + 1) * STEP)
        total[:, at] = jnp.dot(lowered[...], tiles[:, at], preferred_element_type=F32)
    sibling = outs[-1]
    for k, offset in enumerate(offsets_core):
        start = pl.multiple_of((where[0] ^ offset) * width, width)
        outs[k][...] = total[pl.ds(start, width), :]
        start = pl.multiple_of((where[0] ^ 1 ^ offset) * width, width)
        sibling[k * width : (k + 1) * width, :] = total[pl.ds(start, width), :].astype(sibling.dtype)


def partial_adjoint(where, tiles, shares, offsets_col, offsets_core, width, chunks):
    rows, cols = tiles.shape
    own = width // (2 * len(offsets_core))
    heights = [own] * len(offsets_core) + [own * len(offsets_core)]
    vmem = pl.BlockSpec(memory_space=pltpu.VMEM)
    return pl.pallas_call(
        functools.partial(adjoint_kernel, offsets_col=offsets_col, offsets_core=offsets_core, chunks=chunks),
        in_specs=[pl.BlockSpec(memory_space=pltpu.SMEM)] + [vmem] * (1 + len(shares)),
        out_specs=[vmem] * len(heights),
        out_shape=[jax.ShapeDtypeStruct((h, cols), F32) for h in heights],
        scratch_shapes=[pltpu.VMEM((width, rows), BF16), pltpu.VMEM((width, cols), F32)],
        compiler_params=pltpu.CompilerParams(vmem_limit_bytes=VMEM_LIMIT),
        cost_estimate=pl.CostEstimate(
            flops=2 * width * cols * rows, bytes_accessed=4 * width * (rows + cols), transcendentals=0
        ),
        name="partial_adjoint",
    )(where, tiles, *shares)


def join(parts, group):
    length = parts[0].shape[1]
    return jnp.concatenate([p.reshape(-1, group, length) for p in parts], axis=1).reshape(-1, length)


def local(green, mask, probes):
    n_row, n_col = lax.axis_size("row"), lax.axis_size("col")
    where = jnp.stack([lax.axis_index("row"), lax.axis_index("col")]).astype(jnp.int32)
    own_width = probes.shape[1]
    chunks = CHUNKS if own_width % (16 * CHUNKS) == 0 and n_row % n_col == 0 else 1
    piece = own_width // chunks
    width = own_width * n_row
    offsets_col = list(range(n_col))
    offsets_core = list(range(0, n_row, 2))
    gather_core = [0] + offsets_core[:0:-1]
    offsets_row = gather_core + [offset ^ 1 for offset in gather_core]
    far_first = [0] + offsets_col[:0:-1]

    tiles, token = masked(green, mask)

    own = probes.T
    held = [own] + [exchange(own, "row", offset) for offset in gather_core[1:]]
    held, token = lax.optimization_barrier((held, token))
    blocks = held + [exchange(block, "row", 1) for block in held]

    parts = partial_sketch(where, tiles, blocks, token, offsets_row, offsets_col, chunks)
    totals, shares = [], []
    for chunk in range(chunks):
        terms = parts[chunk * n_col : (chunk + 1) * n_col]
        total = terms[0]
        for offset in offsets_col[1:]:
            total = total + exchange(terms[offset], "col", offset).astype(F32)
        totals.append(total)
        lowered = total.astype(BF16)
        shares.append([lowered] + [exchange(lowered, "col", offset) for offset in far_first[1:]])

    flat = [share for per_chunk in shares for share in per_chunk]
    *mine, others = partial_adjoint(where, tiles, flat, far_first, offsets_core, width, chunks)
    others = exchange(others, "row", 1)
    pairs = [m + others[k * own_width : (k + 1) * own_width] for k, m in enumerate(mine)]
    adjoint = pairs[0]
    for offset, pair in zip(offsets_core[1:], pairs[1:]):
        adjoint = adjoint + exchange(pair.astype(BF16), "row", offset).astype(F32)
    return join(totals, piece).T, adjoint.T


def solution(mesh):
    in_specs = (P("row", "col"), P("row", "col"), P("col", "row"))
    out_specs = (P("row", "col"), P("col", "row"))
    return jax.shard_map(local, mesh=mesh, in_specs=in_specs, out_specs=out_specs, check_vma=False)
```

time: 91.6 us -> 88.3 us (0.964); the launches traced: 90.3 us -> 88.1 us
  waiting for transfers between devices: 48.2 us -> 23.7 us
  starting transfers between devices: 21.8 us -> 44.1 us
    ppermute x17 -> x23, waiting for transfers between devices: 48.2 us -> 23.7 us  [exchange(): return lax.ppermute(value, axis, [(i, i ^ offset) for i in range(size)])]
    ppermute x17 -> x23, starting transfers between devices: 21.8 us -> 44.1 us  [exchange(): return lax.ppermute(value, axis, [(i, i ^ offset) for i in range(size)])]
  transfers between devices with their start and end apart: 17 -> 23, of which waited for: 12 -> 11; matrix products, arithmetic and copies ran while one was open for 0% -> 1% of each run, Pallas kernels for 5% -> 5%
where the time goes in v6:
time: 88.3 us; the launch traced here: 88.1 us
  starting transfers between devices  44.1 us (50%)
  waiting for transfers between devices  23.7 us (27%)
  Pallas kernels  10.3 us (12%)
  local copies, waits for them, and re-layouts  7.33 us (8%)
  other arithmetic  1.91 us (2%)
    ppermute x23, starting transfers between devices, exchange(): return lax.ppermute(value, axis, [(i, i ^ offset) for i in range(size)])  44.1 us
    ppermute x23, waiting for transfers between devices, exchange(): return lax.ppermute(value, axis, [(i, i ^ offset) for i in range(size)])  23.7 us
    unnamed x8, local copies, waits for them, and re-layouts  7.33 us
    pallas_call x1, Pallas kernels, masked(): pl.pallas_call(functools.partial(mask_kernel, block=rows // mask.shape[0]...  4.22 us
    pallas_call x1, Pallas kernels, partial_adjoint(): pl.pallas_call(functools.partial(adjoint_kernel, offsets_col=offsets_col,...  3.07 us
    pallas_call x1, Pallas kernels, partial_sketch(): pl.pallas_call(functools.partial(sketch_kernel, offsets_row=offsets_row,...  3.02 us
  transfers between devices with their start and end apart: 23, of which 11 were waited for; matrix products, arithmetic and copies ran while one was open for 1% of the time, Pallas kernels for 5%

profile of v6, /device:TPU:0, one launch (start us, length us, event | category | flops | bytes accessed | tf_op | source)
XLA Modules:
  0.0 88.1 jit_solution(14534537196400949498)
XLA Ops:
  0.6 3.0 %collective-permute-start.2 = (bf16[32,2048]{1,0:T(8,128)(2,1)}, bf16[32,2048]{1,0:T(8,128)(2,1)S(1)}, u32[]{:S(2)}, u32[]{:S(2)}) collective-permute-start(bf16[32,2048]{1,0:T(8,128)(2,1)} %bitcast.10), channel_id=1, source_target_pairs={{0,8},{4,12},{8,0},{12,4},{16,24},{20,28},{24,16},{28,20},{1,9},{5... | collective-permute-start | bytes 393224 | tf_op jit(solution)/shard_map/ppermute | solution.py:18
  3.6 1.5 %collective-permute-start.1 = (bf16[32,2048]{1,0:T(8,128)(2,1)}, bf16[32,2048]{1,0:T(8,128)(2,1)S(1)}, u32[]{:S(2)}, u32[]{:S(2)}) collective-permute-start(bf16[32,2048]{1,0:T(8,128)(2,1)} %bitcast.11), channel_id=1, source_target_pairs={{0,16},{4,20},{8,24},{12,28},{16,0},{20,4},{24,8},{28,12},{1,17},{... | collective-permute-start | bytes 393224 | tf_op jit(solution)/shard_map/ppermute | solution.py:18
  5.2 0.7 copy-done.3
  5.9 4.2 %masked_tiles.1 = (bf16[2048,2048]{1,0:T(8,128)(2,1)S(1)}, f32[8,128]{1,0:T(8,128)S(1)}) custom-call(s32[8,8]{1,0:T(8,128)S(1)} %copy-done.3, bf16[2048,2048]{1,0:T(8,128)(2,1)} %green_ref.1), custom_call_target="tpu_custom_call" | custom-call | bytes 8388608 | tf_op jit(solution)/shard_map/masked_tiles/pallas_call | solution.py:41
  10.1 3.3 %copy-done = bf16[2048,2048]{1,0:T(8,128)(2,1)} copy-done((bf16[2048,2048]{1,0:T(8,128)(2,1)}, bf16[2048,2048]{1,0:T(8,128)(2,1)S(1)}, u32[]{:S(2)}) %copy-start) | copy-done | bytes 8388632
  13.5 0.5 collective-permute-start.4
  15.5 3.4 %copy-done.1 = bf16[2048,2048]{1,0:T(8,128)(2,1)S(1)} copy-done((bf16[2048,2048]{1,0:T(8,128)(2,1)S(1)}, bf16[2048,2048]{1,0:T(8,128)(2,1)}, u32[]{:S(2)}) %copy-start.1) | copy-done | bytes 8388632
  18.9 3.0 %partial_sketch.1 = (f32[32,2048]{1,0:T(8,128)S(1)}, bf16[32,2048]{1,0:T(8,128)(2,1)S(1)}, bf16[32,2048]{1,0:T(8,128)(2,1)S(1)}, bf16[32,2048]{1,0:T(8,128)(2,1)...) custom-call(s32[2]{0:T(128)S(1)} %pad_add_fusion.where, ...), custom_call_target="tpu_custom_call" | custom-call | flops 2147483648 | bytes 4194304 | tf_op jit(solution)/shard_map/partial_sketch/pallas_call | solution.py:79
  21.9 2.2 %collective-permute-start.7 = (bf16[32,2048]{1,0:T(8,128)(2,1)S(1)}, bf16[32,2048]{1,0:T(8,128)(2,1)S(1)}, u32[]{:S(2)}, u32[]{:S(2)}) collective-permute-start(bf16[32,2048]{1,0:T(8,128)(2,1)S(1)} %get-tuple-element.30), channel_id=1, source_target_pairs={{0,1},{1,0},{2,3},{3,2},{4,5},{5,4},{6,7},{7,6},{8,9},{9,8},{10,11... | collective-permute-start | bytes 393224 | tf_op jit(solution)/shard_map/ppermute | solution.py:18
  24.1 2.6 %collective-permute-start.8 = (bf16[32,2048]{1,0:T(8,128)(2,1)S(1)}, bf16[32,2048]{1,0:T(8,128)(2,1)S(1)}, u32[]{:S(2)}, u32[]{:S(2)}) collective-permute-start(bf16[32,2048]{1,0:T(8,128)(2,1)S(1)} %get-tuple-element.31), channel_id=1, source_target_pairs={{0,2},{1,3},{2,0},{3,1},{4,6},{5,7},{6,4},{7,5},{8,10},{9,11},{10,... | collective-permute-start | bytes 393224 | tf_op jit(solution)/shard_map/ppermute | solution.py:18
  26.7 0.8 collective-permute-start.10
  27.6 3.5 %collective-permute-start.11 = (bf16[32,2048]{1,0:T(8,128)(2,1)S(1)}, bf16[32,2048]{1,0:T(8,128)(2,1)S(1)}, u32[]{:S(2)}, u32[]{:S(2)}) collective-permute-start(bf16[32,2048]{1,0:T(8,128)(2,1)S(1)} %get-tuple-element.35), channel_id=1, source_target_pairs={{0,2},{1,3},{2,0},{3,1},{4,6},{5,7},{6,4},{7,5},{8,10},{9,11},{10,... | collective-permute-start | bytes 393224 | tf_op jit(solution)/shard_map/ppermute | solution.py:18
  31.1 2.9 %collective-permute-start.12 = (bf16[32,2048]{1,0:T(8,128)(2,1)S(1)}, bf16[32,2048]{1,0:T(8,128)(2,1)S(1)}, u32[]{:S(2)}, u32[]{:S(2)}) collective-permute-start(bf16[32,2048]{1,0:T(8,128)(2,1)S(1)} %get-tuple-element.36), channel_id=1, source_target_pairs={{0,3},{1,2},{2,1},{3,0},{4,7},{5,6},{6,5},{7,4},{8,11},{9,10},{10,... | collective-permute-start | bytes 393224 | tf_op jit(solution)/shard_map/ppermute | solution.py:18
  34.0 3.0 %collective-permute-done.8 = bf16[32,2048]{1,0:T(8,128)(2,1)S(1)} collective-permute-done((bf16[32,2048]{1,0:T(8,128)(2,1)S(1)}, bf16[32,2048]{1,0:T(8,128)(2,1)S(1)}, u32[]{:S(2)}, u32[]{:S(2)}) %collective-permute-start.8) | collective-permute-done | bytes 131104 | tf_op jit(solution)/shard_map/ppermute | solution.py:18
  37.1 9.1 %collective-permute-start.15 = (bf16[32,2048]{1,0:T(8,128)(2,1)S(1)}, bf16[32,2048]{1,0:T(8,128)(2,1)S(1)}, u32[]{:S(2)}, u32[]{:S(2)}) collective-permute-start(bf16[32,2048]{1,0:T(8,128)(2,1)S(1)} %get-tuple-element.44.refs_0_), channel_id=1, source_target_pairs={{0,1},{1,0},{2,3},{3,2},{4,5},{5,4},{6,7},{7,6},{8,9},{9,8},{10,11... | collective-permute-start | bytes 393224 | tf_op jit(solution)/shard_map/ppermute | solution.py:18
  46.1 1.2 %collective-permute-start.14 = (bf16[32,2048]{1,0:T(8,128)(2,1)S(1)}, bf16[32,2048]{1,0:T(8,128)(2,1)S(1)}, u32[]{:S(2)}, u32[]{:S(2)}) collective-permute-start(bf16[32,2048]{1,0:T(8,128)(2,1)S(1)} %get-tuple-element.44.refs_0_), channel_id=1, source_target_pairs={{0,2},{1,3},{2,0},{3,1},{4,6},{5,7},{6,4},{7,5},{8,10},{9,11},{10,... | collective-permute-start | bytes 393224 | tf_op jit(solution)/shard_map/ppermute | solution.py:18
  47.3 1.4 %collective-permute-start.13 = (bf16[32,2048]{1,0:T(8,128)(2,1)S(1)}, bf16[32,2048]{1,0:T(8,128)(2,1)S(1)}, u32[]{:S(2)}, u32[]{:S(2)}) collective-permute-start(bf16[32,2048]{1,0:T(8,128)(2,1)S(1)} %get-tuple-element.44.refs_0_), channel_id=1, source_target_pairs={{0,3},{1,2},{2,1},{3,0},{4,7},{5,6},{6,5},{7,4},{8,11},{9,10},{10,... | collective-permute-start | bytes 393224 | tf_op jit(solution)/shard_map/ppermute | solution.py:18
  48.8 8.6 %collective-permute-start.18 = (bf16[32,2048]{1,0:T(8,128)(2,1)S(1)}, bf16[32,2048]{1,0:T(8,128)(2,1)S(1)}, u32[]{:S(2)}, u32[]{:S(2)}) collective-permute-start(bf16[32,2048]{1,0:T(8,128)(2,1)S(1)} %get-tuple-element.42.refs_4_), channel_id=1, source_target_pairs={{0,1},{1,0},{2,3},{3,2},{4,5},{5,4},{6,7},{7,6},{8,9},{9,8},{10,11... | collective-permute-start | bytes 393224 | tf_op jit(solution)/shard_map/ppermute | solution.py:18
  57.4 1.2 %collective-permute-start.17 = (bf16[32,2048]{1,0:T(8,128)(2,1)S(1)}, bf16[32,2048]{1,0:T(8,128)(2,1)S(1)}, u32[]{:S(2)}, u32[]{:S(2)}) collective-permute-start(bf16[32,2048]{1,0:T(8,128)(2,1)S(1)} %get-tuple-element.42.refs_4_), channel_id=1, source_target_pairs={{0,2},{1,3},{2,0},{3,1},{4,6},{5,7},{6,4},{7,5},{8,10},{9,11},{10,... | collective-permute-start | bytes 393224 | tf_op jit(solution)/shard_map/ppermute | solution.py:18
  58.6 1.4 %collective-permute-start.16 = (bf16[32,2048]{1,0:T(8,128)(2,1)S(1)}, bf16[32,2048]{1,0:T(8,128)(2,1)S(1)}, u32[]{:S(2)}, u32[]{:S(2)}) collective-permute-start(bf16[32,2048]{1,0:T(8,128)(2,1)S(1)} %get-tuple-element.42.refs_4_), channel_id=1, source_target_pairs={{0,3},{1,2},{2,1},{3,0},{4,7},{5,6},{6,5},{7,4},{8,11},{9,10},{10,... | collective-permute-start | bytes 393224 | tf_op jit(solution)/shard_map/ppermute | solution.py:18
  60.0 1.3 %collective-permute-done.18.refs_7_ = bf16[32,2048]{1,0:T(8,128)(2,1)S(1)} collective-permute-done((bf16[32,2048]{1,0:T(8,128)(2,1)S(1)}, bf16[32,2048]{1,0:T(8,128)(2,1)S(1)}, u32[]{:S(2)}, u32[]{:S(2)}) %collective-permute-start.18) | collective-permute-done | bytes 131104 | tf_op jit(solution)/shard_map/ppermute | solution.py:18
  61.3 9.5 %collective-permute-done.17.refs_6_ = bf16[32,2048]{1,0:T(8,128)(2,1)S(1)} collective-permute-done((bf16[32,2048]{1,0:T(8,128)(2,1)S(1)}, bf16[32,2048]{1,0:T(8,128)(2,1)S(1)}, u32[]{:S(2)}, u32[]{:S(2)}) %collective-permute-start.17) | collective-permute-done | bytes 131104 | tf_op jit(solution)/shard_map/ppermute | solution.py:18
  70.7 3.1 %partial_adjoint.1 = (f32[32,2048]{1,0:T(8,128)S(1)}, f32[32,2048]{1,0:T(8,128)S(1)}, f32[32,2048]{1,0:T(8,128)S(1)}, f32[32,2048]{1,0:T(8,128)S(1)}, f32[128,2048]{1,0:T(8,128)S(1)}) custom-call(s32[2]{0:T(128)S(1)} %pad_add_fusion.where, bf16[2048,2048]{1,0:T(8,128)(2,1)S(1)} %copy-done.1, bf16[32,2048]{1,0:T(8,128)(2,1)S(1)} %get-tuple-element.44.refs_0_, ...), custom_call_target="tpu_custom_call" | custom-call | flops 2147483648 | bytes 4194304 | tf_op jit(solution)/shard_map/partial_adjoint/pallas_call | solution.py:123
  73.9 2.6 %collective-permute-done.19 = f32[128,2048]{1,0:T(8,128)S(1)} collective-permute-done((f32[128,2048]{1,0:T(8,128)S(1)}, f32[128,2048]{1,0:T(8,128)S(1)}, u32[]{:S(2)}, u32[]{:S(2)}) %collective-permute-start.19) | collective-permute-done | bytes 1048608 | tf_op jit(solution)/shard_map/ppermute | solution.py:18
  76.6 1.4 %collective-permute-start.20 = (bf16[32,2048]{1,0:T(8,128)(2,1)S(1)}, bf16[32,2048]{1,0:T(8,128)(2,1)S(1)}, u32[]{:S(2)}, u32[]{:S(2)}) collective-permute-start(bf16[32,2048]{1,0:T(8,128)(2,1)S(1)} %get-tuple-element.46), channel_id=1, source_target_pairs={{0,8},{4,12},{8,0},{12,4},{16,24},{20,28},{24,16},{28,20},{1,9},{5... | collective-permute-start | bytes 393224 | tf_op jit(solution)/shard_map/ppermute | solution.py:18
  78.0 1.5 %collective-permute-start.22 = (bf16[32,2048]{1,0:T(8,128)(2,1)S(1)}, bf16[32,2048]{1,0:T(8,128)(2,1)S(1)}, u32[]{:S(2)}, u32[]{:S(2)}) collective-permute-start(bf16[32,2048]{1,0:T(8,128)(2,1)S(1)} %get-tuple-element.47), channel_id=1, source_target_pairs={{0,24},{4,28},{8,16},{12,20},{16,8},{20,12},{24,0},{28,4},{1,25},{... | collective-permute-start | bytes 393224 | tf_op jit(solution)/shard_map/ppermute | solution.py:18
  79.5 0.7 collective-permute-start.21
  80.2 0.8 pad_maximum_fusion
  81.0 2.0 %collective-permute-done.20 = bf16[32,2048]{1,0:T(8,128)(2,1)S(1)} collective-permute-done((bf16[32,2048]{1,0:T(8,128)(2,1)S(1)}, bf16[32,2048]{1,0:T(8,128)(2,1)S(1)}, u32[]{:S(2)}, u32[]{:S(2)}) %collective-permute-start.20) | collective-permute-done | bytes 131104 | tf_op jit(solution)/shard_map/ppermute | solution.py:18
  83.0 3.0 %collective-permute-done.22 = bf16[32,2048]{1,0:T(8,128)(2,1)S(1)} collective-permute-done((bf16[32,2048]{1,0:T(8,128)(2,1)S(1)}, bf16[32,2048]{1,0:T(8,128)(2,1)S(1)}, u32[]{:S(2)}, u32[]{:S(2)}) %collective-permute-start.22) | collective-permute-done | bytes 131104 | tf_op jit(solution)/shard_map/ppermute | solution.py:18
  86.0 1.4 %collective-permute-done.21 = bf16[32,2048]{1,0:T(8,128)(2,1)S(1)} collective-permute-done((bf16[32,2048]{1,0:T(8,128)(2,1)S(1)}, bf16[32,2048]{1,0:T(8,128)(2,1)S(1)}, u32[]{:S(2)}, u32[]{:S(2)}) %collective-permute-start.21) | collective-permute-done | bytes 131104 | tf_op jit(solution)/shard_map/ppermute | solution.py:18
  87.3 0.8 fusion.6
  (31 shorter events, 2.0 us)
Async XLA Ops:
  0.6 12.8 %copy-start.2 = (bf16[2048,32]{0,1:T(8,128)(2,1)S(1)}, bf16[2048,32]{0,1:T(8,128)(2,1)}, u32[]{:S(2)}) copy-start(bf16[2048,32]{0,1:T(8,128)(2,1)} %param.5) | copy-start | bytes 393220
  0.6 12.7 %collective-permute-start.2 = (bf16[32,2048]{1,0:T(8,128)(2,1)}, bf16[32,2048]{1,0:T(8,128)(2,1)S(1)}, u32[]{:S(2)}, u32[]{:S(2)}) collective-permute-start(bf16[32,2048]{1,0:T(8,128)(2,1)} %bitcast.10), channel_id=1, source_target_pairs={{0,8},{4,12},{8,0},{12,4},{16,24},{20,28},{24,16},{28,20},{1,9},{5... | collective-permute-start | bytes 393224 | tf_op jit(solution)/shard_map/ppermute | solution.py:18
  3.6 9.7 %collective-permute-start.1 = (bf16[32,2048]{1,0:T(8,128)(2,1)}, bf16[32,2048]{1,0:T(8,128)(2,1)S(1)}, u32[]{:S(2)}, u32[]{:S(2)}) collective-permute-start(bf16[32,2048]{1,0:T(8,128)(2,1)} %bitcast.11), channel_id=1, source_target_pairs={{0,16},{4,20},{8,24},{12,28},{16,0},{20,4},{24,8},{28,12},{1,17},{... | collective-permute-start | bytes 393224 | tf_op jit(solution)/shard_map/ppermute | solution.py:18
  5.2 8.2 %collective-permute-start = (bf16[32,2048]{1,0:T(8,128)(2,1)}, bf16[32,2048]{1,0:T(8,128)(2,1)S(1)}, u32[]{:S(2)}, u32[]{:S(2)}) collective-permute-start(bf16[32,2048]{1,0:T(8,128)(2,1)} %bitcast.12), channel_id=1, source_target_pairs={{0,24},{4,28},{8,16},{12,20},{16,8},{20,12},{24,0},{28,4},{1,25},{... | collective-permute-start | bytes 393224 | tf_op jit(solution)/shard_map/ppermute | solution.py:18
  5.2 0.7 copy-start.3
  10.1 3.3 %copy-start = (bf16[2048,2048]{1,0:T(8,128)(2,1)}, bf16[2048,2048]{1,0:T(8,128)(2,1)S(1)}, u32[]{:S(2)}) copy-start(bf16[2048,2048]{1,0:T(8,128)(2,1)S(1)} %get-tuple-element.22.tiles) | copy-start | bytes 25165828
  13.4 1.4 %collective-permute-start.3 = (bf16[32,2048]{1,0:T(8,128)(2,1)S(1)}, bf16[32,2048]{1,0:T(8,128)(2,1)S(1)}, u32[]{:S(2)}, u32[]{:S(2)}) collective-permute-start(bf16[32,2048]{1,0:T(8,128)(2,1)S(1)} %bitcast.13), channel_id=1, source_target_pairs={{0,4},{4,0},{8,12},{12,8},{16,20},{20,16},{24,28},{28,24},{1,5},{5... | collective-permute-start | bytes 393224 | tf_op jit(solution)/shard_map/ppermute | solution.py:18
  13.5 1.5 %collective-permute-start.4 = (bf16[32,2048]{1,0:T(8,128)(2,1)S(1)}, bf16[32,2048]{1,0:T(8,128)(2,1)S(1)}, u32[]{:S(2)}, u32[]{:S(2)}) collective-permute-start(bf16[32,2048]{1,0:T(8,128)(2,1)S(1)} %collective-permute-done.refs_1_), channel_id=1, source_target_pairs={{0,4},{4,0},{8,12},{12,8},{16,20},{20,16},{24,28},{28,24},{1,5},{5... | collective-permute-start | bytes 393224 | tf_op jit(solution)/shard_map/ppermute | solution.py:18
  14.0 1.3 %collective-permute-start.5 = (bf16[32,2048]{1,0:T(8,128)(2,1)S(1)}, bf16[32,2048]{1,0:T(8,128)(2,1)S(1)}, u32[]{:S(2)}, u32[]{:S(2)}) collective-permute-start(bf16[32,2048]{1,0:T(8,128)(2,1)S(1)} %collective-permute-done.1.refs_2_), channel_id=1, source_target_pairs={{0,4},{4,0},{8,12},{12,8},{16,20},{20,16},{24,28},{28,24},{1,5},{5... | collective-permute-start | bytes 393224 | tf_op jit(solution)/shard_map/ppermute | solution.py:18
  14.0 1.5 %collective-permute-start.6 = (bf16[32,2048]{1,0:T(8,128)(2,1)S(1)}, bf16[32,2048]{1,0:T(8,128)(2,1)S(1)}, u32[]{:S(2)}, u32[]{:S(2)}) collective-permute-start(bf16[32,2048]{1,0:T(8,128)(2,1)S(1)} %collective-permute-done.2.refs_3_), channel_id=1, source_target_pairs={{0,4},{4,0},{8,12},{12,8},{16,20},{20,16},{24,28},{28,24},{1,5},{5... | collective-permute-start | bytes 393224 | tf_op jit(solution)/shard_map/ppermute | solution.py:18
  15.5 3.4 %copy-start.1 = (bf16[2048,2048]{1,0:T(8,128)(2,1)S(1)}, bf16[2048,2048]{1,0:T(8,128)(2,1)}, u32[]{:S(2)}) copy-start(bf16[2048,2048]{1,0:T(8,128)(2,1)} %copy-done) | copy-start | bytes 25165828
  21.9 9.2 %collective-permute-start.7 = (bf16[32,2048]{1,0:T(8,128)(2,1)S(1)}, bf16[32,2048]{1,0:T(8,128)(2,1)S(1)}, u32[]{:S(2)}, u32[]{:S(2)}) collective-permute-start(bf16[32,2048]{1,0:T(8,128)(2,1)S(1)} %get-tuple-element.30), channel_id=1, source_target_pairs={{0,1},{1,0},{2,3},{3,2},{4,5},{5,4},{6,7},{7,6},{8,9},{9,8},{10,11... | collective-permute-start | bytes 393224 | tf_op jit(solution)/shard_map/ppermute | solution.py:18
  24.1 12.9 %collective-permute-start.8 = (bf16[32,2048]{1,0:T(8,128)(2,1)S(1)}, bf16[32,2048]{1,0:T(8,128)(2,1)S(1)}, u32[]{:S(2)}, u32[]{:S(2)}) collective-permute-start(bf16[32,2048]{1,0:T(8,128)(2,1)S(1)} %get-tuple-element.31), channel_id=1, source_target_pairs={{0,2},{1,3},{2,0},{3,1},{4,6},{5,7},{6,4},{7,5},{8,10},{9,11},{10,... | collective-permute-start | bytes 393224 | tf_op jit(solution)/shard_map/ppermute | solution.py:18
  26.7 10.3 %collective-permute-start.9 = (bf16[32,2048]{1,0:T(8,128)(2,1)S(1)}, bf16[32,2048]{1,0:T(8,128)(2,1)S(1)}, u32[]{:S(2)}, u32[]{:S(2)}) collective-permute-start(bf16[32,2048]{1,0:T(8,128)(2,1)S(1)} %get-tuple-element.32), channel_id=1, source_target_pairs={{0,3},{1,2},{2,1},{3,0},{4,7},{5,6},{6,5},{7,4},{8,11},{9,10},{10,... | collective-permute-start | bytes 393224 | tf_op jit(solution)/shard_map/ppermute | solution.py:18
  26.7 20.6 %collective-permute-start.10 = (bf16[32,2048]{1,0:T(8,128)(2,1)S(1)}, bf16[32,2048]{1,0:T(8,128)(2,1)S(1)}, u32[]{:S(2)}, u32[]{:S(2)}) collective-permute-start(bf16[32,2048]{1,0:T(8,128)(2,1)S(1)} %get-tuple-element.34), channel_id=1, source_target_pairs={{0,1},{1,0},{2,3},{3,2},{4,5},{5,4},{6,7},{7,6},{8,9},{9,8},{10,11... | collective-permute-start | bytes 393224 | tf_op jit(solution)/shard_map/ppermute | solution.py:18
  27.6 21.1 %collective-permute-start.11 = (bf16[32,2048]{1,0:T(8,128)(2,1)S(1)}, bf16[32,2048]{1,0:T(8,128)(2,1)S(1)}, u32[]{:S(2)}, u32[]{:S(2)}) collective-permute-start(bf16[32,2048]{1,0:T(8,128)(2,1)S(1)} %get-tuple-element.35), channel_id=1, source_target_pairs={{0,2},{1,3},{2,0},{3,1},{4,6},{5,7},{6,4},{7,5},{8,10},{9,11},{10,... | collective-permute-start | bytes 393224 | tf_op jit(solution)/shard_map/ppermute | solution.py:18
  31.1 17.6 %collective-permute-start.12 = (bf16[32,2048]{1,0:T(8,128)(2,1)S(1)}, bf16[32,2048]{1,0:T(8,128)(2,1)S(1)}, u32[]{:S(2)}, u32[]{:S(2)}) collective-permute-start(bf16[32,2048]{1,0:T(8,128)(2,1)S(1)} %get-tuple-element.36), channel_id=1, source_target_pairs={{0,3},{1,2},{2,1},{3,0},{4,7},{5,6},{6,5},{7,4},{8,11},{9,10},{10,... | collective-permute-start | bytes 393224 | tf_op jit(solution)/shard_map/ppermute | solution.py:18
  37.1 21.5 %collective-permute-start.15 = (bf16[32,2048]{1,0:T(8,128)(2,1)S(1)}, bf16[32,2048]{1,0:T(8,128)(2,1)S(1)}, u32[]{:S(2)}, u32[]{:S(2)}) collective-permute-start(bf16[32,2048]{1,0:T(8,128)(2,1)S(1)} %get-tuple-element.44.refs_0_), channel_id=1, source_target_pairs={{0,1},{1,0},{2,3},{3,2},{4,5},{5,4},{6,7},{7,6},{8,9},{9,8},{10,11... | collective-permute-start | bytes 393224 | tf_op jit(solution)/shard_map/ppermute | solution.py:18
  46.1 13.8 %collective-permute-start.14 = (bf16[32,2048]{1,0:T(8,128)(2,1)S(1)}, bf16[32,2048]{1,0:T(8,128)(2,1)S(1)}, u32[]{:S(2)}, u32[]{:S(2)}) collective-permute-start(bf16[32,2048]{1,0:T(8,128)(2,1)S(1)} %get-tuple-element.44.refs_0_), channel_id=1, source_target_pairs={{0,2},{1,3},{2,0},{3,1},{4,6},{5,7},{6,4},{7,5},{8,10},{9,11},{10,... | collective-permute-start | bytes 393224 | tf_op jit(solution)/shard_map/ppermute | solution.py:18
  47.3 12.7 %collective-permute-start.13 = (bf16[32,2048]{1,0:T(8,128)(2,1)S(1)}, bf16[32,2048]{1,0:T(8,128)(2,1)S(1)}, u32[]{:S(2)}, u32[]{:S(2)}) collective-permute-start(bf16[32,2048]{1,0:T(8,128)(2,1)S(1)} %get-tuple-element.44.refs_0_), channel_id=1, source_target_pairs={{0,3},{1,2},{2,1},{3,0},{4,7},{5,6},{6,5},{7,4},{8,11},{9,10},{10,... | collective-permute-start | bytes 393224 | tf_op jit(solution)/shard_map/ppermute | solution.py:18
  48.8 12.5 %collective-permute-start.18 = (bf16[32,2048]{1,0:T(8,128)(2,1)S(1)}, bf16[32,2048]{1,0:T(8,128)(2,1)S(1)}, u32[]{:S(2)}, u32[]{:S(2)}) collective-permute-start(bf16[32,2048]{1,0:T(8,128)(2,1)S(1)} %get-tuple-element.42.refs_4_), channel_id=1, source_target_pairs={{0,1},{1,0},{2,3},{3,2},{4,5},{5,4},{6,7},{7,6},{8,9},{9,8},{10,11... | collective-permute-start | bytes 393224 | tf_op jit(solution)/shard_map/ppermute | solution.py:18
  57.4 13.3 %collective-permute-start.17 = (bf16[32,2048]{1,0:T(8,128)(2,1)S(1)}, bf16[32,2048]{1,0:T(8,128)(2,1)S(1)}, u32[]{:S(2)}, u32[]{:S(2)}) collective-permute-start(bf16[32,2048]{1,0:T(8,128)(2,1)S(1)} %get-tuple-element.42.refs_4_), channel_id=1, source_target_pairs={{0,2},{1,3},{2,0},{3,1},{4,6},{5,7},{6,4},{7,5},{8,10},{9,11},{10,... | collective-permute-start | bytes 393224 | tf_op jit(solution)/shard_map/ppermute | solution.py:18
  58.6 12.1 %collective-permute-start.16 = (bf16[32,2048]{1,0:T(8,128)(2,1)S(1)}, bf16[32,2048]{1,0:T(8,128)(2,1)S(1)}, u32[]{:S(2)}, u32[]{:S(2)}) collective-permute-start(bf16[32,2048]{1,0:T(8,128)(2,1)S(1)} %get-tuple-element.42.refs_4_), channel_id=1, source_target_pairs={{0,3},{1,2},{2,1},{3,0},{4,7},{5,6},{6,5},{7,4},{8,11},{9,10},{10,... | collective-permute-start | bytes 393224 | tf_op jit(solution)/shard_map/ppermute | solution.py:18
  73.8 2.7 %collective-permute-start.19 = (f32[128,2048]{1,0:T(8,128)S(1)}, f32[128,2048]{1,0:T(8,128)S(1)}, u32[]{:S(2)}, u32[]{:S(2)}) collective-permute-start(f32[128,2048]{1,0:T(8,128)S(1)} %get-tuple-element.38), channel_id=1, source_target_pairs={{0,4},{4,0},{8,12},{12,8},{16,20},{20,16},{24,28},{28,24},{1,5},{5... | collective-permute-start | bytes 3145736 | tf_op jit(solution)/shard_map/ppermute | solution.py:18
  76.6 6.4 %collective-permute-start.20 = (bf16[32,2048]{1,0:T(8,128)(2,1)S(1)}, bf16[32,2048]{1,0:T(8,128)(2,1)S(1)}, u32[]{:S(2)}, u32[]{:S(2)}) collective-permute-start(bf16[32,2048]{1,0:T(8,128)(2,1)S(1)} %get-tuple-element.46), channel_id=1, source_target_pairs={{0,8},{4,12},{8,0},{12,4},{16,24},{20,28},{24,16},{28,20},{1,9},{5... | collective-permute-start | bytes 393224 | tf_op jit(solution)/shard_map/ppermute | solution.py:18
  78.0 8.0 %collective-permute-start.22 = (bf16[32,2048]{1,0:T(8,128)(2,1)S(1)}, bf16[32,2048]{1,0:T(8,128)(2,1)S(1)}, u32[]{:S(2)}, u32[]{:S(2)}) collective-permute-start(bf16[32,2048]{1,0:T(8,128)(2,1)S(1)} %get-tuple-element.47), channel_id=1, source_target_pairs={{0,24},{4,28},{8,16},{12,20},{16,8},{20,12},{24,0},{28,4},{1,25},{... | collective-permute-start | bytes 393224 | tf_op jit(solution)/shard_map/ppermute | solution.py:18
  79.5 7.8 %collective-permute-start.21 = (bf16[32,2048]{1,0:T(8,128)(2,1)S(1)}, bf16[32,2048]{1,0:T(8,128)(2,1)S(1)}, u32[]{:S(2)}, u32[]{:S(2)}) collective-permute-start(bf16[32,2048]{1,0:T(8,128)(2,1)S(1)} %get-tuple-element.48), channel_id=1, source_target_pairs={{0,16},{4,20},{8,24},{12,28},{16,0},{20,4},{24,8},{28,12},{1,17},{... | collective-permute-start | bytes 393224 | tf_op jit(solution)/shard_map/ppermute | solution.py:18

commit v7 on v6

--- a/solution.py
+++ b/solution.py
@@ -86,7 +86,7 @@
         scratch_shapes=[pltpu.VMEM((width, cols), BF16), pltpu.VMEM((width, rows), F32)],
         compiler_params=pltpu.CompilerParams(vmem_limit_bytes=VMEM_LIMIT),
         cost_estimate=pl.CostEstimate(
-            flops=2 * width * cols * rows, bytes_accessed=4 * width * (rows + cols), transcendentals=0
+            flops=2 * width * cols * rows, bytes_accessed=2 * rows * cols, transcendentals=0
         ),
         name="partial_sketch",
     )(where, tiles, token, *blocks)
@@ -128,7 +128,7 @@
         scratch_shapes=[pltpu.VMEM((width, rows), BF16), pltpu.VMEM((width, cols), F32)],
         compiler_params=pltpu.CompilerParams(vmem_limit_bytes=VMEM_LIMIT),
         cost_estimate=pl.CostEstimate(
-            flops=2 * width * cols * rows, bytes_accessed=4 * width * (rows + cols), transcendentals=0
+            flops=2 * width * cols * rows, bytes_accessed=2 * rows * cols, transcendentals=0
         ),
         name="partial_adjoint",
     )(where, tiles, *shares)

time: 88.3 us -> 88.3 us (level)
  no operation moved by 1% of the time
where the time goes in v7:
time: 88.3 us; the launch traced here: 88.1 us
  starting transfers between devices  44.2 us (50%)
  waiting for transfers between devices  23.7 us (27%)
  Pallas kernels  10.3 us (12%)
  local copies, waits for them, and re-layouts  7.33 us (8%)
  other arithmetic  1.91 us (2%)
    ppermute x23, starting transfers between devices, exchange(): return lax.ppermute(value, axis, [(i, i ^ offset) for i in range(size)])  44.2 us
    ppermute x23, waiting for transfers between devices, exchange(): return lax.ppermute(value, axis, [(i, i ^ offset) for i in range(size)])  23.7 us
    unnamed x8, local copies, waits for them, and re-layouts  7.33 us
    pallas_call x1, Pallas kernels, masked(): pl.pallas_call(functools.partial(mask_kernel, block=rows // mask.shape[0]...  4.19 us
    pallas_call x1, Pallas kernels, partial_adjoint(): pl.pallas_call(functools.partial(adjoint_kernel, offsets_col=offsets_col,...  3.06 us
    pallas_call x1, Pallas kernels, partial_sketch(): pl.pallas_call(functools.partial(sketch_kernel, offsets_row=offsets_row,...  3.02 us
  transfers between devices with their start and end apart: 23, of which 11 were waited for; matrix products, arithmetic and copies ran while one was open for 1% of the time, Pallas kernels for 5%

profile of v7, /device:TPU:0, one launch (start us, length us, event | category | flops | bytes accessed | tf_op | source)
XLA Modules:
  0.0 88.1 jit_solution(14534537196400949498)
XLA Ops:
  0.6 3.0 %collective-permute-start.2 = (bf16[32,2048]{1,0:T(8,128)(2,1)}, bf16[32,2048]{1,0:T(8,128)(2,1)S(1)}, u32[]{:S(2)}, u32[]{:S(2)}) collective-permute-start(bf16[32,2048]{1,0:T(8,128)(2,1)} %bitcast.10), channel_id=1, source_target_pairs={{0,8},{4,12},{8,0},{12,4},{16,24},{20,28},{24,16},{28,20},{1,9},{5... | collective-permute-start | bytes 393224 | tf_op jit(solution)/shard_map/ppermute | solution.py:18
  3.6 1.5 %collective-permute-start.1 = (bf16[32,2048]{1,0:T(8,128)(2,1)}, bf16[32,2048]{1,0:T(8,128)(2,1)S(1)}, u32[]{:S(2)}, u32[]{:S(2)}) collective-permute-start(bf16[32,2048]{1,0:T(8,128)(2,1)} %bitcast.11), channel_id=1, source_target_pairs={{0,16},{4,20},{8,24},{12,28},{16,0},{20,4},{24,8},{28,12},{1,17},{... | collective-permute-start | bytes 393224 | tf_op jit(solution)/shard_map/ppermute | solution.py:18
  5.2 0.7 copy-done.3
  5.9 4.2 %masked_tiles.1 = (bf16[2048,2048]{1,0:T(8,128)(2,1)S(1)}, f32[8,128]{1,0:T(8,128)S(1)}) custom-call(s32[8,8]{1,0:T(8,128)S(1)} %copy-done.3, bf16[2048,2048]{1,0:T(8,128)(2,1)} %green_ref.1), custom_call_target="tpu_custom_call" | custom-call | bytes 8388608 | tf_op jit(solution)/shard_map/masked_tiles/pallas_call | solution.py:41
  10.1 3.3 %copy-done = bf16[2048,2048]{1,0:T(8,128)(2,1)} copy-done((bf16[2048,2048]{1,0:T(8,128)(2,1)}, bf16[2048,2048]{1,0:T(8,128)(2,1)S(1)}, u32[]{:S(2)}) %copy-start) | copy-done | bytes 8388632
  13.4 0.5 collective-permute-start.4
  15.5 3.4 %copy-done.1 = bf16[2048,2048]{1,0:T(8,128)(2,1)S(1)} copy-done((bf16[2048,2048]{1,0:T(8,128)(2,1)S(1)}, bf16[2048,2048]{1,0:T(8,128)(2,1)}, u32[]{:S(2)}) %copy-start.1) | copy-done | bytes 8388632
  18.8 3.0 %partial_sketch.1 = (f32[32,2048]{1,0:T(8,128)S(1)}, bf16[32,2048]{1,0:T(8,128)(2,1)S(1)}, bf16[32,2048]{1,0:T(8,128)(2,1)S(1)}, bf16[32,2048]{1,0:T(8,128)(2,1)...) custom-call(s32[2]{0:T(128)S(1)} %pad_add_fusion.where, ...), custom_call_target="tpu_custom_call" | custom-call | flops 2147483648 | bytes 8388608 | tf_op jit(solution)/shard_map/partial_sketch/pallas_call | solution.py:79
  21.9 2.2 %collective-permute-start.7 = (bf16[32,2048]{1,0:T(8,128)(2,1)S(1)}, bf16[32,2048]{1,0:T(8,128)(2,1)S(1)}, u32[]{:S(2)}, u32[]{:S(2)}) collective-permute-start(bf16[32,2048]{1,0:T(8,128)(2,1)S(1)} %get-tuple-element.30), channel_id=1, source_target_pairs={{0,1},{1,0},{2,3},{3,2},{4,5},{5,4},{6,7},{7,6},{8,9},{9,8},{10,11... | collective-permute-start | bytes 393224 | tf_op jit(solution)/shard_map/ppermute | solution.py:18
  24.1 2.7 %collective-permute-start.8 = (bf16[32,2048]{1,0:T(8,128)(2,1)S(1)}, bf16[32,2048]{1,0:T(8,128)(2,1)S(1)}, u32[]{:S(2)}, u32[]{:S(2)}) collective-permute-start(bf16[32,2048]{1,0:T(8,128)(2,1)S(1)} %get-tuple-element.31), channel_id=1, source_target_pairs={{0,2},{1,3},{2,0},{3,1},{4,6},{5,7},{6,4},{7,5},{8,10},{9,11},{10,... | collective-permute-start | bytes 393224 | tf_op jit(solution)/shard_map/ppermute | solution.py:18
  26.7 0.8 collective-permute-start.10
  27.5 3.6 %collective-permute-start.11 = (bf16[32,2048]{1,0:T(8,128)(2,1)S(1)}, bf16[32,2048]{1,0:T(8,128)(2,1)S(1)}, u32[]{:S(2)}, u32[]{:S(2)}) collective-permute-start(bf16[32,2048]{1,0:T(8,128)(2,1)S(1)} %get-tuple-element.35), channel_id=1, source_target_pairs={{0,2},{1,3},{2,0},{3,1},{4,6},{5,7},{6,4},{7,5},{8,10},{9,11},{10,... | collective-permute-start | bytes 393224 | tf_op jit(solution)/shard_map/ppermute | solution.py:18
  31.1 2.9 %collective-permute-start.12 = (bf16[32,2048]{1,0:T(8,128)(2,1)S(1)}, bf16[32,2048]{1,0:T(8,128)(2,1)S(1)}, u32[]{:S(2)}, u32[]{:S(2)}) collective-permute-start(bf16[32,2048]{1,0:T(8,128)(2,1)S(1)} %get-tuple-element.36), channel_id=1, source_target_pairs={{0,3},{1,2},{2,1},{3,0},{4,7},{5,6},{6,5},{7,4},{8,11},{9,10},{10,... | collective-permute-start | bytes 393224 | tf_op jit(solution)/shard_map/ppermute | solution.py:18
  34.0 3.0 %collective-permute-done.8 = bf16[32,2048]{1,0:T(8,128)(2,1)S(1)} collective-permute-done((bf16[32,2048]{1,0:T(8,128)(2,1)S(1)}, bf16[32,2048]{1,0:T(8,128)(2,1)S(1)}, u32[]{:S(2)}, u32[]{:S(2)}) %collective-permute-start.8) | collective-permute-done | bytes 131104 | tf_op jit(solution)/shard_map/ppermute | solution.py:18
  37.0 9.1 %collective-permute-start.15 = (bf16[32,2048]{1,0:T(8,128)(2,1)S(1)}, bf16[32,2048]{1,0:T(8,128)(2,1)S(1)}, u32[]{:S(2)}, u32[]{:S(2)}) collective-permute-start(bf16[32,2048]{1,0:T(8,128)(2,1)S(1)} %get-tuple-element.44.refs_0_), channel_id=1, source_target_pairs={{0,1},{1,0},{2,3},{3,2},{4,5},{5,4},{6,7},{7,6},{8,9},{9,8},{10,11... | collective-permute-start | bytes 393224 | tf_op jit(solution)/shard_map/ppermute | solution.py:18
  46.1 1.2 %collective-permute-start.14 = (bf16[32,2048]{1,0:T(8,128)(2,1)S(1)}, bf16[32,2048]{1,0:T(8,128)(2,1)S(1)}, u32[]{:S(2)}, u32[]{:S(2)}) collective-permute-start(bf16[32,2048]{1,0:T(8,128)(2,1)S(1)} %get-tuple-element.44.refs_0_), channel_id=1, source_target_pairs={{0,2},{1,3},{2,0},{3,1},{4,6},{5,7},{6,4},{7,5},{8,10},{9,11},{10,... | collective-permute-start | bytes 393224 | tf_op jit(solution)/shard_map/ppermute | solution.py:18
  47.3 1.4 %collective-permute-start.13 = (bf16[32,2048]{1,0:T(8,128)(2,1)S(1)}, bf16[32,2048]{1,0:T(8,128)(2,1)S(1)}, u32[]{:S(2)}, u32[]{:S(2)}) collective-permute-start(bf16[32,2048]{1,0:T(8,128)(2,1)S(1)} %get-tuple-element.44.refs_0_), channel_id=1, source_target_pairs={{0,3},{1,2},{2,1},{3,0},{4,7},{5,6},{6,5},{7,4},{8,11},{9,10},{10,... | collective-permute-start | bytes 393224 | tf_op jit(solution)/shard_map/ppermute | solution.py:18
  48.8 8.5 %collective-permute-start.18 = (bf16[32,2048]{1,0:T(8,128)(2,1)S(1)}, bf16[32,2048]{1,0:T(8,128)(2,1)S(1)}, u32[]{:S(2)}, u32[]{:S(2)}) collective-permute-start(bf16[32,2048]{1,0:T(8,128)(2,1)S(1)} %get-tuple-element.42.refs_4_), channel_id=1, source_target_pairs={{0,1},{1,0},{2,3},{3,2},{4,5},{5,4},{6,7},{7,6},{8,9},{9,8},{10,11... | collective-permute-start | bytes 393224 | tf_op jit(solution)/shard_map/ppermute | solution.py:18
  57.3 1.3 %collective-permute-start.17 = (bf16[32,2048]{1,0:T(8,128)(2,1)S(1)}, bf16[32,2048]{1,0:T(8,128)(2,1)S(1)}, u32[]{:S(2)}, u32[]{:S(2)}) collective-permute-start(bf16[32,2048]{1,0:T(8,128)(2,1)S(1)} %get-tuple-element.42.refs_4_), channel_id=1, source_target_pairs={{0,2},{1,3},{2,0},{3,1},{4,6},{5,7},{6,4},{7,5},{8,10},{9,11},{10,... | collective-permute-start | bytes 393224 | tf_op jit(solution)/shard_map/ppermute | solution.py:18
  58.6 1.4 %collective-permute-start.16 = (bf16[32,2048]{1,0:T(8,128)(2,1)S(1)}, bf16[32,2048]{1,0:T(8,128)(2,1)S(1)}, u32[]{:S(2)}, u32[]{:S(2)}) collective-permute-start(bf16[32,2048]{1,0:T(8,128)(2,1)S(1)} %get-tuple-element.42.refs_4_), channel_id=1, source_target_pairs={{0,3},{1,2},{2,1},{3,0},{4,7},{5,6},{6,5},{7,4},{8,11},{9,10},{10,... | collective-permute-start | bytes 393224 | tf_op jit(solution)/shard_map/ppermute | solution.py:18
  60.0 1.3 %collective-permute-done.18.refs_7_ = bf16[32,2048]{1,0:T(8,128)(2,1)S(1)} collective-permute-done((bf16[32,2048]{1,0:T(8,128)(2,1)S(1)}, bf16[32,2048]{1,0:T(8,128)(2,1)S(1)}, u32[]{:S(2)}, u32[]{:S(2)}) %collective-permute-start.18) | collective-permute-done | bytes 131104 | tf_op jit(solution)/shard_map/ppermute | solution.py:18
  61.3 9.4 %collective-permute-done.17.refs_6_ = bf16[32,2048]{1,0:T(8,128)(2,1)S(1)} collective-permute-done((bf16[32,2048]{1,0:T(8,128)(2,1)S(1)}, bf16[32,2048]{1,0:T(8,128)(2,1)S(1)}, u32[]{:S(2)}, u32[]{:S(2)}) %collective-permute-start.17) | collective-permute-done | bytes 131104 | tf_op jit(solution)/shard_map/ppermute | solution.py:18
  70.7 3.1 %partial_adjoint.1 = (f32[32,2048]{1,0:T(8,128)S(1)}, f32[32,2048]{1,0:T(8,128)S(1)}, f32[32,2048]{1,0:T(8,128)S(1)}, f32[32,2048]{1,0:T(8,128)S(1)}, f32[128,2048]{1,0:T(8,128)S(1)}) custom-call(s32[2]{0:T(128)S(1)} %pad_add_fusion.where, bf16[2048,2048]{1,0:T(8,128)(2,1)S(1)} %copy-done.1, bf16[32,2048]{1,0:T(8,128)(2,1)S(1)} %get-tuple-element.44.refs_0_, ...), custom_call_target="tpu_custom_call" | custom-call | flops 2147483648 | bytes 8388608 | tf_op jit(solution)/shard_map/partial_adjoint/pallas_call | solution.py:123
  73.8 2.6 %collective-permute-done.19 = f32[128,2048]{1,0:T(8,128)S(1)} collective-permute-done((f32[128,2048]{1,0:T(8,128)S(1)}, f32[128,2048]{1,0:T(8,128)S(1)}, u32[]{:S(2)}, u32[]{:S(2)}) %collective-permute-start.19) | collective-permute-done | bytes 1048608 | tf_op jit(solution)/shard_map/ppermute | solution.py:18
  76.6 1.4 %collective-permute-start.20 = (bf16[32,2048]{1,0:T(8,128)(2,1)S(1)}, bf16[32,2048]{1,0:T(8,128)(2,1)S(1)}, u32[]{:S(2)}, u32[]{:S(2)}) collective-permute-start(bf16[32,2048]{1,0:T(8,128)(2,1)S(1)} %get-tuple-element.46), channel_id=1, source_target_pairs={{0,8},{4,12},{8,0},{12,4},{16,24},{20,28},{24,16},{28,20},{1,9},{5... | collective-permute-start | bytes 393224 | tf_op jit(solution)/shard_map/ppermute | solution.py:18
  78.0 1.5 %collective-permute-start.22 = (bf16[32,2048]{1,0:T(8,128)(2,1)S(1)}, bf16[32,2048]{1,0:T(8,128)(2,1)S(1)}, u32[]{:S(2)}, u32[]{:S(2)}) collective-permute-start(bf16[32,2048]{1,0:T(8,128)(2,1)S(1)} %get-tuple-element.47), channel_id=1, source_target_pairs={{0,24},{4,28},{8,16},{12,20},{16,8},{20,12},{24,0},{28,4},{1,25},{... | collective-permute-start | bytes 393224 | tf_op jit(solution)/shard_map/ppermute | solution.py:18
  79.5 0.6 collective-permute-start.21
  80.1 0.8 pad_maximum_fusion
  81.0 1.9 %collective-permute-done.20 = bf16[32,2048]{1,0:T(8,128)(2,1)S(1)} collective-permute-done((bf16[32,2048]{1,0:T(8,128)(2,1)S(1)}, bf16[32,2048]{1,0:T(8,128)(2,1)S(1)}, u32[]{:S(2)}, u32[]{:S(2)}) %collective-permute-start.20) | collective-permute-done | bytes 131104 | tf_op jit(solution)/shard_map/ppermute | solution.py:18
  82.9 3.0 %collective-permute-done.22 = bf16[32,2048]{1,0:T(8,128)(2,1)S(1)} collective-permute-done((bf16[32,2048]{1,0:T(8,128)(2,1)S(1)}, bf16[32,2048]{1,0:T(8,128)(2,1)S(1)}, u32[]{:S(2)}, u32[]{:S(2)}) %collective-permute-start.22) | collective-permute-done | bytes 131104 | tf_op jit(solution)/shard_map/ppermute | solution.py:18
  86.0 1.4 %collective-permute-done.21 = bf16[32,2048]{1,0:T(8,128)(2,1)S(1)} collective-permute-done((bf16[32,2048]{1,0:T(8,128)(2,1)S(1)}, bf16[32,2048]{1,0:T(8,128)(2,1)S(1)}, u32[]{:S(2)}, u32[]{:S(2)}) %collective-permute-start.21) | collective-permute-done | bytes 131104 | tf_op jit(solution)/shard_map/ppermute | solution.py:18
  87.3 0.8 fusion.6
  (31 shorter events, 2.0 us)
Async XLA Ops:
  0.6 12.7 %copy-start.2 = (bf16[2048,32]{0,1:T(8,128)(2,1)S(1)}, bf16[2048,32]{0,1:T(8,128)(2,1)}, u32[]{:S(2)}) copy-start(bf16[2048,32]{0,1:T(8,128)(2,1)} %param.5) | copy-start | bytes 393220
  0.6 12.7 %collective-permute-start.2 = (bf16[32,2048]{1,0:T(8,128)(2,1)}, bf16[32,2048]{1,0:T(8,128)(2,1)S(1)}, u32[]{:S(2)}, u32[]{:S(2)}) collective-permute-start(bf16[32,2048]{1,0:T(8,128)(2,1)} %bitcast.10), channel_id=1, source_target_pairs={{0,8},{4,12},{8,0},{12,4},{16,24},{20,28},{24,16},{28,20},{1,9},{5... | collective-permute-start | bytes 393224 | tf_op jit(solution)/shard_map/ppermute | solution.py:18
  3.6 9.7 %collective-permute-start.1 = (bf16[32,2048]{1,0:T(8,128)(2,1)}, bf16[32,2048]{1,0:T(8,128)(2,1)S(1)}, u32[]{:S(2)}, u32[]{:S(2)}) collective-permute-start(bf16[32,2048]{1,0:T(8,128)(2,1)} %bitcast.11), channel_id=1, source_target_pairs={{0,16},{4,20},{8,24},{12,28},{16,0},{20,4},{24,8},{28,12},{1,17},{... | collective-permute-start | bytes 393224 | tf_op jit(solution)/shard_map/ppermute | solution.py:18
  5.2 8.2 %collective-permute-start = (bf16[32,2048]{1,0:T(8,128)(2,1)}, bf16[32,2048]{1,0:T(8,128)(2,1)S(1)}, u32[]{:S(2)}, u32[]{:S(2)}) collective-permute-start(bf16[32,2048]{1,0:T(8,128)(2,1)} %bitcast.12), channel_id=1, source_target_pairs={{0,24},{4,28},{8,16},{12,20},{16,8},{20,12},{24,0},{28,4},{1,25},{... | collective-permute-start | bytes 393224 | tf_op jit(solution)/shard_map/ppermute | solution.py:18
  5.2 0.7 copy-start.3
  10.1 3.3 %copy-start = (bf16[2048,2048]{1,0:T(8,128)(2,1)}, bf16[2048,2048]{1,0:T(8,128)(2,1)S(1)}, u32[]{:S(2)}) copy-start(bf16[2048,2048]{1,0:T(8,128)(2,1)S(1)} %get-tuple-element.22.tiles) | copy-start | bytes 25165828
  13.4 1.4 %collective-permute-start.3 = (bf16[32,2048]{1,0:T(8,128)(2,1)S(1)}, bf16[32,2048]{1,0:T(8,128)(2,1)S(1)}, u32[]{:S(2)}, u32[]{:S(2)}) collective-permute-start(bf16[32,2048]{1,0:T(8,128)(2,1)S(1)} %bitcast.13), channel_id=1, source_target_pairs={{0,4},{4,0},{8,12},{12,8},{16,20},{20,16},{24,28},{28,24},{1,5},{5... | collective-permute-start | bytes 393224 | tf_op jit(solution)/shard_map/ppermute | solution.py:18
  13.4 1.5 %collective-permute-start.4 = (bf16[32,2048]{1,0:T(8,128)(2,1)S(1)}, bf16[32,2048]{1,0:T(8,128)(2,1)S(1)}, u32[]{:S(2)}, u32[]{:S(2)}) collective-permute-start(bf16[32,2048]{1,0:T(8,128)(2,1)S(1)} %collective-permute-done.refs_1_), channel_id=1, source_target_pairs={{0,4},{4,0},{8,12},{12,8},{16,20},{20,16},{24,28},{28,24},{1,5},{5... | collective-permute-start | bytes 393224 | tf_op jit(solution)/shard_map/ppermute | solution.py:18
  13.9 1.3 %collective-permute-start.5 = (bf16[32,2048]{1,0:T(8,128)(2,1)S(1)}, bf16[32,2048]{1,0:T(8,128)(2,1)S(1)}, u32[]{:S(2)}, u32[]{:S(2)}) collective-permute-start(bf16[32,2048]{1,0:T(8,128)(2,1)S(1)} %collective-permute-done.1.refs_2_), channel_id=1, source_target_pairs={{0,4},{4,0},{8,12},{12,8},{16,20},{20,16},{24,28},{28,24},{1,5},{5... | collective-permute-start | bytes 393224 | tf_op jit(solution)/shard_map/ppermute | solution.py:18
  14.0 1.5 %collective-permute-start.6 = (bf16[32,2048]{1,0:T(8,128)(2,1)S(1)}, bf16[32,2048]{1,0:T(8,128)(2,1)S(1)}, u32[]{:S(2)}, u32[]{:S(2)}) collective-permute-start(bf16[32,2048]{1,0:T(8,128)(2,1)S(1)} %collective-permute-done.2.refs_3_), channel_id=1, source_target_pairs={{0,4},{4,0},{8,12},{12,8},{16,20},{20,16},{24,28},{28,24},{1,5},{5... | collective-permute-start | bytes 393224 | tf_op jit(solution)/shard_map/ppermute | solution.py:18
  15.5 3.4 %copy-start.1 = (bf16[2048,2048]{1,0:T(8,128)(2,1)S(1)}, bf16[2048,2048]{1,0:T(8,128)(2,1)}, u32[]{:S(2)}) copy-start(bf16[2048,2048]{1,0:T(8,128)(2,1)} %copy-done) | copy-start | bytes 25165828
  21.9 9.2 %collective-permute-start.7 = (bf16[32,2048]{1,0:T(8,128)(2,1)S(1)}, bf16[32,2048]{1,0:T(8,128)(2,1)S(1)}, u32[]{:S(2)}, u32[]{:S(2)}) collective-permute-start(bf16[32,2048]{1,0:T(8,128)(2,1)S(1)} %get-tuple-element.30), channel_id=1, source_target_pairs={{0,1},{1,0},{2,3},{3,2},{4,5},{5,4},{6,7},{7,6},{8,9},{9,8},{10,11... | collective-permute-start | bytes 393224 | tf_op jit(solution)/shard_map/ppermute | solution.py:18
  24.1 12.9 %collective-permute-start.8 = (bf16[32,2048]{1,0:T(8,128)(2,1)S(1)}, bf16[32,2048]{1,0:T(8,128)(2,1)S(1)}, u32[]{:S(2)}, u32[]{:S(2)}) collective-permute-start(bf16[32,2048]{1,0:T(8,128)(2,1)S(1)} %get-tuple-element.31), channel_id=1, source_target_pairs={{0,2},{1,3},{2,0},{3,1},{4,6},{5,7},{6,4},{7,5},{8,10},{9,11},{10,... | collective-permute-start | bytes 393224 | tf_op jit(solution)/shard_map/ppermute | solution.py:18
  26.7 10.2 %collective-permute-start.9 = (bf16[32,2048]{1,0:T(8,128)(2,1)S(1)}, bf16[32,2048]{1,0:T(8,128)(2,1)S(1)}, u32[]{:S(2)}, u32[]{:S(2)}) collective-permute-start(bf16[32,2048]{1,0:T(8,128)(2,1)S(1)} %get-tuple-element.32), channel_id=1, source_target_pairs={{0,3},{1,2},{2,1},{3,0},{4,7},{5,6},{6,5},{7,4},{8,11},{9,10},{10,... | collective-permute-start | bytes 393224 | tf_op jit(solution)/shard_map/ppermute | solution.py:18
  26.7 20.6 %collective-permute-start.10 = (bf16[32,2048]{1,0:T(8,128)(2,1)S(1)}, bf16[32,2048]{1,0:T(8,128)(2,1)S(1)}, u32[]{:S(2)}, u32[]{:S(2)}) collective-permute-start(bf16[32,2048]{1,0:T(8,128)(2,1)S(1)} %get-tuple-element.34), channel_id=1, source_target_pairs={{0,1},{1,0},{2,3},{3,2},{4,5},{5,4},{6,7},{7,6},{8,9},{9,8},{10,11... | collective-permute-start | bytes 393224 | tf_op jit(solution)/shard_map/ppermute | solution.py:18
  27.5 21.2 %collective-permute-start.11 = (bf16[32,2048]{1,0:T(8,128)(2,1)S(1)}, bf16[32,2048]{1,0:T(8,128)(2,1)S(1)}, u32[]{:S(2)}, u32[]{:S(2)}) collective-permute-start(bf16[32,2048]{1,0:T(8,128)(2,1)S(1)} %get-tuple-element.35), channel_id=1, source_target_pairs={{0,2},{1,3},{2,0},{3,1},{4,6},{5,7},{6,4},{7,5},{8,10},{9,11},{10,... | collective-permute-start | bytes 393224 | tf_op jit(solution)/shard_map/ppermute | solution.py:18
  31.1 17.6 %collective-permute-start.12 = (bf16[32,2048]{1,0:T(8,128)(2,1)S(1)}, bf16[32,2048]{1,0:T(8,128)(2,1)S(1)}, u32[]{:S(2)}, u32[]{:S(2)}) collective-permute-start(bf16[32,2048]{1,0:T(8,128)(2,1)S(1)} %get-tuple-element.36), channel_id=1, source_target_pairs={{0,3},{1,2},{2,1},{3,0},{4,7},{5,6},{6,5},{7,4},{8,11},{9,10},{10,... | collective-permute-start | bytes 393224 | tf_op jit(solution)/shard_map/ppermute | solution.py:18
  37.0 21.5 %collective-permute-start.15 = (bf16[32,2048]{1,0:T(8,128)(2,1)S(1)}, bf16[32,2048]{1,0:T(8,128)(2,1)S(1)}, u32[]{:S(2)}, u32[]{:S(2)}) collective-permute-start(bf16[32,2048]{1,0:T(8,128)(2,1)S(1)} %get-tuple-element.44.refs_0_), channel_id=1, source_target_pairs={{0,1},{1,0},{2,3},{3,2},{4,5},{5,4},{6,7},{7,6},{8,9},{9,8},{10,11... | collective-permute-start | bytes 393224 | tf_op jit(solution)/shard_map/ppermute | solution.py:18
  46.1 13.9 %collective-permute-start.14 = (bf16[32,2048]{1,0:T(8,128)(2,1)S(1)}, bf16[32,2048]{1,0:T(8,128)(2,1)S(1)}, u32[]{:S(2)}, u32[]{:S(2)}) collective-permute-start(bf16[32,2048]{1,0:T(8,128)(2,1)S(1)} %get-tuple-element.44.refs_0_), channel_id=1, source_target_pairs={{0,2},{1,3},{2,0},{3,1},{4,6},{5,7},{6,4},{7,5},{8,10},{9,11},{10,... | collective-permute-start | bytes 393224 | tf_op jit(solution)/shard_map/ppermute | solution.py:18
  47.3 12.7 %collective-permute-start.13 = (bf16[32,2048]{1,0:T(8,128)(2,1)S(1)}, bf16[32,2048]{1,0:T(8,128)(2,1)S(1)}, u32[]{:S(2)}, u32[]{:S(2)}) collective-permute-start(bf16[32,2048]{1,0:T(8,128)(2,1)S(1)} %get-tuple-element.44.refs_0_), channel_id=1, source_target_pairs={{0,3},{1,2},{2,1},{3,0},{4,7},{5,6},{6,5},{7,4},{8,11},{9,10},{10,... | collective-permute-start | bytes 393224 | tf_op jit(solution)/shard_map/ppermute | solution.py:18
  48.8 12.5 %collective-permute-start.18 = (bf16[32,2048]{1,0:T(8,128)(2,1)S(1)}, bf16[32,2048]{1,0:T(8,128)(2,1)S(1)}, u32[]{:S(2)}, u32[]{:S(2)}) collective-permute-start(bf16[32,2048]{1,0:T(8,128)(2,1)S(1)} %get-tuple-element.42.refs_4_), channel_id=1, source_target_pairs={{0,1},{1,0},{2,3},{3,2},{4,5},{5,4},{6,7},{7,6},{8,9},{9,8},{10,11... | collective-permute-start | bytes 393224 | tf_op jit(solution)/shard_map/ppermute | solution.py:18
  57.3 13.4 %collective-permute-start.17 = (bf16[32,2048]{1,0:T(8,128)(2,1)S(1)}, bf16[32,2048]{1,0:T(8,128)(2,1)S(1)}, u32[]{:S(2)}, u32[]{:S(2)}) collective-permute-start(bf16[32,2048]{1,0:T(8,128)(2,1)S(1)} %get-tuple-element.42.refs_4_), channel_id=1, source_target_pairs={{0,2},{1,3},{2,0},{3,1},{4,6},{5,7},{6,4},{7,5},{8,10},{9,11},{10,... | collective-permute-start | bytes 393224 | tf_op jit(solution)/shard_map/ppermute | solution.py:18
  58.6 12.1 %collective-permute-start.16 = (bf16[32,2048]{1,0:T(8,128)(2,1)S(1)}, bf16[32,2048]{1,0:T(8,128)(2,1)S(1)}, u32[]{:S(2)}, u32[]{:S(2)}) collective-permute-start(bf16[32,2048]{1,0:T(8,128)(2,1)S(1)} %get-tuple-element.42.refs_4_), channel_id=1, source_target_pairs={{0,3},{1,2},{2,1},{3,0},{4,7},{5,6},{6,5},{7,4},{8,11},{9,10},{10,... | collective-permute-start | bytes 393224 | tf_op jit(solution)/shard_map/ppermute | solution.py:18
  73.8 2.7 %collective-permute-start.19 = (f32[128,2048]{1,0:T(8,128)S(1)}, f32[128,2048]{1,0:T(8,128)S(1)}, u32[]{:S(2)}, u32[]{:S(2)}) collective-permute-start(f32[128,2048]{1,0:T(8,128)S(1)} %get-tuple-element.38), channel_id=1, source_target_pairs={{0,4},{4,0},{8,12},{12,8},{16,20},{20,16},{24,28},{28,24},{1,5},{5... | collective-permute-start | bytes 3145736 | tf_op jit(solution)/shard_map/ppermute | solution.py:18
  76.6 6.3 %collective-permute-start.20 = (bf16[32,2048]{1,0:T(8,128)(2,1)S(1)}, bf16[32,2048]{1,0:T(8,128)(2,1)S(1)}, u32[]{:S(2)}, u32[]{:S(2)}) collective-permute-start(bf16[32,2048]{1,0:T(8,128)(2,1)S(1)} %get-tuple-element.46), channel_id=1, source_target_pairs={{0,8},{4,12},{8,0},{12,4},{16,24},{20,28},{24,16},{28,20},{1,9},{5... | collective-permute-start | bytes 393224 | tf_op jit(solution)/shard_map/ppermute | solution.py:18
  78.0 8.0 %collective-permute-start.22 = (bf16[32,2048]{1,0:T(8,128)(2,1)S(1)}, bf16[32,2048]{1,0:T(8,128)(2,1)S(1)}, u32[]{:S(2)}, u32[]{:S(2)}) collective-permute-start(bf16[32,2048]{1,0:T(8,128)(2,1)S(1)} %get-tuple-element.47), channel_id=1, source_target_pairs={{0,24},{4,28},{8,16},{12,20},{16,8},{20,12},{24,0},{28,4},{1,25},{... | collective-permute-start | bytes 393224 | tf_op jit(solution)/shard_map/ppermute | solution.py:18
  79.5 7.8 %collective-permute-start.21 = (bf16[32,2048]{1,0:T(8,128)(2,1)S(1)}, bf16[32,2048]{1,0:T(8,128)(2,1)S(1)}, u32[]{:S(2)}, u32[]{:S(2)}) collective-permute-start(bf16[32,2048]{1,0:T(8,128)(2,1)S(1)} %get-tuple-element.48), channel_id=1, source_target_pairs={{0,16},{4,20},{8,24},{12,28},{16,0},{20,4},{24,8},{28,12},{1,17},{... | collective-permute-start | bytes 393224 | tf_op jit(solution)/shard_map/ppermute | solution.py:18

commit v8 on v7

--- a/solution.py
+++ b/solution.py
@@ -18,7 +18,7 @@
     return lax.ppermute(value, axis, [(i, i ^ offset) for i in range(size)])
 
 
-def mask_kernel(mask_ref, green_ref, tiles, token, sems, *, block):
+def mask_kernel(where, mask_ref, green_ref, tiles, token, sems, *, block):
     rows, cols = tiles.shape
     token[...] = jnp.zeros(token.shape, token.dtype)
     copies = []
@@ -36,18 +36,18 @@
                     tiles[i * block : (i + 1) * block, j * block : (j + 1) * block] = jnp.zeros((block, block), BF16)
 
 
-def masked(green, mask):
+def masked(where, green, mask):
     rows, cols = green.shape
     return pl.pallas_call(
         functools.partial(mask_kernel, block=rows // mask.shape[0]),
-        in_specs=[pl.BlockSpec(memory_space=pltpu.SMEM), pl.BlockSpec(memory_space=pltpu.HBM)],
+        in_specs=[pl.BlockSpec(memory_space=pltpu.SMEM)] * 2 + [pl.BlockSpec(memory_space=pltpu.HBM)],
         out_specs=[pl.BlockSpec(memory_space=pltpu.VMEM)] * 2,
         out_shape=[pltpu.VMEM((rows, cols), BF16), jax.ShapeDtypeStruct((8, 128), F32)],
         scratch_shapes=[pltpu.SemaphoreType.DMA((rows // STEP,))],
         compiler_params=pltpu.CompilerParams(vmem_limit_bytes=VMEM_LIMIT),
         cost_estimate=pl.CostEstimate(flops=0, bytes_accessed=2 * rows * cols, transcendentals=0),
         name="masked_tiles",
-    )(mask, pltpu.with_memory_space_constraint(green, pltpu.HBM))
+    )(where, mask, pltpu.with_memory_space_constraint(green, pltpu.HBM))
 
 
 def sketch_kernel(where, tiles, token, *refs, offsets_row, offsets_col, piece):
@@ -152,7 +152,7 @@
     offsets_row = gather_core + [offset ^ 1 for offset in gather_core]
     far_first = [0] + offsets_col[:0:-1]
 
-    tiles, token = masked(green, mask)
+    tiles, token = masked(where, green, mask)
 
     own = probes.T
     held = [own] + [exchange(own, "row", offset) for offset in gather_core[1:]]

time: 88.3 us -> 82.8 us (0.938)
  local copies, waits for them, and re-layouts: 7.33 us -> 0.69 us
  waiting for transfers between devices: 23.7 us -> 25.5 us
    unnamed x8 -> x4, local copies, waits for them, and re-layouts: 7.33 us -> 0.69 us
    ppermute x23, waiting for transfers between devices: 23.7 us -> 25.5 us  [exchange(): return lax.ppermute(value, axis, [(i, i ^ offset) for i in range(size)])]
  transfers between devices with their start and end apart: 23 -> 23, of which waited for: 11 -> 12; matrix products, arithmetic and copies ran while one was open for 1% -> 1% of each run, Pallas kernels for 5% -> 5%
where the time goes in v8:
time: 82.8 us; the launch traced here: 82.6 us
  starting transfers between devices  43.5 us (53%)
  waiting for transfers between devices  25.5 us (31%)
  Pallas kernels  10.4 us (13%)
  other arithmetic  1.91 us (2%)
    ppermute x23, starting transfers between devices, exchange(): return lax.ppermute(value, axis, [(i, i ^ offset) for i in range(size)])  43.5 us
    ppermute x23, waiting for transfers between devices, exchange(): return lax.ppermute(value, axis, [(i, i ^ offset) for i in range(size)])  25.5 us
    pallas_call x1, Pallas kernels, masked(): pl.pallas_call(functools.partial(mask_kernel, block=rows // mask.shape[0]...  4.21 us
    pallas_call x1, Pallas kernels, partial_adjoint(): pl.pallas_call(functools.partial(adjoint_kernel, offsets_col=offsets_col,...  3.11 us
    pallas_call x1, Pallas kernels, partial_sketch(): pl.pallas_call(functools.partial(sketch_kernel, offsets_row=offsets_row,...  3.03 us
  transfers between devices with their start and end apart: 23, of which 12 were waited for; matrix products, arithmetic and copies ran while one was open for 1% of the time, Pallas kernels for 5%

profile of v8, /device:TPU:0, one launch (start us, length us, event | category | flops | bytes accessed | tf_op | source)
XLA Modules:
  0.0 82.6 jit_solution(6593186609358369629)
XLA Ops:
  0.6 3.0 %collective-permute-start.2 = (bf16[32,2048]{1,0:T(8,128)(2,1)}, bf16[32,2048]{1,0:T(8,128)(2,1)S(1)}, u32[]{:S(2)}, u32[]{:S(2)}) collective-permute-start(bf16[32,2048]{1,0:T(8,128)(2,1)} %bitcast.10), channel_id=1, source_target_pairs={{0,8},{4,12},{8,0},{12,4},{16,24},{20,28},{24,16},{28,20},{1,9},{5... | collective-permute-start | bytes 393224 | tf_op jit(solution)/shard_map/ppermute | solution.py:18
  3.6 1.5 %collective-permute-start.1 = (bf16[32,2048]{1,0:T(8,128)(2,1)}, bf16[32,2048]{1,0:T(8,128)(2,1)S(1)}, u32[]{:S(2)}, u32[]{:S(2)}) collective-permute-start(bf16[32,2048]{1,0:T(8,128)(2,1)} %bitcast.11), channel_id=1, source_target_pairs={{0,16},{4,20},{8,24},{12,28},{16,0},{20,4},{24,8},{28,12},{1,17},{... | collective-permute-start | bytes 393224 | tf_op jit(solution)/shard_map/ppermute | solution.py:18
  5.3 0.7 copy-done.1
  5.9 4.2 %masked_tiles.1 = (bf16[2048,2048]{1,0:T(8,128)(2,1)S(1)}, f32[8,128]{1,0:T(8,128)S(1)}) custom-call(s32[2]{0:T(128)S(1)} %pad_add_fusion.where, s32[8,8]{1,0:T(8,128)S(1)} %copy-done.1, bf16[2048,2048]{1,0:T(8,128)(2,1)} %green_ref.1), custom_call_target="tpu_custom_call" | custom-call | bytes 8388608 | tf_op jit(solution)/shard_map/masked_tiles/pallas_call | solution.py:41
  10.2 1.5 %collective-permute-done.1.refs_2_ = bf16[32,2048]{1,0:T(8,128)(2,1)S(1)} collective-permute-done((bf16[32,2048]{1,0:T(8,128)(2,1)}, bf16[32,2048]{1,0:T(8,128)(2,1)S(1)}, u32[]{:S(2)}, u32[]{:S(2)}) %collective-permute-start.1) | collective-permute-done | bytes 131104 | tf_op jit(solution)/shard_map/ppermute | solution.py:18
  11.6 0.5 collective-permute-start.4
  12.2 0.4 collective-permute-start.6
  13.7 3.0 %partial_sketch.1 = (f32[32,2048]{1,0:T(8,128)S(1)}, bf16[32,2048]{1,0:T(8,128)(2,1)S(1)}, bf16[32,2048]{1,0:T(8,128)(2,1)S(1)}, bf16[32,2048]{1,0:T(8,128)(2,1)...) custom-call(s32[2]{0:T(128)S(1)} %pad_add_fusion.where, ...), custom_call_target="tpu_custom_call" | custom-call | flops 2147483648 | bytes 8388608 | tf_op jit(solution)/shard_map/partial_sketch/pallas_call | solution.py:79
  16.7 1.6 %collective-permute-start.7 = (bf16[32,2048]{1,0:T(8,128)(2,1)S(1)}, bf16[32,2048]{1,0:T(8,128)(2,1)S(1)}, u32[]{:S(2)}, u32[]{:S(2)}) collective-permute-start(bf16[32,2048]{1,0:T(8,128)(2,1)S(1)} %get-tuple-element.30), channel_id=1, source_target_pairs={{0,1},{1,0},{2,3},{3,2},{4,5},{5,4},{6,7},{7,6},{8,9},{9,8},{10,11... | collective-permute-start | bytes 393224 | tf_op jit(solution)/shard_map/ppermute | solution.py:18
  18.4 2.6 %collective-permute-start.8 = (bf16[32,2048]{1,0:T(8,128)(2,1)S(1)}, bf16[32,2048]{1,0:T(8,128)(2,1)S(1)}, u32[]{:S(2)}, u32[]{:S(2)}) collective-permute-start(bf16[32,2048]{1,0:T(8,128)(2,1)S(1)} %get-tuple-element.31), channel_id=1, source_target_pairs={{0,2},{1,3},{2,0},{3,1},{4,6},{5,7},{6,4},{7,5},{8,10},{9,11},{10,... | collective-permute-start | bytes 393224 | tf_op jit(solution)/shard_map/ppermute | solution.py:18
  21.2 0.7 collective-permute-start.10
  21.9 3.5 %collective-permute-start.11 = (bf16[32,2048]{1,0:T(8,128)(2,1)S(1)}, bf16[32,2048]{1,0:T(8,128)(2,1)S(1)}, u32[]{:S(2)}, u32[]{:S(2)}) collective-permute-start(bf16[32,2048]{1,0:T(8,128)(2,1)S(1)} %get-tuple-element.35), channel_id=1, source_target_pairs={{0,2},{1,3},{2,0},{3,1},{4,6},{5,7},{6,4},{7,5},{8,10},{9,11},{10,... | collective-permute-start | bytes 393224 | tf_op jit(solution)/shard_map/ppermute | solution.py:18
  25.4 2.9 %collective-permute-start.12 = (bf16[32,2048]{1,0:T(8,128)(2,1)S(1)}, bf16[32,2048]{1,0:T(8,128)(2,1)S(1)}, u32[]{:S(2)}, u32[]{:S(2)}) collective-permute-start(bf16[32,2048]{1,0:T(8,128)(2,1)S(1)} %get-tuple-element.36), channel_id=1, source_target_pairs={{0,3},{1,2},{2,1},{3,0},{4,7},{5,6},{6,5},{7,4},{8,11},{9,10},{10,... | collective-permute-start | bytes 393224 | tf_op jit(solution)/shard_map/ppermute | solution.py:18
  28.3 3.1 %collective-permute-done.8 = bf16[32,2048]{1,0:T(8,128)(2,1)S(1)} collective-permute-done((bf16[32,2048]{1,0:T(8,128)(2,1)S(1)}, bf16[32,2048]{1,0:T(8,128)(2,1)S(1)}, u32[]{:S(2)}, u32[]{:S(2)}) %collective-permute-start.8) | collective-permute-done | bytes 131104 | tf_op jit(solution)/shard_map/ppermute | solution.py:18
  31.4 9.1 %collective-permute-start.15 = (bf16[32,2048]{1,0:T(8,128)(2,1)S(1)}, bf16[32,2048]{1,0:T(8,128)(2,1)S(1)}, u32[]{:S(2)}, u32[]{:S(2)}) collective-permute-start(bf16[32,2048]{1,0:T(8,128)(2,1)S(1)} %get-tuple-element.44.refs_0_), channel_id=1, source_target_pairs={{0,1},{1,0},{2,3},{3,2},{4,5},{5,4},{6,7},{7,6},{8,9},{9,8},{10,11... | collective-permute-start | bytes 393224 | tf_op jit(solution)/shard_map/ppermute | solution.py:18
  40.5 1.1 %collective-permute-start.14 = (bf16[32,2048]{1,0:T(8,128)(2,1)S(1)}, bf16[32,2048]{1,0:T(8,128)(2,1)S(1)}, u32[]{:S(2)}, u32[]{:S(2)}) collective-permute-start(bf16[32,2048]{1,0:T(8,128)(2,1)S(1)} %get-tuple-element.44.refs_0_), channel_id=1, source_target_pairs={{0,2},{1,3},{2,0},{3,1},{4,6},{5,7},{6,4},{7,5},{8,10},{9,11},{10,... | collective-permute-start | bytes 393224 | tf_op jit(solution)/shard_map/ppermute | solution.py:18
  41.6 1.4 %collective-permute-start.13 = (bf16[32,2048]{1,0:T(8,128)(2,1)S(1)}, bf16[32,2048]{1,0:T(8,128)(2,1)S(1)}, u32[]{:S(2)}, u32[]{:S(2)}) collective-permute-start(bf16[32,2048]{1,0:T(8,128)(2,1)S(1)} %get-tuple-element.44.refs_0_), channel_id=1, source_target_pairs={{0,3},{1,2},{2,1},{3,0},{4,7},{5,6},{6,5},{7,4},{8,11},{9,10},{10,... | collective-permute-start | bytes 393224 | tf_op jit(solution)/shard_map/ppermute | solution.py:18
  43.0 8.7 %collective-permute-start.18 = (bf16[32,2048]{1,0:T(8,128)(2,1)S(1)}, bf16[32,2048]{1,0:T(8,128)(2,1)S(1)}, u32[]{:S(2)}, u32[]{:S(2)}) collective-permute-start(bf16[32,2048]{1,0:T(8,128)(2,1)S(1)} %get-tuple-element.42.refs_4_), channel_id=1, source_target_pairs={{0,1},{1,0},{2,3},{3,2},{4,5},{5,4},{6,7},{7,6},{8,9},{9,8},{10,11... | collective-permute-start | bytes 393224 | tf_op jit(solution)/shard_map/ppermute | solution.py:18
  51.7 1.1 %collective-permute-start.17 = (bf16[32,2048]{1,0:T(8,128)(2,1)S(1)}, bf16[32,2048]{1,0:T(8,128)(2,1)S(1)}, u32[]{:S(2)}, u32[]{:S(2)}) collective-permute-start(bf16[32,2048]{1,0:T(8,128)(2,1)S(1)} %get-tuple-element.42.refs_4_), channel_id=1, source_target_pairs={{0,2},{1,3},{2,0},{3,1},{4,6},{5,7},{6,4},{7,5},{8,10},{9,11},{10,... | collective-permute-start | bytes 393224 | tf_op jit(solution)/shard_map/ppermute | solution.py:18
  52.8 1.4 %collective-permute-start.16 = (bf16[32,2048]{1,0:T(8,128)(2,1)S(1)}, bf16[32,2048]{1,0:T(8,128)(2,1)S(1)}, u32[]{:S(2)}, u32[]{:S(2)}) collective-permute-start(bf16[32,2048]{1,0:T(8,128)(2,1)S(1)} %get-tuple-element.42.refs_4_), channel_id=1, source_target_pairs={{0,3},{1,2},{2,1},{3,0},{4,7},{5,6},{6,5},{7,4},{8,11},{9,10},{10,... | collective-permute-start | bytes 393224 | tf_op jit(solution)/shard_map/ppermute | solution.py:18
  54.2 1.3 %collective-permute-done.18.refs_7_ = bf16[32,2048]{1,0:T(8,128)(2,1)S(1)} collective-permute-done((bf16[32,2048]{1,0:T(8,128)(2,1)S(1)}, bf16[32,2048]{1,0:T(8,128)(2,1)S(1)}, u32[]{:S(2)}, u32[]{:S(2)}) %collective-permute-start.18) | collective-permute-done | bytes 131104 | tf_op jit(solution)/shard_map/ppermute | solution.py:18
  55.5 9.6 %collective-permute-done.17.refs_6_ = bf16[32,2048]{1,0:T(8,128)(2,1)S(1)} collective-permute-done((bf16[32,2048]{1,0:T(8,128)(2,1)S(1)}, bf16[32,2048]{1,0:T(8,128)(2,1)S(1)}, u32[]{:S(2)}, u32[]{:S(2)}) %collective-permute-start.17) | collective-permute-done | bytes 131104 | tf_op jit(solution)/shard_map/ppermute | solution.py:18
  65.0 3.1 %partial_adjoint.1 = (f32[32,2048]{1,0:T(8,128)S(1)}, f32[32,2048]{1,0:T(8,128)S(1)}, f32[32,2048]{1,0:T(8,128)S(1)}, f32[32,2048]{1,0:T(8,128)S(1)}, f32[128,2048]{1,0:T(8,128)S(1)}) custom-call(s32[2]{0:T(128)S(1)} %pad_add_fusion.where, bf16[2048,2048]{1,0:T(8,128)(2,1)S(1)} %get-tuple-element.22.tiles, bf16[32,2048]{1,0:T(8,128)(2,1)S(1)} %get-tuple-element.44.refs_0_, ...), custom_call_target="tpu_custom_call" | custom-call | flops 2147483648 | bytes 8388608 | tf_op jit(solution)/shard_map/partial_adjoint/pallas_call | solution.py:123
  68.2 2.6 %collective-permute-done.19 = f32[128,2048]{1,0:T(8,128)S(1)} collective-permute-done((f32[128,2048]{1,0:T(8,128)S(1)}, f32[128,2048]{1,0:T(8,128)S(1)}, u32[]{:S(2)}, u32[]{:S(2)}) %collective-permute-start.19) | collective-permute-done | bytes 1048608 | tf_op jit(solution)/shard_map/ppermute | solution.py:18
  71.0 1.3 %collective-permute-start.20 = (bf16[32,2048]{1,0:T(8,128)(2,1)S(1)}, bf16[32,2048]{1,0:T(8,128)(2,1)S(1)}, u32[]{:S(2)}, u32[]{:S(2)}) collective-permute-start(bf16[32,2048]{1,0:T(8,128)(2,1)S(1)} %get-tuple-element.46), channel_id=1, source_target_pairs={{0,8},{4,12},{8,0},{12,4},{16,24},{20,28},{24,16},{28,20},{1,9},{5... | collective-permute-start | bytes 393224 | tf_op jit(solution)/shard_map/ppermute | solution.py:18
  72.3 1.7 %collective-permute-start.22 = (bf16[32,2048]{1,0:T(8,128)(2,1)S(1)}, bf16[32,2048]{1,0:T(8,128)(2,1)S(1)}, u32[]{:S(2)}, u32[]{:S(2)}) collective-permute-start(bf16[32,2048]{1,0:T(8,128)(2,1)S(1)} %get-tuple-element.47), channel_id=1, source_target_pairs={{0,24},{4,28},{8,16},{12,20},{16,8},{20,12},{24,0},{28,4},{1,25},{... | collective-permute-start | bytes 393224 | tf_op jit(solution)/shard_map/ppermute | solution.py:18
  74.0 0.5 collective-permute-start.21
  74.5 0.8 %pad_maximum_fusion = f32[2,32,2048]{2,1,0:T(8,128)} fusion(f32[2,16,2048]{2,1,0:T(8,128)S(1)} %bitcast.16, f32[2,16,2048]{2,1,0:T(8,128)S(1)} %bitcast.15), kind=kLoop, calls=%fused_computation | loop fusion | flops 131072 | bytes 1048576 | tf_op jit(solution)/shard_map/concatenate | solution.py:139
  75.4 2.0 %collective-permute-done.20 = bf16[32,2048]{1,0:T(8,128)(2,1)S(1)} collective-permute-done((bf16[32,2048]{1,0:T(8,128)(2,1)S(1)}, bf16[32,2048]{1,0:T(8,128)(2,1)S(1)}, u32[]{:S(2)}, u32[]{:S(2)}) %collective-permute-start.20) | collective-permute-done | bytes 131104 | tf_op jit(solution)/shard_map/ppermute | solution.py:18
  77.4 3.1 %collective-permute-done.22 = bf16[32,2048]{1,0:T(8,128)(2,1)S(1)} collective-permute-done((bf16[32,2048]{1,0:T(8,128)(2,1)S(1)}, bf16[32,2048]{1,0:T(8,128)(2,1)S(1)}, u32[]{:S(2)}, u32[]{:S(2)}) %collective-permute-start.22) | collective-permute-done | bytes 131104 | tf_op jit(solution)/shard_map/ppermute | solution.py:18
  80.5 1.4 %collective-permute-done.21 = bf16[32,2048]{1,0:T(8,128)(2,1)S(1)} collective-permute-done((bf16[32,2048]{1,0:T(8,128)(2,1)S(1)}, bf16[32,2048]{1,0:T(8,128)(2,1)S(1)}, u32[]{:S(2)}, u32[]{:S(2)}) %collective-permute-start.21) | collective-permute-done | bytes 131104 | tf_op jit(solution)/shard_map/ppermute | solution.py:18
  81.8 0.8 fusion.6
  (27 shorter events, 1.8 us)
Async XLA Ops:
  0.6 11.0 %copy-start = (bf16[2048,32]{0,1:T(8,128)(2,1)S(1)}, bf16[2048,32]{0,1:T(8,128)(2,1)}, u32[]{:S(2)}) copy-start(bf16[2048,32]{0,1:T(8,128)(2,1)} %param.5) | copy-start | bytes 393220
  0.6 9.5 %collective-permute-start.2 = (bf16[32,2048]{1,0:T(8,128)(2,1)}, bf16[32,2048]{1,0:T(8,128)(2,1)S(1)}, u32[]{:S(2)}, u32[]{:S(2)}) collective-permute-start(bf16[32,2048]{1,0:T(8,128)(2,1)} %bitcast.10), channel_id=1, source_target_pairs={{0,8},{4,12},{8,0},{12,4},{16,24},{20,28},{24,16},{28,20},{1,9},{5... | collective-permute-start | bytes 393224 | tf_op jit(solution)/shard_map/ppermute | solution.py:18
  3.6 8.0 %collective-permute-start.1 = (bf16[32,2048]{1,0:T(8,128)(2,1)}, bf16[32,2048]{1,0:T(8,128)(2,1)S(1)}, u32[]{:S(2)}, u32[]{:S(2)}) collective-permute-start(bf16[32,2048]{1,0:T(8,128)(2,1)} %bitcast.11), channel_id=1, source_target_pairs={{0,16},{4,20},{8,24},{12,28},{16,0},{20,4},{24,8},{28,12},{1,17},{... | collective-permute-start | bytes 393224 | tf_op jit(solution)/shard_map/ppermute | solution.py:18
  5.2 6.5 %collective-permute-start = (bf16[32,2048]{1,0:T(8,128)(2,1)}, bf16[32,2048]{1,0:T(8,128)(2,1)S(1)}, u32[]{:S(2)}, u32[]{:S(2)}) collective-permute-start(bf16[32,2048]{1,0:T(8,128)(2,1)} %bitcast.12), channel_id=1, source_target_pairs={{0,24},{4,28},{8,16},{12,20},{16,8},{20,12},{24,0},{28,4},{1,25},{... | collective-permute-start | bytes 393224 | tf_op jit(solution)/shard_map/ppermute | solution.py:18
  5.3 0.7 copy-start.1
  11.6 1.4 %collective-permute-start.3 = (bf16[32,2048]{1,0:T(8,128)(2,1)S(1)}, bf16[32,2048]{1,0:T(8,128)(2,1)S(1)}, u32[]{:S(2)}, u32[]{:S(2)}) collective-permute-start(bf16[32,2048]{1,0:T(8,128)(2,1)S(1)} %bitcast.13), channel_id=1, source_target_pairs={{0,4},{4,0},{8,12},{12,8},{16,20},{20,16},{24,28},{28,24},{1,5},{5... | collective-permute-start | bytes 393224 | tf_op jit(solution)/shard_map/ppermute | solution.py:18
  11.6 1.5 %collective-permute-start.4 = (bf16[32,2048]{1,0:T(8,128)(2,1)S(1)}, bf16[32,2048]{1,0:T(8,128)(2,1)S(1)}, u32[]{:S(2)}, u32[]{:S(2)}) collective-permute-start(bf16[32,2048]{1,0:T(8,128)(2,1)S(1)} %collective-permute-done.refs_1_), channel_id=1, source_target_pairs={{0,4},{4,0},{8,12},{12,8},{16,20},{20,16},{24,28},{28,24},{1,5},{5... | collective-permute-start | bytes 393224 | tf_op jit(solution)/shard_map/ppermute | solution.py:18
  12.1 1.3 %collective-permute-start.5 = (bf16[32,2048]{1,0:T(8,128)(2,1)S(1)}, bf16[32,2048]{1,0:T(8,128)(2,1)S(1)}, u32[]{:S(2)}, u32[]{:S(2)}) collective-permute-start(bf16[32,2048]{1,0:T(8,128)(2,1)S(1)} %collective-permute-done.1.refs_2_), channel_id=1, source_target_pairs={{0,4},{4,0},{8,12},{12,8},{16,20},{20,16},{24,28},{28,24},{1,5},{5... | collective-permute-start | bytes 393224 | tf_op jit(solution)/shard_map/ppermute | solution.py:18
  12.2 1.5 %collective-permute-start.6 = (bf16[32,2048]{1,0:T(8,128)(2,1)S(1)}, bf16[32,2048]{1,0:T(8,128)(2,1)S(1)}, u32[]{:S(2)}, u32[]{:S(2)}) collective-permute-start(bf16[32,2048]{1,0:T(8,128)(2,1)S(1)} %collective-permute-done.2.refs_3_), channel_id=1, source_target_pairs={{0,4},{4,0},{8,12},{12,8},{16,20},{20,16},{24,28},{28,24},{1,5},{5... | collective-permute-start | bytes 393224 | tf_op jit(solution)/shard_map/ppermute | solution.py:18
  16.7 8.6 %collective-permute-start.7 = (bf16[32,2048]{1,0:T(8,128)(2,1)S(1)}, bf16[32,2048]{1,0:T(8,128)(2,1)S(1)}, u32[]{:S(2)}, u32[]{:S(2)}) collective-permute-start(bf16[32,2048]{1,0:T(8,128)(2,1)S(1)} %get-tuple-element.30), channel_id=1, source_target_pairs={{0,1},{1,0},{2,3},{3,2},{4,5},{5,4},{6,7},{7,6},{8,9},{9,8},{10,11... | collective-permute-start | bytes 393224 | tf_op jit(solution)/shard_map/ppermute | solution.py:18
  18.4 13.0 %collective-permute-start.8 = (bf16[32,2048]{1,0:T(8,128)(2,1)S(1)}, bf16[32,2048]{1,0:T(8,128)(2,1)S(1)}, u32[]{:S(2)}, u32[]{:S(2)}) collective-permute-start(bf16[32,2048]{1,0:T(8,128)(2,1)S(1)} %get-tuple-element.31), channel_id=1, source_target_pairs={{0,2},{1,3},{2,0},{3,1},{4,6},{5,7},{6,4},{7,5},{8,10},{9,11},{10,... | collective-permute-start | bytes 393224 | tf_op jit(solution)/shard_map/ppermute | solution.py:18
  21.0 10.4 %collective-permute-start.9 = (bf16[32,2048]{1,0:T(8,128)(2,1)S(1)}, bf16[32,2048]{1,0:T(8,128)(2,1)S(1)}, u32[]{:S(2)}, u32[]{:S(2)}) collective-permute-start(bf16[32,2048]{1,0:T(8,128)(2,1)S(1)} %get-tuple-element.32), channel_id=1, source_target_pairs={{0,3},{1,2},{2,1},{3,0},{4,7},{5,6},{6,5},{7,4},{8,11},{9,10},{10,... | collective-permute-start | bytes 393224 | tf_op jit(solution)/shard_map/ppermute | solution.py:18
  21.2 20.4 %collective-permute-start.10 = (bf16[32,2048]{1,0:T(8,128)(2,1)S(1)}, bf16[32,2048]{1,0:T(8,128)(2,1)S(1)}, u32[]{:S(2)}, u32[]{:S(2)}) collective-permute-start(bf16[32,2048]{1,0:T(8,128)(2,1)S(1)} %get-tuple-element.34), channel_id=1, source_target_pairs={{0,1},{1,0},{2,3},{3,2},{4,5},{5,4},{6,7},{7,6},{8,9},{9,8},{10,11... | collective-permute-start | bytes 393224 | tf_op jit(solution)/shard_map/ppermute | solution.py:18
  21.9 21.1 %collective-permute-start.11 = (bf16[32,2048]{1,0:T(8,128)(2,1)S(1)}, bf16[32,2048]{1,0:T(8,128)(2,1)S(1)}, u32[]{:S(2)}, u32[]{:S(2)}) collective-permute-start(bf16[32,2048]{1,0:T(8,128)(2,1)S(1)} %get-tuple-element.35), channel_id=1, source_target_pairs={{0,2},{1,3},{2,0},{3,1},{4,6},{5,7},{6,4},{7,5},{8,10},{9,11},{10,... | collective-permute-start | bytes 393224 | tf_op jit(solution)/shard_map/ppermute | solution.py:18
  25.4 17.6 %collective-permute-start.12 = (bf16[32,2048]{1,0:T(8,128)(2,1)S(1)}, bf16[32,2048]{1,0:T(8,128)(2,1)S(1)}, u32[]{:S(2)}, u32[]{:S(2)}) collective-permute-start(bf16[32,2048]{1,0:T(8,128)(2,1)S(1)} %get-tuple-element.36), channel_id=1, source_target_pairs={{0,3},{1,2},{2,1},{3,0},{4,7},{5,6},{6,5},{7,4},{8,11},{9,10},{10,... | collective-permute-start | bytes 393224 | tf_op jit(solution)/shard_map/ppermute | solution.py:18
  31.4 21.4 %collective-permute-start.15 = (bf16[32,2048]{1,0:T(8,128)(2,1)S(1)}, bf16[32,2048]{1,0:T(8,128)(2,1)S(1)}, u32[]{:S(2)}, u32[]{:S(2)}) collective-permute-start(bf16[32,2048]{1,0:T(8,128)(2,1)S(1)} %get-tuple-element.44.refs_0_), channel_id=1, source_target_pairs={{0,1},{1,0},{2,3},{3,2},{4,5},{5,4},{6,7},{7,6},{8,9},{9,8},{10,11... | collective-permute-start | bytes 393224 | tf_op jit(solution)/shard_map/ppermute | solution.py:18
  40.5 13.8 %collective-permute-start.14 = (bf16[32,2048]{1,0:T(8,128)(2,1)S(1)}, bf16[32,2048]{1,0:T(8,128)(2,1)S(1)}, u32[]{:S(2)}, u32[]{:S(2)}) collective-permute-start(bf16[32,2048]{1,0:T(8,128)(2,1)S(1)} %get-tuple-element.44.refs_0_), channel_id=1, source_target_pairs={{0,2},{1,3},{2,0},{3,1},{4,6},{5,7},{6,4},{7,5},{8,10},{9,11},{10,... | collective-permute-start | bytes 393224 | tf_op jit(solution)/shard_map/ppermute | solution.py:18
  41.6 12.7 %collective-permute-start.13 = (bf16[32,2048]{1,0:T(8,128)(2,1)S(1)}, bf16[32,2048]{1,0:T(8,128)(2,1)S(1)}, u32[]{:S(2)}, u32[]{:S(2)}) collective-permute-start(bf16[32,2048]{1,0:T(8,128)(2,1)S(1)} %get-tuple-element.44.refs_0_), channel_id=1, source_target_pairs={{0,3},{1,2},{2,1},{3,0},{4,7},{5,6},{6,5},{7,4},{8,11},{9,10},{10,... | collective-permute-start | bytes 393224 | tf_op jit(solution)/shard_map/ppermute | solution.py:18
  43.0 12.5 %collective-permute-start.18 = (bf16[32,2048]{1,0:T(8,128)(2,1)S(1)}, bf16[32,2048]{1,0:T(8,128)(2,1)S(1)}, u32[]{:S(2)}, u32[]{:S(2)}) collective-permute-start(bf16[32,2048]{1,0:T(8,128)(2,1)S(1)} %get-tuple-element.42.refs_4_), channel_id=1, source_target_pairs={{0,1},{1,0},{2,3},{3,2},{4,5},{5,4},{6,7},{7,6},{8,9},{9,8},{10,11... | collective-permute-start | bytes 393224 | tf_op jit(solution)/shard_map/ppermute | solution.py:18
  51.7 13.3 %collective-permute-start.17 = (bf16[32,2048]{1,0:T(8,128)(2,1)S(1)}, bf16[32,2048]{1,0:T(8,128)(2,1)S(1)}, u32[]{:S(2)}, u32[]{:S(2)}) collective-permute-start(bf16[32,2048]{1,0:T(8,128)(2,1)S(1)} %get-tuple-element.42.refs_4_), channel_id=1, source_target_pairs={{0,2},{1,3},{2,0},{3,1},{4,6},{5,7},{6,4},{7,5},{8,10},{9,11},{10,... | collective-permute-start | bytes 393224 | tf_op jit(solution)/shard_map/ppermute | solution.py:18
  52.8 12.2 %collective-permute-start.16 = (bf16[32,2048]{1,0:T(8,128)(2,1)S(1)}, bf16[32,2048]{1,0:T(8,128)(2,1)S(1)}, u32[]{:S(2)}, u32[]{:S(2)}) collective-permute-start(bf16[32,2048]{1,0:T(8,128)(2,1)S(1)} %get-tuple-element.42.refs_4_), channel_id=1, source_target_pairs={{0,3},{1,2},{2,1},{3,0},{4,7},{5,6},{6,5},{7,4},{8,11},{9,10},{10,... | collective-permute-start | bytes 393224 | tf_op jit(solution)/shard_map/ppermute | solution.py:18
  68.2 2.7 %collective-permute-start.19 = (f32[128,2048]{1,0:T(8,128)S(1)}, f32[128,2048]{1,0:T(8,128)S(1)}, u32[]{:S(2)}, u32[]{:S(2)}) collective-permute-start(f32[128,2048]{1,0:T(8,128)S(1)} %get-tuple-element.38), channel_id=1, source_target_pairs={{0,4},{4,0},{8,12},{12,8},{16,20},{20,16},{24,28},{28,24},{1,5},{5... | collective-permute-start | bytes 3145736 | tf_op jit(solution)/shard_map/ppermute | solution.py:18
  71.0 6.4 %collective-permute-start.20 = (bf16[32,2048]{1,0:T(8,128)(2,1)S(1)}, bf16[32,2048]{1,0:T(8,128)(2,1)S(1)}, u32[]{:S(2)}, u32[]{:S(2)}) collective-permute-start(bf16[32,2048]{1,0:T(8,128)(2,1)S(1)} %get-tuple-element.46), channel_id=1, source_target_pairs={{0,8},{4,12},{8,0},{12,4},{16,24},{20,28},{24,16},{28,20},{1,9},{5... | collective-permute-start | bytes 393224 | tf_op jit(solution)/shard_map/ppermute | solution.py:18
  72.3 8.2 %collective-permute-start.22 = (bf16[32,2048]{1,0:T(8,128)(2,1)S(1)}, bf16[32,2048]{1,0:T(8,128)(2,1)S(1)}, u32[]{:S(2)}, u32[]{:S(2)}) collective-permute-start(bf16[32,2048]{1,0:T(8,128)(2,1)S(1)} %get-tuple-element.47), channel_id=1, source_target_pairs={{0,24},{4,28},{8,16},{12,20},{16,8},{20,12},{24,0},{28,4},{1,25},{... | collective-permute-start | bytes 393224 | tf_op jit(solution)/shard_map/ppermute | solution.py:18
  74.0 7.8 %collective-permute-start.21 = (bf16[32,2048]{1,0:T(8,128)(2,1)S(1)}, bf16[32,2048]{1,0:T(8,128)(2,1)S(1)}, u32[]{:S(2)}, u32[]{:S(2)}) collective-permute-start(bf16[32,2048]{1,0:T(8,128)(2,1)S(1)} %get-tuple-element.48), channel_id=1, source_target_pairs={{0,16},{4,20},{8,24},{12,28},{16,0},{20,4},{24,8},{28,12},{1,17},{... | collective-permute-start | bytes 393224 | tf_op jit(solution)/shard_map/ppermute | solution.py:18

commit v9 on v8

--- a/solution.py
+++ b/solution.py
@@ -16,6 +16,76 @@
 def exchange(value, axis, offset):
     size = lax.axis_size(axis)
     return lax.ppermute(value, axis, [(i, i ^ offset) for i in range(size)])
+
+
+def at_end(where, size):
+    return (where[1] == 0) | (where[1] == size - 1)
+
+
+def pass_kernel(where, mine, came, out):
+    @pl.when(at_end(where, 4))
+    def _():
+        out[...] = mine[...].astype(BF16)
+
+    @pl.when(jnp.logical_not(at_end(where, 4)))
+    def _():
+        out[...] = (mine[...] + came[...].astype(F32)).astype(BF16)
+
+
+def choose_kernel(where, mine, came, out):
+    @pl.when(at_end(where, 4))
+    def _():
+        out[...] = mine[...]
+
+    @pl.when(jnp.logical_not(at_end(where, 4)))
+    def _():
+        out[...] = came[...]
+
+
+def total_kernel(where, mine, near, far, came, total, lowered):
+    total[...] = mine[...] + near[...].astype(F32) + far[...].astype(F32)
+
+    @pl.when(at_end(where, 4))
+    def _():
+        total[...] += came[...].astype(F32)
+
+    lowered[...] = total[...].astype(BF16)
+
+
+def small(kernel, where, *values, types):
+    vmem = pl.BlockSpec(memory_space=pltpu.VMEM)
+    return pl.pallas_call(
+        kernel,
+        in_specs=[pl.BlockSpec(memory_space=pltpu.SMEM)] + [vmem] * len(values),
+        out_specs=[vmem] * len(types),
+        out_shape=[jax.ShapeDtypeStruct(values[0].shape, kind) for kind in types],
+        compiler_params=pltpu.CompilerParams(vmem_limit_bytes=VMEM_LIMIT),
+        cost_estimate=pl.CostEstimate(flops=values[0].size, bytes_accessed=8 * values[0].size, transcendentals=0),
+        name=kernel.__name__.replace("_kernel", "_rows"),
+    )(where, *values)
+
+
+def window_sums(where, terms):
+    size = len(terms)
+    if size == 4:
+        came = lax.ppermute(terms[2], "col", [(0, 1), (3, 2), (2, 0), (1, 3)])
+        near = exchange(terms[1], "col", 1)
+        (onward,) = small(pass_kernel, where, terms[3], came, types=[BF16])
+        far = exchange(onward, "col", 3)
+        return small(total_kernel, where, terms[0], near, far, came, types=[F32, BF16])
+    total = terms[0]
+    for offset in range(1, size):
+        total = total + exchange(terms[offset].astype(BF16), "col", offset).astype(F32)
+    return total, total.astype(BF16)
+
+
+def window_spread(where, lowered, size):
+    if size == 4:
+        far = exchange(lowered, "col", 3)
+        near = exchange(lowered, "col", 1)
+        (onward,) = small(choose_kernel, where, lowered, far, types=[BF16])
+        return [lowered, near, lax.ppermute(onward, "col", [(0, 2), (3, 1), (1, 0), (2, 3)]), far]
+    return [lowered] + [exchange(lowered, "col", offset) for offset in range(1, size)]
 
 
 def mask_kernel(where, mask_ref, green_ref, tiles, token, sems, *, block):
@@ -75,7 +145,8 @@
     width = blocks[0].shape[0] * len(blocks)
     share = width // len(offsets_col) // chunks
     vmem = pl.BlockSpec(memory_space=pltpu.VMEM)
-    outs = [jax.ShapeDtypeStruct((share, rows), F32 if offset == 0 else BF16) for offset in offsets_col] * chunks
+    exact = (0, offsets_col[-1])
+    outs = [jax.ShapeDtypeStruct((share, rows), F32 if offset in exact else BF16) for offset in offsets_col] * chunks
     return pl.pallas_call(
         functools.partial(
             sketch_kernel, offsets_row=offsets_row, offsets_col=offsets_col, piece=blocks[0].shape[0] // chunks
@@ -150,7 +221,6 @@
     offsets_core = list(range(0, n_row, 2))
     gather_core = [0] + offsets_core[:0:-1]
     offsets_row = gather_core + [offset ^ 1 for offset in gather_core]
-    far_first = [0] + offsets_col[:0:-1]
 
     tiles, token = masked(where, green, mask)
 
@@ -162,16 +232,12 @@
     parts = partial_sketch(where, tiles, blocks, token, offsets_row, offsets_col, chunks)
     totals, shares = [], []
     for chunk in range(chunks):
-        terms = parts[chunk * n_col : (chunk + 1) * n_col]
-        total = terms[0]
-        for offset in offsets_col[1:]:
-            total = total + exchange(terms[offset], "col", offset).astype(F32)
+        total, lowered = window_sums(where, parts[chunk * n_col : (chunk + 1) * n_col])
         totals.append(total)
-        lowered = total.astype(BF16)
-        shares.append([lowered] + [exchange(lowered, "col", offset) for offset in far_first[1:]])
+        shares.append(window_spread(where, lowered, n_col))
 
     flat = [share for per_chunk in shares for share in per_chunk]
-    *mine, others = partial_adjoint(where, tiles, flat, far_first, offsets_core, width, chunks)
+    *mine, others = partial_adjoint(where, tiles, flat, offsets_col, offsets_core, width, chunks)
     others = exchange(others, "row", 1)
     pairs = [m + others[k * own_width : (k + 1) * own_width] for k, m in enumerate(mine)]
     adjoint = pairs[0]

time: 82.8 us -> 74.4 us (0.90)
  starting transfers between devices: 43.5 us -> 35.3 us
  waiting for transfers between devices: 25.5 us -> 21.9 us
  Pallas kernels: 10.4 us -> 13.8 us
    ppermute x23 -> x19, starting transfers between devices: 43.5 us -> 25.4 us  [exchange(): return lax.ppermute(value, axis, [(i, i ^ offset) for i in range(size)])]
    ppermute x0 -> x4, starting transfers between devices: none -> 9.85 us  [the longest x2 5.62 us: window_spread(): lax.ppermute(onward, 'col', [(0, 2), (3, 1), (1, 0), (2, 3)])]
    ppermute x23 -> x19, waiting for transfers between devices: 25.5 us -> 16.5 us  [exchange(): return lax.ppermute(value, axis, [(i, i ^ offset) for i in range(size)])]
    ppermute x0 -> x4, waiting for transfers between devices: none -> 5.45 us  [the longest x2 2.81 us: window_spread(): lax.ppermute(onward, 'col', [(0, 2), (3, 1), (1, 0), (2, 3)])]
    pallas_call x0 -> x6, Pallas kernels: none -> 3.49 us  [small(): pl.pallas_call(kernel, in_specs=[pl.BlockSpec(memory_space=pltpu.SMEM)] +...]
  transfers between devices with their start and end apart: 23 -> 23, of which waited for: 12 -> 15; matrix products, arithmetic and copies ran while one was open for 1% -> 1% of each run, Pallas kernels for 5% -> 10%
where the time goes in v9:
time: 74.4 us; the launch traced here: 74.2 us
  starting transfers between devices  35.3 us (47%)
  waiting for transfers between devices  21.9 us (29%)
  Pallas kernels  13.8 us (19%)
  other arithmetic  1.75 us (2%)
  between operations  0.76 us (1%)
    ppermute x19, starting transfers between devices, exchange(): return lax.ppermute(value, axis, [(i, i ^ offset) for i in range(size)])  25.4 us
    ppermute x19, waiting for transfers between devices, exchange(): return lax.ppermute(value, axis, [(i, i ^ offset) for i in range(size)])  16.5 us
    ppermute x2, starting transfers between devices, window_spread(): lax.ppermute(onward, 'col', [(0, 2), (3, 1), (1, 0), (2, 3)])  5.62 us
    ppermute x2, starting transfers between devices, window_sums(): came = lax.ppermute(terms[2], 'col', [(0, 1), (3, 2), (2, 0), (1, 3)])  4.23 us
    pallas_call x1, Pallas kernels, masked(): pl.pallas_call(functools.partial(mask_kernel, block=rows // mask.shape[0]...  4.16 us
    pallas_call x6, Pallas kernels, small(): pl.pallas_call(kernel, in_specs=[pl.BlockSpec(memory_space=pltpu.SMEM)] +...  3.49 us
    pallas_call x1, Pallas kernels, partial_adjoint(): pl.pallas_call(functools.partial(adjoint_kernel, offsets_col=offsets_col,...  3.11 us
    pallas_call x1, Pallas kernels, partial_sketch(): pl.pallas_call(functools.partial(sketch_kernel, offsets_row=offsets_row,...  3.04 us
  transfers between devices with their start and end apart: 23, of which 15 were waited for; matrix products, arithmetic and copies ran while one was open for 1% of the time, Pallas kernels for 10%

profile of v9, /device:TPU:0, one launch (start us, length us, event | category | flops | bytes accessed | tf_op | source)
XLA Modules:
  0.0 74.2 jit_solution(2370180006596261452)
XLA Ops:
  0.6 3.0 %collective-permute-start.2 = (bf16[32,2048]{1,0:T(8,128)(2,1)}, bf16[32,2048]{1,0:T(8,128)(2,1)S(1)}, u32[]{:S(2)}, u32[]{:S(2)}) collective-permute-start(bf16[32,2048]{1,0:T(8,128)(2,1)} %bitcast.12), channel_id=1, source_target_pairs={{0,8},{4,12},{8,0},{12,4},{16,24},{20,28},{24,16},{28,20},{1,9},{5... | collective-permute-start | bytes 393224 | tf_op jit(solution)/shard_map/ppermute | solution.py:18
  3.6 1.5 %collective-permute-start.1 = (bf16[32,2048]{1,0:T(8,128)(2,1)}, bf16[32,2048]{1,0:T(8,128)(2,1)S(1)}, u32[]{:S(2)}, u32[]{:S(2)}) collective-permute-start(bf16[32,2048]{1,0:T(8,128)(2,1)} %bitcast.13), channel_id=1, source_target_pairs={{0,16},{4,20},{8,24},{12,28},{16,0},{20,4},{24,8},{28,12},{1,17},{... | collective-permute-start | bytes 393224 | tf_op jit(solution)/shard_map/ppermute | solution.py:18
  5.3 0.7 copy-done.1
  5.9 4.2 %masked_tiles.1 = (bf16[2048,2048]{1,0:T(8,128)(2,1)S(1)}, f32[8,128]{1,0:T(8,128)S(1)}) custom-call(s32[2]{0:T(128)S(1)} %pad_add_fusion.where, s32[8,8]{1,0:T(8,128)S(1)} %copy-done.1, bf16[2048,2048]{1,0:T(8,128)(2,1)} %green_ref.1), custom_call_target="tpu_custom_call" | custom-call | bytes 8388608 | tf_op jit(solution)/shard_map/masked_tiles/pallas_call | solution.py:111
  10.1 1.5 %collective-permute-done.1.refs_2_ = bf16[32,2048]{1,0:T(8,128)(2,1)S(1)} collective-permute-done((bf16[32,2048]{1,0:T(8,128)(2,1)}, bf16[32,2048]{1,0:T(8,128)(2,1)S(1)}, u32[]{:S(2)}, u32[]{:S(2)}) %collective-permute-start.1) | collective-permute-done | bytes 131104 | tf_op jit(solution)/shard_map/ppermute | solution.py:18
  13.7 3.0 %partial_sketch.1 = (f32[32,2048]{1,0:T(8,128)S(1)}, bf16[32,2048]{1,0:T(8,128)(2,1)S(1)}, bf16[32,2048]{1,0:T(8,128)(2,1)S(1)}, f32[32,2048]{1,0:T(8,128)S(1)},...) custom-call(s32[2]{0:T(128)S(1)} %pad_add_fusion.where, ...), custom_call_target="tpu_custom_call" | custom-call | flops 2147483648 | bytes 8388608 | tf_op jit(solution)/shard_map/partial_sketch/pallas_call | solution.py:150
  16.7 1.6 %collective-permute-start.8 = (bf16[32,2048]{1,0:T(8,128)(2,1)S(1)}, bf16[32,2048]{1,0:T(8,128)(2,1)S(1)}, u32[]{:S(2)}, u32[]{:S(2)}) collective-permute-start(bf16[32,2048]{1,0:T(8,128)(2,1)S(1)} %get-tuple-element.36), channel_id=1, source_target_pairs={{0,1},{3,2},{2,0},{1,3},{4,5},{7,6},{6,4},{5,7},{8,9},{11,10},{10,... | collective-permute-start | bytes 393224 | tf_op jit(solution)/shard_map/ppermute | solution.py:71
  18.4 2.6 %collective-permute-start.11 = (bf16[32,2048]{1,0:T(8,128)(2,1)S(1)}, bf16[32,2048]{1,0:T(8,128)(2,1)S(1)}, u32[]{:S(2)}, u32[]{:S(2)}) collective-permute-start(bf16[32,2048]{1,0:T(8,128)(2,1)S(1)} %get-tuple-element.41), channel_id=1, source_target_pairs={{0,1},{3,2},{2,0},{1,3},{4,5},{7,6},{6,4},{5,7},{8,9},{11,10},{10,... | collective-permute-start | bytes 393224 | tf_op jit(solution)/shard_map/ppermute | solution.py:71
  21.4 2.6 %collective-permute-done.8.came = bf16[32,2048]{1,0:T(8,128)(2,1)S(1)} collective-permute-done((bf16[32,2048]{1,0:T(8,128)(2,1)S(1)}, bf16[32,2048]{1,0:T(8,128)(2,1)S(1)}, u32[]{:S(2)}, u32[]{:S(2)}) %collective-permute-start.8) | collective-permute-done | bytes 131104 | tf_op jit(solution)/shard_map/ppermute | solution.py:71
  24.6 3.7 %collective-permute-start.9 = (bf16[32,2048]{1,0:T(8,128)(2,1)S(1)}, bf16[32,2048]{1,0:T(8,128)(2,1)S(1)}, u32[]{:S(2)}, u32[]{:S(2)}) collective-permute-start(bf16[32,2048]{1,0:T(8,128)(2,1)S(1)} %pass_rows.2), channel_id=1, source_target_pairs={{0,3},{1,2},{2,1},{3,0},{4,7},{5,6},{6,5},{7,4},{8,11},{9,10},{10,... | collective-permute-start | bytes 393224 | tf_op jit(solution)/shard_map/ppermute | solution.py:18
  28.4 0.6 pass_rows.3
  28.9 2.2 %collective-permute-start.12 = (bf16[32,2048]{1,0:T(8,128)(2,1)S(1)}, bf16[32,2048]{1,0:T(8,128)(2,1)S(1)}, u32[]{:S(2)}, u32[]{:S(2)}) collective-permute-start(bf16[32,2048]{1,0:T(8,128)(2,1)S(1)} %pass_rows.3), channel_id=1, source_target_pairs={{0,3},{1,2},{2,1},{3,0},{4,7},{5,6},{6,5},{7,4},{8,11},{9,10},{10,... | collective-permute-start | bytes 393224 | tf_op jit(solution)/shard_map/ppermute | solution.py:18
  31.1 2.5 %collective-permute-done.9.far = bf16[32,2048]{1,0:T(8,128)(2,1)S(1)} collective-permute-done((bf16[32,2048]{1,0:T(8,128)(2,1)S(1)}, bf16[32,2048]{1,0:T(8,128)(2,1)S(1)}, u32[]{:S(2)}, u32[]{:S(2)}) %collective-permute-start.9) | collective-permute-done | bytes 131104 | tf_op jit(solution)/shard_map/ppermute | solution.py:18
  33.6 0.6 total_rows.2
  34.2 3.2 %collective-permute-start.14 = (bf16[32,2048]{1,0:T(8,128)(2,1)S(1)}, bf16[32,2048]{1,0:T(8,128)(2,1)S(1)}, u32[]{:S(2)}, u32[]{:S(2)}) collective-permute-start(bf16[32,2048]{1,0:T(8,128)(2,1)S(1)} %get-tuple-element.43.mine.refs_0_), channel_id=1, source_target_pairs={{0,3},{1,2},{2,1},{3,0},{4,7},{5,6},{6,5},{7,4},{8,11},{9,10},{10,... | collective-permute-start | bytes 393224 | tf_op jit(solution)/shard_map/ppermute | solution.py:18
  37.4 1.9 %collective-permute-done.12.far = bf16[32,2048]{1,0:T(8,128)(2,1)S(1)} collective-permute-done((bf16[32,2048]{1,0:T(8,128)(2,1)S(1)}, bf16[32,2048]{1,0:T(8,128)(2,1)S(1)}, u32[]{:S(2)}, u32[]{:S(2)}) %collective-permute-start.12) | collective-permute-done | bytes 131104 | tf_op jit(solution)/shard_map/ppermute | solution.py:18
  39.3 0.6 total_rows.3
  39.9 2.6 %collective-permute-start.17 = (bf16[32,2048]{1,0:T(8,128)(2,1)S(1)}, bf16[32,2048]{1,0:T(8,128)(2,1)S(1)}, u32[]{:S(2)}, u32[]{:S(2)}) collective-permute-start(bf16[32,2048]{1,0:T(8,128)(2,1)S(1)} %get-tuple-element.44.mine.refs_4_), channel_id=1, source_target_pairs={{0,3},{1,2},{2,1},{3,0},{4,7},{5,6},{6,5},{7,4},{8,11},{9,10},{10,... | collective-permute-start | bytes 393224 | tf_op jit(solution)/shard_map/ppermute | solution.py:18
  42.5 4.1 %collective-permute-start.13 = (bf16[32,2048]{1,0:T(8,128)(2,1)S(1)}, bf16[32,2048]{1,0:T(8,128)(2,1)S(1)}, u32[]{:S(2)}, u32[]{:S(2)}) collective-permute-start(bf16[32,2048]{1,0:T(8,128)(2,1)S(1)} %get-tuple-element.43.mine.refs_0_), channel_id=1, source_target_pairs={{0,1},{1,0},{2,3},{3,2},{4,5},{5,4},{6,7},{7,6},{8,9},{9,8},{10,11... | collective-permute-start | bytes 393224 | tf_op jit(solution)/shard_map/ppermute | solution.py:18
  47.2 2.6 %collective-permute-start.15 = (bf16[32,2048]{1,0:T(8,128)(2,1)S(1)}, bf16[32,2048]{1,0:T(8,128)(2,1)S(1)}, u32[]{:S(2)}, u32[]{:S(2)}) collective-permute-start(bf16[32,2048]{1,0:T(8,128)(2,1)S(1)} %choose_rows.2), channel_id=1, source_target_pairs={{0,2},{3,1},{1,0},{2,3},{4,6},{7,5},{5,4},{6,7},{8,10},{11,9},{9,8... | collective-permute-start | bytes 393224 | tf_op jit(solution)/shard_map/ppermute | solution.py:87
  50.4 3.0 %collective-permute-start.18 = (bf16[32,2048]{1,0:T(8,128)(2,1)S(1)}, bf16[32,2048]{1,0:T(8,128)(2,1)S(1)}, u32[]{:S(2)}, u32[]{:S(2)}) collective-permute-start(bf16[32,2048]{1,0:T(8,128)(2,1)S(1)} %choose_rows.3), channel_id=1, source_target_pairs={{0,2},{3,1},{1,0},{2,3},{4,6},{7,5},{5,4},{6,7},{8,10},{11,9},{9,8... | collective-permute-start | bytes 393224 | tf_op jit(solution)/shard_map/ppermute | solution.py:87
  53.9 1.4 %collective-permute-done.15.refs_2_ = bf16[32,2048]{1,0:T(8,128)(2,1)S(1)} collective-permute-done((bf16[32,2048]{1,0:T(8,128)(2,1)S(1)}, bf16[32,2048]{1,0:T(8,128)(2,1)S(1)}, u32[]{:S(2)}, u32[]{:S(2)}) %collective-permute-start.15) | collective-permute-done | bytes 131104 | tf_op jit(solution)/shard_map/ppermute | solution.py:87
  55.3 1.4 %collective-permute-done.18.refs_6_ = bf16[32,2048]{1,0:T(8,128)(2,1)S(1)} collective-permute-done((bf16[32,2048]{1,0:T(8,128)(2,1)S(1)}, bf16[32,2048]{1,0:T(8,128)(2,1)S(1)}, u32[]{:S(2)}, u32[]{:S(2)}) %collective-permute-start.18) | collective-permute-done | bytes 131104 | tf_op jit(solution)/shard_map/ppermute | solution.py:87
  56.7 3.1 %partial_adjoint.1 = (f32[32,2048]{1,0:T(8,128)S(1)}, f32[32,2048]{1,0:T(8,128)S(1)}, f32[32,2048]{1,0:T(8,128)S(1)}, f32[32,2048]{1,0:T(8,128)S(1)}, f32[128,2048]{1,0:T(8,128)S(1)}) custom-call(s32[2]{0:T(128)S(1)} %pad_add_fusion.where, bf16[2048,2048]{1,0:T(8,128)(2,1)S(1)} %get-tuple-element.26.tiles, ...), custom_call_target="tpu_custom_call" | custom-call | flops 2147483648 | bytes 8388608 | tf_op jit(solution)/shard_map/partial_adjoint/pallas_call | solution.py:194
  59.9 2.6 %collective-permute-done.19 = f32[128,2048]{1,0:T(8,128)S(1)} collective-permute-done((f32[128,2048]{1,0:T(8,128)S(1)}, f32[128,2048]{1,0:T(8,128)S(1)}, u32[]{:S(2)}, u32[]{:S(2)}) %collective-permute-start.19) | collective-permute-done | bytes 1048608 | tf_op jit(solution)/shard_map/ppermute | solution.py:18
  62.6 1.3 %collective-permute-start.20 = (bf16[32,2048]{1,0:T(8,128)(2,1)S(1)}, bf16[32,2048]{1,0:T(8,128)(2,1)S(1)}, u32[]{:S(2)}, u32[]{:S(2)}) collective-permute-start(bf16[32,2048]{1,0:T(8,128)(2,1)S(1)} %get-tuple-element.50), channel_id=1, source_target_pairs={{0,8},{4,12},{8,0},{12,4},{16,24},{20,28},{24,16},{28,20},{1,9},{5... | collective-permute-start | bytes 393224 | tf_op jit(solution)/shard_map/ppermute | solution.py:18
  63.9 1.7 %collective-permute-start.22 = (bf16[32,2048]{1,0:T(8,128)(2,1)S(1)}, bf16[32,2048]{1,0:T(8,128)(2,1)S(1)}, u32[]{:S(2)}, u32[]{:S(2)}) collective-permute-start(bf16[32,2048]{1,0:T(8,128)(2,1)S(1)} %get-tuple-element.51), channel_id=1, source_target_pairs={{0,24},{4,28},{8,16},{12,20},{16,8},{20,12},{24,0},{28,4},{1,25},{... | collective-permute-start | bytes 393224 | tf_op jit(solution)/shard_map/ppermute | solution.py:18
  66.1 0.8 %pad_maximum_fusion = f32[2,32,2048]{2,1,0:T(8,128)} fusion(f32[2,16,2048]{2,1,0:T(8,128)S(1)} %bitcast.11, f32[2,16,2048]{2,1,0:T(8,128)S(1)} %bitcast.10), kind=kLoop, calls=%fused_computation | loop fusion | flops 131072 | bytes 1048576 | tf_op jit(solution)/shard_map/concatenate | solution.py:210
  67.0 2.0 %collective-permute-done.20 = bf16[32,2048]{1,0:T(8,128)(2,1)S(1)} collective-permute-done((bf16[32,2048]{1,0:T(8,128)(2,1)S(1)}, bf16[32,2048]{1,0:T(8,128)(2,1)S(1)}, u32[]{:S(2)}, u32[]{:S(2)}) %collective-permute-start.20) | collective-permute-done | bytes 131104 | tf_op jit(solution)/shard_map/ppermute | solution.py:18
  69.0 3.1 %collective-permute-done.22 = bf16[32,2048]{1,0:T(8,128)(2,1)S(1)} collective-permute-done((bf16[32,2048]{1,0:T(8,128)(2,1)S(1)}, bf16[32,2048]{1,0:T(8,128)(2,1)S(1)}, u32[]{:S(2)}, u32[]{:S(2)}) %collective-permute-start.22) | collective-permute-done | bytes 131104 | tf_op jit(solution)/shard_map/ppermute | solution.py:18
  72.1 1.4 %collective-permute-done.21 = bf16[32,2048]{1,0:T(8,128)(2,1)S(1)} collective-permute-done((bf16[32,2048]{1,0:T(8,128)(2,1)S(1)}, bf16[32,2048]{1,0:T(8,128)(2,1)S(1)}, u32[]{:S(2)}, u32[]{:S(2)}) %collective-permute-start.21) | collective-permute-done | bytes 131104 | tf_op jit(solution)/shard_map/ppermute | solution.py:18
  73.4 0.8 %fusion.6 = f32[2048,32]{0,1:T(8,128)} fusion(f32[32,2048]{1,0:T(8,128)S(1)} %get-tuple-element.45, f32[128,2048]{1,0:T(8,128)S(1)} %collective-permute-done.19, bf16[32,2048]{1,0:T(8,128)(2,1)S(1)} %collective-permute-done.22, bf16[32,2048]{1,0:T(8,128)(2,1)S(1)} %collective-permute-done.21, bf16[32,2048]{1,0:T(8,128)(2,1)S(1)} %collective-permute-done.20), kind=kLoop, calls=%fused_computation.11 | loop fusion | flops 458752 | bytes 1179648 | tf_op jit(solution)/shard_map/transpose | solution.py:246
  (31 shorter events, 5.5 us)
Async XLA Ops:
  0.6 11.0 %copy-start = (bf16[2048,32]{0,1:T(8,128)(2,1)S(1)}, bf16[2048,32]{0,1:T(8,128)(2,1)}, u32[]{:S(2)}) copy-start(bf16[2048,32]{0,1:T(8,128)(2,1)} %param.5) | copy-start | bytes 393220
  0.6 9.5 %collective-permute-start.2 = (bf16[32,2048]{1,0:T(8,128)(2,1)}, bf16[32,2048]{1,0:T(8,128)(2,1)S(1)}, u32[]{:S(2)}, u32[]{:S(2)}) collective-permute-start(bf16[32,2048]{1,0:T(8,128)(2,1)} %bitcast.12), channel_id=1, source_target_pairs={{0,8},{4,12},{8,0},{12,4},{16,24},{20,28},{24,16},{28,20},{1,9},{5... | collective-permute-start | bytes 393224 | tf_op jit(solution)/shard_map/ppermute | solution.py:18
  3.6 8.0 %collective-permute-start.1 = (bf16[32,2048]{1,0:T(8,128)(2,1)}, bf16[32,2048]{1,0:T(8,128)(2,1)S(1)}, u32[]{:S(2)}, u32[]{:S(2)}) collective-permute-start(bf16[32,2048]{1,0:T(8,128)(2,1)} %bitcast.13), channel_id=1, source_target_pairs={{0,16},{4,20},{8,24},{12,28},{16,0},{20,4},{24,8},{28,12},{1,17},{... | collective-permute-start | bytes 393224 | tf_op jit(solution)/shard_map/ppermute | solution.py:18
  5.2 6.5 %collective-permute-start = (bf16[32,2048]{1,0:T(8,128)(2,1)}, bf16[32,2048]{1,0:T(8,128)(2,1)S(1)}, u32[]{:S(2)}, u32[]{:S(2)}) collective-permute-start(bf16[32,2048]{1,0:T(8,128)(2,1)} %bitcast.14), channel_id=1, source_target_pairs={{0,24},{4,28},{8,16},{12,20},{16,8},{20,12},{24,0},{28,4},{1,25},{... | collective-permute-start | bytes 393224 | tf_op jit(solution)/shard_map/ppermute | solution.py:18
  5.3 0.7 copy-start.1
  11.6 1.4 %collective-permute-start.3 = (bf16[32,2048]{1,0:T(8,128)(2,1)S(1)}, bf16[32,2048]{1,0:T(8,128)(2,1)S(1)}, u32[]{:S(2)}, u32[]{:S(2)}) collective-permute-start(bf16[32,2048]{1,0:T(8,128)(2,1)S(1)} %bitcast.15), channel_id=1, source_target_pairs={{0,4},{4,0},{8,12},{12,8},{16,20},{20,16},{24,28},{28,24},{1,5},{5... | collective-permute-start | bytes 393224 | tf_op jit(solution)/shard_map/ppermute | solution.py:18
  11.6 1.5 %collective-permute-start.4 = (bf16[32,2048]{1,0:T(8,128)(2,1)S(1)}, bf16[32,2048]{1,0:T(8,128)(2,1)S(1)}, u32[]{:S(2)}, u32[]{:S(2)}) collective-permute-start(bf16[32,2048]{1,0:T(8,128)(2,1)S(1)} %collective-permute-done.refs_1_), channel_id=1, source_target_pairs={{0,4},{4,0},{8,12},{12,8},{16,20},{20,16},{24,28},{28,24},{1,5},{5... | collective-permute-start | bytes 393224 | tf_op jit(solution)/shard_map/ppermute | solution.py:18
  12.1 1.3 %collective-permute-start.5 = (bf16[32,2048]{1,0:T(8,128)(2,1)S(1)}, bf16[32,2048]{1,0:T(8,128)(2,1)S(1)}, u32[]{:S(2)}, u32[]{:S(2)}) collective-permute-start(bf16[32,2048]{1,0:T(8,128)(2,1)S(1)} %collective-permute-done.1.refs_2_), channel_id=1, source_target_pairs={{0,4},{4,0},{8,12},{12,8},{16,20},{20,16},{24,28},{28,24},{1,5},{5... | collective-permute-start | bytes 393224 | tf_op jit(solution)/shard_map/ppermute | solution.py:18
  12.2 1.5 %collective-permute-start.6 = (bf16[32,2048]{1,0:T(8,128)(2,1)S(1)}, bf16[32,2048]{1,0:T(8,128)(2,1)S(1)}, u32[]{:S(2)}, u32[]{:S(2)}) collective-permute-start(bf16[32,2048]{1,0:T(8,128)(2,1)S(1)} %collective-permute-done.2.refs_3_), channel_id=1, source_target_pairs={{0,4},{4,0},{8,12},{12,8},{16,20},{20,16},{24,28},{28,24},{1,5},{5... | collective-permute-start | bytes 393224 | tf_op jit(solution)/shard_map/ppermute | solution.py:18
  16.7 7.3 %collective-permute-start.8 = (bf16[32,2048]{1,0:T(8,128)(2,1)S(1)}, bf16[32,2048]{1,0:T(8,128)(2,1)S(1)}, u32[]{:S(2)}, u32[]{:S(2)}) collective-permute-start(bf16[32,2048]{1,0:T(8,128)(2,1)S(1)} %get-tuple-element.36), channel_id=1, source_target_pairs={{0,1},{3,2},{2,0},{1,3},{4,5},{7,6},{6,4},{5,7},{8,9},{11,10},{10,... | collective-permute-start | bytes 393224 | tf_op jit(solution)/shard_map/ppermute | solution.py:71
  18.4 10.0 %collective-permute-start.11 = (bf16[32,2048]{1,0:T(8,128)(2,1)S(1)}, bf16[32,2048]{1,0:T(8,128)(2,1)S(1)}, u32[]{:S(2)}, u32[]{:S(2)}) collective-permute-start(bf16[32,2048]{1,0:T(8,128)(2,1)S(1)} %get-tuple-element.41), channel_id=1, source_target_pairs={{0,1},{3,2},{2,0},{1,3},{4,5},{7,6},{6,4},{5,7},{8,9},{11,10},{10,... | collective-permute-start | bytes 393224 | tf_op jit(solution)/shard_map/ppermute | solution.py:71
  21.0 10.2 %collective-permute-start.7 = (bf16[32,2048]{1,0:T(8,128)(2,1)S(1)}, bf16[32,2048]{1,0:T(8,128)(2,1)S(1)}, u32[]{:S(2)}, u32[]{:S(2)}) collective-permute-start(bf16[32,2048]{1,0:T(8,128)(2,1)S(1)} %get-tuple-element.34), channel_id=1, source_target_pairs={{0,1},{1,0},{2,3},{3,2},{4,5},{5,4},{6,7},{7,6},{8,9},{9,8},{10,11... | collective-permute-start | bytes 393224 | tf_op jit(solution)/shard_map/ppermute | solution.py:18
  24.6 8.9 %collective-permute-start.9 = (bf16[32,2048]{1,0:T(8,128)(2,1)S(1)}, bf16[32,2048]{1,0:T(8,128)(2,1)S(1)}, u32[]{:S(2)}, u32[]{:S(2)}) collective-permute-start(bf16[32,2048]{1,0:T(8,128)(2,1)S(1)} %pass_rows.2), channel_id=1, source_target_pairs={{0,3},{1,2},{2,1},{3,0},{4,7},{5,6},{6,5},{7,4},{8,11},{9,10},{10,... | collective-permute-start | bytes 393224 | tf_op jit(solution)/shard_map/ppermute | solution.py:18
  28.4 9.1 %collective-permute-start.10 = (bf16[32,2048]{1,0:T(8,128)(2,1)S(1)}, bf16[32,2048]{1,0:T(8,128)(2,1)S(1)}, u32[]{:S(2)}, u32[]{:S(2)}) collective-permute-start(bf16[32,2048]{1,0:T(8,128)(2,1)S(1)} %get-tuple-element.39), channel_id=1, source_target_pairs={{0,1},{1,0},{2,3},{3,2},{4,5},{5,4},{6,7},{7,6},{8,9},{9,8},{10,11... | collective-permute-start | bytes 393224 | tf_op jit(solution)/shard_map/ppermute | solution.py:18
  28.9 10.4 %collective-permute-start.12 = (bf16[32,2048]{1,0:T(8,128)(2,1)S(1)}, bf16[32,2048]{1,0:T(8,128)(2,1)S(1)}, u32[]{:S(2)}, u32[]{:S(2)}) collective-permute-start(bf16[32,2048]{1,0:T(8,128)(2,1)S(1)} %pass_rows.3), channel_id=1, source_target_pairs={{0,3},{1,2},{2,1},{3,0},{4,7},{5,6},{6,5},{7,4},{8,11},{9,10},{10,... | collective-permute-start | bytes 393224 | tf_op jit(solution)/shard_map/ppermute | solution.py:18
  34.2 12.4 %collective-permute-start.14 = (bf16[32,2048]{1,0:T(8,128)(2,1)S(1)}, bf16[32,2048]{1,0:T(8,128)(2,1)S(1)}, u32[]{:S(2)}, u32[]{:S(2)}) collective-permute-start(bf16[32,2048]{1,0:T(8,128)(2,1)S(1)} %get-tuple-element.43.mine.refs_0_), channel_id=1, source_target_pairs={{0,3},{1,2},{2,1},{3,0},{4,7},{5,6},{6,5},{7,4},{8,11},{9,10},{10,... | collective-permute-start | bytes 393224 | tf_op jit(solution)/shard_map/ppermute | solution.py:18
  39.9 9.9 %collective-permute-start.17 = (bf16[32,2048]{1,0:T(8,128)(2,1)S(1)}, bf16[32,2048]{1,0:T(8,128)(2,1)S(1)}, u32[]{:S(2)}, u32[]{:S(2)}) collective-permute-start(bf16[32,2048]{1,0:T(8,128)(2,1)S(1)} %get-tuple-element.44.mine.refs_4_), channel_id=1, source_target_pairs={{0,3},{1,2},{2,1},{3,0},{4,7},{5,6},{6,5},{7,4},{8,11},{9,10},{10,... | collective-permute-start | bytes 393224 | tf_op jit(solution)/shard_map/ppermute | solution.py:18
  42.5 10.9 %collective-permute-start.13 = (bf16[32,2048]{1,0:T(8,128)(2,1)S(1)}, bf16[32,2048]{1,0:T(8,128)(2,1)S(1)}, u32[]{:S(2)}, u32[]{:S(2)}) collective-permute-start(bf16[32,2048]{1,0:T(8,128)(2,1)S(1)} %get-tuple-element.43.mine.refs_0_), channel_id=1, source_target_pairs={{0,1},{1,0},{2,3},{3,2},{4,5},{5,4},{6,7},{7,6},{8,9},{9,8},{10,11... | collective-permute-start | bytes 393224 | tf_op jit(solution)/shard_map/ppermute | solution.py:18
  46.6 7.3 %collective-permute-start.16 = (bf16[32,2048]{1,0:T(8,128)(2,1)S(1)}, bf16[32,2048]{1,0:T(8,128)(2,1)S(1)}, u32[]{:S(2)}, u32[]{:S(2)}) collective-permute-start(bf16[32,2048]{1,0:T(8,128)(2,1)S(1)} %get-tuple-element.44.mine.refs_4_), channel_id=1, source_target_pairs={{0,1},{1,0},{2,3},{3,2},{4,5},{5,4},{6,7},{7,6},{8,9},{9,8},{10,11... | collective-permute-start | bytes 393224 | tf_op jit(solution)/shard_map/ppermute | solution.py:18
  47.2 8.1 %collective-permute-start.15 = (bf16[32,2048]{1,0:T(8,128)(2,1)S(1)}, bf16[32,2048]{1,0:T(8,128)(2,1)S(1)}, u32[]{:S(2)}, u32[]{:S(2)}) collective-permute-start(bf16[32,2048]{1,0:T(8,128)(2,1)S(1)} %choose_rows.2), channel_id=1, source_target_pairs={{0,2},{3,1},{1,0},{2,3},{4,6},{7,5},{5,4},{6,7},{8,10},{11,9},{9,8... | collective-permute-start | bytes 393224 | tf_op jit(solution)/shard_map/ppermute | solution.py:87
  50.4 6.3 %collective-permute-start.18 = (bf16[32,2048]{1,0:T(8,128)(2,1)S(1)}, bf16[32,2048]{1,0:T(8,128)(2,1)S(1)}, u32[]{:S(2)}, u32[]{:S(2)}) collective-permute-start(bf16[32,2048]{1,0:T(8,128)(2,1)S(1)} %choose_rows.3), channel_id=1, source_target_pairs={{0,2},{3,1},{1,0},{2,3},{4,6},{7,5},{5,4},{6,7},{8,10},{11,9},{9,8... | collective-permute-start | bytes 393224 | tf_op jit(solution)/shard_map/ppermute | solution.py:87
  59.8 2.7 %collective-permute-start.19 = (f32[128,2048]{1,0:T(8,128)S(1)}, f32[128,2048]{1,0:T(8,128)S(1)}, u32[]{:S(2)}, u32[]{:S(2)}) collective-permute-start(f32[128,2048]{1,0:T(8,128)S(1)} %get-tuple-element.46), channel_id=1, source_target_pairs={{0,4},{4,0},{8,12},{12,8},{16,20},{20,16},{24,28},{28,24},{1,5},{5... | collective-permute-start | bytes 3145736 | tf_op jit(solution)/shard_map/ppermute | solution.py:18
  62.6 6.4 %collective-permute-start.20 = (bf16[32,2048]{1,0:T(8,128)(2,1)S(1)}, bf16[32,2048]{1,0:T(8,128)(2,1)S(1)}, u32[]{:S(2)}, u32[]{:S(2)}) collective-permute-start(bf16[32,2048]{1,0:T(8,128)(2,1)S(1)} %get-tuple-element.50), channel_id=1, source_target_pairs={{0,8},{4,12},{8,0},{12,4},{16,24},{20,28},{24,16},{28,20},{1,9},{5... | collective-permute-start | bytes 393224 | tf_op jit(solution)/shard_map/ppermute | solution.py:18
  63.9 8.2 %collective-permute-start.22 = (bf16[32,2048]{1,0:T(8,128)(2,1)S(1)}, bf16[32,2048]{1,0:T(8,128)(2,1)S(1)}, u32[]{:S(2)}, u32[]{:S(2)}) collective-permute-start(bf16[32,2048]{1,0:T(8,128)(2,1)S(1)} %get-tuple-element.51), channel_id=1, source_target_pairs={{0,24},{4,28},{8,16},{12,20},{16,8},{20,12},{24,0},{28,4},{1,25},{... | collective-permute-start | bytes 393224 | tf_op jit(solution)/shard_map/ppermute | solution.py:18
  65.6 7.8 %collective-permute-start.21 = (bf16[32,2048]{1,0:T(8,128)(2,1)S(1)}, bf16[32,2048]{1,0:T(8,128)(2,1)S(1)}, u32[]{:S(2)}, u32[]{:S(2)}) collective-permute-start(bf16[32,2048]{1,0:T(8,128)(2,1)S(1)} %get-tuple-element.52), channel_id=1, source_target_pairs={{0,16},{4,20},{8,24},{12,28},{16,0},{20,4},{24,8},{28,12},{1,17},{... | collective-permute-start | bytes 393224 | tf_op jit(solution)/shard_map/ppermute | solution.py:18

commit v10 on v8

--- a/solution.py
+++ b/solution.py
@@ -18,14 +18,44 @@
     return lax.ppermute(value, axis, [(i, i ^ offset) for i in range(size)])
 
 
-def mask_kernel(where, mask_ref, green_ref, tiles, token, sems, *, block):
+def at_end(where, size):
+    return (where[1] == 0) | (where[1] == size - 1)
+
+
+def window_sums(terms, ends):
+    size = len(terms)
+    if size == 4:
+        came = lax.ppermute(terms[2], "col", [(0, 1), (3, 2), (2, 0), (1, 3)]).astype(F32)
+        near = exchange(terms[1], "col", 1).astype(F32)
+        onward = terms[3] + jnp.where(ends > 0, 0.0, came)
+        far = exchange(onward.astype(BF16), "col", 3).astype(F32)
+        return terms[0] + near + far + jnp.where(ends > 0, came, 0.0)
+    total = terms[0]
+    for offset in range(1, size):
+        total = total + exchange(terms[offset].astype(BF16), "col", offset).astype(F32)
+    return total
+
+
+def window_spread(lowered, ends, size):
+    if size == 4:
+        far = exchange(lowered, "col", 3)
+        near = exchange(lowered, "col", 1)
+        onward = jnp.where(ends > 0, lowered, far)
+        return [lowered, near, lax.ppermute(onward, "col", [(0, 2), (3, 1), (1, 0), (2, 3)]), far]
+    return [lowered] + [exchange(lowered, "col", offset) for offset in range(1, size)]
+
+
+def mask_kernel(where, mask_hbm, green_ref, tiles, token, mask_ref, mask_sem, sems, *, block):
     rows, cols = tiles.shape
     token[...] = jnp.zeros(token.shape, token.dtype)
+    levels = pltpu.make_async_copy(mask_hbm, mask_ref, mask_sem)
+    levels.start()
     copies = []
     for step in range(rows // STEP):
         at = pl.ds(step * STEP, STEP)
         copies.append(pltpu.make_async_copy(green_ref.at[at], tiles.at[at], sems.at[step]))
         copies[-1].start()
+    levels.wait()
     for step, copy in enumerate(copies):
         copy.wait()
         for i in range(step * STEP // block, (step + 1) * STEP // block):
@@ -40,19 +70,26 @@
     rows, cols = green.shape
     return pl.pallas_call(
         functools.partial(mask_kernel, block=rows // mask.shape[0]),
-        in_specs=[pl.BlockSpec(memory_space=pltpu.SMEM)] * 2 + [pl.BlockSpec(memory_space=pltpu.HBM)],
+        in_specs=[pl.BlockSpec(memory_space=pltpu.SMEM)] + [pl.BlockSpec(memory_space=pltpu.HBM)] * 2,
         out_specs=[pl.BlockSpec(memory_space=pltpu.VMEM)] * 2,
         out_shape=[pltpu.VMEM((rows, cols), BF16), jax.ShapeDtypeStruct((8, 128), F32)],
-        scratch_shapes=[pltpu.SemaphoreType.DMA((rows // STEP,))],
+        scratch_shapes=[
+            pltpu.SMEM(mask.shape, mask.dtype),
+            pltpu.SemaphoreType.DMA,
+            pltpu.SemaphoreType.DMA((rows // STEP,)),
+        ],
         compiler_params=pltpu.CompilerParams(vmem_limit_bytes=VMEM_LIMIT),
         cost_estimate=pl.CostEstimate(flops=0, bytes_accessed=2 * rows * cols, transcendentals=0),
         name="masked_tiles",
-    )(where, mask, pltpu.with_memory_space_constraint(green, pltpu.HBM))
+    )(where, *(pltpu.with_memory_space_constraint(array, pltpu.HBM) for array in (mask, green)))
 
 
 def sketch_kernel(where, tiles, token, *refs, offsets_row, offsets_col, piece):
-    blocks, outs = refs[: len(offsets_row)], refs[len(offsets_row) : -2]
+    chunks = refs[0].shape[0] // piece
+    blocks, outs = refs[: len(offsets_row)], refs[len(offsets_row) : -2 - chunks]
     probes, total = refs[-2:]
+    for ends in refs[-2 - chunks : -2]:
+        ends[...] = jnp.full(ends.shape, at_end(where, len(offsets_col)).astype(F32))
     width = blocks[0].shape[0]
     for offset, ref in zip(offsets_row, blocks):
         start = pl.multiple_of((where[0] ^ offset) * width, width)
@@ -75,7 +112,9 @@
     width = blocks[0].shape[0] * len(blocks)
     share = width // len(offsets_col) // chunks
     vmem = pl.BlockSpec(memory_space=pltpu.VMEM)
-    outs = [jax.ShapeDtypeStruct((share, rows), F32 if offset == 0 else BF16) for offset in offsets_col] * chunks
+    exact = (0, offsets_col[-1])
+    outs = [jax.ShapeDtypeStruct((share, rows), F32 if offset in exact else BF16) for offset in offsets_col] * chunks
+    outs += [jax.ShapeDtypeStruct((share, rows), F32)] * chunks
     return pl.pallas_call(
         functools.partial(
             sketch_kernel, offsets_row=offsets_row, offsets_col=offsets_col, piece=blocks[0].shape[0] // chunks
@@ -150,28 +189,24 @@
     offsets_core = list(range(0, n_row, 2))
     gather_core = [0] + offsets_core[:0:-1]
     offsets_row = gather_core + [offset ^ 1 for offset in gather_core]
-    far_first = [0] + offsets_col[:0:-1]
 
     tiles, token = masked(where, green, mask)
 
     own = probes.T
     held = [own] + [exchange(own, "row", offset) for offset in gather_core[1:]]
+    twin = exchange(own, "row", 1)
     held, token = lax.optimization_barrier((held, token))
-    blocks = held + [exchange(block, "row", 1) for block in held]
+    blocks = held + [twin] + [exchange(block, "row", 1) for block in held[1:]]
 
     parts = partial_sketch(where, tiles, blocks, token, offsets_row, offsets_col, chunks)
     totals, shares = [], []
+    parts, ends = parts[:-chunks], parts[-chunks:]
     for chunk in range(chunks):
-        terms = parts[chunk * n_col : (chunk + 1) * n_col]
-        total = terms[0]
-        for offset in offsets_col[1:]:
-            total = total + exchange(terms[offset], "col", offset).astype(F32)
-        totals.append(total)
-        lowered = total.astype(BF16)
-        shares.append([lowered] + [exchange(lowered, "col", offset) for offset in far_first[1:]])
+        totals.append(window_sums(parts[chunk * n_col : (chunk + 1) * n_col], ends[chunk]))
+        shares.append(window_spread(totals[-1].astype(BF16), ends[chunk], n_col))
 
     flat = [share for per_chunk in shares for share in per_chunk]
-    *mine, others = partial_adjoint(where, tiles, flat, far_first, offsets_core, width, chunks)
+    *mine, others = partial_adjoint(where, tiles, flat, offsets_col, offsets_core, width, chunks)
     others = exchange(others, "row", 1)
     pairs = [m + others[k * own_width : (k + 1) * own_width] for k, m in enumerate(mine)]
     adjoint = pairs[0]

time: 82.8 us -> 77.3 us (0.934)
  starting transfers between devices: 43.5 us -> 37.7 us
    ppermute x23 -> x19, starting transfers between devices: 43.5 us -> 29.4 us  [exchange(): return lax.ppermute(value, axis, [(i, i ^ offset) for i in range(size)])]
    ppermute x0 -> x4, starting transfers between devices: none -> 8.28 us  [the longest x2 4.65 us: window_spread(): lax.ppermute(onward, 'col', [(0, 2), (3, 1), (1, 0), (2, 3)])]
    ppermute x0 -> x4, waiting for transfers between devices: none -> 7.32 us  [the longest x2 4.33 us: window_spread(): lax.ppermute(onward, 'col', [(0, 2), (3, 1), (1, 0), (2, 3)])]
    ppermute x23 -> x19, waiting for transfers between devices: 25.5 us -> 18.9 us  [exchange(): return lax.ppermute(value, axis, [(i, i ^ offset) for i in range(size)])]
  transfers between devices with their start and end apart: 23 -> 23, of which waited for: 12 -> 15; matrix products, arithmetic and copies ran while one was open for 1% -> 2% of each run, Pallas kernels for 5% -> 5%
where the time goes in v10:
time: 77.3 us; the launch traced here: 77.2 us
  starting transfers between devices  37.7 us (49%)
  waiting for transfers between devices  26.3 us (34%)
  Pallas kernels  10.3 us (13%)
  other arithmetic  2.18 us (3%)
    ppermute x19, starting transfers between devices, exchange(): return lax.ppermute(value, axis, [(i, i ^ offset) for i in range(size)])  29.4 us
    ppermute x19, waiting for transfers between devices, exchange(): return lax.ppermute(value, axis, [(i, i ^ offset) for i in range(size)])  18.9 us
    ppermute x2, starting transfers between devices, window_spread(): lax.ppermute(onward, 'col', [(0, 2), (3, 1), (1, 0), (2, 3)])  4.65 us
    ppermute x2, waiting for transfers between devices, window_spread(): lax.ppermute(onward, 'col', [(0, 2), (3, 1), (1, 0), (2, 3)])  4.33 us
    pallas_call x1, Pallas kernels, masked(): pl.pallas_call(functools.partial(mask_kernel, block=rows // mask.shape[0]...  4.12 us
    ppermute x2, starting transfers between devices, window_sums(): lax.ppermute(terms[2], 'col', [(0, 1), (3, 2), (2, 0), (1, 3)]).astype(F32)  3.62 us
    pallas_call x1, Pallas kernels, partial_adjoint(): pl.pallas_call(functools.partial(adjoint_kernel, offsets_col=offsets_col,...  3.1 us
    pallas_call x1, Pallas kernels, partial_sketch(): pl.pallas_call(functools.partial(sketch_kernel, offsets_row=offsets_row,...  3.07 us
  transfers between devices with their start and end apart: 23, of which 15 were waited for; matrix products, arithmetic and copies ran while one was open for 2% of the time, Pallas kernels for 5%

profile of v10, /device:TPU:0, one launch (start us, length us, event | category | flops | bytes accessed | tf_op | source)
XLA Modules:
  0.0 77.2 jit_solution(240254218654965145)
XLA Ops:
  0.6 3.0 %collective-permute-start.2 = (bf16[32,2048]{1,0:T(8,128)(2,1)}, bf16[32,2048]{1,0:T(8,128)(2,1)S(1)}, u32[]{:S(2)}, u32[]{:S(2)}) collective-permute-start(bf16[32,2048]{1,0:T(8,128)(2,1)} %bitcast.10), channel_id=1, source_target_pairs={{0,8},{4,12},{8,0},{12,4},{16,24},{20,28},{24,16},{28,20},{1,9},{5... | collective-permute-start | bytes 393224 | tf_op jit(solution)/shard_map/ppermute | solution.py:18
  3.6 1.5 %collective-permute-start.1 = (bf16[32,2048]{1,0:T(8,128)(2,1)}, bf16[32,2048]{1,0:T(8,128)(2,1)S(1)}, u32[]{:S(2)}, u32[]{:S(2)}) collective-permute-start(bf16[32,2048]{1,0:T(8,128)(2,1)} %bitcast.11), channel_id=1, source_target_pairs={{0,16},{4,20},{8,24},{12,28},{16,0},{20,4},{24,8},{28,12},{1,17},{... | collective-permute-start | bytes 393224 | tf_op jit(solution)/shard_map/ppermute | solution.py:18
  5.3 4.1 %masked_tiles.1 = (bf16[2048,2048]{1,0:T(8,128)(2,1)S(1)}, f32[8,128]{1,0:T(8,128)S(1)}) custom-call(s32[2]{0:T(128)S(1)} %pad_add_fusion.where, s32[8,8]{1,0:T(8,128)} %mask_hbm.1, bf16[2048,2048]{1,0:T(8,128)(2,1)} %green_ref.1), custom_call_target="tpu_custom_call" | custom-call | bytes 8388608 | tf_op jit(solution)/shard_map/masked_tiles/pallas_call | solution.py:71
  9.4 2.2 %collective-permute-done.1.refs_2_ = bf16[32,2048]{1,0:T(8,128)(2,1)S(1)} collective-permute-done((bf16[32,2048]{1,0:T(8,128)(2,1)}, bf16[32,2048]{1,0:T(8,128)(2,1)S(1)}, u32[]{:S(2)}, u32[]{:S(2)}) %collective-permute-start.1) | collective-permute-done | bytes 131104 | tf_op jit(solution)/shard_map/ppermute | solution.py:18
  11.6 0.5 collective-permute-start.5
  12.2 0.8 %collective-permute-done.4.refs_5_ = bf16[32,2048]{1,0:T(8,128)(2,1)S(1)} collective-permute-done((bf16[32,2048]{1,0:T(8,128)(2,1)S(1)}, bf16[32,2048]{1,0:T(8,128)(2,1)S(1)}, u32[]{:S(2)}, u32[]{:S(2)}) %collective-permute-start.4) | collective-permute-done | bytes 131104 | tf_op jit(solution)/shard_map/ppermute | solution.py:18
  13.5 3.1 %partial_sketch.1 = (f32[32,2048]{1,0:T(8,128)S(1)}, bf16[32,2048]{1,0:T(8,128)(2,1)S(1)}, bf16[32,2048]{1,0:T(8,128)(2,1)S(1)}, f32[32,2048]{1,0:T(8,128)S(1)},...) custom-call(s32[2]{0:T(128)S(1)} %pad_add_fusion.where, ...), custom_call_target="tpu_custom_call" | custom-call | flops 2147483648 | bytes 8388608 | tf_op jit(solution)/shard_map/partial_sketch/pallas_call | solution.py:118
  16.6 1.6 %collective-permute-start.8 = (bf16[32,2048]{1,0:T(8,128)(2,1)S(1)}, bf16[32,2048]{1,0:T(8,128)(2,1)S(1)}, u32[]{:S(2)}, u32[]{:S(2)}) collective-permute-start(bf16[32,2048]{1,0:T(8,128)(2,1)S(1)} %get-tuple-element.35), channel_id=1, source_target_pairs={{0,1},{3,2},{2,0},{1,3},{4,5},{7,6},{6,4},{5,7},{8,9},{11,10},{10,... | collective-permute-start | bytes 393224 | tf_op jit(solution)/shard_map/ppermute | solution.py:28
  18.2 2.6 %collective-permute-start.7 = (bf16[32,2048]{1,0:T(8,128)(2,1)S(1)}, bf16[32,2048]{1,0:T(8,128)(2,1)S(1)}, u32[]{:S(2)}, u32[]{:S(2)}) collective-permute-start(bf16[32,2048]{1,0:T(8,128)(2,1)S(1)} %get-tuple-element.32), channel_id=1, source_target_pairs={{0,1},{1,0},{2,3},{3,2},{4,5},{5,4},{6,7},{7,6},{8,9},{9,8},{10,11... | collective-permute-start | bytes 393224 | tf_op jit(solution)/shard_map/ppermute | solution.py:18
  20.8 2.0 %collective-permute-start.11 = (bf16[32,2048]{1,0:T(8,128)(2,1)S(1)}, bf16[32,2048]{1,0:T(8,128)(2,1)S(1)}, u32[]{:S(2)}, u32[]{:S(2)}) collective-permute-start(bf16[32,2048]{1,0:T(8,128)(2,1)S(1)} %get-tuple-element.40), channel_id=1, source_target_pairs={{0,1},{3,2},{2,0},{1,3},{4,5},{7,6},{6,4},{5,7},{8,9},{11,10},{10,... | collective-permute-start | bytes 393224 | tf_op jit(solution)/shard_map/ppermute | solution.py:28
  23.3 4.4 %collective-permute-start.9 = (bf16[32,2048]{1,0:T(8,128)(2,1)S(1)}, bf16[32,2048]{1,0:T(8,128)(2,1)S(1)}, u32[]{:S(2)}, u32[]{:S(2)}) collective-permute-start(bf16[32,2048]{1,0:T(8,128)(2,1)S(1)} %get-tuple-element.50), channel_id=1, source_target_pairs={{0,3},{1,2},{2,1},{3,0},{4,7},{5,6},{6,5},{7,4},{8,11},{9,10},{10,... | collective-permute-start | bytes 393224 | tf_op jit(solution)/shard_map/ppermute | solution.py:18
  27.7 2.6 %collective-permute-done.11 = bf16[32,2048]{1,0:T(8,128)(2,1)S(1)} collective-permute-done((bf16[32,2048]{1,0:T(8,128)(2,1)S(1)}, bf16[32,2048]{1,0:T(8,128)(2,1)S(1)}, u32[]{:S(2)}, u32[]{:S(2)}) %collective-permute-start.11) | collective-permute-done | bytes 131104 | tf_op jit(solution)/shard_map/ppermute | solution.py:28
  30.4 2.7 %collective-permute-start.12 = (bf16[32,2048]{1,0:T(8,128)(2,1)S(1)}, bf16[32,2048]{1,0:T(8,128)(2,1)S(1)}, u32[]{:S(2)}, u32[]{:S(2)}) collective-permute-start(bf16[32,2048]{1,0:T(8,128)(2,1)S(1)} %get-tuple-element.52), channel_id=1, source_target_pairs={{0,3},{1,2},{2,1},{3,0},{4,7},{5,6},{6,5},{7,4},{8,11},{9,10},{10,... | collective-permute-start | bytes 393224 | tf_op jit(solution)/shard_map/ppermute | solution.py:18
  33.1 3.2 %collective-permute-done.9 = bf16[32,2048]{1,0:T(8,128)(2,1)S(1)} collective-permute-done((bf16[32,2048]{1,0:T(8,128)(2,1)S(1)}, bf16[32,2048]{1,0:T(8,128)(2,1)S(1)}, u32[]{:S(2)}, u32[]{:S(2)}) %collective-permute-start.9) | collective-permute-done | bytes 131104 | tf_op jit(solution)/shard_map/ppermute | solution.py:18
  36.4 1.3 %collective-permute-start.14 = (bf16[32,2048]{1,0:T(8,128)(2,1)S(1)}, bf16[32,2048]{1,0:T(8,128)(2,1)S(1)}, u32[]{:S(2)}, u32[]{:S(2)}) collective-permute-start(bf16[32,2048]{1,0:T(8,128)(2,1)S(1)} %get-tuple-element.48.refs_0_), channel_id=1, source_target_pairs={{0,3},{1,2},{2,1},{3,0},{4,7},{5,6},{6,5},{7,4},{8,11},{9,10},{10,... | collective-permute-start | bytes 393224 | tf_op jit(solution)/shard_map/ppermute | solution.py:18
  37.8 0.6 collective-permute-done.12
  38.5 2.0 %collective-permute-start.17 = (bf16[32,2048]{1,0:T(8,128)(2,1)S(1)}, bf16[32,2048]{1,0:T(8,128)(2,1)S(1)}, u32[]{:S(2)}, u32[]{:S(2)}) collective-permute-start(bf16[32,2048]{1,0:T(8,128)(2,1)S(1)} %get-tuple-element.46.refs_4_), channel_id=1, source_target_pairs={{0,3},{1,2},{2,1},{3,0},{4,7},{5,6},{6,5},{7,4},{8,11},{9,10},{10,... | collective-permute-start | bytes 393224 | tf_op jit(solution)/shard_map/ppermute | solution.py:18
  40.5 7.6 %collective-permute-start.13 = (bf16[32,2048]{1,0:T(8,128)(2,1)S(1)}, bf16[32,2048]{1,0:T(8,128)(2,1)S(1)}, u32[]{:S(2)}, u32[]{:S(2)}) collective-permute-start(bf16[32,2048]{1,0:T(8,128)(2,1)S(1)} %get-tuple-element.48.refs_0_), channel_id=1, source_target_pairs={{0,1},{1,0},{2,3},{3,2},{4,5},{5,4},{6,7},{7,6},{8,9},{9,8},{10,11... | collective-permute-start | bytes 393224 | tf_op jit(solution)/shard_map/ppermute | solution.py:18
  48.2 2.9 %collective-permute-start.15 = (bf16[32,2048]{1,0:T(8,128)(2,1)S(1)}, bf16[32,2048]{1,0:T(8,128)(2,1)S(1)}, u32[]{:S(2)}, u32[]{:S(2)}) collective-permute-start(bf16[32,2048]{1,0:T(8,128)(2,1)S(1)} %select_n.25), channel_id=1, source_target_pairs={{0,2},{3,1},{1,0},{2,3},{4,6},{7,5},{5,4},{6,7},{8,10},{11,9},{9,8... | collective-permute-start | bytes 393224 | tf_op jit(solution)/shard_map/ppermute | solution.py:44
  51.2 1.7 %collective-permute-start.18 = (bf16[32,2048]{1,0:T(8,128)(2,1)S(1)}, bf16[32,2048]{1,0:T(8,128)(2,1)S(1)}, u32[]{:S(2)}, u32[]{:S(2)}) collective-permute-start(bf16[32,2048]{1,0:T(8,128)(2,1)S(1)} %select_n.26), channel_id=1, source_target_pairs={{0,2},{3,1},{1,0},{2,3},{4,6},{7,5},{5,4},{6,7},{8,10},{11,9},{9,8... | collective-permute-start | bytes 393224 | tf_op jit(solution)/shard_map/ppermute | solution.py:44
  52.9 2.4 %collective-permute-done.16.refs_5_ = bf16[32,2048]{1,0:T(8,128)(2,1)S(1)} collective-permute-done((bf16[32,2048]{1,0:T(8,128)(2,1)S(1)}, bf16[32,2048]{1,0:T(8,128)(2,1)S(1)}, u32[]{:S(2)}, u32[]{:S(2)}) %collective-permute-start.16) | collective-permute-done | bytes 131104 | tf_op jit(solution)/shard_map/ppermute | solution.py:18
  55.3 2.8 %collective-permute-done.15.refs_2_ = bf16[32,2048]{1,0:T(8,128)(2,1)S(1)} collective-permute-done((bf16[32,2048]{1,0:T(8,128)(2,1)S(1)}, bf16[32,2048]{1,0:T(8,128)(2,1)S(1)}, u32[]{:S(2)}, u32[]{:S(2)}) %collective-permute-start.15) | collective-permute-done | bytes 131104 | tf_op jit(solution)/shard_map/ppermute | solution.py:44
  58.1 1.5 %collective-permute-done.18.refs_6_ = bf16[32,2048]{1,0:T(8,128)(2,1)S(1)} collective-permute-done((bf16[32,2048]{1,0:T(8,128)(2,1)S(1)}, bf16[32,2048]{1,0:T(8,128)(2,1)S(1)}, u32[]{:S(2)}, u32[]{:S(2)}) %collective-permute-start.18) | collective-permute-done | bytes 131104 | tf_op jit(solution)/shard_map/ppermute | solution.py:44
  59.6 3.1 %partial_adjoint.1 = (f32[32,2048]{1,0:T(8,128)S(1)}, f32[32,2048]{1,0:T(8,128)S(1)}, f32[32,2048]{1,0:T(8,128)S(1)}, f32[32,2048]{1,0:T(8,128)S(1)}, f32[128,2048]{1,0:T(8,128)S(1)}) custom-call(s32[2]{0:T(128)S(1)} %pad_add_fusion.where, bf16[2048,2048]{1,0:T(8,128)(2,1)S(1)} %get-tuple-element.24.tiles, bf16[32,2048]{1,0:T(8,128)(2,1)S(1)} %get-tuple-element.48.refs_0_, ...), custom_call_target="tpu_custom_call" | custom-call | flops 2147483648 | bytes 8388608 | tf_op jit(solution)/shard_map/partial_adjoint/pallas_call | solution.py:162
  62.8 2.6 %collective-permute-done.19 = f32[128,2048]{1,0:T(8,128)S(1)} collective-permute-done((f32[128,2048]{1,0:T(8,128)S(1)}, f32[128,2048]{1,0:T(8,128)S(1)}, u32[]{:S(2)}, u32[]{:S(2)}) %collective-permute-start.19) | collective-permute-done | bytes 1048608 | tf_op jit(solution)/shard_map/ppermute | solution.py:18
  65.6 1.3 %collective-permute-start.20 = (bf16[32,2048]{1,0:T(8,128)(2,1)S(1)}, bf16[32,2048]{1,0:T(8,128)(2,1)S(1)}, u32[]{:S(2)}, u32[]{:S(2)}) collective-permute-start(bf16[32,2048]{1,0:T(8,128)(2,1)S(1)} %get-tuple-element.54), channel_id=1, source_target_pairs={{0,8},{4,12},{8,0},{12,4},{16,24},{20,28},{24,16},{28,20},{1,9},{5... | collective-permute-start | bytes 393224 | tf_op jit(solution)/shard_map/ppermute | solution.py:18
  66.9 1.8 %collective-permute-start.22 = (bf16[32,2048]{1,0:T(8,128)(2,1)S(1)}, bf16[32,2048]{1,0:T(8,128)(2,1)S(1)}, u32[]{:S(2)}, u32[]{:S(2)}) collective-permute-start(bf16[32,2048]{1,0:T(8,128)(2,1)S(1)} %get-tuple-element.55), channel_id=1, source_target_pairs={{0,24},{4,28},{8,16},{12,20},{16,8},{20,12},{24,0},{28,4},{1,25},{... | collective-permute-start | bytes 393224 | tf_op jit(solution)/shard_map/ppermute | solution.py:18
  69.1 0.8 %pad_maximum_fusion = f32[2,32,2048]{2,1,0:T(8,128)} fusion(f32[2,16,2048]{2,1,0:T(8,128)S(1)} %bitcast.16, f32[2,16,2048]{2,1,0:T(8,128)S(1)} %bitcast.15), kind=kLoop, calls=%fused_computation | loop fusion | flops 131072 | bytes 1048576 | tf_op jit(solution)/shard_map/concatenate | solution.py:178
  70.0 2.0 %collective-permute-done.20 = bf16[32,2048]{1,0:T(8,128)(2,1)S(1)} collective-permute-done((bf16[32,2048]{1,0:T(8,128)(2,1)S(1)}, bf16[32,2048]{1,0:T(8,128)(2,1)S(1)}, u32[]{:S(2)}, u32[]{:S(2)}) %collective-permute-start.20) | collective-permute-done | bytes 131104 | tf_op jit(solution)/shard_map/ppermute | solution.py:18
  72.0 3.1 %collective-permute-done.22 = bf16[32,2048]{1,0:T(8,128)(2,1)S(1)} collective-permute-done((bf16[32,2048]{1,0:T(8,128)(2,1)S(1)}, bf16[32,2048]{1,0:T(8,128)(2,1)S(1)}, u32[]{:S(2)}, u32[]{:S(2)}) %collective-permute-start.22) | collective-permute-done | bytes 131104 | tf_op jit(solution)/shard_map/ppermute | solution.py:18
  75.1 1.4 %collective-permute-done.21 = bf16[32,2048]{1,0:T(8,128)(2,1)S(1)} collective-permute-done((bf16[32,2048]{1,0:T(8,128)(2,1)S(1)}, bf16[32,2048]{1,0:T(8,128)(2,1)S(1)}, u32[]{:S(2)}, u32[]{:S(2)}) %collective-permute-start.21) | collective-permute-done | bytes 131104 | tf_op jit(solution)/shard_map/ppermute | solution.py:18
  76.4 0.8 fusion.12
  (29 shorter events, 2.2 us)
Async XLA Ops:
  0.6 12.9 %copy-start = (bf16[2048,32]{0,1:T(8,128)(2,1)S(1)}, bf16[2048,32]{0,1:T(8,128)(2,1)}, u32[]{:S(2)}) copy-start(bf16[2048,32]{0,1:T(8,128)(2,1)} %param.5) | copy-start | bytes 393220
  0.6 8.8 %collective-permute-start.2 = (bf16[32,2048]{1,0:T(8,128)(2,1)}, bf16[32,2048]{1,0:T(8,128)(2,1)S(1)}, u32[]{:S(2)}, u32[]{:S(2)}) collective-permute-start(bf16[32,2048]{1,0:T(8,128)(2,1)} %bitcast.10), channel_id=1, source_target_pairs={{0,8},{4,12},{8,0},{12,4},{16,24},{20,28},{24,16},{28,20},{1,9},{5... | collective-permute-start | bytes 393224 | tf_op jit(solution)/shard_map/ppermute | solution.py:18
  3.6 8.0 %collective-permute-start.1 = (bf16[32,2048]{1,0:T(8,128)(2,1)}, bf16[32,2048]{1,0:T(8,128)(2,1)S(1)}, u32[]{:S(2)}, u32[]{:S(2)}) collective-permute-start(bf16[32,2048]{1,0:T(8,128)(2,1)} %bitcast.11), channel_id=1, source_target_pairs={{0,16},{4,20},{8,24},{12,28},{16,0},{20,4},{24,8},{28,12},{1,17},{... | collective-permute-start | bytes 393224 | tf_op jit(solution)/shard_map/ppermute | solution.py:18
  5.2 6.5 %collective-permute-start = (bf16[32,2048]{1,0:T(8,128)(2,1)}, bf16[32,2048]{1,0:T(8,128)(2,1)S(1)}, u32[]{:S(2)}, u32[]{:S(2)}) collective-permute-start(bf16[32,2048]{1,0:T(8,128)(2,1)} %bitcast.12), channel_id=1, source_target_pairs={{0,24},{4,28},{8,16},{12,20},{16,8},{20,12},{24,0},{28,4},{1,25},{... | collective-permute-start | bytes 393224 | tf_op jit(solution)/shard_map/ppermute | solution.py:18
  5.2 7.0 %collective-permute-start.3 = (bf16[32,2048]{1,0:T(8,128)(2,1)}, bf16[32,2048]{1,0:T(8,128)(2,1)S(1)}, u32[]{:S(2)}, u32[]{:S(2)}) collective-permute-start(bf16[32,2048]{1,0:T(8,128)(2,1)} %bitcast.13), channel_id=1, source_target_pairs={{0,4},{4,0},{8,12},{12,8},{16,20},{20,16},{24,28},{28,24},{1,5},{5... | collective-permute-start | bytes 393224 | tf_op jit(solution)/shard_map/ppermute | solution.py:18
  11.6 1.3 %collective-permute-start.4 = (bf16[32,2048]{1,0:T(8,128)(2,1)S(1)}, bf16[32,2048]{1,0:T(8,128)(2,1)S(1)}, u32[]{:S(2)}, u32[]{:S(2)}) collective-permute-start(bf16[32,2048]{1,0:T(8,128)(2,1)S(1)} %collective-permute-done.refs_1_), channel_id=1, source_target_pairs={{0,4},{4,0},{8,12},{12,8},{16,20},{20,16},{24,28},{28,24},{1,5},{5... | collective-permute-start | bytes 393224 | tf_op jit(solution)/shard_map/ppermute | solution.py:18
  11.6 1.5 %collective-permute-start.5 = (bf16[32,2048]{1,0:T(8,128)(2,1)S(1)}, bf16[32,2048]{1,0:T(8,128)(2,1)S(1)}, u32[]{:S(2)}, u32[]{:S(2)}) collective-permute-start(bf16[32,2048]{1,0:T(8,128)(2,1)S(1)} %collective-permute-done.1.refs_2_), channel_id=1, source_target_pairs={{0,4},{4,0},{8,12},{12,8},{16,20},{20,16},{24,28},{28,24},{1,5},{5... | collective-permute-start | bytes 393224 | tf_op jit(solution)/shard_map/ppermute | solution.py:18
  12.1 1.3 %collective-permute-start.6 = (bf16[32,2048]{1,0:T(8,128)(2,1)S(1)}, bf16[32,2048]{1,0:T(8,128)(2,1)S(1)}, u32[]{:S(2)}, u32[]{:S(2)}) collective-permute-start(bf16[32,2048]{1,0:T(8,128)(2,1)S(1)} %collective-permute-done.2.refs_3_), channel_id=1, source_target_pairs={{0,4},{4,0},{8,12},{12,8},{16,20},{20,16},{24,28},{28,24},{1,5},{5... | collective-permute-start | bytes 393224 | tf_op jit(solution)/shard_map/ppermute | solution.py:18
  16.6 6.6 %collective-permute-start.8 = (bf16[32,2048]{1,0:T(8,128)(2,1)S(1)}, bf16[32,2048]{1,0:T(8,128)(2,1)S(1)}, u32[]{:S(2)}, u32[]{:S(2)}) collective-permute-start(bf16[32,2048]{1,0:T(8,128)(2,1)S(1)} %get-tuple-element.35), channel_id=1, source_target_pairs={{0,1},{3,2},{2,0},{1,3},{4,5},{7,6},{6,4},{5,7},{8,9},{11,10},{10,... | collective-permute-start | bytes 393224 | tf_op jit(solution)/shard_map/ppermute | solution.py:28
  18.2 14.9 %collective-permute-start.7 = (bf16[32,2048]{1,0:T(8,128)(2,1)S(1)}, bf16[32,2048]{1,0:T(8,128)(2,1)S(1)}, u32[]{:S(2)}, u32[]{:S(2)}) collective-permute-start(bf16[32,2048]{1,0:T(8,128)(2,1)S(1)} %get-tuple-element.32), channel_id=1, source_target_pairs={{0,1},{1,0},{2,3},{3,2},{4,5},{5,4},{6,7},{7,6},{8,9},{9,8},{10,11... | collective-permute-start | bytes 393224 | tf_op jit(solution)/shard_map/ppermute | solution.py:18
  20.8 17.0 %collective-permute-start.10 = (bf16[32,2048]{1,0:T(8,128)(2,1)S(1)}, bf16[32,2048]{1,0:T(8,128)(2,1)S(1)}, u32[]{:S(2)}, u32[]{:S(2)}) collective-permute-start(bf16[32,2048]{1,0:T(8,128)(2,1)S(1)} %get-tuple-element.37), channel_id=1, source_target_pairs={{0,1},{1,0},{2,3},{3,2},{4,5},{5,4},{6,7},{7,6},{8,9},{9,8},{10,11... | collective-permute-start | bytes 393224 | tf_op jit(solution)/shard_map/ppermute | solution.py:18
  20.8 9.5 %collective-permute-start.11 = (bf16[32,2048]{1,0:T(8,128)(2,1)S(1)}, bf16[32,2048]{1,0:T(8,128)(2,1)S(1)}, u32[]{:S(2)}, u32[]{:S(2)}) collective-permute-start(bf16[32,2048]{1,0:T(8,128)(2,1)S(1)} %get-tuple-element.40), channel_id=1, source_target_pairs={{0,1},{3,2},{2,0},{1,3},{4,5},{7,6},{6,4},{5,7},{8,9},{11,10},{10,... | collective-permute-start | bytes 393224 | tf_op jit(solution)/shard_map/ppermute | solution.py:28
  23.3 13.0 %collective-permute-start.9 = (bf16[32,2048]{1,0:T(8,128)(2,1)S(1)}, bf16[32,2048]{1,0:T(8,128)(2,1)S(1)}, u32[]{:S(2)}, u32[]{:S(2)}) collective-permute-start(bf16[32,2048]{1,0:T(8,128)(2,1)S(1)} %get-tuple-element.50), channel_id=1, source_target_pairs={{0,3},{1,2},{2,1},{3,0},{4,7},{5,6},{6,5},{7,4},{8,11},{9,10},{10,... | collective-permute-start | bytes 393224 | tf_op jit(solution)/shard_map/ppermute | solution.py:18
  30.4 8.0 %collective-permute-start.12 = (bf16[32,2048]{1,0:T(8,128)(2,1)S(1)}, bf16[32,2048]{1,0:T(8,128)(2,1)S(1)}, u32[]{:S(2)}, u32[]{:S(2)}) collective-permute-start(bf16[32,2048]{1,0:T(8,128)(2,1)S(1)} %get-tuple-element.52), channel_id=1, source_target_pairs={{0,3},{1,2},{2,1},{3,0},{4,7},{5,6},{6,5},{7,4},{8,11},{9,10},{10,... | collective-permute-start | bytes 393224 | tf_op jit(solution)/shard_map/ppermute | solution.py:18
  36.4 11.7 %collective-permute-start.14 = (bf16[32,2048]{1,0:T(8,128)(2,1)S(1)}, bf16[32,2048]{1,0:T(8,128)(2,1)S(1)}, u32[]{:S(2)}, u32[]{:S(2)}) collective-permute-start(bf16[32,2048]{1,0:T(8,128)(2,1)S(1)} %get-tuple-element.48.refs_0_), channel_id=1, source_target_pairs={{0,3},{1,2},{2,1},{3,0},{4,7},{5,6},{6,5},{7,4},{8,11},{9,10},{10,... | collective-permute-start | bytes 393224 | tf_op jit(solution)/shard_map/ppermute | solution.py:18
  38.5 12.6 %collective-permute-start.17 = (bf16[32,2048]{1,0:T(8,128)(2,1)S(1)}, bf16[32,2048]{1,0:T(8,128)(2,1)S(1)}, u32[]{:S(2)}, u32[]{:S(2)}) collective-permute-start(bf16[32,2048]{1,0:T(8,128)(2,1)S(1)} %get-tuple-element.46.refs_4_), channel_id=1, source_target_pairs={{0,3},{1,2},{2,1},{3,0},{4,7},{5,6},{6,5},{7,4},{8,11},{9,10},{10,... | collective-permute-start | bytes 393224 | tf_op jit(solution)/shard_map/ppermute | solution.py:18
  40.5 12.5 %collective-permute-start.13 = (bf16[32,2048]{1,0:T(8,128)(2,1)S(1)}, bf16[32,2048]{1,0:T(8,128)(2,1)S(1)}, u32[]{:S(2)}, u32[]{:S(2)}) collective-permute-start(bf16[32,2048]{1,0:T(8,128)(2,1)S(1)} %get-tuple-element.48.refs_0_), channel_id=1, source_target_pairs={{0,1},{1,0},{2,3},{3,2},{4,5},{5,4},{6,7},{7,6},{8,9},{9,8},{10,11... | collective-permute-start | bytes 393224 | tf_op jit(solution)/shard_map/ppermute | solution.py:18
  48.1 7.2 %collective-permute-start.16 = (bf16[32,2048]{1,0:T(8,128)(2,1)S(1)}, bf16[32,2048]{1,0:T(8,128)(2,1)S(1)}, u32[]{:S(2)}, u32[]{:S(2)}) collective-permute-start(bf16[32,2048]{1,0:T(8,128)(2,1)S(1)} %get-tuple-element.46.refs_4_), channel_id=1, source_target_pairs={{0,1},{1,0},{2,3},{3,2},{4,5},{5,4},{6,7},{7,6},{8,9},{9,8},{10,11... | collective-permute-start | bytes 393224 | tf_op jit(solution)/shard_map/ppermute | solution.py:18
  48.2 9.9 %collective-permute-start.15 = (bf16[32,2048]{1,0:T(8,128)(2,1)S(1)}, bf16[32,2048]{1,0:T(8,128)(2,1)S(1)}, u32[]{:S(2)}, u32[]{:S(2)}) collective-permute-start(bf16[32,2048]{1,0:T(8,128)(2,1)S(1)} %select_n.25), channel_id=1, source_target_pairs={{0,2},{3,1},{1,0},{2,3},{4,6},{7,5},{5,4},{6,7},{8,10},{11,9},{9,8... | collective-permute-start | bytes 393224 | tf_op jit(solution)/shard_map/ppermute | solution.py:44
  51.2 8.5 %collective-permute-start.18 = (bf16[32,2048]{1,0:T(8,128)(2,1)S(1)}, bf16[32,2048]{1,0:T(8,128)(2,1)S(1)}, u32[]{:S(2)}, u32[]{:S(2)}) collective-permute-start(bf16[32,2048]{1,0:T(8,128)(2,1)S(1)} %select_n.26), channel_id=1, source_target_pairs={{0,2},{3,1},{1,0},{2,3},{4,6},{7,5},{5,4},{6,7},{8,10},{11,9},{9,8... | collective-permute-start | bytes 393224 | tf_op jit(solution)/shard_map/ppermute | solution.py:44
  62.8 2.7 %collective-permute-start.19 = (f32[128,2048]{1,0:T(8,128)S(1)}, f32[128,2048]{1,0:T(8,128)S(1)}, u32[]{:S(2)}, u32[]{:S(2)}) collective-permute-start(f32[128,2048]{1,0:T(8,128)S(1)} %get-tuple-element.42), channel_id=1, source_target_pairs={{0,4},{4,0},{8,12},{12,8},{16,20},{20,16},{24,28},{28,24},{1,5},{5... | collective-permute-start | bytes 3145736 | tf_op jit(solution)/shard_map/ppermute | solution.py:18
  65.6 6.4 %collective-permute-start.20 = (bf16[32,2048]{1,0:T(8,128)(2,1)S(1)}, bf16[32,2048]{1,0:T(8,128)(2,1)S(1)}, u32[]{:S(2)}, u32[]{:S(2)}) collective-permute-start(bf16[32,2048]{1,0:T(8,128)(2,1)S(1)} %get-tuple-element.54), channel_id=1, source_target_pairs={{0,8},{4,12},{8,0},{12,4},{16,24},{20,28},{24,16},{28,20},{1,9},{5... | collective-permute-start | bytes 393224 | tf_op jit(solution)/shard_map/ppermute | solution.py:18
  66.9 8.2 %collective-permute-start.22 = (bf16[32,2048]{1,0:T(8,128)(2,1)S(1)}, bf16[32,2048]{1,0:T(8,128)(2,1)S(1)}, u32[]{:S(2)}, u32[]{:S(2)}) collective-permute-start(bf16[32,2048]{1,0:T(8,128)(2,1)S(1)} %get-tuple-element.55), channel_id=1, source_target_pairs={{0,24},{4,28},{8,16},{12,20},{16,8},{20,12},{24,0},{28,4},{1,25},{... | collective-permute-start | bytes 393224 | tf_op jit(solution)/shard_map/ppermute | solution.py:18
  68.6 7.8 %collective-permute-start.21 = (bf16[32,2048]{1,0:T(8,128)(2,1)S(1)}, bf16[32,2048]{1,0:T(8,128)(2,1)S(1)}, u32[]{:S(2)}, u32[]{:S(2)}) collective-permute-start(bf16[32,2048]{1,0:T(8,128)(2,1)S(1)} %get-tuple-element.56), channel_id=1, source_target_pairs={{0,16},{4,20},{8,24},{12,28},{16,0},{20,4},{24,8},{28,12},{1,17},{... | collective-permute-start | bytes 393224 | tf_op jit(solution)/shard_map/ppermute | solution.py:18

commit v11 on v10

--- a/solution.py
+++ b/solution.py
@@ -22,13 +22,19 @@
     return (where[1] == 0) | (where[1] == size - 1)
 
 
+def after(value, earlier):
+    return lax.optimization_barrier((value, earlier))[0]
+
+
 def window_sums(terms, ends):
     size = len(terms)
     if size == 4:
-        came = lax.ppermute(terms[2], "col", [(0, 1), (3, 2), (2, 0), (1, 3)]).astype(F32)
-        near = exchange(terms[1], "col", 1).astype(F32)
+        came = lax.ppermute(terms[2], "col", [(0, 1), (3, 2), (2, 0), (1, 3)])
+        came = came.astype(F32)
         onward = terms[3] + jnp.where(ends > 0, 0.0, came)
-        far = exchange(onward.astype(BF16), "col", 3).astype(F32)
+        onward = onward.astype(BF16)
+        far = exchange(onward, "col", 3).astype(F32)
+        near = exchange(after(terms[1], onward), "col", 1).astype(F32)
         return terms[0] + near + far + jnp.where(ends > 0, came, 0.0)
     total = terms[0]
     for offset in range(1, size):
@@ -210,8 +216,8 @@
     others = exchange(others, "row", 1)
     pairs = [m + others[k * own_width : (k + 1) * own_width] for k, m in enumerate(mine)]
     adjoint = pairs[0]
-    for offset, pair in zip(offsets_core[1:], pairs[1:]):
-        adjoint = adjoint + exchange(pair.astype(BF16), "row", offset).astype(F32)
+    for offset in offsets_core[1:2] + offsets_core[:1:-1]:
+        adjoint = adjoint + exchange(pairs[offset // 2].astype(BF16), "row", offset).astype(F32)
     return join(totals, piece).T, adjoint.T
 
 

time: 77.3 us -> 72.4 us (0.937)
  starting transfers between devices: 37.7 us -> 33.1 us
    ppermute x19, starting transfers between devices: 29.4 us -> 21.1 us  [exchange(): return lax.ppermute(value, axis, [(i, i ^ offset) for i in range(size)])]
    ppermute x2, starting transfers between devices: 4.65 us -> 7.73 us  [window_spread(): lax.ppermute(onward, 'col', [(0, 2), (3, 1), (1, 0), (2, 3)])]
    ppermute x2, waiting for transfers between devices: 4.33 us -> 3.52 us  [window_spread(): lax.ppermute(onward, 'col', [(0, 2), (3, 1), (1, 0), (2, 3)])]
  transfers between devices with their start and end apart: 23 -> 23, of which waited for: 15 -> 15; matrix products, arithmetic and copies ran while one was open for 2% -> 2% of each run, Pallas kernels for 5% -> 6%
where the time goes in v11:
time: 72.4 us; the launch traced here: 72.3 us
  starting transfers between devices  33.1 us (46%)
  waiting for transfers between devices  25.9 us (36%)
  Pallas kernels  10.4 us (14%)
  other arithmetic  2.18 us (3%)
  between operations  0.73 us (1%)
    ppermute x19, starting transfers between devices, exchange(): return lax.ppermute(value, axis, [(i, i ^ offset) for i in range(size)])  21.1 us
    ppermute x19, waiting for transfers between devices, exchange(): return lax.ppermute(value, axis, [(i, i ^ offset) for i in range(size)])  19.3 us
    ppermute x2, starting transfers between devices, window_spread(): lax.ppermute(onward, 'col', [(0, 2), (3, 1), (1, 0), (2, 3)])  7.73 us
    ppermute x2, starting transfers between devices, window_sums(): came = lax.ppermute(terms[2], 'col', [(0, 1), (3, 2), (2, 0), (1, 3)])  4.23 us
    pallas_call x1, Pallas kernels, masked(): pl.pallas_call(functools.partial(mask_kernel, block=rows // mask.shape[0]...  4.19 us
    ppermute x2, waiting for transfers between devices, window_spread(): lax.ppermute(onward, 'col', [(0, 2), (3, 1), (1, 0), (2, 3)])  3.52 us
    pallas_call x1, Pallas kernels, partial_adjoint(): pl.pallas_call(functools.partial(adjoint_kernel, offsets_col=offsets_col,...  3.1 us
    pallas_call x1, Pallas kernels, partial_sketch(): pl.pallas_call(functools.partial(sketch_kernel, offsets_row=offsets_row,...  3.07 us
  transfers between devices with their start and end apart: 23, of which 15 were waited for; matrix products, arithmetic and copies ran while one was open for 2% of the time, Pallas kernels for 6%

profile of v11, /device:TPU:0, one launch (start us, length us, event | category | flops | bytes accessed | tf_op | source)
XLA Modules:
  0.0 72.3 jit_solution(2496881951306776797)
XLA Ops:
  0.6 3.0 %collective-permute-start.2 = (bf16[32,2048]{1,0:T(8,128)(2,1)}, bf16[32,2048]{1,0:T(8,128)(2,1)S(1)}, u32[]{:S(2)}, u32[]{:S(2)}) collective-permute-start(bf16[32,2048]{1,0:T(8,128)(2,1)} %bitcast.10), channel_id=1, source_target_pairs={{0,8},{4,12},{8,0},{12,4},{16,24},{20,28},{24,16},{28,20},{1,9},{5... | collective-permute-start | bytes 393224 | tf_op jit(solution)/shard_map/ppermute | solution.py:18
  3.6 1.5 %collective-permute-start.1 = (bf16[32,2048]{1,0:T(8,128)(2,1)}, bf16[32,2048]{1,0:T(8,128)(2,1)S(1)}, u32[]{:S(2)}, u32[]{:S(2)}) collective-permute-start(bf16[32,2048]{1,0:T(8,128)(2,1)} %bitcast.11), channel_id=1, source_target_pairs={{0,16},{4,20},{8,24},{12,28},{16,0},{20,4},{24,8},{28,12},{1,17},{... | collective-permute-start | bytes 393224 | tf_op jit(solution)/shard_map/ppermute | solution.py:18
  5.3 4.2 %masked_tiles.1 = (bf16[2048,2048]{1,0:T(8,128)(2,1)S(1)}, f32[8,128]{1,0:T(8,128)S(1)}) custom-call(s32[2]{0:T(128)S(1)} %pad_add_fusion.where, s32[8,8]{1,0:T(8,128)} %mask_hbm.1, bf16[2048,2048]{1,0:T(8,128)(2,1)} %green_ref.1), custom_call_target="tpu_custom_call" | custom-call | bytes 8388608 | tf_op jit(solution)/shard_map/masked_tiles/pallas_call | solution.py:77
  9.5 2.2 %collective-permute-done.1.refs_2_ = bf16[32,2048]{1,0:T(8,128)(2,1)S(1)} collective-permute-done((bf16[32,2048]{1,0:T(8,128)(2,1)}, bf16[32,2048]{1,0:T(8,128)(2,1)S(1)}, u32[]{:S(2)}, u32[]{:S(2)}) %collective-permute-start.1) | collective-permute-done | bytes 131104 | tf_op jit(solution)/shard_map/ppermute | solution.py:18
  11.6 0.5 collective-permute-start.5
  12.2 0.8 %collective-permute-done.4.refs_5_ = bf16[32,2048]{1,0:T(8,128)(2,1)S(1)} collective-permute-done((bf16[32,2048]{1,0:T(8,128)(2,1)S(1)}, bf16[32,2048]{1,0:T(8,128)(2,1)S(1)}, u32[]{:S(2)}, u32[]{:S(2)}) %collective-permute-start.4) | collective-permute-done | bytes 131104 | tf_op jit(solution)/shard_map/ppermute | solution.py:18
  13.5 3.1 %partial_sketch.1 = (f32[32,2048]{1,0:T(8,128)S(1)}, bf16[32,2048]{1,0:T(8,128)(2,1)S(1)}, bf16[32,2048]{1,0:T(8,128)(2,1)S(1)}, f32[32,2048]{1,0:T(8,128)S(1)},...) custom-call(s32[2]{0:T(128)S(1)} %pad_add_fusion.where, ...), custom_call_target="tpu_custom_call" | custom-call | flops 2147483648 | bytes 8388608 | tf_op jit(solution)/shard_map/partial_sketch/pallas_call | solution.py:124
  16.6 1.6 %collective-permute-start.7 = (bf16[32,2048]{1,0:T(8,128)(2,1)S(1)}, bf16[32,2048]{1,0:T(8,128)(2,1)S(1)}, u32[]{:S(2)}, u32[]{:S(2)}) collective-permute-start(bf16[32,2048]{1,0:T(8,128)(2,1)S(1)} %get-tuple-element.37), channel_id=1, source_target_pairs={{0,1},{3,2},{2,0},{1,3},{4,5},{7,6},{6,4},{5,7},{8,9},{11,10},{10,... | collective-permute-start | bytes 393224 | tf_op jit(solution)/shard_map/ppermute | solution.py:32
  18.2 2.6 %collective-permute-start.10 = (bf16[32,2048]{1,0:T(8,128)(2,1)S(1)}, bf16[32,2048]{1,0:T(8,128)(2,1)S(1)}, u32[]{:S(2)}, u32[]{:S(2)}) collective-permute-start(bf16[32,2048]{1,0:T(8,128)(2,1)S(1)} %get-tuple-element.43), channel_id=1, source_target_pairs={{0,1},{3,2},{2,0},{1,3},{4,5},{7,6},{6,4},{5,7},{8,9},{11,10},{10,... | collective-permute-start | bytes 393224 | tf_op jit(solution)/shard_map/ppermute | solution.py:32
  20.8 3.1 %collective-permute-done.7 = bf16[32,2048]{1,0:T(8,128)(2,1)S(1)} collective-permute-done((bf16[32,2048]{1,0:T(8,128)(2,1)S(1)}, bf16[32,2048]{1,0:T(8,128)(2,1)S(1)}, u32[]{:S(2)}, u32[]{:S(2)}) %collective-permute-start.7) | collective-permute-done | bytes 131104 | tf_op jit(solution)/shard_map/ppermute | solution.py:32
  23.9 3.7 %collective-permute-start.9 = (bf16[32,2048]{1,0:T(8,128)(2,1)S(1)}, bf16[32,2048]{1,0:T(8,128)(2,1)S(1)}, u32[]{:S(2)}, u32[]{:S(2)}) collective-permute-start(bf16[32,2048]{1,0:T(8,128)(2,1)S(1)} %get-tuple-element.54), channel_id=1, source_target_pairs={{0,3},{1,2},{2,1},{3,0},{4,7},{5,6},{6,5},{7,4},{8,11},{9,10},{10,... | collective-permute-start | bytes 393224 | tf_op jit(solution)/shard_map/ppermute | solution.py:18
  27.7 2.7 %collective-permute-start.12 = (bf16[32,2048]{1,0:T(8,128)(2,1)S(1)}, bf16[32,2048]{1,0:T(8,128)(2,1)S(1)}, u32[]{:S(2)}, u32[]{:S(2)}) collective-permute-start(bf16[32,2048]{1,0:T(8,128)(2,1)S(1)} %get-tuple-element.56), channel_id=1, source_target_pairs={{0,3},{1,2},{2,1},{3,0},{4,7},{5,6},{6,5},{7,4},{8,11},{9,10},{10,... | collective-permute-start | bytes 393224 | tf_op jit(solution)/shard_map/ppermute | solution.py:18
  30.4 5.8 %collective-permute-done.8 = bf16[32,2048]{1,0:T(8,128)(2,1)S(1)} collective-permute-done((bf16[32,2048]{1,0:T(8,128)(2,1)S(1)}, bf16[32,2048]{1,0:T(8,128)(2,1)S(1)}, u32[]{:S(2)}, u32[]{:S(2)}) %collective-permute-start.8) | collective-permute-done | bytes 131104 | tf_op jit(solution)/shard_map/ppermute | solution.py:18
  36.3 1.7 %collective-permute-start.14 = (bf16[32,2048]{1,0:T(8,128)(2,1)S(1)}, bf16[32,2048]{1,0:T(8,128)(2,1)S(1)}, u32[]{:S(2)}, u32[]{:S(2)}) collective-permute-start(bf16[32,2048]{1,0:T(8,128)(2,1)S(1)} %get-tuple-element.52.refs_0_), channel_id=1, source_target_pairs={{0,3},{1,2},{2,1},{3,0},{4,7},{5,6},{6,5},{7,4},{8,11},{9,10},{10,... | collective-permute-start | bytes 393224 | tf_op jit(solution)/shard_map/ppermute | solution.py:18
  38.0 1.8 %collective-permute-done.11 = bf16[32,2048]{1,0:T(8,128)(2,1)S(1)} collective-permute-done((bf16[32,2048]{1,0:T(8,128)(2,1)S(1)}, bf16[32,2048]{1,0:T(8,128)(2,1)S(1)}, u32[]{:S(2)}, u32[]{:S(2)}) %collective-permute-start.11) | collective-permute-done | bytes 131104 | tf_op jit(solution)/shard_map/ppermute | solution.py:18
  40.0 2.3 %collective-permute-start.17 = (bf16[32,2048]{1,0:T(8,128)(2,1)S(1)}, bf16[32,2048]{1,0:T(8,128)(2,1)S(1)}, u32[]{:S(2)}, u32[]{:S(2)}) collective-permute-start(bf16[32,2048]{1,0:T(8,128)(2,1)S(1)} %get-tuple-element.50.refs_4_), channel_id=1, source_target_pairs={{0,3},{1,2},{2,1},{3,0},{4,7},{5,6},{6,5},{7,4},{8,11},{9,10},{10,... | collective-permute-start | bytes 393224 | tf_op jit(solution)/shard_map/ppermute | solution.py:18
  42.2 0.5 collective-permute-start.13
  42.8 1.5 %collective-permute-start.16 = (bf16[32,2048]{1,0:T(8,128)(2,1)S(1)}, bf16[32,2048]{1,0:T(8,128)(2,1)S(1)}, u32[]{:S(2)}, u32[]{:S(2)}) collective-permute-start(bf16[32,2048]{1,0:T(8,128)(2,1)S(1)} %get-tuple-element.50.refs_4_), channel_id=1, source_target_pairs={{0,1},{1,0},{2,3},{3,2},{4,5},{5,4},{6,7},{7,6},{8,9},{9,8},{10,11... | collective-permute-start | bytes 393224 | tf_op jit(solution)/shard_map/ppermute | solution.py:18
  44.6 4.0 %collective-permute-start.15 = (bf16[32,2048]{1,0:T(8,128)(2,1)S(1)}, bf16[32,2048]{1,0:T(8,128)(2,1)S(1)}, u32[]{:S(2)}, u32[]{:S(2)}) collective-permute-start(bf16[32,2048]{1,0:T(8,128)(2,1)S(1)} %select_n.25), channel_id=1, source_target_pairs={{0,2},{3,1},{1,0},{2,3},{4,6},{7,5},{5,4},{6,7},{8,10},{11,9},{9,8... | collective-permute-start | bytes 393224 | tf_op jit(solution)/shard_map/ppermute | solution.py:50
  48.7 3.7 %collective-permute-start.18 = (bf16[32,2048]{1,0:T(8,128)(2,1)S(1)}, bf16[32,2048]{1,0:T(8,128)(2,1)S(1)}, u32[]{:S(2)}, u32[]{:S(2)}) collective-permute-start(bf16[32,2048]{1,0:T(8,128)(2,1)S(1)} %select_n.26), channel_id=1, source_target_pairs={{0,2},{3,1},{1,0},{2,3},{4,6},{7,5},{5,4},{6,7},{8,10},{11,9},{9,8... | collective-permute-start | bytes 393224 | tf_op jit(solution)/shard_map/ppermute | solution.py:50
  52.7 2.1 %collective-permute-done.15.refs_2_ = bf16[32,2048]{1,0:T(8,128)(2,1)S(1)} collective-permute-done((bf16[32,2048]{1,0:T(8,128)(2,1)S(1)}, bf16[32,2048]{1,0:T(8,128)(2,1)S(1)}, u32[]{:S(2)}, u32[]{:S(2)}) %collective-permute-start.15) | collective-permute-done | bytes 131104 | tf_op jit(solution)/shard_map/ppermute | solution.py:50
  54.8 1.4 %collective-permute-done.18.refs_6_ = bf16[32,2048]{1,0:T(8,128)(2,1)S(1)} collective-permute-done((bf16[32,2048]{1,0:T(8,128)(2,1)S(1)}, bf16[32,2048]{1,0:T(8,128)(2,1)S(1)}, u32[]{:S(2)}, u32[]{:S(2)}) %collective-permute-start.18) | collective-permute-done | bytes 131104 | tf_op jit(solution)/shard_map/ppermute | solution.py:50
  56.2 3.1 %partial_adjoint.1 = (f32[32,2048]{1,0:T(8,128)S(1)}, f32[32,2048]{1,0:T(8,128)S(1)}, f32[32,2048]{1,0:T(8,128)S(1)}, f32[32,2048]{1,0:T(8,128)S(1)}, f32[128,2048]{1,0:T(8,128)S(1)}) custom-call(s32[2]{0:T(128)S(1)} %pad_add_fusion.where, bf16[2048,2048]{1,0:T(8,128)(2,1)S(1)} %get-tuple-element.26.tiles, bf16[32,2048]{1,0:T(8,128)(2,1)S(1)} %get-tuple-element.52.refs_0_, ...), custom_call_target="tpu_custom_call" | custom-call | flops 2147483648 | bytes 8388608 | tf_op jit(solution)/shard_map/partial_adjoint/pallas_call | solution.py:168
  59.4 2.6 %collective-permute-done.19 = f32[128,2048]{1,0:T(8,128)S(1)} collective-permute-done((f32[128,2048]{1,0:T(8,128)S(1)}, f32[128,2048]{1,0:T(8,128)S(1)}, u32[]{:S(2)}, u32[]{:S(2)}) %collective-permute-start.19) | collective-permute-done | bytes 1048608 | tf_op jit(solution)/shard_map/ppermute | solution.py:18
  62.1 1.3 %collective-permute-start.20 = (bf16[32,2048]{1,0:T(8,128)(2,1)S(1)}, bf16[32,2048]{1,0:T(8,128)(2,1)S(1)}, u32[]{:S(2)}, u32[]{:S(2)}) collective-permute-start(bf16[32,2048]{1,0:T(8,128)(2,1)S(1)} %get-tuple-element.58), channel_id=1, source_target_pairs={{0,8},{4,12},{8,0},{12,4},{16,24},{20,28},{24,16},{28,20},{1,9},{5... | collective-permute-start | bytes 393224 | tf_op jit(solution)/shard_map/ppermute | solution.py:18
  63.4 0.8 %collective-permute-start.22 = (bf16[32,2048]{1,0:T(8,128)(2,1)S(1)}, bf16[32,2048]{1,0:T(8,128)(2,1)S(1)}, u32[]{:S(2)}, u32[]{:S(2)}) collective-permute-start(bf16[32,2048]{1,0:T(8,128)(2,1)S(1)} %get-tuple-element.59), channel_id=1, source_target_pairs={{0,16},{4,20},{8,24},{12,28},{16,0},{20,4},{24,8},{28,12},{1,17},{... | collective-permute-start | bytes 393224 | tf_op jit(solution)/shard_map/ppermute | solution.py:18
  64.3 1.4 %collective-permute-start.21 = (bf16[32,2048]{1,0:T(8,128)(2,1)S(1)}, bf16[32,2048]{1,0:T(8,128)(2,1)S(1)}, u32[]{:S(2)}, u32[]{:S(2)}) collective-permute-start(bf16[32,2048]{1,0:T(8,128)(2,1)S(1)} %get-tuple-element.60), channel_id=1, source_target_pairs={{0,24},{4,28},{8,16},{12,20},{16,8},{20,12},{24,0},{28,4},{1,25},{... | collective-permute-start | bytes 393224 | tf_op jit(solution)/shard_map/ppermute | solution.py:18
  65.7 0.8 %pad_maximum_fusion = f32[2,32,2048]{2,1,0:T(8,128)} fusion(f32[2,16,2048]{2,1,0:T(8,128)S(1)} %bitcast.16, f32[2,16,2048]{2,1,0:T(8,128)S(1)} %bitcast.15), kind=kLoop, calls=%fused_computation | loop fusion | flops 131072 | bytes 1048576 | tf_op jit(solution)/shard_map/concatenate | solution.py:184
  66.5 1.9 %collective-permute-done.20 = bf16[32,2048]{1,0:T(8,128)(2,1)S(1)} collective-permute-done((bf16[32,2048]{1,0:T(8,128)(2,1)S(1)}, bf16[32,2048]{1,0:T(8,128)(2,1)S(1)}, u32[]{:S(2)}, u32[]{:S(2)}) %collective-permute-start.20) | collective-permute-done | bytes 131104 | tf_op jit(solution)/shard_map/ppermute | solution.py:18
  68.4 1.5 %collective-permute-done.22 = bf16[32,2048]{1,0:T(8,128)(2,1)S(1)} collective-permute-done((bf16[32,2048]{1,0:T(8,128)(2,1)S(1)}, bf16[32,2048]{1,0:T(8,128)(2,1)S(1)}, u32[]{:S(2)}, u32[]{:S(2)}) %collective-permute-start.22) | collective-permute-done | bytes 131104 | tf_op jit(solution)/shard_map/ppermute | solution.py:18
  69.9 1.6 %collective-permute-done.21 = bf16[32,2048]{1,0:T(8,128)(2,1)S(1)} collective-permute-done((bf16[32,2048]{1,0:T(8,128)(2,1)S(1)}, bf16[32,2048]{1,0:T(8,128)(2,1)S(1)}, u32[]{:S(2)}, u32[]{:S(2)}) %collective-permute-start.21) | collective-permute-done | bytes 131104 | tf_op jit(solution)/shard_map/ppermute | solution.py:18
  71.5 0.8 %fusion.12 = f32[2048,32]{0,1:T(8,128)} fusion(f32[32,2048]{1,0:T(8,128)S(1)} %get-tuple-element.45, f32[128,2048]{1,0:T(8,128)S(1)} %collective-permute-done.19, bf16[32,2048]{1,0:T(8,128)(2,1)S(1)} %collective-permute-done.22, bf16[32,2048]{1,0:T(8,128)(2,1)S(1)} %collective-permute-done.21, bf16[32,2048]{1,0:T(8,128)(2,1)S(1)} %collective-permute-done.20), kind=kLoop, calls=%fused_computation.21 | loop fusion | flops 458752 | bytes 1179648 | tf_op jit(solution)/shard_map/transpose | solution.py:221
  (29 shorter events, 1.8 us)
Async XLA Ops:
  0.6 12.9 %copy-start = (bf16[2048,32]{0,1:T(8,128)(2,1)S(1)}, bf16[2048,32]{0,1:T(8,128)(2,1)}, u32[]{:S(2)}) copy-start(bf16[2048,32]{0,1:T(8,128)(2,1)} %param.5) | copy-start | bytes 393220
  0.6 8.8 %collective-permute-start.2 = (bf16[32,2048]{1,0:T(8,128)(2,1)}, bf16[32,2048]{1,0:T(8,128)(2,1)S(1)}, u32[]{:S(2)}, u32[]{:S(2)}) collective-permute-start(bf16[32,2048]{1,0:T(8,128)(2,1)} %bitcast.10), channel_id=1, source_target_pairs={{0,8},{4,12},{8,0},{12,4},{16,24},{20,28},{24,16},{28,20},{1,9},{5... | collective-permute-start | bytes 393224 | tf_op jit(solution)/shard_map/ppermute | solution.py:18
  3.6 8.0 %collective-permute-start.1 = (bf16[32,2048]{1,0:T(8,128)(2,1)}, bf16[32,2048]{1,0:T(8,128)(2,1)S(1)}, u32[]{:S(2)}, u32[]{:S(2)}) collective-permute-start(bf16[32,2048]{1,0:T(8,128)(2,1)} %bitcast.11), channel_id=1, source_target_pairs={{0,16},{4,20},{8,24},{12,28},{16,0},{20,4},{24,8},{28,12},{1,17},{... | collective-permute-start | bytes 393224 | tf_op jit(solution)/shard_map/ppermute | solution.py:18
  5.2 6.5 %collective-permute-start = (bf16[32,2048]{1,0:T(8,128)(2,1)}, bf16[32,2048]{1,0:T(8,128)(2,1)S(1)}, u32[]{:S(2)}, u32[]{:S(2)}) collective-permute-start(bf16[32,2048]{1,0:T(8,128)(2,1)} %bitcast.12), channel_id=1, source_target_pairs={{0,24},{4,28},{8,16},{12,20},{16,8},{20,12},{24,0},{28,4},{1,25},{... | collective-permute-start | bytes 393224 | tf_op jit(solution)/shard_map/ppermute | solution.py:18
  5.2 7.0 %collective-permute-start.3 = (bf16[32,2048]{1,0:T(8,128)(2,1)}, bf16[32,2048]{1,0:T(8,128)(2,1)S(1)}, u32[]{:S(2)}, u32[]{:S(2)}) collective-permute-start(bf16[32,2048]{1,0:T(8,128)(2,1)} %bitcast.13), channel_id=1, source_target_pairs={{0,4},{4,0},{8,12},{12,8},{16,20},{20,16},{24,28},{28,24},{1,5},{5... | collective-permute-start | bytes 393224 | tf_op jit(solution)/shard_map/ppermute | solution.py:18
  11.6 1.3 %collective-permute-start.4 = (bf16[32,2048]{1,0:T(8,128)(2,1)S(1)}, bf16[32,2048]{1,0:T(8,128)(2,1)S(1)}, u32[]{:S(2)}, u32[]{:S(2)}) collective-permute-start(bf16[32,2048]{1,0:T(8,128)(2,1)S(1)} %collective-permute-done.refs_1_), channel_id=1, source_target_pairs={{0,4},{4,0},{8,12},{12,8},{16,20},{20,16},{24,28},{28,24},{1,5},{5... | collective-permute-start | bytes 393224 | tf_op jit(solution)/shard_map/ppermute | solution.py:18
  11.6 1.5 %collective-permute-start.5 = (bf16[32,2048]{1,0:T(8,128)(2,1)S(1)}, bf16[32,2048]{1,0:T(8,128)(2,1)S(1)}, u32[]{:S(2)}, u32[]{:S(2)}) collective-permute-start(bf16[32,2048]{1,0:T(8,128)(2,1)S(1)} %collective-permute-done.1.refs_2_), channel_id=1, source_target_pairs={{0,4},{4,0},{8,12},{12,8},{16,20},{20,16},{24,28},{28,24},{1,5},{5... | collective-permute-start | bytes 393224 | tf_op jit(solution)/shard_map/ppermute | solution.py:18
  12.1 1.3 %collective-permute-start.6 = (bf16[32,2048]{1,0:T(8,128)(2,1)S(1)}, bf16[32,2048]{1,0:T(8,128)(2,1)S(1)}, u32[]{:S(2)}, u32[]{:S(2)}) collective-permute-start(bf16[32,2048]{1,0:T(8,128)(2,1)S(1)} %collective-permute-done.2.refs_3_), channel_id=1, source_target_pairs={{0,4},{4,0},{8,12},{12,8},{16,20},{20,16},{24,28},{28,24},{1,5},{5... | collective-permute-start | bytes 393224 | tf_op jit(solution)/shard_map/ppermute | solution.py:18
  16.6 7.3 %collective-permute-start.7 = (bf16[32,2048]{1,0:T(8,128)(2,1)S(1)}, bf16[32,2048]{1,0:T(8,128)(2,1)S(1)}, u32[]{:S(2)}, u32[]{:S(2)}) collective-permute-start(bf16[32,2048]{1,0:T(8,128)(2,1)S(1)} %get-tuple-element.37), channel_id=1, source_target_pairs={{0,1},{3,2},{2,0},{1,3},{4,5},{7,6},{6,4},{5,7},{8,9},{11,10},{10,... | collective-permute-start | bytes 393224 | tf_op jit(solution)/shard_map/ppermute | solution.py:32
  18.2 9.4 %collective-permute-start.10 = (bf16[32,2048]{1,0:T(8,128)(2,1)S(1)}, bf16[32,2048]{1,0:T(8,128)(2,1)S(1)}, u32[]{:S(2)}, u32[]{:S(2)}) collective-permute-start(bf16[32,2048]{1,0:T(8,128)(2,1)S(1)} %get-tuple-element.43), channel_id=1, source_target_pairs={{0,1},{3,2},{2,0},{1,3},{4,5},{7,6},{6,4},{5,7},{8,9},{11,10},{10,... | collective-permute-start | bytes 393224 | tf_op jit(solution)/shard_map/ppermute | solution.py:32
  23.9 12.3 %collective-permute-start.9 = (bf16[32,2048]{1,0:T(8,128)(2,1)S(1)}, bf16[32,2048]{1,0:T(8,128)(2,1)S(1)}, u32[]{:S(2)}, u32[]{:S(2)}) collective-permute-start(bf16[32,2048]{1,0:T(8,128)(2,1)S(1)} %get-tuple-element.54), channel_id=1, source_target_pairs={{0,3},{1,2},{2,1},{3,0},{4,7},{5,6},{6,5},{7,4},{8,11},{9,10},{10,... | collective-permute-start | bytes 393224 | tf_op jit(solution)/shard_map/ppermute | solution.py:18
  27.6 8.6 %collective-permute-start.8 = (bf16[32,2048]{1,0:T(8,128)(2,1)S(1)}, bf16[32,2048]{1,0:T(8,128)(2,1)S(1)}, u32[]{:S(2)}, u32[]{:S(2)}) collective-permute-start(bf16[32,2048]{1,0:T(8,128)(2,1)S(1)} %get-tuple-element.38), channel_id=1, source_target_pairs={{0,1},{1,0},{2,3},{3,2},{4,5},{5,4},{6,7},{7,6},{8,9},{9,8},{10,11... | collective-permute-start | bytes 393224 | tf_op jit(solution)/shard_map/ppermute | solution.py:18
  27.7 12.2 %collective-permute-start.12 = (bf16[32,2048]{1,0:T(8,128)(2,1)S(1)}, bf16[32,2048]{1,0:T(8,128)(2,1)S(1)}, u32[]{:S(2)}, u32[]{:S(2)}) collective-permute-start(bf16[32,2048]{1,0:T(8,128)(2,1)S(1)} %get-tuple-element.56), channel_id=1, source_target_pairs={{0,3},{1,2},{2,1},{3,0},{4,7},{5,6},{6,5},{7,4},{8,11},{9,10},{10,... | collective-permute-start | bytes 393224 | tf_op jit(solution)/shard_map/ppermute | solution.py:18
  30.4 9.4 %collective-permute-start.11 = (bf16[32,2048]{1,0:T(8,128)(2,1)S(1)}, bf16[32,2048]{1,0:T(8,128)(2,1)S(1)}, u32[]{:S(2)}, u32[]{:S(2)}) collective-permute-start(bf16[32,2048]{1,0:T(8,128)(2,1)S(1)} %get-tuple-element.44), channel_id=1, source_target_pairs={{0,1},{1,0},{2,3},{3,2},{4,5},{5,4},{6,7},{7,6},{8,9},{9,8},{10,11... | collective-permute-start | bytes 393224 | tf_op jit(solution)/shard_map/ppermute | solution.py:18
  36.3 8.3 %collective-permute-start.14 = (bf16[32,2048]{1,0:T(8,128)(2,1)S(1)}, bf16[32,2048]{1,0:T(8,128)(2,1)S(1)}, u32[]{:S(2)}, u32[]{:S(2)}) collective-permute-start(bf16[32,2048]{1,0:T(8,128)(2,1)S(1)} %get-tuple-element.52.refs_0_), channel_id=1, source_target_pairs={{0,3},{1,2},{2,1},{3,0},{4,7},{5,6},{6,5},{7,4},{8,11},{9,10},{10,... | collective-permute-start | bytes 393224 | tf_op jit(solution)/shard_map/ppermute | solution.py:18
  40.0 8.7 %collective-permute-start.17 = (bf16[32,2048]{1,0:T(8,128)(2,1)S(1)}, bf16[32,2048]{1,0:T(8,128)(2,1)S(1)}, u32[]{:S(2)}, u32[]{:S(2)}) collective-permute-start(bf16[32,2048]{1,0:T(8,128)(2,1)S(1)} %get-tuple-element.50.refs_4_), channel_id=1, source_target_pairs={{0,3},{1,2},{2,1},{3,0},{4,7},{5,6},{6,5},{7,4},{8,11},{9,10},{10,... | collective-permute-start | bytes 393224 | tf_op jit(solution)/shard_map/ppermute | solution.py:18
  42.2 10.2 %collective-permute-start.13 = (bf16[32,2048]{1,0:T(8,128)(2,1)S(1)}, bf16[32,2048]{1,0:T(8,128)(2,1)S(1)}, u32[]{:S(2)}, u32[]{:S(2)}) collective-permute-start(bf16[32,2048]{1,0:T(8,128)(2,1)S(1)} %get-tuple-element.52.refs_0_), channel_id=1, source_target_pairs={{0,1},{1,0},{2,3},{3,2},{4,5},{5,4},{6,7},{7,6},{8,9},{9,8},{10,11... | collective-permute-start | bytes 393224 | tf_op jit(solution)/shard_map/ppermute | solution.py:18
  42.8 9.9 %collective-permute-start.16 = (bf16[32,2048]{1,0:T(8,128)(2,1)S(1)}, bf16[32,2048]{1,0:T(8,128)(2,1)S(1)}, u32[]{:S(2)}, u32[]{:S(2)}) collective-permute-start(bf16[32,2048]{1,0:T(8,128)(2,1)S(1)} %get-tuple-element.50.refs_4_), channel_id=1, source_target_pairs={{0,1},{1,0},{2,3},{3,2},{4,5},{5,4},{6,7},{7,6},{8,9},{9,8},{10,11... | collective-permute-start | bytes 393224 | tf_op jit(solution)/shard_map/ppermute | solution.py:18
  44.6 10.2 %collective-permute-start.15 = (bf16[32,2048]{1,0:T(8,128)(2,1)S(1)}, bf16[32,2048]{1,0:T(8,128)(2,1)S(1)}, u32[]{:S(2)}, u32[]{:S(2)}) collective-permute-start(bf16[32,2048]{1,0:T(8,128)(2,1)S(1)} %select_n.25), channel_id=1, source_target_pairs={{0,2},{3,1},{1,0},{2,3},{4,6},{7,5},{5,4},{6,7},{8,10},{11,9},{9,8... | collective-permute-start | bytes 393224 | tf_op jit(solution)/shard_map/ppermute | solution.py:50
  48.7 7.5 %collective-permute-start.18 = (bf16[32,2048]{1,0:T(8,128)(2,1)S(1)}, bf16[32,2048]{1,0:T(8,128)(2,1)S(1)}, u32[]{:S(2)}, u32[]{:S(2)}) collective-permute-start(bf16[32,2048]{1,0:T(8,128)(2,1)S(1)} %select_n.26), channel_id=1, source_target_pairs={{0,2},{3,1},{1,0},{2,3},{4,6},{7,5},{5,4},{6,7},{8,10},{11,9},{9,8... | collective-permute-start | bytes 393224 | tf_op jit(solution)/shard_map/ppermute | solution.py:50
  59.3 2.7 %collective-permute-start.19 = (f32[128,2048]{1,0:T(8,128)S(1)}, f32[128,2048]{1,0:T(8,128)S(1)}, u32[]{:S(2)}, u32[]{:S(2)}) collective-permute-start(f32[128,2048]{1,0:T(8,128)S(1)} %get-tuple-element.46), channel_id=1, source_target_pairs={{0,4},{4,0},{8,12},{12,8},{16,20},{20,16},{24,28},{28,24},{1,5},{5... | collective-permute-start | bytes 3145736 | tf_op jit(solution)/shard_map/ppermute | solution.py:18
  62.1 6.2 %collective-permute-start.20 = (bf16[32,2048]{1,0:T(8,128)(2,1)S(1)}, bf16[32,2048]{1,0:T(8,128)(2,1)S(1)}, u32[]{:S(2)}, u32[]{:S(2)}) collective-permute-start(bf16[32,2048]{1,0:T(8,128)(2,1)S(1)} %get-tuple-element.58), channel_id=1, source_target_pairs={{0,8},{4,12},{8,0},{12,4},{16,24},{20,28},{24,16},{28,20},{1,9},{5... | collective-permute-start | bytes 393224 | tf_op jit(solution)/shard_map/ppermute | solution.py:18
  63.4 6.4 %collective-permute-start.22 = (bf16[32,2048]{1,0:T(8,128)(2,1)S(1)}, bf16[32,2048]{1,0:T(8,128)(2,1)S(1)}, u32[]{:S(2)}, u32[]{:S(2)}) collective-permute-start(bf16[32,2048]{1,0:T(8,128)(2,1)S(1)} %get-tuple-element.59), channel_id=1, source_target_pairs={{0,16},{4,20},{8,24},{12,28},{16,0},{20,4},{24,8},{28,12},{1,17},{... | collective-permute-start | bytes 393224 | tf_op jit(solution)/shard_map/ppermute | solution.py:18
  64.3 7.2 %collective-permute-start.21 = (bf16[32,2048]{1,0:T(8,128)(2,1)S(1)}, bf16[32,2048]{1,0:T(8,128)(2,1)S(1)}, u32[]{:S(2)}, u32[]{:S(2)}) collective-permute-start(bf16[32,2048]{1,0:T(8,128)(2,1)S(1)} %get-tuple-element.60), channel_id=1, source_target_pairs={{0,24},{4,28},{8,16},{12,20},{16,8},{20,12},{24,0},{28,4},{1,25},{... | collective-permute-start | bytes 393224 | tf_op jit(solution)/shard_map/ppermute | solution.py:18

commit v12 on v11

v12 whole, which is shorter than its diff:
```python
import functools

import jax
import jax.numpy as jnp
from jax import lax
from jax.experimental import pallas as pl
from jax.experimental.pallas import tpu as pltpu
from jax.sharding import PartitionSpec as P

F32, BF16 = jnp.float32, jnp.bfloat16
VMEM_LIMIT = 28 * 2**20
STEP = 512
CHUNKS = 2


def exchange(value, axis, offset):
    size = lax.axis_size(axis)
    return lax.ppermute(value, axis, [(i, i ^ offset) for i in range(size)])


def at_end(where, size):
    return (where[1] == 0) | (where[1] == size - 1)


def after(value, earlier):
    return lax.optimization_barrier((value, earlier))[0]


def window_sums(terms, ends):
    size = len(terms)
    if size == 4:
        came = lax.ppermute(terms[2], "col", [(0, 1), (3, 2), (2, 0), (1, 3)])
        came = came.astype(F32)
        onward = terms[3] + jnp.where(ends > 0, 0.0, came)
        onward = onward.astype(BF16)
        far = exchange(onward, "col", 3).astype(F32)
        near = exchange(after(terms[1], onward), "col", 1).astype(F32)
        return terms[0] + near + far + jnp.where(ends > 0, came, 0.0)
    total = terms[0]
    for offset in range(1, size):
        total = total + exchange(terms[offset].astype(BF16), "col", offset).astype(F32)
    return total


def window_spread(lowered, ends, size):
    if size == 4:
        far = exchange(lowered, "col", 3)
        near = exchange(lowered, "col", 1)
        onward = jnp.where(ends > 0, lowered, far)
        return [lowered, near, lax.ppermute(onward, "col", [(0, 2), (3, 1), (1, 0), (2, 3)]), far]
    return [lowered] + [exchange(lowered, "col", offset) for offset in range(1, size)]


def mask_kernel(where, mask_hbm, green_ref, tiles, token, mask_ref, mask_sem, sems, *, block):
    rows, cols = tiles.shape
    token[...] = jnp.zeros(token.shape, token.dtype)
    levels = pltpu.make_async_copy(mask_hbm, mask_ref, mask_sem)
    levels.start()
    copies = []
    for step in range(rows // STEP):
        at = pl.ds(step * STEP, STEP)
        copies.append(pltpu.make_async_copy(green_ref.at[at], tiles.at[at], sems.at[step]))
        copies[-1].start()
    levels.wait()
    for step, copy in enumerate(copies):
        copy.wait()
        for i in range(step * STEP // block, (step + 1) * STEP // block):
            for j in range(cols // block):

                @pl.when(mask_ref[i, j] == 0)
                def _():
                    tiles[i * block : (i + 1) * block, j * block : (j + 1) * block] = jnp.zeros((block, block), BF16)


def masked(where, green, mask):
    rows, cols = green.shape
    return pl.pallas_call(
        functools.partial(mask_kernel, block=rows // mask.shape[0]),
        in_specs=[pl.BlockSpec(memory_space=pltpu.SMEM)] + [pl.BlockSpec(memory_space=pltpu.HBM)] * 2,
        out_specs=[pl.BlockSpec(memory_space=pltpu.VMEM)] * 2,
        out_shape=[pltpu.VMEM((rows, cols), BF16), jax.ShapeDtypeStruct((8, 128), F32)],
        scratch_shapes=[
            pltpu.SMEM(mask.shape, mask.dtype),
            pltpu.SemaphoreType.DMA,
            pltpu.SemaphoreType.DMA((rows // STEP,)),
        ],
        compiler_params=pltpu.CompilerParams(vmem_limit_bytes=VMEM_LIMIT),
        cost_estimate=pl.CostEstimate(flops=0, bytes_accessed=2 * rows * cols, transcendentals=0),
        name="masked_tiles",
    )(where, *(pltpu.with_memory_space_constraint(array, pltpu.HBM) for array in (mask, green)))


def sketch_kernel(where, tiles, token, *refs, base, offsets_row, offsets_col):
    blocks, outs, ends, probes = refs[: len(offsets_row)], refs[len(offsets_row) : -2], refs[-2], refs[-1]
    own = blocks[0].shape[0]
    ratio = len(offsets_row) // len(offsets_col)
    share = own * ratio
    ends[...] = jnp.full(ends.shape, at_end(where, len(offsets_col)).astype(F32))
    for offset, ref in zip(offsets_row, blocks):
        column = where[0] ^ offset
        start = (lax.div(column, ratio) ^ where[1]) * share + lax.rem(column, ratio) * own
        probes[pl.ds(pl.multiple_of(start, own), own), :] = ref[...]
    for step in range(ends.shape[1] // STEP):
        rows, at = slice(base + step * STEP, base + (step + 1) * STEP), slice(step * STEP, (step + 1) * STEP)
        term = lax.dot_general(probes[...], tiles[rows, :], (((1,), (1,)), ((), ())), preferred_element_type=F32)
        for k, out in enumerate(outs):
            out[:, at] = term[k * share : (k + 1) * share].astype(out.dtype)


def partial_sketch(where, tiles, blocks, token, offsets_row, offsets_col, chunk, chunks):
    rows, cols = tiles.shape
    rows //= chunks
    width = blocks[0].shape[0] * len(blocks)
    share = width // len(offsets_col)
    vmem = pl.BlockSpec(memory_space=pltpu.VMEM)
    exact = (0, offsets_col[-1])
    outs = [jax.ShapeDtypeStruct((share, rows), F32 if offset in exact else BF16) for offset in offsets_col]
    outs.append(jax.ShapeDtypeStruct((share, rows), F32))
    return pl.pallas_call(
        functools.partial(sketch_kernel, base=chunk * rows, offsets_row=offsets_row, offsets_col=offsets_col),
        in_specs=[pl.BlockSpec(memory_space=pltpu.SMEM)] + [vmem] * (2 + len(blocks)),
        out_specs=[vmem] * len(outs),
        out_shape=outs,
        scratch_shapes=[pltpu.VMEM((width, cols), BF16)],
        compiler_params=pltpu.CompilerParams(vmem_limit_bytes=VMEM_LIMIT),
        cost_estimate=pl.CostEstimate(
            flops=2 * width * cols * rows, bytes_accessed=2 * rows * cols, transcendentals=0
        ),
        name="partial_sketch",
    )(where, tiles, token, *blocks)


def adjoint_kernel(where, tiles, *refs, base, parts, offsets_col, devices):
    shares, earlier, outs, lowered = refs[: len(offsets_col)], refs[len(offsets_col) : -1 - parts], refs[-1 - parts : -1], refs[-1]
    share, rows = shares[0].shape
    ratio = devices // len(offsets_col)
    own = share // ratio
    for offset, ref in zip(offsets_col, shares):
        for n in range(ratio):
            apart = where[0] ^ ((where[1] ^ offset) * ratio + n)
            start = ((apart >> 1) + (apart & 1) * (devices // 2)) * own
            lowered[pl.ds(pl.multiple_of(start, own), own), :] = ref[n * own : (n + 1) * own, :]
    for step in range(tiles.shape[1] // STEP):
        at = slice(step * STEP, (step + 1) * STEP)
        term = jnp.dot(lowered[...], tiles[base : base + rows, at], preferred_element_type=F32)
        if earlier:
            term += earlier[0][:, at]
        height = outs[0].shape[0]
        for k, out in enumerate(outs):
            out[:, at] = term[k * height : (k + 1) * height]


def partial_adjoint(where, tiles, shares, earlier, offsets_col, devices, chunk, chunks):
    rows, cols = tiles.shape
    rows //= chunks
    width = shares[0].shape[0] * len(offsets_col)
    parts = 2 if chunk == chunks - 1 else 1
    vmem = pl.BlockSpec(memory_space=pltpu.VMEM)
    return pl.pallas_call(
        functools.partial(
            adjoint_kernel, base=chunk * rows, parts=parts, offsets_col=offsets_col, devices=devices
        ),
        in_specs=[pl.BlockSpec(memory_space=pltpu.SMEM)] + [vmem] * (1 + len(shares) + len(earlier)),
        out_specs=[vmem] * parts,
        out_shape=[jax.ShapeDtypeStruct((width // parts, cols), F32)] * parts,
        scratch_shapes=[pltpu.VMEM((width, rows), BF16)],
        compiler_params=pltpu.CompilerParams(vmem_limit_bytes=VMEM_LIMIT),
        cost_estimate=pl.CostEstimate(
            flops=2 * width * cols * rows, bytes_accessed=2 * rows * cols, transcendentals=0
        ),
        name="partial_adjoint",
    )(where, tiles, *shares, *earlier)


def local(green, mask, probes):
    n_row, n_col = lax.axis_size("row"), lax.axis_size("col")
    where = jnp.stack([lax.axis_index("row"), lax.axis_index("col")]).astype(jnp.int32)
    own_width = probes.shape[1]
    chunks = CHUNKS if green.shape[0] % (CHUNKS * STEP) == 0 else 1
    offsets_col = list(range(n_col))
    offsets_core = list(range(0, n_row, 2))
    gather_core = [0] + offsets_core[:0:-1]
    offsets_row = gather_core + [offset ^ 1 for offset in gather_core]
    tiles, token = masked(where, green, mask)

    own = probes.T
    held = [own] + [exchange(own, "row", offset) for offset in gather_core[1:]]
    twin = exchange(own, "row", 1)
    held, token = lax.optimization_barrier((held, token))
    blocks = held + [twin] + [exchange(block, "row", 1) for block in held[1:]]

    totals, shares = [], []
    for chunk in range(chunks):
        *parts, ends = partial_sketch(where, tiles, blocks, token, offsets_row, offsets_col, chunk, chunks)
        totals.append(window_sums(parts, ends))
        shares.append(window_spread(totals[-1].astype(BF16), ends, n_col))

    earlier = []
    for chunk in range(chunks):
        earlier = partial_adjoint(where, tiles, shares[chunk], earlier, offsets_col, n_row, chunk, chunks)
    mine, others = earlier
    others = exchange(others, "row", 1)
    cuts = [slice(k * own_width, (k + 1) * own_width) for k in range(len(offsets_core))]
    pairs = [mine[cut] + others[cut] for cut in cuts]
    adjoint = pairs[0]
    for offset in offsets_core[1:2] + offsets_core[:1:-1]:
        adjoint = adjoint + exchange(pairs[offset // 2].astype(BF16), "row", offset).astype(F32)
    return jnp.concatenate(totals, axis=1).T, adjoint.T


def solution(mesh):
    in_specs = (P("row", "col"), P("row", "col"), P("col", "row"))
    out_specs = (P("row", "col"), P("col", "row"))
    return jax.shard_map(local, mesh=mesh, in_specs=in_specs, out_specs=out_specs, check_vma=False)
```

time: 72.4 us -> 70.2 us (0.970)
  starting transfers between devices: 33.1 us -> 31 us
  waiting for transfers between devices: 25.9 us -> 24.5 us
  Pallas kernels: 10.4 us -> 11.6 us
    ppermute x19, waiting for transfers between devices: 19.3 us -> 21.7 us  [exchange(): return lax.ppermute(value, axis, [(i, i ^ offset) for i in range(size)])]
    ppermute x19, starting transfers between devices: 21.1 us -> 19 us  [exchange(): return lax.ppermute(value, axis, [(i, i ^ offset) for i in range(size)])]
    ppermute x2, waiting for transfers between devices: 3.52 us -> 1.41 us  [window_spread(): lax.ppermute(onward, 'col', [(0, 2), (3, 1), (1, 0), (2, 3)])]
    ppermute x2, waiting for transfers between devices: 3.06 us -> 1.49 us  [window_sums(): came = lax.ppermute(terms[2], 'col', [(0, 1), (3, 2), (2, 0), (1, 3)])]
    pallas_call x2 -> x4, Pallas kernels: 6.17 us -> 7.39 us  [the longest x2 3.71 us: partial_sketch(): pl.pallas_call(functools.partial(sketch_kernel, base=chunk * rows, offset...]
    transpose x1 -> x2, other arithmetic: 0.77 us -> 1.61 us  [local(): return (jnp.concatenate(totals, axis=1).T, adjoint.T)]
    concatenate x1 -> x0, other arithmetic: 0.83 us -> none  [join(): jnp.concatenate([p.reshape(-1, group, length) for p in parts], axis=1)]
  transfers between devices with their start and end apart: 23 -> 23, of which waited for: 15 -> 15; matrix products, arithmetic and copies ran while one was open for 2% -> 2% of each run, Pallas kernels for 6% -> 11%
where the time goes in v12:
time: 70.2 us; the launch traced here: 70.1 us
  starting transfers between devices  31 us (44%)
  waiting for transfers between devices  24.5 us (35%)
  Pallas kernels  11.6 us (17%)
  other arithmetic  2.22 us (3%)
  between operations  0.74 us (1%)
    ppermute x19, waiting for transfers between devices, exchange(): return lax.ppermute(value, axis, [(i, i ^ offset) for i in range(size)])  21.7 us
    ppermute x19, starting transfers between devices, exchange(): return lax.ppermute(value, axis, [(i, i ^ offset) for i in range(size)])  19 us
    ppermute x2, starting transfers between devices, window_spread(): lax.ppermute(onward, 'col', [(0, 2), (3, 1), (1, 0), (2, 3)])  7.73 us
    ppermute x2, starting transfers between devices, window_sums(): came = lax.ppermute(terms[2], 'col', [(0, 1), (3, 2), (2, 0), (1, 3)])  4.26 us
    pallas_call x1, Pallas kernels, masked(): pl.pallas_call(functools.partial(mask_kernel, block=rows // mask.shape[0]...  4.19 us
    pallas_call x2, Pallas kernels, partial_sketch(): pl.pallas_call(functools.partial(sketch_kernel, base=chunk * rows, offset...  3.71 us
    pallas_call x2, Pallas kernels, partial_adjoint(): pl.pallas_call(functools.partial(adjoint_kernel, base=chunk * rows, parts...  3.68 us
    transpose x2, other arithmetic, local(): return (jnp.concatenate(totals, axis=1).T, adjoint.T)  1.61 us
  transfers between devices with their start and end apart: 23, of which 15 were waited for; matrix products, arithmetic and copies ran while one was open for 2% of the time, Pallas kernels for 11%

profile of v12, /device:TPU:0, one launch (start us, length us, event | category | flops | bytes accessed | tf_op | source)
XLA Modules:
  0.0 70.1 jit_solution(12383152288201677789)
XLA Ops:
  0.6 3.0 %collective-permute-start.2 = (bf16[32,2048]{1,0:T(8,128)(2,1)}, bf16[32,2048]{1,0:T(8,128)(2,1)S(1)}, u32[]{:S(2)}, u32[]{:S(2)}) collective-permute-start(bf16[32,2048]{1,0:T(8,128)(2,1)} %bitcast.7), channel_id=1, source_target_pairs={{0,8},{4,12},{8,0},{12,4},{16,24},{20,28},{24,16},{28,20},{1,9},{5... | collective-permute-start | bytes 393224 | tf_op jit(solution)/shard_map/ppermute | solution.py:18
  3.6 1.5 %collective-permute-start.1 = (bf16[32,2048]{1,0:T(8,128)(2,1)}, bf16[32,2048]{1,0:T(8,128)(2,1)S(1)}, u32[]{:S(2)}, u32[]{:S(2)}) collective-permute-start(bf16[32,2048]{1,0:T(8,128)(2,1)} %bitcast.8), channel_id=1, source_target_pairs={{0,16},{4,20},{8,24},{12,28},{16,0},{20,4},{24,8},{28,12},{1,17},{... | collective-permute-start | bytes 393224 | tf_op jit(solution)/shard_map/ppermute | solution.py:18
  5.3 4.2 %masked_tiles.1 = (bf16[2048,2048]{1,0:T(8,128)(2,1)S(1)}, f32[8,128]{1,0:T(8,128)S(1)}) custom-call(s32[2]{0:T(128)S(1)} %pad_add_fusion.where, s32[8,8]{1,0:T(8,128)} %mask_hbm.1, bf16[2048,2048]{1,0:T(8,128)(2,1)} %green_ref.1), custom_call_target="tpu_custom_call" | custom-call | bytes 8388608 | tf_op jit(solution)/shard_map/masked_tiles/pallas_call | solution.py:77
  9.5 2.2 %collective-permute-done.1.refs_2_ = bf16[32,2048]{1,0:T(8,128)(2,1)S(1)} collective-permute-done((bf16[32,2048]{1,0:T(8,128)(2,1)}, bf16[32,2048]{1,0:T(8,128)(2,1)S(1)}, u32[]{:S(2)}, u32[]{:S(2)}) %collective-permute-start.1) | collective-permute-done | bytes 131104 | tf_op jit(solution)/shard_map/ppermute | solution.py:18
  12.2 0.8 %collective-permute-done.4.refs_5_ = bf16[32,2048]{1,0:T(8,128)(2,1)S(1)} collective-permute-done((bf16[32,2048]{1,0:T(8,128)(2,1)S(1)}, bf16[32,2048]{1,0:T(8,128)(2,1)S(1)}, u32[]{:S(2)}, u32[]{:S(2)}) %collective-permute-start.4) | collective-permute-done | bytes 131104 | tf_op jit(solution)/shard_map/ppermute | solution.py:18
  13.5 1.9 %partial_sketch.2 = (f32[64,1024]{1,0:T(8,128)S(1)}, bf16[64,1024]{1,0:T(8,128)(2,1)S(1)}, bf16[64,1024]{1,0:T(8,128)(2,1)S(1)}, f32[64,1024]{1,0:T(8,128)S(1)}, f32[64,1024]{1,0:T(8,128)S(1)}) custom-call(s32[2]{0:T(128)S(1)} %pad_add_fusion.where, bf16[2048,2048]{1,0:T(8,128)(2,1)S(1)} %get-tuple-element.23.tiles, f32[8,128]{1,0:T(8,128)S(1)} %get-tuple-element.25.token, ...), custom_call_target="tpu_custom_call" | custom-call | flops 1073741824 | bytes 4194304 | tf_op jit(solution)/shard_map/partial_sketch/pallas_call | solution.py:119
  15.4 1.6 %collective-permute-start.7 = (bf16[64,1024]{1,0:T(8,128)(2,1)S(1)}, bf16[64,1024]{1,0:T(8,128)(2,1)S(1)}, u32[]{:S(2)}, u32[]{:S(2)}) collective-permute-start(bf16[64,1024]{1,0:T(8,128)(2,1)S(1)} %get-tuple-element.34), channel_id=1, source_target_pairs={{0,1},{3,2},{2,0},{1,3},{4,5},{7,6},{6,4},{5,7},{8,9},{11,10},{10,... | collective-permute-start | bytes 393224 | tf_op jit(solution)/shard_map/ppermute | solution.py:32
  17.0 1.9 %partial_sketch.3 = (f32[64,1024]{1,0:T(8,128)S(1)}, bf16[64,1024]{1,0:T(8,128)(2,1)S(1)}, bf16[64,1024]{1,0:T(8,128)(2,1)S(1)}, f32[64,1024]{1,0:T(8,128)S(1)}, f32[64,1024]{1,0:T(8,128)S(1)}) custom-call(s32[2]{0:T(128)S(1)} %pad_add_fusion.where, bf16[2048,2048]{1,0:T(8,128)(2,1)S(1)} %get-tuple-element.23.tiles, f32[8,128]{1,0:T(8,128)S(1)} %get-tuple-element.25.token, ...), custom_call_target="tpu_custom_call" | custom-call | flops 1073741824 | bytes 4194304 | tf_op jit(solution)/shard_map/partial_sketch/pallas_call | solution.py:119
  18.8 2.6 %collective-permute-start.10 = (bf16[64,1024]{1,0:T(8,128)(2,1)S(1)}, bf16[64,1024]{1,0:T(8,128)(2,1)S(1)}, u32[]{:S(2)}, u32[]{:S(2)}) collective-permute-start(bf16[64,1024]{1,0:T(8,128)(2,1)S(1)} %get-tuple-element.40), channel_id=1, source_target_pairs={{0,1},{3,2},{2,0},{1,3},{4,5},{7,6},{6,4},{5,7},{8,9},{11,10},{10,... | collective-permute-start | bytes 393224 | tf_op jit(solution)/shard_map/ppermute | solution.py:32
  22.0 4.4 %collective-permute-start.9 = (bf16[64,1024]{1,0:T(8,128)(2,1)S(1)}, bf16[64,1024]{1,0:T(8,128)(2,1)S(1)}, u32[]{:S(2)}, u32[]{:S(2)}) collective-permute-start(bf16[64,1024]{1,0:T(8,128)(2,1)S(1)} %get-tuple-element.48), channel_id=1, source_target_pairs={{0,3},{1,2},{2,1},{3,0},{4,7},{5,6},{6,5},{7,4},{8,11},{9,10},{10,... | collective-permute-start | bytes 393224 | tf_op jit(solution)/shard_map/ppermute | solution.py:18
  26.3 1.1 %collective-permute-done.10 = bf16[64,1024]{1,0:T(8,128)(2,1)S(1)} collective-permute-done((bf16[64,1024]{1,0:T(8,128)(2,1)S(1)}, bf16[64,1024]{1,0:T(8,128)(2,1)S(1)}, u32[]{:S(2)}, u32[]{:S(2)}) %collective-permute-start.10) | collective-permute-done | bytes 131104 | tf_op jit(solution)/shard_map/ppermute | solution.py:32
  27.5 1.7 %collective-permute-start.12 = (bf16[64,1024]{1,0:T(8,128)(2,1)S(1)}, bf16[64,1024]{1,0:T(8,128)(2,1)S(1)}, u32[]{:S(2)}, u32[]{:S(2)}) collective-permute-start(bf16[64,1024]{1,0:T(8,128)(2,1)S(1)} %get-tuple-element.50), channel_id=1, source_target_pairs={{0,3},{1,2},{2,1},{3,0},{4,7},{5,6},{6,5},{7,4},{8,11},{9,10},{10,... | collective-permute-start | bytes 393224 | tf_op jit(solution)/shard_map/ppermute | solution.py:18
  29.1 6.0 %collective-permute-done.8 = bf16[64,1024]{1,0:T(8,128)(2,1)S(1)} collective-permute-done((bf16[64,1024]{1,0:T(8,128)(2,1)S(1)}, bf16[64,1024]{1,0:T(8,128)(2,1)S(1)}, u32[]{:S(2)}, u32[]{:S(2)}) %collective-permute-start.8) | collective-permute-done | bytes 131104 | tf_op jit(solution)/shard_map/ppermute | solution.py:18
  35.3 1.5 %collective-permute-start.17 = (bf16[64,1024]{1,0:T(8,128)(2,1)S(1)}, bf16[64,1024]{1,0:T(8,128)(2,1)S(1)}, u32[]{:S(2)}, u32[]{:S(2)}) collective-permute-start(bf16[64,1024]{1,0:T(8,128)(2,1)S(1)} %get-tuple-element.44.refs_0_), channel_id=1, source_target_pairs={{0,3},{1,2},{2,1},{3,0},{4,7},{5,6},{6,5},{7,4},{8,11},{9,10},{10,... | collective-permute-start | bytes 393224 | tf_op jit(solution)/shard_map/ppermute | solution.py:18
  36.8 1.8 %collective-permute-done.11 = bf16[64,1024]{1,0:T(8,128)(2,1)S(1)} collective-permute-done((bf16[64,1024]{1,0:T(8,128)(2,1)S(1)}, bf16[64,1024]{1,0:T(8,128)(2,1)S(1)}, u32[]{:S(2)}, u32[]{:S(2)}) %collective-permute-start.11) | collective-permute-done | bytes 131104 | tf_op jit(solution)/shard_map/ppermute | solution.py:18
  38.7 2.1 %collective-permute-start.14 = (bf16[64,1024]{1,0:T(8,128)(2,1)S(1)}, bf16[64,1024]{1,0:T(8,128)(2,1)S(1)}, u32[]{:S(2)}, u32[]{:S(2)}) collective-permute-start(bf16[64,1024]{1,0:T(8,128)(2,1)S(1)} %get-tuple-element.46.refs_0_), channel_id=1, source_target_pairs={{0,3},{1,2},{2,1},{3,0},{4,7},{5,6},{6,5},{7,4},{8,11},{9,10},{10,... | collective-permute-start | bytes 393224 | tf_op jit(solution)/shard_map/ppermute | solution.py:18
  40.9 0.6 collective-permute-start.16
  41.5 2.1 %collective-permute-done.17.refs_3_ = bf16[64,1024]{1,0:T(8,128)(2,1)S(1)} collective-permute-done((bf16[64,1024]{1,0:T(8,128)(2,1)S(1)}, bf16[64,1024]{1,0:T(8,128)(2,1)S(1)}, u32[]{:S(2)}, u32[]{:S(2)}) %collective-permute-start.17) | collective-permute-done | bytes 131104 | tf_op jit(solution)/shard_map/ppermute | solution.py:18
  43.6 4.3 %collective-permute-start.18 = (bf16[64,1024]{1,0:T(8,128)(2,1)S(1)}, bf16[64,1024]{1,0:T(8,128)(2,1)S(1)}, u32[]{:S(2)}, u32[]{:S(2)}) collective-permute-start(bf16[64,1024]{1,0:T(8,128)(2,1)S(1)} %select_n.26), channel_id=1, source_target_pairs={{0,2},{3,1},{1,0},{2,3},{4,6},{7,5},{5,4},{6,7},{8,10},{11,9},{9,8... | collective-permute-start | bytes 393224 | tf_op jit(solution)/shard_map/ppermute | solution.py:50
  47.9 3.5 %collective-permute-start.15 = (bf16[64,1024]{1,0:T(8,128)(2,1)S(1)}, bf16[64,1024]{1,0:T(8,128)(2,1)S(1)}, u32[]{:S(2)}, u32[]{:S(2)}) collective-permute-start(bf16[64,1024]{1,0:T(8,128)(2,1)S(1)} %select_n.25), channel_id=1, source_target_pairs={{0,2},{3,1},{1,0},{2,3},{4,6},{7,5},{5,4},{6,7},{8,10},{11,9},{9,8... | collective-permute-start | bytes 393224 | tf_op jit(solution)/shard_map/ppermute | solution.py:50
  51.4 1.8 %partial_adjoint.2.refs_4_ = f32[256,2048]{1,0:T(8,128)S(1)} custom-call(s32[2]{0:T(128)S(1)} %pad_add_fusion.where, bf16[2048,2048]{1,0:T(8,128)(2,1)S(1)} %get-tuple-element.23.tiles, bf16[64,1024]{1,0:T(8,128)(2,1)S(1)} %get-tuple-element.44.refs_0_, bf16[64,1024]{1,0:T(8,128)(2,1)S(1)} %collective-permute-done.16.refs_1_, ...), custom_call_target="tpu_custom_call" | custom-call | flops 1073741824 | bytes 4194304 | tf_op jit(solution)/shard_map/partial_adjoint/pallas_call | solution.py:159
  53.8 1.4 %collective-permute-done.15.refs_2_ = bf16[64,1024]{1,0:T(8,128)(2,1)S(1)} collective-permute-done((bf16[64,1024]{1,0:T(8,128)(2,1)S(1)}, bf16[64,1024]{1,0:T(8,128)(2,1)S(1)}, u32[]{:S(2)}, u32[]{:S(2)}) %collective-permute-start.15) | collective-permute-done | bytes 131104 | tf_op jit(solution)/shard_map/ppermute | solution.py:50
  55.2 1.8 %partial_adjoint.3 = (f32[128,2048]{1,0:T(8,128)S(1)}, f32[128,2048]{1,0:T(8,128)S(1)}) custom-call(s32[2]{0:T(128)S(1)} %pad_add_fusion.where, bf16[2048,2048]{1,0:T(8,128)(2,1)S(1)} %get-tuple-element.23.tiles, bf16[64,1024]{1,0:T(8,128)(2,1)S(1)} %get-tuple-element.46.refs_0_, bf16[64,1024]{1,0:T(8,128)(2,1)S(1)} %collective-permute-done.13.refs_1_, ...), custom_call_target="tpu_custom_call" | custom-call | flops 1073741824 | bytes 4194304 | tf_op jit(solution)/shard_map/partial_adjoint/pallas_call | solution.py:159
  57.2 2.6 %collective-permute-done.19 = f32[128,2048]{1,0:T(8,128)S(1)} collective-permute-done((f32[128,2048]{1,0:T(8,128)S(1)}, f32[128,2048]{1,0:T(8,128)S(1)}, u32[]{:S(2)}, u32[]{:S(2)}) %collective-permute-start.19) | collective-permute-done | bytes 1048608 | tf_op jit(solution)/shard_map/ppermute | solution.py:18
  59.9 1.3 %collective-permute-start.20 = (bf16[32,2048]{1,0:T(8,128)(2,1)S(1)}, bf16[32,2048]{1,0:T(8,128)(2,1)S(1)}, u32[]{:S(2)}, u32[]{:S(2)}) collective-permute-start(bf16[32,2048]{1,0:T(8,128)(2,1)S(1)} %get-tuple-element.52), channel_id=1, source_target_pairs={{0,8},{4,12},{8,0},{12,4},{16,24},{20,28},{24,16},{28,20},{1,9},{5... | collective-permute-start | bytes 393224 | tf_op jit(solution)/shard_map/ppermute | solution.py:18
  61.2 0.8 %collective-permute-start.22 = (bf16[32,2048]{1,0:T(8,128)(2,1)S(1)}, bf16[32,2048]{1,0:T(8,128)(2,1)S(1)}, u32[]{:S(2)}, u32[]{:S(2)}) collective-permute-start(bf16[32,2048]{1,0:T(8,128)(2,1)S(1)} %get-tuple-element.53), channel_id=1, source_target_pairs={{0,16},{4,20},{8,24},{12,28},{16,0},{20,4},{24,8},{28,12},{1,17},{... | collective-permute-start | bytes 393224 | tf_op jit(solution)/shard_map/ppermute | solution.py:18
  62.0 1.4 %collective-permute-start.21 = (bf16[32,2048]{1,0:T(8,128)(2,1)S(1)}, bf16[32,2048]{1,0:T(8,128)(2,1)S(1)}, u32[]{:S(2)}, u32[]{:S(2)}) collective-permute-start(bf16[32,2048]{1,0:T(8,128)(2,1)S(1)} %get-tuple-element.54), channel_id=1, source_target_pairs={{0,24},{4,28},{8,16},{12,20},{16,8},{20,12},{24,0},{28,4},{1,25},{... | collective-permute-start | bytes 393224 | tf_op jit(solution)/shard_map/ppermute | solution.py:18
  63.5 0.8 %maximum_bitcast_fusion = f32[2048,64]{0,1:T(8,128)} fusion(f32[64,1024]{1,0:T(8,128)S(1)} %get-tuple-element.47, f32[64,1024]{1,0:T(8,128)S(1)} %get-tuple-element.45), kind=kLoop, calls=%fused_computation | loop fusion | flops 131072 | bytes 1048576 | tf_op jit(solution)/shard_map/transpose | solution.py:208
  64.3 1.9 %collective-permute-done.20 = bf16[32,2048]{1,0:T(8,128)(2,1)S(1)} collective-permute-done((bf16[32,2048]{1,0:T(8,128)(2,1)S(1)}, bf16[32,2048]{1,0:T(8,128)(2,1)S(1)}, u32[]{:S(2)}, u32[]{:S(2)}) %collective-permute-start.20) | collective-permute-done | bytes 131104 | tf_op jit(solution)/shard_map/ppermute | solution.py:18
  66.1 1.5 %collective-permute-done.22 = bf16[32,2048]{1,0:T(8,128)(2,1)S(1)} collective-permute-done((bf16[32,2048]{1,0:T(8,128)(2,1)S(1)}, bf16[32,2048]{1,0:T(8,128)(2,1)S(1)}, u32[]{:S(2)}, u32[]{:S(2)}) %collective-permute-start.22) | collective-permute-done | bytes 131104 | tf_op jit(solution)/shard_map/ppermute | solution.py:18
  67.6 1.6 %collective-permute-done.21 = bf16[32,2048]{1,0:T(8,128)(2,1)S(1)} collective-permute-done((bf16[32,2048]{1,0:T(8,128)(2,1)S(1)}, bf16[32,2048]{1,0:T(8,128)(2,1)S(1)}, u32[]{:S(2)}, u32[]{:S(2)}) %collective-permute-start.21) | collective-permute-done | bytes 131104 | tf_op jit(solution)/shard_map/ppermute | solution.py:18
  69.3 0.8 %fusion.12 = f32[2048,32]{0,1:T(8,128)} fusion(f32[128,2048]{1,0:T(8,128)S(1)} %collective-permute-done.19, bf16[32,2048]{1,0:T(8,128)(2,1)S(1)} %collective-permute-done.22, bf16[32,2048]{1,0:T(8,128)(2,1)S(1)} %collective-permute-done.21, bf16[32,2048]{1,0:T(8,128)(2,1)S(1)} %collective-permute-done.20, f32[128,2048]{1,0:T(8,128)S(1)} %get-tuple-element.42), kind=kLoop, calls=%fused_computation.21 | loop fusion | flops 458752 | bytes 1179648 | tf_op jit(solution)/shard_map/transpose | solution.py:208
  (31 shorter events, 2.7 us)
Async XLA Ops:
  0.6 12.9 %copy-start = (bf16[2048,32]{0,1:T(8,128)(2,1)S(1)}, bf16[2048,32]{0,1:T(8,128)(2,1)}, u32[]{:S(2)}) copy-start(bf16[2048,32]{0,1:T(8,128)(2,1)} %param.5) | copy-start | bytes 393220
  0.6 8.8 %collective-permute-start.2 = (bf16[32,2048]{1,0:T(8,128)(2,1)}, bf16[32,2048]{1,0:T(8,128)(2,1)S(1)}, u32[]{:S(2)}, u32[]{:S(2)}) collective-permute-start(bf16[32,2048]{1,0:T(8,128)(2,1)} %bitcast.7), channel_id=1, source_target_pairs={{0,8},{4,12},{8,0},{12,4},{16,24},{20,28},{24,16},{28,20},{1,9},{5... | collective-permute-start | bytes 393224 | tf_op jit(solution)/shard_map/ppermute | solution.py:18
  3.6 8.0 %collective-permute-start.1 = (bf16[32,2048]{1,0:T(8,128)(2,1)}, bf16[32,2048]{1,0:T(8,128)(2,1)S(1)}, u32[]{:S(2)}, u32[]{:S(2)}) collective-permute-start(bf16[32,2048]{1,0:T(8,128)(2,1)} %bitcast.8), channel_id=1, source_target_pairs={{0,16},{4,20},{8,24},{12,28},{16,0},{20,4},{24,8},{28,12},{1,17},{... | collective-permute-start | bytes 393224 | tf_op jit(solution)/shard_map/ppermute | solution.py:18
  5.2 6.5 %collective-permute-start = (bf16[32,2048]{1,0:T(8,128)(2,1)}, bf16[32,2048]{1,0:T(8,128)(2,1)S(1)}, u32[]{:S(2)}, u32[]{:S(2)}) collective-permute-start(bf16[32,2048]{1,0:T(8,128)(2,1)} %bitcast.9), channel_id=1, source_target_pairs={{0,24},{4,28},{8,16},{12,20},{16,8},{20,12},{24,0},{28,4},{1,25},{... | collective-permute-start | bytes 393224 | tf_op jit(solution)/shard_map/ppermute | solution.py:18
  5.2 7.0 %collective-permute-start.3 = (bf16[32,2048]{1,0:T(8,128)(2,1)}, bf16[32,2048]{1,0:T(8,128)(2,1)S(1)}, u32[]{:S(2)}, u32[]{:S(2)}) collective-permute-start(bf16[32,2048]{1,0:T(8,128)(2,1)} %bitcast.10), channel_id=1, source_target_pairs={{0,4},{4,0},{8,12},{12,8},{16,20},{20,16},{24,28},{28,24},{1,5},{5... | collective-permute-start | bytes 393224 | tf_op jit(solution)/shard_map/ppermute | solution.py:18
  11.6 1.3 %collective-permute-start.4 = (bf16[32,2048]{1,0:T(8,128)(2,1)S(1)}, bf16[32,2048]{1,0:T(8,128)(2,1)S(1)}, u32[]{:S(2)}, u32[]{:S(2)}) collective-permute-start(bf16[32,2048]{1,0:T(8,128)(2,1)S(1)} %collective-permute-done.refs_1_), channel_id=1, source_target_pairs={{0,4},{4,0},{8,12},{12,8},{16,20},{20,16},{24,28},{28,24},{1,5},{5... | collective-permute-start | bytes 393224 | tf_op jit(solution)/shard_map/ppermute | solution.py:18
  11.6 1.5 %collective-permute-start.5 = (bf16[32,2048]{1,0:T(8,128)(2,1)S(1)}, bf16[32,2048]{1,0:T(8,128)(2,1)S(1)}, u32[]{:S(2)}, u32[]{:S(2)}) collective-permute-start(bf16[32,2048]{1,0:T(8,128)(2,1)S(1)} %collective-permute-done.1.refs_2_), channel_id=1, source_target_pairs={{0,4},{4,0},{8,12},{12,8},{16,20},{20,16},{24,28},{28,24},{1,5},{5... | collective-permute-start | bytes 393224 | tf_op jit(solution)/shard_map/ppermute | solution.py:18
  12.1 1.3 %collective-permute-start.6 = (bf16[32,2048]{1,0:T(8,128)(2,1)S(1)}, bf16[32,2048]{1,0:T(8,128)(2,1)S(1)}, u32[]{:S(2)}, u32[]{:S(2)}) collective-permute-start(bf16[32,2048]{1,0:T(8,128)(2,1)S(1)} %collective-permute-done.2.refs_3_), channel_id=1, source_target_pairs={{0,4},{4,0},{8,12},{12,8},{16,20},{20,16},{24,28},{28,24},{1,5},{5... | collective-permute-start | bytes 393224 | tf_op jit(solution)/shard_map/ppermute | solution.py:18
  15.4 6.5 %collective-permute-start.7 = (bf16[64,1024]{1,0:T(8,128)(2,1)S(1)}, bf16[64,1024]{1,0:T(8,128)(2,1)S(1)}, u32[]{:S(2)}, u32[]{:S(2)}) collective-permute-start(bf16[64,1024]{1,0:T(8,128)(2,1)S(1)} %get-tuple-element.34), channel_id=1, source_target_pairs={{0,1},{3,2},{2,0},{1,3},{4,5},{7,6},{6,4},{5,7},{8,9},{11,10},{10,... | collective-permute-start | bytes 393224 | tf_op jit(solution)/shard_map/ppermute | solution.py:32
  18.8 8.6 %collective-permute-start.10 = (bf16[64,1024]{1,0:T(8,128)(2,1)S(1)}, bf16[64,1024]{1,0:T(8,128)(2,1)S(1)}, u32[]{:S(2)}, u32[]{:S(2)}) collective-permute-start(bf16[64,1024]{1,0:T(8,128)(2,1)S(1)} %get-tuple-element.40), channel_id=1, source_target_pairs={{0,1},{3,2},{2,0},{1,3},{4,5},{7,6},{6,4},{5,7},{8,9},{11,10},{10,... | collective-permute-start | bytes 393224 | tf_op jit(solution)/shard_map/ppermute | solution.py:32
  22.0 13.2 %collective-permute-start.9 = (bf16[64,1024]{1,0:T(8,128)(2,1)S(1)}, bf16[64,1024]{1,0:T(8,128)(2,1)S(1)}, u32[]{:S(2)}, u32[]{:S(2)}) collective-permute-start(bf16[64,1024]{1,0:T(8,128)(2,1)S(1)} %get-tuple-element.48), channel_id=1, source_target_pairs={{0,3},{1,2},{2,1},{3,0},{4,7},{5,6},{6,5},{7,4},{8,11},{9,10},{10,... | collective-permute-start | bytes 393224 | tf_op jit(solution)/shard_map/ppermute | solution.py:18
  26.3 8.9 %collective-permute-start.8 = (bf16[64,1024]{1,0:T(8,128)(2,1)S(1)}, bf16[64,1024]{1,0:T(8,128)(2,1)S(1)}, u32[]{:S(2)}, u32[]{:S(2)}) collective-permute-start(bf16[64,1024]{1,0:T(8,128)(2,1)S(1)} %get-tuple-element.35), channel_id=1, source_target_pairs={{0,1},{1,0},{2,3},{3,2},{4,5},{5,4},{6,7},{7,6},{8,9},{9,8},{10,11... | collective-permute-start | bytes 393224 | tf_op jit(solution)/shard_map/ppermute | solution.py:18
  27.5 11.2 %collective-permute-start.12 = (bf16[64,1024]{1,0:T(8,128)(2,1)S(1)}, bf16[64,1024]{1,0:T(8,128)(2,1)S(1)}, u32[]{:S(2)}, u32[]{:S(2)}) collective-permute-start(bf16[64,1024]{1,0:T(8,128)(2,1)S(1)} %get-tuple-element.50), channel_id=1, source_target_pairs={{0,3},{1,2},{2,1},{3,0},{4,7},{5,6},{6,5},{7,4},{8,11},{9,10},{10,... | collective-permute-start | bytes 393224 | tf_op jit(solution)/shard_map/ppermute | solution.py:18
  29.1 9.5 %collective-permute-start.11 = (bf16[64,1024]{1,0:T(8,128)(2,1)S(1)}, bf16[64,1024]{1,0:T(8,128)(2,1)S(1)}, u32[]{:S(2)}, u32[]{:S(2)}) collective-permute-start(bf16[64,1024]{1,0:T(8,128)(2,1)S(1)} %get-tuple-element.41), channel_id=1, source_target_pairs={{0,1},{1,0},{2,3},{3,2},{4,5},{5,4},{6,7},{7,6},{8,9},{9,8},{10,11... | collective-permute-start | bytes 393224 | tf_op jit(solution)/shard_map/ppermute | solution.py:18
  35.3 8.3 %collective-permute-start.17 = (bf16[64,1024]{1,0:T(8,128)(2,1)S(1)}, bf16[64,1024]{1,0:T(8,128)(2,1)S(1)}, u32[]{:S(2)}, u32[]{:S(2)}) collective-permute-start(bf16[64,1024]{1,0:T(8,128)(2,1)S(1)} %get-tuple-element.44.refs_0_), channel_id=1, source_target_pairs={{0,3},{1,2},{2,1},{3,0},{4,7},{5,6},{6,5},{7,4},{8,11},{9,10},{10,... | collective-permute-start | bytes 393224 | tf_op jit(solution)/shard_map/ppermute | solution.py:18
  38.7 9.1 %collective-permute-start.14 = (bf16[64,1024]{1,0:T(8,128)(2,1)S(1)}, bf16[64,1024]{1,0:T(8,128)(2,1)S(1)}, u32[]{:S(2)}, u32[]{:S(2)}) collective-permute-start(bf16[64,1024]{1,0:T(8,128)(2,1)S(1)} %get-tuple-element.46.refs_0_), channel_id=1, source_target_pairs={{0,3},{1,2},{2,1},{3,0},{4,7},{5,6},{6,5},{7,4},{8,11},{9,10},{10,... | collective-permute-start | bytes 393224 | tf_op jit(solution)/shard_map/ppermute | solution.py:18
  40.9 10.5 %collective-permute-start.16 = (bf16[64,1024]{1,0:T(8,128)(2,1)S(1)}, bf16[64,1024]{1,0:T(8,128)(2,1)S(1)}, u32[]{:S(2)}, u32[]{:S(2)}) collective-permute-start(bf16[64,1024]{1,0:T(8,128)(2,1)S(1)} %get-tuple-element.44.refs_0_), channel_id=1, source_target_pairs={{0,1},{1,0},{2,3},{3,2},{4,5},{5,4},{6,7},{7,6},{8,9},{9,8},{10,11... | collective-permute-start | bytes 393224 | tf_op jit(solution)/shard_map/ppermute | solution.py:18
  43.6 7.8 %collective-permute-start.18 = (bf16[64,1024]{1,0:T(8,128)(2,1)S(1)}, bf16[64,1024]{1,0:T(8,128)(2,1)S(1)}, u32[]{:S(2)}, u32[]{:S(2)}) collective-permute-start(bf16[64,1024]{1,0:T(8,128)(2,1)S(1)} %select_n.26), channel_id=1, source_target_pairs={{0,2},{3,1},{1,0},{2,3},{4,6},{7,5},{5,4},{6,7},{8,10},{11,9},{9,8... | collective-permute-start | bytes 393224 | tf_op jit(solution)/shard_map/ppermute | solution.py:50
  47.9 5.9 %collective-permute-start.13 = (bf16[64,1024]{1,0:T(8,128)(2,1)S(1)}, bf16[64,1024]{1,0:T(8,128)(2,1)S(1)}, u32[]{:S(2)}, u32[]{:S(2)}) collective-permute-start(bf16[64,1024]{1,0:T(8,128)(2,1)S(1)} %get-tuple-element.46.refs_0_), channel_id=1, source_target_pairs={{0,1},{1,0},{2,3},{3,2},{4,5},{5,4},{6,7},{7,6},{8,9},{9,8},{10,11... | collective-permute-start | bytes 393224 | tf_op jit(solution)/shard_map/ppermute | solution.py:18
  47.9 7.3 %collective-permute-start.15 = (bf16[64,1024]{1,0:T(8,128)(2,1)S(1)}, bf16[64,1024]{1,0:T(8,128)(2,1)S(1)}, u32[]{:S(2)}, u32[]{:S(2)}) collective-permute-start(bf16[64,1024]{1,0:T(8,128)(2,1)S(1)} %select_n.25), channel_id=1, source_target_pairs={{0,2},{3,1},{1,0},{2,3},{4,6},{7,5},{5,4},{6,7},{8,10},{11,9},{9,8... | collective-permute-start | bytes 393224 | tf_op jit(solution)/shard_map/ppermute | solution.py:50
  57.1 2.7 %collective-permute-start.19 = (f32[128,2048]{1,0:T(8,128)S(1)}, f32[128,2048]{1,0:T(8,128)S(1)}, u32[]{:S(2)}, u32[]{:S(2)}) collective-permute-start(f32[128,2048]{1,0:T(8,128)S(1)} %get-tuple-element.43), channel_id=1, source_target_pairs={{0,4},{4,0},{8,12},{12,8},{16,20},{20,16},{24,28},{28,24},{1,5},{5... | collective-permute-start | bytes 3145736 | tf_op jit(solution)/shard_map/ppermute | solution.py:18
  59.9 6.2 %collective-permute-start.20 = (bf16[32,2048]{1,0:T(8,128)(2,1)S(1)}, bf16[32,2048]{1,0:T(8,128)(2,1)S(1)}, u32[]{:S(2)}, u32[]{:S(2)}) collective-permute-start(bf16[32,2048]{1,0:T(8,128)(2,1)S(1)} %get-tuple-element.52), channel_id=1, source_target_pairs={{0,8},{4,12},{8,0},{12,4},{16,24},{20,28},{24,16},{28,20},{1,9},{5... | collective-permute-start | bytes 393224 | tf_op jit(solution)/shard_map/ppermute | solution.py:18
  61.2 6.4 %collective-permute-start.22 = (bf16[32,2048]{1,0:T(8,128)(2,1)S(1)}, bf16[32,2048]{1,0:T(8,128)(2,1)S(1)}, u32[]{:S(2)}, u32[]{:S(2)}) collective-permute-start(bf16[32,2048]{1,0:T(8,128)(2,1)S(1)} %get-tuple-element.53), channel_id=1, source_target_pairs={{0,16},{4,20},{8,24},{12,28},{16,0},{20,4},{24,8},{28,12},{1,17},{... | collective-permute-start | bytes 393224 | tf_op jit(solution)/shard_map/ppermute | solution.py:18
  62.0 7.2 %collective-permute-start.21 = (bf16[32,2048]{1,0:T(8,128)(2,1)S(1)}, bf16[32,2048]{1,0:T(8,128)(2,1)S(1)}, u32[]{:S(2)}, u32[]{:S(2)}) collective-permute-start(bf16[32,2048]{1,0:T(8,128)(2,1)S(1)} %get-tuple-element.54), channel_id=1, source_target_pairs={{0,24},{4,28},{8,16},{12,20},{16,8},{20,12},{24,0},{28,4},{1,25},{... | collective-permute-start | bytes 393224 | tf_op jit(solution)/shard_map/ppermute | solution.py:18

commit v13 on v12

--- a/solution.py
+++ b/solution.py
@@ -91,15 +91,17 @@
 
 
 def sketch_kernel(where, tiles, token, *refs, base, offsets_row, offsets_col):
-    blocks, outs, ends, probes = refs[: len(offsets_row)], refs[len(offsets_row) : -2], refs[-2], refs[-1]
-    own = blocks[0].shape[0]
+    count = len(refs) - 2 - len(offsets_col)
+    blocks, outs, ends, probes = refs[:count], refs[count:-2], refs[-2], refs[-1]
+    own = probes.shape[0] // len(offsets_row)
     ratio = len(offsets_row) // len(offsets_col)
     share = own * ratio
     ends[...] = jnp.full(ends.shape, at_end(where, len(offsets_col)).astype(F32))
-    for offset, ref in zip(offsets_row, blocks):
+    pieces = [(ref, at) for ref in blocks for at in range(0, ref.shape[0], own)]
+    for offset, (ref, at) in zip(offsets_row, pieces):
         column = where[0] ^ offset
         start = (lax.div(column, ratio) ^ where[1]) * share + lax.rem(column, ratio) * own
-        probes[pl.ds(pl.multiple_of(start, own), own), :] = ref[...]
+        probes[pl.ds(pl.multiple_of(start, own), own), :] = ref[at : at + own, :]
     for step in range(ends.shape[1] // STEP):
         rows, at = slice(base + step * STEP, base + (step + 1) * STEP), slice(step * STEP, (step + 1) * STEP)
         term = lax.dot_general(probes[...], tiles[rows, :], (((1,), (1,)), ((), ())), preferred_element_type=F32)
@@ -185,9 +187,9 @@
 
     own = probes.T
     held = [own] + [exchange(own, "row", offset) for offset in gather_core[1:]]
-    twin = exchange(own, "row", 1)
     held, token = lax.optimization_barrier((held, token))
-    blocks = held + [twin] + [exchange(block, "row", 1) for block in held[1:]]
+    held = jnp.concatenate(held)
+    blocks = [held, exchange(held, "row", 1)]
 
     totals, shares = [], []
     for chunk in range(chunks):

time: 70.2 us -> 70.3 us (level)
  waiting for transfers between devices: 24.5 us -> 25.3 us
    ppermute x19 -> x16, waiting for transfers between devices: 21.7 us -> 22.4 us  [exchange(): return lax.ppermute(value, axis, [(i, i ^ offset) for i in range(size)])]
    ppermute x19 -> x16, starting transfers between devices: 19 us -> 18.3 us  [exchange(): return lax.ppermute(value, axis, [(i, i ^ offset) for i in range(size)])]
  transfers between devices with their start and end apart: 23 -> 20, of which waited for: 15 -> 13; matrix products, arithmetic and copies ran while one was open for 2% -> 2% of each run, Pallas kernels for 11% -> 11%
where the time goes in v13:
time: 70.3 us; the launch traced here: 70.2 us
  starting transfers between devices  30.3 us (43%)
  waiting for transfers between devices  25.3 us (36%)
  Pallas kernels  11.5 us (16%)
  other arithmetic  2.22 us (3%)
  between operations  0.77 us (1%)
    ppermute x16, waiting for transfers between devices, exchange(): return lax.ppermute(value, axis, [(i, i ^ offset) for i in range(size)])  22.4 us
    ppermute x16, starting transfers between devices, exchange(): return lax.ppermute(value, axis, [(i, i ^ offset) for i in range(size)])  18.3 us
    ppermute x2, starting transfers between devices, window_spread(): lax.ppermute(onward, 'col', [(0, 2), (3, 1), (1, 0), (2, 3)])  7.74 us
    ppermute x2, starting transfers between devices, window_sums(): came = lax.ppermute(terms[2], 'col', [(0, 1), (3, 2), (2, 0), (1, 3)])  4.26 us
    pallas_call x1, Pallas kernels, masked(): pl.pallas_call(functools.partial(mask_kernel, block=rows // mask.shape[0]...  4.11 us
    pallas_call x2, Pallas kernels, partial_sketch(): pl.pallas_call(functools.partial(sketch_kernel, base=chunk * rows, offset...  3.71 us
    pallas_call x2, Pallas kernels, partial_adjoint(): pl.pallas_call(functools.partial(adjoint_kernel, base=chunk * rows, parts...  3.68 us
    transpose x2, other arithmetic, local(): return (jnp.concatenate(totals, axis=1).T, adjoint.T)  1.61 us
  transfers between devices with their start and end apart: 20, of which 13 were waited for; matrix products, arithmetic and copies ran while one was open for 2% of the time, Pallas kernels for 11%

profile of v13, /device:TPU:0, one launch (start us, length us, event | category | flops | bytes accessed | tf_op | source)
XLA Modules:
  0.0 70.2 jit_solution(1966747343599163020)
XLA Ops:
  0.6 3.0 %collective-permute-start.2 = (bf16[32,2048]{1,0:T(8,128)(2,1)}, bf16[32,2048]{1,0:T(8,128)(2,1)S(1)}, u32[]{:S(2)}, u32[]{:S(2)}) collective-permute-start(bf16[32,2048]{1,0:T(8,128)(2,1)} %bitcast.7), channel_id=1, source_target_pairs={{0,8},{4,12},{8,0},{12,4},{16,24},{20,28},{24,16},{28,20},{1,9},{5... | collective-permute-start | bytes 393224 | tf_op jit(solution)/shard_map/ppermute | solution.py:18
  3.6 1.5 %collective-permute-start.1 = (bf16[32,2048]{1,0:T(8,128)(2,1)}, bf16[32,2048]{1,0:T(8,128)(2,1)S(1)}, u32[]{:S(2)}, u32[]{:S(2)}) collective-permute-start(bf16[32,2048]{1,0:T(8,128)(2,1)} %bitcast.8), channel_id=1, source_target_pairs={{0,16},{4,20},{8,24},{12,28},{16,0},{20,4},{24,8},{28,12},{1,17},{... | collective-permute-start | bytes 393224 | tf_op jit(solution)/shard_map/ppermute | solution.py:18
  5.3 4.1 %masked_tiles.1 = (bf16[2048,2048]{1,0:T(8,128)(2,1)S(1)}, f32[8,128]{1,0:T(8,128)S(1)}) custom-call(s32[2]{0:T(128)S(1)} %pad_add_fusion.where, s32[8,8]{1,0:T(8,128)} %mask_hbm.1, bf16[2048,2048]{1,0:T(8,128)(2,1)} %green_ref.1), custom_call_target="tpu_custom_call" | custom-call | bytes 8388608 | tf_op jit(solution)/shard_map/masked_tiles/pallas_call | solution.py:77
  9.4 2.2 %collective-permute-done.1 = bf16[32,2048]{1,0:T(8,128)(2,1)S(1)} collective-permute-done((bf16[32,2048]{1,0:T(8,128)(2,1)}, bf16[32,2048]{1,0:T(8,128)(2,1)S(1)}, u32[]{:S(2)}, u32[]{:S(2)}) %collective-permute-start.1) | collective-permute-done | bytes 131104 | tf_op jit(solution)/shard_map/ppermute | solution.py:18
  11.8 1.9 %collective-permute-done.3.refs_1_ = bf16[128,2048]{1,0:T(8,128)(2,1)S(1)} collective-permute-done((bf16[128,2048]{1,0:T(8,128)(2,1)S(1)}, bf16[128,2048]{1,0:T(8,128)(2,1)S(1)}, u32[]{:S(2)}, u32[]{:S(2)}) %collective-permute-start.3) | collective-permute-done | bytes 524320 | tf_op jit(solution)/shard_map/ppermute | solution.py:18
  13.7 1.9 %partial_sketch.2 = (f32[64,1024]{1,0:T(8,128)S(1)}, bf16[64,1024]{1,0:T(8,128)(2,1)S(1)}, bf16[64,1024]{1,0:T(8,128)(2,1)S(1)}, f32[64,1024]{1,0:T(8,128)S(1)}, f32[64,1024]{1,0:T(8,128)S(1)}) custom-call(s32[2]{0:T(128)S(1)} %pad_add_fusion.where, bf16[2048,2048]{1,0:T(8,128)(2,1)S(1)} %get-tuple-element.23.tiles, f32[8,128]{1,0:T(8,128)S(1)} %get-tuple-element.25.token, ...), custom_call_target="tpu_custom_call" | custom-call | flops 1073741824 | bytes 4194304 | tf_op jit(solution)/shard_map/partial_sketch/pallas_call | solution.py:121
  15.6 1.6 %collective-permute-start.4 = (bf16[64,1024]{1,0:T(8,128)(2,1)S(1)}, bf16[64,1024]{1,0:T(8,128)(2,1)S(1)}, u32[]{:S(2)}, u32[]{:S(2)}) collective-permute-start(bf16[64,1024]{1,0:T(8,128)(2,1)S(1)} %get-tuple-element.34), channel_id=1, source_target_pairs={{0,1},{3,2},{2,0},{1,3},{4,5},{7,6},{6,4},{5,7},{8,9},{11,10},{10,... | collective-permute-start | bytes 393224 | tf_op jit(solution)/shard_map/ppermute | solution.py:32
  17.2 1.9 %partial_sketch.3 = (f32[64,1024]{1,0:T(8,128)S(1)}, bf16[64,1024]{1,0:T(8,128)(2,1)S(1)}, bf16[64,1024]{1,0:T(8,128)(2,1)S(1)}, f32[64,1024]{1,0:T(8,128)S(1)}, f32[64,1024]{1,0:T(8,128)S(1)}) custom-call(s32[2]{0:T(128)S(1)} %pad_add_fusion.where, bf16[2048,2048]{1,0:T(8,128)(2,1)S(1)} %get-tuple-element.23.tiles, f32[8,128]{1,0:T(8,128)S(1)} %get-tuple-element.25.token, ...), custom_call_target="tpu_custom_call" | custom-call | flops 1073741824 | bytes 4194304 | tf_op jit(solution)/shard_map/partial_sketch/pallas_call | solution.py:121
  19.0 2.6 %collective-permute-start.7 = (bf16[64,1024]{1,0:T(8,128)(2,1)S(1)}, bf16[64,1024]{1,0:T(8,128)(2,1)S(1)}, u32[]{:S(2)}, u32[]{:S(2)}) collective-permute-start(bf16[64,1024]{1,0:T(8,128)(2,1)S(1)} %get-tuple-element.40), channel_id=1, source_target_pairs={{0,1},{3,2},{2,0},{1,3},{4,5},{7,6},{6,4},{5,7},{8,9},{11,10},{10,... | collective-permute-start | bytes 393224 | tf_op jit(solution)/shard_map/ppermute | solution.py:32
  22.1 4.4 %collective-permute-start.6 = (bf16[64,1024]{1,0:T(8,128)(2,1)S(1)}, bf16[64,1024]{1,0:T(8,128)(2,1)S(1)}, u32[]{:S(2)}, u32[]{:S(2)}) collective-permute-start(bf16[64,1024]{1,0:T(8,128)(2,1)S(1)} %get-tuple-element.48), channel_id=1, source_target_pairs={{0,3},{1,2},{2,1},{3,0},{4,7},{5,6},{6,5},{7,4},{8,11},{9,10},{10,... | collective-permute-start | bytes 393224 | tf_op jit(solution)/shard_map/ppermute | solution.py:18
  26.5 1.2 %collective-permute-done.7 = bf16[64,1024]{1,0:T(8,128)(2,1)S(1)} collective-permute-done((bf16[64,1024]{1,0:T(8,128)(2,1)S(1)}, bf16[64,1024]{1,0:T(8,128)(2,1)S(1)}, u32[]{:S(2)}, u32[]{:S(2)}) %collective-permute-start.7) | collective-permute-done | bytes 131104 | tf_op jit(solution)/shard_map/ppermute | solution.py:32
  27.7 1.6 %collective-permute-start.9 = (bf16[64,1024]{1,0:T(8,128)(2,1)S(1)}, bf16[64,1024]{1,0:T(8,128)(2,1)S(1)}, u32[]{:S(2)}, u32[]{:S(2)}) collective-permute-start(bf16[64,1024]{1,0:T(8,128)(2,1)S(1)} %get-tuple-element.50), channel_id=1, source_target_pairs={{0,3},{1,2},{2,1},{3,0},{4,7},{5,6},{6,5},{7,4},{8,11},{9,10},{10,... | collective-permute-start | bytes 393224 | tf_op jit(solution)/shard_map/ppermute | solution.py:18
  29.3 6.0 %collective-permute-done.5 = bf16[64,1024]{1,0:T(8,128)(2,1)S(1)} collective-permute-done((bf16[64,1024]{1,0:T(8,128)(2,1)S(1)}, bf16[64,1024]{1,0:T(8,128)(2,1)S(1)}, u32[]{:S(2)}, u32[]{:S(2)}) %collective-permute-start.5) | collective-permute-done | bytes 131104 | tf_op jit(solution)/shard_map/ppermute | solution.py:18
  35.4 1.5 %collective-permute-start.14 = (bf16[64,1024]{1,0:T(8,128)(2,1)S(1)}, bf16[64,1024]{1,0:T(8,128)(2,1)S(1)}, u32[]{:S(2)}, u32[]{:S(2)}) collective-permute-start(bf16[64,1024]{1,0:T(8,128)(2,1)S(1)} %get-tuple-element.44.refs_0_), channel_id=1, source_target_pairs={{0,3},{1,2},{2,1},{3,0},{4,7},{5,6},{6,5},{7,4},{8,11},{9,10},{10,... | collective-permute-start | bytes 393224 | tf_op jit(solution)/shard_map/ppermute | solution.py:18
  36.9 1.9 %collective-permute-done.8 = bf16[64,1024]{1,0:T(8,128)(2,1)S(1)} collective-permute-done((bf16[64,1024]{1,0:T(8,128)(2,1)S(1)}, bf16[64,1024]{1,0:T(8,128)(2,1)S(1)}, u32[]{:S(2)}, u32[]{:S(2)}) %collective-permute-start.8) | collective-permute-done | bytes 131104 | tf_op jit(solution)/shard_map/ppermute | solution.py:18
  38.9 2.2 %collective-permute-start.11 = (bf16[64,1024]{1,0:T(8,128)(2,1)S(1)}, bf16[64,1024]{1,0:T(8,128)(2,1)S(1)}, u32[]{:S(2)}, u32[]{:S(2)}) collective-permute-start(bf16[64,1024]{1,0:T(8,128)(2,1)S(1)} %get-tuple-element.46.refs_0_), channel_id=1, source_target_pairs={{0,3},{1,2},{2,1},{3,0},{4,7},{5,6},{6,5},{7,4},{8,11},{9,10},{10,... | collective-permute-start | bytes 393224 | tf_op jit(solution)/shard_map/ppermute | solution.py:18
  41.6 2.1 %collective-permute-done.14.refs_3_ = bf16[64,1024]{1,0:T(8,128)(2,1)S(1)} collective-permute-done((bf16[64,1024]{1,0:T(8,128)(2,1)S(1)}, bf16[64,1024]{1,0:T(8,128)(2,1)S(1)}, u32[]{:S(2)}, u32[]{:S(2)}) %collective-permute-start.14) | collective-permute-done | bytes 131104 | tf_op jit(solution)/shard_map/ppermute | solution.py:18
  43.7 4.3 %collective-permute-start.15 = (bf16[64,1024]{1,0:T(8,128)(2,1)S(1)}, bf16[64,1024]{1,0:T(8,128)(2,1)S(1)}, u32[]{:S(2)}, u32[]{:S(2)}) collective-permute-start(bf16[64,1024]{1,0:T(8,128)(2,1)S(1)} %select_n.26), channel_id=1, source_target_pairs={{0,2},{3,1},{1,0},{2,3},{4,6},{7,5},{5,4},{6,7},{8,10},{11,9},{9,8... | collective-permute-start | bytes 393224 | tf_op jit(solution)/shard_map/ppermute | solution.py:50
  48.1 3.5 %collective-permute-start.12 = (bf16[64,1024]{1,0:T(8,128)(2,1)S(1)}, bf16[64,1024]{1,0:T(8,128)(2,1)S(1)}, u32[]{:S(2)}, u32[]{:S(2)}) collective-permute-start(bf16[64,1024]{1,0:T(8,128)(2,1)S(1)} %select_n.25), channel_id=1, source_target_pairs={{0,2},{3,1},{1,0},{2,3},{4,6},{7,5},{5,4},{6,7},{8,10},{11,9},{9,8... | collective-permute-start | bytes 393224 | tf_op jit(solution)/shard_map/ppermute | solution.py:50
  51.5 1.8 %partial_adjoint.2.refs_4_ = f32[256,2048]{1,0:T(8,128)S(1)} custom-call(s32[2]{0:T(128)S(1)} %pad_add_fusion.where, bf16[2048,2048]{1,0:T(8,128)(2,1)S(1)} %get-tuple-element.23.tiles, bf16[64,1024]{1,0:T(8,128)(2,1)S(1)} %get-tuple-element.44.refs_0_, bf16[64,1024]{1,0:T(8,128)(2,1)S(1)} %collective-permute-done.13.refs_1_, ...), custom_call_target="tpu_custom_call" | custom-call | flops 1073741824 | bytes 4194304 | tf_op jit(solution)/shard_map/partial_adjoint/pallas_call | solution.py:161
  53.4 0.6 collective-permute-done.10.refs_1_
  54.0 1.4 %collective-permute-done.12.refs_2_ = bf16[64,1024]{1,0:T(8,128)(2,1)S(1)} collective-permute-done((bf16[64,1024]{1,0:T(8,128)(2,1)S(1)}, bf16[64,1024]{1,0:T(8,128)(2,1)S(1)}, u32[]{:S(2)}, u32[]{:S(2)}) %collective-permute-start.12) | collective-permute-done | bytes 131104 | tf_op jit(solution)/shard_map/ppermute | solution.py:50
  55.4 1.8 %partial_adjoint.3 = (f32[128,2048]{1,0:T(8,128)S(1)}, f32[128,2048]{1,0:T(8,128)S(1)}) custom-call(s32[2]{0:T(128)S(1)} %pad_add_fusion.where, bf16[2048,2048]{1,0:T(8,128)(2,1)S(1)} %get-tuple-element.23.tiles, bf16[64,1024]{1,0:T(8,128)(2,1)S(1)} %get-tuple-element.46.refs_0_, bf16[64,1024]{1,0:T(8,128)(2,1)S(1)} %collective-permute-done.10.refs_1_, ...), custom_call_target="tpu_custom_call" | custom-call | flops 1073741824 | bytes 4194304 | tf_op jit(solution)/shard_map/partial_adjoint/pallas_call | solution.py:161
  57.3 2.6 %collective-permute-done.16 = f32[128,2048]{1,0:T(8,128)S(1)} collective-permute-done((f32[128,2048]{1,0:T(8,128)S(1)}, f32[128,2048]{1,0:T(8,128)S(1)}, u32[]{:S(2)}, u32[]{:S(2)}) %collective-permute-start.16) | collective-permute-done | bytes 1048608 | tf_op jit(solution)/shard_map/ppermute | solution.py:18
  60.0 1.3 %collective-permute-start.17 = (bf16[32,2048]{1,0:T(8,128)(2,1)S(1)}, bf16[32,2048]{1,0:T(8,128)(2,1)S(1)}, u32[]{:S(2)}, u32[]{:S(2)}) collective-permute-start(bf16[32,2048]{1,0:T(8,128)(2,1)S(1)} %get-tuple-element.52), channel_id=1, source_target_pairs={{0,8},{4,12},{8,0},{12,4},{16,24},{20,28},{24,16},{28,20},{1,9},{5... | collective-permute-start | bytes 393224 | tf_op jit(solution)/shard_map/ppermute | solution.py:18
  61.3 0.8 %collective-permute-start.19 = (bf16[32,2048]{1,0:T(8,128)(2,1)S(1)}, bf16[32,2048]{1,0:T(8,128)(2,1)S(1)}, u32[]{:S(2)}, u32[]{:S(2)}) collective-permute-start(bf16[32,2048]{1,0:T(8,128)(2,1)S(1)} %get-tuple-element.53), channel_id=1, source_target_pairs={{0,16},{4,20},{8,24},{12,28},{16,0},{20,4},{24,8},{28,12},{1,17},{... | collective-permute-start | bytes 393224 | tf_op jit(solution)/shard_map/ppermute | solution.py:18
  62.2 1.4 %collective-permute-start.18 = (bf16[32,2048]{1,0:T(8,128)(2,1)S(1)}, bf16[32,2048]{1,0:T(8,128)(2,1)S(1)}, u32[]{:S(2)}, u32[]{:S(2)}) collective-permute-start(bf16[32,2048]{1,0:T(8,128)(2,1)S(1)} %get-tuple-element.54), channel_id=1, source_target_pairs={{0,24},{4,28},{8,16},{12,20},{16,8},{20,12},{24,0},{28,4},{1,25},{... | collective-permute-start | bytes 393224 | tf_op jit(solution)/shard_map/ppermute | solution.py:18
  63.6 0.8 %maximum_bitcast_fusion = f32[2048,64]{0,1:T(8,128)} fusion(f32[64,1024]{1,0:T(8,128)S(1)} %get-tuple-element.47, f32[64,1024]{1,0:T(8,128)S(1)} %get-tuple-element.45), kind=kLoop, calls=%fused_computation | loop fusion | flops 131072 | bytes 1048576 | tf_op jit(solution)/shard_map/transpose | solution.py:210
  64.4 1.9 %collective-permute-done.17 = bf16[32,2048]{1,0:T(8,128)(2,1)S(1)} collective-permute-done((bf16[32,2048]{1,0:T(8,128)(2,1)S(1)}, bf16[32,2048]{1,0:T(8,128)(2,1)S(1)}, u32[]{:S(2)}, u32[]{:S(2)}) %collective-permute-start.17) | collective-permute-done | bytes 131104 | tf_op jit(solution)/shard_map/ppermute | solution.py:18
  66.3 1.5 %collective-permute-done.19 = bf16[32,2048]{1,0:T(8,128)(2,1)S(1)} collective-permute-done((bf16[32,2048]{1,0:T(8,128)(2,1)S(1)}, bf16[32,2048]{1,0:T(8,128)(2,1)S(1)}, u32[]{:S(2)}, u32[]{:S(2)}) %collective-permute-start.19) | collective-permute-done | bytes 131104 | tf_op jit(solution)/shard_map/ppermute | solution.py:18
  67.8 1.6 %collective-permute-done.18 = bf16[32,2048]{1,0:T(8,128)(2,1)S(1)} collective-permute-done((bf16[32,2048]{1,0:T(8,128)(2,1)S(1)}, bf16[32,2048]{1,0:T(8,128)(2,1)S(1)}, u32[]{:S(2)}, u32[]{:S(2)}) %collective-permute-start.18) | collective-permute-done | bytes 131104 | tf_op jit(solution)/shard_map/ppermute | solution.py:18
  69.4 0.8 %fusion.12 = f32[2048,32]{0,1:T(8,128)} fusion(f32[128,2048]{1,0:T(8,128)S(1)} %collective-permute-done.16, bf16[32,2048]{1,0:T(8,128)(2,1)S(1)} %collective-permute-done.19, bf16[32,2048]{1,0:T(8,128)(2,1)S(1)} %collective-permute-done.18, bf16[32,2048]{1,0:T(8,128)(2,1)S(1)} %collective-permute-done.17, f32[128,2048]{1,0:T(8,128)S(1)} %get-tuple-element.42), kind=kLoop, calls=%fused_computation.21 | loop fusion | flops 458752 | bytes 1179648 | tf_op jit(solution)/shard_map/transpose | solution.py:210
  (29 shorter events, 1.8 us)
Async XLA Ops:
  0.6 11.0 %copy-start = (bf16[2048,32]{0,1:T(8,128)(2,1)S(1)}, bf16[2048,32]{0,1:T(8,128)(2,1)}, u32[]{:S(2)}) copy-start(bf16[2048,32]{0,1:T(8,128)(2,1)} %param.5) | copy-start | bytes 393220
  0.6 8.7 %collective-permute-start.2 = (bf16[32,2048]{1,0:T(8,128)(2,1)}, bf16[32,2048]{1,0:T(8,128)(2,1)S(1)}, u32[]{:S(2)}, u32[]{:S(2)}) collective-permute-start(bf16[32,2048]{1,0:T(8,128)(2,1)} %bitcast.7), channel_id=1, source_target_pairs={{0,8},{4,12},{8,0},{12,4},{16,24},{20,28},{24,16},{28,20},{1,9},{5... | collective-permute-start | bytes 393224 | tf_op jit(solution)/shard_map/ppermute | solution.py:18
  3.6 8.0 %collective-permute-start.1 = (bf16[32,2048]{1,0:T(8,128)(2,1)}, bf16[32,2048]{1,0:T(8,128)(2,1)S(1)}, u32[]{:S(2)}, u32[]{:S(2)}) collective-permute-start(bf16[32,2048]{1,0:T(8,128)(2,1)} %bitcast.8), channel_id=1, source_target_pairs={{0,16},{4,20},{8,24},{12,28},{16,0},{20,4},{24,8},{28,12},{1,17},{... | collective-permute-start | bytes 393224 | tf_op jit(solution)/shard_map/ppermute | solution.py:18
  5.2 6.5 %collective-permute-start = (bf16[32,2048]{1,0:T(8,128)(2,1)}, bf16[32,2048]{1,0:T(8,128)(2,1)S(1)}, u32[]{:S(2)}, u32[]{:S(2)}) collective-permute-start(bf16[32,2048]{1,0:T(8,128)(2,1)} %bitcast.9), channel_id=1, source_target_pairs={{0,24},{4,28},{8,16},{12,20},{16,8},{20,12},{24,0},{28,4},{1,25},{... | collective-permute-start | bytes 393224 | tf_op jit(solution)/shard_map/ppermute | solution.py:18
  11.7 2.0 %collective-permute-start.3 = (bf16[128,2048]{1,0:T(8,128)(2,1)S(1)}, bf16[128,2048]{1,0:T(8,128)(2,1)S(1)}, u32[]{:S(2)}, u32[]{:S(2)}) collective-permute-start(bf16[128,2048]{1,0:T(8,128)(2,1)S(1)} %constant_dynamic-update-slice_fusion.refs_0_), channel_id=1, source_target_pairs={{0,4},{4,0},{8,12},{12,8},{16,20},{20,16},{24,28},{28,24},{1,5},{5... | collective-permute-start | bytes 1572872 | tf_op jit(solution)/shard_map/ppermute | solution.py:18
  15.6 6.5 %collective-permute-start.4 = (bf16[64,1024]{1,0:T(8,128)(2,1)S(1)}, bf16[64,1024]{1,0:T(8,128)(2,1)S(1)}, u32[]{:S(2)}, u32[]{:S(2)}) collective-permute-start(bf16[64,1024]{1,0:T(8,128)(2,1)S(1)} %get-tuple-element.34), channel_id=1, source_target_pairs={{0,1},{3,2},{2,0},{1,3},{4,5},{7,6},{6,4},{5,7},{8,9},{11,10},{10,... | collective-permute-start | bytes 393224 | tf_op jit(solution)/shard_map/ppermute | solution.py:32
  19.0 8.6 %collective-permute-start.7 = (bf16[64,1024]{1,0:T(8,128)(2,1)S(1)}, bf16[64,1024]{1,0:T(8,128)(2,1)S(1)}, u32[]{:S(2)}, u32[]{:S(2)}) collective-permute-start(bf16[64,1024]{1,0:T(8,128)(2,1)S(1)} %get-tuple-element.40), channel_id=1, source_target_pairs={{0,1},{3,2},{2,0},{1,3},{4,5},{7,6},{6,4},{5,7},{8,9},{11,10},{10,... | collective-permute-start | bytes 393224 | tf_op jit(solution)/shard_map/ppermute | solution.py:32
  22.1 13.2 %collective-permute-start.6 = (bf16[64,1024]{1,0:T(8,128)(2,1)S(1)}, bf16[64,1024]{1,0:T(8,128)(2,1)S(1)}, u32[]{:S(2)}, u32[]{:S(2)}) collective-permute-start(bf16[64,1024]{1,0:T(8,128)(2,1)S(1)} %get-tuple-element.48), channel_id=1, source_target_pairs={{0,3},{1,2},{2,1},{3,0},{4,7},{5,6},{6,5},{7,4},{8,11},{9,10},{10,... | collective-permute-start | bytes 393224 | tf_op jit(solution)/shard_map/ppermute | solution.py:18
  26.5 8.9 %collective-permute-start.5 = (bf16[64,1024]{1,0:T(8,128)(2,1)S(1)}, bf16[64,1024]{1,0:T(8,128)(2,1)S(1)}, u32[]{:S(2)}, u32[]{:S(2)}) collective-permute-start(bf16[64,1024]{1,0:T(8,128)(2,1)S(1)} %get-tuple-element.35), channel_id=1, source_target_pairs={{0,1},{1,0},{2,3},{3,2},{4,5},{5,4},{6,7},{7,6},{8,9},{9,8},{10,11... | collective-permute-start | bytes 393224 | tf_op jit(solution)/shard_map/ppermute | solution.py:18
  27.7 11.1 %collective-permute-start.9 = (bf16[64,1024]{1,0:T(8,128)(2,1)S(1)}, bf16[64,1024]{1,0:T(8,128)(2,1)S(1)}, u32[]{:S(2)}, u32[]{:S(2)}) collective-permute-start(bf16[64,1024]{1,0:T(8,128)(2,1)S(1)} %get-tuple-element.50), channel_id=1, source_target_pairs={{0,3},{1,2},{2,1},{3,0},{4,7},{5,6},{6,5},{7,4},{8,11},{9,10},{10,... | collective-permute-start | bytes 393224 | tf_op jit(solution)/shard_map/ppermute | solution.py:18
  29.3 9.5 %collective-permute-start.8 = (bf16[64,1024]{1,0:T(8,128)(2,1)S(1)}, bf16[64,1024]{1,0:T(8,128)(2,1)S(1)}, u32[]{:S(2)}, u32[]{:S(2)}) collective-permute-start(bf16[64,1024]{1,0:T(8,128)(2,1)S(1)} %get-tuple-element.41), channel_id=1, source_target_pairs={{0,1},{1,0},{2,3},{3,2},{4,5},{5,4},{6,7},{7,6},{8,9},{9,8},{10,11... | collective-permute-start | bytes 393224 | tf_op jit(solution)/shard_map/ppermute | solution.py:18
  35.4 8.2 %collective-permute-start.14 = (bf16[64,1024]{1,0:T(8,128)(2,1)S(1)}, bf16[64,1024]{1,0:T(8,128)(2,1)S(1)}, u32[]{:S(2)}, u32[]{:S(2)}) collective-permute-start(bf16[64,1024]{1,0:T(8,128)(2,1)S(1)} %get-tuple-element.44.refs_0_), channel_id=1, source_target_pairs={{0,3},{1,2},{2,1},{3,0},{4,7},{5,6},{6,5},{7,4},{8,11},{9,10},{10,... | collective-permute-start | bytes 393224 | tf_op jit(solution)/shard_map/ppermute | solution.py:18
  38.9 9.1 %collective-permute-start.11 = (bf16[64,1024]{1,0:T(8,128)(2,1)S(1)}, bf16[64,1024]{1,0:T(8,128)(2,1)S(1)}, u32[]{:S(2)}, u32[]{:S(2)}) collective-permute-start(bf16[64,1024]{1,0:T(8,128)(2,1)S(1)} %get-tuple-element.46.refs_0_), channel_id=1, source_target_pairs={{0,3},{1,2},{2,1},{3,0},{4,7},{5,6},{6,5},{7,4},{8,11},{9,10},{10,... | collective-permute-start | bytes 393224 | tf_op jit(solution)/shard_map/ppermute | solution.py:18
  41.0 10.5 %collective-permute-start.13 = (bf16[64,1024]{1,0:T(8,128)(2,1)S(1)}, bf16[64,1024]{1,0:T(8,128)(2,1)S(1)}, u32[]{:S(2)}, u32[]{:S(2)}) collective-permute-start(bf16[64,1024]{1,0:T(8,128)(2,1)S(1)} %get-tuple-element.44.refs_0_), channel_id=1, source_target_pairs={{0,1},{1,0},{2,3},{3,2},{4,5},{5,4},{6,7},{7,6},{8,9},{9,8},{10,11... | collective-permute-start | bytes 393224 | tf_op jit(solution)/shard_map/ppermute | solution.py:18
  43.7 7.8 %collective-permute-start.15 = (bf16[64,1024]{1,0:T(8,128)(2,1)S(1)}, bf16[64,1024]{1,0:T(8,128)(2,1)S(1)}, u32[]{:S(2)}, u32[]{:S(2)}) collective-permute-start(bf16[64,1024]{1,0:T(8,128)(2,1)S(1)} %select_n.26), channel_id=1, source_target_pairs={{0,2},{3,1},{1,0},{2,3},{4,6},{7,5},{5,4},{6,7},{8,10},{11,9},{9,8... | collective-permute-start | bytes 393224 | tf_op jit(solution)/shard_map/ppermute | solution.py:50
  48.0 6.0 %collective-permute-start.10 = (bf16[64,1024]{1,0:T(8,128)(2,1)S(1)}, bf16[64,1024]{1,0:T(8,128)(2,1)S(1)}, u32[]{:S(2)}, u32[]{:S(2)}) collective-permute-start(bf16[64,1024]{1,0:T(8,128)(2,1)S(1)} %get-tuple-element.46.refs_0_), channel_id=1, source_target_pairs={{0,1},{1,0},{2,3},{3,2},{4,5},{5,4},{6,7},{7,6},{8,9},{9,8},{10,11... | collective-permute-start | bytes 393224 | tf_op jit(solution)/shard_map/ppermute | solution.py:18
  48.1 7.3 %collective-permute-start.12 = (bf16[64,1024]{1,0:T(8,128)(2,1)S(1)}, bf16[64,1024]{1,0:T(8,128)(2,1)S(1)}, u32[]{:S(2)}, u32[]{:S(2)}) collective-permute-start(bf16[64,1024]{1,0:T(8,128)(2,1)S(1)} %select_n.25), channel_id=1, source_target_pairs={{0,2},{3,1},{1,0},{2,3},{4,6},{7,5},{5,4},{6,7},{8,10},{11,9},{9,8... | collective-permute-start | bytes 393224 | tf_op jit(solution)/shard_map/ppermute | solution.py:50
  57.2 2.7 %collective-permute-start.16 = (f32[128,2048]{1,0:T(8,128)S(1)}, f32[128,2048]{1,0:T(8,128)S(1)}, u32[]{:S(2)}, u32[]{:S(2)}) collective-permute-start(f32[128,2048]{1,0:T(8,128)S(1)} %get-tuple-element.43), channel_id=1, source_target_pairs={{0,4},{4,0},{8,12},{12,8},{16,20},{20,16},{24,28},{28,24},{1,5},{5... | collective-permute-start | bytes 3145736 | tf_op jit(solution)/shard_map/ppermute | solution.py:18
  60.0 6.3 %collective-permute-start.17 = (bf16[32,2048]{1,0:T(8,128)(2,1)S(1)}, bf16[32,2048]{1,0:T(8,128)(2,1)S(1)}, u32[]{:S(2)}, u32[]{:S(2)}) collective-permute-start(bf16[32,2048]{1,0:T(8,128)(2,1)S(1)} %get-tuple-element.52), channel_id=1, source_target_pairs={{0,8},{4,12},{8,0},{12,4},{16,24},{20,28},{24,16},{28,20},{1,9},{5... | collective-permute-start | bytes 393224 | tf_op jit(solution)/shard_map/ppermute | solution.py:18
  61.3 6.5 %collective-permute-start.19 = (bf16[32,2048]{1,0:T(8,128)(2,1)S(1)}, bf16[32,2048]{1,0:T(8,128)(2,1)S(1)}, u32[]{:S(2)}, u32[]{:S(2)}) collective-permute-start(bf16[32,2048]{1,0:T(8,128)(2,1)S(1)} %get-tuple-element.53), channel_id=1, source_target_pairs={{0,16},{4,20},{8,24},{12,28},{16,0},{20,4},{24,8},{28,12},{1,17},{... | collective-permute-start | bytes 393224 | tf_op jit(solution)/shard_map/ppermute | solution.py:18
  62.2 7.2 %collective-permute-start.18 = (bf16[32,2048]{1,0:T(8,128)(2,1)S(1)}, bf16[32,2048]{1,0:T(8,128)(2,1)S(1)}, u32[]{:S(2)}, u32[]{:S(2)}) collective-permute-start(bf16[32,2048]{1,0:T(8,128)(2,1)S(1)} %get-tuple-element.54), channel_id=1, source_target_pairs={{0,24},{4,28},{8,16},{12,20},{16,8},{20,12},{24,0},{28,4},{1,25},{... | collective-permute-start | bytes 393224 | tf_op jit(solution)/shard_map/ppermute | solution.py:18

commit v14 on v12

--- a/solution.py
+++ b/solution.py
@@ -166,7 +166,7 @@
         scratch_shapes=[pltpu.VMEM((width, rows), BF16)],
         compiler_params=pltpu.CompilerParams(vmem_limit_bytes=VMEM_LIMIT),
         cost_estimate=pl.CostEstimate(
-            flops=2 * width * cols * rows, bytes_accessed=2 * rows * cols, transcendentals=0
+            flops=0, bytes_accessed=0, transcendentals=0
         ),
         name="partial_adjoint",
     )(where, tiles, *shares, *earlier)

time: 70.2 us -> 70.4 us (level)
  starting transfers between devices: 31 us -> 32.1 us
  waiting for transfers between devices: 24.5 us -> 23.6 us
    ppermute x19, waiting for transfers between devices: 21.7 us -> 19.7 us  [exchange(): return lax.ppermute(value, axis, [(i, i ^ offset) for i in range(size)])]
    ppermute x19, starting transfers between devices: 19 us -> 20.4 us  [exchange(): return lax.ppermute(value, axis, [(i, i ^ offset) for i in range(size)])]
    ppermute x2, waiting for transfers between devices: 1.41 us -> 2.43 us  [window_spread(): lax.ppermute(onward, 'col', [(0, 2), (3, 1), (1, 0), (2, 3)])]
  transfers between devices with their start and end apart: 23 -> 23, of which waited for: 15 -> 14; matrix products, arithmetic and copies ran while one was open for 2% -> 2% of each run, Pallas kernels for 11% -> 11%
where the time goes in v14:
time: 70.4 us; the launch traced here: 70.3 us
  starting transfers between devices  32.1 us (46%)
  waiting for transfers between devices  23.6 us (34%)
  Pallas kernels  11.5 us (16%)
  other arithmetic  2.22 us (3%)
  between operations  0.75 us (1%)
    ppermute x19, starting transfers between devices, exchange(): return lax.ppermute(value, axis, [(i, i ^ offset) for i in range(size)])  20.4 us
    ppermute x19, waiting for transfers between devices, exchange(): return lax.ppermute(value, axis, [(i, i ^ offset) for i in range(size)])  19.7 us
    ppermute x2, starting transfers between devices, window_spread(): lax.ppermute(onward, 'col', [(0, 2), (3, 1), (1, 0), (2, 3)])  7.46 us
    ppermute x2, starting transfers between devices, window_sums(): came = lax.ppermute(terms[2], 'col', [(0, 1), (3, 2), (2, 0), (1, 3)])  4.26 us
    pallas_call x1, Pallas kernels, masked(): pl.pallas_call(functools.partial(mask_kernel, block=rows // mask.shape[0]...  4.15 us
    pallas_call x2, Pallas kernels, partial_sketch(): pl.pallas_call(functools.partial(sketch_kernel, base=chunk * rows, offset...  3.71 us
    pallas_call x2, Pallas kernels, partial_adjoint(): pl.pallas_call(functools.partial(adjoint_kernel, base=chunk * rows, parts...  3.68 us
    ppermute x2, waiting for transfers between devices, window_spread(): lax.ppermute(onward, 'col', [(0, 2), (3, 1), (1, 0), (2, 3)])  2.43 us
  transfers between devices with their start and end apart: 23, of which 14 were waited for; matrix products, arithmetic and copies ran while one was open for 2% of the time, Pallas kernels for 11%

profile of v14, /device:TPU:0, one launch (start us, length us, event | category | flops | bytes accessed | tf_op | source)
XLA Modules:
  0.0 70.3 jit_solution(16531592962898980199)
XLA Ops:
  0.6 3.0 %collective-permute-start.2 = (bf16[32,2048]{1,0:T(8,128)(2,1)}, bf16[32,2048]{1,0:T(8,128)(2,1)S(1)}, u32[]{:S(2)}, u32[]{:S(2)}) collective-permute-start(bf16[32,2048]{1,0:T(8,128)(2,1)} %bitcast.7), channel_id=1, source_target_pairs={{0,8},{4,12},{8,0},{12,4},{16,24},{20,28},{24,16},{28,20},{1,9},{5... | collective-permute-start | bytes 393224 | tf_op jit(solution)/shard_map/ppermute | solution.py:18
  3.6 1.5 %collective-permute-start.1 = (bf16[32,2048]{1,0:T(8,128)(2,1)}, bf16[32,2048]{1,0:T(8,128)(2,1)S(1)}, u32[]{:S(2)}, u32[]{:S(2)}) collective-permute-start(bf16[32,2048]{1,0:T(8,128)(2,1)} %bitcast.8), channel_id=1, source_target_pairs={{0,16},{4,20},{8,24},{12,28},{16,0},{20,4},{24,8},{28,12},{1,17},{... | collective-permute-start | bytes 393224 | tf_op jit(solution)/shard_map/ppermute | solution.py:18
  5.3 4.1 %masked_tiles.1 = (bf16[2048,2048]{1,0:T(8,128)(2,1)S(1)}, f32[8,128]{1,0:T(8,128)S(1)}) custom-call(s32[2]{0:T(128)S(1)} %pad_add_fusion.where, s32[8,8]{1,0:T(8,128)} %mask_hbm.1, bf16[2048,2048]{1,0:T(8,128)(2,1)} %green_ref.1), custom_call_target="tpu_custom_call" | custom-call | bytes 8388608 | tf_op jit(solution)/shard_map/masked_tiles/pallas_call | solution.py:77
  9.4 2.2 %collective-permute-done.1.refs_2_ = bf16[32,2048]{1,0:T(8,128)(2,1)S(1)} collective-permute-done((bf16[32,2048]{1,0:T(8,128)(2,1)}, bf16[32,2048]{1,0:T(8,128)(2,1)S(1)}, u32[]{:S(2)}, u32[]{:S(2)}) %collective-permute-start.1) | collective-permute-done | bytes 131104 | tf_op jit(solution)/shard_map/ppermute | solution.py:18
  12.2 0.8 %collective-permute-done.4.refs_5_ = bf16[32,2048]{1,0:T(8,128)(2,1)S(1)} collective-permute-done((bf16[32,2048]{1,0:T(8,128)(2,1)S(1)}, bf16[32,2048]{1,0:T(8,128)(2,1)S(1)}, u32[]{:S(2)}, u32[]{:S(2)}) %collective-permute-start.4) | collective-permute-done | bytes 131104 | tf_op jit(solution)/shard_map/ppermute | solution.py:18
  13.5 1.9 %partial_sketch.2 = (f32[64,1024]{1,0:T(8,128)S(1)}, bf16[64,1024]{1,0:T(8,128)(2,1)S(1)}, bf16[64,1024]{1,0:T(8,128)(2,1)S(1)}, f32[64,1024]{1,0:T(8,128)S(1)}, f32[64,1024]{1,0:T(8,128)S(1)}) custom-call(s32[2]{0:T(128)S(1)} %pad_add_fusion.where, bf16[2048,2048]{1,0:T(8,128)(2,1)S(1)} %get-tuple-element.23.tiles, f32[8,128]{1,0:T(8,128)S(1)} %get-tuple-element.25.token, ...), custom_call_target="tpu_custom_call" | custom-call | flops 1073741824 | bytes 4194304 | tf_op jit(solution)/shard_map/partial_sketch/pallas_call | solution.py:119
  15.4 1.6 %collective-permute-start.7 = (bf16[64,1024]{1,0:T(8,128)(2,1)S(1)}, bf16[64,1024]{1,0:T(8,128)(2,1)S(1)}, u32[]{:S(2)}, u32[]{:S(2)}) collective-permute-start(bf16[64,1024]{1,0:T(8,128)(2,1)S(1)} %get-tuple-element.34), channel_id=1, source_target_pairs={{0,1},{3,2},{2,0},{1,3},{4,5},{7,6},{6,4},{5,7},{8,9},{11,10},{10,... | collective-permute-start | bytes 393224 | tf_op jit(solution)/shard_map/ppermute | solution.py:32
  17.0 1.9 %partial_sketch.3 = (f32[64,1024]{1,0:T(8,128)S(1)}, bf16[64,1024]{1,0:T(8,128)(2,1)S(1)}, bf16[64,1024]{1,0:T(8,128)(2,1)S(1)}, f32[64,1024]{1,0:T(8,128)S(1)}, f32[64,1024]{1,0:T(8,128)S(1)}) custom-call(s32[2]{0:T(128)S(1)} %pad_add_fusion.where, bf16[2048,2048]{1,0:T(8,128)(2,1)S(1)} %get-tuple-element.23.tiles, f32[8,128]{1,0:T(8,128)S(1)} %get-tuple-element.25.token, ...), custom_call_target="tpu_custom_call" | custom-call | flops 1073741824 | bytes 4194304 | tf_op jit(solution)/shard_map/partial_sketch/pallas_call | solution.py:119
  18.8 2.6 %collective-permute-start.10 = (bf16[64,1024]{1,0:T(8,128)(2,1)S(1)}, bf16[64,1024]{1,0:T(8,128)(2,1)S(1)}, u32[]{:S(2)}, u32[]{:S(2)}) collective-permute-start(bf16[64,1024]{1,0:T(8,128)(2,1)S(1)} %get-tuple-element.40), channel_id=1, source_target_pairs={{0,1},{3,2},{2,0},{1,3},{4,5},{7,6},{6,4},{5,7},{8,9},{11,10},{10,... | collective-permute-start | bytes 393224 | tf_op jit(solution)/shard_map/ppermute | solution.py:32
  22.0 4.4 %collective-permute-start.9 = (bf16[64,1024]{1,0:T(8,128)(2,1)S(1)}, bf16[64,1024]{1,0:T(8,128)(2,1)S(1)}, u32[]{:S(2)}, u32[]{:S(2)}) collective-permute-start(bf16[64,1024]{1,0:T(8,128)(2,1)S(1)} %get-tuple-element.48), channel_id=1, source_target_pairs={{0,3},{1,2},{2,1},{3,0},{4,7},{5,6},{6,5},{7,4},{8,11},{9,10},{10,... | collective-permute-start | bytes 393224 | tf_op jit(solution)/shard_map/ppermute | solution.py:18
  26.3 1.1 %collective-permute-done.10 = bf16[64,1024]{1,0:T(8,128)(2,1)S(1)} collective-permute-done((bf16[64,1024]{1,0:T(8,128)(2,1)S(1)}, bf16[64,1024]{1,0:T(8,128)(2,1)S(1)}, u32[]{:S(2)}, u32[]{:S(2)}) %collective-permute-start.10) | collective-permute-done | bytes 131104 | tf_op jit(solution)/shard_map/ppermute | solution.py:32
  27.5 1.7 %collective-permute-start.12 = (bf16[64,1024]{1,0:T(8,128)(2,1)S(1)}, bf16[64,1024]{1,0:T(8,128)(2,1)S(1)}, u32[]{:S(2)}, u32[]{:S(2)}) collective-permute-start(bf16[64,1024]{1,0:T(8,128)(2,1)S(1)} %get-tuple-element.50), channel_id=1, source_target_pairs={{0,3},{1,2},{2,1},{3,0},{4,7},{5,6},{6,5},{7,4},{8,11},{9,10},{10,... | collective-permute-start | bytes 393224 | tf_op jit(solution)/shard_map/ppermute | solution.py:18
  29.1 6.0 %collective-permute-done.8 = bf16[64,1024]{1,0:T(8,128)(2,1)S(1)} collective-permute-done((bf16[64,1024]{1,0:T(8,128)(2,1)S(1)}, bf16[64,1024]{1,0:T(8,128)(2,1)S(1)}, u32[]{:S(2)}, u32[]{:S(2)}) %collective-permute-start.8) | collective-permute-done | bytes 131104 | tf_op jit(solution)/shard_map/ppermute | solution.py:18
  35.3 1.5 %collective-permute-start.17 = (bf16[64,1024]{1,0:T(8,128)(2,1)S(1)}, bf16[64,1024]{1,0:T(8,128)(2,1)S(1)}, u32[]{:S(2)}, u32[]{:S(2)}) collective-permute-start(bf16[64,1024]{1,0:T(8,128)(2,1)S(1)} %get-tuple-element.44.refs_0_), channel_id=1, source_target_pairs={{0,3},{1,2},{2,1},{3,0},{4,7},{5,6},{6,5},{7,4},{8,11},{9,10},{10,... | collective-permute-start | bytes 393224 | tf_op jit(solution)/shard_map/ppermute | solution.py:18
  36.8 1.8 %collective-permute-done.11 = bf16[64,1024]{1,0:T(8,128)(2,1)S(1)} collective-permute-done((bf16[64,1024]{1,0:T(8,128)(2,1)S(1)}, bf16[64,1024]{1,0:T(8,128)(2,1)S(1)}, u32[]{:S(2)}, u32[]{:S(2)}) %collective-permute-start.11) | collective-permute-done | bytes 131104 | tf_op jit(solution)/shard_map/ppermute | solution.py:18
  38.7 2.1 %collective-permute-start.14 = (bf16[64,1024]{1,0:T(8,128)(2,1)S(1)}, bf16[64,1024]{1,0:T(8,128)(2,1)S(1)}, u32[]{:S(2)}, u32[]{:S(2)}) collective-permute-start(bf16[64,1024]{1,0:T(8,128)(2,1)S(1)} %get-tuple-element.46.refs_0_), channel_id=1, source_target_pairs={{0,3},{1,2},{2,1},{3,0},{4,7},{5,6},{6,5},{7,4},{8,11},{9,10},{10,... | collective-permute-start | bytes 393224 | tf_op jit(solution)/shard_map/ppermute | solution.py:18
  41.5 1.4 %collective-permute-start.13 = (bf16[64,1024]{1,0:T(8,128)(2,1)S(1)}, bf16[64,1024]{1,0:T(8,128)(2,1)S(1)}, u32[]{:S(2)}, u32[]{:S(2)}) collective-permute-start(bf16[64,1024]{1,0:T(8,128)(2,1)S(1)} %get-tuple-element.46.refs_0_), channel_id=1, source_target_pairs={{0,1},{1,0},{2,3},{3,2},{4,5},{5,4},{6,7},{7,6},{8,9},{9,8},{10,11... | collective-permute-start | bytes 393224 | tf_op jit(solution)/shard_map/ppermute | solution.py:18
  42.9 0.6 collective-permute-done.17.refs_3_
  43.6 3.8 %collective-permute-start.18 = (bf16[64,1024]{1,0:T(8,128)(2,1)S(1)}, bf16[64,1024]{1,0:T(8,128)(2,1)S(1)}, u32[]{:S(2)}, u32[]{:S(2)}) collective-permute-start(bf16[64,1024]{1,0:T(8,128)(2,1)S(1)} %select_n.26), channel_id=1, source_target_pairs={{0,2},{3,1},{1,0},{2,3},{4,6},{7,5},{5,4},{6,7},{8,10},{11,9},{9,8... | collective-permute-start | bytes 393224 | tf_op jit(solution)/shard_map/ppermute | solution.py:50
  47.5 3.6 %collective-permute-start.15 = (bf16[64,1024]{1,0:T(8,128)(2,1)S(1)}, bf16[64,1024]{1,0:T(8,128)(2,1)S(1)}, u32[]{:S(2)}, u32[]{:S(2)}) collective-permute-start(bf16[64,1024]{1,0:T(8,128)(2,1)S(1)} %select_n.25), channel_id=1, source_target_pairs={{0,2},{3,1},{1,0},{2,3},{4,6},{7,5},{5,4},{6,7},{8,10},{11,9},{9,8... | collective-permute-start | bytes 393224 | tf_op jit(solution)/shard_map/ppermute | solution.py:50
  51.1 2.4 %collective-permute-done.18.refs_2_ = bf16[64,1024]{1,0:T(8,128)(2,1)S(1)} collective-permute-done((bf16[64,1024]{1,0:T(8,128)(2,1)S(1)}, bf16[64,1024]{1,0:T(8,128)(2,1)S(1)}, u32[]{:S(2)}, u32[]{:S(2)}) %collective-permute-start.18) | collective-permute-done | bytes 131104 | tf_op jit(solution)/shard_map/ppermute | solution.py:50
  53.5 1.8 %partial_adjoint.2.refs_4_ = f32[256,2048]{1,0:T(8,128)S(1)} custom-call(s32[2]{0:T(128)S(1)} %pad_add_fusion.where, bf16[2048,2048]{1,0:T(8,128)(2,1)S(1)} %get-tuple-element.23.tiles, bf16[64,1024]{1,0:T(8,128)(2,1)S(1)} %get-tuple-element.44.refs_0_, bf16[64,1024]{1,0:T(8,128)(2,1)S(1)} %collective-permute-done.16.refs_1_, ...), custom_call_target="tpu_custom_call" | custom-call | tf_op jit(solution)/shard_map/partial_adjoint/pallas_call | solution.py:159
  55.4 1.9 %partial_adjoint.3 = (f32[128,2048]{1,0:T(8,128)S(1)}, f32[128,2048]{1,0:T(8,128)S(1)}) custom-call(s32[2]{0:T(128)S(1)} %pad_add_fusion.where, bf16[2048,2048]{1,0:T(8,128)(2,1)S(1)} %get-tuple-element.23.tiles, bf16[64,1024]{1,0:T(8,128)(2,1)S(1)} %get-tuple-element.46.refs_0_, bf16[64,1024]{1,0:T(8,128)(2,1)S(1)} %collective-permute-done.13.refs_1_, ...), custom_call_target="tpu_custom_call" | custom-call | tf_op jit(solution)/shard_map/partial_adjoint/pallas_call | solution.py:159
  57.3 2.6 %collective-permute-done.19 = f32[128,2048]{1,0:T(8,128)S(1)} collective-permute-done((f32[128,2048]{1,0:T(8,128)S(1)}, f32[128,2048]{1,0:T(8,128)S(1)}, u32[]{:S(2)}, u32[]{:S(2)}) %collective-permute-start.19) | collective-permute-done | bytes 1048608 | tf_op jit(solution)/shard_map/ppermute | solution.py:18
  60.1 1.3 %collective-permute-start.20 = (bf16[32,2048]{1,0:T(8,128)(2,1)S(1)}, bf16[32,2048]{1,0:T(8,128)(2,1)S(1)}, u32[]{:S(2)}, u32[]{:S(2)}) collective-permute-start(bf16[32,2048]{1,0:T(8,128)(2,1)S(1)} %get-tuple-element.52), channel_id=1, source_target_pairs={{0,8},{4,12},{8,0},{12,4},{16,24},{20,28},{24,16},{28,20},{1,9},{5... | collective-permute-start | bytes 393224 | tf_op jit(solution)/shard_map/ppermute | solution.py:18
  61.4 0.9 %collective-permute-start.22 = (bf16[32,2048]{1,0:T(8,128)(2,1)S(1)}, bf16[32,2048]{1,0:T(8,128)(2,1)S(1)}, u32[]{:S(2)}, u32[]{:S(2)}) collective-permute-start(bf16[32,2048]{1,0:T(8,128)(2,1)S(1)} %get-tuple-element.53), channel_id=1, source_target_pairs={{0,16},{4,20},{8,24},{12,28},{16,0},{20,4},{24,8},{28,12},{1,17},{... | collective-permute-start | bytes 393224 | tf_op jit(solution)/shard_map/ppermute | solution.py:18
  62.2 1.4 %collective-permute-start.21 = (bf16[32,2048]{1,0:T(8,128)(2,1)S(1)}, bf16[32,2048]{1,0:T(8,128)(2,1)S(1)}, u32[]{:S(2)}, u32[]{:S(2)}) collective-permute-start(bf16[32,2048]{1,0:T(8,128)(2,1)S(1)} %get-tuple-element.54), channel_id=1, source_target_pairs={{0,24},{4,28},{8,16},{12,20},{16,8},{20,12},{24,0},{28,4},{1,25},{... | collective-permute-start | bytes 393224 | tf_op jit(solution)/shard_map/ppermute | solution.py:18
  63.6 0.8 %maximum_bitcast_fusion = f32[2048,64]{0,1:T(8,128)} fusion(f32[64,1024]{1,0:T(8,128)S(1)} %get-tuple-element.47, f32[64,1024]{1,0:T(8,128)S(1)} %get-tuple-element.45), kind=kLoop, calls=%fused_computation | loop fusion | flops 131072 | bytes 1048576 | tf_op jit(solution)/shard_map/transpose | solution.py:208
  64.5 1.9 %collective-permute-done.20 = bf16[32,2048]{1,0:T(8,128)(2,1)S(1)} collective-permute-done((bf16[32,2048]{1,0:T(8,128)(2,1)S(1)}, bf16[32,2048]{1,0:T(8,128)(2,1)S(1)}, u32[]{:S(2)}, u32[]{:S(2)}) %collective-permute-start.20) | collective-permute-done | bytes 131104 | tf_op jit(solution)/shard_map/ppermute | solution.py:18
  66.4 1.5 %collective-permute-done.22 = bf16[32,2048]{1,0:T(8,128)(2,1)S(1)} collective-permute-done((bf16[32,2048]{1,0:T(8,128)(2,1)S(1)}, bf16[32,2048]{1,0:T(8,128)(2,1)S(1)}, u32[]{:S(2)}, u32[]{:S(2)}) %collective-permute-start.22) | collective-permute-done | bytes 131104 | tf_op jit(solution)/shard_map/ppermute | solution.py:18
  67.8 1.6 %collective-permute-done.21 = bf16[32,2048]{1,0:T(8,128)(2,1)S(1)} collective-permute-done((bf16[32,2048]{1,0:T(8,128)(2,1)S(1)}, bf16[32,2048]{1,0:T(8,128)(2,1)S(1)}, u32[]{:S(2)}, u32[]{:S(2)}) %collective-permute-start.21) | collective-permute-done | bytes 131104 | tf_op jit(solution)/shard_map/ppermute | solution.py:18
  69.5 0.8 %fusion.12 = f32[2048,32]{0,1:T(8,128)} fusion(f32[128,2048]{1,0:T(8,128)S(1)} %collective-permute-done.19, bf16[32,2048]{1,0:T(8,128)(2,1)S(1)} %collective-permute-done.22, bf16[32,2048]{1,0:T(8,128)(2,1)S(1)} %collective-permute-done.21, bf16[32,2048]{1,0:T(8,128)(2,1)S(1)} %collective-permute-done.20, f32[128,2048]{1,0:T(8,128)S(1)} %get-tuple-element.42), kind=kLoop, calls=%fused_computation.21 | loop fusion | flops 458752 | bytes 1179648 | tf_op jit(solution)/shard_map/transpose | solution.py:208
  (31 shorter events, 2.8 us)
Async XLA Ops:
  0.6 12.9 %copy-start = (bf16[2048,32]{0,1:T(8,128)(2,1)S(1)}, bf16[2048,32]{0,1:T(8,128)(2,1)}, u32[]{:S(2)}) copy-start(bf16[2048,32]{0,1:T(8,128)(2,1)} %param.5) | copy-start | bytes 393220
  0.6 8.8 %collective-permute-start.2 = (bf16[32,2048]{1,0:T(8,128)(2,1)}, bf16[32,2048]{1,0:T(8,128)(2,1)S(1)}, u32[]{:S(2)}, u32[]{:S(2)}) collective-permute-start(bf16[32,2048]{1,0:T(8,128)(2,1)} %bitcast.7), channel_id=1, source_target_pairs={{0,8},{4,12},{8,0},{12,4},{16,24},{20,28},{24,16},{28,20},{1,9},{5... | collective-permute-start | bytes 393224 | tf_op jit(solution)/shard_map/ppermute | solution.py:18
  3.6 8.0 %collective-permute-start.1 = (bf16[32,2048]{1,0:T(8,128)(2,1)}, bf16[32,2048]{1,0:T(8,128)(2,1)S(1)}, u32[]{:S(2)}, u32[]{:S(2)}) collective-permute-start(bf16[32,2048]{1,0:T(8,128)(2,1)} %bitcast.8), channel_id=1, source_target_pairs={{0,16},{4,20},{8,24},{12,28},{16,0},{20,4},{24,8},{28,12},{1,17},{... | collective-permute-start | bytes 393224 | tf_op jit(solution)/shard_map/ppermute | solution.py:18
  5.2 6.5 %collective-permute-start = (bf16[32,2048]{1,0:T(8,128)(2,1)}, bf16[32,2048]{1,0:T(8,128)(2,1)S(1)}, u32[]{:S(2)}, u32[]{:S(2)}) collective-permute-start(bf16[32,2048]{1,0:T(8,128)(2,1)} %bitcast.9), channel_id=1, source_target_pairs={{0,24},{4,28},{8,16},{12,20},{16,8},{20,12},{24,0},{28,4},{1,25},{... | collective-permute-start | bytes 393224 | tf_op jit(solution)/shard_map/ppermute | solution.py:18
  5.2 7.0 %collective-permute-start.3 = (bf16[32,2048]{1,0:T(8,128)(2,1)}, bf16[32,2048]{1,0:T(8,128)(2,1)S(1)}, u32[]{:S(2)}, u32[]{:S(2)}) collective-permute-start(bf16[32,2048]{1,0:T(8,128)(2,1)} %bitcast.10), channel_id=1, source_target_pairs={{0,4},{4,0},{8,12},{12,8},{16,20},{20,16},{24,28},{28,24},{1,5},{5... | collective-permute-start | bytes 393224 | tf_op jit(solution)/shard_map/ppermute | solution.py:18
  11.6 1.3 %collective-permute-start.4 = (bf16[32,2048]{1,0:T(8,128)(2,1)S(1)}, bf16[32,2048]{1,0:T(8,128)(2,1)S(1)}, u32[]{:S(2)}, u32[]{:S(2)}) collective-permute-start(bf16[32,2048]{1,0:T(8,128)(2,1)S(1)} %collective-permute-done.refs_1_), channel_id=1, source_target_pairs={{0,4},{4,0},{8,12},{12,8},{16,20},{20,16},{24,28},{28,24},{1,5},{5... | collective-permute-start | bytes 393224 | tf_op jit(solution)/shard_map/ppermute | solution.py:18
  11.6 1.5 %collective-permute-start.5 = (bf16[32,2048]{1,0:T(8,128)(2,1)S(1)}, bf16[32,2048]{1,0:T(8,128)(2,1)S(1)}, u32[]{:S(2)}, u32[]{:S(2)}) collective-permute-start(bf16[32,2048]{1,0:T(8,128)(2,1)S(1)} %collective-permute-done.1.refs_2_), channel_id=1, source_target_pairs={{0,4},{4,0},{8,12},{12,8},{16,20},{20,16},{24,28},{28,24},{1,5},{5... | collective-permute-start | bytes 393224 | tf_op jit(solution)/shard_map/ppermute | solution.py:18
  12.1 1.3 %collective-permute-start.6 = (bf16[32,2048]{1,0:T(8,128)(2,1)S(1)}, bf16[32,2048]{1,0:T(8,128)(2,1)S(1)}, u32[]{:S(2)}, u32[]{:S(2)}) collective-permute-start(bf16[32,2048]{1,0:T(8,128)(2,1)S(1)} %collective-permute-done.2.refs_3_), channel_id=1, source_target_pairs={{0,4},{4,0},{8,12},{12,8},{16,20},{20,16},{24,28},{28,24},{1,5},{5... | collective-permute-start | bytes 393224 | tf_op jit(solution)/shard_map/ppermute | solution.py:18
  15.4 6.5 %collective-permute-start.7 = (bf16[64,1024]{1,0:T(8,128)(2,1)S(1)}, bf16[64,1024]{1,0:T(8,128)(2,1)S(1)}, u32[]{:S(2)}, u32[]{:S(2)}) collective-permute-start(bf16[64,1024]{1,0:T(8,128)(2,1)S(1)} %get-tuple-element.34), channel_id=1, source_target_pairs={{0,1},{3,2},{2,0},{1,3},{4,5},{7,6},{6,4},{5,7},{8,9},{11,10},{10,... | collective-permute-start | bytes 393224 | tf_op jit(solution)/shard_map/ppermute | solution.py:32
  18.8 8.6 %collective-permute-start.10 = (bf16[64,1024]{1,0:T(8,128)(2,1)S(1)}, bf16[64,1024]{1,0:T(8,128)(2,1)S(1)}, u32[]{:S(2)}, u32[]{:S(2)}) collective-permute-start(bf16[64,1024]{1,0:T(8,128)(2,1)S(1)} %get-tuple-element.40), channel_id=1, source_target_pairs={{0,1},{3,2},{2,0},{1,3},{4,5},{7,6},{6,4},{5,7},{8,9},{11,10},{10,... | collective-permute-start | bytes 393224 | tf_op jit(solution)/shard_map/ppermute | solution.py:32
  22.0 13.2 %collective-permute-start.9 = (bf16[64,1024]{1,0:T(8,128)(2,1)S(1)}, bf16[64,1024]{1,0:T(8,128)(2,1)S(1)}, u32[]{:S(2)}, u32[]{:S(2)}) collective-permute-start(bf16[64,1024]{1,0:T(8,128)(2,1)S(1)} %get-tuple-element.48), channel_id=1, source_target_pairs={{0,3},{1,2},{2,1},{3,0},{4,7},{5,6},{6,5},{7,4},{8,11},{9,10},{10,... | collective-permute-start | bytes 393224 | tf_op jit(solution)/shard_map/ppermute | solution.py:18
  26.3 8.9 %collective-permute-start.8 = (bf16[64,1024]{1,0:T(8,128)(2,1)S(1)}, bf16[64,1024]{1,0:T(8,128)(2,1)S(1)}, u32[]{:S(2)}, u32[]{:S(2)}) collective-permute-start(bf16[64,1024]{1,0:T(8,128)(2,1)S(1)} %get-tuple-element.35), channel_id=1, source_target_pairs={{0,1},{1,0},{2,3},{3,2},{4,5},{5,4},{6,7},{7,6},{8,9},{9,8},{10,11... | collective-permute-start | bytes 393224 | tf_op jit(solution)/shard_map/ppermute | solution.py:18
  27.5 11.2 %collective-permute-start.12 = (bf16[64,1024]{1,0:T(8,128)(2,1)S(1)}, bf16[64,1024]{1,0:T(8,128)(2,1)S(1)}, u32[]{:S(2)}, u32[]{:S(2)}) collective-permute-start(bf16[64,1024]{1,0:T(8,128)(2,1)S(1)} %get-tuple-element.50), channel_id=1, source_target_pairs={{0,3},{1,2},{2,1},{3,0},{4,7},{5,6},{6,5},{7,4},{8,11},{9,10},{10,... | collective-permute-start | bytes 393224 | tf_op jit(solution)/shard_map/ppermute | solution.py:18
  29.1 9.5 %collective-permute-start.11 = (bf16[64,1024]{1,0:T(8,128)(2,1)S(1)}, bf16[64,1024]{1,0:T(8,128)(2,1)S(1)}, u32[]{:S(2)}, u32[]{:S(2)}) collective-permute-start(bf16[64,1024]{1,0:T(8,128)(2,1)S(1)} %get-tuple-element.41), channel_id=1, source_target_pairs={{0,1},{1,0},{2,3},{3,2},{4,5},{5,4},{6,7},{7,6},{8,9},{9,8},{10,11... | collective-permute-start | bytes 393224 | tf_op jit(solution)/shard_map/ppermute | solution.py:18
  35.3 8.3 %collective-permute-start.17 = (bf16[64,1024]{1,0:T(8,128)(2,1)S(1)}, bf16[64,1024]{1,0:T(8,128)(2,1)S(1)}, u32[]{:S(2)}, u32[]{:S(2)}) collective-permute-start(bf16[64,1024]{1,0:T(8,128)(2,1)S(1)} %get-tuple-element.44.refs_0_), channel_id=1, source_target_pairs={{0,3},{1,2},{2,1},{3,0},{4,7},{5,6},{6,5},{7,4},{8,11},{9,10},{10,... | collective-permute-start | bytes 393224 | tf_op jit(solution)/shard_map/ppermute | solution.py:18
  38.7 8.7 %collective-permute-start.14 = (bf16[64,1024]{1,0:T(8,128)(2,1)S(1)}, bf16[64,1024]{1,0:T(8,128)(2,1)S(1)}, u32[]{:S(2)}, u32[]{:S(2)}) collective-permute-start(bf16[64,1024]{1,0:T(8,128)(2,1)S(1)} %get-tuple-element.46.refs_0_), channel_id=1, source_target_pairs={{0,3},{1,2},{2,1},{3,0},{4,7},{5,6},{6,5},{7,4},{8,11},{9,10},{10,... | collective-permute-start | bytes 393224 | tf_op jit(solution)/shard_map/ppermute | solution.py:18
  40.9 10.2 %collective-permute-start.16 = (bf16[64,1024]{1,0:T(8,128)(2,1)S(1)}, bf16[64,1024]{1,0:T(8,128)(2,1)S(1)}, u32[]{:S(2)}, u32[]{:S(2)}) collective-permute-start(bf16[64,1024]{1,0:T(8,128)(2,1)S(1)} %get-tuple-element.44.refs_0_), channel_id=1, source_target_pairs={{0,1},{1,0},{2,3},{3,2},{4,5},{5,4},{6,7},{7,6},{8,9},{9,8},{10,11... | collective-permute-start | bytes 393224 | tf_op jit(solution)/shard_map/ppermute | solution.py:18
  41.5 13.9 %collective-permute-start.13 = (bf16[64,1024]{1,0:T(8,128)(2,1)S(1)}, bf16[64,1024]{1,0:T(8,128)(2,1)S(1)}, u32[]{:S(2)}, u32[]{:S(2)}) collective-permute-start(bf16[64,1024]{1,0:T(8,128)(2,1)S(1)} %get-tuple-element.46.refs_0_), channel_id=1, source_target_pairs={{0,1},{1,0},{2,3},{3,2},{4,5},{5,4},{6,7},{7,6},{8,9},{9,8},{10,11... | collective-permute-start | bytes 393224 | tf_op jit(solution)/shard_map/ppermute | solution.py:18
  43.6 9.9 %collective-permute-start.18 = (bf16[64,1024]{1,0:T(8,128)(2,1)S(1)}, bf16[64,1024]{1,0:T(8,128)(2,1)S(1)}, u32[]{:S(2)}, u32[]{:S(2)}) collective-permute-start(bf16[64,1024]{1,0:T(8,128)(2,1)S(1)} %select_n.26), channel_id=1, source_target_pairs={{0,2},{3,1},{1,0},{2,3},{4,6},{7,5},{5,4},{6,7},{8,10},{11,9},{9,8... | collective-permute-start | bytes 393224 | tf_op jit(solution)/shard_map/ppermute | solution.py:50
  47.5 7.9 %collective-permute-start.15 = (bf16[64,1024]{1,0:T(8,128)(2,1)S(1)}, bf16[64,1024]{1,0:T(8,128)(2,1)S(1)}, u32[]{:S(2)}, u32[]{:S(2)}) collective-permute-start(bf16[64,1024]{1,0:T(8,128)(2,1)S(1)} %select_n.25), channel_id=1, source_target_pairs={{0,2},{3,1},{1,0},{2,3},{4,6},{7,5},{5,4},{6,7},{8,10},{11,9},{9,8... | collective-permute-start | bytes 393224 | tf_op jit(solution)/shard_map/ppermute | solution.py:50
  57.3 2.7 %collective-permute-start.19 = (f32[128,2048]{1,0:T(8,128)S(1)}, f32[128,2048]{1,0:T(8,128)S(1)}, u32[]{:S(2)}, u32[]{:S(2)}) collective-permute-start(f32[128,2048]{1,0:T(8,128)S(1)} %get-tuple-element.43), channel_id=1, source_target_pairs={{0,4},{4,0},{8,12},{12,8},{16,20},{20,16},{24,28},{28,24},{1,5},{5... | collective-permute-start | bytes 3145736 | tf_op jit(solution)/shard_map/ppermute | solution.py:18
  60.1 6.3 %collective-permute-start.20 = (bf16[32,2048]{1,0:T(8,128)(2,1)S(1)}, bf16[32,2048]{1,0:T(8,128)(2,1)S(1)}, u32[]{:S(2)}, u32[]{:S(2)}) collective-permute-start(bf16[32,2048]{1,0:T(8,128)(2,1)S(1)} %get-tuple-element.52), channel_id=1, source_target_pairs={{0,8},{4,12},{8,0},{12,4},{16,24},{20,28},{24,16},{28,20},{1,9},{5... | collective-permute-start | bytes 393224 | tf_op jit(solution)/shard_map/ppermute | solution.py:18
  61.4 6.5 %collective-permute-start.22 = (bf16[32,2048]{1,0:T(8,128)(2,1)S(1)}, bf16[32,2048]{1,0:T(8,128)(2,1)S(1)}, u32[]{:S(2)}, u32[]{:S(2)}) collective-permute-start(bf16[32,2048]{1,0:T(8,128)(2,1)S(1)} %get-tuple-element.53), channel_id=1, source_target_pairs={{0,16},{4,20},{8,24},{12,28},{16,0},{20,4},{24,8},{28,12},{1,17},{... | collective-permute-start | bytes 393224 | tf_op jit(solution)/shard_map/ppermute | solution.py:18
  62.2 7.2 %collective-permute-start.21 = (bf16[32,2048]{1,0:T(8,128)(2,1)S(1)}, bf16[32,2048]{1,0:T(8,128)(2,1)S(1)}, u32[]{:S(2)}, u32[]{:S(2)}) collective-permute-start(bf16[32,2048]{1,0:T(8,128)(2,1)S(1)} %get-tuple-element.54), channel_id=1, source_target_pairs={{0,24},{4,28},{8,16},{12,20},{16,8},{20,12},{24,0},{28,4},{1,25},{... | collective-permute-start | bytes 393224 | tf_op jit(solution)/shard_map/ppermute | solution.py:18

commit v15 on v14

--- a/solution.py
+++ b/solution.py
@@ -154,7 +154,7 @@
     rows, cols = tiles.shape
     rows //= chunks
     width = shares[0].shape[0] * len(offsets_col)
-    parts = 2 if chunk == chunks - 1 else 1
+    parts = 4 if chunk == chunks - 1 else 1
     vmem = pl.BlockSpec(memory_space=pltpu.VMEM)
     return pl.pallas_call(
         functools.partial(
@@ -198,12 +198,13 @@
     earlier = []
     for chunk in range(chunks):
         earlier = partial_adjoint(where, tiles, shares[chunk], earlier, offsets_col, n_row, chunk, chunks)
-    mine, others = earlier
-    others = exchange(others, "row", 1)
-    cuts = [slice(k * own_width, (k + 1) * own_width) for k in range(len(offsets_core))]
-    pairs = [mine[cut] + others[cut] for cut in cuts]
+    pairs = []
+    for mine, others in (earlier[1::2], earlier[::2]):
+        others = exchange(others, "row", 1)
+        bands = [slice(at, at + own_width) for at in range(0, mine.shape[0], own_width)]
+        pairs = [mine[band] + others[band] for band in bands] + pairs
     adjoint = pairs[0]
-    for offset in offsets_core[1:2] + offsets_core[:1:-1]:
+    for offset in offsets_core[1:]:
         adjoint = adjoint + exchange(pairs[offset // 2].astype(BF16), "row", offset).astype(F32)
     return jnp.concatenate(totals, axis=1).T, adjoint.T
 

time: 70.4 us -> 69.7 us (0.990)
  waiting for transfers between devices: 23.6 us -> 22.3 us
    ppermute x19 -> x20, waiting for transfers between devices: 19.7 us -> 18.4 us  [exchange(): return lax.ppermute(value, axis, [(i, i ^ offset) for i in range(size)])]
    ppermute x19 -> x20, starting transfers between devices: 20.4 us -> 20.9 us  [exchange(): return lax.ppermute(value, axis, [(i, i ^ offset) for i in range(size)])]
  transfers between devices with their start and end apart: 23 -> 24, of which waited for: 14 -> 14; matrix products, arithmetic and copies ran while one was open for 2% -> 2% of each run, Pallas kernels for 11% -> 11%
where the time goes in v15:
time: 69.7 us; the launch traced here: 69.5 us
  starting transfers between devices  32.6 us (47%)
  waiting for transfers between devices  22.3 us (32%)
  Pallas kernels  11.6 us (17%)
  other arithmetic  2.21 us (3%)
  between operations  0.76 us (1%)
    ppermute x20, starting transfers between devices, exchange(): return lax.ppermute(value, axis, [(i, i ^ offset) for i in range(size)])  20.9 us
    ppermute x20, waiting for transfers between devices, exchange(): return lax.ppermute(value, axis, [(i, i ^ offset) for i in range(size)])  18.4 us
    ppermute x2, starting transfers between devices, window_spread(): lax.ppermute(onward, 'col', [(0, 2), (3, 1), (1, 0), (2, 3)])  7.45 us
    ppermute x2, starting transfers between devices, window_sums(): came = lax.ppermute(terms[2], 'col', [(0, 1), (3, 2), (2, 0), (1, 3)])  4.26 us
    pallas_call x1, Pallas kernels, masked(): pl.pallas_call(functools.partial(mask_kernel, block=rows // mask.shape[0]...  4.2 us
    pallas_call x2, Pallas kernels, partial_sketch(): pl.pallas_call(functools.partial(sketch_kernel, base=chunk * rows, offset...  3.71 us
    pallas_call x2, Pallas kernels, partial_adjoint(): pl.pallas_call(functools.partial(adjoint_kernel, base=chunk * rows, parts...  3.68 us
    ppermute x2, waiting for transfers between devices, window_spread(): lax.ppermute(onward, 'col', [(0, 2), (3, 1), (1, 0), (2, 3)])  2.47 us
  transfers between devices with their start and end apart: 24, of which 14 were waited for; matrix products, arithmetic and copies ran while one was open for 2% of the time, Pallas kernels for 11%

profile of v15, /device:TPU:0, one launch (start us, length us, event | category | flops | bytes accessed | tf_op | source)
XLA Modules:
  0.0 69.5 jit_solution(15371734914992927991)
XLA Ops:
  0.6 3.0 %collective-permute-start.2 = (bf16[32,2048]{1,0:T(8,128)(2,1)}, bf16[32,2048]{1,0:T(8,128)(2,1)S(1)}, u32[]{:S(2)}, u32[]{:S(2)}) collective-permute-start(bf16[32,2048]{1,0:T(8,128)(2,1)} %bitcast.7), channel_id=1, source_target_pairs={{0,8},{4,12},{8,0},{12,4},{16,24},{20,28},{24,16},{28,20},{1,9},{5... | collective-permute-start | bytes 393224 | tf_op jit(solution)/shard_map/ppermute | solution.py:18
  3.6 1.5 %collective-permute-start.1 = (bf16[32,2048]{1,0:T(8,128)(2,1)}, bf16[32,2048]{1,0:T(8,128)(2,1)S(1)}, u32[]{:S(2)}, u32[]{:S(2)}) collective-permute-start(bf16[32,2048]{1,0:T(8,128)(2,1)} %bitcast.8), channel_id=1, source_target_pairs={{0,16},{4,20},{8,24},{12,28},{16,0},{20,4},{24,8},{28,12},{1,17},{... | collective-permute-start | bytes 393224 | tf_op jit(solution)/shard_map/ppermute | solution.py:18
  5.3 4.2 %masked_tiles.1 = (bf16[2048,2048]{1,0:T(8,128)(2,1)S(1)}, f32[8,128]{1,0:T(8,128)S(1)}) custom-call(s32[2]{0:T(128)S(1)} %pad_add_fusion.where, s32[8,8]{1,0:T(8,128)} %mask_hbm.1, bf16[2048,2048]{1,0:T(8,128)(2,1)} %green_ref.1), custom_call_target="tpu_custom_call" | custom-call | bytes 8388608 | tf_op jit(solution)/shard_map/masked_tiles/pallas_call | solution.py:77
  9.5 2.2 %collective-permute-done.1.refs_2_ = bf16[32,2048]{1,0:T(8,128)(2,1)S(1)} collective-permute-done((bf16[32,2048]{1,0:T(8,128)(2,1)}, bf16[32,2048]{1,0:T(8,128)(2,1)S(1)}, u32[]{:S(2)}, u32[]{:S(2)}) %collective-permute-start.1) | collective-permute-done | bytes 131104 | tf_op jit(solution)/shard_map/ppermute | solution.py:18
  12.2 0.8 %collective-permute-done.4.refs_5_ = bf16[32,2048]{1,0:T(8,128)(2,1)S(1)} collective-permute-done((bf16[32,2048]{1,0:T(8,128)(2,1)S(1)}, bf16[32,2048]{1,0:T(8,128)(2,1)S(1)}, u32[]{:S(2)}, u32[]{:S(2)}) %collective-permute-start.4) | collective-permute-done | bytes 131104 | tf_op jit(solution)/shard_map/ppermute | solution.py:18
  13.5 1.9 %partial_sketch.2 = (f32[64,1024]{1,0:T(8,128)S(1)}, bf16[64,1024]{1,0:T(8,128)(2,1)S(1)}, bf16[64,1024]{1,0:T(8,128)(2,1)S(1)}, f32[64,1024]{1,0:T(8,128)S(1)}, f32[64,1024]{1,0:T(8,128)S(1)}) custom-call(s32[2]{0:T(128)S(1)} %pad_add_fusion.where, bf16[2048,2048]{1,0:T(8,128)(2,1)S(1)} %get-tuple-element.25.tiles, f32[8,128]{1,0:T(8,128)S(1)} %get-tuple-element.27.token, ...), custom_call_target="tpu_custom_call" | custom-call | flops 1073741824 | bytes 4194304 | tf_op jit(solution)/shard_map/partial_sketch/pallas_call | solution.py:119
  15.4 1.6 %collective-permute-start.7 = (bf16[64,1024]{1,0:T(8,128)(2,1)S(1)}, bf16[64,1024]{1,0:T(8,128)(2,1)S(1)}, u32[]{:S(2)}, u32[]{:S(2)}) collective-permute-start(bf16[64,1024]{1,0:T(8,128)(2,1)S(1)} %get-tuple-element.36), channel_id=1, source_target_pairs={{0,1},{3,2},{2,0},{1,3},{4,5},{7,6},{6,4},{5,7},{8,9},{11,10},{10,... | collective-permute-start | bytes 393224 | tf_op jit(solution)/shard_map/ppermute | solution.py:32
  17.0 1.9 %partial_sketch.3 = (f32[64,1024]{1,0:T(8,128)S(1)}, bf16[64,1024]{1,0:T(8,128)(2,1)S(1)}, bf16[64,1024]{1,0:T(8,128)(2,1)S(1)}, f32[64,1024]{1,0:T(8,128)S(1)}, f32[64,1024]{1,0:T(8,128)S(1)}) custom-call(s32[2]{0:T(128)S(1)} %pad_add_fusion.where, bf16[2048,2048]{1,0:T(8,128)(2,1)S(1)} %get-tuple-element.25.tiles, f32[8,128]{1,0:T(8,128)S(1)} %get-tuple-element.27.token, ...), custom_call_target="tpu_custom_call" | custom-call | flops 1073741824 | bytes 4194304 | tf_op jit(solution)/shard_map/partial_sketch/pallas_call | solution.py:119
  18.8 2.6 %collective-permute-start.10 = (bf16[64,1024]{1,0:T(8,128)(2,1)S(1)}, bf16[64,1024]{1,0:T(8,128)(2,1)S(1)}, u32[]{:S(2)}, u32[]{:S(2)}) collective-permute-start(bf16[64,1024]{1,0:T(8,128)(2,1)S(1)} %get-tuple-element.42), channel_id=1, source_target_pairs={{0,1},{3,2},{2,0},{1,3},{4,5},{7,6},{6,4},{5,7},{8,9},{11,10},{10,... | collective-permute-start | bytes 393224 | tf_op jit(solution)/shard_map/ppermute | solution.py:32
  22.0 4.4 %collective-permute-start.9 = (bf16[64,1024]{1,0:T(8,128)(2,1)S(1)}, bf16[64,1024]{1,0:T(8,128)(2,1)S(1)}, u32[]{:S(2)}, u32[]{:S(2)}) collective-permute-start(bf16[64,1024]{1,0:T(8,128)(2,1)S(1)} %get-tuple-element.52), channel_id=1, source_target_pairs={{0,3},{1,2},{2,1},{3,0},{4,7},{5,6},{6,5},{7,4},{8,11},{9,10},{10,... | collective-permute-start | bytes 393224 | tf_op jit(solution)/shard_map/ppermute | solution.py:18
  26.3 1.1 %collective-permute-done.10 = bf16[64,1024]{1,0:T(8,128)(2,1)S(1)} collective-permute-done((bf16[64,1024]{1,0:T(8,128)(2,1)S(1)}, bf16[64,1024]{1,0:T(8,128)(2,1)S(1)}, u32[]{:S(2)}, u32[]{:S(2)}) %collective-permute-start.10) | collective-permute-done | bytes 131104 | tf_op jit(solution)/shard_map/ppermute | solution.py:32
  27.5 1.7 %collective-permute-start.12 = (bf16[64,1024]{1,0:T(8,128)(2,1)S(1)}, bf16[64,1024]{1,0:T(8,128)(2,1)S(1)}, u32[]{:S(2)}, u32[]{:S(2)}) collective-permute-start(bf16[64,1024]{1,0:T(8,128)(2,1)S(1)} %get-tuple-element.54), channel_id=1, source_target_pairs={{0,3},{1,2},{2,1},{3,0},{4,7},{5,6},{6,5},{7,4},{8,11},{9,10},{10,... | collective-permute-start | bytes 393224 | tf_op jit(solution)/shard_map/ppermute | solution.py:18
  29.1 6.0 %collective-permute-done.8 = bf16[64,1024]{1,0:T(8,128)(2,1)S(1)} collective-permute-done((bf16[64,1024]{1,0:T(8,128)(2,1)S(1)}, bf16[64,1024]{1,0:T(8,128)(2,1)S(1)}, u32[]{:S(2)}, u32[]{:S(2)}) %collective-permute-start.8) | collective-permute-done | bytes 131104 | tf_op jit(solution)/shard_map/ppermute | solution.py:18
  35.3 1.5 %collective-permute-start.17 = (bf16[64,1024]{1,0:T(8,128)(2,1)S(1)}, bf16[64,1024]{1,0:T(8,128)(2,1)S(1)}, u32[]{:S(2)}, u32[]{:S(2)}) collective-permute-start(bf16[64,1024]{1,0:T(8,128)(2,1)S(1)} %get-tuple-element.48.refs_0_), channel_id=1, source_target_pairs={{0,3},{1,2},{2,1},{3,0},{4,7},{5,6},{6,5},{7,4},{8,11},{9,10},{10,... | collective-permute-start | bytes 393224 | tf_op jit(solution)/shard_map/ppermute | solution.py:18
  36.8 1.8 %collective-permute-done.11 = bf16[64,1024]{1,0:T(8,128)(2,1)S(1)} collective-permute-done((bf16[64,1024]{1,0:T(8,128)(2,1)S(1)}, bf16[64,1024]{1,0:T(8,128)(2,1)S(1)}, u32[]{:S(2)}, u32[]{:S(2)}) %collective-permute-start.11) | collective-permute-done | bytes 131104 | tf_op jit(solution)/shard_map/ppermute | solution.py:18
  38.7 2.1 %collective-permute-start.14 = (bf16[64,1024]{1,0:T(8,128)(2,1)S(1)}, bf16[64,1024]{1,0:T(8,128)(2,1)S(1)}, u32[]{:S(2)}, u32[]{:S(2)}) collective-permute-start(bf16[64,1024]{1,0:T(8,128)(2,1)S(1)} %get-tuple-element.50.refs_0_), channel_id=1, source_target_pairs={{0,3},{1,2},{2,1},{3,0},{4,7},{5,6},{6,5},{7,4},{8,11},{9,10},{10,... | collective-permute-start | bytes 393224 | tf_op jit(solution)/shard_map/ppermute | solution.py:18
  41.5 1.4 %collective-permute-start.13 = (bf16[64,1024]{1,0:T(8,128)(2,1)S(1)}, bf16[64,1024]{1,0:T(8,128)(2,1)S(1)}, u32[]{:S(2)}, u32[]{:S(2)}) collective-permute-start(bf16[64,1024]{1,0:T(8,128)(2,1)S(1)} %get-tuple-element.50.refs_0_), channel_id=1, source_target_pairs={{0,1},{1,0},{2,3},{3,2},{4,5},{5,4},{6,7},{7,6},{8,9},{9,8},{10,11... | collective-permute-start | bytes 393224 | tf_op jit(solution)/shard_map/ppermute | solution.py:18
  42.9 0.6 collective-permute-done.17.refs_3_
  43.6 3.8 %collective-permute-start.18 = (bf16[64,1024]{1,0:T(8,128)(2,1)S(1)}, bf16[64,1024]{1,0:T(8,128)(2,1)S(1)}, u32[]{:S(2)}, u32[]{:S(2)}) collective-permute-start(bf16[64,1024]{1,0:T(8,128)(2,1)S(1)} %select_n.26), channel_id=1, source_target_pairs={{0,2},{3,1},{1,0},{2,3},{4,6},{7,5},{5,4},{6,7},{8,10},{11,9},{9,8... | collective-permute-start | bytes 393224 | tf_op jit(solution)/shard_map/ppermute | solution.py:50
  47.5 3.6 %collective-permute-start.15 = (bf16[64,1024]{1,0:T(8,128)(2,1)S(1)}, bf16[64,1024]{1,0:T(8,128)(2,1)S(1)}, u32[]{:S(2)}, u32[]{:S(2)}) collective-permute-start(bf16[64,1024]{1,0:T(8,128)(2,1)S(1)} %select_n.25), channel_id=1, source_target_pairs={{0,2},{3,1},{1,0},{2,3},{4,6},{7,5},{5,4},{6,7},{8,10},{11,9},{9,8... | collective-permute-start | bytes 393224 | tf_op jit(solution)/shard_map/ppermute | solution.py:50
  51.1 2.5 %collective-permute-done.18.refs_2_ = bf16[64,1024]{1,0:T(8,128)(2,1)S(1)} collective-permute-done((bf16[64,1024]{1,0:T(8,128)(2,1)S(1)}, bf16[64,1024]{1,0:T(8,128)(2,1)S(1)}, u32[]{:S(2)}, u32[]{:S(2)}) %collective-permute-start.18) | collective-permute-done | bytes 131104 | tf_op jit(solution)/shard_map/ppermute | solution.py:50
  53.6 1.8 %partial_adjoint.2.refs_4_ = f32[256,2048]{1,0:T(8,128)S(1)} custom-call(s32[2]{0:T(128)S(1)} %pad_add_fusion.where, bf16[2048,2048]{1,0:T(8,128)(2,1)S(1)} %get-tuple-element.25.tiles, bf16[64,1024]{1,0:T(8,128)(2,1)S(1)} %get-tuple-element.48.refs_0_, bf16[64,1024]{1,0:T(8,128)(2,1)S(1)} %collective-permute-done.16.refs_1_, ...), custom_call_target="tpu_custom_call" | custom-call | tf_op jit(solution)/shard_map/partial_adjoint/pallas_call | solution.py:159
  55.4 1.9 %partial_adjoint.3 = (f32[64,2048]{1,0:T(8,128)S(1)}, f32[64,2048]{1,0:T(8,128)S(1)}, f32[64,2048]{1,0:T(8,128)S(1)}, f32[64,2048]{1,0:T(8,128)S(1)}) custom-call(s32[2]{0:T(128)S(1)} %pad_add_fusion.where, bf16[2048,2048]{1,0:T(8,128)(2,1)S(1)} %get-tuple-element.25.tiles, bf16[64,1024]{1,0:T(8,128)(2,1)S(1)} %get-tuple-element.50.refs_0_, ...), custom_call_target="tpu_custom_call" | custom-call | tf_op jit(solution)/shard_map/partial_adjoint/pallas_call | solution.py:159
  57.9 1.4 %collective-permute-done.19 = f32[64,2048]{1,0:T(8,128)S(1)} collective-permute-done((f32[64,2048]{1,0:T(8,128)S(1)}, f32[64,2048]{1,0:T(8,128)S(1)}, u32[]{:S(2)}, u32[]{:S(2)}) %collective-permute-start.19) | collective-permute-done | bytes 524320 | tf_op jit(solution)/shard_map/ppermute | solution.py:18
  59.3 1.2 %collective-permute-start.20 = (bf16[32,2048]{1,0:T(8,128)(2,1)S(1)}, bf16[32,2048]{1,0:T(8,128)(2,1)S(1)}, u32[]{:S(2)}, u32[]{:S(2)}) collective-permute-start(bf16[32,2048]{1,0:T(8,128)(2,1)S(1)} %fusion.8), channel_id=1, source_target_pairs={{0,8},{4,12},{8,0},{12,4},{16,24},{20,28},{24,16},{28,20},{1,9},{5... | collective-permute-start | bytes 393224 | tf_op jit(solution)/shard_map/ppermute | solution.py:18
  60.6 1.1 %collective-permute-start.22 = (bf16[32,2048]{1,0:T(8,128)(2,1)S(1)}, bf16[32,2048]{1,0:T(8,128)(2,1)S(1)}, u32[]{:S(2)}, u32[]{:S(2)}) collective-permute-start(bf16[32,2048]{1,0:T(8,128)(2,1)S(1)} %get-tuple-element.56), channel_id=1, source_target_pairs={{0,16},{4,20},{8,24},{12,28},{16,0},{20,4},{24,8},{28,12},{1,17},{... | collective-permute-start | bytes 393224 | tf_op jit(solution)/shard_map/ppermute | solution.py:18
  61.7 1.3 %collective-permute-start.23 = (bf16[32,2048]{1,0:T(8,128)(2,1)S(1)}, bf16[32,2048]{1,0:T(8,128)(2,1)S(1)}, u32[]{:S(2)}, u32[]{:S(2)}) collective-permute-start(bf16[32,2048]{1,0:T(8,128)(2,1)S(1)} %get-tuple-element.57), channel_id=1, source_target_pairs={{0,24},{4,28},{8,16},{12,20},{16,8},{20,12},{24,0},{28,4},{1,25},{... | collective-permute-start | bytes 393224 | tf_op jit(solution)/shard_map/ppermute | solution.py:18
  63.0 0.8 %maximum_bitcast_fusion = f32[2048,64]{0,1:T(8,128)} fusion(f32[64,1024]{1,0:T(8,128)S(1)} %get-tuple-element.51, f32[64,1024]{1,0:T(8,128)S(1)} %get-tuple-element.49), kind=kLoop, calls=%fused_computation | loop fusion | flops 131072 | bytes 1048576 | tf_op jit(solution)/shard_map/transpose | solution.py:209
  63.8 1.6 %collective-permute-done.20 = bf16[32,2048]{1,0:T(8,128)(2,1)S(1)} collective-permute-done((bf16[32,2048]{1,0:T(8,128)(2,1)S(1)}, bf16[32,2048]{1,0:T(8,128)(2,1)S(1)}, u32[]{:S(2)}, u32[]{:S(2)}) %collective-permute-start.20) | collective-permute-done | bytes 131104 | tf_op jit(solution)/shard_map/ppermute | solution.py:18
  65.4 2.1 %collective-permute-done.22 = bf16[32,2048]{1,0:T(8,128)(2,1)S(1)} collective-permute-done((bf16[32,2048]{1,0:T(8,128)(2,1)S(1)}, bf16[32,2048]{1,0:T(8,128)(2,1)S(1)}, u32[]{:S(2)}, u32[]{:S(2)}) %collective-permute-start.22) | collective-permute-done | bytes 131104 | tf_op jit(solution)/shard_map/ppermute | solution.py:18
  67.6 1.2 %collective-permute-done.23 = bf16[32,2048]{1,0:T(8,128)(2,1)S(1)} collective-permute-done((bf16[32,2048]{1,0:T(8,128)(2,1)S(1)}, bf16[32,2048]{1,0:T(8,128)(2,1)S(1)}, u32[]{:S(2)}, u32[]{:S(2)}) %collective-permute-start.23) | collective-permute-done | bytes 131104 | tf_op jit(solution)/shard_map/ppermute | solution.py:18
  68.8 0.8 %fusion.12 = f32[2048,32]{0,1:T(8,128)} fusion(f32[64,2048]{1,0:T(8,128)S(1)} %collective-permute-done.19, bf16[32,2048]{1,0:T(8,128)(2,1)S(1)} %collective-permute-done.23, bf16[32,2048]{1,0:T(8,128)(2,1)S(1)} %collective-permute-done.22, bf16[32,2048]{1,0:T(8,128)(2,1)S(1)} %collective-permute-done.20, f32[64,2048]{1,0:T(8,128)S(1)} %get-tuple-element.44), kind=kLoop, calls=%fused_computation.21 | loop fusion | flops 458752 | bytes 1179648 | tf_op jit(solution)/shard_map/transpose | solution.py:209
  (34 shorter events, 3.3 us)
Async XLA Ops:
  0.6 12.9 %copy-start = (bf16[2048,32]{0,1:T(8,128)(2,1)S(1)}, bf16[2048,32]{0,1:T(8,128)(2,1)}, u32[]{:S(2)}) copy-start(bf16[2048,32]{0,1:T(8,128)(2,1)} %param.5) | copy-start | bytes 393220
  0.6 8.8 %collective-permute-start.2 = (bf16[32,2048]{1,0:T(8,128)(2,1)}, bf16[32,2048]{1,0:T(8,128)(2,1)S(1)}, u32[]{:S(2)}, u32[]{:S(2)}) collective-permute-start(bf16[32,2048]{1,0:T(8,128)(2,1)} %bitcast.7), channel_id=1, source_target_pairs={{0,8},{4,12},{8,0},{12,4},{16,24},{20,28},{24,16},{28,20},{1,9},{5... | collective-permute-start | bytes 393224 | tf_op jit(solution)/shard_map/ppermute | solution.py:18
  3.6 8.0 %collective-permute-start.1 = (bf16[32,2048]{1,0:T(8,128)(2,1)}, bf16[32,2048]{1,0:T(8,128)(2,1)S(1)}, u32[]{:S(2)}, u32[]{:S(2)}) collective-permute-start(bf16[32,2048]{1,0:T(8,128)(2,1)} %bitcast.8), channel_id=1, source_target_pairs={{0,16},{4,20},{8,24},{12,28},{16,0},{20,4},{24,8},{28,12},{1,17},{... | collective-permute-start | bytes 393224 | tf_op jit(solution)/shard_map/ppermute | solution.py:18
  5.2 6.5 %collective-permute-start = (bf16[32,2048]{1,0:T(8,128)(2,1)}, bf16[32,2048]{1,0:T(8,128)(2,1)S(1)}, u32[]{:S(2)}, u32[]{:S(2)}) collective-permute-start(bf16[32,2048]{1,0:T(8,128)(2,1)} %bitcast.9), channel_id=1, source_target_pairs={{0,24},{4,28},{8,16},{12,20},{16,8},{20,12},{24,0},{28,4},{1,25},{... | collective-permute-start | bytes 393224 | tf_op jit(solution)/shard_map/ppermute | solution.py:18
  5.2 7.0 %collective-permute-start.3 = (bf16[32,2048]{1,0:T(8,128)(2,1)}, bf16[32,2048]{1,0:T(8,128)(2,1)S(1)}, u32[]{:S(2)}, u32[]{:S(2)}) collective-permute-start(bf16[32,2048]{1,0:T(8,128)(2,1)} %bitcast.10), channel_id=1, source_target_pairs={{0,4},{4,0},{8,12},{12,8},{16,20},{20,16},{24,28},{28,24},{1,5},{5... | collective-permute-start | bytes 393224 | tf_op jit(solution)/shard_map/ppermute | solution.py:18
  11.6 1.3 %collective-permute-start.4 = (bf16[32,2048]{1,0:T(8,128)(2,1)S(1)}, bf16[32,2048]{1,0:T(8,128)(2,1)S(1)}, u32[]{:S(2)}, u32[]{:S(2)}) collective-permute-start(bf16[32,2048]{1,0:T(8,128)(2,1)S(1)} %collective-permute-done.refs_1_), channel_id=1, source_target_pairs={{0,4},{4,0},{8,12},{12,8},{16,20},{20,16},{24,28},{28,24},{1,5},{5... | collective-permute-start | bytes 393224 | tf_op jit(solution)/shard_map/ppermute | solution.py:18
  11.6 1.5 %collective-permute-start.5 = (bf16[32,2048]{1,0:T(8,128)(2,1)S(1)}, bf16[32,2048]{1,0:T(8,128)(2,1)S(1)}, u32[]{:S(2)}, u32[]{:S(2)}) collective-permute-start(bf16[32,2048]{1,0:T(8,128)(2,1)S(1)} %collective-permute-done.1.refs_2_), channel_id=1, source_target_pairs={{0,4},{4,0},{8,12},{12,8},{16,20},{20,16},{24,28},{28,24},{1,5},{5... | collective-permute-start | bytes 393224 | tf_op jit(solution)/shard_map/ppermute | solution.py:18
  12.1 1.3 %collective-permute-start.6 = (bf16[32,2048]{1,0:T(8,128)(2,1)S(1)}, bf16[32,2048]{1,0:T(8,128)(2,1)S(1)}, u32[]{:S(2)}, u32[]{:S(2)}) collective-permute-start(bf16[32,2048]{1,0:T(8,128)(2,1)S(1)} %collective-permute-done.2.refs_3_), channel_id=1, source_target_pairs={{0,4},{4,0},{8,12},{12,8},{16,20},{20,16},{24,28},{28,24},{1,5},{5... | collective-permute-start | bytes 393224 | tf_op jit(solution)/shard_map/ppermute | solution.py:18
  15.4 6.5 %collective-permute-start.7 = (bf16[64,1024]{1,0:T(8,128)(2,1)S(1)}, bf16[64,1024]{1,0:T(8,128)(2,1)S(1)}, u32[]{:S(2)}, u32[]{:S(2)}) collective-permute-start(bf16[64,1024]{1,0:T(8,128)(2,1)S(1)} %get-tuple-element.36), channel_id=1, source_target_pairs={{0,1},{3,2},{2,0},{1,3},{4,5},{7,6},{6,4},{5,7},{8,9},{11,10},{10,... | collective-permute-start | bytes 393224 | tf_op jit(solution)/shard_map/ppermute | solution.py:32
  18.8 8.6 %collective-permute-start.10 = (bf16[64,1024]{1,0:T(8,128)(2,1)S(1)}, bf16[64,1024]{1,0:T(8,128)(2,1)S(1)}, u32[]{:S(2)}, u32[]{:S(2)}) collective-permute-start(bf16[64,1024]{1,0:T(8,128)(2,1)S(1)} %get-tuple-element.42), channel_id=1, source_target_pairs={{0,1},{3,2},{2,0},{1,3},{4,5},{7,6},{6,4},{5,7},{8,9},{11,10},{10,... | collective-permute-start | bytes 393224 | tf_op jit(solution)/shard_map/ppermute | solution.py:32
  22.0 13.2 %collective-permute-start.9 = (bf16[64,1024]{1,0:T(8,128)(2,1)S(1)}, bf16[64,1024]{1,0:T(8,128)(2,1)S(1)}, u32[]{:S(2)}, u32[]{:S(2)}) collective-permute-start(bf16[64,1024]{1,0:T(8,128)(2,1)S(1)} %get-tuple-element.52), channel_id=1, source_target_pairs={{0,3},{1,2},{2,1},{3,0},{4,7},{5,6},{6,5},{7,4},{8,11},{9,10},{10,... | collective-permute-start | bytes 393224 | tf_op jit(solution)/shard_map/ppermute | solution.py:18
  26.3 8.9 %collective-permute-start.8 = (bf16[64,1024]{1,0:T(8,128)(2,1)S(1)}, bf16[64,1024]{1,0:T(8,128)(2,1)S(1)}, u32[]{:S(2)}, u32[]{:S(2)}) collective-permute-start(bf16[64,1024]{1,0:T(8,128)(2,1)S(1)} %get-tuple-element.37), channel_id=1, source_target_pairs={{0,1},{1,0},{2,3},{3,2},{4,5},{5,4},{6,7},{7,6},{8,9},{9,8},{10,11... | collective-permute-start | bytes 393224 | tf_op jit(solution)/shard_map/ppermute | solution.py:18
  27.5 11.2 %collective-permute-start.12 = (bf16[64,1024]{1,0:T(8,128)(2,1)S(1)}, bf16[64,1024]{1,0:T(8,128)(2,1)S(1)}, u32[]{:S(2)}, u32[]{:S(2)}) collective-permute-start(bf16[64,1024]{1,0:T(8,128)(2,1)S(1)} %get-tuple-element.54), channel_id=1, source_target_pairs={{0,3},{1,2},{2,1},{3,0},{4,7},{5,6},{6,5},{7,4},{8,11},{9,10},{10,... | collective-permute-start | bytes 393224 | tf_op jit(solution)/shard_map/ppermute | solution.py:18
  29.1 9.5 %collective-permute-start.11 = (bf16[64,1024]{1,0:T(8,128)(2,1)S(1)}, bf16[64,1024]{1,0:T(8,128)(2,1)S(1)}, u32[]{:S(2)}, u32[]{:S(2)}) collective-permute-start(bf16[64,1024]{1,0:T(8,128)(2,1)S(1)} %get-tuple-element.43), channel_id=1, source_target_pairs={{0,1},{1,0},{2,3},{3,2},{4,5},{5,4},{6,7},{7,6},{8,9},{9,8},{10,11... | collective-permute-start | bytes 393224 | tf_op jit(solution)/shard_map/ppermute | solution.py:18
  35.3 8.3 %collective-permute-start.17 = (bf16[64,1024]{1,0:T(8,128)(2,1)S(1)}, bf16[64,1024]{1,0:T(8,128)(2,1)S(1)}, u32[]{:S(2)}, u32[]{:S(2)}) collective-permute-start(bf16[64,1024]{1,0:T(8,128)(2,1)S(1)} %get-tuple-element.48.refs_0_), channel_id=1, source_target_pairs={{0,3},{1,2},{2,1},{3,0},{4,7},{5,6},{6,5},{7,4},{8,11},{9,10},{10,... | collective-permute-start | bytes 393224 | tf_op jit(solution)/shard_map/ppermute | solution.py:18
  38.7 8.7 %collective-permute-start.14 = (bf16[64,1024]{1,0:T(8,128)(2,1)S(1)}, bf16[64,1024]{1,0:T(8,128)(2,1)S(1)}, u32[]{:S(2)}, u32[]{:S(2)}) collective-permute-start(bf16[64,1024]{1,0:T(8,128)(2,1)S(1)} %get-tuple-element.50.refs_0_), channel_id=1, source_target_pairs={{0,3},{1,2},{2,1},{3,0},{4,7},{5,6},{6,5},{7,4},{8,11},{9,10},{10,... | collective-permute-start | bytes 393224 | tf_op jit(solution)/shard_map/ppermute | solution.py:18
  40.9 10.2 %collective-permute-start.16 = (bf16[64,1024]{1,0:T(8,128)(2,1)S(1)}, bf16[64,1024]{1,0:T(8,128)(2,1)S(1)}, u32[]{:S(2)}, u32[]{:S(2)}) collective-permute-start(bf16[64,1024]{1,0:T(8,128)(2,1)S(1)} %get-tuple-element.48.refs_0_), channel_id=1, source_target_pairs={{0,1},{1,0},{2,3},{3,2},{4,5},{5,4},{6,7},{7,6},{8,9},{9,8},{10,11... | collective-permute-start | bytes 393224 | tf_op jit(solution)/shard_map/ppermute | solution.py:18
  41.5 13.9 %collective-permute-start.13 = (bf16[64,1024]{1,0:T(8,128)(2,1)S(1)}, bf16[64,1024]{1,0:T(8,128)(2,1)S(1)}, u32[]{:S(2)}, u32[]{:S(2)}) collective-permute-start(bf16[64,1024]{1,0:T(8,128)(2,1)S(1)} %get-tuple-element.50.refs_0_), channel_id=1, source_target_pairs={{0,1},{1,0},{2,3},{3,2},{4,5},{5,4},{6,7},{7,6},{8,9},{9,8},{10,11... | collective-permute-start | bytes 393224 | tf_op jit(solution)/shard_map/ppermute | solution.py:18
  43.6 10.0 %collective-permute-start.18 = (bf16[64,1024]{1,0:T(8,128)(2,1)S(1)}, bf16[64,1024]{1,0:T(8,128)(2,1)S(1)}, u32[]{:S(2)}, u32[]{:S(2)}) collective-permute-start(bf16[64,1024]{1,0:T(8,128)(2,1)S(1)} %select_n.26), channel_id=1, source_target_pairs={{0,2},{3,1},{1,0},{2,3},{4,6},{7,5},{5,4},{6,7},{8,10},{11,9},{9,8... | collective-permute-start | bytes 393224 | tf_op jit(solution)/shard_map/ppermute | solution.py:50
  47.5 7.9 %collective-permute-start.15 = (bf16[64,1024]{1,0:T(8,128)(2,1)S(1)}, bf16[64,1024]{1,0:T(8,128)(2,1)S(1)}, u32[]{:S(2)}, u32[]{:S(2)}) collective-permute-start(bf16[64,1024]{1,0:T(8,128)(2,1)S(1)} %select_n.25), channel_id=1, source_target_pairs={{0,2},{3,1},{1,0},{2,3},{4,6},{7,5},{5,4},{6,7},{8,10},{11,9},{9,8... | collective-permute-start | bytes 393224 | tf_op jit(solution)/shard_map/ppermute | solution.py:50
  57.3 2.0 %collective-permute-start.19 = (f32[64,2048]{1,0:T(8,128)S(1)}, f32[64,2048]{1,0:T(8,128)S(1)}, u32[]{:S(2)}, u32[]{:S(2)}) collective-permute-start(f32[64,2048]{1,0:T(8,128)S(1)} %get-tuple-element.45), channel_id=1, source_target_pairs={{0,4},{4,0},{8,12},{12,8},{16,20},{20,16},{24,28},{28,24},{1,5},{5... | collective-permute-start | bytes 1572872 | tf_op jit(solution)/shard_map/ppermute | solution.py:18
  57.4 3.2 %collective-permute-start.21 = (f32[64,2048]{1,0:T(8,128)S(1)}, f32[64,2048]{1,0:T(8,128)S(1)}, u32[]{:S(2)}, u32[]{:S(2)}) collective-permute-start(f32[64,2048]{1,0:T(8,128)S(1)} %get-tuple-element.47), channel_id=1, source_target_pairs={{0,4},{4,0},{8,12},{12,8},{16,20},{20,16},{24,28},{28,24},{1,5},{5... | collective-permute-start | bytes 1572872 | tf_op jit(solution)/shard_map/ppermute | solution.py:18
  59.3 6.1 %collective-permute-start.20 = (bf16[32,2048]{1,0:T(8,128)(2,1)S(1)}, bf16[32,2048]{1,0:T(8,128)(2,1)S(1)}, u32[]{:S(2)}, u32[]{:S(2)}) collective-permute-start(bf16[32,2048]{1,0:T(8,128)(2,1)S(1)} %fusion.8), channel_id=1, source_target_pairs={{0,8},{4,12},{8,0},{12,4},{16,24},{20,28},{24,16},{28,20},{1,9},{5... | collective-permute-start | bytes 393224 | tf_op jit(solution)/shard_map/ppermute | solution.py:18
  60.6 6.9 %collective-permute-start.22 = (bf16[32,2048]{1,0:T(8,128)(2,1)S(1)}, bf16[32,2048]{1,0:T(8,128)(2,1)S(1)}, u32[]{:S(2)}, u32[]{:S(2)}) collective-permute-start(bf16[32,2048]{1,0:T(8,128)(2,1)S(1)} %get-tuple-element.56), channel_id=1, source_target_pairs={{0,16},{4,20},{8,24},{12,28},{16,0},{20,4},{24,8},{28,12},{1,17},{... | collective-permute-start | bytes 393224 | tf_op jit(solution)/shard_map/ppermute | solution.py:18
  61.7 7.1 %collective-permute-start.23 = (bf16[32,2048]{1,0:T(8,128)(2,1)S(1)}, bf16[32,2048]{1,0:T(8,128)(2,1)S(1)}, u32[]{:S(2)}, u32[]{:S(2)}) collective-permute-start(bf16[32,2048]{1,0:T(8,128)(2,1)S(1)} %get-tuple-element.57), channel_id=1, source_target_pairs={{0,24},{4,28},{8,16},{12,20},{16,8},{20,12},{24,0},{28,4},{1,25},{... | collective-permute-start | bytes 393224 | tf_op jit(solution)/shard_map/ppermute | solution.py:18

commit v16 on v15

--- a/solution.py
+++ b/solution.py
@@ -130,7 +130,7 @@
     )(where, tiles, token, *blocks)
 
 
-def adjoint_kernel(where, tiles, *refs, base, parts, offsets_col, devices):
+def adjoint_kernel(where, tiles, *refs, base, span, parts, offsets_col, devices):
     shares, earlier, outs, lowered = refs[: len(offsets_col)], refs[len(offsets_col) : -1 - parts], refs[-1 - parts : -1], refs[-1]
     share, rows = shares[0].shape
     ratio = devices // len(offsets_col)
@@ -142,27 +142,27 @@
             lowered[pl.ds(pl.multiple_of(start, own), own), :] = ref[n * own : (n + 1) * own, :]
     for step in range(tiles.shape[1] // STEP):
         at = slice(step * STEP, (step + 1) * STEP)
-        term = jnp.dot(lowered[...], tiles[base : base + rows, at], preferred_element_type=F32)
+        term = jnp.dot(lowered[span, :], tiles[base : base + rows, at], preferred_element_type=F32)
         if earlier:
-            term += earlier[0][:, at]
+            term += earlier[0][span, at]
         height = outs[0].shape[0]
         for k, out in enumerate(outs):
             out[:, at] = term[k * height : (k + 1) * height]
 
 
-def partial_adjoint(where, tiles, shares, earlier, offsets_col, devices, chunk, chunks):
-    rows, cols = tiles.shape
-    rows //= chunks
-    width = shares[0].shape[0] * len(offsets_col)
-    parts = 4 if chunk == chunks - 1 else 1
+def partial_adjoint(where, tiles, shares, earlier, span, parts, offsets_col, devices, base):
+    cols = tiles.shape[1]
+    share, rows = shares[0].shape
+    width = share * len(offsets_col)
+    height = (span.stop - span.start) // parts
     vmem = pl.BlockSpec(memory_space=pltpu.VMEM)
     return pl.pallas_call(
         functools.partial(
-            adjoint_kernel, base=chunk * rows, parts=parts, offsets_col=offsets_col, devices=devices
+            adjoint_kernel, base=base, span=span, parts=parts, offsets_col=offsets_col, devices=devices
         ),
         in_specs=[pl.BlockSpec(memory_space=pltpu.SMEM)] + [vmem] * (1 + len(shares) + len(earlier)),
         out_specs=[vmem] * parts,
-        out_shape=[jax.ShapeDtypeStruct((width // parts, cols), F32)] * parts,
+        out_shape=[jax.ShapeDtypeStruct((height, cols), F32)] * parts,
         scratch_shapes=[pltpu.VMEM((width, rows), BF16)],
         compiler_params=pltpu.CompilerParams(vmem_limit_bytes=VMEM_LIMIT),
         cost_estimate=pl.CostEstimate(
@@ -179,7 +179,7 @@
     chunks = CHUNKS if green.shape[0] % (CHUNKS * STEP) == 0 else 1
     offsets_col = list(range(n_col))
     offsets_core = list(range(0, n_row, 2))
-    gather_core = [0] + offsets_core[:0:-1]
+    gather_core = offsets_core
     offsets_row = gather_core + [offset ^ 1 for offset in gather_core]
     tiles, token = masked(where, green, mask)
 
@@ -196,15 +196,23 @@
         shares.append(window_spread(totals[-1].astype(BF16), ends, n_col))
 
     earlier = []
-    for chunk in range(chunks):
-        earlier = partial_adjoint(where, tiles, shares[chunk], earlier, offsets_col, n_row, chunk, chunks)
+    length = green.shape[0] // chunks
+    width = own_width * n_row
+    for chunk in range(chunks - 1):
+        earlier = partial_adjoint(
+            where, tiles, shares[chunk], earlier, slice(0, width), 1, offsets_col, n_row, chunk * length
+        )
+    theirs, ours = (
+        partial_adjoint(where, tiles, shares[-1], earlier, span, 2, offsets_col, n_row, (chunks - 1) * length)
+        for span in (slice(width // 2, width), slice(0, width // 2))
+    )
     pairs = []
-    for mine, others in (earlier[1::2], earlier[::2]):
+    for mine, others in zip(ours[::-1], theirs[::-1]):
         others = exchange(others, "row", 1)
         bands = [slice(at, at + own_width) for at in range(0, mine.shape[0], own_width)]
         pairs = [mine[band] + others[band] for band in bands] + pairs
     adjoint = pairs[0]
-    for offset in offsets_core[1:]:
+    for offset in offsets_core[1:2] + offsets_core[:1:-1]:
         adjoint = adjoint + exchange(pairs[offset // 2].astype(BF16), "row", offset).astype(F32)
     return jnp.concatenate(totals, axis=1).T, adjoint.T
 

time: 69.7 us -> 69.3 us (level)
  waiting for transfers between devices: 22.3 us -> 21.3 us
  Pallas kernels: 11.6 us -> 12.3 us
    pallas_call x2 -> x3, Pallas kernels: 3.68 us -> 4.44 us  [partial_adjoint(): pl.pallas_call(functools.partial(adjoint_kernel, base=base, span=span, pa...]
    ppermute x20, waiting for transfers between devices: 18.4 us -> 17.7 us  [exchange(): return lax.ppermute(value, axis, [(i, i ^ offset) for i in range(size)])]
  transfers between devices with their start and end apart: 24 -> 24, of which waited for: 14 -> 16; matrix products, arithmetic and copies ran while one was open for 2% -> 2% of each run, Pallas kernels for 11% -> 13%
where the time goes in v16:
time: 69.3 us; the launch traced here: 69.2 us
  starting transfers between devices  32.6 us (47%)
  waiting for transfers between devices  21.3 us (31%)
  Pallas kernels  12.3 us (18%)
  other arithmetic  2.18 us (3%)
  between operations  0.76 us (1%)
    ppermute x20, starting transfers between devices, exchange(): return lax.ppermute(value, axis, [(i, i ^ offset) for i in range(size)])  20.9 us
    ppermute x20, waiting for transfers between devices, exchange(): return lax.ppermute(value, axis, [(i, i ^ offset) for i in range(size)])  17.7 us
    ppermute x2, starting transfers between devices, window_spread(): lax.ppermute(onward, 'col', [(0, 2), (3, 1), (1, 0), (2, 3)])  7.47 us
    pallas_call x3, Pallas kernels, partial_adjoint(): pl.pallas_call(functools.partial(adjoint_kernel, base=base, span=span, pa...  4.44 us
    ppermute x2, starting transfers between devices, window_sums(): came = lax.ppermute(terms[2], 'col', [(0, 1), (3, 2), (2, 0), (1, 3)])  4.26 us
    pallas_call x1, Pallas kernels, masked(): pl.pallas_call(functools.partial(mask_kernel, block=rows // mask.shape[0]...  4.11 us
    pallas_call x2, Pallas kernels, partial_sketch(): pl.pallas_call(functools.partial(sketch_kernel, base=chunk * rows, offset...  3.71 us
    ppermute x2, waiting for transfers between devices, window_spread(): lax.ppermute(onward, 'col', [(0, 2), (3, 1), (1, 0), (2, 3)])  2.15 us
  transfers between devices with their start and end apart: 24, of which 16 were waited for; matrix products, arithmetic and copies ran while one was open for 2% of the time, Pallas kernels for 13%

profile of v16, /device:TPU:0, one launch (start us, length us, event | category | flops | bytes accessed | tf_op | source)
XLA Modules:
  0.0 69.2 jit_solution(10679504135437959608)
XLA Ops:
  0.6 3.0 %collective-permute-start = (bf16[32,2048]{1,0:T(8,128)(2,1)}, bf16[32,2048]{1,0:T(8,128)(2,1)S(1)}, u32[]{:S(2)}, u32[]{:S(2)}) collective-permute-start(bf16[32,2048]{1,0:T(8,128)(2,1)} %bitcast.7), channel_id=1, source_target_pairs={{0,8},{4,12},{8,0},{12,4},{16,24},{20,28},{24,16},{28,20},{1,9},{5... | collective-permute-start | bytes 393224 | tf_op jit(solution)/shard_map/ppermute | solution.py:18
  3.6 1.5 %collective-permute-start.1 = (bf16[32,2048]{1,0:T(8,128)(2,1)}, bf16[32,2048]{1,0:T(8,128)(2,1)S(1)}, u32[]{:S(2)}, u32[]{:S(2)}) collective-permute-start(bf16[32,2048]{1,0:T(8,128)(2,1)} %bitcast.8), channel_id=1, source_target_pairs={{0,16},{4,20},{8,24},{12,28},{16,0},{20,4},{24,8},{28,12},{1,17},{... | collective-permute-start | bytes 393224 | tf_op jit(solution)/shard_map/ppermute | solution.py:18
  5.3 4.1 %masked_tiles.1 = (bf16[2048,2048]{1,0:T(8,128)(2,1)S(1)}, f32[8,128]{1,0:T(8,128)S(1)}) custom-call(s32[2]{0:T(128)S(1)} %pad_add_fusion.where, s32[8,8]{1,0:T(8,128)} %mask_hbm.1, bf16[2048,2048]{1,0:T(8,128)(2,1)} %green_ref.1), custom_call_target="tpu_custom_call" | custom-call | bytes 8388608 | tf_op jit(solution)/shard_map/masked_tiles/pallas_call | solution.py:77
  9.4 2.2 %collective-permute-done.1.refs_2_ = bf16[32,2048]{1,0:T(8,128)(2,1)S(1)} collective-permute-done((bf16[32,2048]{1,0:T(8,128)(2,1)}, bf16[32,2048]{1,0:T(8,128)(2,1)S(1)}, u32[]{:S(2)}, u32[]{:S(2)}) %collective-permute-start.1) | collective-permute-done | bytes 131104 | tf_op jit(solution)/shard_map/ppermute | solution.py:18
  12.2 0.8 %collective-permute-done.4.refs_5_ = bf16[32,2048]{1,0:T(8,128)(2,1)S(1)} collective-permute-done((bf16[32,2048]{1,0:T(8,128)(2,1)S(1)}, bf16[32,2048]{1,0:T(8,128)(2,1)S(1)}, u32[]{:S(2)}, u32[]{:S(2)}) %collective-permute-start.4) | collective-permute-done | bytes 131104 | tf_op jit(solution)/shard_map/ppermute | solution.py:18
  13.5 1.9 %partial_sketch.2 = (f32[64,1024]{1,0:T(8,128)S(1)}, bf16[64,1024]{1,0:T(8,128)(2,1)S(1)}, bf16[64,1024]{1,0:T(8,128)(2,1)S(1)}, f32[64,1024]{1,0:T(8,128)S(1)}, f32[64,1024]{1,0:T(8,128)S(1)}) custom-call(s32[2]{0:T(128)S(1)} %pad_add_fusion.where, bf16[2048,2048]{1,0:T(8,128)(2,1)S(1)} %get-tuple-element.25.tiles, f32[8,128]{1,0:T(8,128)S(1)} %get-tuple-element.27.token, ...), custom_call_target="tpu_custom_call" | custom-call | flops 1073741824 | bytes 4194304 | tf_op jit(solution)/shard_map/partial_sketch/pallas_call | solution.py:119
  15.4 1.6 %collective-permute-start.7 = (bf16[64,1024]{1,0:T(8,128)(2,1)S(1)}, bf16[64,1024]{1,0:T(8,128)(2,1)S(1)}, u32[]{:S(2)}, u32[]{:S(2)}) collective-permute-start(bf16[64,1024]{1,0:T(8,128)(2,1)S(1)} %get-tuple-element.36), channel_id=1, source_target_pairs={{0,1},{3,2},{2,0},{1,3},{4,5},{7,6},{6,4},{5,7},{8,9},{11,10},{10,... | collective-permute-start | bytes 393224 | tf_op jit(solution)/shard_map/ppermute | solution.py:32
  17.0 1.9 %partial_sketch.3 = (f32[64,1024]{1,0:T(8,128)S(1)}, bf16[64,1024]{1,0:T(8,128)(2,1)S(1)}, bf16[64,1024]{1,0:T(8,128)(2,1)S(1)}, f32[64,1024]{1,0:T(8,128)S(1)}, f32[64,1024]{1,0:T(8,128)S(1)}) custom-call(s32[2]{0:T(128)S(1)} %pad_add_fusion.where, bf16[2048,2048]{1,0:T(8,128)(2,1)S(1)} %get-tuple-element.25.tiles, f32[8,128]{1,0:T(8,128)S(1)} %get-tuple-element.27.token, ...), custom_call_target="tpu_custom_call" | custom-call | flops 1073741824 | bytes 4194304 | tf_op jit(solution)/shard_map/partial_sketch/pallas_call | solution.py:119
  18.8 2.6 %collective-permute-start.10 = (bf16[64,1024]{1,0:T(8,128)(2,1)S(1)}, bf16[64,1024]{1,0:T(8,128)(2,1)S(1)}, u32[]{:S(2)}, u32[]{:S(2)}) collective-permute-start(bf16[64,1024]{1,0:T(8,128)(2,1)S(1)} %get-tuple-element.42), channel_id=1, source_target_pairs={{0,1},{3,2},{2,0},{1,3},{4,5},{7,6},{6,4},{5,7},{8,9},{11,10},{10,... | collective-permute-start | bytes 393224 | tf_op jit(solution)/shard_map/ppermute | solution.py:32
  22.0 4.4 %collective-permute-start.9 = (bf16[64,1024]{1,0:T(8,128)(2,1)S(1)}, bf16[64,1024]{1,0:T(8,128)(2,1)S(1)}, u32[]{:S(2)}, u32[]{:S(2)}) collective-permute-start(bf16[64,1024]{1,0:T(8,128)(2,1)S(1)} %get-tuple-element.52), channel_id=1, source_target_pairs={{0,3},{1,2},{2,1},{3,0},{4,7},{5,6},{6,5},{7,4},{8,11},{9,10},{10,... | collective-permute-start | bytes 393224 | tf_op jit(solution)/shard_map/ppermute | solution.py:18
  26.3 1.1 %collective-permute-done.10 = bf16[64,1024]{1,0:T(8,128)(2,1)S(1)} collective-permute-done((bf16[64,1024]{1,0:T(8,128)(2,1)S(1)}, bf16[64,1024]{1,0:T(8,128)(2,1)S(1)}, u32[]{:S(2)}, u32[]{:S(2)}) %collective-permute-start.10) | collective-permute-done | bytes 131104 | tf_op jit(solution)/shard_map/ppermute | solution.py:32
  27.5 1.7 %collective-permute-start.12 = (bf16[64,1024]{1,0:T(8,128)(2,1)S(1)}, bf16[64,1024]{1,0:T(8,128)(2,1)S(1)}, u32[]{:S(2)}, u32[]{:S(2)}) collective-permute-start(bf16[64,1024]{1,0:T(8,128)(2,1)S(1)} %get-tuple-element.54), channel_id=1, source_target_pairs={{0,3},{1,2},{2,1},{3,0},{4,7},{5,6},{6,5},{7,4},{8,11},{9,10},{10,... | collective-permute-start | bytes 393224 | tf_op jit(solution)/shard_map/ppermute | solution.py:18
  29.1 1.8 %collective-permute-done.9 = bf16[64,1024]{1,0:T(8,128)(2,1)S(1)} collective-permute-done((bf16[64,1024]{1,0:T(8,128)(2,1)S(1)}, bf16[64,1024]{1,0:T(8,128)(2,1)S(1)}, u32[]{:S(2)}, u32[]{:S(2)}) %collective-permute-start.9) | collective-permute-done | bytes 131104 | tf_op jit(solution)/shard_map/ppermute | solution.py:18
  30.9 4.3 %collective-permute-done.8 = bf16[64,1024]{1,0:T(8,128)(2,1)S(1)} collective-permute-done((bf16[64,1024]{1,0:T(8,128)(2,1)S(1)}, bf16[64,1024]{1,0:T(8,128)(2,1)S(1)}, u32[]{:S(2)}, u32[]{:S(2)}) %collective-permute-start.8) | collective-permute-done | bytes 131104 | tf_op jit(solution)/shard_map/ppermute | solution.py:18
  35.3 1.5 %collective-permute-start.17 = (bf16[64,1024]{1,0:T(8,128)(2,1)S(1)}, bf16[64,1024]{1,0:T(8,128)(2,1)S(1)}, u32[]{:S(2)}, u32[]{:S(2)}) collective-permute-start(bf16[64,1024]{1,0:T(8,128)(2,1)S(1)} %get-tuple-element.48.refs_0_), channel_id=1, source_target_pairs={{0,3},{1,2},{2,1},{3,0},{4,7},{5,6},{6,5},{7,4},{8,11},{9,10},{10,... | collective-permute-start | bytes 393224 | tf_op jit(solution)/shard_map/ppermute | solution.py:18
  36.8 1.9 %collective-permute-done.11 = bf16[64,1024]{1,0:T(8,128)(2,1)S(1)} collective-permute-done((bf16[64,1024]{1,0:T(8,128)(2,1)S(1)}, bf16[64,1024]{1,0:T(8,128)(2,1)S(1)}, u32[]{:S(2)}, u32[]{:S(2)}) %collective-permute-start.11) | collective-permute-done | bytes 131104 | tf_op jit(solution)/shard_map/ppermute | solution.py:18
  38.7 2.1 %collective-permute-start.14 = (bf16[64,1024]{1,0:T(8,128)(2,1)S(1)}, bf16[64,1024]{1,0:T(8,128)(2,1)S(1)}, u32[]{:S(2)}, u32[]{:S(2)}) collective-permute-start(bf16[64,1024]{1,0:T(8,128)(2,1)S(1)} %get-tuple-element.50.refs_0_), channel_id=1, source_target_pairs={{0,3},{1,2},{2,1},{3,0},{4,7},{5,6},{6,5},{7,4},{8,11},{9,10},{10,... | collective-permute-start | bytes 393224 | tf_op jit(solution)/shard_map/ppermute | solution.py:18
  41.5 1.4 %collective-permute-start.16 = (bf16[64,1024]{1,0:T(8,128)(2,1)S(1)}, bf16[64,1024]{1,0:T(8,128)(2,1)S(1)}, u32[]{:S(2)}, u32[]{:S(2)}) collective-permute-start(bf16[64,1024]{1,0:T(8,128)(2,1)S(1)} %get-tuple-element.48.refs_0_), channel_id=1, source_target_pairs={{0,1},{1,0},{2,3},{3,2},{4,5},{5,4},{6,7},{7,6},{8,9},{9,8},{10,11... | collective-permute-start | bytes 393224 | tf_op jit(solution)/shard_map/ppermute | solution.py:18
  43.6 3.8 %collective-permute-start.18 = (bf16[64,1024]{1,0:T(8,128)(2,1)S(1)}, bf16[64,1024]{1,0:T(8,128)(2,1)S(1)}, u32[]{:S(2)}, u32[]{:S(2)}) collective-permute-start(bf16[64,1024]{1,0:T(8,128)(2,1)S(1)} %select_n.26), channel_id=1, source_target_pairs={{0,2},{3,1},{1,0},{2,3},{4,6},{7,5},{5,4},{6,7},{8,10},{11,9},{9,8... | collective-permute-start | bytes 393224 | tf_op jit(solution)/shard_map/ppermute | solution.py:50
  47.5 3.6 %collective-permute-start.15 = (bf16[64,1024]{1,0:T(8,128)(2,1)S(1)}, bf16[64,1024]{1,0:T(8,128)(2,1)S(1)}, u32[]{:S(2)}, u32[]{:S(2)}) collective-permute-start(bf16[64,1024]{1,0:T(8,128)(2,1)S(1)} %select_n.25), channel_id=1, source_target_pairs={{0,2},{3,1},{1,0},{2,3},{4,6},{7,5},{5,4},{6,7},{8,10},{11,9},{9,8... | collective-permute-start | bytes 393224 | tf_op jit(solution)/shard_map/ppermute | solution.py:50
  51.4 2.1 %collective-permute-done.18.refs_2_ = bf16[64,1024]{1,0:T(8,128)(2,1)S(1)} collective-permute-done((bf16[64,1024]{1,0:T(8,128)(2,1)S(1)}, bf16[64,1024]{1,0:T(8,128)(2,1)S(1)}, u32[]{:S(2)}, u32[]{:S(2)}) %collective-permute-start.18) | collective-permute-done | bytes 131104 | tf_op jit(solution)/shard_map/ppermute | solution.py:50
  53.6 1.8 %partial_adjoint.3.refs_4_ = f32[256,2048]{1,0:T(8,128)S(1)} custom-call(s32[2]{0:T(128)S(1)} %pad_add_fusion.where, bf16[2048,2048]{1,0:T(8,128)(2,1)S(1)} %get-tuple-element.25.tiles, bf16[64,1024]{1,0:T(8,128)(2,1)S(1)} %get-tuple-element.48.refs_0_, bf16[64,1024]{1,0:T(8,128)(2,1)S(1)} %collective-permute-done.16.refs_1_, ...), custom_call_target="tpu_custom_call" | custom-call | tf_op jit(solution)/shard_map/partial_adjoint/pallas_call | solution.py:159
  55.4 1.3 %partial_adjoint.5 = (f32[64,2048]{1,0:T(8,128)S(1)}, f32[64,2048]{1,0:T(8,128)S(1)}) custom-call(s32[2]{0:T(128)S(1)} %pad_add_fusion.where, bf16[2048,2048]{1,0:T(8,128)(2,1)S(1)} %get-tuple-element.25.tiles, bf16[64,1024]{1,0:T(8,128)(2,1)S(1)} %get-tuple-element.50.refs_0_, bf16[64,1024]{1,0:T(8,128)(2,1)S(1)} %collective-permute-done.13.refs_1_, ...), custom_call_target="tpu_custom_call" | custom-call | tf_op jit(solution)/shard_map/partial_adjoint/pallas_call | solution.py:159
  57.3 1.3 %partial_adjoint.4 = (f32[64,2048]{1,0:T(8,128)S(1)}, f32[64,2048]{1,0:T(8,128)S(1)}) custom-call(s32[2]{0:T(128)S(1)} %pad_add_fusion.where, bf16[2048,2048]{1,0:T(8,128)(2,1)S(1)} %get-tuple-element.25.tiles, bf16[64,1024]{1,0:T(8,128)(2,1)S(1)} %get-tuple-element.50.refs_0_, bf16[64,1024]{1,0:T(8,128)(2,1)S(1)} %collective-permute-done.13.refs_1_, ...), custom_call_target="tpu_custom_call" | custom-call | tf_op jit(solution)/shard_map/partial_adjoint/pallas_call | solution.py:159
  58.8 1.6 %collective-permute-start.23 = (bf16[32,2048]{1,0:T(8,128)(2,1)S(1)}, bf16[32,2048]{1,0:T(8,128)(2,1)S(1)}, u32[]{:S(2)}, u32[]{:S(2)}) collective-permute-start(bf16[32,2048]{1,0:T(8,128)(2,1)S(1)} %get-tuple-element.57), channel_id=1, source_target_pairs={{0,16},{4,20},{8,24},{12,28},{16,0},{20,4},{24,8},{28,12},{1,17},{... | collective-permute-start | bytes 393224 | tf_op jit(solution)/shard_map/ppermute | solution.py:18
  60.4 1.1 %collective-permute-start.22 = (bf16[32,2048]{1,0:T(8,128)(2,1)S(1)}, bf16[32,2048]{1,0:T(8,128)(2,1)S(1)}, u32[]{:S(2)}, u32[]{:S(2)}) collective-permute-start(bf16[32,2048]{1,0:T(8,128)(2,1)S(1)} %get-tuple-element.56), channel_id=1, source_target_pairs={{0,24},{4,28},{8,16},{12,20},{16,8},{20,12},{24,0},{28,4},{1,25},{... | collective-permute-start | bytes 393224 | tf_op jit(solution)/shard_map/ppermute | solution.py:18
  61.5 0.9 %collective-permute-start.20 = (bf16[32,2048]{1,0:T(8,128)(2,1)S(1)}, bf16[32,2048]{1,0:T(8,128)(2,1)S(1)}, u32[]{:S(2)}, u32[]{:S(2)}) collective-permute-start(bf16[32,2048]{1,0:T(8,128)(2,1)S(1)} %fusion.8), channel_id=1, source_target_pairs={{0,8},{4,12},{8,0},{12,4},{16,24},{20,28},{24,16},{28,20},{1,9},{5... | collective-permute-start | bytes 393224 | tf_op jit(solution)/shard_map/ppermute | solution.py:18
  62.4 0.8 %maximum_bitcast_fusion = f32[2048,64]{0,1:T(8,128)} fusion(f32[64,1024]{1,0:T(8,128)S(1)} %get-tuple-element.51, f32[64,1024]{1,0:T(8,128)S(1)} %get-tuple-element.49), kind=kLoop, calls=%fused_computation | loop fusion | flops 131072 | bytes 1048576 | tf_op jit(solution)/shard_map/transpose | solution.py:217
  63.3 3.5 %collective-permute-done.23 = bf16[32,2048]{1,0:T(8,128)(2,1)S(1)} collective-permute-done((bf16[32,2048]{1,0:T(8,128)(2,1)S(1)}, bf16[32,2048]{1,0:T(8,128)(2,1)S(1)}, u32[]{:S(2)}, u32[]{:S(2)}) %collective-permute-start.23) | collective-permute-done | bytes 131104 | tf_op jit(solution)/shard_map/ppermute | solution.py:18
  66.7 0.9 %collective-permute-done.22 = bf16[32,2048]{1,0:T(8,128)(2,1)S(1)} collective-permute-done((bf16[32,2048]{1,0:T(8,128)(2,1)S(1)}, bf16[32,2048]{1,0:T(8,128)(2,1)S(1)}, u32[]{:S(2)}, u32[]{:S(2)}) %collective-permute-start.22) | collective-permute-done | bytes 131104 | tf_op jit(solution)/shard_map/ppermute | solution.py:18
  67.6 0.8 %collective-permute-done.20 = bf16[32,2048]{1,0:T(8,128)(2,1)S(1)} collective-permute-done((bf16[32,2048]{1,0:T(8,128)(2,1)S(1)}, bf16[32,2048]{1,0:T(8,128)(2,1)S(1)}, u32[]{:S(2)}, u32[]{:S(2)}) %collective-permute-start.20) | collective-permute-done | bytes 131104 | tf_op jit(solution)/shard_map/ppermute | solution.py:18
  68.4 0.8 %fusion.12 = f32[2048,32]{0,1:T(8,128)} fusion(f32[64,2048]{1,0:T(8,128)S(1)} %collective-permute-done.19, bf16[32,2048]{1,0:T(8,128)(2,1)S(1)} %collective-permute-done.23, bf16[32,2048]{1,0:T(8,128)(2,1)S(1)} %collective-permute-done.22, bf16[32,2048]{1,0:T(8,128)(2,1)S(1)} %collective-permute-done.20, f32[64,2048]{1,0:T(8,128)S(1)} %get-tuple-element.44), kind=kLoop, calls=%fused_computation.21 | loop fusion | flops 458752 | bytes 1179648 | tf_op jit(solution)/shard_map/transpose | solution.py:217
  (35 shorter events, 4.3 us)
Async XLA Ops:
  0.6 12.9 %copy-start = (bf16[2048,32]{0,1:T(8,128)(2,1)S(1)}, bf16[2048,32]{0,1:T(8,128)(2,1)}, u32[]{:S(2)}) copy-start(bf16[2048,32]{0,1:T(8,128)(2,1)} %param.5) | copy-start | bytes 393220
  0.6 8.7 %collective-permute-start = (bf16[32,2048]{1,0:T(8,128)(2,1)}, bf16[32,2048]{1,0:T(8,128)(2,1)S(1)}, u32[]{:S(2)}, u32[]{:S(2)}) collective-permute-start(bf16[32,2048]{1,0:T(8,128)(2,1)} %bitcast.7), channel_id=1, source_target_pairs={{0,8},{4,12},{8,0},{12,4},{16,24},{20,28},{24,16},{28,20},{1,9},{5... | collective-permute-start | bytes 393224 | tf_op jit(solution)/shard_map/ppermute | solution.py:18
  3.6 8.0 %collective-permute-start.1 = (bf16[32,2048]{1,0:T(8,128)(2,1)}, bf16[32,2048]{1,0:T(8,128)(2,1)S(1)}, u32[]{:S(2)}, u32[]{:S(2)}) collective-permute-start(bf16[32,2048]{1,0:T(8,128)(2,1)} %bitcast.8), channel_id=1, source_target_pairs={{0,16},{4,20},{8,24},{12,28},{16,0},{20,4},{24,8},{28,12},{1,17},{... | collective-permute-start | bytes 393224 | tf_op jit(solution)/shard_map/ppermute | solution.py:18
  5.2 6.5 %collective-permute-start.2 = (bf16[32,2048]{1,0:T(8,128)(2,1)}, bf16[32,2048]{1,0:T(8,128)(2,1)S(1)}, u32[]{:S(2)}, u32[]{:S(2)}) collective-permute-start(bf16[32,2048]{1,0:T(8,128)(2,1)} %bitcast.9), channel_id=1, source_target_pairs={{0,24},{4,28},{8,16},{12,20},{16,8},{20,12},{24,0},{28,4},{1,25},{... | collective-permute-start | bytes 393224 | tf_op jit(solution)/shard_map/ppermute | solution.py:18
  5.2 7.0 %collective-permute-start.3 = (bf16[32,2048]{1,0:T(8,128)(2,1)}, bf16[32,2048]{1,0:T(8,128)(2,1)S(1)}, u32[]{:S(2)}, u32[]{:S(2)}) collective-permute-start(bf16[32,2048]{1,0:T(8,128)(2,1)} %bitcast.10), channel_id=1, source_target_pairs={{0,4},{4,0},{8,12},{12,8},{16,20},{20,16},{24,28},{28,24},{1,5},{5... | collective-permute-start | bytes 393224 | tf_op jit(solution)/shard_map/ppermute | solution.py:18
  11.6 1.3 %collective-permute-start.4 = (bf16[32,2048]{1,0:T(8,128)(2,1)S(1)}, bf16[32,2048]{1,0:T(8,128)(2,1)S(1)}, u32[]{:S(2)}, u32[]{:S(2)}) collective-permute-start(bf16[32,2048]{1,0:T(8,128)(2,1)S(1)} %collective-permute-done.refs_1_), channel_id=1, source_target_pairs={{0,4},{4,0},{8,12},{12,8},{16,20},{20,16},{24,28},{28,24},{1,5},{5... | collective-permute-start | bytes 393224 | tf_op jit(solution)/shard_map/ppermute | solution.py:18
  11.6 1.5 %collective-permute-start.5 = (bf16[32,2048]{1,0:T(8,128)(2,1)S(1)}, bf16[32,2048]{1,0:T(8,128)(2,1)S(1)}, u32[]{:S(2)}, u32[]{:S(2)}) collective-permute-start(bf16[32,2048]{1,0:T(8,128)(2,1)S(1)} %collective-permute-done.1.refs_2_), channel_id=1, source_target_pairs={{0,4},{4,0},{8,12},{12,8},{16,20},{20,16},{24,28},{28,24},{1,5},{5... | collective-permute-start | bytes 393224 | tf_op jit(solution)/shard_map/ppermute | solution.py:18
  12.1 1.3 %collective-permute-start.6 = (bf16[32,2048]{1,0:T(8,128)(2,1)S(1)}, bf16[32,2048]{1,0:T(8,128)(2,1)S(1)}, u32[]{:S(2)}, u32[]{:S(2)}) collective-permute-start(bf16[32,2048]{1,0:T(8,128)(2,1)S(1)} %collective-permute-done.2.refs_3_), channel_id=1, source_target_pairs={{0,4},{4,0},{8,12},{12,8},{16,20},{20,16},{24,28},{28,24},{1,5},{5... | collective-permute-start | bytes 393224 | tf_op jit(solution)/shard_map/ppermute | solution.py:18
  15.4 6.5 %collective-permute-start.7 = (bf16[64,1024]{1,0:T(8,128)(2,1)S(1)}, bf16[64,1024]{1,0:T(8,128)(2,1)S(1)}, u32[]{:S(2)}, u32[]{:S(2)}) collective-permute-start(bf16[64,1024]{1,0:T(8,128)(2,1)S(1)} %get-tuple-element.36), channel_id=1, source_target_pairs={{0,1},{3,2},{2,0},{1,3},{4,5},{7,6},{6,4},{5,7},{8,9},{11,10},{10,... | collective-permute-start | bytes 393224 | tf_op jit(solution)/shard_map/ppermute | solution.py:32
  18.8 8.6 %collective-permute-start.10 = (bf16[64,1024]{1,0:T(8,128)(2,1)S(1)}, bf16[64,1024]{1,0:T(8,128)(2,1)S(1)}, u32[]{:S(2)}, u32[]{:S(2)}) collective-permute-start(bf16[64,1024]{1,0:T(8,128)(2,1)S(1)} %get-tuple-element.42), channel_id=1, source_target_pairs={{0,1},{3,2},{2,0},{1,3},{4,5},{7,6},{6,4},{5,7},{8,9},{11,10},{10,... | collective-permute-start | bytes 393224 | tf_op jit(solution)/shard_map/ppermute | solution.py:32
  22.0 8.9 %collective-permute-start.9 = (bf16[64,1024]{1,0:T(8,128)(2,1)S(1)}, bf16[64,1024]{1,0:T(8,128)(2,1)S(1)}, u32[]{:S(2)}, u32[]{:S(2)}) collective-permute-start(bf16[64,1024]{1,0:T(8,128)(2,1)S(1)} %get-tuple-element.52), channel_id=1, source_target_pairs={{0,3},{1,2},{2,1},{3,0},{4,7},{5,6},{6,5},{7,4},{8,11},{9,10},{10,... | collective-permute-start | bytes 393224 | tf_op jit(solution)/shard_map/ppermute | solution.py:18
  26.3 8.9 %collective-permute-start.8 = (bf16[64,1024]{1,0:T(8,128)(2,1)S(1)}, bf16[64,1024]{1,0:T(8,128)(2,1)S(1)}, u32[]{:S(2)}, u32[]{:S(2)}) collective-permute-start(bf16[64,1024]{1,0:T(8,128)(2,1)S(1)} %get-tuple-element.37), channel_id=1, source_target_pairs={{0,1},{1,0},{2,3},{3,2},{4,5},{5,4},{6,7},{7,6},{8,9},{9,8},{10,11... | collective-permute-start | bytes 393224 | tf_op jit(solution)/shard_map/ppermute | solution.py:18
  27.5 9.3 %collective-permute-start.12 = (bf16[64,1024]{1,0:T(8,128)(2,1)S(1)}, bf16[64,1024]{1,0:T(8,128)(2,1)S(1)}, u32[]{:S(2)}, u32[]{:S(2)}) collective-permute-start(bf16[64,1024]{1,0:T(8,128)(2,1)S(1)} %get-tuple-element.54), channel_id=1, source_target_pairs={{0,3},{1,2},{2,1},{3,0},{4,7},{5,6},{6,5},{7,4},{8,11},{9,10},{10,... | collective-permute-start | bytes 393224 | tf_op jit(solution)/shard_map/ppermute | solution.py:18
  29.1 9.5 %collective-permute-start.11 = (bf16[64,1024]{1,0:T(8,128)(2,1)S(1)}, bf16[64,1024]{1,0:T(8,128)(2,1)S(1)}, u32[]{:S(2)}, u32[]{:S(2)}) collective-permute-start(bf16[64,1024]{1,0:T(8,128)(2,1)S(1)} %get-tuple-element.43), channel_id=1, source_target_pairs={{0,1},{1,0},{2,3},{3,2},{4,5},{5,4},{6,7},{7,6},{8,9},{9,8},{10,11... | collective-permute-start | bytes 393224 | tf_op jit(solution)/shard_map/ppermute | solution.py:18
  35.3 8.2 %collective-permute-start.17 = (bf16[64,1024]{1,0:T(8,128)(2,1)S(1)}, bf16[64,1024]{1,0:T(8,128)(2,1)S(1)}, u32[]{:S(2)}, u32[]{:S(2)}) collective-permute-start(bf16[64,1024]{1,0:T(8,128)(2,1)S(1)} %get-tuple-element.48.refs_0_), channel_id=1, source_target_pairs={{0,3},{1,2},{2,1},{3,0},{4,7},{5,6},{6,5},{7,4},{8,11},{9,10},{10,... | collective-permute-start | bytes 393224 | tf_op jit(solution)/shard_map/ppermute | solution.py:18
  38.7 8.7 %collective-permute-start.14 = (bf16[64,1024]{1,0:T(8,128)(2,1)S(1)}, bf16[64,1024]{1,0:T(8,128)(2,1)S(1)}, u32[]{:S(2)}, u32[]{:S(2)}) collective-permute-start(bf16[64,1024]{1,0:T(8,128)(2,1)S(1)} %get-tuple-element.50.refs_0_), channel_id=1, source_target_pairs={{0,3},{1,2},{2,1},{3,0},{4,7},{5,6},{6,5},{7,4},{8,11},{9,10},{10,... | collective-permute-start | bytes 393224 | tf_op jit(solution)/shard_map/ppermute | solution.py:18
  40.9 14.5 %collective-permute-start.13 = (bf16[64,1024]{1,0:T(8,128)(2,1)S(1)}, bf16[64,1024]{1,0:T(8,128)(2,1)S(1)}, u32[]{:S(2)}, u32[]{:S(2)}) collective-permute-start(bf16[64,1024]{1,0:T(8,128)(2,1)S(1)} %get-tuple-element.50.refs_0_), channel_id=1, source_target_pairs={{0,1},{1,0},{2,3},{3,2},{4,5},{5,4},{6,7},{7,6},{8,9},{9,8},{10,11... | collective-permute-start | bytes 393224 | tf_op jit(solution)/shard_map/ppermute | solution.py:18
  41.5 9.9 %collective-permute-start.16 = (bf16[64,1024]{1,0:T(8,128)(2,1)S(1)}, bf16[64,1024]{1,0:T(8,128)(2,1)S(1)}, u32[]{:S(2)}, u32[]{:S(2)}) collective-permute-start(bf16[64,1024]{1,0:T(8,128)(2,1)S(1)} %get-tuple-element.48.refs_0_), channel_id=1, source_target_pairs={{0,1},{1,0},{2,3},{3,2},{4,5},{5,4},{6,7},{7,6},{8,9},{9,8},{10,11... | collective-permute-start | bytes 393224 | tf_op jit(solution)/shard_map/ppermute | solution.py:18
  43.6 10.0 %collective-permute-start.18 = (bf16[64,1024]{1,0:T(8,128)(2,1)S(1)}, bf16[64,1024]{1,0:T(8,128)(2,1)S(1)}, u32[]{:S(2)}, u32[]{:S(2)}) collective-permute-start(bf16[64,1024]{1,0:T(8,128)(2,1)S(1)} %select_n.26), channel_id=1, source_target_pairs={{0,2},{3,1},{1,0},{2,3},{4,6},{7,5},{5,4},{6,7},{8,10},{11,9},{9,8... | collective-permute-start | bytes 393224 | tf_op jit(solution)/shard_map/ppermute | solution.py:50
  47.5 7.9 %collective-permute-start.15 = (bf16[64,1024]{1,0:T(8,128)(2,1)S(1)}, bf16[64,1024]{1,0:T(8,128)(2,1)S(1)}, u32[]{:S(2)}, u32[]{:S(2)}) collective-permute-start(bf16[64,1024]{1,0:T(8,128)(2,1)S(1)} %select_n.25), channel_id=1, source_target_pairs={{0,2},{3,1},{1,0},{2,3},{4,6},{7,5},{5,4},{6,7},{8,10},{11,9},{9,8... | collective-permute-start | bytes 393224 | tf_op jit(solution)/shard_map/ppermute | solution.py:50
  56.7 2.0 %collective-permute-start.21 = (f32[64,2048]{1,0:T(8,128)S(1)}, f32[64,2048]{1,0:T(8,128)S(1)}, u32[]{:S(2)}, u32[]{:S(2)}) collective-permute-start(f32[64,2048]{1,0:T(8,128)S(1)} %get-tuple-element.47), channel_id=1, source_target_pairs={{0,4},{4,0},{8,12},{12,8},{16,20},{20,16},{24,28},{28,24},{1,5},{5... | collective-permute-start | bytes 1572872 | tf_op jit(solution)/shard_map/ppermute | solution.py:18
  56.8 4.7 %collective-permute-start.19 = (f32[64,2048]{1,0:T(8,128)S(1)}, f32[64,2048]{1,0:T(8,128)S(1)}, u32[]{:S(2)}, u32[]{:S(2)}) collective-permute-start(f32[64,2048]{1,0:T(8,128)S(1)} %get-tuple-element.45), channel_id=1, source_target_pairs={{0,4},{4,0},{8,12},{12,8},{16,20},{20,16},{24,28},{28,24},{1,5},{5... | collective-permute-start | bytes 1572872 | tf_op jit(solution)/shard_map/ppermute | solution.py:18
  58.8 7.9 %collective-permute-start.23 = (bf16[32,2048]{1,0:T(8,128)(2,1)S(1)}, bf16[32,2048]{1,0:T(8,128)(2,1)S(1)}, u32[]{:S(2)}, u32[]{:S(2)}) collective-permute-start(bf16[32,2048]{1,0:T(8,128)(2,1)S(1)} %get-tuple-element.57), channel_id=1, source_target_pairs={{0,16},{4,20},{8,24},{12,28},{16,0},{20,4},{24,8},{28,12},{1,17},{... | collective-permute-start | bytes 393224 | tf_op jit(solution)/shard_map/ppermute | solution.py:18
  60.4 7.3 %collective-permute-start.22 = (bf16[32,2048]{1,0:T(8,128)(2,1)S(1)}, bf16[32,2048]{1,0:T(8,128)(2,1)S(1)}, u32[]{:S(2)}, u32[]{:S(2)}) collective-permute-start(bf16[32,2048]{1,0:T(8,128)(2,1)S(1)} %get-tuple-element.56), channel_id=1, source_target_pairs={{0,24},{4,28},{8,16},{12,20},{16,8},{20,12},{24,0},{28,4},{1,25},{... | collective-permute-start | bytes 393224 | tf_op jit(solution)/shard_map/ppermute | solution.py:18
  61.5 6.9 %collective-permute-start.20 = (bf16[32,2048]{1,0:T(8,128)(2,1)S(1)}, bf16[32,2048]{1,0:T(8,128)(2,1)S(1)}, u32[]{:S(2)}, u32[]{:S(2)}) collective-permute-start(bf16[32,2048]{1,0:T(8,128)(2,1)S(1)} %fusion.8), channel_id=1, source_target_pairs={{0,8},{4,12},{8,0},{12,4},{16,24},{20,28},{24,16},{28,20},{1,9},{5... | collective-permute-start | bytes 393224 | tf_op jit(solution)/shard_map/ppermute | solution.py:18

commit v17 on v15

--- a/solution.py
+++ b/solution.py
@@ -10,7 +10,6 @@
 F32, BF16 = jnp.float32, jnp.bfloat16
 VMEM_LIMIT = 28 * 2**20
 STEP = 512
-CHUNKS = 2
 
 
 def exchange(value, axis, offset):
@@ -26,20 +25,21 @@
     return lax.optimization_barrier((value, earlier))[0]
 
 
-def window_sums(terms, ends):
+def window_sums(terms, ends, earlier):
     size = len(terms)
+    came = ends
     if size == 4:
         came = lax.ppermute(terms[2], "col", [(0, 1), (3, 2), (2, 0), (1, 3)])
-        came = came.astype(F32)
-        onward = terms[3] + jnp.where(ends > 0, 0.0, came)
+        extra = came.astype(F32)
+        onward = terms[3] + jnp.where(ends > 0, 0.0, extra)
         onward = onward.astype(BF16)
         far = exchange(onward, "col", 3).astype(F32)
         near = exchange(after(terms[1], onward), "col", 1).astype(F32)
-        return terms[0] + near + far + jnp.where(ends > 0, came, 0.0)
+        return after(terms[0], earlier) + near + far + jnp.where(ends > 0, extra, 0.0), came
     total = terms[0]
     for offset in range(1, size):
         total = total + exchange(terms[offset].astype(BF16), "col", offset).astype(F32)
-    return total
+    return total, came
 
 
 def window_spread(lowered, ends, size):
@@ -107,9 +107,8 @@
             out[:, at] = term[k * share : (k + 1) * share].astype(out.dtype)
 
 
-def partial_sketch(where, tiles, blocks, token, offsets_row, offsets_col, chunk, chunks):
-    rows, cols = tiles.shape
-    rows //= chunks
+def partial_sketch(where, tiles, blocks, token, offsets_row, offsets_col, base, rows):
+    cols = tiles.shape[1]
     width = blocks[0].shape[0] * len(blocks)
     share = width // len(offsets_col)
     vmem = pl.BlockSpec(memory_space=pltpu.VMEM)
@@ -117,7 +116,7 @@
     outs = [jax.ShapeDtypeStruct((share, rows), F32 if offset in exact else BF16) for offset in offsets_col]
     outs.append(jax.ShapeDtypeStruct((share, rows), F32))
     return pl.pallas_call(
-        functools.partial(sketch_kernel, base=chunk * rows, offsets_row=offsets_row, offsets_col=offsets_col),
+        functools.partial(sketch_kernel, base=base, offsets_row=offsets_row, offsets_col=offsets_col),
         in_specs=[pl.BlockSpec(memory_space=pltpu.SMEM)] + [vmem] * (2 + len(blocks)),
         out_specs=[vmem] * len(outs),
         out_shape=outs,
@@ -150,15 +149,14 @@
             out[:, at] = term[k * height : (k + 1) * height]
 
 
-def partial_adjoint(where, tiles, shares, earlier, offsets_col, devices, chunk, chunks):
-    rows, cols = tiles.shape
-    rows //= chunks
-    width = shares[0].shape[0] * len(offsets_col)
-    parts = 4 if chunk == chunks - 1 else 1
+def partial_adjoint(where, tiles, shares, earlier, parts, offsets_col, devices, base):
+    cols = tiles.shape[1]
+    share, rows = shares[0].shape
+    width = share * len(offsets_col)
     vmem = pl.BlockSpec(memory_space=pltpu.VMEM)
     return pl.pallas_call(
         functools.partial(
-            adjoint_kernel, base=chunk * rows, parts=parts, offsets_col=offsets_col, devices=devices
+            adjoint_kernel, base=base, parts=parts, offsets_col=offsets_col, devices=devices
         ),
         in_specs=[pl.BlockSpec(memory_space=pltpu.SMEM)] + [vmem] * (1 + len(shares) + len(earlier)),
         out_specs=[vmem] * parts,
@@ -172,11 +170,16 @@
     )(where, tiles, *shares, *earlier)
 
 
+def chunk_cuts(rows):
+    quarter = rows // 4
+    return [(0, quarter), (quarter, 2 * quarter), (3 * quarter, quarter)]
+
+
 def local(green, mask, probes):
     n_row, n_col = lax.axis_size("row"), lax.axis_size("col")
     where = jnp.stack([lax.axis_index("row"), lax.axis_index("col")]).astype(jnp.int32)
     own_width = probes.shape[1]
-    chunks = CHUNKS if green.shape[0] % (CHUNKS * STEP) == 0 else 1
+    cuts = chunk_cuts(green.shape[0])
     offsets_col = list(range(n_col))
     offsets_core = list(range(0, n_row, 2))
     gather_core = [0] + offsets_core[:0:-1]
@@ -189,15 +192,21 @@
     held, token = lax.optimization_barrier((held, token))
     blocks = held + [twin] + [exchange(block, "row", 1) for block in held[1:]]
 
-    totals, shares = [], []
-    for chunk in range(chunks):
-        *parts, ends = partial_sketch(where, tiles, blocks, token, offsets_row, offsets_col, chunk, chunks)
-        totals.append(window_sums(parts, ends))
+    totals, shares, firsts = [], [], []
+    earlier = token
+    for base, rows in cuts:
+        *parts, ends = partial_sketch(where, tiles, blocks, token, offsets_row, offsets_col, base, rows)
+        total, came = window_sums(parts, ends, earlier)
+        token = after(ends, firsts[0]) if firsts else ends
+        firsts.append(came)
+        totals.append(total)
         shares.append(window_spread(totals[-1].astype(BF16), ends, n_col))
+        earlier = shares[-1][-1 if len(shares) == 1 else 0]
 
     earlier = []
-    for chunk in range(chunks):
-        earlier = partial_adjoint(where, tiles, shares[chunk], earlier, offsets_col, n_row, chunk, chunks)
+    for chunk, (base, rows) in enumerate(cuts):
+        parts = 4 if chunk == len(cuts) - 1 else 1
+        earlier = partial_adjoint(where, tiles, shares[chunk], earlier, parts, offsets_col, n_row, base)
     pairs = []
     for mine, others in (earlier[1::2], earlier[::2]):
         others = exchange(others, "row", 1)

time: 69.7 us -> 73.2 us (1.050)
  starting transfers between devices: 32.6 us -> 36.7 us
  waiting for transfers between devices: 22.3 us -> 20.2 us
  Pallas kernels: 11.6 us -> 13.1 us
    ppermute x20 -> x24, starting transfers between devices: 20.9 us -> 23.7 us  [exchange(): return lax.ppermute(value, axis, [(i, i ^ offset) for i in range(size)])]
    ppermute x2 -> x3, waiting for transfers between devices: 2.47 us -> 0.01 us  [window_spread(): lax.ppermute(onward, 'col', [(0, 2), (3, 1), (1, 0), (2, 3)])]
    ppermute x2 -> x3, starting transfers between devices: 4.26 us -> 6.35 us  [window_sums(): came = lax.ppermute(terms[2], 'col', [(0, 1), (3, 2), (2, 0), (1, 3)])]
    ppermute x20 -> x24, waiting for transfers between devices: 18.4 us -> 20.2 us  [exchange(): return lax.ppermute(value, axis, [(i, i ^ offset) for i in range(size)])]
    pallas_call x4 -> x6, Pallas kernels: 7.39 us -> 8.88 us  [the longest x3 4.47 us: partial_sketch(): pl.pallas_call(functools.partial(sketch_kernel, base=base, offsets_row=of...]
    ppermute x2 -> x3, waiting for transfers between devices: 1.49 us -> 0.01 us  [window_sums(): came = lax.ppermute(terms[2], 'col', [(0, 1), (3, 2), (2, 0), (1, 3)])]
    ppermute x2 -> x3, starting transfers between devices: 7.45 us -> 6.68 us  [window_spread(): lax.ppermute(onward, 'col', [(0, 2), (3, 1), (1, 0), (2, 3)])]
  transfers between devices with their start and end apart: 24 -> 30, of which waited for: 14 -> 11; matrix products, arithmetic and copies ran while one was open for 2% -> 2% of each run, Pallas kernels for 11% -> 14%
where the time goes in v17:
time: 73.2 us; the launch traced here: 73 us
  starting transfers between devices  36.7 us (50%)
  waiting for transfers between devices  20.2 us (28%)
  Pallas kernels  13.1 us (18%)
  other arithmetic  2.22 us (3%)
  between operations  0.8 us (1%)
    ppermute x24, starting transfers between devices, exchange(): return lax.ppermute(value, axis, [(i, i ^ offset) for i in range(size)])  23.7 us
    ppermute x24, waiting for transfers between devices, exchange(): return lax.ppermute(value, axis, [(i, i ^ offset) for i in range(size)])  20.2 us
    ppermute x3, starting transfers between devices, window_spread(): lax.ppermute(onward, 'col', [(0, 2), (3, 1), (1, 0), (2, 3)])  6.68 us
    ppermute x3, starting transfers between devices, window_sums(): came = lax.ppermute(terms[2], 'col', [(0, 1), (3, 2), (2, 0), (1, 3)])  6.35 us
    pallas_call x3, Pallas kernels, partial_sketch(): pl.pallas_call(functools.partial(sketch_kernel, base=base, offsets_row=of...  4.47 us
    pallas_call x3, Pallas kernels, partial_adjoint(): pl.pallas_call(functools.partial(adjoint_kernel, base=base, parts=parts,...  4.41 us
    pallas_call x1, Pallas kernels, masked(): pl.pallas_call(functools.partial(mask_kernel, block=rows // mask.shape[0]...  4.19 us
    transpose x2, other arithmetic, local(): return (jnp.concatenate(totals, axis=1).T, adjoint.T)  1.61 us
  transfers between devices with their start and end apart: 30, of which 11 were waited for; matrix products, arithmetic and copies ran while one was open for 2% of the time, Pallas kernels for 14%

profile of v17, /device:TPU:0, one launch (start us, length us, event | category | flops | bytes accessed | tf_op | source)
XLA Modules:
  0.0 73.0 jit_solution(14730769666735327058)
XLA Ops:
  0.6 3.0 %collective-permute-start.2 = (bf16[32,2048]{1,0:T(8,128)(2,1)}, bf16[32,2048]{1,0:T(8,128)(2,1)S(1)}, u32[]{:S(2)}, u32[]{:S(2)}) collective-permute-start(bf16[32,2048]{1,0:T(8,128)(2,1)} %bitcast.7), channel_id=1, source_target_pairs={{0,8},{4,12},{8,0},{12,4},{16,24},{20,28},{24,16},{28,20},{1,9},{5... | collective-permute-start | bytes 393224 | tf_op jit(solution)/shard_map/ppermute | solution.py:17
  3.6 1.5 %collective-permute-start.1 = (bf16[32,2048]{1,0:T(8,128)(2,1)}, bf16[32,2048]{1,0:T(8,128)(2,1)S(1)}, u32[]{:S(2)}, u32[]{:S(2)}) collective-permute-start(bf16[32,2048]{1,0:T(8,128)(2,1)} %bitcast.8), channel_id=1, source_target_pairs={{0,16},{4,20},{8,24},{12,28},{16,0},{20,4},{24,8},{28,12},{1,17},{... | collective-permute-start | bytes 393224 | tf_op jit(solution)/shard_map/ppermute | solution.py:17
  5.3 4.2 %masked_tiles.1 = (bf16[2048,2048]{1,0:T(8,128)(2,1)S(1)}, f32[8,128]{1,0:T(8,128)S(1)}) custom-call(s32[2]{0:T(128)S(1)} %pad_add_fusion.where, s32[8,8]{1,0:T(8,128)} %mask_hbm.1, bf16[2048,2048]{1,0:T(8,128)(2,1)} %green_ref.1), custom_call_target="tpu_custom_call" | custom-call | bytes 8388608 | tf_op jit(solution)/shard_map/masked_tiles/pallas_call | solution.py:77
  9.5 2.2 %collective-permute-done.1.refs_2_ = bf16[32,2048]{1,0:T(8,128)(2,1)S(1)} collective-permute-done((bf16[32,2048]{1,0:T(8,128)(2,1)}, bf16[32,2048]{1,0:T(8,128)(2,1)S(1)}, u32[]{:S(2)}, u32[]{:S(2)}) %collective-permute-start.1) | collective-permute-done | bytes 131104 | tf_op jit(solution)/shard_map/ppermute | solution.py:17
  13.5 1.3 %partial_sketch.3 = (f32[64,512]{1,0:T(8,128)S(1)}, bf16[64,512]{1,0:T(8,128)(2,1)S(1)}, bf16[64,512]{1,0:T(8,128)(2,1)S(1)}, f32[64,512]{1,0:T(8,128)S(1)}, f32[64,512]{1,0:T(8,128)S(1)}) custom-call(s32[2]{0:T(128)S(1)} %pad_add_fusion.where, bf16[2048,2048]{1,0:T(8,128)(2,1)S(1)} %get-tuple-element.35.tiles, f32[8,128]{1,0:T(8,128)S(1)} %get-tuple-element.37.token, ...), custom_call_target="tpu_custom_call" | custom-call | flops 536870912 | bytes 2097152 | tf_op jit(solution)/shard_map/partial_sketch/pallas_call | solution.py:118
  14.8 1.6 %collective-permute-start.7 = (bf16[64,512]{1,0:T(8,128)(2,1)S(1)}, bf16[64,512]{1,0:T(8,128)(2,1)S(1)}, u32[]{:S(2)}, u32[]{:S(2)}) collective-permute-start(bf16[64,512]{1,0:T(8,128)(2,1)S(1)} %get-tuple-element.47), channel_id=1, source_target_pairs={{0,1},{3,2},{2,0},{1,3},{4,5},{7,6},{6,4},{5,7},{8,9},{11,10},{10,... | collective-permute-start | bytes 196616 | tf_op jit(solution)/shard_map/ppermute | solution.py:32
  16.4 1.9 %partial_sketch.4 = (f32[64,1024]{1,0:T(8,128)S(1)}, bf16[64,1024]{1,0:T(8,128)(2,1)S(1)}, bf16[64,1024]{1,0:T(8,128)(2,1)S(1)}, f32[64,1024]{1,0:T(8,128)S(1)}, f32[64,1024]{1,0:T(8,128)S(1)}) custom-call(s32[2]{0:T(128)S(1)} %pad_add_fusion.where, bf16[2048,2048]{1,0:T(8,128)(2,1)S(1)} %get-tuple-element.35.tiles, f32[64,512]{1,0:T(8,128)S(1)} %get-tuple-element.46.token, ...), custom_call_target="tpu_custom_call" | custom-call | flops 1073741824 | bytes 4194304 | tf_op jit(solution)/shard_map/partial_sketch/pallas_call | solution.py:118
  18.3 2.6 %collective-permute-start.11 = (bf16[64,1024]{1,0:T(8,128)(2,1)S(1)}, bf16[64,1024]{1,0:T(8,128)(2,1)S(1)}, u32[]{:S(2)}, u32[]{:S(2)}) collective-permute-start(bf16[64,1024]{1,0:T(8,128)(2,1)S(1)} %get-tuple-element.54), channel_id=1, source_target_pairs={{0,1},{3,2},{2,0},{1,3},{4,5},{7,6},{6,4},{5,7},{8,9},{11,10},{10,... | collective-permute-start | bytes 393224 | tf_op jit(solution)/shard_map/ppermute | solution.py:32
  21.0 2.7 %collective-permute-start.9 = (bf16[64,512]{1,0:T(8,128)(2,1)S(1)}, bf16[64,512]{1,0:T(8,128)(2,1)S(1)}, u32[]{:S(2)}, u32[]{:S(2)}) collective-permute-start(bf16[64,512]{1,0:T(8,128)(2,1)S(1)} %get-tuple-element.74), channel_id=1, source_target_pairs={{0,3},{1,2},{2,1},{3,0},{4,7},{5,6},{6,5},{7,4},{8,11},{9,10},{10,... | collective-permute-start | bytes 196616 | tf_op jit(solution)/shard_map/ppermute | solution.py:17
  23.7 1.3 %partial_sketch.5 = (f32[64,512]{1,0:T(8,128)S(1)}, bf16[64,512]{1,0:T(8,128)(2,1)S(1)}, bf16[64,512]{1,0:T(8,128)(2,1)S(1)}, f32[64,512]{1,0:T(8,128)S(1)}, f32[64,512]{1,0:T(8,128)S(1)}) custom-call(s32[2]{0:T(128)S(1)} %pad_add_fusion.where, bf16[2048,2048]{1,0:T(8,128)(2,1)S(1)} %get-tuple-element.35.tiles, f32[64,1024]{1,0:T(8,128)S(1)} %get-tuple-element.56.token, ...), custom_call_target="tpu_custom_call" | custom-call | flops 536870912 | bytes 2097152 | tf_op jit(solution)/shard_map/partial_sketch/pallas_call | solution.py:118
  25.1 2.1 %collective-permute-start.14 = (bf16[64,512]{1,0:T(8,128)(2,1)S(1)}, bf16[64,512]{1,0:T(8,128)(2,1)S(1)}, u32[]{:S(2)}, u32[]{:S(2)}) collective-permute-start(bf16[64,512]{1,0:T(8,128)(2,1)S(1)} %get-tuple-element.62), channel_id=1, source_target_pairs={{0,1},{3,2},{2,0},{1,3},{4,5},{7,6},{6,4},{5,7},{8,9},{11,10},{10,... | collective-permute-start | bytes 196616 | tf_op jit(solution)/shard_map/ppermute | solution.py:32
  27.2 1.3 %collective-permute-start.13 = (bf16[64,1024]{1,0:T(8,128)(2,1)S(1)}, bf16[64,1024]{1,0:T(8,128)(2,1)S(1)}, u32[]{:S(2)}, u32[]{:S(2)}) collective-permute-start(bf16[64,1024]{1,0:T(8,128)(2,1)S(1)} %get-tuple-element.76), channel_id=1, source_target_pairs={{0,3},{1,2},{2,1},{3,0},{4,7},{5,6},{6,5},{7,4},{8,11},{9,10},{10,... | collective-permute-start | bytes 393224 | tf_op jit(solution)/shard_map/ppermute | solution.py:17
  28.8 2.4 %collective-permute-start.10 = (bf16[64,512]{1,0:T(8,128)(2,1)S(1)}, bf16[64,512]{1,0:T(8,128)(2,1)S(1)}, u32[]{:S(2)}, u32[]{:S(2)}) collective-permute-start(bf16[64,512]{1,0:T(8,128)(2,1)S(1)} %get-tuple-element.72.refs_0_), channel_id=1, source_target_pairs={{0,3},{1,2},{2,1},{3,0},{4,7},{5,6},{6,5},{7,4},{8,11},{9,10},{10,... | collective-permute-start | bytes 196616 | tf_op jit(solution)/shard_map/ppermute | solution.py:17
  31.3 2.7 %collective-permute-start.16 = (bf16[64,512]{1,0:T(8,128)(2,1)S(1)}, bf16[64,512]{1,0:T(8,128)(2,1)S(1)}, u32[]{:S(2)}, u32[]{:S(2)}) collective-permute-start(bf16[64,512]{1,0:T(8,128)(2,1)S(1)} %get-tuple-element.78), channel_id=1, source_target_pairs={{0,3},{1,2},{2,1},{3,0},{4,7},{5,6},{6,5},{7,4},{8,11},{9,10},{10,... | collective-permute-start | bytes 196616 | tf_op jit(solution)/shard_map/ppermute | solution.py:17
  34.0 5.1 %collective-permute-done.10.refs_3_ = bf16[64,512]{1,0:T(8,128)(2,1)S(1)} collective-permute-done((bf16[64,512]{1,0:T(8,128)(2,1)S(1)}, bf16[64,512]{1,0:T(8,128)(2,1)S(1)}, u32[]{:S(2)}, u32[]{:S(2)}) %collective-permute-start.10) | collective-permute-done | bytes 65568 | tf_op jit(solution)/shard_map/ppermute | solution.py:17
  39.3 1.8 %collective-permute-start.21 = (bf16[64,1024]{1,0:T(8,128)(2,1)S(1)}, bf16[64,1024]{1,0:T(8,128)(2,1)S(1)}, u32[]{:S(2)}, u32[]{:S(2)}) collective-permute-start(bf16[64,1024]{1,0:T(8,128)(2,1)S(1)} %get-tuple-element.70.refs_0_), channel_id=1, source_target_pairs={{0,3},{1,2},{2,1},{3,0},{4,7},{5,6},{6,5},{7,4},{8,11},{9,10},{10,... | collective-permute-start | bytes 393224 | tf_op jit(solution)/shard_map/ppermute | solution.py:17
  42.0 1.3 %collective-permute-start.18 = (bf16[64,512]{1,0:T(8,128)(2,1)S(1)}, bf16[64,512]{1,0:T(8,128)(2,1)S(1)}, u32[]{:S(2)}, u32[]{:S(2)}) collective-permute-start(bf16[64,512]{1,0:T(8,128)(2,1)S(1)} %get-tuple-element.68.refs_0_), channel_id=1, source_target_pairs={{0,3},{1,2},{2,1},{3,0},{4,7},{5,6},{6,5},{7,4},{8,11},{9,10},{10,... | collective-permute-start | bytes 196616 | tf_op jit(solution)/shard_map/ppermute | solution.py:17
  43.3 3.1 %collective-permute-done.21.refs_3_ = bf16[64,1024]{1,0:T(8,128)(2,1)S(1)} collective-permute-done((bf16[64,1024]{1,0:T(8,128)(2,1)S(1)}, bf16[64,1024]{1,0:T(8,128)(2,1)S(1)}, u32[]{:S(2)}, u32[]{:S(2)}) %collective-permute-start.21) | collective-permute-done | bytes 131104 | tf_op jit(solution)/shard_map/ppermute | solution.py:17
  46.4 4.5 %collective-permute-start.22 = (bf16[64,1024]{1,0:T(8,128)(2,1)S(1)}, bf16[64,1024]{1,0:T(8,128)(2,1)S(1)}, u32[]{:S(2)}, u32[]{:S(2)}) collective-permute-start(bf16[64,1024]{1,0:T(8,128)(2,1)S(1)} %select_n.40), channel_id=1, source_target_pairs={{0,2},{3,1},{1,0},{2,3},{4,6},{7,5},{5,4},{6,7},{8,10},{11,9},{9,8... | collective-permute-start | bytes 393224 | tf_op jit(solution)/shard_map/ppermute | solution.py:50
  50.9 1.1 %collective-permute-start.24 = (bf16[64,512]{1,0:T(8,128)(2,1)S(1)}, bf16[64,512]{1,0:T(8,128)(2,1)S(1)}, u32[]{:S(2)}, u32[]{:S(2)}) collective-permute-start(bf16[64,512]{1,0:T(8,128)(2,1)S(1)} %select_n.41), channel_id=1, source_target_pairs={{0,2},{3,1},{1,0},{2,3},{4,6},{7,5},{5,4},{6,7},{8,10},{11,9},{9,8... | collective-permute-start | bytes 196616 | tf_op jit(solution)/shard_map/ppermute | solution.py:50
  52.0 1.1 %collective-permute-start.17 = (bf16[64,512]{1,0:T(8,128)(2,1)S(1)}, bf16[64,512]{1,0:T(8,128)(2,1)S(1)}, u32[]{:S(2)}, u32[]{:S(2)}) collective-permute-start(bf16[64,512]{1,0:T(8,128)(2,1)S(1)} %get-tuple-element.68.refs_0_), channel_id=1, source_target_pairs={{0,1},{1,0},{2,3},{3,2},{4,5},{5,4},{6,7},{7,6},{8,9},{9,8},{10,11... | collective-permute-start | bytes 196616 | tf_op jit(solution)/shard_map/ppermute | solution.py:17
  53.1 2.0 %collective-permute-done.23.refs_1_ = bf16[64,512]{1,0:T(8,128)(2,1)S(1)} collective-permute-done((bf16[64,512]{1,0:T(8,128)(2,1)S(1)}, bf16[64,512]{1,0:T(8,128)(2,1)S(1)}, u32[]{:S(2)}, u32[]{:S(2)}) %collective-permute-start.23) | collective-permute-done | bytes 65568 | tf_op jit(solution)/shard_map/ppermute | solution.py:17
  55.1 1.1 %collective-permute-start.19 = (bf16[64,512]{1,0:T(8,128)(2,1)S(1)}, bf16[64,512]{1,0:T(8,128)(2,1)S(1)}, u32[]{:S(2)}, u32[]{:S(2)}) collective-permute-start(bf16[64,512]{1,0:T(8,128)(2,1)S(1)} %select_n.39), channel_id=1, source_target_pairs={{0,2},{3,1},{1,0},{2,3},{4,6},{7,5},{5,4},{6,7},{8,10},{11,9},{9,8... | collective-permute-start | bytes 196616 | tf_op jit(solution)/shard_map/ppermute | solution.py:50
  56.3 1.3 %partial_adjoint.3.refs_4_ = f32[256,2048]{1,0:T(8,128)S(1)} custom-call(s32[2]{0:T(128)S(1)} %pad_add_fusion.where, bf16[2048,2048]{1,0:T(8,128)(2,1)S(1)} %get-tuple-element.35.tiles, bf16[64,512]{1,0:T(8,128)(2,1)S(1)} %get-tuple-element.72.refs_0_, bf16[64,512]{1,0:T(8,128)(2,1)S(1)} %collective-permute-done.23.refs_1_, ...), custom_call_target="tpu_custom_call" | custom-call | tf_op jit(solution)/shard_map/partial_adjoint/pallas_call | solution.py:157
  57.6 1.9 %partial_adjoint.4.refs_4_ = f32[256,2048]{1,0:T(8,128)S(1)} custom-call(s32[2]{0:T(128)S(1)} %pad_add_fusion.where, bf16[2048,2048]{1,0:T(8,128)(2,1)S(1)} %get-tuple-element.35.tiles, bf16[64,1024]{1,0:T(8,128)(2,1)S(1)} %get-tuple-element.70.refs_0_, bf16[64,1024]{1,0:T(8,128)(2,1)S(1)} %collective-permute-done.20.refs_1_, ...), custom_call_target="tpu_custom_call" | custom-call | tf_op jit(solution)/shard_map/partial_adjoint/pallas_call | solution.py:157
  59.4 1.3 %partial_adjoint.5 = (f32[64,2048]{1,0:T(8,128)S(1)}, f32[64,2048]{1,0:T(8,128)S(1)}, f32[64,2048]{1,0:T(8,128)S(1)}, f32[64,2048]{1,0:T(8,128)S(1)}) custom-call(s32[2]{0:T(128)S(1)} %pad_add_fusion.where, bf16[2048,2048]{1,0:T(8,128)(2,1)S(1)} %get-tuple-element.35.tiles, bf16[64,512]{1,0:T(8,128)(2,1)S(1)} %get-tuple-element.68.refs_0_, ...), custom_call_target="tpu_custom_call" | custom-call | tf_op jit(solution)/shard_map/partial_adjoint/pallas_call | solution.py:157
  61.3 1.4 %collective-permute-done.25 = f32[64,2048]{1,0:T(8,128)S(1)} collective-permute-done((f32[64,2048]{1,0:T(8,128)S(1)}, f32[64,2048]{1,0:T(8,128)S(1)}, u32[]{:S(2)}, u32[]{:S(2)}) %collective-permute-start.25) | collective-permute-done | bytes 524320 | tf_op jit(solution)/shard_map/ppermute | solution.py:17
  62.7 1.3 %collective-permute-start.26 = (bf16[32,2048]{1,0:T(8,128)(2,1)S(1)}, bf16[32,2048]{1,0:T(8,128)(2,1)S(1)}, u32[]{:S(2)}, u32[]{:S(2)}) collective-permute-start(bf16[32,2048]{1,0:T(8,128)(2,1)S(1)} %fusion.5), channel_id=1, source_target_pairs={{0,8},{4,12},{8,0},{12,4},{16,24},{20,28},{24,16},{28,20},{1,9},{5... | collective-permute-start | bytes 393224 | tf_op jit(solution)/shard_map/ppermute | solution.py:17
  65.1 1.3 %collective-permute-start.29 = (bf16[32,2048]{1,0:T(8,128)(2,1)S(1)}, bf16[32,2048]{1,0:T(8,128)(2,1)S(1)}, u32[]{:S(2)}, u32[]{:S(2)}) collective-permute-start(bf16[32,2048]{1,0:T(8,128)(2,1)S(1)} %get-tuple-element.81), channel_id=1, source_target_pairs={{0,24},{4,28},{8,16},{12,20},{16,8},{20,12},{24,0},{28,4},{1,25},{... | collective-permute-start | bytes 393224 | tf_op jit(solution)/shard_map/ppermute | solution.py:17
  67.3 1.6 %collective-permute-done.26 = bf16[32,2048]{1,0:T(8,128)(2,1)S(1)} collective-permute-done((bf16[32,2048]{1,0:T(8,128)(2,1)S(1)}, bf16[32,2048]{1,0:T(8,128)(2,1)S(1)}, u32[]{:S(2)}, u32[]{:S(2)}) %collective-permute-start.26) | collective-permute-done | bytes 131104 | tf_op jit(solution)/shard_map/ppermute | solution.py:17
  68.8 2.2 %collective-permute-done.28 = bf16[32,2048]{1,0:T(8,128)(2,1)S(1)} collective-permute-done((bf16[32,2048]{1,0:T(8,128)(2,1)S(1)}, bf16[32,2048]{1,0:T(8,128)(2,1)S(1)}, u32[]{:S(2)}, u32[]{:S(2)}) %collective-permute-start.28) | collective-permute-done | bytes 131104 | tf_op jit(solution)/shard_map/ppermute | solution.py:17
  71.0 1.2 %collective-permute-done.29 = bf16[32,2048]{1,0:T(8,128)(2,1)S(1)} collective-permute-done((bf16[32,2048]{1,0:T(8,128)(2,1)S(1)}, bf16[32,2048]{1,0:T(8,128)(2,1)S(1)}, u32[]{:S(2)}, u32[]{:S(2)}) %collective-permute-start.29) | collective-permute-done | bytes 131104 | tf_op jit(solution)/shard_map/ppermute | solution.py:17
  (51 shorter events, 6.9 us)
Async XLA Ops:
  0.6 12.9 %copy-start = (bf16[2048,32]{0,1:T(8,128)(2,1)S(1)}, bf16[2048,32]{0,1:T(8,128)(2,1)}, u32[]{:S(2)}) copy-start(bf16[2048,32]{0,1:T(8,128)(2,1)} %param.5) | copy-start | bytes 393220
  0.6 8.8 %collective-permute-start.2 = (bf16[32,2048]{1,0:T(8,128)(2,1)}, bf16[32,2048]{1,0:T(8,128)(2,1)S(1)}, u32[]{:S(2)}, u32[]{:S(2)}) collective-permute-start(bf16[32,2048]{1,0:T(8,128)(2,1)} %bitcast.7), channel_id=1, source_target_pairs={{0,8},{4,12},{8,0},{12,4},{16,24},{20,28},{24,16},{28,20},{1,9},{5... | collective-permute-start | bytes 393224 | tf_op jit(solution)/shard_map/ppermute | solution.py:17
  3.6 8.0 %collective-permute-start.1 = (bf16[32,2048]{1,0:T(8,128)(2,1)}, bf16[32,2048]{1,0:T(8,128)(2,1)S(1)}, u32[]{:S(2)}, u32[]{:S(2)}) collective-permute-start(bf16[32,2048]{1,0:T(8,128)(2,1)} %bitcast.8), channel_id=1, source_target_pairs={{0,16},{4,20},{8,24},{12,28},{16,0},{20,4},{24,8},{28,12},{1,17},{... | collective-permute-start | bytes 393224 | tf_op jit(solution)/shard_map/ppermute | solution.py:17
  5.2 6.5 %collective-permute-start = (bf16[32,2048]{1,0:T(8,128)(2,1)}, bf16[32,2048]{1,0:T(8,128)(2,1)S(1)}, u32[]{:S(2)}, u32[]{:S(2)}) collective-permute-start(bf16[32,2048]{1,0:T(8,128)(2,1)} %bitcast.9), channel_id=1, source_target_pairs={{0,24},{4,28},{8,16},{12,20},{16,8},{20,12},{24,0},{28,4},{1,25},{... | collective-permute-start | bytes 393224 | tf_op jit(solution)/shard_map/ppermute | solution.py:17
  5.2 7.0 %collective-permute-start.3 = (bf16[32,2048]{1,0:T(8,128)(2,1)}, bf16[32,2048]{1,0:T(8,128)(2,1)S(1)}, u32[]{:S(2)}, u32[]{:S(2)}) collective-permute-start(bf16[32,2048]{1,0:T(8,128)(2,1)} %bitcast.10), channel_id=1, source_target_pairs={{0,4},{4,0},{8,12},{12,8},{16,20},{20,16},{24,28},{28,24},{1,5},{5... | collective-permute-start | bytes 393224 | tf_op jit(solution)/shard_map/ppermute | solution.py:17
  11.6 1.3 %collective-permute-start.4 = (bf16[32,2048]{1,0:T(8,128)(2,1)S(1)}, bf16[32,2048]{1,0:T(8,128)(2,1)S(1)}, u32[]{:S(2)}, u32[]{:S(2)}) collective-permute-start(bf16[32,2048]{1,0:T(8,128)(2,1)S(1)} %collective-permute-done.refs_1_), channel_id=1, source_target_pairs={{0,4},{4,0},{8,12},{12,8},{16,20},{20,16},{24,28},{28,24},{1,5},{5... | collective-permute-start | bytes 393224 | tf_op jit(solution)/shard_map/ppermute | solution.py:17
  11.6 1.5 %collective-permute-start.5 = (bf16[32,2048]{1,0:T(8,128)(2,1)S(1)}, bf16[32,2048]{1,0:T(8,128)(2,1)S(1)}, u32[]{:S(2)}, u32[]{:S(2)}) collective-permute-start(bf16[32,2048]{1,0:T(8,128)(2,1)S(1)} %collective-permute-done.1.refs_2_), channel_id=1, source_target_pairs={{0,4},{4,0},{8,12},{12,8},{16,20},{20,16},{24,28},{28,24},{1,5},{5... | collective-permute-start | bytes 393224 | tf_op jit(solution)/shard_map/ppermute | solution.py:17
  12.1 1.3 %collective-permute-start.6 = (bf16[32,2048]{1,0:T(8,128)(2,1)S(1)}, bf16[32,2048]{1,0:T(8,128)(2,1)S(1)}, u32[]{:S(2)}, u32[]{:S(2)}) collective-permute-start(bf16[32,2048]{1,0:T(8,128)(2,1)S(1)} %collective-permute-done.2.refs_3_), channel_id=1, source_target_pairs={{0,4},{4,0},{8,12},{12,8},{16,20},{20,16},{24,28},{28,24},{1,5},{5... | collective-permute-start | bytes 393224 | tf_op jit(solution)/shard_map/ppermute | solution.py:17
  14.8 6.1 %collective-permute-start.7 = (bf16[64,512]{1,0:T(8,128)(2,1)S(1)}, bf16[64,512]{1,0:T(8,128)(2,1)S(1)}, u32[]{:S(2)}, u32[]{:S(2)}) collective-permute-start(bf16[64,512]{1,0:T(8,128)(2,1)S(1)} %get-tuple-element.47), channel_id=1, source_target_pairs={{0,1},{3,2},{2,0},{1,3},{4,5},{7,6},{6,4},{5,7},{8,9},{11,10},{10,... | collective-permute-start | bytes 196616 | tf_op jit(solution)/shard_map/ppermute | solution.py:32
  18.3 8.8 %collective-permute-start.11 = (bf16[64,1024]{1,0:T(8,128)(2,1)S(1)}, bf16[64,1024]{1,0:T(8,128)(2,1)S(1)}, u32[]{:S(2)}, u32[]{:S(2)}) collective-permute-start(bf16[64,1024]{1,0:T(8,128)(2,1)S(1)} %get-tuple-element.54), channel_id=1, source_target_pairs={{0,1},{3,2},{2,0},{1,3},{4,5},{7,6},{6,4},{5,7},{8,9},{11,10},{10,... | collective-permute-start | bytes 393224 | tf_op jit(solution)/shard_map/ppermute | solution.py:32
  21.0 7.8 %collective-permute-start.9 = (bf16[64,512]{1,0:T(8,128)(2,1)S(1)}, bf16[64,512]{1,0:T(8,128)(2,1)S(1)}, u32[]{:S(2)}, u32[]{:S(2)}) collective-permute-start(bf16[64,512]{1,0:T(8,128)(2,1)S(1)} %get-tuple-element.74), channel_id=1, source_target_pairs={{0,3},{1,2},{2,1},{3,0},{4,7},{5,6},{6,5},{7,4},{8,11},{9,10},{10,... | collective-permute-start | bytes 196616 | tf_op jit(solution)/shard_map/ppermute | solution.py:17
  23.7 5.0 %collective-permute-start.8 = (bf16[64,512]{1,0:T(8,128)(2,1)S(1)}, bf16[64,512]{1,0:T(8,128)(2,1)S(1)}, u32[]{:S(2)}, u32[]{:S(2)}) collective-permute-start(bf16[64,512]{1,0:T(8,128)(2,1)S(1)} %get-tuple-element.48), channel_id=1, source_target_pairs={{0,1},{1,0},{2,3},{3,2},{4,5},{5,4},{6,7},{7,6},{8,9},{9,8},{10,11... | collective-permute-start | bytes 196616 | tf_op jit(solution)/shard_map/ppermute | solution.py:17
  25.1 6.2 %collective-permute-start.14 = (bf16[64,512]{1,0:T(8,128)(2,1)S(1)}, bf16[64,512]{1,0:T(8,128)(2,1)S(1)}, u32[]{:S(2)}, u32[]{:S(2)}) collective-permute-start(bf16[64,512]{1,0:T(8,128)(2,1)S(1)} %get-tuple-element.62), channel_id=1, source_target_pairs={{0,1},{3,2},{2,0},{1,3},{4,5},{7,6},{6,4},{5,7},{8,9},{11,10},{10,... | collective-permute-start | bytes 196616 | tf_op jit(solution)/shard_map/ppermute | solution.py:32
  27.2 12.0 %collective-permute-start.13 = (bf16[64,1024]{1,0:T(8,128)(2,1)S(1)}, bf16[64,1024]{1,0:T(8,128)(2,1)S(1)}, u32[]{:S(2)}, u32[]{:S(2)}) collective-permute-start(bf16[64,1024]{1,0:T(8,128)(2,1)S(1)} %get-tuple-element.76), channel_id=1, source_target_pairs={{0,3},{1,2},{2,1},{3,0},{4,7},{5,6},{6,5},{7,4},{8,11},{9,10},{10,... | collective-permute-start | bytes 393224 | tf_op jit(solution)/shard_map/ppermute | solution.py:17
  28.5 10.6 %collective-permute-start.12 = (bf16[64,1024]{1,0:T(8,128)(2,1)S(1)}, bf16[64,1024]{1,0:T(8,128)(2,1)S(1)}, u32[]{:S(2)}, u32[]{:S(2)}) collective-permute-start(bf16[64,1024]{1,0:T(8,128)(2,1)S(1)} %get-tuple-element.55), channel_id=1, source_target_pairs={{0,1},{1,0},{2,3},{3,2},{4,5},{5,4},{6,7},{7,6},{8,9},{9,8},{10,11... | collective-permute-start | bytes 393224 | tf_op jit(solution)/shard_map/ppermute | solution.py:17
  28.8 10.3 %collective-permute-start.10 = (bf16[64,512]{1,0:T(8,128)(2,1)S(1)}, bf16[64,512]{1,0:T(8,128)(2,1)S(1)}, u32[]{:S(2)}, u32[]{:S(2)}) collective-permute-start(bf16[64,512]{1,0:T(8,128)(2,1)S(1)} %get-tuple-element.72.refs_0_), channel_id=1, source_target_pairs={{0,3},{1,2},{2,1},{3,0},{4,7},{5,6},{6,5},{7,4},{8,11},{9,10},{10,... | collective-permute-start | bytes 196616 | tf_op jit(solution)/shard_map/ppermute | solution.py:17
  31.3 10.7 %collective-permute-start.16 = (bf16[64,512]{1,0:T(8,128)(2,1)S(1)}, bf16[64,512]{1,0:T(8,128)(2,1)S(1)}, u32[]{:S(2)}, u32[]{:S(2)}) collective-permute-start(bf16[64,512]{1,0:T(8,128)(2,1)S(1)} %get-tuple-element.78), channel_id=1, source_target_pairs={{0,3},{1,2},{2,1},{3,0},{4,7},{5,6},{6,5},{7,4},{8,11},{9,10},{10,... | collective-permute-start | bytes 196616 | tf_op jit(solution)/shard_map/ppermute | solution.py:17
  34.0 7.9 %collective-permute-start.15 = (bf16[64,512]{1,0:T(8,128)(2,1)S(1)}, bf16[64,512]{1,0:T(8,128)(2,1)S(1)}, u32[]{:S(2)}, u32[]{:S(2)}) collective-permute-start(bf16[64,512]{1,0:T(8,128)(2,1)S(1)} %get-tuple-element.63), channel_id=1, source_target_pairs={{0,1},{1,0},{2,3},{3,2},{4,5},{5,4},{6,7},{7,6},{8,9},{9,8},{10,11... | collective-permute-start | bytes 196616 | tf_op jit(solution)/shard_map/ppermute | solution.py:17
  39.3 7.1 %collective-permute-start.21 = (bf16[64,1024]{1,0:T(8,128)(2,1)S(1)}, bf16[64,1024]{1,0:T(8,128)(2,1)S(1)}, u32[]{:S(2)}, u32[]{:S(2)}) collective-permute-start(bf16[64,1024]{1,0:T(8,128)(2,1)S(1)} %get-tuple-element.70.refs_0_), channel_id=1, source_target_pairs={{0,3},{1,2},{2,1},{3,0},{4,7},{5,6},{6,5},{7,4},{8,11},{9,10},{10,... | collective-permute-start | bytes 393224 | tf_op jit(solution)/shard_map/ppermute | solution.py:17
  41.0 16.5 %collective-permute-start.20 = (bf16[64,1024]{1,0:T(8,128)(2,1)S(1)}, bf16[64,1024]{1,0:T(8,128)(2,1)S(1)}, u32[]{:S(2)}, u32[]{:S(2)}) collective-permute-start(bf16[64,1024]{1,0:T(8,128)(2,1)S(1)} %get-tuple-element.70.refs_0_), channel_id=1, source_target_pairs={{0,1},{1,0},{2,3},{3,2},{4,5},{5,4},{6,7},{7,6},{8,9},{9,8},{10,11... | collective-permute-start | bytes 393224 | tf_op jit(solution)/shard_map/ppermute | solution.py:17
  42.0 10.0 %collective-permute-start.18 = (bf16[64,512]{1,0:T(8,128)(2,1)S(1)}, bf16[64,512]{1,0:T(8,128)(2,1)S(1)}, u32[]{:S(2)}, u32[]{:S(2)}) collective-permute-start(bf16[64,512]{1,0:T(8,128)(2,1)S(1)} %get-tuple-element.68.refs_0_), channel_id=1, source_target_pairs={{0,3},{1,2},{2,1},{3,0},{4,7},{5,6},{6,5},{7,4},{8,11},{9,10},{10,... | collective-permute-start | bytes 196616 | tf_op jit(solution)/shard_map/ppermute | solution.py:17
  46.4 11.2 %collective-permute-start.22 = (bf16[64,1024]{1,0:T(8,128)(2,1)S(1)}, bf16[64,1024]{1,0:T(8,128)(2,1)S(1)}, u32[]{:S(2)}, u32[]{:S(2)}) collective-permute-start(bf16[64,1024]{1,0:T(8,128)(2,1)S(1)} %select_n.40), channel_id=1, source_target_pairs={{0,2},{3,1},{1,0},{2,3},{4,6},{7,5},{5,4},{6,7},{8,10},{11,9},{9,8... | collective-permute-start | bytes 393224 | tf_op jit(solution)/shard_map/ppermute | solution.py:50
  50.9 4.3 %collective-permute-start.23 = (bf16[64,512]{1,0:T(8,128)(2,1)S(1)}, bf16[64,512]{1,0:T(8,128)(2,1)S(1)}, u32[]{:S(2)}, u32[]{:S(2)}) collective-permute-start(bf16[64,512]{1,0:T(8,128)(2,1)S(1)} %get-tuple-element.72.refs_0_), channel_id=1, source_target_pairs={{0,1},{1,0},{2,3},{3,2},{4,5},{5,4},{6,7},{7,6},{8,9},{9,8},{10,11... | collective-permute-start | bytes 196616 | tf_op jit(solution)/shard_map/ppermute | solution.py:17
  50.9 5.4 %collective-permute-start.24 = (bf16[64,512]{1,0:T(8,128)(2,1)S(1)}, bf16[64,512]{1,0:T(8,128)(2,1)S(1)}, u32[]{:S(2)}, u32[]{:S(2)}) collective-permute-start(bf16[64,512]{1,0:T(8,128)(2,1)S(1)} %select_n.41), channel_id=1, source_target_pairs={{0,2},{3,1},{1,0},{2,3},{4,6},{7,5},{5,4},{6,7},{8,10},{11,9},{9,8... | collective-permute-start | bytes 196616 | tf_op jit(solution)/shard_map/ppermute | solution.py:50
  52.0 7.4 %collective-permute-start.17 = (bf16[64,512]{1,0:T(8,128)(2,1)S(1)}, bf16[64,512]{1,0:T(8,128)(2,1)S(1)}, u32[]{:S(2)}, u32[]{:S(2)}) collective-permute-start(bf16[64,512]{1,0:T(8,128)(2,1)S(1)} %get-tuple-element.68.refs_0_), channel_id=1, source_target_pairs={{0,1},{1,0},{2,3},{3,2},{4,5},{5,4},{6,7},{7,6},{8,9},{9,8},{10,11... | collective-permute-start | bytes 196616 | tf_op jit(solution)/shard_map/ppermute | solution.py:17
  55.1 4.3 %collective-permute-start.19 = (bf16[64,512]{1,0:T(8,128)(2,1)S(1)}, bf16[64,512]{1,0:T(8,128)(2,1)S(1)}, u32[]{:S(2)}, u32[]{:S(2)}) collective-permute-start(bf16[64,512]{1,0:T(8,128)(2,1)S(1)} %select_n.39), channel_id=1, source_target_pairs={{0,2},{3,1},{1,0},{2,3},{4,6},{7,5},{5,4},{6,7},{8,10},{11,9},{9,8... | collective-permute-start | bytes 196616 | tf_op jit(solution)/shard_map/ppermute | solution.py:50
  60.7 2.0 %collective-permute-start.25 = (f32[64,2048]{1,0:T(8,128)S(1)}, f32[64,2048]{1,0:T(8,128)S(1)}, u32[]{:S(2)}, u32[]{:S(2)}) collective-permute-start(f32[64,2048]{1,0:T(8,128)S(1)} %get-tuple-element.65), channel_id=1, source_target_pairs={{0,4},{4,0},{8,12},{12,8},{16,20},{20,16},{24,28},{28,24},{1,5},{5... | collective-permute-start | bytes 1572872 | tf_op jit(solution)/shard_map/ppermute | solution.py:17
  60.8 3.2 %collective-permute-start.27 = (f32[64,2048]{1,0:T(8,128)S(1)}, f32[64,2048]{1,0:T(8,128)S(1)}, u32[]{:S(2)}, u32[]{:S(2)}) collective-permute-start(f32[64,2048]{1,0:T(8,128)S(1)} %get-tuple-element.67), channel_id=1, source_target_pairs={{0,4},{4,0},{8,12},{12,8},{16,20},{20,16},{24,28},{28,24},{1,5},{5... | collective-permute-start | bytes 1572872 | tf_op jit(solution)/shard_map/ppermute | solution.py:17
  62.7 6.1 %collective-permute-start.26 = (bf16[32,2048]{1,0:T(8,128)(2,1)S(1)}, bf16[32,2048]{1,0:T(8,128)(2,1)S(1)}, u32[]{:S(2)}, u32[]{:S(2)}) collective-permute-start(bf16[32,2048]{1,0:T(8,128)(2,1)S(1)} %fusion.5), channel_id=1, source_target_pairs={{0,8},{4,12},{8,0},{12,4},{16,24},{20,28},{24,16},{28,20},{1,9},{5... | collective-permute-start | bytes 393224 | tf_op jit(solution)/shard_map/ppermute | solution.py:17
  64.1 6.9 %collective-permute-start.28 = (bf16[32,2048]{1,0:T(8,128)(2,1)S(1)}, bf16[32,2048]{1,0:T(8,128)(2,1)S(1)}, u32[]{:S(2)}, u32[]{:S(2)}) collective-permute-start(bf16[32,2048]{1,0:T(8,128)(2,1)S(1)} %get-tuple-element.80), channel_id=1, source_target_pairs={{0,16},{4,20},{8,24},{12,28},{16,0},{20,4},{24,8},{28,12},{1,17},{... | collective-permute-start | bytes 393224 | tf_op jit(solution)/shard_map/ppermute | solution.py:17
  65.1 7.1 %collective-permute-start.29 = (bf16[32,2048]{1,0:T(8,128)(2,1)S(1)}, bf16[32,2048]{1,0:T(8,128)(2,1)S(1)}, u32[]{:S(2)}, u32[]{:S(2)}) collective-permute-start(bf16[32,2048]{1,0:T(8,128)(2,1)S(1)} %get-tuple-element.81), channel_id=1, source_target_pairs={{0,24},{4,28},{8,16},{12,20},{16,8},{20,12},{24,0},{28,4},{1,25},{... | collective-permute-start | bytes 393224 | tf_op jit(solution)/shard_map/ppermute | solution.py:17

commit v18 on v15

--- a/solution.py
+++ b/solution.py
@@ -18,8 +18,9 @@
     return lax.ppermute(value, axis, [(i, i ^ offset) for i in range(size)])
 
 
-def at_end(where, size):
-    return (where[1] == 0) | (where[1] == size - 1)
+def at_end(size):
+    place = lax.axis_index("col")
+    return (place == 0) | (place == size - 1)
 
 
 def after(value, earlier):
@@ -51,7 +52,7 @@
     return [lowered] + [exchange(lowered, "col", offset) for offset in range(1, size)]
 
 
-def mask_kernel(where, mask_hbm, green_ref, tiles, token, mask_ref, mask_sem, sems, *, block):
+def mask_kernel(mask_hbm, green_ref, tiles, token, mask_ref, mask_sem, sems, *, block):
     rows, cols = tiles.shape
     token[...] = jnp.zeros(token.shape, token.dtype)
     levels = pltpu.make_async_copy(mask_hbm, mask_ref, mask_sem)
@@ -72,11 +73,11 @@
                     tiles[i * block : (i + 1) * block, j * block : (j + 1) * block] = jnp.zeros((block, block), BF16)
 
 
-def masked(where, green, mask):
+def masked(green, mask):
     rows, cols = green.shape
     return pl.pallas_call(
         functools.partial(mask_kernel, block=rows // mask.shape[0]),
-        in_specs=[pl.BlockSpec(memory_space=pltpu.SMEM)] + [pl.BlockSpec(memory_space=pltpu.HBM)] * 2,
+        in_specs=[pl.BlockSpec(memory_space=pltpu.HBM)] * 2,
         out_specs=[pl.BlockSpec(memory_space=pltpu.VMEM)] * 2,
         out_shape=[pltpu.VMEM((rows, cols), BF16), jax.ShapeDtypeStruct((8, 128), F32)],
         scratch_shapes=[
@@ -87,18 +88,19 @@
         compiler_params=pltpu.CompilerParams(vmem_limit_bytes=VMEM_LIMIT),
         cost_estimate=pl.CostEstimate(flops=0, bytes_accessed=2 * rows * cols, transcendentals=0),
         name="masked_tiles",
-    )(where, *(pltpu.with_memory_space_constraint(array, pltpu.HBM) for array in (mask, green)))
-
-
-def sketch_kernel(where, tiles, token, *refs, base, offsets_row, offsets_col):
+    )(*(pltpu.with_memory_space_constraint(array, pltpu.HBM) for array in (mask, green)))
+
+
+def sketch_kernel(tiles, token, *refs, base, offsets_row, offsets_col):
     blocks, outs, ends, probes = refs[: len(offsets_row)], refs[len(offsets_row) : -2], refs[-2], refs[-1]
     own = blocks[0].shape[0]
     ratio = len(offsets_row) // len(offsets_col)
     share = own * ratio
-    ends[...] = jnp.full(ends.shape, at_end(where, len(offsets_col)).astype(F32))
+    ends[...] = jnp.full(ends.shape, at_end(len(offsets_col)).astype(F32))
+    row, col = lax.axis_index("row"), lax.axis_index("col")
     for offset, ref in zip(offsets_row, blocks):
-        column = where[0] ^ offset
-        start = (lax.div(column, ratio) ^ where[1]) * share + lax.rem(column, ratio) * own
+        column = row ^ offset
+        start = (lax.div(column, ratio) ^ col) * share + lax.rem(column, ratio) * own
         probes[pl.ds(pl.multiple_of(start, own), own), :] = ref[...]
     for step in range(ends.shape[1] // STEP):
         rows, at = slice(base + step * STEP, base + (step + 1) * STEP), slice(step * STEP, (step + 1) * STEP)
@@ -107,7 +109,7 @@
             out[:, at] = term[k * share : (k + 1) * share].astype(out.dtype)
 
 
-def partial_sketch(where, tiles, blocks, token, offsets_row, offsets_col, chunk, chunks):
+def partial_sketch(tiles, blocks, token, offsets_row, offsets_col, chunk, chunks):
     rows, cols = tiles.shape
     rows //= chunks
     width = blocks[0].shape[0] * len(blocks)
@@ -118,7 +120,7 @@
     outs.append(jax.ShapeDtypeStruct((share, rows), F32))
     return pl.pallas_call(
         functools.partial(sketch_kernel, base=chunk * rows, offsets_row=offsets_row, offsets_col=offsets_col),
-        in_specs=[pl.BlockSpec(memory_space=pltpu.SMEM)] + [vmem] * (2 + len(blocks)),
+        in_specs=[vmem] * (2 + len(blocks)),
         out_specs=[vmem] * len(outs),
         out_shape=outs,
         scratch_shapes=[pltpu.VMEM((width, cols), BF16)],
@@ -127,17 +129,18 @@
             flops=2 * width * cols * rows, bytes_accessed=2 * rows * cols, transcendentals=0
         ),
         name="partial_sketch",
-    )(where, tiles, token, *blocks)
-
-
-def adjoint_kernel(where, tiles, *refs, base, parts, offsets_col, devices):
+    )(tiles, token, *blocks)
+
+
+def adjoint_kernel(tiles, *refs, base, parts, offsets_col, devices):
     shares, earlier, outs, lowered = refs[: len(offsets_col)], refs[len(offsets_col) : -1 - parts], refs[-1 - parts : -1], refs[-1]
     share, rows = shares[0].shape
     ratio = devices // len(offsets_col)
     own = share // ratio
+    row, col = lax.axis_index("row"), lax.axis_index("col")
     for offset, ref in zip(offsets_col, shares):
         for n in range(ratio):
-            apart = where[0] ^ ((where[1] ^ offset) * ratio + n)
+            apart = row ^ ((col ^ offset) * ratio + n)
             start = ((apart >> 1) + (apart & 1) * (devices // 2)) * own
             lowered[pl.ds(pl.multiple_of(start, own), own), :] = ref[n * own : (n + 1) * own, :]
     for step in range(tiles.shape[1] // STEP):
@@ -150,7 +153,7 @@
             out[:, at] = term[k * height : (k + 1) * height]
 
 
-def partial_adjoint(where, tiles, shares, earlier, offsets_col, devices, chunk, chunks):
+def partial_adjoint(tiles, shares, earlier, offsets_col, devices, chunk, chunks):
     rows, cols = tiles.shape
     rows //= chunks
     width = shares[0].shape[0] * len(offsets_col)
@@ -160,7 +163,7 @@
         functools.partial(
             adjoint_kernel, base=chunk * rows, parts=parts, offsets_col=offsets_col, devices=devices
         ),
-        in_specs=[pl.BlockSpec(memory_space=pltpu.SMEM)] + [vmem] * (1 + len(shares) + len(earlier)),
+        in_specs=[vmem] * (1 + len(shares) + len(earlier)),
         out_specs=[vmem] * parts,
         out_shape=[jax.ShapeDtypeStruct((width // parts, cols), F32)] * parts,
         scratch_shapes=[pltpu.VMEM((width, rows), BF16)],
@@ -169,19 +172,18 @@
             flops=0, bytes_accessed=0, transcendentals=0
         ),
         name="partial_adjoint",
-    )(where, tiles, *shares, *earlier)
+    )(tiles, *shares, *earlier)
 
 
 def local(green, mask, probes):
     n_row, n_col = lax.axis_size("row"), lax.axis_size("col")
-    where = jnp.stack([lax.axis_index("row"), lax.axis_index("col")]).astype(jnp.int32)
     own_width = probes.shape[1]
     chunks = CHUNKS if green.shape[0] % (CHUNKS * STEP) == 0 else 1
     offsets_col = list(range(n_col))
     offsets_core = list(range(0, n_row, 2))
     gather_core = [0] + offsets_core[:0:-1]
     offsets_row = gather_core + [offset ^ 1 for offset in gather_core]
-    tiles, token = masked(where, green, mask)
+    tiles, token = masked(green, mask)
 
     own = probes.T
     held = [own] + [exchange(own, "row", offset) for offset in gather_core[1:]]
@@ -191,13 +193,13 @@
 
     totals, shares = [], []
     for chunk in range(chunks):
-        *parts, ends = partial_sketch(where, tiles, blocks, token, offsets_row, offsets_col, chunk, chunks)
+        *parts, ends = partial_sketch(tiles, blocks, token, offsets_row, offsets_col, chunk, chunks)
         totals.append(window_sums(parts, ends))
         shares.append(window_spread(totals[-1].astype(BF16), ends, n_col))
 
     earlier = []
     for chunk in range(chunks):
-        earlier = partial_adjoint(where, tiles, shares[chunk], earlier, offsets_col, n_row, chunk, chunks)
+        earlier = partial_adjoint(tiles, shares[chunk], earlier, offsets_col, n_row, chunk, chunks)
     pairs = []
     for mine, others in (earlier[1::2], earlier[::2]):
         others = exchange(others, "row", 1)

time: 69.7 us -> 68.2 us (0.978)
  Pallas kernels: 11.6 us -> 8.81 us
  starting transfers between devices: 32.6 us -> 34 us
    ppermute x20, starting transfers between devices: 20.9 us -> 22.2 us  [exchange(): return lax.ppermute(value, axis, [(i, i ^ offset) for i in range(size)])]
    pallas_call x2, Pallas kernels: 3.68 us -> 2.53 us  [partial_adjoint(): pl.pallas_call(functools.partial(adjoint_kernel, base=chunk * rows, parts...]
    pallas_call x2, Pallas kernels: 3.71 us -> 2.63 us  [partial_sketch(): pl.pallas_call(functools.partial(sketch_kernel, base=chunk * rows, offset...]
  transfers between devices with their start and end apart: 24 -> 24, of which waited for: 14 -> 13; matrix products, arithmetic and copies ran while one was open for 2% -> 2% of each run, Pallas kernels for 11% -> 9%
where the time goes in v18:
time: 68.2 us; the launch traced here: 68 us
  starting transfers between devices  34 us (50%)
  waiting for transfers between devices  22.3 us (33%)
  Pallas kernels  8.81 us (13%)
  other arithmetic  2.14 us (3%)
  between operations  0.75 us (1%)
    ppermute x20, starting transfers between devices, exchange(): return lax.ppermute(value, axis, [(i, i ^ offset) for i in range(size)])  22.2 us
    ppermute x20, waiting for transfers between devices, exchange(): return lax.ppermute(value, axis, [(i, i ^ offset) for i in range(size)])  18.7 us
    ppermute x2, starting transfers between devices, window_spread(): lax.ppermute(onward, 'col', [(0, 2), (3, 1), (1, 0), (2, 3)])  7.58 us
    ppermute x2, starting transfers between devices, window_sums(): came = lax.ppermute(terms[2], 'col', [(0, 1), (3, 2), (2, 0), (1, 3)])  4.28 us
    pallas_call x1, Pallas kernels, masked(): pl.pallas_call(functools.partial(mask_kernel, block=rows // mask.shape[0]...  3.65 us
    pallas_call x2, Pallas kernels, partial_sketch(): pl.pallas_call(functools.partial(sketch_kernel, base=chunk * rows, offset...  2.63 us
    ppermute x2, waiting for transfers between devices, window_spread(): lax.ppermute(onward, 'col', [(0, 2), (3, 1), (1, 0), (2, 3)])  2.54 us
    pallas_call x2, Pallas kernels, partial_adjoint(): pl.pallas_call(functools.partial(adjoint_kernel, base=chunk * rows, parts...  2.53 us
  transfers between devices with their start and end apart: 24, of which 13 were waited for; matrix products, arithmetic and copies ran while one was open for 2% of the time, Pallas kernels for 9%

profile of v18, /device:TPU:0, one launch (start us, length us, event | category | flops | bytes accessed | tf_op | source)
XLA Modules:
  0.0 68.0 jit_solution(17716639184205126488)
XLA Ops:
  0.6 3.0 %collective-permute-start.2 = (bf16[32,2048]{1,0:T(8,128)(2,1)}, bf16[32,2048]{1,0:T(8,128)(2,1)S(1)}, u32[]{:S(2)}, u32[]{:S(2)}) collective-permute-start(bf16[32,2048]{1,0:T(8,128)(2,1)} %bitcast.5), channel_id=1, source_target_pairs={{0,8},{4,12},{8,0},{12,4},{16,24},{20,28},{24,16},{28,20},{1,9},{5... | collective-permute-start | bytes 393224 | tf_op jit(solution)/shard_map/ppermute | solution.py:18
  3.6 1.5 %collective-permute-start.1 = (bf16[32,2048]{1,0:T(8,128)(2,1)}, bf16[32,2048]{1,0:T(8,128)(2,1)S(1)}, u32[]{:S(2)}, u32[]{:S(2)}) collective-permute-start(bf16[32,2048]{1,0:T(8,128)(2,1)} %bitcast.6), channel_id=1, source_target_pairs={{0,16},{4,20},{8,24},{12,28},{16,0},{20,4},{24,8},{28,12},{1,17},{... | collective-permute-start | bytes 393224 | tf_op jit(solution)/shard_map/ppermute | solution.py:18
  5.2 3.7 %masked_tiles.1 = (bf16[2048,2048]{1,0:T(8,128)(2,1)S(1)}, f32[8,128]{1,0:T(8,128)S(1)}) custom-call(s32[8,8]{1,0:T(8,128)} %mask_hbm.1, bf16[2048,2048]{1,0:T(8,128)(2,1)} %green_ref.1), custom_call_target="tpu_custom_call" | custom-call | bytes 8388608 | tf_op jit(solution)/shard_map/masked_tiles/pallas_call | solution.py:78
  8.9 2.8 %collective-permute-done.1.refs_2_ = bf16[32,2048]{1,0:T(8,128)(2,1)S(1)} collective-permute-done((bf16[32,2048]{1,0:T(8,128)(2,1)}, bf16[32,2048]{1,0:T(8,128)(2,1)S(1)}, u32[]{:S(2)}, u32[]{:S(2)}) %collective-permute-start.1) | collective-permute-done | bytes 131104 | tf_op jit(solution)/shard_map/ppermute | solution.py:18
  11.6 0.5 collective-permute-start.5
  12.2 0.8 %collective-permute-done.4.refs_5_ = bf16[32,2048]{1,0:T(8,128)(2,1)S(1)} collective-permute-done((bf16[32,2048]{1,0:T(8,128)(2,1)S(1)}, bf16[32,2048]{1,0:T(8,128)(2,1)S(1)}, u32[]{:S(2)}, u32[]{:S(2)}) %collective-permute-start.4) | collective-permute-done | bytes 131104 | tf_op jit(solution)/shard_map/ppermute | solution.py:18
  13.5 1.3 %partial_sketch.2 = (f32[64,1024]{1,0:T(8,128)S(1)}, bf16[64,1024]{1,0:T(8,128)(2,1)S(1)}, bf16[64,1024]{1,0:T(8,128)(2,1)S(1)}, f32[64,1024]{1,0:T(8,128)S(1)}, f32[64,1024]{1,0:T(8,128)S(1)}) custom-call(bf16[2048,2048]{1,0:T(8,128)(2,1)S(1)} %get-tuple-element.25.tiles, f32[8,128]{1,0:T(8,128)S(1)} %get-tuple-element.27.token, ...), custom_call_target="tpu_custom_call" | custom-call | flops 1073741824 | bytes 4194304 | tf_op jit(solution)/shard_map/partial_sketch/pallas_call | solution.py:121
  14.8 1.6 %collective-permute-start.7 = (bf16[64,1024]{1,0:T(8,128)(2,1)S(1)}, bf16[64,1024]{1,0:T(8,128)(2,1)S(1)}, u32[]{:S(2)}, u32[]{:S(2)}) collective-permute-start(bf16[64,1024]{1,0:T(8,128)(2,1)S(1)} %get-tuple-element.36), channel_id=1, source_target_pairs={{0,1},{3,2},{2,0},{1,3},{4,5},{7,6},{6,4},{5,7},{8,9},{11,10},{10,... | collective-permute-start | bytes 393224 | tf_op jit(solution)/shard_map/ppermute | solution.py:33
  16.5 1.3 %partial_sketch.3 = (f32[64,1024]{1,0:T(8,128)S(1)}, bf16[64,1024]{1,0:T(8,128)(2,1)S(1)}, bf16[64,1024]{1,0:T(8,128)(2,1)S(1)}, f32[64,1024]{1,0:T(8,128)S(1)}, f32[64,1024]{1,0:T(8,128)S(1)}) custom-call(bf16[2048,2048]{1,0:T(8,128)(2,1)S(1)} %get-tuple-element.25.tiles, f32[8,128]{1,0:T(8,128)S(1)} %get-tuple-element.27.token, ...), custom_call_target="tpu_custom_call" | custom-call | flops 1073741824 | bytes 4194304 | tf_op jit(solution)/shard_map/partial_sketch/pallas_call | solution.py:121
  17.8 2.6 %collective-permute-start.10 = (bf16[64,1024]{1,0:T(8,128)(2,1)S(1)}, bf16[64,1024]{1,0:T(8,128)(2,1)S(1)}, u32[]{:S(2)}, u32[]{:S(2)}) collective-permute-start(bf16[64,1024]{1,0:T(8,128)(2,1)S(1)} %get-tuple-element.42), channel_id=1, source_target_pairs={{0,1},{3,2},{2,0},{1,3},{4,5},{7,6},{6,4},{5,7},{8,9},{11,10},{10,... | collective-permute-start | bytes 393224 | tf_op jit(solution)/shard_map/ppermute | solution.py:33
  20.4 1.0 %collective-permute-done.7 = bf16[64,1024]{1,0:T(8,128)(2,1)S(1)} collective-permute-done((bf16[64,1024]{1,0:T(8,128)(2,1)S(1)}, bf16[64,1024]{1,0:T(8,128)(2,1)S(1)}, u32[]{:S(2)}, u32[]{:S(2)}) %collective-permute-start.7) | collective-permute-done | bytes 131104 | tf_op jit(solution)/shard_map/ppermute | solution.py:33
  21.5 4.3 %collective-permute-start.9 = (bf16[64,1024]{1,0:T(8,128)(2,1)S(1)}, bf16[64,1024]{1,0:T(8,128)(2,1)S(1)}, u32[]{:S(2)}, u32[]{:S(2)}) collective-permute-start(bf16[64,1024]{1,0:T(8,128)(2,1)S(1)} %get-tuple-element.52), channel_id=1, source_target_pairs={{0,3},{1,2},{2,1},{3,0},{4,7},{5,6},{6,5},{7,4},{8,11},{9,10},{10,... | collective-permute-start | bytes 393224 | tf_op jit(solution)/shard_map/ppermute | solution.py:18
  25.9 2.7 %collective-permute-start.12 = (bf16[64,1024]{1,0:T(8,128)(2,1)S(1)}, bf16[64,1024]{1,0:T(8,128)(2,1)S(1)}, u32[]{:S(2)}, u32[]{:S(2)}) collective-permute-start(bf16[64,1024]{1,0:T(8,128)(2,1)S(1)} %get-tuple-element.54), channel_id=1, source_target_pairs={{0,3},{1,2},{2,1},{3,0},{4,7},{5,6},{6,5},{7,4},{8,11},{9,10},{10,... | collective-permute-start | bytes 393224 | tf_op jit(solution)/shard_map/ppermute | solution.py:18
  28.7 5.9 %collective-permute-done.8 = bf16[64,1024]{1,0:T(8,128)(2,1)S(1)} collective-permute-done((bf16[64,1024]{1,0:T(8,128)(2,1)S(1)}, bf16[64,1024]{1,0:T(8,128)(2,1)S(1)}, u32[]{:S(2)}, u32[]{:S(2)}) %collective-permute-start.8) | collective-permute-done | bytes 131104 | tf_op jit(solution)/shard_map/ppermute | solution.py:18
  34.7 1.6 %collective-permute-start.17 = (bf16[64,1024]{1,0:T(8,128)(2,1)S(1)}, bf16[64,1024]{1,0:T(8,128)(2,1)S(1)}, u32[]{:S(2)}, u32[]{:S(2)}) collective-permute-start(bf16[64,1024]{1,0:T(8,128)(2,1)S(1)} %get-tuple-element.48.refs_0_), channel_id=1, source_target_pairs={{0,3},{1,2},{2,1},{3,0},{4,7},{5,6},{6,5},{7,4},{8,11},{9,10},{10,... | collective-permute-start | bytes 393224 | tf_op jit(solution)/shard_map/ppermute | solution.py:18
  36.2 1.8 %collective-permute-done.11 = bf16[64,1024]{1,0:T(8,128)(2,1)S(1)} collective-permute-done((bf16[64,1024]{1,0:T(8,128)(2,1)S(1)}, bf16[64,1024]{1,0:T(8,128)(2,1)S(1)}, u32[]{:S(2)}, u32[]{:S(2)}) %collective-permute-start.11) | collective-permute-done | bytes 131104 | tf_op jit(solution)/shard_map/ppermute | solution.py:18
  38.2 2.3 %collective-permute-start.14 = (bf16[64,1024]{1,0:T(8,128)(2,1)S(1)}, bf16[64,1024]{1,0:T(8,128)(2,1)S(1)}, u32[]{:S(2)}, u32[]{:S(2)}) collective-permute-start(bf16[64,1024]{1,0:T(8,128)(2,1)S(1)} %get-tuple-element.50.refs_0_), channel_id=1, source_target_pairs={{0,3},{1,2},{2,1},{3,0},{4,7},{5,6},{6,5},{7,4},{8,11},{9,10},{10,... | collective-permute-start | bytes 393224 | tf_op jit(solution)/shard_map/ppermute | solution.py:18
  40.4 0.5 collective-permute-start.16
  41.0 1.5 %collective-permute-start.13 = (bf16[64,1024]{1,0:T(8,128)(2,1)S(1)}, bf16[64,1024]{1,0:T(8,128)(2,1)S(1)}, u32[]{:S(2)}, u32[]{:S(2)}) collective-permute-start(bf16[64,1024]{1,0:T(8,128)(2,1)S(1)} %get-tuple-element.50.refs_0_), channel_id=1, source_target_pairs={{0,1},{1,0},{2,3},{3,2},{4,5},{5,4},{6,7},{7,6},{8,9},{9,8},{10,11... | collective-permute-start | bytes 393224 | tf_op jit(solution)/shard_map/ppermute | solution.py:18
  43.0 3.9 %collective-permute-start.18 = (bf16[64,1024]{1,0:T(8,128)(2,1)S(1)}, bf16[64,1024]{1,0:T(8,128)(2,1)S(1)}, u32[]{:S(2)}, u32[]{:S(2)}) collective-permute-start(bf16[64,1024]{1,0:T(8,128)(2,1)S(1)} %select_n.26), channel_id=1, source_target_pairs={{0,2},{3,1},{1,0},{2,3},{4,6},{7,5},{5,4},{6,7},{8,10},{11,9},{9,8... | collective-permute-start | bytes 393224 | tf_op jit(solution)/shard_map/ppermute | solution.py:51
  46.9 3.7 %collective-permute-start.15 = (bf16[64,1024]{1,0:T(8,128)(2,1)S(1)}, bf16[64,1024]{1,0:T(8,128)(2,1)S(1)}, u32[]{:S(2)}, u32[]{:S(2)}) collective-permute-start(bf16[64,1024]{1,0:T(8,128)(2,1)S(1)} %select_n.25), channel_id=1, source_target_pairs={{0,2},{3,1},{1,0},{2,3},{4,6},{7,5},{5,4},{6,7},{8,10},{11,9},{9,8... | collective-permute-start | bytes 393224 | tf_op jit(solution)/shard_map/ppermute | solution.py:51
  50.6 2.4 %collective-permute-done.18.refs_2_ = bf16[64,1024]{1,0:T(8,128)(2,1)S(1)} collective-permute-done((bf16[64,1024]{1,0:T(8,128)(2,1)S(1)}, bf16[64,1024]{1,0:T(8,128)(2,1)S(1)}, u32[]{:S(2)}, u32[]{:S(2)}) %collective-permute-start.18) | collective-permute-done | bytes 131104 | tf_op jit(solution)/shard_map/ppermute | solution.py:51
  53.1 1.3 %partial_adjoint.2.refs_4_ = f32[256,2048]{1,0:T(8,128)S(1)} custom-call(bf16[2048,2048]{1,0:T(8,128)(2,1)S(1)} %get-tuple-element.25.tiles, bf16[64,1024]{1,0:T(8,128)(2,1)S(1)} %get-tuple-element.48.refs_0_, bf16[64,1024]{1,0:T(8,128)(2,1)S(1)} %collective-permute-done.16.refs_1_, bf16[64,1024]{1,0:T(8,128)(2,1)S(1)} %collective-permute-done.18.refs_2_, ...), custom_call_target="tpu_custom_call" | custom-call | tf_op jit(solution)/shard_map/partial_adjoint/pallas_call | solution.py:162
  54.5 1.3 %partial_adjoint.3 = (f32[64,2048]{1,0:T(8,128)S(1)}, f32[64,2048]{1,0:T(8,128)S(1)}, f32[64,2048]{1,0:T(8,128)S(1)}, f32[64,2048]{1,0:T(8,128)S(1)}) custom-call(bf16[2048,2048]{1,0:T(8,128)(2,1)S(1)} %get-tuple-element.25.tiles, bf16[64,1024]{1,0:T(8,128)(2,1)S(1)} %get-tuple-element.50.refs_0_, bf16[64,1024]{1,0:T(8,128)(2,1)S(1)} %collective-permute-done.13.refs_1_, ...), custom_call_target="tpu_custom_call" | custom-call | tf_op jit(solution)/shard_map/partial_adjoint/pallas_call | solution.py:162
  56.3 1.4 %collective-permute-done.19 = f32[64,2048]{1,0:T(8,128)S(1)} collective-permute-done((f32[64,2048]{1,0:T(8,128)S(1)}, f32[64,2048]{1,0:T(8,128)S(1)}, u32[]{:S(2)}, u32[]{:S(2)}) %collective-permute-start.19) | collective-permute-done | bytes 524320 | tf_op jit(solution)/shard_map/ppermute | solution.py:18
  57.7 1.3 %collective-permute-start.20 = (bf16[32,2048]{1,0:T(8,128)(2,1)S(1)}, bf16[32,2048]{1,0:T(8,128)(2,1)S(1)}, u32[]{:S(2)}, u32[]{:S(2)}) collective-permute-start(bf16[32,2048]{1,0:T(8,128)(2,1)S(1)} %fusion.8), channel_id=1, source_target_pairs={{0,8},{4,12},{8,0},{12,4},{16,24},{20,28},{24,16},{28,20},{1,9},{5... | collective-permute-start | bytes 393224 | tf_op jit(solution)/shard_map/ppermute | solution.py:18
  59.1 1.0 %collective-permute-start.22 = (bf16[32,2048]{1,0:T(8,128)(2,1)S(1)}, bf16[32,2048]{1,0:T(8,128)(2,1)S(1)}, u32[]{:S(2)}, u32[]{:S(2)}) collective-permute-start(bf16[32,2048]{1,0:T(8,128)(2,1)S(1)} %get-tuple-element.56), channel_id=1, source_target_pairs={{0,16},{4,20},{8,24},{12,28},{16,0},{20,4},{24,8},{28,12},{1,17},{... | collective-permute-start | bytes 393224 | tf_op jit(solution)/shard_map/ppermute | solution.py:18
  60.1 1.3 %collective-permute-start.23 = (bf16[32,2048]{1,0:T(8,128)(2,1)S(1)}, bf16[32,2048]{1,0:T(8,128)(2,1)S(1)}, u32[]{:S(2)}, u32[]{:S(2)}) collective-permute-start(bf16[32,2048]{1,0:T(8,128)(2,1)S(1)} %get-tuple-element.57), channel_id=1, source_target_pairs={{0,24},{4,28},{8,16},{12,20},{16,8},{20,12},{24,0},{28,4},{1,25},{... | collective-permute-start | bytes 393224 | tf_op jit(solution)/shard_map/ppermute | solution.py:18
  61.4 0.8 %maximum_bitcast_fusion = f32[2048,64]{0,1:T(8,128)} fusion(f32[64,1024]{1,0:T(8,128)S(1)} %get-tuple-element.51, f32[64,1024]{1,0:T(8,128)S(1)} %get-tuple-element.49), kind=kLoop, calls=%fused_computation | loop fusion | flops 131072 | bytes 1048576 | tf_op jit(solution)/shard_map/transpose | solution.py:211
  62.3 1.6 %collective-permute-done.20 = bf16[32,2048]{1,0:T(8,128)(2,1)S(1)} collective-permute-done((bf16[32,2048]{1,0:T(8,128)(2,1)S(1)}, bf16[32,2048]{1,0:T(8,128)(2,1)S(1)}, u32[]{:S(2)}, u32[]{:S(2)}) %collective-permute-start.20) | collective-permute-done | bytes 131104 | tf_op jit(solution)/shard_map/ppermute | solution.py:18
  63.8 3.4 %collective-permute-done.22 = bf16[32,2048]{1,0:T(8,128)(2,1)S(1)} collective-permute-done((bf16[32,2048]{1,0:T(8,128)(2,1)S(1)}, bf16[32,2048]{1,0:T(8,128)(2,1)S(1)}, u32[]{:S(2)}, u32[]{:S(2)}) %collective-permute-start.22) | collective-permute-done | bytes 131104 | tf_op jit(solution)/shard_map/ppermute | solution.py:18
  67.2 0.8 %fusion.12 = f32[2048,32]{0,1:T(8,128)} fusion(f32[64,2048]{1,0:T(8,128)S(1)} %collective-permute-done.19, bf16[32,2048]{1,0:T(8,128)(2,1)S(1)} %collective-permute-done.23, bf16[32,2048]{1,0:T(8,128)(2,1)S(1)} %collective-permute-done.22, bf16[32,2048]{1,0:T(8,128)(2,1)S(1)} %collective-permute-done.20, f32[64,2048]{1,0:T(8,128)S(1)} %get-tuple-element.44), kind=kLoop, calls=%fused_computation.21 | loop fusion | flops 458752 | bytes 1179648 | tf_op jit(solution)/shard_map/transpose | solution.py:211
  (33 shorter events, 2.3 us)
Async XLA Ops:
  0.6 12.9 %copy-start = (bf16[2048,32]{0,1:T(8,128)(2,1)S(1)}, bf16[2048,32]{0,1:T(8,128)(2,1)}, u32[]{:S(2)}) copy-start(bf16[2048,32]{0,1:T(8,128)(2,1)} %param.5) | copy-start | bytes 393220
  0.6 8.2 %collective-permute-start.2 = (bf16[32,2048]{1,0:T(8,128)(2,1)}, bf16[32,2048]{1,0:T(8,128)(2,1)S(1)}, u32[]{:S(2)}, u32[]{:S(2)}) collective-permute-start(bf16[32,2048]{1,0:T(8,128)(2,1)} %bitcast.5), channel_id=1, source_target_pairs={{0,8},{4,12},{8,0},{12,4},{16,24},{20,28},{24,16},{28,20},{1,9},{5... | collective-permute-start | bytes 393224 | tf_op jit(solution)/shard_map/ppermute | solution.py:18
  3.6 8.0 %collective-permute-start.1 = (bf16[32,2048]{1,0:T(8,128)(2,1)}, bf16[32,2048]{1,0:T(8,128)(2,1)S(1)}, u32[]{:S(2)}, u32[]{:S(2)}) collective-permute-start(bf16[32,2048]{1,0:T(8,128)(2,1)} %bitcast.6), channel_id=1, source_target_pairs={{0,16},{4,20},{8,24},{12,28},{16,0},{20,4},{24,8},{28,12},{1,17},{... | collective-permute-start | bytes 393224 | tf_op jit(solution)/shard_map/ppermute | solution.py:18
  5.2 6.5 %collective-permute-start = (bf16[32,2048]{1,0:T(8,128)(2,1)}, bf16[32,2048]{1,0:T(8,128)(2,1)S(1)}, u32[]{:S(2)}, u32[]{:S(2)}) collective-permute-start(bf16[32,2048]{1,0:T(8,128)(2,1)} %bitcast.7), channel_id=1, source_target_pairs={{0,24},{4,28},{8,16},{12,20},{16,8},{20,12},{24,0},{28,4},{1,25},{... | collective-permute-start | bytes 393224 | tf_op jit(solution)/shard_map/ppermute | solution.py:18
  5.2 7.0 %collective-permute-start.3 = (bf16[32,2048]{1,0:T(8,128)(2,1)}, bf16[32,2048]{1,0:T(8,128)(2,1)S(1)}, u32[]{:S(2)}, u32[]{:S(2)}) collective-permute-start(bf16[32,2048]{1,0:T(8,128)(2,1)} %bitcast.8), channel_id=1, source_target_pairs={{0,4},{4,0},{8,12},{12,8},{16,20},{20,16},{24,28},{28,24},{1,5},{5... | collective-permute-start | bytes 393224 | tf_op jit(solution)/shard_map/ppermute | solution.py:18
  11.6 1.3 %collective-permute-start.4 = (bf16[32,2048]{1,0:T(8,128)(2,1)S(1)}, bf16[32,2048]{1,0:T(8,128)(2,1)S(1)}, u32[]{:S(2)}, u32[]{:S(2)}) collective-permute-start(bf16[32,2048]{1,0:T(8,128)(2,1)S(1)} %collective-permute-done.refs_1_), channel_id=1, source_target_pairs={{0,4},{4,0},{8,12},{12,8},{16,20},{20,16},{24,28},{28,24},{1,5},{5... | collective-permute-start | bytes 393224 | tf_op jit(solution)/shard_map/ppermute | solution.py:18
  11.6 1.5 %collective-permute-start.5 = (bf16[32,2048]{1,0:T(8,128)(2,1)S(1)}, bf16[32,2048]{1,0:T(8,128)(2,1)S(1)}, u32[]{:S(2)}, u32[]{:S(2)}) collective-permute-start(bf16[32,2048]{1,0:T(8,128)(2,1)S(1)} %collective-permute-done.1.refs_2_), channel_id=1, source_target_pairs={{0,4},{4,0},{8,12},{12,8},{16,20},{20,16},{24,28},{28,24},{1,5},{5... | collective-permute-start | bytes 393224 | tf_op jit(solution)/shard_map/ppermute | solution.py:18
  12.1 1.3 %collective-permute-start.6 = (bf16[32,2048]{1,0:T(8,128)(2,1)S(1)}, bf16[32,2048]{1,0:T(8,128)(2,1)S(1)}, u32[]{:S(2)}, u32[]{:S(2)}) collective-permute-start(bf16[32,2048]{1,0:T(8,128)(2,1)S(1)} %collective-permute-done.2.refs_3_), channel_id=1, source_target_pairs={{0,4},{4,0},{8,12},{12,8},{16,20},{20,16},{24,28},{28,24},{1,5},{5... | collective-permute-start | bytes 393224 | tf_op jit(solution)/shard_map/ppermute | solution.py:18
  14.8 6.6 %collective-permute-start.7 = (bf16[64,1024]{1,0:T(8,128)(2,1)S(1)}, bf16[64,1024]{1,0:T(8,128)(2,1)S(1)}, u32[]{:S(2)}, u32[]{:S(2)}) collective-permute-start(bf16[64,1024]{1,0:T(8,128)(2,1)S(1)} %get-tuple-element.36), channel_id=1, source_target_pairs={{0,1},{3,2},{2,0},{1,3},{4,5},{7,6},{6,4},{5,7},{8,9},{11,10},{10,... | collective-permute-start | bytes 393224 | tf_op jit(solution)/shard_map/ppermute | solution.py:33
  17.8 8.1 %collective-permute-start.10 = (bf16[64,1024]{1,0:T(8,128)(2,1)S(1)}, bf16[64,1024]{1,0:T(8,128)(2,1)S(1)}, u32[]{:S(2)}, u32[]{:S(2)}) collective-permute-start(bf16[64,1024]{1,0:T(8,128)(2,1)S(1)} %get-tuple-element.42), channel_id=1, source_target_pairs={{0,1},{3,2},{2,0},{1,3},{4,5},{7,6},{6,4},{5,7},{8,9},{11,10},{10,... | collective-permute-start | bytes 393224 | tf_op jit(solution)/shard_map/ppermute | solution.py:33
  21.5 13.1 %collective-permute-start.9 = (bf16[64,1024]{1,0:T(8,128)(2,1)S(1)}, bf16[64,1024]{1,0:T(8,128)(2,1)S(1)}, u32[]{:S(2)}, u32[]{:S(2)}) collective-permute-start(bf16[64,1024]{1,0:T(8,128)(2,1)S(1)} %get-tuple-element.52), channel_id=1, source_target_pairs={{0,3},{1,2},{2,1},{3,0},{4,7},{5,6},{6,5},{7,4},{8,11},{9,10},{10,... | collective-permute-start | bytes 393224 | tf_op jit(solution)/shard_map/ppermute | solution.py:18
  25.8 8.7 %collective-permute-start.8 = (bf16[64,1024]{1,0:T(8,128)(2,1)S(1)}, bf16[64,1024]{1,0:T(8,128)(2,1)S(1)}, u32[]{:S(2)}, u32[]{:S(2)}) collective-permute-start(bf16[64,1024]{1,0:T(8,128)(2,1)S(1)} %get-tuple-element.37), channel_id=1, source_target_pairs={{0,1},{1,0},{2,3},{3,2},{4,5},{5,4},{6,7},{7,6},{8,9},{9,8},{10,11... | collective-permute-start | bytes 393224 | tf_op jit(solution)/shard_map/ppermute | solution.py:18
  25.9 12.2 %collective-permute-start.12 = (bf16[64,1024]{1,0:T(8,128)(2,1)S(1)}, bf16[64,1024]{1,0:T(8,128)(2,1)S(1)}, u32[]{:S(2)}, u32[]{:S(2)}) collective-permute-start(bf16[64,1024]{1,0:T(8,128)(2,1)S(1)} %get-tuple-element.54), channel_id=1, source_target_pairs={{0,3},{1,2},{2,1},{3,0},{4,7},{5,6},{6,5},{7,4},{8,11},{9,10},{10,... | collective-permute-start | bytes 393224 | tf_op jit(solution)/shard_map/ppermute | solution.py:18
  28.7 9.4 %collective-permute-start.11 = (bf16[64,1024]{1,0:T(8,128)(2,1)S(1)}, bf16[64,1024]{1,0:T(8,128)(2,1)S(1)}, u32[]{:S(2)}, u32[]{:S(2)}) collective-permute-start(bf16[64,1024]{1,0:T(8,128)(2,1)S(1)} %get-tuple-element.43), channel_id=1, source_target_pairs={{0,1},{1,0},{2,3},{3,2},{4,5},{5,4},{6,7},{7,6},{8,9},{9,8},{10,11... | collective-permute-start | bytes 393224 | tf_op jit(solution)/shard_map/ppermute | solution.py:18
  34.7 8.3 %collective-permute-start.17 = (bf16[64,1024]{1,0:T(8,128)(2,1)S(1)}, bf16[64,1024]{1,0:T(8,128)(2,1)S(1)}, u32[]{:S(2)}, u32[]{:S(2)}) collective-permute-start(bf16[64,1024]{1,0:T(8,128)(2,1)S(1)} %get-tuple-element.48.refs_0_), channel_id=1, source_target_pairs={{0,3},{1,2},{2,1},{3,0},{4,7},{5,6},{6,5},{7,4},{8,11},{9,10},{10,... | collective-permute-start | bytes 393224 | tf_op jit(solution)/shard_map/ppermute | solution.py:18
  38.2 8.7 %collective-permute-start.14 = (bf16[64,1024]{1,0:T(8,128)(2,1)S(1)}, bf16[64,1024]{1,0:T(8,128)(2,1)S(1)}, u32[]{:S(2)}, u32[]{:S(2)}) collective-permute-start(bf16[64,1024]{1,0:T(8,128)(2,1)S(1)} %get-tuple-element.50.refs_0_), channel_id=1, source_target_pairs={{0,3},{1,2},{2,1},{3,0},{4,7},{5,6},{6,5},{7,4},{8,11},{9,10},{10,... | collective-permute-start | bytes 393224 | tf_op jit(solution)/shard_map/ppermute | solution.py:18
  40.4 10.2 %collective-permute-start.16 = (bf16[64,1024]{1,0:T(8,128)(2,1)S(1)}, bf16[64,1024]{1,0:T(8,128)(2,1)S(1)}, u32[]{:S(2)}, u32[]{:S(2)}) collective-permute-start(bf16[64,1024]{1,0:T(8,128)(2,1)S(1)} %get-tuple-element.48.refs_0_), channel_id=1, source_target_pairs={{0,1},{1,0},{2,3},{3,2},{4,5},{5,4},{6,7},{7,6},{8,9},{9,8},{10,11... | collective-permute-start | bytes 393224 | tf_op jit(solution)/shard_map/ppermute | solution.py:18
  41.0 13.3 %collective-permute-start.13 = (bf16[64,1024]{1,0:T(8,128)(2,1)S(1)}, bf16[64,1024]{1,0:T(8,128)(2,1)S(1)}, u32[]{:S(2)}, u32[]{:S(2)}) collective-permute-start(bf16[64,1024]{1,0:T(8,128)(2,1)S(1)} %get-tuple-element.50.refs_0_), channel_id=1, source_target_pairs={{0,1},{1,0},{2,3},{3,2},{4,5},{5,4},{6,7},{7,6},{8,9},{9,8},{10,11... | collective-permute-start | bytes 393224 | tf_op jit(solution)/shard_map/ppermute | solution.py:18
  43.0 10.1 %collective-permute-start.18 = (bf16[64,1024]{1,0:T(8,128)(2,1)S(1)}, bf16[64,1024]{1,0:T(8,128)(2,1)S(1)}, u32[]{:S(2)}, u32[]{:S(2)}) collective-permute-start(bf16[64,1024]{1,0:T(8,128)(2,1)S(1)} %select_n.26), channel_id=1, source_target_pairs={{0,2},{3,1},{1,0},{2,3},{4,6},{7,5},{5,4},{6,7},{8,10},{11,9},{9,8... | collective-permute-start | bytes 393224 | tf_op jit(solution)/shard_map/ppermute | solution.py:51
  46.9 7.5 %collective-permute-start.15 = (bf16[64,1024]{1,0:T(8,128)(2,1)S(1)}, bf16[64,1024]{1,0:T(8,128)(2,1)S(1)}, u32[]{:S(2)}, u32[]{:S(2)}) collective-permute-start(bf16[64,1024]{1,0:T(8,128)(2,1)S(1)} %select_n.25), channel_id=1, source_target_pairs={{0,2},{3,1},{1,0},{2,3},{4,6},{7,5},{5,4},{6,7},{8,10},{11,9},{9,8... | collective-permute-start | bytes 393224 | tf_op jit(solution)/shard_map/ppermute | solution.py:51
  55.7 2.0 %collective-permute-start.19 = (f32[64,2048]{1,0:T(8,128)S(1)}, f32[64,2048]{1,0:T(8,128)S(1)}, u32[]{:S(2)}, u32[]{:S(2)}) collective-permute-start(f32[64,2048]{1,0:T(8,128)S(1)} %get-tuple-element.45), channel_id=1, source_target_pairs={{0,4},{4,0},{8,12},{12,8},{16,20},{20,16},{24,28},{28,24},{1,5},{5... | collective-permute-start | bytes 1572872 | tf_op jit(solution)/shard_map/ppermute | solution.py:18
  55.8 3.2 %collective-permute-start.21 = (f32[64,2048]{1,0:T(8,128)S(1)}, f32[64,2048]{1,0:T(8,128)S(1)}, u32[]{:S(2)}, u32[]{:S(2)}) collective-permute-start(f32[64,2048]{1,0:T(8,128)S(1)} %get-tuple-element.47), channel_id=1, source_target_pairs={{0,4},{4,0},{8,12},{12,8},{16,20},{20,16},{24,28},{28,24},{1,5},{5... | collective-permute-start | bytes 1572872 | tf_op jit(solution)/shard_map/ppermute | solution.py:18
  57.7 6.1 %collective-permute-start.20 = (bf16[32,2048]{1,0:T(8,128)(2,1)S(1)}, bf16[32,2048]{1,0:T(8,128)(2,1)S(1)}, u32[]{:S(2)}, u32[]{:S(2)}) collective-permute-start(bf16[32,2048]{1,0:T(8,128)(2,1)S(1)} %fusion.8), channel_id=1, source_target_pairs={{0,8},{4,12},{8,0},{12,4},{16,24},{20,28},{24,16},{28,20},{1,9},{5... | collective-permute-start | bytes 393224 | tf_op jit(solution)/shard_map/ppermute | solution.py:18
  59.1 8.1 %collective-permute-start.22 = (bf16[32,2048]{1,0:T(8,128)(2,1)S(1)}, bf16[32,2048]{1,0:T(8,128)(2,1)S(1)}, u32[]{:S(2)}, u32[]{:S(2)}) collective-permute-start(bf16[32,2048]{1,0:T(8,128)(2,1)S(1)} %get-tuple-element.56), channel_id=1, source_target_pairs={{0,16},{4,20},{8,24},{12,28},{16,0},{20,4},{24,8},{28,12},{1,17},{... | collective-permute-start | bytes 393224 | tf_op jit(solution)/shard_map/ppermute | solution.py:18
  60.1 7.1 %collective-permute-start.23 = (bf16[32,2048]{1,0:T(8,128)(2,1)S(1)}, bf16[32,2048]{1,0:T(8,128)(2,1)S(1)}, u32[]{:S(2)}, u32[]{:S(2)}) collective-permute-start(bf16[32,2048]{1,0:T(8,128)(2,1)S(1)} %get-tuple-element.57), channel_id=1, source_target_pairs={{0,24},{4,28},{8,16},{12,20},{16,8},{20,12},{24,0},{28,4},{1,25},{... | collective-permute-start | bytes 393224 | tf_op jit(solution)/shard_map/ppermute | solution.py:18

commit v19 on v18

--- a/solution.py
+++ b/solution.py
@@ -92,16 +92,18 @@
 
 
 def sketch_kernel(tiles, token, *refs, base, offsets_row, offsets_col):
-    blocks, outs, ends, probes = refs[: len(offsets_row)], refs[len(offsets_row) : -2], refs[-2], refs[-1]
+    count = len(refs) - 2 - len(offsets_col)
+    blocks, outs, ends, probes = refs[:count], refs[count:-2], refs[-2], refs[-1]
     own = blocks[0].shape[0]
     ratio = len(offsets_row) // len(offsets_col)
     share = own * ratio
     ends[...] = jnp.full(ends.shape, at_end(len(offsets_col)).astype(F32))
     row, col = lax.axis_index("row"), lax.axis_index("col")
-    for offset, ref in zip(offsets_row, blocks):
+    pieces = [(ref, at) for ref in blocks for at in range(0, ref.shape[0], own)]
+    for offset, (ref, at) in zip(offsets_row, pieces):
         column = row ^ offset
         start = (lax.div(column, ratio) ^ col) * share + lax.rem(column, ratio) * own
-        probes[pl.ds(pl.multiple_of(start, own), own), :] = ref[...]
+        probes[pl.ds(pl.multiple_of(start, own), own), :] = ref[at : at + own, :]
     for step in range(ends.shape[1] // STEP):
         rows, at = slice(base + step * STEP, base + (step + 1) * STEP), slice(step * STEP, (step + 1) * STEP)
         term = lax.dot_general(probes[...], tiles[rows, :], (((1,), (1,)), ((), ())), preferred_element_type=F32)
@@ -112,7 +114,7 @@
 def partial_sketch(tiles, blocks, token, offsets_row, offsets_col, chunk, chunks):
     rows, cols = tiles.shape
     rows //= chunks
-    width = blocks[0].shape[0] * len(blocks)
+    width = blocks[0].shape[0] * len(offsets_row)
     share = width // len(offsets_col)
     vmem = pl.BlockSpec(memory_space=pltpu.VMEM)
     exact = (0, offsets_col[-1])
@@ -132,7 +134,7 @@
     )(tiles, token, *blocks)
 
 
-def adjoint_kernel(tiles, *refs, base, parts, offsets_col, devices):
+def adjoint_kernel(tiles, *refs, base, span, parts, offsets_col, devices):
     shares, earlier, outs, lowered = refs[: len(offsets_col)], refs[len(offsets_col) : -1 - parts], refs[-1 - parts : -1], refs[-1]
     share, rows = shares[0].shape
     ratio = devices // len(offsets_col)
@@ -145,27 +147,27 @@
             lowered[pl.ds(pl.multiple_of(start, own), own), :] = ref[n * own : (n + 1) * own, :]
     for step in range(tiles.shape[1] // STEP):
         at = slice(step * STEP, (step + 1) * STEP)
-        term = jnp.dot(lowered[...], tiles[base : base + rows, at], preferred_element_type=F32)
+        term = jnp.dot(lowered[span, :], tiles[base : base + rows, at], preferred_element_type=F32)
         if earlier:
-            term += earlier[0][:, at]
+            term += earlier[0][span, at]
         height = outs[0].shape[0]
         for k, out in enumerate(outs):
             out[:, at] = term[k * height : (k + 1) * height]
 
 
-def partial_adjoint(tiles, shares, earlier, offsets_col, devices, chunk, chunks):
-    rows, cols = tiles.shape
-    rows //= chunks
-    width = shares[0].shape[0] * len(offsets_col)
-    parts = 4 if chunk == chunks - 1 else 1
+def partial_adjoint(tiles, shares, earlier, span, parts, offsets_col, devices, base):
+    cols = tiles.shape[1]
+    share, rows = shares[0].shape
+    width = share * len(offsets_col)
+    height = (span.stop - span.start) // parts
     vmem = pl.BlockSpec(memory_space=pltpu.VMEM)
     return pl.pallas_call(
         functools.partial(
-            adjoint_kernel, base=chunk * rows, parts=parts, offsets_col=offsets_col, devices=devices
+            adjoint_kernel, base=base, span=span, parts=parts, offsets_col=offsets_col, devices=devices
         ),
         in_specs=[vmem] * (1 + len(shares) + len(earlier)),
         out_specs=[vmem] * parts,
-        out_shape=[jax.ShapeDtypeStruct((width // parts, cols), F32)] * parts,
+        out_shape=[jax.ShapeDtypeStruct((height, cols), F32)] * parts,
         scratch_shapes=[pltpu.VMEM((width, rows), BF16)],
         compiler_params=pltpu.CompilerParams(vmem_limit_bytes=VMEM_LIMIT),
         cost_estimate=pl.CostEstimate(
@@ -181,15 +183,15 @@
     chunks = CHUNKS if green.shape[0] % (CHUNKS * STEP) == 0 else 1
     offsets_col = list(range(n_col))
     offsets_core = list(range(0, n_row, 2))
-    gather_core = [0] + offsets_core[:0:-1]
+    gather_core = offsets_core
     offsets_row = gather_core + [offset ^ 1 for offset in gather_core]
     tiles, token = masked(green, mask)
 
     own = probes.T
     held = [own] + [exchange(own, "row", offset) for offset in gather_core[1:]]
     twin = exchange(own, "row", 1)
-    held, token = lax.optimization_barrier((held, token))
-    blocks = held + [twin] + [exchange(block, "row", 1) for block in held[1:]]
+    held, twin, token = lax.optimization_barrier((held, twin, token))
+    blocks = held + [twin, exchange(jnp.concatenate(held[1:]), "row", 1)]
 
     totals, shares = [], []
     for chunk in range(chunks):
@@ -198,15 +200,25 @@
         shares.append(window_spread(totals[-1].astype(BF16), ends, n_col))
 
     earlier = []
-    for chunk in range(chunks):
-        earlier = partial_adjoint(tiles, shares[chunk], earlier, offsets_col, n_row, chunk, chunks)
+    length = green.shape[0] // chunks
+    width = own_width * n_row
+    for chunk in range(chunks - 1):
+        earlier = partial_adjoint(
+            tiles, shares[chunk], earlier, slice(0, width), 1, offsets_col, n_row, chunk * length
+        )
+    theirs, ours = (
+        partial_adjoint(tiles, shares[-1], earlier, span, 2, offsets_col, n_row, (chunks - 1) * length)
+        for span in (slice(width // 2, width), slice(0, width // 2))
+    )
     pairs = []
-    for mine, others in (earlier[1::2], earlier[::2]):
+    for mine, others in zip(ours, theirs):
         others = exchange(others, "row", 1)
+        if pairs:
+            mine = after(mine, pairs[-1])
         bands = [slice(at, at + own_width) for at in range(0, mine.shape[0], own_width)]
-        pairs = [mine[band] + others[band] for band in bands] + pairs
+        pairs += [mine[band] + others[band] for band in bands]
     adjoint = pairs[0]
-    for offset in offsets_core[1:]:
+    for offset in offsets_core[1:2] + offsets_core[:1:-1]:
         adjoint = adjoint + exchange(pairs[offset // 2].astype(BF16), "row", offset).astype(F32)
     return jnp.concatenate(totals, axis=1).T, adjoint.T
 

time: 68.2 us -> 67.6 us (level)
  waiting for transfers between devices: 22.3 us -> 21.6 us
    ppermute x20 -> x18, waiting for transfers between devices: 18.7 us -> 18.4 us  [exchange(): return lax.ppermute(value, axis, [(i, i ^ offset) for i in range(size)])]
    pallas_call x2 -> x3, Pallas kernels: 2.53 us -> 2.74 us  [partial_adjoint(): pl.pallas_call(functools.partial(adjoint_kernel, base=base, span=span, pa...]
    ppermute x20 -> x18, starting transfers between devices: 22.2 us -> 22 us  [exchange(): return lax.ppermute(value, axis, [(i, i ^ offset) for i in range(size)])]
  transfers between devices with their start and end apart: 24 -> 22, of which waited for: 13 -> 13; matrix products, arithmetic and copies ran while one was open for 2% -> 2% of each run, Pallas kernels for 9% -> 10%
where the time goes in v19:
time: 67.6 us; the launch traced here: 67.4 us
  starting transfers between devices  33.9 us (50%)
  waiting for transfers between devices  21.6 us (32%)
  Pallas kernels  9.03 us (13%)
  other arithmetic  2.13 us (3%)
  between operations  0.77 us (1%)
    ppermute x18, starting transfers between devices, exchange(): return lax.ppermute(value, axis, [(i, i ^ offset) for i in range(size)])  22 us
    ppermute x18, waiting for transfers between devices, exchange(): return lax.ppermute(value, axis, [(i, i ^ offset) for i in range(size)])  18.4 us
    ppermute x2, starting transfers between devices, window_spread(): lax.ppermute(onward, 'col', [(0, 2), (3, 1), (1, 0), (2, 3)])  7.7 us
    ppermute x2, starting transfers between devices, window_sums(): came = lax.ppermute(terms[2], 'col', [(0, 1), (3, 2), (2, 0), (1, 3)])  4.27 us
    pallas_call x1, Pallas kernels, masked(): pl.pallas_call(functools.partial(mask_kernel, block=rows // mask.shape[0]...  3.65 us
    pallas_call x3, Pallas kernels, partial_adjoint(): pl.pallas_call(functools.partial(adjoint_kernel, base=base, span=span, pa...  2.74 us
    pallas_call x2, Pallas kernels, partial_sketch(): pl.pallas_call(functools.partial(sketch_kernel, base=chunk * rows, offset...  2.64 us
    ppermute x2, waiting for transfers between devices, window_spread(): lax.ppermute(onward, 'col', [(0, 2), (3, 1), (1, 0), (2, 3)])  2.23 us
  transfers between devices with their start and end apart: 22, of which 13 were waited for; matrix products, arithmetic and copies ran while one was open for 2% of the time, Pallas kernels for 10%

profile of v19, /device:TPU:0, one launch (start us, length us, event | category | flops | bytes accessed | tf_op | source)
XLA Modules:
  0.0 67.4 jit_solution(14780421158616998577)
XLA Ops:
  0.6 3.0 %collective-permute-start = (bf16[32,2048]{1,0:T(8,128)(2,1)}, bf16[32,2048]{1,0:T(8,128)(2,1)S(1)}, u32[]{:S(2)}, u32[]{:S(2)}) collective-permute-start(bf16[32,2048]{1,0:T(8,128)(2,1)} %bitcast.5), channel_id=1, source_target_pairs={{0,8},{4,12},{8,0},{12,4},{16,24},{20,28},{24,16},{28,20},{1,9},{5... | collective-permute-start | bytes 393224 | tf_op jit(solution)/shard_map/ppermute | solution.py:18
  3.6 1.5 %collective-permute-start.1 = (bf16[32,2048]{1,0:T(8,128)(2,1)}, bf16[32,2048]{1,0:T(8,128)(2,1)S(1)}, u32[]{:S(2)}, u32[]{:S(2)}) collective-permute-start(bf16[32,2048]{1,0:T(8,128)(2,1)} %bitcast.6), channel_id=1, source_target_pairs={{0,16},{4,20},{8,24},{12,28},{16,0},{20,4},{24,8},{28,12},{1,17},{... | collective-permute-start | bytes 393224 | tf_op jit(solution)/shard_map/ppermute | solution.py:18
  5.2 3.6 %masked_tiles.1 = (bf16[2048,2048]{1,0:T(8,128)(2,1)S(1)}, f32[8,128]{1,0:T(8,128)S(1)}) custom-call(s32[8,8]{1,0:T(8,128)} %mask_hbm.1, bf16[2048,2048]{1,0:T(8,128)(2,1)} %green_ref.1), custom_call_target="tpu_custom_call" | custom-call | bytes 8388608 | tf_op jit(solution)/shard_map/masked_tiles/pallas_call | solution.py:78
  8.9 2.8 %collective-permute-done.1.refs_2_ = bf16[32,2048]{1,0:T(8,128)(2,1)S(1)} collective-permute-done((bf16[32,2048]{1,0:T(8,128)(2,1)}, bf16[32,2048]{1,0:T(8,128)(2,1)S(1)}, u32[]{:S(2)}, u32[]{:S(2)}) %collective-permute-start.1) | collective-permute-done | bytes 131104 | tf_op jit(solution)/shard_map/ppermute | solution.py:18
  11.7 1.7 %collective-permute-done.4.refs_5_ = bf16[96,2048]{1,0:T(8,128)(2,1)S(1)} collective-permute-done((bf16[96,2048]{1,0:T(8,128)(2,1)S(1)}, bf16[96,2048]{1,0:T(8,128)(2,1)S(1)}, u32[]{:S(2)}, u32[]{:S(2)}) %collective-permute-start.4) | collective-permute-done | bytes 393248 | tf_op jit(solution)/shard_map/ppermute | solution.py:18
  13.5 1.3 %partial_sketch.2 = (f32[64,1024]{1,0:T(8,128)S(1)}, bf16[64,1024]{1,0:T(8,128)(2,1)S(1)}, bf16[64,1024]{1,0:T(8,128)(2,1)S(1)}, f32[64,1024]{1,0:T(8,128)S(1)}, f32[64,1024]{1,0:T(8,128)S(1)}) custom-call(bf16[2048,2048]{1,0:T(8,128)(2,1)S(1)} %get-tuple-element.27.tiles, f32[8,128]{1,0:T(8,128)S(1)} %get-tuple-element.29.token, ...), custom_call_target="tpu_custom_call" | custom-call | flops 1073741824 | bytes 4194304 | tf_op jit(solution)/shard_map/partial_sketch/pallas_call | solution.py:123
  14.8 1.6 %collective-permute-start.5 = (bf16[64,1024]{1,0:T(8,128)(2,1)S(1)}, bf16[64,1024]{1,0:T(8,128)(2,1)S(1)}, u32[]{:S(2)}, u32[]{:S(2)}) collective-permute-start(bf16[64,1024]{1,0:T(8,128)(2,1)S(1)} %get-tuple-element.39), channel_id=1, source_target_pairs={{0,1},{3,2},{2,0},{1,3},{4,5},{7,6},{6,4},{5,7},{8,9},{11,10},{10,... | collective-permute-start | bytes 393224 | tf_op jit(solution)/shard_map/ppermute | solution.py:33
  16.4 1.3 %partial_sketch.3 = (f32[64,1024]{1,0:T(8,128)S(1)}, bf16[64,1024]{1,0:T(8,128)(2,1)S(1)}, bf16[64,1024]{1,0:T(8,128)(2,1)S(1)}, f32[64,1024]{1,0:T(8,128)S(1)}, f32[64,1024]{1,0:T(8,128)S(1)}) custom-call(bf16[2048,2048]{1,0:T(8,128)(2,1)S(1)} %get-tuple-element.27.tiles, f32[8,128]{1,0:T(8,128)S(1)} %get-tuple-element.29.token, ...), custom_call_target="tpu_custom_call" | custom-call | flops 1073741824 | bytes 4194304 | tf_op jit(solution)/shard_map/partial_sketch/pallas_call | solution.py:123
  17.7 2.6 %collective-permute-start.8 = (bf16[64,1024]{1,0:T(8,128)(2,1)S(1)}, bf16[64,1024]{1,0:T(8,128)(2,1)S(1)}, u32[]{:S(2)}, u32[]{:S(2)}) collective-permute-start(bf16[64,1024]{1,0:T(8,128)(2,1)S(1)} %get-tuple-element.45), channel_id=1, source_target_pairs={{0,1},{3,2},{2,0},{1,3},{4,5},{7,6},{6,4},{5,7},{8,9},{11,10},{10,... | collective-permute-start | bytes 393224 | tf_op jit(solution)/shard_map/ppermute | solution.py:33
  20.4 0.9 %collective-permute-done.5 = bf16[64,1024]{1,0:T(8,128)(2,1)S(1)} collective-permute-done((bf16[64,1024]{1,0:T(8,128)(2,1)S(1)}, bf16[64,1024]{1,0:T(8,128)(2,1)S(1)}, u32[]{:S(2)}, u32[]{:S(2)}) %collective-permute-start.5) | collective-permute-done | bytes 131104 | tf_op jit(solution)/shard_map/ppermute | solution.py:33
  21.4 4.4 %collective-permute-start.7 = (bf16[64,1024]{1,0:T(8,128)(2,1)S(1)}, bf16[64,1024]{1,0:T(8,128)(2,1)S(1)}, u32[]{:S(2)}, u32[]{:S(2)}) collective-permute-start(bf16[64,1024]{1,0:T(8,128)(2,1)S(1)} %get-tuple-element.56), channel_id=1, source_target_pairs={{0,3},{1,2},{2,1},{3,0},{4,7},{5,6},{6,5},{7,4},{8,11},{9,10},{10,... | collective-permute-start | bytes 393224 | tf_op jit(solution)/shard_map/ppermute | solution.py:18
  25.9 2.7 %collective-permute-start.10 = (bf16[64,1024]{1,0:T(8,128)(2,1)S(1)}, bf16[64,1024]{1,0:T(8,128)(2,1)S(1)}, u32[]{:S(2)}, u32[]{:S(2)}) collective-permute-start(bf16[64,1024]{1,0:T(8,128)(2,1)S(1)} %get-tuple-element.58), channel_id=1, source_target_pairs={{0,3},{1,2},{2,1},{3,0},{4,7},{5,6},{6,5},{7,4},{8,11},{9,10},{10,... | collective-permute-start | bytes 393224 | tf_op jit(solution)/shard_map/ppermute | solution.py:18
  28.6 1.8 %collective-permute-done.7 = bf16[64,1024]{1,0:T(8,128)(2,1)S(1)} collective-permute-done((bf16[64,1024]{1,0:T(8,128)(2,1)S(1)}, bf16[64,1024]{1,0:T(8,128)(2,1)S(1)}, u32[]{:S(2)}, u32[]{:S(2)}) %collective-permute-start.7) | collective-permute-done | bytes 131104 | tf_op jit(solution)/shard_map/ppermute | solution.py:18
  30.4 4.0 %collective-permute-done.6 = bf16[64,1024]{1,0:T(8,128)(2,1)S(1)} collective-permute-done((bf16[64,1024]{1,0:T(8,128)(2,1)S(1)}, bf16[64,1024]{1,0:T(8,128)(2,1)S(1)}, u32[]{:S(2)}, u32[]{:S(2)}) %collective-permute-start.6) | collective-permute-done | bytes 131104 | tf_op jit(solution)/shard_map/ppermute | solution.py:18
  34.5 1.6 %collective-permute-start.15 = (bf16[64,1024]{1,0:T(8,128)(2,1)S(1)}, bf16[64,1024]{1,0:T(8,128)(2,1)S(1)}, u32[]{:S(2)}, u32[]{:S(2)}) collective-permute-start(bf16[64,1024]{1,0:T(8,128)(2,1)S(1)} %get-tuple-element.52.refs_0_), channel_id=1, source_target_pairs={{0,3},{1,2},{2,1},{3,0},{4,7},{5,6},{6,5},{7,4},{8,11},{9,10},{10,... | collective-permute-start | bytes 393224 | tf_op jit(solution)/shard_map/ppermute | solution.py:18
  36.1 1.9 %collective-permute-done.9 = bf16[64,1024]{1,0:T(8,128)(2,1)S(1)} collective-permute-done((bf16[64,1024]{1,0:T(8,128)(2,1)S(1)}, bf16[64,1024]{1,0:T(8,128)(2,1)S(1)}, u32[]{:S(2)}, u32[]{:S(2)}) %collective-permute-start.9) | collective-permute-done | bytes 131104 | tf_op jit(solution)/shard_map/ppermute | solution.py:18
  38.1 2.4 %collective-permute-start.12 = (bf16[64,1024]{1,0:T(8,128)(2,1)S(1)}, bf16[64,1024]{1,0:T(8,128)(2,1)S(1)}, u32[]{:S(2)}, u32[]{:S(2)}) collective-permute-start(bf16[64,1024]{1,0:T(8,128)(2,1)S(1)} %get-tuple-element.54.refs_0_), channel_id=1, source_target_pairs={{0,3},{1,2},{2,1},{3,0},{4,7},{5,6},{6,5},{7,4},{8,11},{9,10},{10,... | collective-permute-start | bytes 393224 | tf_op jit(solution)/shard_map/ppermute | solution.py:18
  41.0 1.6 %collective-permute-start.14 = (bf16[64,1024]{1,0:T(8,128)(2,1)S(1)}, bf16[64,1024]{1,0:T(8,128)(2,1)S(1)}, u32[]{:S(2)}, u32[]{:S(2)}) collective-permute-start(bf16[64,1024]{1,0:T(8,128)(2,1)S(1)} %get-tuple-element.52.refs_0_), channel_id=1, source_target_pairs={{0,1},{1,0},{2,3},{3,2},{4,5},{5,4},{6,7},{7,6},{8,9},{9,8},{10,11... | collective-permute-start | bytes 393224 | tf_op jit(solution)/shard_map/ppermute | solution.py:18
  42.8 3.9 %collective-permute-start.16 = (bf16[64,1024]{1,0:T(8,128)(2,1)S(1)}, bf16[64,1024]{1,0:T(8,128)(2,1)S(1)}, u32[]{:S(2)}, u32[]{:S(2)}) collective-permute-start(bf16[64,1024]{1,0:T(8,128)(2,1)S(1)} %select_n.26), channel_id=1, source_target_pairs={{0,2},{3,1},{1,0},{2,3},{4,6},{7,5},{5,4},{6,7},{8,10},{11,9},{9,8... | collective-permute-start | bytes 393224 | tf_op jit(solution)/shard_map/ppermute | solution.py:51
  46.8 3.8 %collective-permute-start.13 = (bf16[64,1024]{1,0:T(8,128)(2,1)S(1)}, bf16[64,1024]{1,0:T(8,128)(2,1)S(1)}, u32[]{:S(2)}, u32[]{:S(2)}) collective-permute-start(bf16[64,1024]{1,0:T(8,128)(2,1)S(1)} %select_n.25), channel_id=1, source_target_pairs={{0,2},{3,1},{1,0},{2,3},{4,6},{7,5},{5,4},{6,7},{8,10},{11,9},{9,8... | collective-permute-start | bytes 393224 | tf_op jit(solution)/shard_map/ppermute | solution.py:51
  50.9 2.1 %collective-permute-done.16.refs_2_ = bf16[64,1024]{1,0:T(8,128)(2,1)S(1)} collective-permute-done((bf16[64,1024]{1,0:T(8,128)(2,1)S(1)}, bf16[64,1024]{1,0:T(8,128)(2,1)S(1)}, u32[]{:S(2)}, u32[]{:S(2)}) %collective-permute-start.16) | collective-permute-done | bytes 131104 | tf_op jit(solution)/shard_map/ppermute | solution.py:51
  53.0 1.3 %partial_adjoint.3.refs_4_ = f32[256,2048]{1,0:T(8,128)S(1)} custom-call(bf16[2048,2048]{1,0:T(8,128)(2,1)S(1)} %get-tuple-element.27.tiles, bf16[64,1024]{1,0:T(8,128)(2,1)S(1)} %get-tuple-element.52.refs_0_, bf16[64,1024]{1,0:T(8,128)(2,1)S(1)} %collective-permute-done.14.refs_1_, bf16[64,1024]{1,0:T(8,128)(2,1)S(1)} %collective-permute-done.16.refs_2_, ...), custom_call_target="tpu_custom_call" | custom-call | tf_op jit(solution)/shard_map/partial_adjoint/pallas_call | solution.py:164
  54.4 0.7 %partial_adjoint.5 = (f32[64,2048]{1,0:T(8,128)S(1)}, f32[64,2048]{1,0:T(8,128)S(1)}) custom-call(bf16[2048,2048]{1,0:T(8,128)(2,1)S(1)} %get-tuple-element.27.tiles, bf16[64,1024]{1,0:T(8,128)(2,1)S(1)} %get-tuple-element.54.refs_0_, bf16[64,1024]{1,0:T(8,128)(2,1)S(1)} %collective-permute-done.11.refs_1_, ...), custom_call_target="tpu_custom_call" | custom-call | tf_op jit(solution)/shard_map/partial_adjoint/pallas_call | solution.py:164
  55.8 0.7 %partial_adjoint.4 = (f32[64,2048]{1,0:T(8,128)S(1)}, f32[64,2048]{1,0:T(8,128)S(1)}) custom-call(bf16[2048,2048]{1,0:T(8,128)(2,1)S(1)} %get-tuple-element.27.tiles, bf16[64,1024]{1,0:T(8,128)(2,1)S(1)} %get-tuple-element.54.refs_0_, bf16[64,1024]{1,0:T(8,128)(2,1)S(1)} %collective-permute-done.11.refs_1_, ...), custom_call_target="tpu_custom_call" | custom-call | tf_op jit(solution)/shard_map/partial_adjoint/pallas_call | solution.py:164
  56.5 0.7 collective-permute-done.17
  57.2 1.3 %collective-permute-start.18 = (bf16[32,2048]{1,0:T(8,128)(2,1)S(1)}, bf16[32,2048]{1,0:T(8,128)(2,1)S(1)}, u32[]{:S(2)}, u32[]{:S(2)}) collective-permute-start(bf16[32,2048]{1,0:T(8,128)(2,1)S(1)} %slice_add_fusion.2), channel_id=1, source_target_pairs={{0,8},{4,12},{8,0},{12,4},{16,24},{20,28},{24,16},{28,20},{1,9},{5... | collective-permute-start | bytes 393224 | tf_op jit(solution)/shard_map/ppermute | solution.py:18
  58.5 1.0 %collective-permute-start.21 = (bf16[32,2048]{1,0:T(8,128)(2,1)S(1)}, bf16[32,2048]{1,0:T(8,128)(2,1)S(1)}, u32[]{:S(2)}, u32[]{:S(2)}) collective-permute-start(bf16[32,2048]{1,0:T(8,128)(2,1)S(1)} %get-tuple-element.61), channel_id=1, source_target_pairs={{0,16},{4,20},{8,24},{12,28},{16,0},{20,4},{24,8},{28,12},{1,17},{... | collective-permute-start | bytes 393224 | tf_op jit(solution)/shard_map/ppermute | solution.py:18
  59.6 1.3 %collective-permute-start.20 = (bf16[32,2048]{1,0:T(8,128)(2,1)S(1)}, bf16[32,2048]{1,0:T(8,128)(2,1)S(1)}, u32[]{:S(2)}, u32[]{:S(2)}) collective-permute-start(bf16[32,2048]{1,0:T(8,128)(2,1)S(1)} %get-tuple-element.60), channel_id=1, source_target_pairs={{0,24},{4,28},{8,16},{12,20},{16,8},{20,12},{24,0},{28,4},{1,25},{... | collective-permute-start | bytes 393224 | tf_op jit(solution)/shard_map/ppermute | solution.py:18
  60.9 0.8 %maximum_bitcast_fusion = f32[2048,64]{0,1:T(8,128)} fusion(f32[64,1024]{1,0:T(8,128)S(1)} %get-tuple-element.55, f32[64,1024]{1,0:T(8,128)S(1)} %get-tuple-element.53), kind=kLoop, calls=%fused_computation | loop fusion | flops 131072 | bytes 1048576 | tf_op jit(solution)/shard_map/transpose | solution.py:223
  61.7 3.7 %collective-permute-done.21 = bf16[32,2048]{1,0:T(8,128)(2,1)S(1)} collective-permute-done((bf16[32,2048]{1,0:T(8,128)(2,1)S(1)}, bf16[32,2048]{1,0:T(8,128)(2,1)S(1)}, u32[]{:S(2)}, u32[]{:S(2)}) %collective-permute-start.21) | collective-permute-done | bytes 131104 | tf_op jit(solution)/shard_map/ppermute | solution.py:18
  65.4 1.2 %collective-permute-done.20 = bf16[32,2048]{1,0:T(8,128)(2,1)S(1)} collective-permute-done((bf16[32,2048]{1,0:T(8,128)(2,1)S(1)}, bf16[32,2048]{1,0:T(8,128)(2,1)S(1)}, u32[]{:S(2)}, u32[]{:S(2)}) %collective-permute-start.20) | collective-permute-done | bytes 131104 | tf_op jit(solution)/shard_map/ppermute | solution.py:18
  66.7 0.8 %fusion.11 = f32[2048,32]{0,1:T(8,128)} fusion(f32[64,2048]{1,0:T(8,128)S(1)} %collective-permute-done.17, bf16[32,2048]{1,0:T(8,128)(2,1)S(1)} %collective-permute-done.21, bf16[32,2048]{1,0:T(8,128)(2,1)S(1)} %collective-permute-done.20, bf16[32,2048]{1,0:T(8,128)(2,1)S(1)} %collective-permute-done.18, f32[64,2048]{1,0:T(8,128)S(1)} %get-tuple-element.47), kind=kLoop, calls=%fused_computation.21 | loop fusion | flops 458752 | bytes 1179648 | tf_op jit(solution)/shard_map/transpose | solution.py:223
  (31 shorter events, 2.4 us)
Async XLA Ops:
  0.6 12.8 %copy-start = (bf16[2048,32]{0,1:T(8,128)(2,1)S(1)}, bf16[2048,32]{0,1:T(8,128)(2,1)}, u32[]{:S(2)}) copy-start(bf16[2048,32]{0,1:T(8,128)(2,1)} %param.5) | copy-start | bytes 393220
  0.6 8.2 %collective-permute-start = (bf16[32,2048]{1,0:T(8,128)(2,1)}, bf16[32,2048]{1,0:T(8,128)(2,1)S(1)}, u32[]{:S(2)}, u32[]{:S(2)}) collective-permute-start(bf16[32,2048]{1,0:T(8,128)(2,1)} %bitcast.5), channel_id=1, source_target_pairs={{0,8},{4,12},{8,0},{12,4},{16,24},{20,28},{24,16},{28,20},{1,9},{5... | collective-permute-start | bytes 393224 | tf_op jit(solution)/shard_map/ppermute | solution.py:18
  3.6 8.0 %collective-permute-start.1 = (bf16[32,2048]{1,0:T(8,128)(2,1)}, bf16[32,2048]{1,0:T(8,128)(2,1)S(1)}, u32[]{:S(2)}, u32[]{:S(2)}) collective-permute-start(bf16[32,2048]{1,0:T(8,128)(2,1)} %bitcast.6), channel_id=1, source_target_pairs={{0,16},{4,20},{8,24},{12,28},{16,0},{20,4},{24,8},{28,12},{1,17},{... | collective-permute-start | bytes 393224 | tf_op jit(solution)/shard_map/ppermute | solution.py:18
  5.2 6.5 %collective-permute-start.2 = (bf16[32,2048]{1,0:T(8,128)(2,1)}, bf16[32,2048]{1,0:T(8,128)(2,1)S(1)}, u32[]{:S(2)}, u32[]{:S(2)}) collective-permute-start(bf16[32,2048]{1,0:T(8,128)(2,1)} %bitcast.7), channel_id=1, source_target_pairs={{0,24},{4,28},{8,16},{12,20},{16,8},{20,12},{24,0},{28,4},{1,25},{... | collective-permute-start | bytes 393224 | tf_op jit(solution)/shard_map/ppermute | solution.py:18
  5.2 6.5 %collective-permute-start.3 = (bf16[32,2048]{1,0:T(8,128)(2,1)}, bf16[32,2048]{1,0:T(8,128)(2,1)S(1)}, u32[]{:S(2)}, u32[]{:S(2)}) collective-permute-start(bf16[32,2048]{1,0:T(8,128)(2,1)} %bitcast.8), channel_id=1, source_target_pairs={{0,4},{4,0},{8,12},{12,8},{16,20},{20,16},{24,28},{28,24},{1,5},{5... | collective-permute-start | bytes 393224 | tf_op jit(solution)/shard_map/ppermute | solution.py:18
  11.7 1.8 %collective-permute-start.4 = (bf16[96,2048]{1,0:T(8,128)(2,1)S(1)}, bf16[96,2048]{1,0:T(8,128)(2,1)S(1)}, u32[]{:S(2)}, u32[]{:S(2)}) collective-permute-start(bf16[96,2048]{1,0:T(8,128)(2,1)S(1)} %pad_maximum_fusion), channel_id=1, source_target_pairs={{0,4},{4,0},{8,12},{12,8},{16,20},{20,16},{24,28},{28,24},{1,5},{5... | collective-permute-start | bytes 1179656 | tf_op jit(solution)/shard_map/ppermute | solution.py:18
  14.8 6.5 %collective-permute-start.5 = (bf16[64,1024]{1,0:T(8,128)(2,1)S(1)}, bf16[64,1024]{1,0:T(8,128)(2,1)S(1)}, u32[]{:S(2)}, u32[]{:S(2)}) collective-permute-start(bf16[64,1024]{1,0:T(8,128)(2,1)S(1)} %get-tuple-element.39), channel_id=1, source_target_pairs={{0,1},{3,2},{2,0},{1,3},{4,5},{7,6},{6,4},{5,7},{8,9},{11,10},{10,... | collective-permute-start | bytes 393224 | tf_op jit(solution)/shard_map/ppermute | solution.py:33
  17.7 8.1 %collective-permute-start.8 = (bf16[64,1024]{1,0:T(8,128)(2,1)S(1)}, bf16[64,1024]{1,0:T(8,128)(2,1)S(1)}, u32[]{:S(2)}, u32[]{:S(2)}) collective-permute-start(bf16[64,1024]{1,0:T(8,128)(2,1)S(1)} %get-tuple-element.45), channel_id=1, source_target_pairs={{0,1},{3,2},{2,0},{1,3},{4,5},{7,6},{6,4},{5,7},{8,9},{11,10},{10,... | collective-permute-start | bytes 393224 | tf_op jit(solution)/shard_map/ppermute | solution.py:33
  21.4 9.0 %collective-permute-start.7 = (bf16[64,1024]{1,0:T(8,128)(2,1)S(1)}, bf16[64,1024]{1,0:T(8,128)(2,1)S(1)}, u32[]{:S(2)}, u32[]{:S(2)}) collective-permute-start(bf16[64,1024]{1,0:T(8,128)(2,1)S(1)} %get-tuple-element.56), channel_id=1, source_target_pairs={{0,3},{1,2},{2,1},{3,0},{4,7},{5,6},{6,5},{7,4},{8,11},{9,10},{10,... | collective-permute-start | bytes 393224 | tf_op jit(solution)/shard_map/ppermute | solution.py:18
  25.8 8.6 %collective-permute-start.6 = (bf16[64,1024]{1,0:T(8,128)(2,1)S(1)}, bf16[64,1024]{1,0:T(8,128)(2,1)S(1)}, u32[]{:S(2)}, u32[]{:S(2)}) collective-permute-start(bf16[64,1024]{1,0:T(8,128)(2,1)S(1)} %get-tuple-element.40), channel_id=1, source_target_pairs={{0,1},{1,0},{2,3},{3,2},{4,5},{5,4},{6,7},{7,6},{8,9},{9,8},{10,11... | collective-permute-start | bytes 393224 | tf_op jit(solution)/shard_map/ppermute | solution.py:18
  25.9 10.2 %collective-permute-start.10 = (bf16[64,1024]{1,0:T(8,128)(2,1)S(1)}, bf16[64,1024]{1,0:T(8,128)(2,1)S(1)}, u32[]{:S(2)}, u32[]{:S(2)}) collective-permute-start(bf16[64,1024]{1,0:T(8,128)(2,1)S(1)} %get-tuple-element.58), channel_id=1, source_target_pairs={{0,3},{1,2},{2,1},{3,0},{4,7},{5,6},{6,5},{7,4},{8,11},{9,10},{10,... | collective-permute-start | bytes 393224 | tf_op jit(solution)/shard_map/ppermute | solution.py:18
  28.6 9.4 %collective-permute-start.9 = (bf16[64,1024]{1,0:T(8,128)(2,1)S(1)}, bf16[64,1024]{1,0:T(8,128)(2,1)S(1)}, u32[]{:S(2)}, u32[]{:S(2)}) collective-permute-start(bf16[64,1024]{1,0:T(8,128)(2,1)S(1)} %get-tuple-element.46), channel_id=1, source_target_pairs={{0,1},{1,0},{2,3},{3,2},{4,5},{5,4},{6,7},{7,6},{8,9},{9,8},{10,11... | collective-permute-start | bytes 393224 | tf_op jit(solution)/shard_map/ppermute | solution.py:18
  34.5 8.3 %collective-permute-start.15 = (bf16[64,1024]{1,0:T(8,128)(2,1)S(1)}, bf16[64,1024]{1,0:T(8,128)(2,1)S(1)}, u32[]{:S(2)}, u32[]{:S(2)}) collective-permute-start(bf16[64,1024]{1,0:T(8,128)(2,1)S(1)} %get-tuple-element.52.refs_0_), channel_id=1, source_target_pairs={{0,3},{1,2},{2,1},{3,0},{4,7},{5,6},{6,5},{7,4},{8,11},{9,10},{10,... | collective-permute-start | bytes 393224 | tf_op jit(solution)/shard_map/ppermute | solution.py:18
  38.1 8.7 %collective-permute-start.12 = (bf16[64,1024]{1,0:T(8,128)(2,1)S(1)}, bf16[64,1024]{1,0:T(8,128)(2,1)S(1)}, u32[]{:S(2)}, u32[]{:S(2)}) collective-permute-start(bf16[64,1024]{1,0:T(8,128)(2,1)S(1)} %get-tuple-element.54.refs_0_), channel_id=1, source_target_pairs={{0,3},{1,2},{2,1},{3,0},{4,7},{5,6},{6,5},{7,4},{8,11},{9,10},{10,... | collective-permute-start | bytes 393224 | tf_op jit(solution)/shard_map/ppermute | solution.py:18
  40.5 13.8 %collective-permute-start.11 = (bf16[64,1024]{1,0:T(8,128)(2,1)S(1)}, bf16[64,1024]{1,0:T(8,128)(2,1)S(1)}, u32[]{:S(2)}, u32[]{:S(2)}) collective-permute-start(bf16[64,1024]{1,0:T(8,128)(2,1)S(1)} %get-tuple-element.54.refs_0_), channel_id=1, source_target_pairs={{0,1},{1,0},{2,3},{3,2},{4,5},{5,4},{6,7},{7,6},{8,9},{9,8},{10,11... | collective-permute-start | bytes 393224 | tf_op jit(solution)/shard_map/ppermute | solution.py:18
  41.0 10.0 %collective-permute-start.14 = (bf16[64,1024]{1,0:T(8,128)(2,1)S(1)}, bf16[64,1024]{1,0:T(8,128)(2,1)S(1)}, u32[]{:S(2)}, u32[]{:S(2)}) collective-permute-start(bf16[64,1024]{1,0:T(8,128)(2,1)S(1)} %get-tuple-element.52.refs_0_), channel_id=1, source_target_pairs={{0,1},{1,0},{2,3},{3,2},{4,5},{5,4},{6,7},{7,6},{8,9},{9,8},{10,11... | collective-permute-start | bytes 393224 | tf_op jit(solution)/shard_map/ppermute | solution.py:18
  42.8 10.2 %collective-permute-start.16 = (bf16[64,1024]{1,0:T(8,128)(2,1)S(1)}, bf16[64,1024]{1,0:T(8,128)(2,1)S(1)}, u32[]{:S(2)}, u32[]{:S(2)}) collective-permute-start(bf16[64,1024]{1,0:T(8,128)(2,1)S(1)} %select_n.26), channel_id=1, source_target_pairs={{0,2},{3,1},{1,0},{2,3},{4,6},{7,5},{5,4},{6,7},{8,10},{11,9},{9,8... | collective-permute-start | bytes 393224 | tf_op jit(solution)/shard_map/ppermute | solution.py:51
  46.8 7.6 %collective-permute-start.13 = (bf16[64,1024]{1,0:T(8,128)(2,1)S(1)}, bf16[64,1024]{1,0:T(8,128)(2,1)S(1)}, u32[]{:S(2)}, u32[]{:S(2)}) collective-permute-start(bf16[64,1024]{1,0:T(8,128)(2,1)S(1)} %select_n.25), channel_id=1, source_target_pairs={{0,2},{3,1},{1,0},{2,3},{4,6},{7,5},{5,4},{6,7},{8,10},{11,9},{9,8... | collective-permute-start | bytes 393224 | tf_op jit(solution)/shard_map/ppermute | solution.py:51
  55.2 2.0 %collective-permute-start.17 = (f32[64,2048]{1,0:T(8,128)S(1)}, f32[64,2048]{1,0:T(8,128)S(1)}, u32[]{:S(2)}, u32[]{:S(2)}) collective-permute-start(f32[64,2048]{1,0:T(8,128)S(1)} %get-tuple-element.48), channel_id=1, source_target_pairs={{0,4},{4,0},{8,12},{12,8},{16,20},{20,16},{24,28},{28,24},{1,5},{5... | collective-permute-start | bytes 1572872 | tf_op jit(solution)/shard_map/ppermute | solution.py:18
  55.3 3.2 %collective-permute-start.19 = (f32[64,2048]{1,0:T(8,128)S(1)}, f32[64,2048]{1,0:T(8,128)S(1)}, u32[]{:S(2)}, u32[]{:S(2)}) collective-permute-start(f32[64,2048]{1,0:T(8,128)S(1)} %get-tuple-element.51), channel_id=1, source_target_pairs={{0,4},{4,0},{8,12},{12,8},{16,20},{20,16},{24,28},{28,24},{1,5},{5... | collective-permute-start | bytes 1572872 | tf_op jit(solution)/shard_map/ppermute | solution.py:18
  57.2 9.5 %collective-permute-start.18 = (bf16[32,2048]{1,0:T(8,128)(2,1)S(1)}, bf16[32,2048]{1,0:T(8,128)(2,1)S(1)}, u32[]{:S(2)}, u32[]{:S(2)}) collective-permute-start(bf16[32,2048]{1,0:T(8,128)(2,1)S(1)} %slice_add_fusion.2), channel_id=1, source_target_pairs={{0,8},{4,12},{8,0},{12,4},{16,24},{20,28},{24,16},{28,20},{1,9},{5... | collective-permute-start | bytes 393224 | tf_op jit(solution)/shard_map/ppermute | solution.py:18
  58.5 6.9 %collective-permute-start.21 = (bf16[32,2048]{1,0:T(8,128)(2,1)S(1)}, bf16[32,2048]{1,0:T(8,128)(2,1)S(1)}, u32[]{:S(2)}, u32[]{:S(2)}) collective-permute-start(bf16[32,2048]{1,0:T(8,128)(2,1)S(1)} %get-tuple-element.61), channel_id=1, source_target_pairs={{0,16},{4,20},{8,24},{12,28},{16,0},{20,4},{24,8},{28,12},{1,17},{... | collective-permute-start | bytes 393224 | tf_op jit(solution)/shard_map/ppermute | solution.py:18
  59.6 7.1 %collective-permute-start.20 = (bf16[32,2048]{1,0:T(8,128)(2,1)S(1)}, bf16[32,2048]{1,0:T(8,128)(2,1)S(1)}, u32[]{:S(2)}, u32[]{:S(2)}) collective-permute-start(bf16[32,2048]{1,0:T(8,128)(2,1)S(1)} %get-tuple-element.60), channel_id=1, source_target_pairs={{0,24},{4,28},{8,16},{12,20},{16,8},{20,12},{24,0},{28,4},{1,25},{... | collective-permute-start | bytes 393224 | tf_op jit(solution)/shard_map/ppermute | solution.py:18

commit v20 on v19

--- a/solution.py
+++ b/solution.py
@@ -190,8 +190,9 @@
     own = probes.T
     held = [own] + [exchange(own, "row", offset) for offset in gather_core[1:]]
     twin = exchange(own, "row", 1)
-    held, twin, token = lax.optimization_barrier((held, twin, token))
-    blocks = held + [twin, exchange(jnp.concatenate(held[1:]), "row", 1)]
+    early, late = held[1:-1], held[-1]
+    early, twin, token = lax.optimization_barrier((early, twin, token))
+    blocks = [own, *early, late, twin, exchange(jnp.concatenate(early), "row", 1), exchange(late, "row", 1)]
 
     totals, shares = [], []
     for chunk in range(chunks):

time: 67.6 us -> 67.5 us (level)
    ppermute x18 -> x19, waiting for transfers between devices: 18.4 us -> 18.3 us  [exchange(): return lax.ppermute(value, axis, [(i, i ^ offset) for i in range(size)])]
    ppermute x18 -> x19, starting transfers between devices: 22 us -> 21.9 us  [exchange(): return lax.ppermute(value, axis, [(i, i ^ offset) for i in range(size)])]
  transfers between devices with their start and end apart: 22 -> 23, of which waited for: 13 -> 14; matrix products, arithmetic and copies ran while one was open for 2% -> 2% of each run, Pallas kernels for 10% -> 10%
where the time goes in v20:
time: 67.5 us; the launch traced here: 67.3 us
  starting transfers between devices  33.9 us (50%)
  waiting for transfers between devices  21.5 us (32%)
  Pallas kernels  9.05 us (13%)
  other arithmetic  2.11 us (3%)
  between operations  0.77 us (1%)
    ppermute x19, starting transfers between devices, exchange(): return lax.ppermute(value, axis, [(i, i ^ offset) for i in range(size)])  21.9 us
    ppermute x19, waiting for transfers between devices, exchange(): return lax.ppermute(value, axis, [(i, i ^ offset) for i in range(size)])  18.3 us
    ppermute x2, starting transfers between devices, window_spread(): lax.ppermute(onward, 'col', [(0, 2), (3, 1), (1, 0), (2, 3)])  7.68 us
    ppermute x2, starting transfers between devices, window_sums(): came = lax.ppermute(terms[2], 'col', [(0, 1), (3, 2), (2, 0), (1, 3)])  4.27 us
    pallas_call x1, Pallas kernels, masked(): pl.pallas_call(functools.partial(mask_kernel, block=rows // mask.shape[0]...  3.66 us
    pallas_call x3, Pallas kernels, partial_adjoint(): pl.pallas_call(functools.partial(adjoint_kernel, base=base, span=span, pa...  2.75 us
    pallas_call x2, Pallas kernels, partial_sketch(): pl.pallas_call(functools.partial(sketch_kernel, base=chunk * rows, offset...  2.64 us
    ppermute x2, waiting for transfers between devices, window_spread(): lax.ppermute(onward, 'col', [(0, 2), (3, 1), (1, 0), (2, 3)])  2.24 us
  transfers between devices with their start and end apart: 23, of which 14 were waited for; matrix products, arithmetic and copies ran while one was open for 2% of the time, Pallas kernels for 10%

profile of v20, /device:TPU:0, one launch (start us, length us, event | category | flops | bytes accessed | tf_op | source)
XLA Modules:
  0.0 67.3 jit_solution(11001005399047287562)
XLA Ops:
  0.6 3.0 %collective-permute-start = (bf16[32,2048]{1,0:T(8,128)(2,1)}, bf16[32,2048]{1,0:T(8,128)(2,1)S(1)}, u32[]{:S(2)}, u32[]{:S(2)}) collective-permute-start(bf16[32,2048]{1,0:T(8,128)(2,1)} %bitcast.5), channel_id=1, source_target_pairs={{0,8},{4,12},{8,0},{12,4},{16,24},{20,28},{24,16},{28,20},{1,9},{5... | collective-permute-start | bytes 393224 | tf_op jit(solution)/shard_map/ppermute | solution.py:18
  3.6 1.5 %collective-permute-start.1 = (bf16[32,2048]{1,0:T(8,128)(2,1)}, bf16[32,2048]{1,0:T(8,128)(2,1)S(1)}, u32[]{:S(2)}, u32[]{:S(2)}) collective-permute-start(bf16[32,2048]{1,0:T(8,128)(2,1)} %bitcast.6), channel_id=1, source_target_pairs={{0,16},{4,20},{8,24},{12,28},{16,0},{20,4},{24,8},{28,12},{1,17},{... | collective-permute-start | bytes 393224 | tf_op jit(solution)/shard_map/ppermute | solution.py:18
  5.2 3.7 %masked_tiles.1 = (bf16[2048,2048]{1,0:T(8,128)(2,1)S(1)}, f32[8,128]{1,0:T(8,128)S(1)}) custom-call(s32[8,8]{1,0:T(8,128)} %mask_hbm.1, bf16[2048,2048]{1,0:T(8,128)(2,1)} %green_ref.1), custom_call_target="tpu_custom_call" | custom-call | bytes 8388608 | tf_op jit(solution)/shard_map/masked_tiles/pallas_call | solution.py:78
  8.9 1.9 %collective-permute-done.1.refs_2_ = bf16[32,2048]{1,0:T(8,128)(2,1)S(1)} collective-permute-done((bf16[32,2048]{1,0:T(8,128)(2,1)}, bf16[32,2048]{1,0:T(8,128)(2,1)S(1)}, u32[]{:S(2)}, u32[]{:S(2)}) %collective-permute-start.1) | collective-permute-done | bytes 131104 | tf_op jit(solution)/shard_map/ppermute | solution.py:18
  10.9 1.3 %collective-permute-done.3.refs_3_ = bf16[32,2048]{1,0:T(8,128)(2,1)S(1)} collective-permute-done((bf16[32,2048]{1,0:T(8,128)(2,1)}, bf16[32,2048]{1,0:T(8,128)(2,1)S(1)}, u32[]{:S(2)}, u32[]{:S(2)}) %collective-permute-start.3) | collective-permute-done | bytes 131104 | tf_op jit(solution)/shard_map/ppermute | solution.py:18
  12.2 1.3 %collective-permute-done.5.refs_6_ = bf16[32,2048]{1,0:T(8,128)(2,1)S(1)} collective-permute-done((bf16[32,2048]{1,0:T(8,128)(2,1)S(1)}, bf16[32,2048]{1,0:T(8,128)(2,1)S(1)}, u32[]{:S(2)}, u32[]{:S(2)}) %collective-permute-start.5) | collective-permute-done | bytes 131104 | tf_op jit(solution)/shard_map/ppermute | solution.py:18
  13.5 1.3 %partial_sketch.2 = (f32[64,1024]{1,0:T(8,128)S(1)}, bf16[64,1024]{1,0:T(8,128)(2,1)S(1)}, bf16[64,1024]{1,0:T(8,128)(2,1)S(1)}, f32[64,1024]{1,0:T(8,128)S(1)}, f32[64,1024]{1,0:T(8,128)S(1)}) custom-call(bf16[2048,2048]{1,0:T(8,128)(2,1)S(1)} %get-tuple-element.25.tiles, f32[8,128]{1,0:T(8,128)S(1)} %get-tuple-element.27.token, ...), custom_call_target="tpu_custom_call" | custom-call | flops 1073741824 | bytes 4194304 | tf_op jit(solution)/shard_map/partial_sketch/pallas_call | solution.py:123
  14.9 1.6 %collective-permute-start.6 = (bf16[64,1024]{1,0:T(8,128)(2,1)S(1)}, bf16[64,1024]{1,0:T(8,128)(2,1)S(1)}, u32[]{:S(2)}, u32[]{:S(2)}) collective-permute-start(bf16[64,1024]{1,0:T(8,128)(2,1)S(1)} %get-tuple-element.35), channel_id=1, source_target_pairs={{0,1},{3,2},{2,0},{1,3},{4,5},{7,6},{6,4},{5,7},{8,9},{11,10},{10,... | collective-permute-start | bytes 393224 | tf_op jit(solution)/shard_map/ppermute | solution.py:33
  16.5 1.3 %partial_sketch.3 = (f32[64,1024]{1,0:T(8,128)S(1)}, bf16[64,1024]{1,0:T(8,128)(2,1)S(1)}, bf16[64,1024]{1,0:T(8,128)(2,1)S(1)}, f32[64,1024]{1,0:T(8,128)S(1)}, f32[64,1024]{1,0:T(8,128)S(1)}) custom-call(bf16[2048,2048]{1,0:T(8,128)(2,1)S(1)} %get-tuple-element.25.tiles, f32[8,128]{1,0:T(8,128)S(1)} %get-tuple-element.27.token, ...), custom_call_target="tpu_custom_call" | custom-call | flops 1073741824 | bytes 4194304 | tf_op jit(solution)/shard_map/partial_sketch/pallas_call | solution.py:123
  17.8 2.6 %collective-permute-start.9 = (bf16[64,1024]{1,0:T(8,128)(2,1)S(1)}, bf16[64,1024]{1,0:T(8,128)(2,1)S(1)}, u32[]{:S(2)}, u32[]{:S(2)}) collective-permute-start(bf16[64,1024]{1,0:T(8,128)(2,1)S(1)} %get-tuple-element.41), channel_id=1, source_target_pairs={{0,1},{3,2},{2,0},{1,3},{4,5},{7,6},{6,4},{5,7},{8,9},{11,10},{10,... | collective-permute-start | bytes 393224 | tf_op jit(solution)/shard_map/ppermute | solution.py:33
  20.5 1.0 %collective-permute-done.6 = bf16[64,1024]{1,0:T(8,128)(2,1)S(1)} collective-permute-done((bf16[64,1024]{1,0:T(8,128)(2,1)S(1)}, bf16[64,1024]{1,0:T(8,128)(2,1)S(1)}, u32[]{:S(2)}, u32[]{:S(2)}) %collective-permute-start.6) | collective-permute-done | bytes 131104 | tf_op jit(solution)/shard_map/ppermute | solution.py:33
  21.5 4.4 %collective-permute-start.8 = (bf16[64,1024]{1,0:T(8,128)(2,1)S(1)}, bf16[64,1024]{1,0:T(8,128)(2,1)S(1)}, u32[]{:S(2)}, u32[]{:S(2)}) collective-permute-start(bf16[64,1024]{1,0:T(8,128)(2,1)S(1)} %get-tuple-element.52), channel_id=1, source_target_pairs={{0,3},{1,2},{2,1},{3,0},{4,7},{5,6},{6,5},{7,4},{8,11},{9,10},{10,... | collective-permute-start | bytes 393224 | tf_op jit(solution)/shard_map/ppermute | solution.py:18
  26.0 2.7 %collective-permute-start.11 = (bf16[64,1024]{1,0:T(8,128)(2,1)S(1)}, bf16[64,1024]{1,0:T(8,128)(2,1)S(1)}, u32[]{:S(2)}, u32[]{:S(2)}) collective-permute-start(bf16[64,1024]{1,0:T(8,128)(2,1)S(1)} %get-tuple-element.54), channel_id=1, source_target_pairs={{0,3},{1,2},{2,1},{3,0},{4,7},{5,6},{6,5},{7,4},{8,11},{9,10},{10,... | collective-permute-start | bytes 393224 | tf_op jit(solution)/shard_map/ppermute | solution.py:18
  28.7 1.8 %collective-permute-done.8 = bf16[64,1024]{1,0:T(8,128)(2,1)S(1)} collective-permute-done((bf16[64,1024]{1,0:T(8,128)(2,1)S(1)}, bf16[64,1024]{1,0:T(8,128)(2,1)S(1)}, u32[]{:S(2)}, u32[]{:S(2)}) %collective-permute-start.8) | collective-permute-done | bytes 131104 | tf_op jit(solution)/shard_map/ppermute | solution.py:18
  30.5 4.1 %collective-permute-done.7 = bf16[64,1024]{1,0:T(8,128)(2,1)S(1)} collective-permute-done((bf16[64,1024]{1,0:T(8,128)(2,1)S(1)}, bf16[64,1024]{1,0:T(8,128)(2,1)S(1)}, u32[]{:S(2)}, u32[]{:S(2)}) %collective-permute-start.7) | collective-permute-done | bytes 131104 | tf_op jit(solution)/shard_map/ppermute | solution.py:18
  34.6 1.6 %collective-permute-start.16 = (bf16[64,1024]{1,0:T(8,128)(2,1)S(1)}, bf16[64,1024]{1,0:T(8,128)(2,1)S(1)}, u32[]{:S(2)}, u32[]{:S(2)}) collective-permute-start(bf16[64,1024]{1,0:T(8,128)(2,1)S(1)} %get-tuple-element.48.refs_0_), channel_id=1, source_target_pairs={{0,3},{1,2},{2,1},{3,0},{4,7},{5,6},{6,5},{7,4},{8,11},{9,10},{10,... | collective-permute-start | bytes 393224 | tf_op jit(solution)/shard_map/ppermute | solution.py:18
  36.2 1.9 %collective-permute-done.10 = bf16[64,1024]{1,0:T(8,128)(2,1)S(1)} collective-permute-done((bf16[64,1024]{1,0:T(8,128)(2,1)S(1)}, bf16[64,1024]{1,0:T(8,128)(2,1)S(1)}, u32[]{:S(2)}, u32[]{:S(2)}) %collective-permute-start.10) | collective-permute-done | bytes 131104 | tf_op jit(solution)/shard_map/ppermute | solution.py:18
  38.2 2.4 %collective-permute-start.13 = (bf16[64,1024]{1,0:T(8,128)(2,1)S(1)}, bf16[64,1024]{1,0:T(8,128)(2,1)S(1)}, u32[]{:S(2)}, u32[]{:S(2)}) collective-permute-start(bf16[64,1024]{1,0:T(8,128)(2,1)S(1)} %get-tuple-element.50.refs_0_), channel_id=1, source_target_pairs={{0,3},{1,2},{2,1},{3,0},{4,7},{5,6},{6,5},{7,4},{8,11},{9,10},{10,... | collective-permute-start | bytes 393224 | tf_op jit(solution)/shard_map/ppermute | solution.py:18
  41.0 1.6 %collective-permute-start.15 = (bf16[64,1024]{1,0:T(8,128)(2,1)S(1)}, bf16[64,1024]{1,0:T(8,128)(2,1)S(1)}, u32[]{:S(2)}, u32[]{:S(2)}) collective-permute-start(bf16[64,1024]{1,0:T(8,128)(2,1)S(1)} %get-tuple-element.48.refs_0_), channel_id=1, source_target_pairs={{0,1},{1,0},{2,3},{3,2},{4,5},{5,4},{6,7},{7,6},{8,9},{9,8},{10,11... | collective-permute-start | bytes 393224 | tf_op jit(solution)/shard_map/ppermute | solution.py:18
  42.9 3.9 %collective-permute-start.17 = (bf16[64,1024]{1,0:T(8,128)(2,1)S(1)}, bf16[64,1024]{1,0:T(8,128)(2,1)S(1)}, u32[]{:S(2)}, u32[]{:S(2)}) collective-permute-start(bf16[64,1024]{1,0:T(8,128)(2,1)S(1)} %select_n.26), channel_id=1, source_target_pairs={{0,2},{3,1},{1,0},{2,3},{4,6},{7,5},{5,4},{6,7},{8,10},{11,9},{9,8... | collective-permute-start | bytes 393224 | tf_op jit(solution)/shard_map/ppermute | solution.py:51
  46.9 3.8 %collective-permute-start.14 = (bf16[64,1024]{1,0:T(8,128)(2,1)S(1)}, bf16[64,1024]{1,0:T(8,128)(2,1)S(1)}, u32[]{:S(2)}, u32[]{:S(2)}) collective-permute-start(bf16[64,1024]{1,0:T(8,128)(2,1)S(1)} %select_n.25), channel_id=1, source_target_pairs={{0,2},{3,1},{1,0},{2,3},{4,6},{7,5},{5,4},{6,7},{8,10},{11,9},{9,8... | collective-permute-start | bytes 393224 | tf_op jit(solution)/shard_map/ppermute | solution.py:51
  51.0 2.1 %collective-permute-done.17.refs_2_ = bf16[64,1024]{1,0:T(8,128)(2,1)S(1)} collective-permute-done((bf16[64,1024]{1,0:T(8,128)(2,1)S(1)}, bf16[64,1024]{1,0:T(8,128)(2,1)S(1)}, u32[]{:S(2)}, u32[]{:S(2)}) %collective-permute-start.17) | collective-permute-done | bytes 131104 | tf_op jit(solution)/shard_map/ppermute | solution.py:51
  53.1 1.3 %partial_adjoint.3.refs_4_ = f32[256,2048]{1,0:T(8,128)S(1)} custom-call(bf16[2048,2048]{1,0:T(8,128)(2,1)S(1)} %get-tuple-element.25.tiles, bf16[64,1024]{1,0:T(8,128)(2,1)S(1)} %get-tuple-element.48.refs_0_, bf16[64,1024]{1,0:T(8,128)(2,1)S(1)} %collective-permute-done.15.refs_1_, bf16[64,1024]{1,0:T(8,128)(2,1)S(1)} %collective-permute-done.17.refs_2_, ...), custom_call_target="tpu_custom_call" | custom-call | tf_op jit(solution)/shard_map/partial_adjoint/pallas_call | solution.py:164
  54.5 0.7 %partial_adjoint.5 = (f32[64,2048]{1,0:T(8,128)S(1)}, f32[64,2048]{1,0:T(8,128)S(1)}) custom-call(bf16[2048,2048]{1,0:T(8,128)(2,1)S(1)} %get-tuple-element.25.tiles, bf16[64,1024]{1,0:T(8,128)(2,1)S(1)} %get-tuple-element.50.refs_0_, bf16[64,1024]{1,0:T(8,128)(2,1)S(1)} %collective-permute-done.12.refs_1_, ...), custom_call_target="tpu_custom_call" | custom-call | tf_op jit(solution)/shard_map/partial_adjoint/pallas_call | solution.py:164
  55.8 0.7 %partial_adjoint.4 = (f32[64,2048]{1,0:T(8,128)S(1)}, f32[64,2048]{1,0:T(8,128)S(1)}) custom-call(bf16[2048,2048]{1,0:T(8,128)(2,1)S(1)} %get-tuple-element.25.tiles, bf16[64,1024]{1,0:T(8,128)(2,1)S(1)} %get-tuple-element.50.refs_0_, bf16[64,1024]{1,0:T(8,128)(2,1)S(1)} %collective-permute-done.12.refs_1_, ...), custom_call_target="tpu_custom_call" | custom-call | tf_op jit(solution)/shard_map/partial_adjoint/pallas_call | solution.py:164
  57.3 0.7 %collective-permute-start.19 = (bf16[32,2048]{1,0:T(8,128)(2,1)S(1)}, bf16[32,2048]{1,0:T(8,128)(2,1)S(1)}, u32[]{:S(2)}, u32[]{:S(2)}) collective-permute-start(bf16[32,2048]{1,0:T(8,128)(2,1)S(1)} %slice_add_fusion.2), channel_id=1, source_target_pairs={{0,8},{4,12},{8,0},{12,4},{16,24},{20,28},{24,16},{28,20},{1,9},{5... | collective-permute-start | bytes 393224 | tf_op jit(solution)/shard_map/ppermute | solution.py:18
  58.1 1.5 %collective-permute-start.22 = (bf16[32,2048]{1,0:T(8,128)(2,1)S(1)}, bf16[32,2048]{1,0:T(8,128)(2,1)S(1)}, u32[]{:S(2)}, u32[]{:S(2)}) collective-permute-start(bf16[32,2048]{1,0:T(8,128)(2,1)S(1)} %get-tuple-element.57), channel_id=1, source_target_pairs={{0,16},{4,20},{8,24},{12,28},{16,0},{20,4},{24,8},{28,12},{1,17},{... | collective-permute-start | bytes 393224 | tf_op jit(solution)/shard_map/ppermute | solution.py:18
  59.5 1.4 %collective-permute-start.21 = (bf16[32,2048]{1,0:T(8,128)(2,1)S(1)}, bf16[32,2048]{1,0:T(8,128)(2,1)S(1)}, u32[]{:S(2)}, u32[]{:S(2)}) collective-permute-start(bf16[32,2048]{1,0:T(8,128)(2,1)S(1)} %get-tuple-element.56), channel_id=1, source_target_pairs={{0,24},{4,28},{8,16},{12,20},{16,8},{20,12},{24,0},{28,4},{1,25},{... | collective-permute-start | bytes 393224 | tf_op jit(solution)/shard_map/ppermute | solution.py:18
  60.9 0.8 %maximum_bitcast_fusion = f32[2048,64]{0,1:T(8,128)} fusion(f32[64,1024]{1,0:T(8,128)S(1)} %get-tuple-element.51, f32[64,1024]{1,0:T(8,128)S(1)} %get-tuple-element.49), kind=kLoop, calls=%fused_computation | loop fusion | flops 131072 | bytes 1048576 | tf_op jit(solution)/shard_map/transpose | solution.py:224
  61.8 3.6 %collective-permute-done.22 = bf16[32,2048]{1,0:T(8,128)(2,1)S(1)} collective-permute-done((bf16[32,2048]{1,0:T(8,128)(2,1)S(1)}, bf16[32,2048]{1,0:T(8,128)(2,1)S(1)}, u32[]{:S(2)}, u32[]{:S(2)}) %collective-permute-start.22) | collective-permute-done | bytes 131104 | tf_op jit(solution)/shard_map/ppermute | solution.py:18
  65.4 1.1 %collective-permute-done.21 = bf16[32,2048]{1,0:T(8,128)(2,1)S(1)} collective-permute-done((bf16[32,2048]{1,0:T(8,128)(2,1)S(1)}, bf16[32,2048]{1,0:T(8,128)(2,1)S(1)}, u32[]{:S(2)}, u32[]{:S(2)}) %collective-permute-start.21) | collective-permute-done | bytes 131104 | tf_op jit(solution)/shard_map/ppermute | solution.py:18
  66.5 0.8 %fusion.11 = f32[2048,32]{0,1:T(8,128)} fusion(f32[64,2048]{1,0:T(8,128)S(1)} %collective-permute-done.18, bf16[32,2048]{1,0:T(8,128)(2,1)S(1)} %collective-permute-done.22, bf16[32,2048]{1,0:T(8,128)(2,1)S(1)} %collective-permute-done.21, bf16[32,2048]{1,0:T(8,128)(2,1)S(1)} %collective-permute-done.19, f32[64,2048]{1,0:T(8,128)S(1)} %get-tuple-element.43), kind=kLoop, calls=%fused_computation.20 | loop fusion | flops 458752 | bytes 1179648 | tf_op jit(solution)/shard_map/transpose | solution.py:224
  (33 shorter events, 3.1 us)
Async XLA Ops:
  0.6 12.9 %copy-start = (bf16[2048,32]{0,1:T(8,128)(2,1)S(1)}, bf16[2048,32]{0,1:T(8,128)(2,1)}, u32[]{:S(2)}) copy-start(bf16[2048,32]{0,1:T(8,128)(2,1)} %param.5) | copy-start | bytes 393220
  0.6 8.2 %collective-permute-start = (bf16[32,2048]{1,0:T(8,128)(2,1)}, bf16[32,2048]{1,0:T(8,128)(2,1)S(1)}, u32[]{:S(2)}, u32[]{:S(2)}) collective-permute-start(bf16[32,2048]{1,0:T(8,128)(2,1)} %bitcast.5), channel_id=1, source_target_pairs={{0,8},{4,12},{8,0},{12,4},{16,24},{20,28},{24,16},{28,20},{1,9},{5... | collective-permute-start | bytes 393224 | tf_op jit(solution)/shard_map/ppermute | solution.py:18
  3.6 7.2 %collective-permute-start.1 = (bf16[32,2048]{1,0:T(8,128)(2,1)}, bf16[32,2048]{1,0:T(8,128)(2,1)S(1)}, u32[]{:S(2)}, u32[]{:S(2)}) collective-permute-start(bf16[32,2048]{1,0:T(8,128)(2,1)} %bitcast.6), channel_id=1, source_target_pairs={{0,16},{4,20},{8,24},{12,28},{16,0},{20,4},{24,8},{28,12},{1,17},{... | collective-permute-start | bytes 393224 | tf_op jit(solution)/shard_map/ppermute | solution.py:18
  5.2 5.6 %collective-permute-start.2 = (bf16[32,2048]{1,0:T(8,128)(2,1)}, bf16[32,2048]{1,0:T(8,128)(2,1)S(1)}, u32[]{:S(2)}, u32[]{:S(2)}) collective-permute-start(bf16[32,2048]{1,0:T(8,128)(2,1)} %bitcast.7), channel_id=1, source_target_pairs={{0,4},{4,0},{8,12},{12,8},{16,20},{20,16},{24,28},{28,24},{1,5},{5... | collective-permute-start | bytes 393224 | tf_op jit(solution)/shard_map/ppermute | solution.py:18
  5.2 7.0 %collective-permute-start.3 = (bf16[32,2048]{1,0:T(8,128)(2,1)}, bf16[32,2048]{1,0:T(8,128)(2,1)S(1)}, u32[]{:S(2)}, u32[]{:S(2)}) collective-permute-start(bf16[32,2048]{1,0:T(8,128)(2,1)} %bitcast.8), channel_id=1, source_target_pairs={{0,24},{4,28},{8,16},{12,20},{16,8},{20,12},{24,0},{28,4},{1,25},{... | collective-permute-start | bytes 393224 | tf_op jit(solution)/shard_map/ppermute | solution.py:18
  10.8 2.7 %collective-permute-start.4 = (bf16[64,2048]{1,0:T(8,128)(2,1)S(1)}, bf16[64,2048]{1,0:T(8,128)(2,1)S(1)}, u32[]{:S(2)}, u32[]{:S(2)}) collective-permute-start(bf16[64,2048]{1,0:T(8,128)(2,1)S(1)} %pad_maximum_fusion), channel_id=1, source_target_pairs={{0,4},{4,0},{8,12},{12,8},{16,20},{20,16},{24,28},{28,24},{1,5},{5... | collective-permute-start | bytes 786440 | tf_op jit(solution)/shard_map/ppermute | solution.py:18
  12.2 1.3 %collective-permute-start.5 = (bf16[32,2048]{1,0:T(8,128)(2,1)S(1)}, bf16[32,2048]{1,0:T(8,128)(2,1)S(1)}, u32[]{:S(2)}, u32[]{:S(2)}) collective-permute-start(bf16[32,2048]{1,0:T(8,128)(2,1)S(1)} %collective-permute-done.3.refs_3_), channel_id=1, source_target_pairs={{0,4},{4,0},{8,12},{12,8},{16,20},{20,16},{24,28},{28,24},{1,5},{5... | collective-permute-start | bytes 393224 | tf_op jit(solution)/shard_map/ppermute | solution.py:18
  14.9 6.6 %collective-permute-start.6 = (bf16[64,1024]{1,0:T(8,128)(2,1)S(1)}, bf16[64,1024]{1,0:T(8,128)(2,1)S(1)}, u32[]{:S(2)}, u32[]{:S(2)}) collective-permute-start(bf16[64,1024]{1,0:T(8,128)(2,1)S(1)} %get-tuple-element.35), channel_id=1, source_target_pairs={{0,1},{3,2},{2,0},{1,3},{4,5},{7,6},{6,4},{5,7},{8,9},{11,10},{10,... | collective-permute-start | bytes 393224 | tf_op jit(solution)/shard_map/ppermute | solution.py:33
  17.8 8.1 %collective-permute-start.9 = (bf16[64,1024]{1,0:T(8,128)(2,1)S(1)}, bf16[64,1024]{1,0:T(8,128)(2,1)S(1)}, u32[]{:S(2)}, u32[]{:S(2)}) collective-permute-start(bf16[64,1024]{1,0:T(8,128)(2,1)S(1)} %get-tuple-element.41), channel_id=1, source_target_pairs={{0,1},{3,2},{2,0},{1,3},{4,5},{7,6},{6,4},{5,7},{8,9},{11,10},{10,... | collective-permute-start | bytes 393224 | tf_op jit(solution)/shard_map/ppermute | solution.py:33
  21.5 8.9 %collective-permute-start.8 = (bf16[64,1024]{1,0:T(8,128)(2,1)S(1)}, bf16[64,1024]{1,0:T(8,128)(2,1)S(1)}, u32[]{:S(2)}, u32[]{:S(2)}) collective-permute-start(bf16[64,1024]{1,0:T(8,128)(2,1)S(1)} %get-tuple-element.52), channel_id=1, source_target_pairs={{0,3},{1,2},{2,1},{3,0},{4,7},{5,6},{6,5},{7,4},{8,11},{9,10},{10,... | collective-permute-start | bytes 393224 | tf_op jit(solution)/shard_map/ppermute | solution.py:18
  25.9 8.6 %collective-permute-start.7 = (bf16[64,1024]{1,0:T(8,128)(2,1)S(1)}, bf16[64,1024]{1,0:T(8,128)(2,1)S(1)}, u32[]{:S(2)}, u32[]{:S(2)}) collective-permute-start(bf16[64,1024]{1,0:T(8,128)(2,1)S(1)} %get-tuple-element.36), channel_id=1, source_target_pairs={{0,1},{1,0},{2,3},{3,2},{4,5},{5,4},{6,7},{7,6},{8,9},{9,8},{10,11... | collective-permute-start | bytes 393224 | tf_op jit(solution)/shard_map/ppermute | solution.py:18
  26.0 10.2 %collective-permute-start.11 = (bf16[64,1024]{1,0:T(8,128)(2,1)S(1)}, bf16[64,1024]{1,0:T(8,128)(2,1)S(1)}, u32[]{:S(2)}, u32[]{:S(2)}) collective-permute-start(bf16[64,1024]{1,0:T(8,128)(2,1)S(1)} %get-tuple-element.54), channel_id=1, source_target_pairs={{0,3},{1,2},{2,1},{3,0},{4,7},{5,6},{6,5},{7,4},{8,11},{9,10},{10,... | collective-permute-start | bytes 393224 | tf_op jit(solution)/shard_map/ppermute | solution.py:18
  28.7 9.4 %collective-permute-start.10 = (bf16[64,1024]{1,0:T(8,128)(2,1)S(1)}, bf16[64,1024]{1,0:T(8,128)(2,1)S(1)}, u32[]{:S(2)}, u32[]{:S(2)}) collective-permute-start(bf16[64,1024]{1,0:T(8,128)(2,1)S(1)} %get-tuple-element.42), channel_id=1, source_target_pairs={{0,1},{1,0},{2,3},{3,2},{4,5},{5,4},{6,7},{7,6},{8,9},{9,8},{10,11... | collective-permute-start | bytes 393224 | tf_op jit(solution)/shard_map/ppermute | solution.py:18
  34.6 8.3 %collective-permute-start.16 = (bf16[64,1024]{1,0:T(8,128)(2,1)S(1)}, bf16[64,1024]{1,0:T(8,128)(2,1)S(1)}, u32[]{:S(2)}, u32[]{:S(2)}) collective-permute-start(bf16[64,1024]{1,0:T(8,128)(2,1)S(1)} %get-tuple-element.48.refs_0_), channel_id=1, source_target_pairs={{0,3},{1,2},{2,1},{3,0},{4,7},{5,6},{6,5},{7,4},{8,11},{9,10},{10,... | collective-permute-start | bytes 393224 | tf_op jit(solution)/shard_map/ppermute | solution.py:18
  38.2 8.7 %collective-permute-start.13 = (bf16[64,1024]{1,0:T(8,128)(2,1)S(1)}, bf16[64,1024]{1,0:T(8,128)(2,1)S(1)}, u32[]{:S(2)}, u32[]{:S(2)}) collective-permute-start(bf16[64,1024]{1,0:T(8,128)(2,1)S(1)} %get-tuple-element.50.refs_0_), channel_id=1, source_target_pairs={{0,3},{1,2},{2,1},{3,0},{4,7},{5,6},{6,5},{7,4},{8,11},{9,10},{10,... | collective-permute-start | bytes 393224 | tf_op jit(solution)/shard_map/ppermute | solution.py:18
  40.6 13.8 %collective-permute-start.12 = (bf16[64,1024]{1,0:T(8,128)(2,1)S(1)}, bf16[64,1024]{1,0:T(8,128)(2,1)S(1)}, u32[]{:S(2)}, u32[]{:S(2)}) collective-permute-start(bf16[64,1024]{1,0:T(8,128)(2,1)S(1)} %get-tuple-element.50.refs_0_), channel_id=1, source_target_pairs={{0,1},{1,0},{2,3},{3,2},{4,5},{5,4},{6,7},{7,6},{8,9},{9,8},{10,11... | collective-permute-start | bytes 393224 | tf_op jit(solution)/shard_map/ppermute | solution.py:18
  41.0 9.9 %collective-permute-start.15 = (bf16[64,1024]{1,0:T(8,128)(2,1)S(1)}, bf16[64,1024]{1,0:T(8,128)(2,1)S(1)}, u32[]{:S(2)}, u32[]{:S(2)}) collective-permute-start(bf16[64,1024]{1,0:T(8,128)(2,1)S(1)} %get-tuple-element.48.refs_0_), channel_id=1, source_target_pairs={{0,1},{1,0},{2,3},{3,2},{4,5},{5,4},{6,7},{7,6},{8,9},{9,8},{10,11... | collective-permute-start | bytes 393224 | tf_op jit(solution)/shard_map/ppermute | solution.py:18
  42.9 10.2 %collective-permute-start.17 = (bf16[64,1024]{1,0:T(8,128)(2,1)S(1)}, bf16[64,1024]{1,0:T(8,128)(2,1)S(1)}, u32[]{:S(2)}, u32[]{:S(2)}) collective-permute-start(bf16[64,1024]{1,0:T(8,128)(2,1)S(1)} %select_n.26), channel_id=1, source_target_pairs={{0,2},{3,1},{1,0},{2,3},{4,6},{7,5},{5,4},{6,7},{8,10},{11,9},{9,8... | collective-permute-start | bytes 393224 | tf_op jit(solution)/shard_map/ppermute | solution.py:51
  46.9 7.6 %collective-permute-start.14 = (bf16[64,1024]{1,0:T(8,128)(2,1)S(1)}, bf16[64,1024]{1,0:T(8,128)(2,1)S(1)}, u32[]{:S(2)}, u32[]{:S(2)}) collective-permute-start(bf16[64,1024]{1,0:T(8,128)(2,1)S(1)} %select_n.25), channel_id=1, source_target_pairs={{0,2},{3,1},{1,0},{2,3},{4,6},{7,5},{5,4},{6,7},{8,10},{11,9},{9,8... | collective-permute-start | bytes 393224 | tf_op jit(solution)/shard_map/ppermute | solution.py:51
  55.3 2.0 %collective-permute-start.18 = (f32[64,2048]{1,0:T(8,128)S(1)}, f32[64,2048]{1,0:T(8,128)S(1)}, u32[]{:S(2)}, u32[]{:S(2)}) collective-permute-start(f32[64,2048]{1,0:T(8,128)S(1)} %get-tuple-element.44), channel_id=1, source_target_pairs={{0,4},{4,0},{8,12},{12,8},{16,20},{20,16},{24,28},{28,24},{1,5},{5... | collective-permute-start | bytes 1572872 | tf_op jit(solution)/shard_map/ppermute | solution.py:18
  55.3 2.7 %collective-permute-start.20 = (f32[64,2048]{1,0:T(8,128)S(1)}, f32[64,2048]{1,0:T(8,128)S(1)}, u32[]{:S(2)}, u32[]{:S(2)}) collective-permute-start(f32[64,2048]{1,0:T(8,128)S(1)} %get-tuple-element.47), channel_id=1, source_target_pairs={{0,4},{4,0},{8,12},{12,8},{16,20},{20,16},{24,28},{28,24},{1,5},{5... | collective-permute-start | bytes 1572872 | tf_op jit(solution)/shard_map/ppermute | solution.py:18
  57.3 9.3 %collective-permute-start.19 = (bf16[32,2048]{1,0:T(8,128)(2,1)S(1)}, bf16[32,2048]{1,0:T(8,128)(2,1)S(1)}, u32[]{:S(2)}, u32[]{:S(2)}) collective-permute-start(bf16[32,2048]{1,0:T(8,128)(2,1)S(1)} %slice_add_fusion.2), channel_id=1, source_target_pairs={{0,8},{4,12},{8,0},{12,4},{16,24},{20,28},{24,16},{28,20},{1,9},{5... | collective-permute-start | bytes 393224 | tf_op jit(solution)/shard_map/ppermute | solution.py:18
  58.1 7.3 %collective-permute-start.22 = (bf16[32,2048]{1,0:T(8,128)(2,1)S(1)}, bf16[32,2048]{1,0:T(8,128)(2,1)S(1)}, u32[]{:S(2)}, u32[]{:S(2)}) collective-permute-start(bf16[32,2048]{1,0:T(8,128)(2,1)S(1)} %get-tuple-element.57), channel_id=1, source_target_pairs={{0,16},{4,20},{8,24},{12,28},{16,0},{20,4},{24,8},{28,12},{1,17},{... | collective-permute-start | bytes 393224 | tf_op jit(solution)/shard_map/ppermute | solution.py:18
  59.5 7.0 %collective-permute-start.21 = (bf16[32,2048]{1,0:T(8,128)(2,1)S(1)}, bf16[32,2048]{1,0:T(8,128)(2,1)S(1)}, u32[]{:S(2)}, u32[]{:S(2)}) collective-permute-start(bf16[32,2048]{1,0:T(8,128)(2,1)S(1)} %get-tuple-element.56), channel_id=1, source_target_pairs={{0,24},{4,28},{8,16},{12,20},{16,8},{20,12},{24,0},{28,4},{1,25},{... | collective-permute-start | bytes 393224 | tf_op jit(solution)/shard_map/ppermute | solution.py:18

commit v21 on v20

--- a/solution.py
+++ b/solution.py
@@ -27,7 +27,7 @@
     return lax.optimization_barrier((value, earlier))[0]
 
 
-def window_sums(terms, ends):
+def window_sums(terms, ends, earlier):
     size = len(terms)
     if size == 4:
         came = lax.ppermute(terms[2], "col", [(0, 1), (3, 2), (2, 0), (1, 3)])
@@ -35,7 +35,7 @@
         onward = terms[3] + jnp.where(ends > 0, 0.0, came)
         onward = onward.astype(BF16)
         far = exchange(onward, "col", 3).astype(F32)
-        near = exchange(after(terms[1], onward), "col", 1).astype(F32)
+        near = exchange(after(terms[1], onward if earlier is None else earlier), "col", 1).astype(F32)
         return terms[0] + near + far + jnp.where(ends > 0, came, 0.0)
     total = terms[0]
     for offset in range(1, size):
@@ -195,9 +195,12 @@
     blocks = [own, *early, late, twin, exchange(jnp.concatenate(early), "row", 1), exchange(late, "row", 1)]
 
     totals, shares = [], []
-    for chunk in range(chunks):
-        *parts, ends = partial_sketch(tiles, blocks, token, offsets_row, offsets_col, chunk, chunks)
-        totals.append(window_sums(parts, ends))
+    parts = [
+        partial_sketch(tiles, blocks, token, offsets_row, offsets_col, chunk, chunks) for chunk in range(chunks)
+    ]
+    for chunk, (*terms, ends) in enumerate(parts):
+        earlier = parts[chunk + 1][-1] if chunk + 1 < chunks else None
+        totals.append(window_sums(terms, ends, earlier))
         shares.append(window_spread(totals[-1].astype(BF16), ends, n_col))
 
     earlier = []

time: 67.5 us -> 69 us (1.022)
  starting transfers between devices: 33.9 us -> 36.2 us
  waiting for transfers between devices: 21.5 us -> 20.8 us
    ppermute x19, starting transfers between devices: 21.9 us -> 25.1 us  [exchange(): return lax.ppermute(value, axis, [(i, i ^ offset) for i in range(size)])]
    ppermute x19, waiting for transfers between devices: 18.3 us -> 16.1 us  [exchange(): return lax.ppermute(value, axis, [(i, i ^ offset) for i in range(size)])]
    ppermute x2, waiting for transfers between devices: 2.24 us -> 4.21 us  [window_spread(): lax.ppermute(onward, 'col', [(0, 2), (3, 1), (1, 0), (2, 3)])]
    ppermute x2, starting transfers between devices: 7.68 us -> 6.78 us  [window_spread(): lax.ppermute(onward, 'col', [(0, 2), (3, 1), (1, 0), (2, 3)])]
  transfers between devices with their start and end apart: 23 -> 23, of which waited for: 14 -> 12; matrix products, arithmetic and copies ran while one was open for 2% -> 2% of each run, Pallas kernels for 10% -> 10%
where the time goes in v21:
time: 69 us; the launch traced here: 68.9 us
  starting transfers between devices  36.2 us (52%)
  waiting for transfers between devices  20.8 us (30%)
  Pallas kernels  9.01 us (13%)
  other arithmetic  2.11 us (3%)
  between operations  0.77 us (1%)
    ppermute x19, starting transfers between devices, exchange(): return lax.ppermute(value, axis, [(i, i ^ offset) for i in range(size)])  25.1 us
    ppermute x19, waiting for transfers between devices, exchange(): return lax.ppermute(value, axis, [(i, i ^ offset) for i in range(size)])  16.1 us
    ppermute x2, starting transfers between devices, window_spread(): lax.ppermute(onward, 'col', [(0, 2), (3, 1), (1, 0), (2, 3)])  6.78 us
    ppermute x2, starting transfers between devices, window_sums(): came = lax.ppermute(terms[2], 'col', [(0, 1), (3, 2), (2, 0), (1, 3)])  4.27 us
    ppermute x2, waiting for transfers between devices, window_spread(): lax.ppermute(onward, 'col', [(0, 2), (3, 1), (1, 0), (2, 3)])  4.21 us
    pallas_call x1, Pallas kernels, masked(): pl.pallas_call(functools.partial(mask_kernel, block=rows // mask.shape[0]...  3.63 us
    pallas_call x3, Pallas kernels, partial_adjoint(): pl.pallas_call(functools.partial(adjoint_kernel, base=base, span=span, pa...  2.74 us
    pallas_call x2, Pallas kernels, partial_sketch(): pl.pallas_call(functools.partial(sketch_kernel, base=chunk * rows, offset...  2.64 us
  transfers between devices with their start and end apart: 23, of which 12 were waited for; matrix products, arithmetic and copies ran while one was open for 2% of the time, Pallas kernels for 10%

profile of v21, /device:TPU:0, one launch (start us, length us, event | category | flops | bytes accessed | tf_op | source)
XLA Modules:
  0.0 68.9 jit_solution(14402296685957453083)
XLA Ops:
  0.6 3.0 %collective-permute-start = (bf16[32,2048]{1,0:T(8,128)(2,1)}, bf16[32,2048]{1,0:T(8,128)(2,1)S(1)}, u32[]{:S(2)}, u32[]{:S(2)}) collective-permute-start(bf16[32,2048]{1,0:T(8,128)(2,1)} %bitcast.5), channel_id=1, source_target_pairs={{0,8},{4,12},{8,0},{12,4},{16,24},{20,28},{24,16},{28,20},{1,9},{5... | collective-permute-start | bytes 393224 | tf_op jit(solution)/shard_map/ppermute | solution.py:18
  3.6 1.5 %collective-permute-start.1 = (bf16[32,2048]{1,0:T(8,128)(2,1)}, bf16[32,2048]{1,0:T(8,128)(2,1)S(1)}, u32[]{:S(2)}, u32[]{:S(2)}) collective-permute-start(bf16[32,2048]{1,0:T(8,128)(2,1)} %bitcast.6), channel_id=1, source_target_pairs={{0,16},{4,20},{8,24},{12,28},{16,0},{20,4},{24,8},{28,12},{1,17},{... | collective-permute-start | bytes 393224 | tf_op jit(solution)/shard_map/ppermute | solution.py:18
  5.2 3.6 %masked_tiles.1 = (bf16[2048,2048]{1,0:T(8,128)(2,1)S(1)}, f32[8,128]{1,0:T(8,128)S(1)}) custom-call(s32[8,8]{1,0:T(8,128)} %mask_hbm.1, bf16[2048,2048]{1,0:T(8,128)(2,1)} %green_ref.1), custom_call_target="tpu_custom_call" | custom-call | bytes 8388608 | tf_op jit(solution)/shard_map/masked_tiles/pallas_call | solution.py:78
  8.8 2.0 %collective-permute-done.1.refs_2_ = bf16[32,2048]{1,0:T(8,128)(2,1)S(1)} collective-permute-done((bf16[32,2048]{1,0:T(8,128)(2,1)}, bf16[32,2048]{1,0:T(8,128)(2,1)S(1)}, u32[]{:S(2)}, u32[]{:S(2)}) %collective-permute-start.1) | collective-permute-done | bytes 131104 | tf_op jit(solution)/shard_map/ppermute | solution.py:18
  10.9 1.3 %collective-permute-done.3.refs_3_ = bf16[32,2048]{1,0:T(8,128)(2,1)S(1)} collective-permute-done((bf16[32,2048]{1,0:T(8,128)(2,1)}, bf16[32,2048]{1,0:T(8,128)(2,1)S(1)}, u32[]{:S(2)}, u32[]{:S(2)}) %collective-permute-start.3) | collective-permute-done | bytes 131104 | tf_op jit(solution)/shard_map/ppermute | solution.py:18
  12.2 1.3 %collective-permute-done.5.refs_6_ = bf16[32,2048]{1,0:T(8,128)(2,1)S(1)} collective-permute-done((bf16[32,2048]{1,0:T(8,128)(2,1)S(1)}, bf16[32,2048]{1,0:T(8,128)(2,1)S(1)}, u32[]{:S(2)}, u32[]{:S(2)}) %collective-permute-start.5) | collective-permute-done | bytes 131104 | tf_op jit(solution)/shard_map/ppermute | solution.py:18
  13.5 1.3 %partial_sketch.2 = (f32[64,1024]{1,0:T(8,128)S(1)}, bf16[64,1024]{1,0:T(8,128)(2,1)S(1)}, bf16[64,1024]{1,0:T(8,128)(2,1)S(1)}, f32[64,1024]{1,0:T(8,128)S(1)}, f32[64,1024]{1,0:T(8,128)S(1)}) custom-call(bf16[2048,2048]{1,0:T(8,128)(2,1)S(1)} %get-tuple-element.25.tiles, f32[8,128]{1,0:T(8,128)S(1)} %get-tuple-element.27.token, ...), custom_call_target="tpu_custom_call" | custom-call | flops 1073741824 | bytes 4194304 | tf_op jit(solution)/shard_map/partial_sketch/pallas_call | solution.py:123
  14.9 1.6 %collective-permute-start.7 = (bf16[64,1024]{1,0:T(8,128)(2,1)S(1)}, bf16[64,1024]{1,0:T(8,128)(2,1)S(1)}, u32[]{:S(2)}, u32[]{:S(2)}) collective-permute-start(bf16[64,1024]{1,0:T(8,128)(2,1)S(1)} %get-tuple-element.37), channel_id=1, source_target_pairs={{0,1},{3,2},{2,0},{1,3},{4,5},{7,6},{6,4},{5,7},{8,9},{11,10},{10,... | collective-permute-start | bytes 393224 | tf_op jit(solution)/shard_map/ppermute | solution.py:33
  16.5 1.3 %partial_sketch.3 = (f32[64,1024]{1,0:T(8,128)S(1)}, bf16[64,1024]{1,0:T(8,128)(2,1)S(1)}, bf16[64,1024]{1,0:T(8,128)(2,1)S(1)}, f32[64,1024]{1,0:T(8,128)S(1)}, f32[64,1024]{1,0:T(8,128)S(1)}) custom-call(bf16[2048,2048]{1,0:T(8,128)(2,1)S(1)} %get-tuple-element.25.tiles, f32[8,128]{1,0:T(8,128)S(1)} %get-tuple-element.27.token, ...), custom_call_target="tpu_custom_call" | custom-call | flops 1073741824 | bytes 4194304 | tf_op jit(solution)/shard_map/partial_sketch/pallas_call | solution.py:123
  17.8 2.6 %collective-permute-start.9 = (bf16[64,1024]{1,0:T(8,128)(2,1)S(1)}, bf16[64,1024]{1,0:T(8,128)(2,1)S(1)}, u32[]{:S(2)}, u32[]{:S(2)}) collective-permute-start(bf16[64,1024]{1,0:T(8,128)(2,1)S(1)} %get-tuple-element.41), channel_id=1, source_target_pairs={{0,1},{3,2},{2,0},{1,3},{4,5},{7,6},{6,4},{5,7},{8,9},{11,10},{10,... | collective-permute-start | bytes 393224 | tf_op jit(solution)/shard_map/ppermute | solution.py:33
  21.5 4.5 %collective-permute-start.8 = (bf16[64,1024]{1,0:T(8,128)(2,1)S(1)}, bf16[64,1024]{1,0:T(8,128)(2,1)S(1)}, u32[]{:S(2)}, u32[]{:S(2)}) collective-permute-start(bf16[64,1024]{1,0:T(8,128)(2,1)S(1)} %get-tuple-element.52), channel_id=1, source_target_pairs={{0,3},{1,2},{2,1},{3,0},{4,7},{5,6},{6,5},{7,4},{8,11},{9,10},{10,... | collective-permute-start | bytes 393224 | tf_op jit(solution)/shard_map/ppermute | solution.py:18
  26.1 2.7 %collective-permute-start.11 = (bf16[64,1024]{1,0:T(8,128)(2,1)S(1)}, bf16[64,1024]{1,0:T(8,128)(2,1)S(1)}, u32[]{:S(2)}, u32[]{:S(2)}) collective-permute-start(bf16[64,1024]{1,0:T(8,128)(2,1)S(1)} %get-tuple-element.54), channel_id=1, source_target_pairs={{0,3},{1,2},{2,1},{3,0},{4,7},{5,6},{6,5},{7,4},{8,11},{9,10},{10,... | collective-permute-start | bytes 393224 | tf_op jit(solution)/shard_map/ppermute | solution.py:18
  28.8 3.2 %collective-permute-done.8 = bf16[64,1024]{1,0:T(8,128)(2,1)S(1)} collective-permute-done((bf16[64,1024]{1,0:T(8,128)(2,1)S(1)}, bf16[64,1024]{1,0:T(8,128)(2,1)S(1)}, u32[]{:S(2)}, u32[]{:S(2)}) %collective-permute-start.8) | collective-permute-done | bytes 131104 | tf_op jit(solution)/shard_map/ppermute | solution.py:18
  32.0 3.6 %collective-permute-start.16 = (bf16[64,1024]{1,0:T(8,128)(2,1)S(1)}, bf16[64,1024]{1,0:T(8,128)(2,1)S(1)}, u32[]{:S(2)}, u32[]{:S(2)}) collective-permute-start(bf16[64,1024]{1,0:T(8,128)(2,1)S(1)} %get-tuple-element.48.refs_0_), channel_id=1, source_target_pairs={{0,3},{1,2},{2,1},{3,0},{4,7},{5,6},{6,5},{7,4},{8,11},{9,10},{10,... | collective-permute-start | bytes 393224 | tf_op jit(solution)/shard_map/ppermute | solution.py:18
  35.6 1.8 %collective-permute-done.10 = bf16[64,1024]{1,0:T(8,128)(2,1)S(1)} collective-permute-done((bf16[64,1024]{1,0:T(8,128)(2,1)S(1)}, bf16[64,1024]{1,0:T(8,128)(2,1)S(1)}, u32[]{:S(2)}, u32[]{:S(2)}) %collective-permute-start.10) | collective-permute-done | bytes 131104 | tf_op jit(solution)/shard_map/ppermute | solution.py:18
  37.5 3.0 %collective-permute-start.13 = (bf16[64,1024]{1,0:T(8,128)(2,1)S(1)}, bf16[64,1024]{1,0:T(8,128)(2,1)S(1)}, u32[]{:S(2)}, u32[]{:S(2)}) collective-permute-start(bf16[64,1024]{1,0:T(8,128)(2,1)S(1)} %get-tuple-element.50.refs_0_), channel_id=1, source_target_pairs={{0,3},{1,2},{2,1},{3,0},{4,7},{5,6},{6,5},{7,4},{8,11},{9,10},{10,... | collective-permute-start | bytes 393224 | tf_op jit(solution)/shard_map/ppermute | solution.py:18
  40.6 1.9 %collective-permute-start.12 = (bf16[64,1024]{1,0:T(8,128)(2,1)S(1)}, bf16[64,1024]{1,0:T(8,128)(2,1)S(1)}, u32[]{:S(2)}, u32[]{:S(2)}) collective-permute-start(bf16[64,1024]{1,0:T(8,128)(2,1)S(1)} %get-tuple-element.50.refs_0_), channel_id=1, source_target_pairs={{0,1},{1,0},{2,3},{3,2},{4,5},{5,4},{6,7},{7,6},{8,9},{9,8},{10,11... | collective-permute-start | bytes 393224 | tf_op jit(solution)/shard_map/ppermute | solution.py:18
  42.7 4.3 %collective-permute-start.17 = (bf16[64,1024]{1,0:T(8,128)(2,1)S(1)}, bf16[64,1024]{1,0:T(8,128)(2,1)S(1)}, u32[]{:S(2)}, u32[]{:S(2)}) collective-permute-start(bf16[64,1024]{1,0:T(8,128)(2,1)S(1)} %select_n.26), channel_id=1, source_target_pairs={{0,2},{3,1},{1,0},{2,3},{4,6},{7,5},{5,4},{6,7},{8,10},{11,9},{9,8... | collective-permute-start | bytes 393224 | tf_op jit(solution)/shard_map/ppermute | solution.py:51
  47.0 2.5 %collective-permute-start.14 = (bf16[64,1024]{1,0:T(8,128)(2,1)S(1)}, bf16[64,1024]{1,0:T(8,128)(2,1)S(1)}, u32[]{:S(2)}, u32[]{:S(2)}) collective-permute-start(bf16[64,1024]{1,0:T(8,128)(2,1)S(1)} %select_n.25), channel_id=1, source_target_pairs={{0,2},{3,1},{1,0},{2,3},{4,6},{7,5},{5,4},{6,7},{8,10},{11,9},{9,8... | collective-permute-start | bytes 393224 | tf_op jit(solution)/shard_map/ppermute | solution.py:51
  49.5 1.1 %collective-permute-done.15.refs_1_ = bf16[64,1024]{1,0:T(8,128)(2,1)S(1)} collective-permute-done((bf16[64,1024]{1,0:T(8,128)(2,1)S(1)}, bf16[64,1024]{1,0:T(8,128)(2,1)S(1)}, u32[]{:S(2)}, u32[]{:S(2)}) %collective-permute-start.15) | collective-permute-done | bytes 131104 | tf_op jit(solution)/shard_map/ppermute | solution.py:18
  50.6 2.8 %collective-permute-done.17.refs_2_ = bf16[64,1024]{1,0:T(8,128)(2,1)S(1)} collective-permute-done((bf16[64,1024]{1,0:T(8,128)(2,1)S(1)}, bf16[64,1024]{1,0:T(8,128)(2,1)S(1)}, u32[]{:S(2)}, u32[]{:S(2)}) %collective-permute-start.17) | collective-permute-done | bytes 131104 | tf_op jit(solution)/shard_map/ppermute | solution.py:51
  53.4 1.3 %partial_adjoint.3.refs_4_ = f32[256,2048]{1,0:T(8,128)S(1)} custom-call(bf16[2048,2048]{1,0:T(8,128)(2,1)S(1)} %get-tuple-element.25.tiles, bf16[64,1024]{1,0:T(8,128)(2,1)S(1)} %get-tuple-element.48.refs_0_, bf16[64,1024]{1,0:T(8,128)(2,1)S(1)} %collective-permute-done.15.refs_1_, bf16[64,1024]{1,0:T(8,128)(2,1)S(1)} %collective-permute-done.17.refs_2_, ...), custom_call_target="tpu_custom_call" | custom-call | tf_op jit(solution)/shard_map/partial_adjoint/pallas_call | solution.py:164
  54.7 1.4 %collective-permute-done.14.refs_2_ = bf16[64,1024]{1,0:T(8,128)(2,1)S(1)} collective-permute-done((bf16[64,1024]{1,0:T(8,128)(2,1)S(1)}, bf16[64,1024]{1,0:T(8,128)(2,1)S(1)}, u32[]{:S(2)}, u32[]{:S(2)}) %collective-permute-start.14) | collective-permute-done | bytes 131104 | tf_op jit(solution)/shard_map/ppermute | solution.py:51
  56.1 0.7 %partial_adjoint.5 = (f32[64,2048]{1,0:T(8,128)S(1)}, f32[64,2048]{1,0:T(8,128)S(1)}) custom-call(bf16[2048,2048]{1,0:T(8,128)(2,1)S(1)} %get-tuple-element.25.tiles, bf16[64,1024]{1,0:T(8,128)(2,1)S(1)} %get-tuple-element.50.refs_0_, bf16[64,1024]{1,0:T(8,128)(2,1)S(1)} %collective-permute-done.12.refs_1_, ...), custom_call_target="tpu_custom_call" | custom-call | tf_op jit(solution)/shard_map/partial_adjoint/pallas_call | solution.py:164
  57.4 0.7 %partial_adjoint.4 = (f32[64,2048]{1,0:T(8,128)S(1)}, f32[64,2048]{1,0:T(8,128)S(1)}) custom-call(bf16[2048,2048]{1,0:T(8,128)(2,1)S(1)} %get-tuple-element.25.tiles, bf16[64,1024]{1,0:T(8,128)(2,1)S(1)} %get-tuple-element.50.refs_0_, bf16[64,1024]{1,0:T(8,128)(2,1)S(1)} %collective-permute-done.12.refs_1_, ...), custom_call_target="tpu_custom_call" | custom-call | tf_op jit(solution)/shard_map/partial_adjoint/pallas_call | solution.py:164
  58.8 0.7 %collective-permute-start.19 = (bf16[32,2048]{1,0:T(8,128)(2,1)S(1)}, bf16[32,2048]{1,0:T(8,128)(2,1)S(1)}, u32[]{:S(2)}, u32[]{:S(2)}) collective-permute-start(bf16[32,2048]{1,0:T(8,128)(2,1)S(1)} %slice_add_fusion.2), channel_id=1, source_target_pairs={{0,8},{4,12},{8,0},{12,4},{16,24},{20,28},{24,16},{28,20},{1,9},{5... | collective-permute-start | bytes 393224 | tf_op jit(solution)/shard_map/ppermute | solution.py:18
  59.6 1.5 %collective-permute-start.22 = (bf16[32,2048]{1,0:T(8,128)(2,1)S(1)}, bf16[32,2048]{1,0:T(8,128)(2,1)S(1)}, u32[]{:S(2)}, u32[]{:S(2)}) collective-permute-start(bf16[32,2048]{1,0:T(8,128)(2,1)S(1)} %get-tuple-element.57), channel_id=1, source_target_pairs={{0,16},{4,20},{8,24},{12,28},{16,0},{20,4},{24,8},{28,12},{1,17},{... | collective-permute-start | bytes 393224 | tf_op jit(solution)/shard_map/ppermute | solution.py:18
  61.1 1.4 %collective-permute-start.21 = (bf16[32,2048]{1,0:T(8,128)(2,1)S(1)}, bf16[32,2048]{1,0:T(8,128)(2,1)S(1)}, u32[]{:S(2)}, u32[]{:S(2)}) collective-permute-start(bf16[32,2048]{1,0:T(8,128)(2,1)S(1)} %get-tuple-element.56), channel_id=1, source_target_pairs={{0,24},{4,28},{8,16},{12,20},{16,8},{20,12},{24,0},{28,4},{1,25},{... | collective-permute-start | bytes 393224 | tf_op jit(solution)/shard_map/ppermute | solution.py:18
  62.5 0.8 %maximum_bitcast_fusion = f32[2048,64]{0,1:T(8,128)} fusion(f32[64,1024]{1,0:T(8,128)S(1)} %get-tuple-element.51, f32[64,1024]{1,0:T(8,128)S(1)} %get-tuple-element.49), kind=kLoop, calls=%fused_computation | loop fusion | flops 131072 | bytes 1048576 | tf_op jit(solution)/shard_map/transpose | solution.py:227
  63.3 3.6 %collective-permute-done.22 = bf16[32,2048]{1,0:T(8,128)(2,1)S(1)} collective-permute-done((bf16[32,2048]{1,0:T(8,128)(2,1)S(1)}, bf16[32,2048]{1,0:T(8,128)(2,1)S(1)}, u32[]{:S(2)}, u32[]{:S(2)}) %collective-permute-start.22) | collective-permute-done | bytes 131104 | tf_op jit(solution)/shard_map/ppermute | solution.py:18
  67.0 1.1 %collective-permute-done.21 = bf16[32,2048]{1,0:T(8,128)(2,1)S(1)} collective-permute-done((bf16[32,2048]{1,0:T(8,128)(2,1)S(1)}, bf16[32,2048]{1,0:T(8,128)(2,1)S(1)}, u32[]{:S(2)}, u32[]{:S(2)}) %collective-permute-start.21) | collective-permute-done | bytes 131104 | tf_op jit(solution)/shard_map/ppermute | solution.py:18
  68.1 0.8 %fusion.11 = f32[2048,32]{0,1:T(8,128)} fusion(f32[64,2048]{1,0:T(8,128)S(1)} %collective-permute-done.18, bf16[32,2048]{1,0:T(8,128)(2,1)S(1)} %collective-permute-done.22, bf16[32,2048]{1,0:T(8,128)(2,1)S(1)} %collective-permute-done.21, bf16[32,2048]{1,0:T(8,128)(2,1)S(1)} %collective-permute-done.19, f32[64,2048]{1,0:T(8,128)S(1)} %get-tuple-element.43), kind=kLoop, calls=%fused_computation.20 | loop fusion | flops 458752 | bytes 1179648 | tf_op jit(solution)/shard_map/transpose | solution.py:227
  (33 shorter events, 3.0 us)
Async XLA Ops:
  0.6 12.9 %copy-start = (bf16[2048,32]{0,1:T(8,128)(2,1)S(1)}, bf16[2048,32]{0,1:T(8,128)(2,1)}, u32[]{:S(2)}) copy-start(bf16[2048,32]{0,1:T(8,128)(2,1)} %param.5) | copy-start | bytes 393220
  0.6 8.2 %collective-permute-start = (bf16[32,2048]{1,0:T(8,128)(2,1)}, bf16[32,2048]{1,0:T(8,128)(2,1)S(1)}, u32[]{:S(2)}, u32[]{:S(2)}) collective-permute-start(bf16[32,2048]{1,0:T(8,128)(2,1)} %bitcast.5), channel_id=1, source_target_pairs={{0,8},{4,12},{8,0},{12,4},{16,24},{20,28},{24,16},{28,20},{1,9},{5... | collective-permute-start | bytes 393224 | tf_op jit(solution)/shard_map/ppermute | solution.py:18
  3.6 7.2 %collective-permute-start.1 = (bf16[32,2048]{1,0:T(8,128)(2,1)}, bf16[32,2048]{1,0:T(8,128)(2,1)S(1)}, u32[]{:S(2)}, u32[]{:S(2)}) collective-permute-start(bf16[32,2048]{1,0:T(8,128)(2,1)} %bitcast.6), channel_id=1, source_target_pairs={{0,16},{4,20},{8,24},{12,28},{16,0},{20,4},{24,8},{28,12},{1,17},{... | collective-permute-start | bytes 393224 | tf_op jit(solution)/shard_map/ppermute | solution.py:18
  5.2 5.6 %collective-permute-start.2 = (bf16[32,2048]{1,0:T(8,128)(2,1)}, bf16[32,2048]{1,0:T(8,128)(2,1)S(1)}, u32[]{:S(2)}, u32[]{:S(2)}) collective-permute-start(bf16[32,2048]{1,0:T(8,128)(2,1)} %bitcast.7), channel_id=1, source_target_pairs={{0,4},{4,0},{8,12},{12,8},{16,20},{20,16},{24,28},{28,24},{1,5},{5... | collective-permute-start | bytes 393224 | tf_op jit(solution)/shard_map/ppermute | solution.py:18
  5.2 7.0 %collective-permute-start.3 = (bf16[32,2048]{1,0:T(8,128)(2,1)}, bf16[32,2048]{1,0:T(8,128)(2,1)S(1)}, u32[]{:S(2)}, u32[]{:S(2)}) collective-permute-start(bf16[32,2048]{1,0:T(8,128)(2,1)} %bitcast.8), channel_id=1, source_target_pairs={{0,24},{4,28},{8,16},{12,20},{16,8},{20,12},{24,0},{28,4},{1,25},{... | collective-permute-start | bytes 393224 | tf_op jit(solution)/shard_map/ppermute | solution.py:18
  10.8 2.7 %collective-permute-start.4 = (bf16[64,2048]{1,0:T(8,128)(2,1)S(1)}, bf16[64,2048]{1,0:T(8,128)(2,1)S(1)}, u32[]{:S(2)}, u32[]{:S(2)}) collective-permute-start(bf16[64,2048]{1,0:T(8,128)(2,1)S(1)} %pad_maximum_fusion), channel_id=1, source_target_pairs={{0,4},{4,0},{8,12},{12,8},{16,20},{20,16},{24,28},{28,24},{1,5},{5... | collective-permute-start | bytes 786440 | tf_op jit(solution)/shard_map/ppermute | solution.py:18
  12.2 1.3 %collective-permute-start.5 = (bf16[32,2048]{1,0:T(8,128)(2,1)S(1)}, bf16[32,2048]{1,0:T(8,128)(2,1)S(1)}, u32[]{:S(2)}, u32[]{:S(2)}) collective-permute-start(bf16[32,2048]{1,0:T(8,128)(2,1)S(1)} %collective-permute-done.3.refs_3_), channel_id=1, source_target_pairs={{0,4},{4,0},{8,12},{12,8},{16,20},{20,16},{24,28},{28,24},{1,5},{5... | collective-permute-start | bytes 393224 | tf_op jit(solution)/shard_map/ppermute | solution.py:18
  14.9 6.6 %collective-permute-start.7 = (bf16[64,1024]{1,0:T(8,128)(2,1)S(1)}, bf16[64,1024]{1,0:T(8,128)(2,1)S(1)}, u32[]{:S(2)}, u32[]{:S(2)}) collective-permute-start(bf16[64,1024]{1,0:T(8,128)(2,1)S(1)} %get-tuple-element.37), channel_id=1, source_target_pairs={{0,1},{3,2},{2,0},{1,3},{4,5},{7,6},{6,4},{5,7},{8,9},{11,10},{10,... | collective-permute-start | bytes 393224 | tf_op jit(solution)/shard_map/ppermute | solution.py:33
  17.8 8.2 %collective-permute-start.9 = (bf16[64,1024]{1,0:T(8,128)(2,1)S(1)}, bf16[64,1024]{1,0:T(8,128)(2,1)S(1)}, u32[]{:S(2)}, u32[]{:S(2)}) collective-permute-start(bf16[64,1024]{1,0:T(8,128)(2,1)S(1)} %get-tuple-element.41), channel_id=1, source_target_pairs={{0,1},{3,2},{2,0},{1,3},{4,5},{7,6},{6,4},{5,7},{8,9},{11,10},{10,... | collective-permute-start | bytes 393224 | tf_op jit(solution)/shard_map/ppermute | solution.py:33
  20.5 8.3 %collective-permute-start.6 = (bf16[64,1024]{1,0:T(8,128)(2,1)S(1)}, bf16[64,1024]{1,0:T(8,128)(2,1)S(1)}, u32[]{:S(2)}, u32[]{:S(2)}) collective-permute-start(bf16[64,1024]{1,0:T(8,128)(2,1)S(1)} %get-tuple-element.34), channel_id=1, source_target_pairs={{0,1},{1,0},{2,3},{3,2},{4,5},{5,4},{6,7},{7,6},{8,9},{9,8},{10,11... | collective-permute-start | bytes 393224 | tf_op jit(solution)/shard_map/ppermute | solution.py:18
  21.5 10.4 %collective-permute-start.8 = (bf16[64,1024]{1,0:T(8,128)(2,1)S(1)}, bf16[64,1024]{1,0:T(8,128)(2,1)S(1)}, u32[]{:S(2)}, u32[]{:S(2)}) collective-permute-start(bf16[64,1024]{1,0:T(8,128)(2,1)S(1)} %get-tuple-element.52), channel_id=1, source_target_pairs={{0,3},{1,2},{2,1},{3,0},{4,7},{5,6},{6,5},{7,4},{8,11},{9,10},{10,... | collective-permute-start | bytes 393224 | tf_op jit(solution)/shard_map/ppermute | solution.py:18
  26.1 9.6 %collective-permute-start.11 = (bf16[64,1024]{1,0:T(8,128)(2,1)S(1)}, bf16[64,1024]{1,0:T(8,128)(2,1)S(1)}, u32[]{:S(2)}, u32[]{:S(2)}) collective-permute-start(bf16[64,1024]{1,0:T(8,128)(2,1)S(1)} %get-tuple-element.54), channel_id=1, source_target_pairs={{0,3},{1,2},{2,1},{3,0},{4,7},{5,6},{6,5},{7,4},{8,11},{9,10},{10,... | collective-permute-start | bytes 393224 | tf_op jit(solution)/shard_map/ppermute | solution.py:18
  28.7 8.7 %collective-permute-start.10 = (bf16[64,1024]{1,0:T(8,128)(2,1)S(1)}, bf16[64,1024]{1,0:T(8,128)(2,1)S(1)}, u32[]{:S(2)}, u32[]{:S(2)}) collective-permute-start(bf16[64,1024]{1,0:T(8,128)(2,1)S(1)} %get-tuple-element.42), channel_id=1, source_target_pairs={{0,1},{1,0},{2,3},{3,2},{4,5},{5,4},{6,7},{7,6},{8,9},{9,8},{10,11... | collective-permute-start | bytes 393224 | tf_op jit(solution)/shard_map/ppermute | solution.py:18
  32.0 10.6 %collective-permute-start.16 = (bf16[64,1024]{1,0:T(8,128)(2,1)S(1)}, bf16[64,1024]{1,0:T(8,128)(2,1)S(1)}, u32[]{:S(2)}, u32[]{:S(2)}) collective-permute-start(bf16[64,1024]{1,0:T(8,128)(2,1)S(1)} %get-tuple-element.48.refs_0_), channel_id=1, source_target_pairs={{0,3},{1,2},{2,1},{3,0},{4,7},{5,6},{6,5},{7,4},{8,11},{9,10},{10,... | collective-permute-start | bytes 393224 | tf_op jit(solution)/shard_map/ppermute | solution.py:18
  37.5 9.4 %collective-permute-start.13 = (bf16[64,1024]{1,0:T(8,128)(2,1)S(1)}, bf16[64,1024]{1,0:T(8,128)(2,1)S(1)}, u32[]{:S(2)}, u32[]{:S(2)}) collective-permute-start(bf16[64,1024]{1,0:T(8,128)(2,1)S(1)} %get-tuple-element.50.refs_0_), channel_id=1, source_target_pairs={{0,3},{1,2},{2,1},{3,0},{4,7},{5,6},{6,5},{7,4},{8,11},{9,10},{10,... | collective-permute-start | bytes 393224 | tf_op jit(solution)/shard_map/ppermute | solution.py:18
  40.6 14.1 %collective-permute-start.12 = (bf16[64,1024]{1,0:T(8,128)(2,1)S(1)}, bf16[64,1024]{1,0:T(8,128)(2,1)S(1)}, u32[]{:S(2)}, u32[]{:S(2)}) collective-permute-start(bf16[64,1024]{1,0:T(8,128)(2,1)S(1)} %get-tuple-element.50.refs_0_), channel_id=1, source_target_pairs={{0,1},{1,0},{2,3},{3,2},{4,5},{5,4},{6,7},{7,6},{8,9},{9,8},{10,11... | collective-permute-start | bytes 393224 | tf_op jit(solution)/shard_map/ppermute | solution.py:18
  42.5 8.1 %collective-permute-start.15 = (bf16[64,1024]{1,0:T(8,128)(2,1)S(1)}, bf16[64,1024]{1,0:T(8,128)(2,1)S(1)}, u32[]{:S(2)}, u32[]{:S(2)}) collective-permute-start(bf16[64,1024]{1,0:T(8,128)(2,1)S(1)} %get-tuple-element.48.refs_0_), channel_id=1, source_target_pairs={{0,1},{1,0},{2,3},{3,2},{4,5},{5,4},{6,7},{7,6},{8,9},{9,8},{10,11... | collective-permute-start | bytes 393224 | tf_op jit(solution)/shard_map/ppermute | solution.py:18
  42.7 10.7 %collective-permute-start.17 = (bf16[64,1024]{1,0:T(8,128)(2,1)S(1)}, bf16[64,1024]{1,0:T(8,128)(2,1)S(1)}, u32[]{:S(2)}, u32[]{:S(2)}) collective-permute-start(bf16[64,1024]{1,0:T(8,128)(2,1)S(1)} %select_n.26), channel_id=1, source_target_pairs={{0,2},{3,1},{1,0},{2,3},{4,6},{7,5},{5,4},{6,7},{8,10},{11,9},{9,8... | collective-permute-start | bytes 393224 | tf_op jit(solution)/shard_map/ppermute | solution.py:51
  47.0 9.0 %collective-permute-start.14 = (bf16[64,1024]{1,0:T(8,128)(2,1)S(1)}, bf16[64,1024]{1,0:T(8,128)(2,1)S(1)}, u32[]{:S(2)}, u32[]{:S(2)}) collective-permute-start(bf16[64,1024]{1,0:T(8,128)(2,1)S(1)} %select_n.25), channel_id=1, source_target_pairs={{0,2},{3,1},{1,0},{2,3},{4,6},{7,5},{5,4},{6,7},{8,10},{11,9},{9,8... | collective-permute-start | bytes 393224 | tf_op jit(solution)/shard_map/ppermute | solution.py:51
  56.8 2.0 %collective-permute-start.18 = (f32[64,2048]{1,0:T(8,128)S(1)}, f32[64,2048]{1,0:T(8,128)S(1)}, u32[]{:S(2)}, u32[]{:S(2)}) collective-permute-start(f32[64,2048]{1,0:T(8,128)S(1)} %get-tuple-element.44), channel_id=1, source_target_pairs={{0,4},{4,0},{8,12},{12,8},{16,20},{20,16},{24,28},{28,24},{1,5},{5... | collective-permute-start | bytes 1572872 | tf_op jit(solution)/shard_map/ppermute | solution.py:18
  56.9 2.7 %collective-permute-start.20 = (f32[64,2048]{1,0:T(8,128)S(1)}, f32[64,2048]{1,0:T(8,128)S(1)}, u32[]{:S(2)}, u32[]{:S(2)}) collective-permute-start(f32[64,2048]{1,0:T(8,128)S(1)} %get-tuple-element.47), channel_id=1, source_target_pairs={{0,4},{4,0},{8,12},{12,8},{16,20},{20,16},{24,28},{28,24},{1,5},{5... | collective-permute-start | bytes 1572872 | tf_op jit(solution)/shard_map/ppermute | solution.py:18
  58.8 9.3 %collective-permute-start.19 = (bf16[32,2048]{1,0:T(8,128)(2,1)S(1)}, bf16[32,2048]{1,0:T(8,128)(2,1)S(1)}, u32[]{:S(2)}, u32[]{:S(2)}) collective-permute-start(bf16[32,2048]{1,0:T(8,128)(2,1)S(1)} %slice_add_fusion.2), channel_id=1, source_target_pairs={{0,8},{4,12},{8,0},{12,4},{16,24},{20,28},{24,16},{28,20},{1,9},{5... | collective-permute-start | bytes 393224 | tf_op jit(solution)/shard_map/ppermute | solution.py:18
  59.6 7.3 %collective-permute-start.22 = (bf16[32,2048]{1,0:T(8,128)(2,1)S(1)}, bf16[32,2048]{1,0:T(8,128)(2,1)S(1)}, u32[]{:S(2)}, u32[]{:S(2)}) collective-permute-start(bf16[32,2048]{1,0:T(8,128)(2,1)S(1)} %get-tuple-element.57), channel_id=1, source_target_pairs={{0,16},{4,20},{8,24},{12,28},{16,0},{20,4},{24,8},{28,12},{1,17},{... | collective-permute-start | bytes 393224 | tf_op jit(solution)/shard_map/ppermute | solution.py:18
  61.1 7.0 %collective-permute-start.21 = (bf16[32,2048]{1,0:T(8,128)(2,1)S(1)}, bf16[32,2048]{1,0:T(8,128)(2,1)S(1)}, u32[]{:S(2)}, u32[]{:S(2)}) collective-permute-start(bf16[32,2048]{1,0:T(8,128)(2,1)S(1)} %get-tuple-element.56), channel_id=1, source_target_pairs={{0,24},{4,28},{8,16},{12,20},{16,8},{20,12},{24,0},{28,4},{1,25},{... | collective-permute-start | bytes 393224 | tf_op jit(solution)/shard_map/ppermute | solution.py:18

commit v22 on v20

--- a/solution.py
+++ b/solution.py
@@ -10,6 +10,7 @@
 F32, BF16 = jnp.float32, jnp.bfloat16
 VMEM_LIMIT = 28 * 2**20
 STEP = 512
+WIDE = 1024
 CHUNKS = 2
 
 
@@ -104,8 +105,8 @@
         column = row ^ offset
         start = (lax.div(column, ratio) ^ col) * share + lax.rem(column, ratio) * own
         probes[pl.ds(pl.multiple_of(start, own), own), :] = ref[at : at + own, :]
-    for step in range(ends.shape[1] // STEP):
-        rows, at = slice(base + step * STEP, base + (step + 1) * STEP), slice(step * STEP, (step + 1) * STEP)
+    for step in range(ends.shape[1] // WIDE):
+        rows, at = slice(base + step * WIDE, base + (step + 1) * WIDE), slice(step * WIDE, (step + 1) * WIDE)
         term = lax.dot_general(probes[...], tiles[rows, :], (((1,), (1,)), ((), ())), preferred_element_type=F32)
         for k, out in enumerate(outs):
             out[:, at] = term[k * share : (k + 1) * share].astype(out.dtype)
@@ -145,8 +146,8 @@
             apart = row ^ ((col ^ offset) * ratio + n)
             start = ((apart >> 1) + (apart & 1) * (devices // 2)) * own
             lowered[pl.ds(pl.multiple_of(start, own), own), :] = ref[n * own : (n + 1) * own, :]
-    for step in range(tiles.shape[1] // STEP):
-        at = slice(step * STEP, (step + 1) * STEP)
+    for step in range(tiles.shape[1] // WIDE):
+        at = slice(step * WIDE, (step + 1) * WIDE)
         term = jnp.dot(lowered[span, :], tiles[base : base + rows, at], preferred_element_type=F32)
         if earlier:
             term += earlier[0][span, at]
@@ -180,7 +181,7 @@
 def local(green, mask, probes):
     n_row, n_col = lax.axis_size("row"), lax.axis_size("col")
     own_width = probes.shape[1]
-    chunks = CHUNKS if green.shape[0] % (CHUNKS * STEP) == 0 else 1
+    chunks = CHUNKS if green.shape[0] % (CHUNKS * WIDE) == 0 else 1
     offsets_col = list(range(n_col))
     offsets_core = list(range(0, n_row, 2))
     gather_core = offsets_core

time: 67.5 us -> 67.5 us (level)
  no operation moved by 1% of the time
where the time goes in v22:
time: 67.5 us; the launch traced here: 67.3 us
  starting transfers between devices  33.9 us (50%)
  waiting for transfers between devices  21.6 us (32%)
  Pallas kernels  8.95 us (13%)
  other arithmetic  2.11 us (3%)
  between operations  0.77 us (1%)
    ppermute x19, starting transfers between devices, exchange(): return lax.ppermute(value, axis, [(i, i ^ offset) for i in range(size)])  21.9 us
    ppermute x19, waiting for transfers between devices, exchange(): return lax.ppermute(value, axis, [(i, i ^ offset) for i in range(size)])  18.4 us
    ppermute x2, starting transfers between devices, window_spread(): lax.ppermute(onward, 'col', [(0, 2), (3, 1), (1, 0), (2, 3)])  7.68 us
    ppermute x2, starting transfers between devices, window_sums(): came = lax.ppermute(terms[2], 'col', [(0, 1), (3, 2), (2, 0), (1, 3)])  4.26 us
    pallas_call x1, Pallas kernels, masked(): pl.pallas_call(functools.partial(mask_kernel, block=rows // mask.shape[0]...  3.56 us
    pallas_call x3, Pallas kernels, partial_adjoint(): pl.pallas_call(functools.partial(adjoint_kernel, base=base, span=span, pa...  2.75 us
    pallas_call x2, Pallas kernels, partial_sketch(): pl.pallas_call(functools.partial(sketch_kernel, base=chunk * rows, offset...  2.64 us
    ppermute x2, waiting for transfers between devices, window_spread(): lax.ppermute(onward, 'col', [(0, 2), (3, 1), (1, 0), (2, 3)])  2.24 us
  transfers between devices with their start and end apart: 23, of which 14 were waited for; matrix products, arithmetic and copies ran while one was open for 2% of the time, Pallas kernels for 10%

profile of v22, /device:TPU:0, one launch (start us, length us, event | category | flops | bytes accessed | tf_op | source)
XLA Modules:
  0.0 67.3 jit_solution(12192005280877999950)
XLA Ops:
  0.6 3.0 %collective-permute-start = (bf16[32,2048]{1,0:T(8,128)(2,1)}, bf16[32,2048]{1,0:T(8,128)(2,1)S(1)}, u32[]{:S(2)}, u32[]{:S(2)}) collective-permute-start(bf16[32,2048]{1,0:T(8,128)(2,1)} %bitcast.5), channel_id=1, source_target_pairs={{0,8},{4,12},{8,0},{12,4},{16,24},{20,28},{24,16},{28,20},{1,9},{5... | collective-permute-start | bytes 393224 | tf_op jit(solution)/shard_map/ppermute | solution.py:19
  3.6 1.5 %collective-permute-start.1 = (bf16[32,2048]{1,0:T(8,128)(2,1)}, bf16[32,2048]{1,0:T(8,128)(2,1)S(1)}, u32[]{:S(2)}, u32[]{:S(2)}) collective-permute-start(bf16[32,2048]{1,0:T(8,128)(2,1)} %bitcast.6), channel_id=1, source_target_pairs={{0,16},{4,20},{8,24},{12,28},{16,0},{20,4},{24,8},{28,12},{1,17},{... | collective-permute-start | bytes 393224 | tf_op jit(solution)/shard_map/ppermute | solution.py:19
  5.2 3.6 %masked_tiles.1 = (bf16[2048,2048]{1,0:T(8,128)(2,1)S(1)}, f32[8,128]{1,0:T(8,128)S(1)}) custom-call(s32[8,8]{1,0:T(8,128)} %mask_hbm.1, bf16[2048,2048]{1,0:T(8,128)(2,1)} %green_ref.1), custom_call_target="tpu_custom_call" | custom-call | bytes 8388608 | tf_op jit(solution)/shard_map/masked_tiles/pallas_call | solution.py:79
  8.8 2.0 %collective-permute-done.1.refs_2_ = bf16[32,2048]{1,0:T(8,128)(2,1)S(1)} collective-permute-done((bf16[32,2048]{1,0:T(8,128)(2,1)}, bf16[32,2048]{1,0:T(8,128)(2,1)S(1)}, u32[]{:S(2)}, u32[]{:S(2)}) %collective-permute-start.1) | collective-permute-done | bytes 131104 | tf_op jit(solution)/shard_map/ppermute | solution.py:19
  10.9 1.3 %collective-permute-done.3.refs_3_ = bf16[32,2048]{1,0:T(8,128)(2,1)S(1)} collective-permute-done((bf16[32,2048]{1,0:T(8,128)(2,1)}, bf16[32,2048]{1,0:T(8,128)(2,1)S(1)}, u32[]{:S(2)}, u32[]{:S(2)}) %collective-permute-start.3) | collective-permute-done | bytes 131104 | tf_op jit(solution)/shard_map/ppermute | solution.py:19
  12.2 1.3 %collective-permute-done.5.refs_6_ = bf16[32,2048]{1,0:T(8,128)(2,1)S(1)} collective-permute-done((bf16[32,2048]{1,0:T(8,128)(2,1)S(1)}, bf16[32,2048]{1,0:T(8,128)(2,1)S(1)}, u32[]{:S(2)}, u32[]{:S(2)}) %collective-permute-start.5) | collective-permute-done | bytes 131104 | tf_op jit(solution)/shard_map/ppermute | solution.py:19
  13.5 1.3 %partial_sketch.2 = (f32[64,1024]{1,0:T(8,128)S(1)}, bf16[64,1024]{1,0:T(8,128)(2,1)S(1)}, bf16[64,1024]{1,0:T(8,128)(2,1)S(1)}, f32[64,1024]{1,0:T(8,128)S(1)}, f32[64,1024]{1,0:T(8,128)S(1)}) custom-call(bf16[2048,2048]{1,0:T(8,128)(2,1)S(1)} %get-tuple-element.25.tiles, f32[8,128]{1,0:T(8,128)S(1)} %get-tuple-element.27.token, ...), custom_call_target="tpu_custom_call" | custom-call | flops 1073741824 | bytes 4194304 | tf_op jit(solution)/shard_map/partial_sketch/pallas_call | solution.py:124
  14.9 1.6 %collective-permute-start.6 = (bf16[64,1024]{1,0:T(8,128)(2,1)S(1)}, bf16[64,1024]{1,0:T(8,128)(2,1)S(1)}, u32[]{:S(2)}, u32[]{:S(2)}) collective-permute-start(bf16[64,1024]{1,0:T(8,128)(2,1)S(1)} %get-tuple-element.35), channel_id=1, source_target_pairs={{0,1},{3,2},{2,0},{1,3},{4,5},{7,6},{6,4},{5,7},{8,9},{11,10},{10,... | collective-permute-start | bytes 393224 | tf_op jit(solution)/shard_map/ppermute | solution.py:34
  16.5 1.3 %partial_sketch.3 = (f32[64,1024]{1,0:T(8,128)S(1)}, bf16[64,1024]{1,0:T(8,128)(2,1)S(1)}, bf16[64,1024]{1,0:T(8,128)(2,1)S(1)}, f32[64,1024]{1,0:T(8,128)S(1)}, f32[64,1024]{1,0:T(8,128)S(1)}) custom-call(bf16[2048,2048]{1,0:T(8,128)(2,1)S(1)} %get-tuple-element.25.tiles, f32[8,128]{1,0:T(8,128)S(1)} %get-tuple-element.27.token, ...), custom_call_target="tpu_custom_call" | custom-call | flops 1073741824 | bytes 4194304 | tf_op jit(solution)/shard_map/partial_sketch/pallas_call | solution.py:124
  17.8 2.6 %collective-permute-start.9 = (bf16[64,1024]{1,0:T(8,128)(2,1)S(1)}, bf16[64,1024]{1,0:T(8,128)(2,1)S(1)}, u32[]{:S(2)}, u32[]{:S(2)}) collective-permute-start(bf16[64,1024]{1,0:T(8,128)(2,1)S(1)} %get-tuple-element.41), channel_id=1, source_target_pairs={{0,1},{3,2},{2,0},{1,3},{4,5},{7,6},{6,4},{5,7},{8,9},{11,10},{10,... | collective-permute-start | bytes 393224 | tf_op jit(solution)/shard_map/ppermute | solution.py:34
  20.5 1.0 %collective-permute-done.6 = bf16[64,1024]{1,0:T(8,128)(2,1)S(1)} collective-permute-done((bf16[64,1024]{1,0:T(8,128)(2,1)S(1)}, bf16[64,1024]{1,0:T(8,128)(2,1)S(1)}, u32[]{:S(2)}, u32[]{:S(2)}) %collective-permute-start.6) | collective-permute-done | bytes 131104 | tf_op jit(solution)/shard_map/ppermute | solution.py:34
  21.5 4.4 %collective-permute-start.8 = (bf16[64,1024]{1,0:T(8,128)(2,1)S(1)}, bf16[64,1024]{1,0:T(8,128)(2,1)S(1)}, u32[]{:S(2)}, u32[]{:S(2)}) collective-permute-start(bf16[64,1024]{1,0:T(8,128)(2,1)S(1)} %get-tuple-element.52), channel_id=1, source_target_pairs={{0,3},{1,2},{2,1},{3,0},{4,7},{5,6},{6,5},{7,4},{8,11},{9,10},{10,... | collective-permute-start | bytes 393224 | tf_op jit(solution)/shard_map/ppermute | solution.py:19
  26.0 2.7 %collective-permute-start.11 = (bf16[64,1024]{1,0:T(8,128)(2,1)S(1)}, bf16[64,1024]{1,0:T(8,128)(2,1)S(1)}, u32[]{:S(2)}, u32[]{:S(2)}) collective-permute-start(bf16[64,1024]{1,0:T(8,128)(2,1)S(1)} %get-tuple-element.54), channel_id=1, source_target_pairs={{0,3},{1,2},{2,1},{3,0},{4,7},{5,6},{6,5},{7,4},{8,11},{9,10},{10,... | collective-permute-start | bytes 393224 | tf_op jit(solution)/shard_map/ppermute | solution.py:19
  28.7 1.8 %collective-permute-done.8 = bf16[64,1024]{1,0:T(8,128)(2,1)S(1)} collective-permute-done((bf16[64,1024]{1,0:T(8,128)(2,1)S(1)}, bf16[64,1024]{1,0:T(8,128)(2,1)S(1)}, u32[]{:S(2)}, u32[]{:S(2)}) %collective-permute-start.8) | collective-permute-done | bytes 131104 | tf_op jit(solution)/shard_map/ppermute | solution.py:19
  30.5 4.1 %collective-permute-done.7 = bf16[64,1024]{1,0:T(8,128)(2,1)S(1)} collective-permute-done((bf16[64,1024]{1,0:T(8,128)(2,1)S(1)}, bf16[64,1024]{1,0:T(8,128)(2,1)S(1)}, u32[]{:S(2)}, u32[]{:S(2)}) %collective-permute-start.7) | collective-permute-done | bytes 131104 | tf_op jit(solution)/shard_map/ppermute | solution.py:19
  34.6 1.6 %collective-permute-start.16 = (bf16[64,1024]{1,0:T(8,128)(2,1)S(1)}, bf16[64,1024]{1,0:T(8,128)(2,1)S(1)}, u32[]{:S(2)}, u32[]{:S(2)}) collective-permute-start(bf16[64,1024]{1,0:T(8,128)(2,1)S(1)} %get-tuple-element.48.refs_0_), channel_id=1, source_target_pairs={{0,3},{1,2},{2,1},{3,0},{4,7},{5,6},{6,5},{7,4},{8,11},{9,10},{10,... | collective-permute-start | bytes 393224 | tf_op jit(solution)/shard_map/ppermute | solution.py:19
  36.2 1.9 %collective-permute-done.10 = bf16[64,1024]{1,0:T(8,128)(2,1)S(1)} collective-permute-done((bf16[64,1024]{1,0:T(8,128)(2,1)S(1)}, bf16[64,1024]{1,0:T(8,128)(2,1)S(1)}, u32[]{:S(2)}, u32[]{:S(2)}) %collective-permute-start.10) | collective-permute-done | bytes 131104 | tf_op jit(solution)/shard_map/ppermute | solution.py:19
  38.2 2.4 %collective-permute-start.13 = (bf16[64,1024]{1,0:T(8,128)(2,1)S(1)}, bf16[64,1024]{1,0:T(8,128)(2,1)S(1)}, u32[]{:S(2)}, u32[]{:S(2)}) collective-permute-start(bf16[64,1024]{1,0:T(8,128)(2,1)S(1)} %get-tuple-element.50.refs_0_), channel_id=1, source_target_pairs={{0,3},{1,2},{2,1},{3,0},{4,7},{5,6},{6,5},{7,4},{8,11},{9,10},{10,... | collective-permute-start | bytes 393224 | tf_op jit(solution)/shard_map/ppermute | solution.py:19
  41.0 1.6 %collective-permute-start.15 = (bf16[64,1024]{1,0:T(8,128)(2,1)S(1)}, bf16[64,1024]{1,0:T(8,128)(2,1)S(1)}, u32[]{:S(2)}, u32[]{:S(2)}) collective-permute-start(bf16[64,1024]{1,0:T(8,128)(2,1)S(1)} %get-tuple-element.48.refs_0_), channel_id=1, source_target_pairs={{0,1},{1,0},{2,3},{3,2},{4,5},{5,4},{6,7},{7,6},{8,9},{9,8},{10,11... | collective-permute-start | bytes 393224 | tf_op jit(solution)/shard_map/ppermute | solution.py:19
  42.9 3.9 %collective-permute-start.17 = (bf16[64,1024]{1,0:T(8,128)(2,1)S(1)}, bf16[64,1024]{1,0:T(8,128)(2,1)S(1)}, u32[]{:S(2)}, u32[]{:S(2)}) collective-permute-start(bf16[64,1024]{1,0:T(8,128)(2,1)S(1)} %select_n.26), channel_id=1, source_target_pairs={{0,2},{3,1},{1,0},{2,3},{4,6},{7,5},{5,4},{6,7},{8,10},{11,9},{9,8... | collective-permute-start | bytes 393224 | tf_op jit(solution)/shard_map/ppermute | solution.py:52
  46.9 3.8 %collective-permute-start.14 = (bf16[64,1024]{1,0:T(8,128)(2,1)S(1)}, bf16[64,1024]{1,0:T(8,128)(2,1)S(1)}, u32[]{:S(2)}, u32[]{:S(2)}) collective-permute-start(bf16[64,1024]{1,0:T(8,128)(2,1)S(1)} %select_n.25), channel_id=1, source_target_pairs={{0,2},{3,1},{1,0},{2,3},{4,6},{7,5},{5,4},{6,7},{8,10},{11,9},{9,8... | collective-permute-start | bytes 393224 | tf_op jit(solution)/shard_map/ppermute | solution.py:52
  51.0 2.1 %collective-permute-done.17.refs_2_ = bf16[64,1024]{1,0:T(8,128)(2,1)S(1)} collective-permute-done((bf16[64,1024]{1,0:T(8,128)(2,1)S(1)}, bf16[64,1024]{1,0:T(8,128)(2,1)S(1)}, u32[]{:S(2)}, u32[]{:S(2)}) %collective-permute-start.17) | collective-permute-done | bytes 131104 | tf_op jit(solution)/shard_map/ppermute | solution.py:52
  53.1 1.3 %partial_adjoint.3.refs_4_ = f32[256,2048]{1,0:T(8,128)S(1)} custom-call(bf16[2048,2048]{1,0:T(8,128)(2,1)S(1)} %get-tuple-element.25.tiles, bf16[64,1024]{1,0:T(8,128)(2,1)S(1)} %get-tuple-element.48.refs_0_, bf16[64,1024]{1,0:T(8,128)(2,1)S(1)} %collective-permute-done.15.refs_1_, bf16[64,1024]{1,0:T(8,128)(2,1)S(1)} %collective-permute-done.17.refs_2_, ...), custom_call_target="tpu_custom_call" | custom-call | tf_op jit(solution)/shard_map/partial_adjoint/pallas_call | solution.py:165
  54.5 0.7 %partial_adjoint.5 = (f32[64,2048]{1,0:T(8,128)S(1)}, f32[64,2048]{1,0:T(8,128)S(1)}) custom-call(bf16[2048,2048]{1,0:T(8,128)(2,1)S(1)} %get-tuple-element.25.tiles, bf16[64,1024]{1,0:T(8,128)(2,1)S(1)} %get-tuple-element.50.refs_0_, bf16[64,1024]{1,0:T(8,128)(2,1)S(1)} %collective-permute-done.12.refs_1_, ...), custom_call_target="tpu_custom_call" | custom-call | tf_op jit(solution)/shard_map/partial_adjoint/pallas_call | solution.py:165
  55.8 0.8 %partial_adjoint.4 = (f32[64,2048]{1,0:T(8,128)S(1)}, f32[64,2048]{1,0:T(8,128)S(1)}) custom-call(bf16[2048,2048]{1,0:T(8,128)(2,1)S(1)} %get-tuple-element.25.tiles, bf16[64,1024]{1,0:T(8,128)(2,1)S(1)} %get-tuple-element.50.refs_0_, bf16[64,1024]{1,0:T(8,128)(2,1)S(1)} %collective-permute-done.12.refs_1_, ...), custom_call_target="tpu_custom_call" | custom-call | tf_op jit(solution)/shard_map/partial_adjoint/pallas_call | solution.py:165
  57.3 0.7 %collective-permute-start.19 = (bf16[32,2048]{1,0:T(8,128)(2,1)S(1)}, bf16[32,2048]{1,0:T(8,128)(2,1)S(1)}, u32[]{:S(2)}, u32[]{:S(2)}) collective-permute-start(bf16[32,2048]{1,0:T(8,128)(2,1)S(1)} %slice_add_fusion.2), channel_id=1, source_target_pairs={{0,8},{4,12},{8,0},{12,4},{16,24},{20,28},{24,16},{28,20},{1,9},{5... | collective-permute-start | bytes 393224 | tf_op jit(solution)/shard_map/ppermute | solution.py:19
  58.1 1.5 %collective-permute-start.22 = (bf16[32,2048]{1,0:T(8,128)(2,1)S(1)}, bf16[32,2048]{1,0:T(8,128)(2,1)S(1)}, u32[]{:S(2)}, u32[]{:S(2)}) collective-permute-start(bf16[32,2048]{1,0:T(8,128)(2,1)S(1)} %get-tuple-element.57), channel_id=1, source_target_pairs={{0,16},{4,20},{8,24},{12,28},{16,0},{20,4},{24,8},{28,12},{1,17},{... | collective-permute-start | bytes 393224 | tf_op jit(solution)/shard_map/ppermute | solution.py:19
  59.5 1.4 %collective-permute-start.21 = (bf16[32,2048]{1,0:T(8,128)(2,1)S(1)}, bf16[32,2048]{1,0:T(8,128)(2,1)S(1)}, u32[]{:S(2)}, u32[]{:S(2)}) collective-permute-start(bf16[32,2048]{1,0:T(8,128)(2,1)S(1)} %get-tuple-element.56), channel_id=1, source_target_pairs={{0,24},{4,28},{8,16},{12,20},{16,8},{20,12},{24,0},{28,4},{1,25},{... | collective-permute-start | bytes 393224 | tf_op jit(solution)/shard_map/ppermute | solution.py:19
  60.9 0.8 %maximum_bitcast_fusion = f32[2048,64]{0,1:T(8,128)} fusion(f32[64,1024]{1,0:T(8,128)S(1)} %get-tuple-element.51, f32[64,1024]{1,0:T(8,128)S(1)} %get-tuple-element.49), kind=kLoop, calls=%fused_computation | loop fusion | flops 131072 | bytes 1048576 | tf_op jit(solution)/shard_map/transpose | solution.py:225
  61.8 3.6 %collective-permute-done.22 = bf16[32,2048]{1,0:T(8,128)(2,1)S(1)} collective-permute-done((bf16[32,2048]{1,0:T(8,128)(2,1)S(1)}, bf16[32,2048]{1,0:T(8,128)(2,1)S(1)}, u32[]{:S(2)}, u32[]{:S(2)}) %collective-permute-start.22) | collective-permute-done | bytes 131104 | tf_op jit(solution)/shard_map/ppermute | solution.py:19
  65.4 1.1 %collective-permute-done.21 = bf16[32,2048]{1,0:T(8,128)(2,1)S(1)} collective-permute-done((bf16[32,2048]{1,0:T(8,128)(2,1)S(1)}, bf16[32,2048]{1,0:T(8,128)(2,1)S(1)}, u32[]{:S(2)}, u32[]{:S(2)}) %collective-permute-start.21) | collective-permute-done | bytes 131104 | tf_op jit(solution)/shard_map/ppermute | solution.py:19
  66.5 0.8 %fusion.11 = f32[2048,32]{0,1:T(8,128)} fusion(f32[64,2048]{1,0:T(8,128)S(1)} %collective-permute-done.18, bf16[32,2048]{1,0:T(8,128)(2,1)S(1)} %collective-permute-done.22, bf16[32,2048]{1,0:T(8,128)(2,1)S(1)} %collective-permute-done.21, bf16[32,2048]{1,0:T(8,128)(2,1)S(1)} %collective-permute-done.19, f32[64,2048]{1,0:T(8,128)S(1)} %get-tuple-element.43), kind=kLoop, calls=%fused_computation.20 | loop fusion | flops 458752 | bytes 1179648 | tf_op jit(solution)/shard_map/transpose | solution.py:225
  (33 shorter events, 3.1 us)
Async XLA Ops:
  0.6 12.9 %copy-start = (bf16[2048,32]{0,1:T(8,128)(2,1)S(1)}, bf16[2048,32]{0,1:T(8,128)(2,1)}, u32[]{:S(2)}) copy-start(bf16[2048,32]{0,1:T(8,128)(2,1)} %param.5) | copy-start | bytes 393220
  0.6 8.1 %collective-permute-start = (bf16[32,2048]{1,0:T(8,128)(2,1)}, bf16[32,2048]{1,0:T(8,128)(2,1)S(1)}, u32[]{:S(2)}, u32[]{:S(2)}) collective-permute-start(bf16[32,2048]{1,0:T(8,128)(2,1)} %bitcast.5), channel_id=1, source_target_pairs={{0,8},{4,12},{8,0},{12,4},{16,24},{20,28},{24,16},{28,20},{1,9},{5... | collective-permute-start | bytes 393224 | tf_op jit(solution)/shard_map/ppermute | solution.py:19
  3.6 7.2 %collective-permute-start.1 = (bf16[32,2048]{1,0:T(8,128)(2,1)}, bf16[32,2048]{1,0:T(8,128)(2,1)S(1)}, u32[]{:S(2)}, u32[]{:S(2)}) collective-permute-start(bf16[32,2048]{1,0:T(8,128)(2,1)} %bitcast.6), channel_id=1, source_target_pairs={{0,16},{4,20},{8,24},{12,28},{16,0},{20,4},{24,8},{28,12},{1,17},{... | collective-permute-start | bytes 393224 | tf_op jit(solution)/shard_map/ppermute | solution.py:19
  5.2 5.6 %collective-permute-start.2 = (bf16[32,2048]{1,0:T(8,128)(2,1)}, bf16[32,2048]{1,0:T(8,128)(2,1)S(1)}, u32[]{:S(2)}, u32[]{:S(2)}) collective-permute-start(bf16[32,2048]{1,0:T(8,128)(2,1)} %bitcast.7), channel_id=1, source_target_pairs={{0,4},{4,0},{8,12},{12,8},{16,20},{20,16},{24,28},{28,24},{1,5},{5... | collective-permute-start | bytes 393224 | tf_op jit(solution)/shard_map/ppermute | solution.py:19
  5.2 7.0 %collective-permute-start.3 = (bf16[32,2048]{1,0:T(8,128)(2,1)}, bf16[32,2048]{1,0:T(8,128)(2,1)S(1)}, u32[]{:S(2)}, u32[]{:S(2)}) collective-permute-start(bf16[32,2048]{1,0:T(8,128)(2,1)} %bitcast.8), channel_id=1, source_target_pairs={{0,24},{4,28},{8,16},{12,20},{16,8},{20,12},{24,0},{28,4},{1,25},{... | collective-permute-start | bytes 393224 | tf_op jit(solution)/shard_map/ppermute | solution.py:19
  10.8 2.7 %collective-permute-start.4 = (bf16[64,2048]{1,0:T(8,128)(2,1)S(1)}, bf16[64,2048]{1,0:T(8,128)(2,1)S(1)}, u32[]{:S(2)}, u32[]{:S(2)}) collective-permute-start(bf16[64,2048]{1,0:T(8,128)(2,1)S(1)} %pad_maximum_fusion), channel_id=1, source_target_pairs={{0,4},{4,0},{8,12},{12,8},{16,20},{20,16},{24,28},{28,24},{1,5},{5... | collective-permute-start | bytes 786440 | tf_op jit(solution)/shard_map/ppermute | solution.py:19
  12.2 1.3 %collective-permute-start.5 = (bf16[32,2048]{1,0:T(8,128)(2,1)S(1)}, bf16[32,2048]{1,0:T(8,128)(2,1)S(1)}, u32[]{:S(2)}, u32[]{:S(2)}) collective-permute-start(bf16[32,2048]{1,0:T(8,128)(2,1)S(1)} %collective-permute-done.3.refs_3_), channel_id=1, source_target_pairs={{0,4},{4,0},{8,12},{12,8},{16,20},{20,16},{24,28},{28,24},{1,5},{5... | collective-permute-start | bytes 393224 | tf_op jit(solution)/shard_map/ppermute | solution.py:19
  14.9 6.6 %collective-permute-start.6 = (bf16[64,1024]{1,0:T(8,128)(2,1)S(1)}, bf16[64,1024]{1,0:T(8,128)(2,1)S(1)}, u32[]{:S(2)}, u32[]{:S(2)}) collective-permute-start(bf16[64,1024]{1,0:T(8,128)(2,1)S(1)} %get-tuple-element.35), channel_id=1, source_target_pairs={{0,1},{3,2},{2,0},{1,3},{4,5},{7,6},{6,4},{5,7},{8,9},{11,10},{10,... | collective-permute-start | bytes 393224 | tf_op jit(solution)/shard_map/ppermute | solution.py:34
  17.8 8.1 %collective-permute-start.9 = (bf16[64,1024]{1,0:T(8,128)(2,1)S(1)}, bf16[64,1024]{1,0:T(8,128)(2,1)S(1)}, u32[]{:S(2)}, u32[]{:S(2)}) collective-permute-start(bf16[64,1024]{1,0:T(8,128)(2,1)S(1)} %get-tuple-element.41), channel_id=1, source_target_pairs={{0,1},{3,2},{2,0},{1,3},{4,5},{7,6},{6,4},{5,7},{8,9},{11,10},{10,... | collective-permute-start | bytes 393224 | tf_op jit(solution)/shard_map/ppermute | solution.py:34
  21.5 9.0 %collective-permute-start.8 = (bf16[64,1024]{1,0:T(8,128)(2,1)S(1)}, bf16[64,1024]{1,0:T(8,128)(2,1)S(1)}, u32[]{:S(2)}, u32[]{:S(2)}) collective-permute-start(bf16[64,1024]{1,0:T(8,128)(2,1)S(1)} %get-tuple-element.52), channel_id=1, source_target_pairs={{0,3},{1,2},{2,1},{3,0},{4,7},{5,6},{6,5},{7,4},{8,11},{9,10},{10,... | collective-permute-start | bytes 393224 | tf_op jit(solution)/shard_map/ppermute | solution.py:19
  25.9 8.6 %collective-permute-start.7 = (bf16[64,1024]{1,0:T(8,128)(2,1)S(1)}, bf16[64,1024]{1,0:T(8,128)(2,1)S(1)}, u32[]{:S(2)}, u32[]{:S(2)}) collective-permute-start(bf16[64,1024]{1,0:T(8,128)(2,1)S(1)} %get-tuple-element.36), channel_id=1, source_target_pairs={{0,1},{1,0},{2,3},{3,2},{4,5},{5,4},{6,7},{7,6},{8,9},{9,8},{10,11... | collective-permute-start | bytes 393224 | tf_op jit(solution)/shard_map/ppermute | solution.py:19
  26.0 10.2 %collective-permute-start.11 = (bf16[64,1024]{1,0:T(8,128)(2,1)S(1)}, bf16[64,1024]{1,0:T(8,128)(2,1)S(1)}, u32[]{:S(2)}, u32[]{:S(2)}) collective-permute-start(bf16[64,1024]{1,0:T(8,128)(2,1)S(1)} %get-tuple-element.54), channel_id=1, source_target_pairs={{0,3},{1,2},{2,1},{3,0},{4,7},{5,6},{6,5},{7,4},{8,11},{9,10},{10,... | collective-permute-start | bytes 393224 | tf_op jit(solution)/shard_map/ppermute | solution.py:19
  28.7 9.4 %collective-permute-start.10 = (bf16[64,1024]{1,0:T(8,128)(2,1)S(1)}, bf16[64,1024]{1,0:T(8,128)(2,1)S(1)}, u32[]{:S(2)}, u32[]{:S(2)}) collective-permute-start(bf16[64,1024]{1,0:T(8,128)(2,1)S(1)} %get-tuple-element.42), channel_id=1, source_target_pairs={{0,1},{1,0},{2,3},{3,2},{4,5},{5,4},{6,7},{7,6},{8,9},{9,8},{10,11... | collective-permute-start | bytes 393224 | tf_op jit(solution)/shard_map/ppermute | solution.py:19
  34.6 8.3 %collective-permute-start.16 = (bf16[64,1024]{1,0:T(8,128)(2,1)S(1)}, bf16[64,1024]{1,0:T(8,128)(2,1)S(1)}, u32[]{:S(2)}, u32[]{:S(2)}) collective-permute-start(bf16[64,1024]{1,0:T(8,128)(2,1)S(1)} %get-tuple-element.48.refs_0_), channel_id=1, source_target_pairs={{0,3},{1,2},{2,1},{3,0},{4,7},{5,6},{6,5},{7,4},{8,11},{9,10},{10,... | collective-permute-start | bytes 393224 | tf_op jit(solution)/shard_map/ppermute | solution.py:19
  38.2 8.7 %collective-permute-start.13 = (bf16[64,1024]{1,0:T(8,128)(2,1)S(1)}, bf16[64,1024]{1,0:T(8,128)(2,1)S(1)}, u32[]{:S(2)}, u32[]{:S(2)}) collective-permute-start(bf16[64,1024]{1,0:T(8,128)(2,1)S(1)} %get-tuple-element.50.refs_0_), channel_id=1, source_target_pairs={{0,3},{1,2},{2,1},{3,0},{4,7},{5,6},{6,5},{7,4},{8,11},{9,10},{10,... | collective-permute-start | bytes 393224 | tf_op jit(solution)/shard_map/ppermute | solution.py:19
  40.6 13.8 %collective-permute-start.12 = (bf16[64,1024]{1,0:T(8,128)(2,1)S(1)}, bf16[64,1024]{1,0:T(8,128)(2,1)S(1)}, u32[]{:S(2)}, u32[]{:S(2)}) collective-permute-start(bf16[64,1024]{1,0:T(8,128)(2,1)S(1)} %get-tuple-element.50.refs_0_), channel_id=1, source_target_pairs={{0,1},{1,0},{2,3},{3,2},{4,5},{5,4},{6,7},{7,6},{8,9},{9,8},{10,11... | collective-permute-start | bytes 393224 | tf_op jit(solution)/shard_map/ppermute | solution.py:19
  41.0 9.9 %collective-permute-start.15 = (bf16[64,1024]{1,0:T(8,128)(2,1)S(1)}, bf16[64,1024]{1,0:T(8,128)(2,1)S(1)}, u32[]{:S(2)}, u32[]{:S(2)}) collective-permute-start(bf16[64,1024]{1,0:T(8,128)(2,1)S(1)} %get-tuple-element.48.refs_0_), channel_id=1, source_target_pairs={{0,1},{1,0},{2,3},{3,2},{4,5},{5,4},{6,7},{7,6},{8,9},{9,8},{10,11... | collective-permute-start | bytes 393224 | tf_op jit(solution)/shard_map/ppermute | solution.py:19
  42.9 10.2 %collective-permute-start.17 = (bf16[64,1024]{1,0:T(8,128)(2,1)S(1)}, bf16[64,1024]{1,0:T(8,128)(2,1)S(1)}, u32[]{:S(2)}, u32[]{:S(2)}) collective-permute-start(bf16[64,1024]{1,0:T(8,128)(2,1)S(1)} %select_n.26), channel_id=1, source_target_pairs={{0,2},{3,1},{1,0},{2,3},{4,6},{7,5},{5,4},{6,7},{8,10},{11,9},{9,8... | collective-permute-start | bytes 393224 | tf_op jit(solution)/shard_map/ppermute | solution.py:52
  46.9 7.6 %collective-permute-start.14 = (bf16[64,1024]{1,0:T(8,128)(2,1)S(1)}, bf16[64,1024]{1,0:T(8,128)(2,1)S(1)}, u32[]{:S(2)}, u32[]{:S(2)}) collective-permute-start(bf16[64,1024]{1,0:T(8,128)(2,1)S(1)} %select_n.25), channel_id=1, source_target_pairs={{0,2},{3,1},{1,0},{2,3},{4,6},{7,5},{5,4},{6,7},{8,10},{11,9},{9,8... | collective-permute-start | bytes 393224 | tf_op jit(solution)/shard_map/ppermute | solution.py:52
  55.2 2.0 %collective-permute-start.18 = (f32[64,2048]{1,0:T(8,128)S(1)}, f32[64,2048]{1,0:T(8,128)S(1)}, u32[]{:S(2)}, u32[]{:S(2)}) collective-permute-start(f32[64,2048]{1,0:T(8,128)S(1)} %get-tuple-element.44), channel_id=1, source_target_pairs={{0,4},{4,0},{8,12},{12,8},{16,20},{20,16},{24,28},{28,24},{1,5},{5... | collective-permute-start | bytes 1572872 | tf_op jit(solution)/shard_map/ppermute | solution.py:19
  55.3 2.7 %collective-permute-start.20 = (f32[64,2048]{1,0:T(8,128)S(1)}, f32[64,2048]{1,0:T(8,128)S(1)}, u32[]{:S(2)}, u32[]{:S(2)}) collective-permute-start(f32[64,2048]{1,0:T(8,128)S(1)} %get-tuple-element.47), channel_id=1, source_target_pairs={{0,4},{4,0},{8,12},{12,8},{16,20},{20,16},{24,28},{28,24},{1,5},{5... | collective-permute-start | bytes 1572872 | tf_op jit(solution)/shard_map/ppermute | solution.py:19
  57.3 9.3 %collective-permute-start.19 = (bf16[32,2048]{1,0:T(8,128)(2,1)S(1)}, bf16[32,2048]{1,0:T(8,128)(2,1)S(1)}, u32[]{:S(2)}, u32[]{:S(2)}) collective-permute-start(bf16[32,2048]{1,0:T(8,128)(2,1)S(1)} %slice_add_fusion.2), channel_id=1, source_target_pairs={{0,8},{4,12},{8,0},{12,4},{16,24},{20,28},{24,16},{28,20},{1,9},{5... | collective-permute-start | bytes 393224 | tf_op jit(solution)/shard_map/ppermute | solution.py:19
  58.1 7.3 %collective-permute-start.22 = (bf16[32,2048]{1,0:T(8,128)(2,1)S(1)}, bf16[32,2048]{1,0:T(8,128)(2,1)S(1)}, u32[]{:S(2)}, u32[]{:S(2)}) collective-permute-start(bf16[32,2048]{1,0:T(8,128)(2,1)S(1)} %get-tuple-element.57), channel_id=1, source_target_pairs={{0,16},{4,20},{8,24},{12,28},{16,0},{20,4},{24,8},{28,12},{1,17},{... | collective-permute-start | bytes 393224 | tf_op jit(solution)/shard_map/ppermute | solution.py:19
  59.5 7.0 %collective-permute-start.21 = (bf16[32,2048]{1,0:T(8,128)(2,1)S(1)}, bf16[32,2048]{1,0:T(8,128)(2,1)S(1)}, u32[]{:S(2)}, u32[]{:S(2)}) collective-permute-start(bf16[32,2048]{1,0:T(8,128)(2,1)S(1)} %get-tuple-element.56), channel_id=1, source_target_pairs={{0,24},{4,28},{8,16},{12,20},{16,8},{20,12},{24,0},{28,4},{1,25},{... | collective-permute-start | bytes 393224 | tf_op jit(solution)/shard_map/ppermute | solution.py:19

commit v23 on v20

--- a/solution.py
+++ b/solution.py
@@ -183,7 +183,7 @@
     chunks = CHUNKS if green.shape[0] % (CHUNKS * STEP) == 0 else 1
     offsets_col = list(range(n_col))
     offsets_core = list(range(0, n_row, 2))
-    gather_core = offsets_core
+    gather_core = [0, offsets_core[-1], *offsets_core[1:-1]]
     offsets_row = gather_core + [offset ^ 1 for offset in gather_core]
     tiles, token = masked(green, mask)
 

time: 67.5 us -> 67.6 us (level)
  no operation moved by 1% of the time
where the time goes in v23:
time: 67.6 us; the launch traced here: 67.5 us
  starting transfers between devices  34.5 us (51%)
  waiting for transfers between devices  21 us (31%)
  Pallas kernels  9.02 us (13%)
  other arithmetic  2.11 us (3%)
  between operations  0.76 us (1%)
    ppermute x19, starting transfers between devices, exchange(): return lax.ppermute(value, axis, [(i, i ^ offset) for i in range(size)])  22.5 us
    ppermute x19, waiting for transfers between devices, exchange(): return lax.ppermute(value, axis, [(i, i ^ offset) for i in range(size)])  17.9 us
    ppermute x2, starting transfers between devices, window_spread(): lax.ppermute(onward, 'col', [(0, 2), (3, 1), (1, 0), (2, 3)])  7.69 us
    ppermute x2, starting transfers between devices, window_sums(): came = lax.ppermute(terms[2], 'col', [(0, 1), (3, 2), (2, 0), (1, 3)])  4.3 us
    pallas_call x1, Pallas kernels, masked(): pl.pallas_call(functools.partial(mask_kernel, block=rows // mask.shape[0]...  3.64 us
    pallas_call x3, Pallas kernels, partial_adjoint(): pl.pallas_call(functools.partial(adjoint_kernel, base=base, span=span, pa...  2.75 us
    pallas_call x2, Pallas kernels, partial_sketch(): pl.pallas_call(functools.partial(sketch_kernel, base=chunk * rows, offset...  2.63 us
    ppermute x2, waiting for transfers between devices, window_spread(): lax.ppermute(onward, 'col', [(0, 2), (3, 1), (1, 0), (2, 3)])  2.24 us
  transfers between devices with their start and end apart: 23, of which 14 were waited for; matrix products, arithmetic and copies ran while one was open for 2% of the time, Pallas kernels for 10%

profile of v23, /device:TPU:0, one launch (start us, length us, event | category | flops | bytes accessed | tf_op | source)
XLA Modules:
  0.0 67.5 jit_solution(9432072844476597738)
XLA Ops:
  0.6 4.0 %collective-permute-start = (bf16[32,2048]{1,0:T(8,128)(2,1)}, bf16[32,2048]{1,0:T(8,128)(2,1)S(1)}, u32[]{:S(2)}, u32[]{:S(2)}) collective-permute-start(bf16[32,2048]{1,0:T(8,128)(2,1)} %bitcast.5), channel_id=1, source_target_pairs={{0,24},{4,28},{8,16},{12,20},{16,8},{20,12},{24,0},{28,4},{1,25},{... | collective-permute-start | bytes 393224 | tf_op jit(solution)/shard_map/ppermute | solution.py:18
  4.6 0.5 collective-permute-start.1
  5.2 3.6 %masked_tiles.1 = (bf16[2048,2048]{1,0:T(8,128)(2,1)S(1)}, f32[8,128]{1,0:T(8,128)S(1)}) custom-call(s32[8,8]{1,0:T(8,128)} %mask_hbm.1, bf16[2048,2048]{1,0:T(8,128)(2,1)} %green_ref.1), custom_call_target="tpu_custom_call" | custom-call | bytes 8388608 | tf_op jit(solution)/shard_map/masked_tiles/pallas_call | solution.py:78
  9.1 2.2 %collective-permute-done.1.refs_2_ = bf16[32,2048]{1,0:T(8,128)(2,1)S(1)} collective-permute-done((bf16[32,2048]{1,0:T(8,128)(2,1)}, bf16[32,2048]{1,0:T(8,128)(2,1)S(1)}, u32[]{:S(2)}, u32[]{:S(2)}) %collective-permute-start.1) | collective-permute-done | bytes 131104 | tf_op jit(solution)/shard_map/ppermute | solution.py:18
  12.0 1.2 %collective-permute-done.5.refs_6_ = bf16[32,2048]{1,0:T(8,128)(2,1)S(1)} collective-permute-done((bf16[32,2048]{1,0:T(8,128)(2,1)S(1)}, bf16[32,2048]{1,0:T(8,128)(2,1)S(1)}, u32[]{:S(2)}, u32[]{:S(2)}) %collective-permute-start.5) | collective-permute-done | bytes 131104 | tf_op jit(solution)/shard_map/ppermute | solution.py:18
  13.2 1.3 %partial_sketch.2 = (f32[64,1024]{1,0:T(8,128)S(1)}, bf16[64,1024]{1,0:T(8,128)(2,1)S(1)}, bf16[64,1024]{1,0:T(8,128)(2,1)S(1)}, f32[64,1024]{1,0:T(8,128)S(1)}, f32[64,1024]{1,0:T(8,128)S(1)}) custom-call(bf16[2048,2048]{1,0:T(8,128)(2,1)S(1)} %get-tuple-element.25.tiles, f32[8,128]{1,0:T(8,128)S(1)} %get-tuple-element.27.token, ...), custom_call_target="tpu_custom_call" | custom-call | flops 1073741824 | bytes 4194304 | tf_op jit(solution)/shard_map/partial_sketch/pallas_call | solution.py:123
  14.5 1.7 %collective-permute-start.6 = (bf16[64,1024]{1,0:T(8,128)(2,1)S(1)}, bf16[64,1024]{1,0:T(8,128)(2,1)S(1)}, u32[]{:S(2)}, u32[]{:S(2)}) collective-permute-start(bf16[64,1024]{1,0:T(8,128)(2,1)S(1)} %get-tuple-element.35), channel_id=1, source_target_pairs={{0,1},{3,2},{2,0},{1,3},{4,5},{7,6},{6,4},{5,7},{8,9},{11,10},{10,... | collective-permute-start | bytes 393224 | tf_op jit(solution)/shard_map/ppermute | solution.py:33
  16.2 1.3 %partial_sketch.3 = (f32[64,1024]{1,0:T(8,128)S(1)}, bf16[64,1024]{1,0:T(8,128)(2,1)S(1)}, bf16[64,1024]{1,0:T(8,128)(2,1)S(1)}, f32[64,1024]{1,0:T(8,128)S(1)}, f32[64,1024]{1,0:T(8,128)S(1)}) custom-call(bf16[2048,2048]{1,0:T(8,128)(2,1)S(1)} %get-tuple-element.25.tiles, f32[8,128]{1,0:T(8,128)S(1)} %get-tuple-element.27.token, ...), custom_call_target="tpu_custom_call" | custom-call | flops 1073741824 | bytes 4194304 | tf_op jit(solution)/shard_map/partial_sketch/pallas_call | solution.py:123
  17.5 2.6 %collective-permute-start.9 = (bf16[64,1024]{1,0:T(8,128)(2,1)S(1)}, bf16[64,1024]{1,0:T(8,128)(2,1)S(1)}, u32[]{:S(2)}, u32[]{:S(2)}) collective-permute-start(bf16[64,1024]{1,0:T(8,128)(2,1)S(1)} %get-tuple-element.41), channel_id=1, source_target_pairs={{0,1},{3,2},{2,0},{1,3},{4,5},{7,6},{6,4},{5,7},{8,9},{11,10},{10,... | collective-permute-start | bytes 393224 | tf_op jit(solution)/shard_map/ppermute | solution.py:33
  20.1 0.9 %collective-permute-done.6 = bf16[64,1024]{1,0:T(8,128)(2,1)S(1)} collective-permute-done((bf16[64,1024]{1,0:T(8,128)(2,1)S(1)}, bf16[64,1024]{1,0:T(8,128)(2,1)S(1)}, u32[]{:S(2)}, u32[]{:S(2)}) %collective-permute-start.6) | collective-permute-done | bytes 131104 | tf_op jit(solution)/shard_map/ppermute | solution.py:33
  21.1 4.5 %collective-permute-start.8 = (bf16[64,1024]{1,0:T(8,128)(2,1)S(1)}, bf16[64,1024]{1,0:T(8,128)(2,1)S(1)}, u32[]{:S(2)}, u32[]{:S(2)}) collective-permute-start(bf16[64,1024]{1,0:T(8,128)(2,1)S(1)} %get-tuple-element.52), channel_id=1, source_target_pairs={{0,3},{1,2},{2,1},{3,0},{4,7},{5,6},{6,5},{7,4},{8,11},{9,10},{10,... | collective-permute-start | bytes 393224 | tf_op jit(solution)/shard_map/ppermute | solution.py:18
  25.6 2.7 %collective-permute-start.11 = (bf16[64,1024]{1,0:T(8,128)(2,1)S(1)}, bf16[64,1024]{1,0:T(8,128)(2,1)S(1)}, u32[]{:S(2)}, u32[]{:S(2)}) collective-permute-start(bf16[64,1024]{1,0:T(8,128)(2,1)S(1)} %get-tuple-element.54), channel_id=1, source_target_pairs={{0,3},{1,2},{2,1},{3,0},{4,7},{5,6},{6,5},{7,4},{8,11},{9,10},{10,... | collective-permute-start | bytes 393224 | tf_op jit(solution)/shard_map/ppermute | solution.py:18
  28.4 1.8 %collective-permute-done.8 = bf16[64,1024]{1,0:T(8,128)(2,1)S(1)} collective-permute-done((bf16[64,1024]{1,0:T(8,128)(2,1)S(1)}, bf16[64,1024]{1,0:T(8,128)(2,1)S(1)}, u32[]{:S(2)}, u32[]{:S(2)}) %collective-permute-start.8) | collective-permute-done | bytes 131104 | tf_op jit(solution)/shard_map/ppermute | solution.py:18
  30.1 4.1 %collective-permute-done.7 = bf16[64,1024]{1,0:T(8,128)(2,1)S(1)} collective-permute-done((bf16[64,1024]{1,0:T(8,128)(2,1)S(1)}, bf16[64,1024]{1,0:T(8,128)(2,1)S(1)}, u32[]{:S(2)}, u32[]{:S(2)}) %collective-permute-start.7) | collective-permute-done | bytes 131104 | tf_op jit(solution)/shard_map/ppermute | solution.py:18
  34.3 1.6 %collective-permute-start.16 = (bf16[64,1024]{1,0:T(8,128)(2,1)S(1)}, bf16[64,1024]{1,0:T(8,128)(2,1)S(1)}, u32[]{:S(2)}, u32[]{:S(2)}) collective-permute-start(bf16[64,1024]{1,0:T(8,128)(2,1)S(1)} %get-tuple-element.48.refs_0_), channel_id=1, source_target_pairs={{0,3},{1,2},{2,1},{3,0},{4,7},{5,6},{6,5},{7,4},{8,11},{9,10},{10,... | collective-permute-start | bytes 393224 | tf_op jit(solution)/shard_map/ppermute | solution.py:18
  35.9 1.9 %collective-permute-done.10 = bf16[64,1024]{1,0:T(8,128)(2,1)S(1)} collective-permute-done((bf16[64,1024]{1,0:T(8,128)(2,1)S(1)}, bf16[64,1024]{1,0:T(8,128)(2,1)S(1)}, u32[]{:S(2)}, u32[]{:S(2)}) %collective-permute-start.10) | collective-permute-done | bytes 131104 | tf_op jit(solution)/shard_map/ppermute | solution.py:18
  37.9 2.4 %collective-permute-start.13 = (bf16[64,1024]{1,0:T(8,128)(2,1)S(1)}, bf16[64,1024]{1,0:T(8,128)(2,1)S(1)}, u32[]{:S(2)}, u32[]{:S(2)}) collective-permute-start(bf16[64,1024]{1,0:T(8,128)(2,1)S(1)} %get-tuple-element.50.refs_0_), channel_id=1, source_target_pairs={{0,3},{1,2},{2,1},{3,0},{4,7},{5,6},{6,5},{7,4},{8,11},{9,10},{10,... | collective-permute-start | bytes 393224 | tf_op jit(solution)/shard_map/ppermute | solution.py:18
  40.7 1.6 %collective-permute-start.15 = (bf16[64,1024]{1,0:T(8,128)(2,1)S(1)}, bf16[64,1024]{1,0:T(8,128)(2,1)S(1)}, u32[]{:S(2)}, u32[]{:S(2)}) collective-permute-start(bf16[64,1024]{1,0:T(8,128)(2,1)S(1)} %get-tuple-element.48.refs_0_), channel_id=1, source_target_pairs={{0,1},{1,0},{2,3},{3,2},{4,5},{5,4},{6,7},{7,6},{8,9},{9,8},{10,11... | collective-permute-start | bytes 393224 | tf_op jit(solution)/shard_map/ppermute | solution.py:18
  42.6 3.9 %collective-permute-start.17 = (bf16[64,1024]{1,0:T(8,128)(2,1)S(1)}, bf16[64,1024]{1,0:T(8,128)(2,1)S(1)}, u32[]{:S(2)}, u32[]{:S(2)}) collective-permute-start(bf16[64,1024]{1,0:T(8,128)(2,1)S(1)} %select_n.26), channel_id=1, source_target_pairs={{0,2},{3,1},{1,0},{2,3},{4,6},{7,5},{5,4},{6,7},{8,10},{11,9},{9,8... | collective-permute-start | bytes 393224 | tf_op jit(solution)/shard_map/ppermute | solution.py:51
  46.6 3.8 %collective-permute-start.14 = (bf16[64,1024]{1,0:T(8,128)(2,1)S(1)}, bf16[64,1024]{1,0:T(8,128)(2,1)S(1)}, u32[]{:S(2)}, u32[]{:S(2)}) collective-permute-start(bf16[64,1024]{1,0:T(8,128)(2,1)S(1)} %select_n.25), channel_id=1, source_target_pairs={{0,2},{3,1},{1,0},{2,3},{4,6},{7,5},{5,4},{6,7},{8,10},{11,9},{9,8... | collective-permute-start | bytes 393224 | tf_op jit(solution)/shard_map/ppermute | solution.py:51
  50.7 2.1 %collective-permute-done.17.refs_2_ = bf16[64,1024]{1,0:T(8,128)(2,1)S(1)} collective-permute-done((bf16[64,1024]{1,0:T(8,128)(2,1)S(1)}, bf16[64,1024]{1,0:T(8,128)(2,1)S(1)}, u32[]{:S(2)}, u32[]{:S(2)}) %collective-permute-start.17) | collective-permute-done | bytes 131104 | tf_op jit(solution)/shard_map/ppermute | solution.py:51
  52.8 1.3 %partial_adjoint.3.refs_4_ = f32[256,2048]{1,0:T(8,128)S(1)} custom-call(bf16[2048,2048]{1,0:T(8,128)(2,1)S(1)} %get-tuple-element.25.tiles, bf16[64,1024]{1,0:T(8,128)(2,1)S(1)} %get-tuple-element.48.refs_0_, bf16[64,1024]{1,0:T(8,128)(2,1)S(1)} %collective-permute-done.15.refs_1_, bf16[64,1024]{1,0:T(8,128)(2,1)S(1)} %collective-permute-done.17.refs_2_, ...), custom_call_target="tpu_custom_call" | custom-call | tf_op jit(solution)/shard_map/partial_adjoint/pallas_call | solution.py:164
  54.2 0.7 %partial_adjoint.5 = (f32[64,2048]{1,0:T(8,128)S(1)}, f32[64,2048]{1,0:T(8,128)S(1)}) custom-call(bf16[2048,2048]{1,0:T(8,128)(2,1)S(1)} %get-tuple-element.25.tiles, bf16[64,1024]{1,0:T(8,128)(2,1)S(1)} %get-tuple-element.50.refs_0_, bf16[64,1024]{1,0:T(8,128)(2,1)S(1)} %collective-permute-done.12.refs_1_, ...), custom_call_target="tpu_custom_call" | custom-call | tf_op jit(solution)/shard_map/partial_adjoint/pallas_call | solution.py:164
  55.0 0.5 collective-permute-start.20
  55.5 0.7 %partial_adjoint.4 = (f32[64,2048]{1,0:T(8,128)S(1)}, f32[64,2048]{1,0:T(8,128)S(1)}) custom-call(bf16[2048,2048]{1,0:T(8,128)(2,1)S(1)} %get-tuple-element.25.tiles, bf16[64,1024]{1,0:T(8,128)(2,1)S(1)} %get-tuple-element.50.refs_0_, bf16[64,1024]{1,0:T(8,128)(2,1)S(1)} %collective-permute-done.12.refs_1_, ...), custom_call_target="tpu_custom_call" | custom-call | tf_op jit(solution)/shard_map/partial_adjoint/pallas_call | solution.py:164
  56.3 0.6 collective-permute-done.18
  56.9 1.5 %collective-permute-start.19 = (bf16[32,2048]{1,0:T(8,128)(2,1)S(1)}, bf16[32,2048]{1,0:T(8,128)(2,1)S(1)}, u32[]{:S(2)}, u32[]{:S(2)}) collective-permute-start(bf16[32,2048]{1,0:T(8,128)(2,1)S(1)} %slice_add_fusion.2), channel_id=1, source_target_pairs={{0,8},{4,12},{8,0},{12,4},{16,24},{20,28},{24,16},{28,20},{1,9},{5... | collective-permute-start | bytes 393224 | tf_op jit(solution)/shard_map/ppermute | solution.py:18
  58.5 1.1 %collective-permute-start.22 = (bf16[32,2048]{1,0:T(8,128)(2,1)S(1)}, bf16[32,2048]{1,0:T(8,128)(2,1)S(1)}, u32[]{:S(2)}, u32[]{:S(2)}) collective-permute-start(bf16[32,2048]{1,0:T(8,128)(2,1)S(1)} %get-tuple-element.57), channel_id=1, source_target_pairs={{0,16},{4,20},{8,24},{12,28},{16,0},{20,4},{24,8},{28,12},{1,17},{... | collective-permute-start | bytes 393224 | tf_op jit(solution)/shard_map/ppermute | solution.py:18
  59.6 1.1 %collective-permute-start.21 = (bf16[32,2048]{1,0:T(8,128)(2,1)S(1)}, bf16[32,2048]{1,0:T(8,128)(2,1)S(1)}, u32[]{:S(2)}, u32[]{:S(2)}) collective-permute-start(bf16[32,2048]{1,0:T(8,128)(2,1)S(1)} %get-tuple-element.56), channel_id=1, source_target_pairs={{0,24},{4,28},{8,16},{12,20},{16,8},{20,12},{24,0},{28,4},{1,25},{... | collective-permute-start | bytes 393224 | tf_op jit(solution)/shard_map/ppermute | solution.py:18
  60.7 0.8 %maximum_bitcast_fusion = f32[2048,64]{0,1:T(8,128)} fusion(f32[64,1024]{1,0:T(8,128)S(1)} %get-tuple-element.51, f32[64,1024]{1,0:T(8,128)S(1)} %get-tuple-element.49), kind=kLoop, calls=%fused_computation | loop fusion | flops 131072 | bytes 1048576 | tf_op jit(solution)/shard_map/transpose | solution.py:224
  61.5 5.1 %collective-permute-done.22 = bf16[32,2048]{1,0:T(8,128)(2,1)S(1)} collective-permute-done((bf16[32,2048]{1,0:T(8,128)(2,1)S(1)}, bf16[32,2048]{1,0:T(8,128)(2,1)S(1)}, u32[]{:S(2)}, u32[]{:S(2)}) %collective-permute-start.22) | collective-permute-done | bytes 131104 | tf_op jit(solution)/shard_map/ppermute | solution.py:18
  66.7 0.8 %fusion.11 = f32[2048,32]{0,1:T(8,128)} fusion(f32[64,2048]{1,0:T(8,128)S(1)} %collective-permute-done.18, bf16[32,2048]{1,0:T(8,128)(2,1)S(1)} %collective-permute-done.22, bf16[32,2048]{1,0:T(8,128)(2,1)S(1)} %collective-permute-done.21, bf16[32,2048]{1,0:T(8,128)(2,1)S(1)} %collective-permute-done.19, f32[64,2048]{1,0:T(8,128)S(1)} %get-tuple-element.43), kind=kLoop, calls=%fused_computation.20 | loop fusion | flops 458752 | bytes 1179648 | tf_op jit(solution)/shard_map/transpose | solution.py:224
  (33 shorter events, 2.7 us)
Async XLA Ops:
  0.6 12.6 %copy-start = (bf16[2048,32]{0,1:T(8,128)(2,1)S(1)}, bf16[2048,32]{0,1:T(8,128)(2,1)}, u32[]{:S(2)}) copy-start(bf16[2048,32]{0,1:T(8,128)(2,1)} %param.5) | copy-start | bytes 393220
  0.6 8.5 %collective-permute-start = (bf16[32,2048]{1,0:T(8,128)(2,1)}, bf16[32,2048]{1,0:T(8,128)(2,1)S(1)}, u32[]{:S(2)}, u32[]{:S(2)}) collective-permute-start(bf16[32,2048]{1,0:T(8,128)(2,1)} %bitcast.5), channel_id=1, source_target_pairs={{0,24},{4,28},{8,16},{12,20},{16,8},{20,12},{24,0},{28,4},{1,25},{... | collective-permute-start | bytes 393224 | tf_op jit(solution)/shard_map/ppermute | solution.py:18
  4.6 6.8 %collective-permute-start.1 = (bf16[32,2048]{1,0:T(8,128)(2,1)}, bf16[32,2048]{1,0:T(8,128)(2,1)S(1)}, u32[]{:S(2)}, u32[]{:S(2)}) collective-permute-start(bf16[32,2048]{1,0:T(8,128)(2,1)} %bitcast.6), channel_id=1, source_target_pairs={{0,8},{4,12},{8,0},{12,4},{16,24},{20,28},{24,16},{28,20},{1,9},{5... | collective-permute-start | bytes 393224 | tf_op jit(solution)/shard_map/ppermute | solution.py:18
  5.1 6.2 %collective-permute-start.2 = (bf16[32,2048]{1,0:T(8,128)(2,1)}, bf16[32,2048]{1,0:T(8,128)(2,1)S(1)}, u32[]{:S(2)}, u32[]{:S(2)}) collective-permute-start(bf16[32,2048]{1,0:T(8,128)(2,1)} %bitcast.7), channel_id=1, source_target_pairs={{0,4},{4,0},{8,12},{12,8},{16,20},{20,16},{24,28},{28,24},{1,5},{5... | collective-permute-start | bytes 393224 | tf_op jit(solution)/shard_map/ppermute | solution.py:18
  5.1 6.5 %collective-permute-start.3 = (bf16[32,2048]{1,0:T(8,128)(2,1)}, bf16[32,2048]{1,0:T(8,128)(2,1)S(1)}, u32[]{:S(2)}, u32[]{:S(2)}) collective-permute-start(bf16[32,2048]{1,0:T(8,128)(2,1)} %bitcast.8), channel_id=1, source_target_pairs={{0,16},{4,20},{8,24},{12,28},{16,0},{20,4},{24,8},{28,12},{1,17},{... | collective-permute-start | bytes 393224 | tf_op jit(solution)/shard_map/ppermute | solution.py:18
  11.4 1.8 %collective-permute-start.4 = (bf16[64,2048]{1,0:T(8,128)(2,1)S(1)}, bf16[64,2048]{1,0:T(8,128)(2,1)S(1)}, u32[]{:S(2)}, u32[]{:S(2)}) collective-permute-start(bf16[64,2048]{1,0:T(8,128)(2,1)S(1)} %pad_maximum_fusion), channel_id=1, source_target_pairs={{0,4},{4,0},{8,12},{12,8},{16,20},{20,16},{24,28},{28,24},{1,5},{5... | collective-permute-start | bytes 786440 | tf_op jit(solution)/shard_map/ppermute | solution.py:18
  11.6 1.6 %collective-permute-start.5 = (bf16[32,2048]{1,0:T(8,128)(2,1)S(1)}, bf16[32,2048]{1,0:T(8,128)(2,1)S(1)}, u32[]{:S(2)}, u32[]{:S(2)}) collective-permute-start(bf16[32,2048]{1,0:T(8,128)(2,1)S(1)} %collective-permute-done.3.refs_3_), channel_id=1, source_target_pairs={{0,4},{4,0},{8,12},{12,8},{16,20},{20,16},{24,28},{28,24},{1,5},{5... | collective-permute-start | bytes 393224 | tf_op jit(solution)/shard_map/ppermute | solution.py:18
  14.5 6.5 %collective-permute-start.6 = (bf16[64,1024]{1,0:T(8,128)(2,1)S(1)}, bf16[64,1024]{1,0:T(8,128)(2,1)S(1)}, u32[]{:S(2)}, u32[]{:S(2)}) collective-permute-start(bf16[64,1024]{1,0:T(8,128)(2,1)S(1)} %get-tuple-element.35), channel_id=1, source_target_pairs={{0,1},{3,2},{2,0},{1,3},{4,5},{7,6},{6,4},{5,7},{8,9},{11,10},{10,... | collective-permute-start | bytes 393224 | tf_op jit(solution)/shard_map/ppermute | solution.py:33
  17.5 8.1 %collective-permute-start.9 = (bf16[64,1024]{1,0:T(8,128)(2,1)S(1)}, bf16[64,1024]{1,0:T(8,128)(2,1)S(1)}, u32[]{:S(2)}, u32[]{:S(2)}) collective-permute-start(bf16[64,1024]{1,0:T(8,128)(2,1)S(1)} %get-tuple-element.41), channel_id=1, source_target_pairs={{0,1},{3,2},{2,0},{1,3},{4,5},{7,6},{6,4},{5,7},{8,9},{11,10},{10,... | collective-permute-start | bytes 393224 | tf_op jit(solution)/shard_map/ppermute | solution.py:33
  21.1 9.0 %collective-permute-start.8 = (bf16[64,1024]{1,0:T(8,128)(2,1)S(1)}, bf16[64,1024]{1,0:T(8,128)(2,1)S(1)}, u32[]{:S(2)}, u32[]{:S(2)}) collective-permute-start(bf16[64,1024]{1,0:T(8,128)(2,1)S(1)} %get-tuple-element.52), channel_id=1, source_target_pairs={{0,3},{1,2},{2,1},{3,0},{4,7},{5,6},{6,5},{7,4},{8,11},{9,10},{10,... | collective-permute-start | bytes 393224 | tf_op jit(solution)/shard_map/ppermute | solution.py:18
  25.6 8.6 %collective-permute-start.7 = (bf16[64,1024]{1,0:T(8,128)(2,1)S(1)}, bf16[64,1024]{1,0:T(8,128)(2,1)S(1)}, u32[]{:S(2)}, u32[]{:S(2)}) collective-permute-start(bf16[64,1024]{1,0:T(8,128)(2,1)S(1)} %get-tuple-element.36), channel_id=1, source_target_pairs={{0,1},{1,0},{2,3},{3,2},{4,5},{5,4},{6,7},{7,6},{8,9},{9,8},{10,11... | collective-permute-start | bytes 393224 | tf_op jit(solution)/shard_map/ppermute | solution.py:18
  25.6 10.2 %collective-permute-start.11 = (bf16[64,1024]{1,0:T(8,128)(2,1)S(1)}, bf16[64,1024]{1,0:T(8,128)(2,1)S(1)}, u32[]{:S(2)}, u32[]{:S(2)}) collective-permute-start(bf16[64,1024]{1,0:T(8,128)(2,1)S(1)} %get-tuple-element.54), channel_id=1, source_target_pairs={{0,3},{1,2},{2,1},{3,0},{4,7},{5,6},{6,5},{7,4},{8,11},{9,10},{10,... | collective-permute-start | bytes 393224 | tf_op jit(solution)/shard_map/ppermute | solution.py:18
  28.4 9.4 %collective-permute-start.10 = (bf16[64,1024]{1,0:T(8,128)(2,1)S(1)}, bf16[64,1024]{1,0:T(8,128)(2,1)S(1)}, u32[]{:S(2)}, u32[]{:S(2)}) collective-permute-start(bf16[64,1024]{1,0:T(8,128)(2,1)S(1)} %get-tuple-element.42), channel_id=1, source_target_pairs={{0,1},{1,0},{2,3},{3,2},{4,5},{5,4},{6,7},{7,6},{8,9},{9,8},{10,11... | collective-permute-start | bytes 393224 | tf_op jit(solution)/shard_map/ppermute | solution.py:18
  34.3 8.3 %collective-permute-start.16 = (bf16[64,1024]{1,0:T(8,128)(2,1)S(1)}, bf16[64,1024]{1,0:T(8,128)(2,1)S(1)}, u32[]{:S(2)}, u32[]{:S(2)}) collective-permute-start(bf16[64,1024]{1,0:T(8,128)(2,1)S(1)} %get-tuple-element.48.refs_0_), channel_id=1, source_target_pairs={{0,3},{1,2},{2,1},{3,0},{4,7},{5,6},{6,5},{7,4},{8,11},{9,10},{10,... | collective-permute-start | bytes 393224 | tf_op jit(solution)/shard_map/ppermute | solution.py:18
  37.9 8.7 %collective-permute-start.13 = (bf16[64,1024]{1,0:T(8,128)(2,1)S(1)}, bf16[64,1024]{1,0:T(8,128)(2,1)S(1)}, u32[]{:S(2)}, u32[]{:S(2)}) collective-permute-start(bf16[64,1024]{1,0:T(8,128)(2,1)S(1)} %get-tuple-element.50.refs_0_), channel_id=1, source_target_pairs={{0,3},{1,2},{2,1},{3,0},{4,7},{5,6},{6,5},{7,4},{8,11},{9,10},{10,... | collective-permute-start | bytes 393224 | tf_op jit(solution)/shard_map/ppermute | solution.py:18
  40.2 13.8 %collective-permute-start.12 = (bf16[64,1024]{1,0:T(8,128)(2,1)S(1)}, bf16[64,1024]{1,0:T(8,128)(2,1)S(1)}, u32[]{:S(2)}, u32[]{:S(2)}) collective-permute-start(bf16[64,1024]{1,0:T(8,128)(2,1)S(1)} %get-tuple-element.50.refs_0_), channel_id=1, source_target_pairs={{0,1},{1,0},{2,3},{3,2},{4,5},{5,4},{6,7},{7,6},{8,9},{9,8},{10,11... | collective-permute-start | bytes 393224 | tf_op jit(solution)/shard_map/ppermute | solution.py:18
  40.7 9.9 %collective-permute-start.15 = (bf16[64,1024]{1,0:T(8,128)(2,1)S(1)}, bf16[64,1024]{1,0:T(8,128)(2,1)S(1)}, u32[]{:S(2)}, u32[]{:S(2)}) collective-permute-start(bf16[64,1024]{1,0:T(8,128)(2,1)S(1)} %get-tuple-element.48.refs_0_), channel_id=1, source_target_pairs={{0,1},{1,0},{2,3},{3,2},{4,5},{5,4},{6,7},{7,6},{8,9},{9,8},{10,11... | collective-permute-start | bytes 393224 | tf_op jit(solution)/shard_map/ppermute | solution.py:18
  42.6 10.2 %collective-permute-start.17 = (bf16[64,1024]{1,0:T(8,128)(2,1)S(1)}, bf16[64,1024]{1,0:T(8,128)(2,1)S(1)}, u32[]{:S(2)}, u32[]{:S(2)}) collective-permute-start(bf16[64,1024]{1,0:T(8,128)(2,1)S(1)} %select_n.26), channel_id=1, source_target_pairs={{0,2},{3,1},{1,0},{2,3},{4,6},{7,5},{5,4},{6,7},{8,10},{11,9},{9,8... | collective-permute-start | bytes 393224 | tf_op jit(solution)/shard_map/ppermute | solution.py:51
  46.6 7.6 %collective-permute-start.14 = (bf16[64,1024]{1,0:T(8,128)(2,1)S(1)}, bf16[64,1024]{1,0:T(8,128)(2,1)S(1)}, u32[]{:S(2)}, u32[]{:S(2)}) collective-permute-start(bf16[64,1024]{1,0:T(8,128)(2,1)S(1)} %select_n.25), channel_id=1, source_target_pairs={{0,2},{3,1},{1,0},{2,3},{4,6},{7,5},{5,4},{6,7},{8,10},{11,9},{9,8... | collective-permute-start | bytes 393224 | tf_op jit(solution)/shard_map/ppermute | solution.py:51
  54.9 2.0 %collective-permute-start.18 = (f32[64,2048]{1,0:T(8,128)S(1)}, f32[64,2048]{1,0:T(8,128)S(1)}, u32[]{:S(2)}, u32[]{:S(2)}) collective-permute-start(f32[64,2048]{1,0:T(8,128)S(1)} %get-tuple-element.44), channel_id=1, source_target_pairs={{0,4},{4,0},{8,12},{12,8},{16,20},{20,16},{24,28},{28,24},{1,5},{5... | collective-permute-start | bytes 1572872 | tf_op jit(solution)/shard_map/ppermute | solution.py:18
  55.0 3.5 %collective-permute-start.20 = (f32[64,2048]{1,0:T(8,128)S(1)}, f32[64,2048]{1,0:T(8,128)S(1)}, u32[]{:S(2)}, u32[]{:S(2)}) collective-permute-start(f32[64,2048]{1,0:T(8,128)S(1)} %get-tuple-element.47), channel_id=1, source_target_pairs={{0,4},{4,0},{8,12},{12,8},{16,20},{20,16},{24,28},{28,24},{1,5},{5... | collective-permute-start | bytes 1572872 | tf_op jit(solution)/shard_map/ppermute | solution.py:18
  56.9 9.7 %collective-permute-start.19 = (bf16[32,2048]{1,0:T(8,128)(2,1)S(1)}, bf16[32,2048]{1,0:T(8,128)(2,1)S(1)}, u32[]{:S(2)}, u32[]{:S(2)}) collective-permute-start(bf16[32,2048]{1,0:T(8,128)(2,1)S(1)} %slice_add_fusion.2), channel_id=1, source_target_pairs={{0,8},{4,12},{8,0},{12,4},{16,24},{20,28},{24,16},{28,20},{1,9},{5... | collective-permute-start | bytes 393224 | tf_op jit(solution)/shard_map/ppermute | solution.py:18
  58.5 8.1 %collective-permute-start.22 = (bf16[32,2048]{1,0:T(8,128)(2,1)S(1)}, bf16[32,2048]{1,0:T(8,128)(2,1)S(1)}, u32[]{:S(2)}, u32[]{:S(2)}) collective-permute-start(bf16[32,2048]{1,0:T(8,128)(2,1)S(1)} %get-tuple-element.57), channel_id=1, source_target_pairs={{0,16},{4,20},{8,24},{12,28},{16,0},{20,4},{24,8},{28,12},{1,17},{... | collective-permute-start | bytes 393224 | tf_op jit(solution)/shard_map/ppermute | solution.py:18
  59.6 7.0 %collective-permute-start.21 = (bf16[32,2048]{1,0:T(8,128)(2,1)S(1)}, bf16[32,2048]{1,0:T(8,128)(2,1)S(1)}, u32[]{:S(2)}, u32[]{:S(2)}) collective-permute-start(bf16[32,2048]{1,0:T(8,128)(2,1)S(1)} %get-tuple-element.56), channel_id=1, source_target_pairs={{0,24},{4,28},{8,16},{12,20},{16,8},{20,12},{24,0},{28,4},{1,25},{... | collective-permute-start | bytes 393224 | tf_op jit(solution)/shard_map/ppermute | solution.py:18

commit v24 on v20

--- a/solution.py
+++ b/solution.py
@@ -27,20 +27,20 @@
     return lax.optimization_barrier((value, earlier))[0]
 
 
-def window_sums(terms, ends):
+def window_sums(terms, ends, first):
     size = len(terms)
     if size == 4:
         came = lax.ppermute(terms[2], "col", [(0, 1), (3, 2), (2, 0), (1, 3)])
         came = came.astype(F32)
         onward = terms[3] + jnp.where(ends > 0, 0.0, came)
         onward = onward.astype(BF16)
-        far = exchange(onward, "col", 3).astype(F32)
-        near = exchange(after(terms[1], onward), "col", 1).astype(F32)
-        return terms[0] + near + far + jnp.where(ends > 0, came, 0.0)
+        far = exchange(onward, "col", 3)
+        near = exchange(after(terms[1], onward if first is None else first), "col", 1).astype(F32)
+        return terms[0] + near + far.astype(F32) + jnp.where(ends > 0, came, 0.0), far
     total = terms[0]
     for offset in range(1, size):
         total = total + exchange(terms[offset].astype(BF16), "col", offset).astype(F32)
-    return total
+    return total, None
 
 
 def window_spread(lowered, ends, size):
@@ -194,10 +194,11 @@
     early, twin, token = lax.optimization_barrier((early, twin, token))
     blocks = [own, *early, late, twin, exchange(jnp.concatenate(early), "row", 1), exchange(late, "row", 1)]
 
-    totals, shares = [], []
+    totals, shares, first = [], [], None
     for chunk in range(chunks):
         *parts, ends = partial_sketch(tiles, blocks, token, offsets_row, offsets_col, chunk, chunks)
-        totals.append(window_sums(parts, ends))
+        total, first = window_sums(parts, ends, first)
+        totals.append(total)
         shares.append(window_spread(totals[-1].astype(BF16), ends, n_col))
 
     earlier = []

time: 67.5 us -> 67.7 us (level)
  waiting for transfers between devices: 21.5 us -> 24.8 us
  starting transfers between devices: 33.9 us -> 30.8 us
    ppermute x2, starting transfers between devices: 7.68 us -> 0.12 us  [window_spread(): lax.ppermute(onward, 'col', [(0, 2), (3, 1), (1, 0), (2, 3)])]
    ppermute x19, starting transfers between devices: 21.9 us -> 26.5 us  [exchange(): return lax.ppermute(value, axis, [(i, i ^ offset) for i in range(size)])]
    ppermute x19, waiting for transfers between devices: 18.3 us -> 20.8 us  [exchange(): return lax.ppermute(value, axis, [(i, i ^ offset) for i in range(size)])]
    ppermute x2, waiting for transfers between devices: 2.24 us -> 2.93 us  [window_spread(): lax.ppermute(onward, 'col', [(0, 2), (3, 1), (1, 0), (2, 3)])]
where the time goes in v24:
time: 67.7 us; the launch traced here: 67.6 us
  starting transfers between devices  30.8 us (45%)
  waiting for transfers between devices  24.8 us (37%)
  Pallas kernels  9.04 us (13%)
  other arithmetic  2.11 us (3%)
  between operations  0.78 us (1%)
    ppermute x19, starting transfers between devices, exchange(): return lax.ppermute(value, axis, [(i, i ^ offset) for i in range(size)])  26.5 us
    ppermute x19, waiting for transfers between devices, exchange(): return lax.ppermute(value, axis, [(i, i ^ offset) for i in range(size)])  20.8 us
    ppermute x2, starting transfers between devices, window_sums(): came = lax.ppermute(terms[2], 'col', [(0, 1), (3, 2), (2, 0), (1, 3)])  4.27 us
    pallas_call x1, Pallas kernels, masked(): pl.pallas_call(functools.partial(mask_kernel, block=rows // mask.shape[0]...  3.65 us
    ppermute x2, waiting for transfers between devices, window_spread(): lax.ppermute(onward, 'col', [(0, 2), (3, 1), (1, 0), (2, 3)])  2.93 us
    pallas_call x3, Pallas kernels, partial_adjoint(): pl.pallas_call(functools.partial(adjoint_kernel, base=base, span=span, pa...  2.76 us
    pallas_call x2, Pallas kernels, partial_sketch(): pl.pallas_call(functools.partial(sketch_kernel, base=chunk * rows, offset...  2.64 us
    transpose x2, other arithmetic, local(): return (jnp.concatenate(totals, axis=1).T, adjoint.T)  1.6 us
  transfers between devices with their start and end apart: 23, of which 14 were waited for; matrix products, arithmetic and copies ran while one was open for 2% of the time, Pallas kernels for 10%

profile of v24, /device:TPU:0, one launch (start us, length us, event | category | flops | bytes accessed | tf_op | source)
XLA Modules:
  0.0 67.6 jit_solution(12433957740659610140)
XLA Ops:
  0.6 3.0 %collective-permute-start = (bf16[32,2048]{1,0:T(8,128)(2,1)}, bf16[32,2048]{1,0:T(8,128)(2,1)S(1)}, u32[]{:S(2)}, u32[]{:S(2)}) collective-permute-start(bf16[32,2048]{1,0:T(8,128)(2,1)} %bitcast.5), channel_id=1, source_target_pairs={{0,8},{4,12},{8,0},{12,4},{16,24},{20,28},{24,16},{28,20},{1,9},{5... | collective-permute-start | bytes 393224 | tf_op jit(solution)/shard_map/ppermute | solution.py:18
  3.6 1.5 %collective-permute-start.1 = (bf16[32,2048]{1,0:T(8,128)(2,1)}, bf16[32,2048]{1,0:T(8,128)(2,1)S(1)}, u32[]{:S(2)}, u32[]{:S(2)}) collective-permute-start(bf16[32,2048]{1,0:T(8,128)(2,1)} %bitcast.6), channel_id=1, source_target_pairs={{0,16},{4,20},{8,24},{12,28},{16,0},{20,4},{24,8},{28,12},{1,17},{... | collective-permute-start | bytes 393224 | tf_op jit(solution)/shard_map/ppermute | solution.py:18
  5.2 3.6 %masked_tiles.1 = (bf16[2048,2048]{1,0:T(8,128)(2,1)S(1)}, f32[8,128]{1,0:T(8,128)S(1)}) custom-call(s32[8,8]{1,0:T(8,128)} %mask_hbm.1, bf16[2048,2048]{1,0:T(8,128)(2,1)} %green_ref.1), custom_call_target="tpu_custom_call" | custom-call | bytes 8388608 | tf_op jit(solution)/shard_map/masked_tiles/pallas_call | solution.py:78
  8.9 2.0 %collective-permute-done.1.refs_2_ = bf16[32,2048]{1,0:T(8,128)(2,1)S(1)} collective-permute-done((bf16[32,2048]{1,0:T(8,128)(2,1)}, bf16[32,2048]{1,0:T(8,128)(2,1)S(1)}, u32[]{:S(2)}, u32[]{:S(2)}) %collective-permute-start.1) | collective-permute-done | bytes 131104 | tf_op jit(solution)/shard_map/ppermute | solution.py:18
  10.9 1.3 %collective-permute-done.3.refs_3_ = bf16[32,2048]{1,0:T(8,128)(2,1)S(1)} collective-permute-done((bf16[32,2048]{1,0:T(8,128)(2,1)}, bf16[32,2048]{1,0:T(8,128)(2,1)S(1)}, u32[]{:S(2)}, u32[]{:S(2)}) %collective-permute-start.3) | collective-permute-done | bytes 131104 | tf_op jit(solution)/shard_map/ppermute | solution.py:18
  12.2 1.3 %collective-permute-done.5.refs_6_ = bf16[32,2048]{1,0:T(8,128)(2,1)S(1)} collective-permute-done((bf16[32,2048]{1,0:T(8,128)(2,1)S(1)}, bf16[32,2048]{1,0:T(8,128)(2,1)S(1)}, u32[]{:S(2)}, u32[]{:S(2)}) %collective-permute-start.5) | collective-permute-done | bytes 131104 | tf_op jit(solution)/shard_map/ppermute | solution.py:18
  13.5 1.3 %partial_sketch.2 = (f32[64,1024]{1,0:T(8,128)S(1)}, bf16[64,1024]{1,0:T(8,128)(2,1)S(1)}, bf16[64,1024]{1,0:T(8,128)(2,1)S(1)}, f32[64,1024]{1,0:T(8,128)S(1)}, f32[64,1024]{1,0:T(8,128)S(1)}) custom-call(bf16[2048,2048]{1,0:T(8,128)(2,1)S(1)} %get-tuple-element.25.tiles, f32[8,128]{1,0:T(8,128)S(1)} %get-tuple-element.27.token, ...), custom_call_target="tpu_custom_call" | custom-call | flops 1073741824 | bytes 4194304 | tf_op jit(solution)/shard_map/partial_sketch/pallas_call | solution.py:123
  14.9 1.6 %collective-permute-start.6 = (bf16[64,1024]{1,0:T(8,128)(2,1)S(1)}, bf16[64,1024]{1,0:T(8,128)(2,1)S(1)}, u32[]{:S(2)}, u32[]{:S(2)}) collective-permute-start(bf16[64,1024]{1,0:T(8,128)(2,1)S(1)} %get-tuple-element.35), channel_id=1, source_target_pairs={{0,1},{3,2},{2,0},{1,3},{4,5},{7,6},{6,4},{5,7},{8,9},{11,10},{10,... | collective-permute-start | bytes 393224 | tf_op jit(solution)/shard_map/ppermute | solution.py:33
  16.5 1.3 %partial_sketch.3 = (f32[64,1024]{1,0:T(8,128)S(1)}, bf16[64,1024]{1,0:T(8,128)(2,1)S(1)}, bf16[64,1024]{1,0:T(8,128)(2,1)S(1)}, f32[64,1024]{1,0:T(8,128)S(1)}, f32[64,1024]{1,0:T(8,128)S(1)}) custom-call(bf16[2048,2048]{1,0:T(8,128)(2,1)S(1)} %get-tuple-element.25.tiles, f32[8,128]{1,0:T(8,128)S(1)} %get-tuple-element.27.token, ...), custom_call_target="tpu_custom_call" | custom-call | flops 1073741824 | bytes 4194304 | tf_op jit(solution)/shard_map/partial_sketch/pallas_call | solution.py:123
  17.8 2.6 %collective-permute-start.10 = (bf16[64,1024]{1,0:T(8,128)(2,1)S(1)}, bf16[64,1024]{1,0:T(8,128)(2,1)S(1)}, u32[]{:S(2)}, u32[]{:S(2)}) collective-permute-start(bf16[64,1024]{1,0:T(8,128)(2,1)S(1)} %get-tuple-element.42), channel_id=1, source_target_pairs={{0,1},{3,2},{2,0},{1,3},{4,5},{7,6},{6,4},{5,7},{8,9},{11,10},{10,... | collective-permute-start | bytes 393224 | tf_op jit(solution)/shard_map/ppermute | solution.py:33
  20.5 1.0 %collective-permute-done.6 = bf16[64,1024]{1,0:T(8,128)(2,1)S(1)} collective-permute-done((bf16[64,1024]{1,0:T(8,128)(2,1)S(1)}, bf16[64,1024]{1,0:T(8,128)(2,1)S(1)}, u32[]{:S(2)}, u32[]{:S(2)}) %collective-permute-start.6) | collective-permute-done | bytes 131104 | tf_op jit(solution)/shard_map/ppermute | solution.py:33
  21.5 4.4 %collective-permute-start.8 = (bf16[64,1024]{1,0:T(8,128)(2,1)S(1)}, bf16[64,1024]{1,0:T(8,128)(2,1)S(1)}, u32[]{:S(2)}, u32[]{:S(2)}) collective-permute-start(bf16[64,1024]{1,0:T(8,128)(2,1)S(1)} %get-tuple-element.52), channel_id=1, source_target_pairs={{0,3},{1,2},{2,1},{3,0},{4,7},{5,6},{6,5},{7,4},{8,11},{9,10},{10,... | collective-permute-start | bytes 393224 | tf_op jit(solution)/shard_map/ppermute | solution.py:18
  26.0 2.7 %collective-permute-start.11 = (bf16[64,1024]{1,0:T(8,128)(2,1)S(1)}, bf16[64,1024]{1,0:T(8,128)(2,1)S(1)}, u32[]{:S(2)}, u32[]{:S(2)}) collective-permute-start(bf16[64,1024]{1,0:T(8,128)(2,1)S(1)} %get-tuple-element.54), channel_id=1, source_target_pairs={{0,3},{1,2},{2,1},{3,0},{4,7},{5,6},{6,5},{7,4},{8,11},{9,10},{10,... | collective-permute-start | bytes 393224 | tf_op jit(solution)/shard_map/ppermute | solution.py:18
  28.7 1.8 %collective-permute-done.8 = bf16[64,1024]{1,0:T(8,128)(2,1)S(1)} collective-permute-done((bf16[64,1024]{1,0:T(8,128)(2,1)S(1)}, bf16[64,1024]{1,0:T(8,128)(2,1)S(1)}, u32[]{:S(2)}, u32[]{:S(2)}) %collective-permute-start.8) | collective-permute-done | bytes 131104 | tf_op jit(solution)/shard_map/ppermute | solution.py:18
  30.5 2.2 %collective-permute-start.9 = (bf16[64,1024]{1,0:T(8,128)(2,1)S(1)}, bf16[64,1024]{1,0:T(8,128)(2,1)S(1)}, u32[]{:S(2)}, u32[]{:S(2)}) collective-permute-start(bf16[64,1024]{1,0:T(8,128)(2,1)S(1)} %get-tuple-element.39), channel_id=1, source_target_pairs={{0,1},{1,0},{2,3},{3,2},{4,5},{5,4},{6,7},{7,6},{8,9},{9,8},{10,11... | collective-permute-start | bytes 393224 | tf_op jit(solution)/shard_map/ppermute | solution.py:18
  32.6 3.1 %collective-permute-done.7 = bf16[64,1024]{1,0:T(8,128)(2,1)S(1)} collective-permute-done((bf16[64,1024]{1,0:T(8,128)(2,1)S(1)}, bf16[64,1024]{1,0:T(8,128)(2,1)S(1)}, u32[]{:S(2)}, u32[]{:S(2)}) %collective-permute-start.7) | collective-permute-done | bytes 131104 | tf_op jit(solution)/shard_map/ppermute | solution.py:18
  36.3 1.8 %collective-permute-done.9 = bf16[64,1024]{1,0:T(8,128)(2,1)S(1)} collective-permute-done((bf16[64,1024]{1,0:T(8,128)(2,1)S(1)}, bf16[64,1024]{1,0:T(8,128)(2,1)S(1)}, u32[]{:S(2)}, u32[]{:S(2)}) %collective-permute-start.9) | collective-permute-done | bytes 131104 | tf_op jit(solution)/shard_map/ppermute | solution.py:18
  38.3 5.8 %collective-permute-start.13 = (bf16[64,1024]{1,0:T(8,128)(2,1)S(1)}, bf16[64,1024]{1,0:T(8,128)(2,1)S(1)}, u32[]{:S(2)}, u32[]{:S(2)}) collective-permute-start(bf16[64,1024]{1,0:T(8,128)(2,1)S(1)} %get-tuple-element.50.refs_0_), channel_id=1, source_target_pairs={{0,3},{1,2},{2,1},{3,0},{4,7},{5,6},{6,5},{7,4},{8,11},{9,10},{10,... | collective-permute-start | bytes 393224 | tf_op jit(solution)/shard_map/ppermute | solution.py:18
  44.1 2.0 %collective-permute-start.12 = (bf16[64,1024]{1,0:T(8,128)(2,1)S(1)}, bf16[64,1024]{1,0:T(8,128)(2,1)S(1)}, u32[]{:S(2)}, u32[]{:S(2)}) collective-permute-start(bf16[64,1024]{1,0:T(8,128)(2,1)S(1)} %get-tuple-element.50.refs_0_), channel_id=1, source_target_pairs={{0,1},{1,0},{2,3},{3,2},{4,5},{5,4},{6,7},{7,6},{8,9},{9,8},{10,11... | collective-permute-start | bytes 393224 | tf_op jit(solution)/shard_map/ppermute | solution.py:18
  46.3 2.3 %collective-permute-done.13.refs_3_ = bf16[64,1024]{1,0:T(8,128)(2,1)S(1)} collective-permute-done((bf16[64,1024]{1,0:T(8,128)(2,1)S(1)}, bf16[64,1024]{1,0:T(8,128)(2,1)S(1)}, u32[]{:S(2)}, u32[]{:S(2)}) %collective-permute-start.13) | collective-permute-done | bytes 131104 | tf_op jit(solution)/shard_map/ppermute | solution.py:18
  48.6 1.9 %collective-permute-done.15.refs_1_ = bf16[64,1024]{1,0:T(8,128)(2,1)S(1)} collective-permute-done((bf16[64,1024]{1,0:T(8,128)(2,1)S(1)}, bf16[64,1024]{1,0:T(8,128)(2,1)S(1)}, u32[]{:S(2)}, u32[]{:S(2)}) %collective-permute-start.15) | collective-permute-done | bytes 131104 | tf_op jit(solution)/shard_map/ppermute | solution.py:18
  50.6 2.8 %collective-permute-done.17.refs_2_ = bf16[64,1024]{1,0:T(8,128)(2,1)S(1)} collective-permute-done((bf16[64,1024]{1,0:T(8,128)(2,1)S(1)}, bf16[64,1024]{1,0:T(8,128)(2,1)S(1)}, u32[]{:S(2)}, u32[]{:S(2)}) %collective-permute-start.17) | collective-permute-done | bytes 131104 | tf_op jit(solution)/shard_map/ppermute | solution.py:51
  53.4 1.3 %partial_adjoint.3.refs_4_ = f32[256,2048]{1,0:T(8,128)S(1)} custom-call(bf16[2048,2048]{1,0:T(8,128)(2,1)S(1)} %get-tuple-element.25.tiles, bf16[64,1024]{1,0:T(8,128)(2,1)S(1)} %get-tuple-element.48.refs_0_, bf16[64,1024]{1,0:T(8,128)(2,1)S(1)} %collective-permute-done.15.refs_1_, bf16[64,1024]{1,0:T(8,128)(2,1)S(1)} %collective-permute-done.17.refs_2_, ...), custom_call_target="tpu_custom_call" | custom-call | tf_op jit(solution)/shard_map/partial_adjoint/pallas_call | solution.py:164
  54.8 0.7 %partial_adjoint.5 = (f32[64,2048]{1,0:T(8,128)S(1)}, f32[64,2048]{1,0:T(8,128)S(1)}) custom-call(bf16[2048,2048]{1,0:T(8,128)(2,1)S(1)} %get-tuple-element.25.tiles, bf16[64,1024]{1,0:T(8,128)(2,1)S(1)} %get-tuple-element.50.refs_0_, bf16[64,1024]{1,0:T(8,128)(2,1)S(1)} %collective-permute-done.12.refs_1_, ...), custom_call_target="tpu_custom_call" | custom-call | tf_op jit(solution)/shard_map/partial_adjoint/pallas_call | solution.py:164
  56.1 0.7 %partial_adjoint.4 = (f32[64,2048]{1,0:T(8,128)S(1)}, f32[64,2048]{1,0:T(8,128)S(1)}) custom-call(bf16[2048,2048]{1,0:T(8,128)(2,1)S(1)} %get-tuple-element.25.tiles, bf16[64,1024]{1,0:T(8,128)(2,1)S(1)} %get-tuple-element.50.refs_0_, bf16[64,1024]{1,0:T(8,128)(2,1)S(1)} %collective-permute-done.12.refs_1_, ...), custom_call_target="tpu_custom_call" | custom-call | tf_op jit(solution)/shard_map/partial_adjoint/pallas_call | solution.py:164
  57.5 0.7 %collective-permute-start.19 = (bf16[32,2048]{1,0:T(8,128)(2,1)S(1)}, bf16[32,2048]{1,0:T(8,128)(2,1)S(1)}, u32[]{:S(2)}, u32[]{:S(2)}) collective-permute-start(bf16[32,2048]{1,0:T(8,128)(2,1)S(1)} %slice_add_fusion.2), channel_id=1, source_target_pairs={{0,8},{4,12},{8,0},{12,4},{16,24},{20,28},{24,16},{28,20},{1,9},{5... | collective-permute-start | bytes 393224 | tf_op jit(solution)/shard_map/ppermute | solution.py:18
  58.3 1.4 %collective-permute-start.22 = (bf16[32,2048]{1,0:T(8,128)(2,1)S(1)}, bf16[32,2048]{1,0:T(8,128)(2,1)S(1)}, u32[]{:S(2)}, u32[]{:S(2)}) collective-permute-start(bf16[32,2048]{1,0:T(8,128)(2,1)S(1)} %get-tuple-element.57), channel_id=1, source_target_pairs={{0,16},{4,20},{8,24},{12,28},{16,0},{20,4},{24,8},{28,12},{1,17},{... | collective-permute-start | bytes 393224 | tf_op jit(solution)/shard_map/ppermute | solution.py:18
  59.8 1.4 %collective-permute-start.21 = (bf16[32,2048]{1,0:T(8,128)(2,1)S(1)}, bf16[32,2048]{1,0:T(8,128)(2,1)S(1)}, u32[]{:S(2)}, u32[]{:S(2)}) collective-permute-start(bf16[32,2048]{1,0:T(8,128)(2,1)S(1)} %get-tuple-element.56), channel_id=1, source_target_pairs={{0,24},{4,28},{8,16},{12,20},{16,8},{20,12},{24,0},{28,4},{1,25},{... | collective-permute-start | bytes 393224 | tf_op jit(solution)/shard_map/ppermute | solution.py:18
  61.2 0.8 %maximum_bitcast_fusion = f32[2048,64]{0,1:T(8,128)} fusion(f32[64,1024]{1,0:T(8,128)S(1)} %get-tuple-element.51, f32[64,1024]{1,0:T(8,128)S(1)} %get-tuple-element.49), kind=kLoop, calls=%fused_computation | loop fusion | flops 131072 | bytes 1048576 | tf_op jit(solution)/shard_map/transpose | solution.py:225
  62.0 3.6 %collective-permute-done.22 = bf16[32,2048]{1,0:T(8,128)(2,1)S(1)} collective-permute-done((bf16[32,2048]{1,0:T(8,128)(2,1)S(1)}, bf16[32,2048]{1,0:T(8,128)(2,1)S(1)}, u32[]{:S(2)}, u32[]{:S(2)}) %collective-permute-start.22) | collective-permute-done | bytes 131104 | tf_op jit(solution)/shard_map/ppermute | solution.py:18
  65.7 1.1 %collective-permute-done.21 = bf16[32,2048]{1,0:T(8,128)(2,1)S(1)} collective-permute-done((bf16[32,2048]{1,0:T(8,128)(2,1)S(1)}, bf16[32,2048]{1,0:T(8,128)(2,1)S(1)}, u32[]{:S(2)}, u32[]{:S(2)}) %collective-permute-start.21) | collective-permute-done | bytes 131104 | tf_op jit(solution)/shard_map/ppermute | solution.py:18
  66.8 0.8 %fusion.11 = f32[2048,32]{0,1:T(8,128)} fusion(f32[64,2048]{1,0:T(8,128)S(1)} %collective-permute-done.18, bf16[32,2048]{1,0:T(8,128)(2,1)S(1)} %collective-permute-done.22, bf16[32,2048]{1,0:T(8,128)(2,1)S(1)} %collective-permute-done.21, bf16[32,2048]{1,0:T(8,128)(2,1)S(1)} %collective-permute-done.19, f32[64,2048]{1,0:T(8,128)S(1)} %get-tuple-element.43), kind=kLoop, calls=%fused_computation.20 | loop fusion | flops 458752 | bytes 1179648 | tf_op jit(solution)/shard_map/transpose | solution.py:225
  (33 shorter events, 2.6 us)
Async XLA Ops:
  0.6 12.9 %copy-start = (bf16[2048,32]{0,1:T(8,128)(2,1)S(1)}, bf16[2048,32]{0,1:T(8,128)(2,1)}, u32[]{:S(2)}) copy-start(bf16[2048,32]{0,1:T(8,128)(2,1)} %param.5) | copy-start | bytes 393220
  0.6 8.2 %collective-permute-start = (bf16[32,2048]{1,0:T(8,128)(2,1)}, bf16[32,2048]{1,0:T(8,128)(2,1)S(1)}, u32[]{:S(2)}, u32[]{:S(2)}) collective-permute-start(bf16[32,2048]{1,0:T(8,128)(2,1)} %bitcast.5), channel_id=1, source_target_pairs={{0,8},{4,12},{8,0},{12,4},{16,24},{20,28},{24,16},{28,20},{1,9},{5... | collective-permute-start | bytes 393224 | tf_op jit(solution)/shard_map/ppermute | solution.py:18
  3.6 7.2 %collective-permute-start.1 = (bf16[32,2048]{1,0:T(8,128)(2,1)}, bf16[32,2048]{1,0:T(8,128)(2,1)S(1)}, u32[]{:S(2)}, u32[]{:S(2)}) collective-permute-start(bf16[32,2048]{1,0:T(8,128)(2,1)} %bitcast.6), channel_id=1, source_target_pairs={{0,16},{4,20},{8,24},{12,28},{16,0},{20,4},{24,8},{28,12},{1,17},{... | collective-permute-start | bytes 393224 | tf_op jit(solution)/shard_map/ppermute | solution.py:18
  5.2 5.6 %collective-permute-start.2 = (bf16[32,2048]{1,0:T(8,128)(2,1)}, bf16[32,2048]{1,0:T(8,128)(2,1)S(1)}, u32[]{:S(2)}, u32[]{:S(2)}) collective-permute-start(bf16[32,2048]{1,0:T(8,128)(2,1)} %bitcast.7), channel_id=1, source_target_pairs={{0,4},{4,0},{8,12},{12,8},{16,20},{20,16},{24,28},{28,24},{1,5},{5... | collective-permute-start | bytes 393224 | tf_op jit(solution)/shard_map/ppermute | solution.py:18
  5.2 7.0 %collective-permute-start.3 = (bf16[32,2048]{1,0:T(8,128)(2,1)}, bf16[32,2048]{1,0:T(8,128)(2,1)S(1)}, u32[]{:S(2)}, u32[]{:S(2)}) collective-permute-start(bf16[32,2048]{1,0:T(8,128)(2,1)} %bitcast.8), channel_id=1, source_target_pairs={{0,24},{4,28},{8,16},{12,20},{16,8},{20,12},{24,0},{28,4},{1,25},{... | collective-permute-start | bytes 393224 | tf_op jit(solution)/shard_map/ppermute | solution.py:18
  10.8 2.7 %collective-permute-start.4 = (bf16[64,2048]{1,0:T(8,128)(2,1)S(1)}, bf16[64,2048]{1,0:T(8,128)(2,1)S(1)}, u32[]{:S(2)}, u32[]{:S(2)}) collective-permute-start(bf16[64,2048]{1,0:T(8,128)(2,1)S(1)} %pad_maximum_fusion), channel_id=1, source_target_pairs={{0,4},{4,0},{8,12},{12,8},{16,20},{20,16},{24,28},{28,24},{1,5},{5... | collective-permute-start | bytes 786440 | tf_op jit(solution)/shard_map/ppermute | solution.py:18
  12.2 1.3 %collective-permute-start.5 = (bf16[32,2048]{1,0:T(8,128)(2,1)S(1)}, bf16[32,2048]{1,0:T(8,128)(2,1)S(1)}, u32[]{:S(2)}, u32[]{:S(2)}) collective-permute-start(bf16[32,2048]{1,0:T(8,128)(2,1)S(1)} %collective-permute-done.3.refs_3_), channel_id=1, source_target_pairs={{0,4},{4,0},{8,12},{12,8},{16,20},{20,16},{24,28},{28,24},{1,5},{5... | collective-permute-start | bytes 393224 | tf_op jit(solution)/shard_map/ppermute | solution.py:18
  14.9 6.6 %collective-permute-start.6 = (bf16[64,1024]{1,0:T(8,128)(2,1)S(1)}, bf16[64,1024]{1,0:T(8,128)(2,1)S(1)}, u32[]{:S(2)}, u32[]{:S(2)}) collective-permute-start(bf16[64,1024]{1,0:T(8,128)(2,1)S(1)} %get-tuple-element.35), channel_id=1, source_target_pairs={{0,1},{3,2},{2,0},{1,3},{4,5},{7,6},{6,4},{5,7},{8,9},{11,10},{10,... | collective-permute-start | bytes 393224 | tf_op jit(solution)/shard_map/ppermute | solution.py:33
  17.8 8.1 %collective-permute-start.10 = (bf16[64,1024]{1,0:T(8,128)(2,1)S(1)}, bf16[64,1024]{1,0:T(8,128)(2,1)S(1)}, u32[]{:S(2)}, u32[]{:S(2)}) collective-permute-start(bf16[64,1024]{1,0:T(8,128)(2,1)S(1)} %get-tuple-element.42), channel_id=1, source_target_pairs={{0,1},{3,2},{2,0},{1,3},{4,5},{7,6},{6,4},{5,7},{8,9},{11,10},{10,... | collective-permute-start | bytes 393224 | tf_op jit(solution)/shard_map/ppermute | solution.py:33
  21.5 8.9 %collective-permute-start.8 = (bf16[64,1024]{1,0:T(8,128)(2,1)S(1)}, bf16[64,1024]{1,0:T(8,128)(2,1)S(1)}, u32[]{:S(2)}, u32[]{:S(2)}) collective-permute-start(bf16[64,1024]{1,0:T(8,128)(2,1)S(1)} %get-tuple-element.52), channel_id=1, source_target_pairs={{0,3},{1,2},{2,1},{3,0},{4,7},{5,6},{6,5},{7,4},{8,11},{9,10},{10,... | collective-permute-start | bytes 393224 | tf_op jit(solution)/shard_map/ppermute | solution.py:18
  25.9 9.8 %collective-permute-start.7 = (bf16[64,1024]{1,0:T(8,128)(2,1)S(1)}, bf16[64,1024]{1,0:T(8,128)(2,1)S(1)}, u32[]{:S(2)}, u32[]{:S(2)}) collective-permute-start(bf16[64,1024]{1,0:T(8,128)(2,1)S(1)} %get-tuple-element.36), channel_id=1, source_target_pairs={{0,1},{1,0},{2,3},{3,2},{4,5},{5,4},{6,7},{7,6},{8,9},{9,8},{10,11... | collective-permute-start | bytes 393224 | tf_op jit(solution)/shard_map/ppermute | solution.py:18
  26.0 10.3 %collective-permute-start.11 = (bf16[64,1024]{1,0:T(8,128)(2,1)S(1)}, bf16[64,1024]{1,0:T(8,128)(2,1)S(1)}, u32[]{:S(2)}, u32[]{:S(2)}) collective-permute-start(bf16[64,1024]{1,0:T(8,128)(2,1)S(1)} %get-tuple-element.54), channel_id=1, source_target_pairs={{0,3},{1,2},{2,1},{3,0},{4,7},{5,6},{6,5},{7,4},{8,11},{9,10},{10,... | collective-permute-start | bytes 393224 | tf_op jit(solution)/shard_map/ppermute | solution.py:18
  30.5 7.7 %collective-permute-start.9 = (bf16[64,1024]{1,0:T(8,128)(2,1)S(1)}, bf16[64,1024]{1,0:T(8,128)(2,1)S(1)}, u32[]{:S(2)}, u32[]{:S(2)}) collective-permute-start(bf16[64,1024]{1,0:T(8,128)(2,1)S(1)} %get-tuple-element.39), channel_id=1, source_target_pairs={{0,1},{1,0},{2,3},{3,2},{4,5},{5,4},{6,7},{7,6},{8,9},{9,8},{10,11... | collective-permute-start | bytes 393224 | tf_op jit(solution)/shard_map/ppermute | solution.py:18
  35.8 10.3 %collective-permute-start.16 = (bf16[64,1024]{1,0:T(8,128)(2,1)S(1)}, bf16[64,1024]{1,0:T(8,128)(2,1)S(1)}, u32[]{:S(2)}, u32[]{:S(2)}) collective-permute-start(bf16[64,1024]{1,0:T(8,128)(2,1)S(1)} %get-tuple-element.48.refs_0_), channel_id=1, source_target_pairs={{0,3},{1,2},{2,1},{3,0},{4,7},{5,6},{6,5},{7,4},{8,11},{9,10},{10,... | collective-permute-start | bytes 393224 | tf_op jit(solution)/shard_map/ppermute | solution.py:18
  38.3 10.3 %collective-permute-start.13 = (bf16[64,1024]{1,0:T(8,128)(2,1)S(1)}, bf16[64,1024]{1,0:T(8,128)(2,1)S(1)}, u32[]{:S(2)}, u32[]{:S(2)}) collective-permute-start(bf16[64,1024]{1,0:T(8,128)(2,1)S(1)} %get-tuple-element.50.refs_0_), channel_id=1, source_target_pairs={{0,3},{1,2},{2,1},{3,0},{4,7},{5,6},{6,5},{7,4},{8,11},{9,10},{10,... | collective-permute-start | bytes 393224 | tf_op jit(solution)/shard_map/ppermute | solution.py:18
  44.1 6.5 %collective-permute-start.15 = (bf16[64,1024]{1,0:T(8,128)(2,1)S(1)}, bf16[64,1024]{1,0:T(8,128)(2,1)S(1)}, u32[]{:S(2)}, u32[]{:S(2)}) collective-permute-start(bf16[64,1024]{1,0:T(8,128)(2,1)S(1)} %get-tuple-element.48.refs_0_), channel_id=1, source_target_pairs={{0,1},{1,0},{2,3},{3,2},{4,5},{5,4},{6,7},{7,6},{8,9},{9,8},{10,11... | collective-permute-start | bytes 393224 | tf_op jit(solution)/shard_map/ppermute | solution.py:18
  44.1 10.5 %collective-permute-start.12 = (bf16[64,1024]{1,0:T(8,128)(2,1)S(1)}, bf16[64,1024]{1,0:T(8,128)(2,1)S(1)}, u32[]{:S(2)}, u32[]{:S(2)}) collective-permute-start(bf16[64,1024]{1,0:T(8,128)(2,1)S(1)} %get-tuple-element.50.refs_0_), channel_id=1, source_target_pairs={{0,1},{1,0},{2,3},{3,2},{4,5},{5,4},{6,7},{7,6},{8,9},{9,8},{10,11... | collective-permute-start | bytes 393224 | tf_op jit(solution)/shard_map/ppermute | solution.py:18
  46.2 7.2 %collective-permute-start.17 = (bf16[64,1024]{1,0:T(8,128)(2,1)S(1)}, bf16[64,1024]{1,0:T(8,128)(2,1)S(1)}, u32[]{:S(2)}, u32[]{:S(2)}) collective-permute-start(bf16[64,1024]{1,0:T(8,128)(2,1)S(1)} %select_n.26), channel_id=1, source_target_pairs={{0,2},{3,1},{1,0},{2,3},{4,6},{7,5},{5,4},{6,7},{8,10},{11,9},{9,8... | collective-permute-start | bytes 393224 | tf_op jit(solution)/shard_map/ppermute | solution.py:51
  48.6 6.2 %collective-permute-start.14 = (bf16[64,1024]{1,0:T(8,128)(2,1)S(1)}, bf16[64,1024]{1,0:T(8,128)(2,1)S(1)}, u32[]{:S(2)}, u32[]{:S(2)}) collective-permute-start(bf16[64,1024]{1,0:T(8,128)(2,1)S(1)} %select_n.25), channel_id=1, source_target_pairs={{0,2},{3,1},{1,0},{2,3},{4,6},{7,5},{5,4},{6,7},{8,10},{11,9},{9,8... | collective-permute-start | bytes 393224 | tf_op jit(solution)/shard_map/ppermute | solution.py:51
  55.5 2.0 %collective-permute-start.18 = (f32[64,2048]{1,0:T(8,128)S(1)}, f32[64,2048]{1,0:T(8,128)S(1)}, u32[]{:S(2)}, u32[]{:S(2)}) collective-permute-start(f32[64,2048]{1,0:T(8,128)S(1)} %get-tuple-element.44), channel_id=1, source_target_pairs={{0,4},{4,0},{8,12},{12,8},{16,20},{20,16},{24,28},{28,24},{1,5},{5... | collective-permute-start | bytes 1572872 | tf_op jit(solution)/shard_map/ppermute | solution.py:18
  55.6 2.7 %collective-permute-start.20 = (f32[64,2048]{1,0:T(8,128)S(1)}, f32[64,2048]{1,0:T(8,128)S(1)}, u32[]{:S(2)}, u32[]{:S(2)}) collective-permute-start(f32[64,2048]{1,0:T(8,128)S(1)} %get-tuple-element.47), channel_id=1, source_target_pairs={{0,4},{4,0},{8,12},{12,8},{16,20},{20,16},{24,28},{28,24},{1,5},{5... | collective-permute-start | bytes 1572872 | tf_op jit(solution)/shard_map/ppermute | solution.py:18
  57.5 9.3 %collective-permute-start.19 = (bf16[32,2048]{1,0:T(8,128)(2,1)S(1)}, bf16[32,2048]{1,0:T(8,128)(2,1)S(1)}, u32[]{:S(2)}, u32[]{:S(2)}) collective-permute-start(bf16[32,2048]{1,0:T(8,128)(2,1)S(1)} %slice_add_fusion.2), channel_id=1, source_target_pairs={{0,8},{4,12},{8,0},{12,4},{16,24},{20,28},{24,16},{28,20},{1,9},{5... | collective-permute-start | bytes 393224 | tf_op jit(solution)/shard_map/ppermute | solution.py:18
  58.3 7.3 %collective-permute-start.22 = (bf16[32,2048]{1,0:T(8,128)(2,1)S(1)}, bf16[32,2048]{1,0:T(8,128)(2,1)S(1)}, u32[]{:S(2)}, u32[]{:S(2)}) collective-permute-start(bf16[32,2048]{1,0:T(8,128)(2,1)S(1)} %get-tuple-element.57), channel_id=1, source_target_pairs={{0,16},{4,20},{8,24},{12,28},{16,0},{20,4},{24,8},{28,12},{1,17},{... | collective-permute-start | bytes 393224 | tf_op jit(solution)/shard_map/ppermute | solution.py:18
  59.8 7.0 %collective-permute-start.21 = (bf16[32,2048]{1,0:T(8,128)(2,1)S(1)}, bf16[32,2048]{1,0:T(8,128)(2,1)S(1)}, u32[]{:S(2)}, u32[]{:S(2)}) collective-permute-start(bf16[32,2048]{1,0:T(8,128)(2,1)S(1)} %get-tuple-element.56), channel_id=1, source_target_pairs={{0,24},{4,28},{8,16},{12,20},{16,8},{20,12},{24,0},{28,4},{1,25},{... | collective-permute-start | bytes 393224 | tf_op jit(solution)/shard_map/ppermute | solution.py:18

commit v25 on v19

--- a/solution.py
+++ b/solution.py
@@ -189,9 +189,9 @@
 
     own = probes.T
     held = [own] + [exchange(own, "row", offset) for offset in gather_core[1:]]
-    twin = exchange(own, "row", 1)
-    held, twin, token = lax.optimization_barrier((held, twin, token))
-    blocks = held + [twin, exchange(jnp.concatenate(held[1:]), "row", 1)]
+    early, late = held[:-1], held[-1]
+    early, token = lax.optimization_barrier((early, token))
+    blocks = [*early, late, exchange(jnp.concatenate(early), "row", 1), exchange(late, "row", 1)]
 
     totals, shares = [], []
     for chunk in range(chunks):

time: 67.6 us -> 71.1 us (1.052)
  waiting for transfers between devices: 21.6 us -> 23.6 us
  starting transfers between devices: 33.9 us -> 35.5 us
    ppermute x18, waiting for transfers between devices: 18.4 us -> 20.4 us  [exchange(): return lax.ppermute(value, axis, [(i, i ^ offset) for i in range(size)])]
    ppermute x18, starting transfers between devices: 22 us -> 23.4 us  [exchange(): return lax.ppermute(value, axis, [(i, i ^ offset) for i in range(size)])]
  transfers between devices with their start and end apart: 22 -> 22, of which waited for: 13 -> 14; matrix products, arithmetic and copies ran while one was open for 2% -> 2% of each run, Pallas kernels for 10% -> 10%
where the time goes in v25:
time: 71.1 us; the launch traced here: 71 us
  starting transfers between devices  35.5 us (50%)
  waiting for transfers between devices  23.6 us (33%)
  Pallas kernels  9.01 us (13%)
  other arithmetic  2.12 us (3%)
  between operations  0.77 us (1%)
    ppermute x18, starting transfers between devices, exchange(): return lax.ppermute(value, axis, [(i, i ^ offset) for i in range(size)])  23.4 us
    ppermute x18, waiting for transfers between devices, exchange(): return lax.ppermute(value, axis, [(i, i ^ offset) for i in range(size)])  20.4 us
    ppermute x2, starting transfers between devices, window_spread(): lax.ppermute(onward, 'col', [(0, 2), (3, 1), (1, 0), (2, 3)])  7.68 us
    ppermute x2, starting transfers between devices, window_sums(): came = lax.ppermute(terms[2], 'col', [(0, 1), (3, 2), (2, 0), (1, 3)])  4.4 us
    pallas_call x1, Pallas kernels, masked(): pl.pallas_call(functools.partial(mask_kernel, block=rows // mask.shape[0]...  3.62 us
    pallas_call x3, Pallas kernels, partial_adjoint(): pl.pallas_call(functools.partial(adjoint_kernel, base=base, span=span, pa...  2.75 us
    pallas_call x2, Pallas kernels, partial_sketch(): pl.pallas_call(functools.partial(sketch_kernel, base=chunk * rows, offset...  2.64 us
    ppermute x2, waiting for transfers between devices, window_spread(): lax.ppermute(onward, 'col', [(0, 2), (3, 1), (1, 0), (2, 3)])  2.23 us
  transfers between devices with their start and end apart: 22, of which 14 were waited for; matrix products, arithmetic and copies ran while one was open for 2% of the time, Pallas kernels for 10%

profile of v25, /device:TPU:0, one launch (start us, length us, event | category | flops | bytes accessed | tf_op | source)
XLA Modules:
  0.0 71.0 jit_solution(5199237295562836139)
XLA Ops:
  0.6 3.0 %collective-permute-start = (bf16[32,2048]{1,0:T(8,128)(2,1)}, bf16[32,2048]{1,0:T(8,128)(2,1)S(1)}, u32[]{:S(2)}, u32[]{:S(2)}) collective-permute-start(bf16[32,2048]{1,0:T(8,128)(2,1)} %bitcast.5), channel_id=1, source_target_pairs={{0,8},{4,12},{8,0},{12,4},{16,24},{20,28},{24,16},{28,20},{1,9},{5... | collective-permute-start | bytes 393224 | tf_op jit(solution)/shard_map/ppermute | solution.py:18
  3.6 1.5 %collective-permute-start.1 = (bf16[32,2048]{1,0:T(8,128)(2,1)}, bf16[32,2048]{1,0:T(8,128)(2,1)S(1)}, u32[]{:S(2)}, u32[]{:S(2)}) collective-permute-start(bf16[32,2048]{1,0:T(8,128)(2,1)} %bitcast.6), channel_id=1, source_target_pairs={{0,16},{4,20},{8,24},{12,28},{16,0},{20,4},{24,8},{28,12},{1,17},{... | collective-permute-start | bytes 393224 | tf_op jit(solution)/shard_map/ppermute | solution.py:18
  5.2 3.6 %masked_tiles.1 = (bf16[2048,2048]{1,0:T(8,128)(2,1)S(1)}, f32[8,128]{1,0:T(8,128)S(1)}) custom-call(s32[8,8]{1,0:T(8,128)} %mask_hbm.1, bf16[2048,2048]{1,0:T(8,128)(2,1)} %green_ref.1), custom_call_target="tpu_custom_call" | custom-call | bytes 8388608 | tf_op jit(solution)/shard_map/masked_tiles/pallas_call | solution.py:78
  8.9 1.6 %collective-permute-start.2 = (bf16[32,2048]{1,0:T(8,128)(2,1)S(1)}, bf16[32,2048]{1,0:T(8,128)(2,1)S(1)}, u32[]{:S(2)}, u32[]{:S(2)}) collective-permute-start(bf16[32,2048]{1,0:T(8,128)(2,1)S(1)} %bitcast.8), channel_id=1, source_target_pairs={{0,24},{4,28},{8,16},{12,20},{16,8},{20,12},{24,0},{28,4},{1,25},{... | collective-permute-start | bytes 393224 | tf_op jit(solution)/shard_map/ppermute | solution.py:18
  10.5 5.3 %collective-permute-done.2.refs_3_ = bf16[32,2048]{1,0:T(8,128)(2,1)S(1)} collective-permute-done((bf16[32,2048]{1,0:T(8,128)(2,1)S(1)}, bf16[32,2048]{1,0:T(8,128)(2,1)S(1)}, u32[]{:S(2)}, u32[]{:S(2)}) %collective-permute-start.2) | collective-permute-done | bytes 131104 | tf_op jit(solution)/shard_map/ppermute | solution.py:18
  15.8 1.3 %collective-permute-done.4.refs_5_ = bf16[32,2048]{1,0:T(8,128)(2,1)S(1)} collective-permute-done((bf16[32,2048]{1,0:T(8,128)(2,1)S(1)}, bf16[32,2048]{1,0:T(8,128)(2,1)S(1)}, u32[]{:S(2)}, u32[]{:S(2)}) %collective-permute-start.4) | collective-permute-done | bytes 131104 | tf_op jit(solution)/shard_map/ppermute | solution.py:18
  17.1 1.3 %partial_sketch.2 = (f32[64,1024]{1,0:T(8,128)S(1)}, bf16[64,1024]{1,0:T(8,128)(2,1)S(1)}, bf16[64,1024]{1,0:T(8,128)(2,1)S(1)}, f32[64,1024]{1,0:T(8,128)S(1)}, f32[64,1024]{1,0:T(8,128)S(1)}) custom-call(bf16[2048,2048]{1,0:T(8,128)(2,1)S(1)} %get-tuple-element.25.tiles, f32[8,128]{1,0:T(8,128)S(1)} %get-tuple-element.27.token, ...), custom_call_target="tpu_custom_call" | custom-call | flops 1073741824 | bytes 4194304 | tf_op jit(solution)/shard_map/partial_sketch/pallas_call | solution.py:123
  18.4 1.7 %collective-permute-start.5 = (bf16[64,1024]{1,0:T(8,128)(2,1)S(1)}, bf16[64,1024]{1,0:T(8,128)(2,1)S(1)}, u32[]{:S(2)}, u32[]{:S(2)}) collective-permute-start(bf16[64,1024]{1,0:T(8,128)(2,1)S(1)} %get-tuple-element.35), channel_id=1, source_target_pairs={{0,1},{3,2},{2,0},{1,3},{4,5},{7,6},{6,4},{5,7},{8,9},{11,10},{10,... | collective-permute-start | bytes 393224 | tf_op jit(solution)/shard_map/ppermute | solution.py:33
  20.2 1.3 %partial_sketch.3 = (f32[64,1024]{1,0:T(8,128)S(1)}, bf16[64,1024]{1,0:T(8,128)(2,1)S(1)}, bf16[64,1024]{1,0:T(8,128)(2,1)S(1)}, f32[64,1024]{1,0:T(8,128)S(1)}, f32[64,1024]{1,0:T(8,128)S(1)}) custom-call(bf16[2048,2048]{1,0:T(8,128)(2,1)S(1)} %get-tuple-element.25.tiles, f32[8,128]{1,0:T(8,128)S(1)} %get-tuple-element.27.token, ...), custom_call_target="tpu_custom_call" | custom-call | flops 1073741824 | bytes 4194304 | tf_op jit(solution)/shard_map/partial_sketch/pallas_call | solution.py:123
  21.5 2.7 %collective-permute-start.8 = (bf16[64,1024]{1,0:T(8,128)(2,1)S(1)}, bf16[64,1024]{1,0:T(8,128)(2,1)S(1)}, u32[]{:S(2)}, u32[]{:S(2)}) collective-permute-start(bf16[64,1024]{1,0:T(8,128)(2,1)S(1)} %get-tuple-element.41), channel_id=1, source_target_pairs={{0,1},{3,2},{2,0},{1,3},{4,5},{7,6},{6,4},{5,7},{8,9},{11,10},{10,... | collective-permute-start | bytes 393224 | tf_op jit(solution)/shard_map/ppermute | solution.py:33
  24.2 0.9 %collective-permute-done.5 = bf16[64,1024]{1,0:T(8,128)(2,1)S(1)} collective-permute-done((bf16[64,1024]{1,0:T(8,128)(2,1)S(1)}, bf16[64,1024]{1,0:T(8,128)(2,1)S(1)}, u32[]{:S(2)}, u32[]{:S(2)}) %collective-permute-start.5) | collective-permute-done | bytes 131104 | tf_op jit(solution)/shard_map/ppermute | solution.py:33
  25.1 4.5 %collective-permute-start.7 = (bf16[64,1024]{1,0:T(8,128)(2,1)S(1)}, bf16[64,1024]{1,0:T(8,128)(2,1)S(1)}, u32[]{:S(2)}, u32[]{:S(2)}) collective-permute-start(bf16[64,1024]{1,0:T(8,128)(2,1)S(1)} %get-tuple-element.52), channel_id=1, source_target_pairs={{0,3},{1,2},{2,1},{3,0},{4,7},{5,6},{6,5},{7,4},{8,11},{9,10},{10,... | collective-permute-start | bytes 393224 | tf_op jit(solution)/shard_map/ppermute | solution.py:18
  29.7 2.7 %collective-permute-start.10 = (bf16[64,1024]{1,0:T(8,128)(2,1)S(1)}, bf16[64,1024]{1,0:T(8,128)(2,1)S(1)}, u32[]{:S(2)}, u32[]{:S(2)}) collective-permute-start(bf16[64,1024]{1,0:T(8,128)(2,1)S(1)} %get-tuple-element.54), channel_id=1, source_target_pairs={{0,3},{1,2},{2,1},{3,0},{4,7},{5,6},{6,5},{7,4},{8,11},{9,10},{10,... | collective-permute-start | bytes 393224 | tf_op jit(solution)/shard_map/ppermute | solution.py:18
  32.4 1.8 %collective-permute-done.7 = bf16[64,1024]{1,0:T(8,128)(2,1)S(1)} collective-permute-done((bf16[64,1024]{1,0:T(8,128)(2,1)S(1)}, bf16[64,1024]{1,0:T(8,128)(2,1)S(1)}, u32[]{:S(2)}, u32[]{:S(2)}) %collective-permute-start.7) | collective-permute-done | bytes 131104 | tf_op jit(solution)/shard_map/ppermute | solution.py:18
  34.2 4.1 %collective-permute-done.6 = bf16[64,1024]{1,0:T(8,128)(2,1)S(1)} collective-permute-done((bf16[64,1024]{1,0:T(8,128)(2,1)S(1)}, bf16[64,1024]{1,0:T(8,128)(2,1)S(1)}, u32[]{:S(2)}, u32[]{:S(2)}) %collective-permute-start.6) | collective-permute-done | bytes 131104 | tf_op jit(solution)/shard_map/ppermute | solution.py:18
  38.3 1.6 %collective-permute-start.15 = (bf16[64,1024]{1,0:T(8,128)(2,1)S(1)}, bf16[64,1024]{1,0:T(8,128)(2,1)S(1)}, u32[]{:S(2)}, u32[]{:S(2)}) collective-permute-start(bf16[64,1024]{1,0:T(8,128)(2,1)S(1)} %get-tuple-element.48.refs_0_), channel_id=1, source_target_pairs={{0,3},{1,2},{2,1},{3,0},{4,7},{5,6},{6,5},{7,4},{8,11},{9,10},{10,... | collective-permute-start | bytes 393224 | tf_op jit(solution)/shard_map/ppermute | solution.py:18
  39.9 1.9 %collective-permute-done.9 = bf16[64,1024]{1,0:T(8,128)(2,1)S(1)} collective-permute-done((bf16[64,1024]{1,0:T(8,128)(2,1)S(1)}, bf16[64,1024]{1,0:T(8,128)(2,1)S(1)}, u32[]{:S(2)}, u32[]{:S(2)}) %collective-permute-start.9) | collective-permute-done | bytes 131104 | tf_op jit(solution)/shard_map/ppermute | solution.py:18
  41.9 2.4 %collective-permute-start.12 = (bf16[64,1024]{1,0:T(8,128)(2,1)S(1)}, bf16[64,1024]{1,0:T(8,128)(2,1)S(1)}, u32[]{:S(2)}, u32[]{:S(2)}) collective-permute-start(bf16[64,1024]{1,0:T(8,128)(2,1)S(1)} %get-tuple-element.50.refs_0_), channel_id=1, source_target_pairs={{0,3},{1,2},{2,1},{3,0},{4,7},{5,6},{6,5},{7,4},{8,11},{9,10},{10,... | collective-permute-start | bytes 393224 | tf_op jit(solution)/shard_map/ppermute | solution.py:18
  44.7 1.6 %collective-permute-start.14 = (bf16[64,1024]{1,0:T(8,128)(2,1)S(1)}, bf16[64,1024]{1,0:T(8,128)(2,1)S(1)}, u32[]{:S(2)}, u32[]{:S(2)}) collective-permute-start(bf16[64,1024]{1,0:T(8,128)(2,1)S(1)} %get-tuple-element.48.refs_0_), channel_id=1, source_target_pairs={{0,1},{1,0},{2,3},{3,2},{4,5},{5,4},{6,7},{7,6},{8,9},{9,8},{10,11... | collective-permute-start | bytes 393224 | tf_op jit(solution)/shard_map/ppermute | solution.py:18
  46.6 3.9 %collective-permute-start.16 = (bf16[64,1024]{1,0:T(8,128)(2,1)S(1)}, bf16[64,1024]{1,0:T(8,128)(2,1)S(1)}, u32[]{:S(2)}, u32[]{:S(2)}) collective-permute-start(bf16[64,1024]{1,0:T(8,128)(2,1)S(1)} %select_n.26), channel_id=1, source_target_pairs={{0,2},{3,1},{1,0},{2,3},{4,6},{7,5},{5,4},{6,7},{8,10},{11,9},{9,8... | collective-permute-start | bytes 393224 | tf_op jit(solution)/shard_map/ppermute | solution.py:51
  50.6 3.8 %collective-permute-start.13 = (bf16[64,1024]{1,0:T(8,128)(2,1)S(1)}, bf16[64,1024]{1,0:T(8,128)(2,1)S(1)}, u32[]{:S(2)}, u32[]{:S(2)}) collective-permute-start(bf16[64,1024]{1,0:T(8,128)(2,1)S(1)} %select_n.25), channel_id=1, source_target_pairs={{0,2},{3,1},{1,0},{2,3},{4,6},{7,5},{5,4},{6,7},{8,10},{11,9},{9,8... | collective-permute-start | bytes 393224 | tf_op jit(solution)/shard_map/ppermute | solution.py:51
  54.7 2.1 %collective-permute-done.16.refs_2_ = bf16[64,1024]{1,0:T(8,128)(2,1)S(1)} collective-permute-done((bf16[64,1024]{1,0:T(8,128)(2,1)S(1)}, bf16[64,1024]{1,0:T(8,128)(2,1)S(1)}, u32[]{:S(2)}, u32[]{:S(2)}) %collective-permute-start.16) | collective-permute-done | bytes 131104 | tf_op jit(solution)/shard_map/ppermute | solution.py:51
  56.8 1.3 %partial_adjoint.3.refs_4_ = f32[256,2048]{1,0:T(8,128)S(1)} custom-call(bf16[2048,2048]{1,0:T(8,128)(2,1)S(1)} %get-tuple-element.25.tiles, bf16[64,1024]{1,0:T(8,128)(2,1)S(1)} %get-tuple-element.48.refs_0_, bf16[64,1024]{1,0:T(8,128)(2,1)S(1)} %collective-permute-done.14.refs_1_, bf16[64,1024]{1,0:T(8,128)(2,1)S(1)} %collective-permute-done.16.refs_2_, ...), custom_call_target="tpu_custom_call" | custom-call | tf_op jit(solution)/shard_map/partial_adjoint/pallas_call | solution.py:164
  58.2 0.7 %partial_adjoint.5 = (f32[64,2048]{1,0:T(8,128)S(1)}, f32[64,2048]{1,0:T(8,128)S(1)}) custom-call(bf16[2048,2048]{1,0:T(8,128)(2,1)S(1)} %get-tuple-element.25.tiles, bf16[64,1024]{1,0:T(8,128)(2,1)S(1)} %get-tuple-element.50.refs_0_, bf16[64,1024]{1,0:T(8,128)(2,1)S(1)} %collective-permute-done.11.refs_1_, ...), custom_call_target="tpu_custom_call" | custom-call | tf_op jit(solution)/shard_map/partial_adjoint/pallas_call | solution.py:164
  59.5 0.7 %partial_adjoint.4 = (f32[64,2048]{1,0:T(8,128)S(1)}, f32[64,2048]{1,0:T(8,128)S(1)}) custom-call(bf16[2048,2048]{1,0:T(8,128)(2,1)S(1)} %get-tuple-element.25.tiles, bf16[64,1024]{1,0:T(8,128)(2,1)S(1)} %get-tuple-element.50.refs_0_, bf16[64,1024]{1,0:T(8,128)(2,1)S(1)} %collective-permute-done.11.refs_1_, ...), custom_call_target="tpu_custom_call" | custom-call | tf_op jit(solution)/shard_map/partial_adjoint/pallas_call | solution.py:164
  60.3 0.6 collective-permute-done.17
  61.7 1.4 %collective-permute-start.21 = (bf16[32,2048]{1,0:T(8,128)(2,1)S(1)}, bf16[32,2048]{1,0:T(8,128)(2,1)S(1)}, u32[]{:S(2)}, u32[]{:S(2)}) collective-permute-start(bf16[32,2048]{1,0:T(8,128)(2,1)S(1)} %get-tuple-element.57), channel_id=1, source_target_pairs={{0,16},{4,20},{8,24},{12,28},{16,0},{20,4},{24,8},{28,12},{1,17},{... | collective-permute-start | bytes 393224 | tf_op jit(solution)/shard_map/ppermute | solution.py:18
  63.2 1.5 %collective-permute-start.20 = (bf16[32,2048]{1,0:T(8,128)(2,1)S(1)}, bf16[32,2048]{1,0:T(8,128)(2,1)S(1)}, u32[]{:S(2)}, u32[]{:S(2)}) collective-permute-start(bf16[32,2048]{1,0:T(8,128)(2,1)S(1)} %get-tuple-element.56), channel_id=1, source_target_pairs={{0,24},{4,28},{8,16},{12,20},{16,8},{20,12},{24,0},{28,4},{1,25},{... | collective-permute-start | bytes 393224 | tf_op jit(solution)/shard_map/ppermute | solution.py:18
  64.6 0.8 %maximum_bitcast_fusion = f32[2048,64]{0,1:T(8,128)} fusion(f32[64,1024]{1,0:T(8,128)S(1)} %get-tuple-element.51, f32[64,1024]{1,0:T(8,128)S(1)} %get-tuple-element.49), kind=kLoop, calls=%fused_computation | loop fusion | flops 131072 | bytes 1048576 | tf_op jit(solution)/shard_map/transpose | solution.py:223
  65.5 3.6 %collective-permute-done.21 = bf16[32,2048]{1,0:T(8,128)(2,1)S(1)} collective-permute-done((bf16[32,2048]{1,0:T(8,128)(2,1)S(1)}, bf16[32,2048]{1,0:T(8,128)(2,1)S(1)}, u32[]{:S(2)}, u32[]{:S(2)}) %collective-permute-start.21) | collective-permute-done | bytes 131104 | tf_op jit(solution)/shard_map/ppermute | solution.py:18
  69.1 1.1 %collective-permute-done.20 = bf16[32,2048]{1,0:T(8,128)(2,1)S(1)} collective-permute-done((bf16[32,2048]{1,0:T(8,128)(2,1)S(1)}, bf16[32,2048]{1,0:T(8,128)(2,1)S(1)}, u32[]{:S(2)}, u32[]{:S(2)}) %collective-permute-start.20) | collective-permute-done | bytes 131104 | tf_op jit(solution)/shard_map/ppermute | solution.py:18
  70.2 0.8 %fusion.11 = f32[2048,32]{0,1:T(8,128)} fusion(f32[64,2048]{1,0:T(8,128)S(1)} %collective-permute-done.17, bf16[32,2048]{1,0:T(8,128)(2,1)S(1)} %collective-permute-done.21, bf16[32,2048]{1,0:T(8,128)(2,1)S(1)} %collective-permute-done.20, bf16[32,2048]{1,0:T(8,128)(2,1)S(1)} %collective-permute-done.18, f32[64,2048]{1,0:T(8,128)S(1)} %get-tuple-element.43), kind=kLoop, calls=%fused_computation.21 | loop fusion | flops 458752 | bytes 1179648 | tf_op jit(solution)/shard_map/transpose | solution.py:223
  (31 shorter events, 3.1 us)
Async XLA Ops:
  0.6 8.2 %copy-start = (bf16[2048,32]{0,1:T(8,128)(2,1)S(1)}, bf16[2048,32]{0,1:T(8,128)(2,1)}, u32[]{:S(2)}) copy-start(bf16[2048,32]{0,1:T(8,128)(2,1)} %param.5) | copy-start | bytes 393220
  0.6 8.2 %collective-permute-start = (bf16[32,2048]{1,0:T(8,128)(2,1)}, bf16[32,2048]{1,0:T(8,128)(2,1)S(1)}, u32[]{:S(2)}, u32[]{:S(2)}) collective-permute-start(bf16[32,2048]{1,0:T(8,128)(2,1)} %bitcast.5), channel_id=1, source_target_pairs={{0,8},{4,12},{8,0},{12,4},{16,24},{20,28},{24,16},{28,20},{1,9},{5... | collective-permute-start | bytes 393224 | tf_op jit(solution)/shard_map/ppermute | solution.py:18
  3.6 5.2 %collective-permute-start.1 = (bf16[32,2048]{1,0:T(8,128)(2,1)}, bf16[32,2048]{1,0:T(8,128)(2,1)S(1)}, u32[]{:S(2)}, u32[]{:S(2)}) collective-permute-start(bf16[32,2048]{1,0:T(8,128)(2,1)} %bitcast.6), channel_id=1, source_target_pairs={{0,16},{4,20},{8,24},{12,28},{16,0},{20,4},{24,8},{28,12},{1,17},{... | collective-permute-start | bytes 393224 | tf_op jit(solution)/shard_map/ppermute | solution.py:18
  8.9 8.2 %collective-permute-start.3 = (bf16[96,2048]{1,0:T(8,128)(2,1)S(1)}, bf16[96,2048]{1,0:T(8,128)(2,1)S(1)}, u32[]{:S(2)}, u32[]{:S(2)}) collective-permute-start(bf16[96,2048]{1,0:T(8,128)(2,1)S(1)} %pad_maximum_fusion), channel_id=1, source_target_pairs={{0,4},{4,0},{8,12},{12,8},{16,20},{20,16},{24,28},{28,24},{1,5},{5... | collective-permute-start | bytes 1179656 | tf_op jit(solution)/shard_map/ppermute | solution.py:18
  8.9 6.8 %collective-permute-start.2 = (bf16[32,2048]{1,0:T(8,128)(2,1)S(1)}, bf16[32,2048]{1,0:T(8,128)(2,1)S(1)}, u32[]{:S(2)}, u32[]{:S(2)}) collective-permute-start(bf16[32,2048]{1,0:T(8,128)(2,1)S(1)} %bitcast.8), channel_id=1, source_target_pairs={{0,24},{4,28},{8,16},{12,20},{16,8},{20,12},{24,0},{28,4},{1,25},{... | collective-permute-start | bytes 393224 | tf_op jit(solution)/shard_map/ppermute | solution.py:18
  15.8 1.3 %collective-permute-start.4 = (bf16[32,2048]{1,0:T(8,128)(2,1)S(1)}, bf16[32,2048]{1,0:T(8,128)(2,1)S(1)}, u32[]{:S(2)}, u32[]{:S(2)}) collective-permute-start(bf16[32,2048]{1,0:T(8,128)(2,1)S(1)} %collective-permute-done.2.refs_3_), channel_id=1, source_target_pairs={{0,4},{4,0},{8,12},{12,8},{16,20},{20,16},{24,28},{28,24},{1,5},{5... | collective-permute-start | bytes 393224 | tf_op jit(solution)/shard_map/ppermute | solution.py:18
  18.4 6.6 %collective-permute-start.5 = (bf16[64,1024]{1,0:T(8,128)(2,1)S(1)}, bf16[64,1024]{1,0:T(8,128)(2,1)S(1)}, u32[]{:S(2)}, u32[]{:S(2)}) collective-permute-start(bf16[64,1024]{1,0:T(8,128)(2,1)S(1)} %get-tuple-element.35), channel_id=1, source_target_pairs={{0,1},{3,2},{2,0},{1,3},{4,5},{7,6},{6,4},{5,7},{8,9},{11,10},{10,... | collective-permute-start | bytes 393224 | tf_op jit(solution)/shard_map/ppermute | solution.py:33
  21.5 8.1 %collective-permute-start.8 = (bf16[64,1024]{1,0:T(8,128)(2,1)S(1)}, bf16[64,1024]{1,0:T(8,128)(2,1)S(1)}, u32[]{:S(2)}, u32[]{:S(2)}) collective-permute-start(bf16[64,1024]{1,0:T(8,128)(2,1)S(1)} %get-tuple-element.41), channel_id=1, source_target_pairs={{0,1},{3,2},{2,0},{1,3},{4,5},{7,6},{6,4},{5,7},{8,9},{11,10},{10,... | collective-permute-start | bytes 393224 | tf_op jit(solution)/shard_map/ppermute | solution.py:33
  25.1 9.0 %collective-permute-start.7 = (bf16[64,1024]{1,0:T(8,128)(2,1)S(1)}, bf16[64,1024]{1,0:T(8,128)(2,1)S(1)}, u32[]{:S(2)}, u32[]{:S(2)}) collective-permute-start(bf16[64,1024]{1,0:T(8,128)(2,1)S(1)} %get-tuple-element.52), channel_id=1, source_target_pairs={{0,3},{1,2},{2,1},{3,0},{4,7},{5,6},{6,5},{7,4},{8,11},{9,10},{10,... | collective-permute-start | bytes 393224 | tf_op jit(solution)/shard_map/ppermute | solution.py:18
  29.6 8.6 %collective-permute-start.6 = (bf16[64,1024]{1,0:T(8,128)(2,1)S(1)}, bf16[64,1024]{1,0:T(8,128)(2,1)S(1)}, u32[]{:S(2)}, u32[]{:S(2)}) collective-permute-start(bf16[64,1024]{1,0:T(8,128)(2,1)S(1)} %get-tuple-element.36), channel_id=1, source_target_pairs={{0,1},{1,0},{2,3},{3,2},{4,5},{5,4},{6,7},{7,6},{8,9},{9,8},{10,11... | collective-permute-start | bytes 393224 | tf_op jit(solution)/shard_map/ppermute | solution.py:18
  29.7 10.2 %collective-permute-start.10 = (bf16[64,1024]{1,0:T(8,128)(2,1)S(1)}, bf16[64,1024]{1,0:T(8,128)(2,1)S(1)}, u32[]{:S(2)}, u32[]{:S(2)}) collective-permute-start(bf16[64,1024]{1,0:T(8,128)(2,1)S(1)} %get-tuple-element.54), channel_id=1, source_target_pairs={{0,3},{1,2},{2,1},{3,0},{4,7},{5,6},{6,5},{7,4},{8,11},{9,10},{10,... | collective-permute-start | bytes 393224 | tf_op jit(solution)/shard_map/ppermute | solution.py:18
  32.4 9.4 %collective-permute-start.9 = (bf16[64,1024]{1,0:T(8,128)(2,1)S(1)}, bf16[64,1024]{1,0:T(8,128)(2,1)S(1)}, u32[]{:S(2)}, u32[]{:S(2)}) collective-permute-start(bf16[64,1024]{1,0:T(8,128)(2,1)S(1)} %get-tuple-element.42), channel_id=1, source_target_pairs={{0,1},{1,0},{2,3},{3,2},{4,5},{5,4},{6,7},{7,6},{8,9},{9,8},{10,11... | collective-permute-start | bytes 393224 | tf_op jit(solution)/shard_map/ppermute | solution.py:18
  38.3 8.3 %collective-permute-start.15 = (bf16[64,1024]{1,0:T(8,128)(2,1)S(1)}, bf16[64,1024]{1,0:T(8,128)(2,1)S(1)}, u32[]{:S(2)}, u32[]{:S(2)}) collective-permute-start(bf16[64,1024]{1,0:T(8,128)(2,1)S(1)} %get-tuple-element.48.refs_0_), channel_id=1, source_target_pairs={{0,3},{1,2},{2,1},{3,0},{4,7},{5,6},{6,5},{7,4},{8,11},{9,10},{10,... | collective-permute-start | bytes 393224 | tf_op jit(solution)/shard_map/ppermute | solution.py:18
  41.9 8.7 %collective-permute-start.12 = (bf16[64,1024]{1,0:T(8,128)(2,1)S(1)}, bf16[64,1024]{1,0:T(8,128)(2,1)S(1)}, u32[]{:S(2)}, u32[]{:S(2)}) collective-permute-start(bf16[64,1024]{1,0:T(8,128)(2,1)S(1)} %get-tuple-element.50.refs_0_), channel_id=1, source_target_pairs={{0,3},{1,2},{2,1},{3,0},{4,7},{5,6},{6,5},{7,4},{8,11},{9,10},{10,... | collective-permute-start | bytes 393224 | tf_op jit(solution)/shard_map/ppermute | solution.py:18
  44.3 13.8 %collective-permute-start.11 = (bf16[64,1024]{1,0:T(8,128)(2,1)S(1)}, bf16[64,1024]{1,0:T(8,128)(2,1)S(1)}, u32[]{:S(2)}, u32[]{:S(2)}) collective-permute-start(bf16[64,1024]{1,0:T(8,128)(2,1)S(1)} %get-tuple-element.50.refs_0_), channel_id=1, source_target_pairs={{0,1},{1,0},{2,3},{3,2},{4,5},{5,4},{6,7},{7,6},{8,9},{9,8},{10,11... | collective-permute-start | bytes 393224 | tf_op jit(solution)/shard_map/ppermute | solution.py:18
  44.7 9.9 %collective-permute-start.14 = (bf16[64,1024]{1,0:T(8,128)(2,1)S(1)}, bf16[64,1024]{1,0:T(8,128)(2,1)S(1)}, u32[]{:S(2)}, u32[]{:S(2)}) collective-permute-start(bf16[64,1024]{1,0:T(8,128)(2,1)S(1)} %get-tuple-element.48.refs_0_), channel_id=1, source_target_pairs={{0,1},{1,0},{2,3},{3,2},{4,5},{5,4},{6,7},{7,6},{8,9},{9,8},{10,11... | collective-permute-start | bytes 393224 | tf_op jit(solution)/shard_map/ppermute | solution.py:18
  46.6 10.2 %collective-permute-start.16 = (bf16[64,1024]{1,0:T(8,128)(2,1)S(1)}, bf16[64,1024]{1,0:T(8,128)(2,1)S(1)}, u32[]{:S(2)}, u32[]{:S(2)}) collective-permute-start(bf16[64,1024]{1,0:T(8,128)(2,1)S(1)} %select_n.26), channel_id=1, source_target_pairs={{0,2},{3,1},{1,0},{2,3},{4,6},{7,5},{5,4},{6,7},{8,10},{11,9},{9,8... | collective-permute-start | bytes 393224 | tf_op jit(solution)/shard_map/ppermute | solution.py:51
  50.6 7.6 %collective-permute-start.13 = (bf16[64,1024]{1,0:T(8,128)(2,1)S(1)}, bf16[64,1024]{1,0:T(8,128)(2,1)S(1)}, u32[]{:S(2)}, u32[]{:S(2)}) collective-permute-start(bf16[64,1024]{1,0:T(8,128)(2,1)S(1)} %select_n.25), channel_id=1, source_target_pairs={{0,2},{3,1},{1,0},{2,3},{4,6},{7,5},{5,4},{6,7},{8,10},{11,9},{9,8... | collective-permute-start | bytes 393224 | tf_op jit(solution)/shard_map/ppermute | solution.py:51
  59.0 2.0 %collective-permute-start.17 = (f32[64,2048]{1,0:T(8,128)S(1)}, f32[64,2048]{1,0:T(8,128)S(1)}, u32[]{:S(2)}, u32[]{:S(2)}) collective-permute-start(f32[64,2048]{1,0:T(8,128)S(1)} %get-tuple-element.44), channel_id=1, source_target_pairs={{0,4},{4,0},{8,12},{12,8},{16,20},{20,16},{24,28},{28,24},{1,5},{5... | collective-permute-start | bytes 1572872 | tf_op jit(solution)/shard_map/ppermute | solution.py:18
  59.0 2.6 %collective-permute-start.19 = (f32[64,2048]{1,0:T(8,128)S(1)}, f32[64,2048]{1,0:T(8,128)S(1)}, u32[]{:S(2)}, u32[]{:S(2)}) collective-permute-start(f32[64,2048]{1,0:T(8,128)S(1)} %get-tuple-element.47), channel_id=1, source_target_pairs={{0,4},{4,0},{8,12},{12,8},{16,20},{20,16},{24,28},{28,24},{1,5},{5... | collective-permute-start | bytes 1572872 | tf_op jit(solution)/shard_map/ppermute | solution.py:18
  61.0 9.2 %collective-permute-start.18 = (bf16[32,2048]{1,0:T(8,128)(2,1)S(1)}, bf16[32,2048]{1,0:T(8,128)(2,1)S(1)}, u32[]{:S(2)}, u32[]{:S(2)}) collective-permute-start(bf16[32,2048]{1,0:T(8,128)(2,1)S(1)} %slice_add_fusion.2), channel_id=1, source_target_pairs={{0,8},{4,12},{8,0},{12,4},{16,24},{20,28},{24,16},{28,20},{1,9},{5... | collective-permute-start | bytes 393224 | tf_op jit(solution)/shard_map/ppermute | solution.py:18
  61.7 7.3 %collective-permute-start.21 = (bf16[32,2048]{1,0:T(8,128)(2,1)S(1)}, bf16[32,2048]{1,0:T(8,128)(2,1)S(1)}, u32[]{:S(2)}, u32[]{:S(2)}) collective-permute-start(bf16[32,2048]{1,0:T(8,128)(2,1)S(1)} %get-tuple-element.57), channel_id=1, source_target_pairs={{0,16},{4,20},{8,24},{12,28},{16,0},{20,4},{24,8},{28,12},{1,17},{... | collective-permute-start | bytes 393224 | tf_op jit(solution)/shard_map/ppermute | solution.py:18
  63.2 7.0 %collective-permute-start.20 = (bf16[32,2048]{1,0:T(8,128)(2,1)S(1)}, bf16[32,2048]{1,0:T(8,128)(2,1)S(1)}, u32[]{:S(2)}, u32[]{:S(2)}) collective-permute-start(bf16[32,2048]{1,0:T(8,128)(2,1)S(1)} %get-tuple-element.56), channel_id=1, source_target_pairs={{0,24},{4,28},{8,16},{12,20},{16,8},{20,12},{24,0},{28,4},{1,25},{... | collective-permute-start | bytes 393224 | tf_op jit(solution)/shard_map/ppermute | solution.py:18
